TPU v7x, 32 devices: a whole 2x2x4 slice. The times are simulated.
32 devices in a mesh: front: 8 (over y, x, core), row: 4 (over z).
Axes of the slice: x: 2, y: 2, z: 4, core: 2. Of those that a mesh axis runs over, the one named last changes fastest.
Arguments:
- rhs_front: bfloat16 [16384, 384], P(('front', 'row')), may hold values from -6 to 6
- rhs_root: float32 [12288, 384], P('row'), may hold values from -6 to 6
- pivot_inverse: bfloat16 [16384, 2048], P(('front', 'row')), may hold values from -0.125 to 0.125
- border_coupling: bfloat16 [49152, 2048], P(('front', 'row')), may hold values from -0.125 to 0.125
- root_inverse: bfloat16 [12288, 12288], P('front', 'row'), may hold values from -0.0546875 to 0.0546875
- border_map: int32 [8, 48], P('front', 'row'), may hold values from 0 to 95, as said below
Outputs:
- front_solution: float32 [16384, 384], P(('front', 'row'))
- root_solution: float32 [12288, 384], P(('front', 'row'))
Inputs may be any that keep to these rules, and one draw needn't show every extreme that they name: `border_map`: for each front and each index r of row, the 12 border blocks held at that index name distinct root blocks, all among blocks r * 24 to (r + 1) * 24 - 1; a root block may be named by many fronts or by none.
All inputs are finite; a program needn't handle non-finite values.
Results may differ from a plain program's by a relative error of at most 0.0075.
Values may be sent and summed in bfloat16 or wider, within the bound.
No kernel may reach another device: no remote copies, remote signals or barrier semaphores. Data moves between devices by JAX's collectives and lax.ppermute only.
A program may use at most 64 MiB of HBM per device.

v0:
```python
import jax
import jax.numpy as jnp
from jax import lax
from jax.sharding import PartitionSpec as P

BLK = 128


def per_device(rhs_front, rhs_root, pivot_inverse, border_coupling, root_inverse, border_map):
    row_at = lax.axis_index("row")
    front_at = lax.axis_index("front")
    width = rhs_front.shape[1]

    def pivot_step(piece):
        return jnp.dot(pivot_inverse, piece, preferred_element_type=jnp.float32)

    inner = pivot_step(lax.all_gather(rhs_front, "row", axis=0, tiled=True))
    inner_half = inner.astype(jnp.bfloat16)
    columns = border_coupling
    contrib = jnp.dot(
        columns,
        lax.all_gather(inner_half, "row", axis=0, tiled=True),
        preferred_element_type=jnp.float32,
    )
    block_local = border_map.shape[1]
    span_rows = root_inverse.shape[1]
    span_blocks = span_rows // BLK
    local_index = border_map[0] - row_at * span_blocks
    select = (local_index[None, :] == jnp.arange(span_blocks, dtype=jnp.int32)[:, None]).astype(
        jnp.float32
    )
    dense = jnp.einsum(
        "kj,jcn->kcn",
        select,
        contrib.reshape(block_local, BLK, width),
        precision=lax.Precision.HIGHEST,
    ).reshape(span_rows, width)
    shares = lax.psum_scatter(dense, "front", scatter_dimension=0, tiled=True)
    own_rhs = lax.dynamic_slice_in_dim(rhs_root, front_at * shares.shape[0], shares.shape[0], 0)
    schur_piece = (own_rhs - shares).astype(jnp.bfloat16)
    schur_rhs = lax.all_gather(schur_piece, "front", axis=0, tiled=True)
    root_solution = lax.psum_scatter(
        jnp.dot(root_inverse, schur_rhs, preferred_element_type=jnp.float32),
        "row",
        scatter_dimension=0,
        tiled=True,
    )
    root_half = root_solution.astype(jnp.bfloat16)
    gathered = lax.all_gather(root_half, ("front", "row"), axis=0, tiled=True)
    ranged = lax.dynamic_slice_in_dim(gathered, row_at * span_rows, span_rows, 0)
    picked = jnp.einsum(
        "kj,kcn->jcn",
        select.astype(jnp.bfloat16),
        ranged.reshape(span_blocks, BLK, width),
        preferred_element_type=jnp.float32,
    )
    picked = picked.astype(jnp.bfloat16).reshape(block_local * BLK, width)
    columns = border_coupling
    pulled = lax.psum_scatter(
        lax.dot_general(
            columns, picked, (((0,), (0,)), ((), ())), preferred_element_type=jnp.float32
        ),
        "row",
        scatter_dimension=0,
        tiled=True,
    ).astype(jnp.bfloat16)
    correction = pivot_step(lax.all_gather(pulled, "row", axis=0, tiled=True))
    return (inner - correction, root_solution)


def solution(mesh):
    in_specs = (
        P(("front", "row"), None),
        P("row", None),
        P(("front", "row"), None),
        P(("front", "row"), None),
        P("front", "row"),
        P("front", "row"),
    )
    out_specs = (P(("front", "row"), None), P(("front", "row"), None))
    return jax.shard_map(
        per_device, mesh=mesh, in_specs=in_specs, out_specs=out_specs, check_vma=False
    )
```

profile of v0, /device:TPU:0, one launch (start us, length us, event | category | flops | bytes accessed | tf_op | source)
XLA Modules:
  0.0 465.0 jit_solution(12569750621025778426)
XLA Ops:
  7.2 0.0 copy-start
  7.2 0.0 all-gather.6.cloned.1.call-start
  7.2 0.7 all-gather.6.cloned.1.call-update
  7.9 0.0 copy-start.2
  7.9 0.0 all-gather.8.cloned.1.call-start
  8.0 41.4 %all-gather.6.cloned.1.call-done = bf16[2048,384]{1,0:T(8,128)(2,1)} async-done(((bf16[512,384]{1,0:T(8,128)(2,1)}), bf16[2048,384]{1,0:T(8,128)(2,1)}) %all-gather.6.cloned.1.call-update) | async-done | bytes 1572880 | tf_op jit(solution)/shard_map/all_gather | solution.py:17
  49.4 0.0 copy-done
  49.4 3.4 fusion.14
  52.8 0.0 all-gather.8.cloned.1.call-update
  52.8 0.0 reduce-scatter.4.cloned.1.call-start
  52.9 0.0 copy-done.2
  52.9 36.0 %all-gather.8.cloned.1.call-done = bf16[2048,384]{1,0:T(8,128)(2,1)} async-done(((bf16[512,384]{1,0:T(8,128)(2,1)}), bf16[2048,384]{1,0:T(8,128)(2,1)}) %all-gather.8.cloned.1.call-update) | async-done | bytes 1572880 | tf_op jit(solution)/shard_map/all_gather | solution.py:22
  88.9 7.3 %convolution_bitcast_fusion.1 = f32[1536,384]{0,1:T(8,128)} fusion(bf16[2048,384]{1,0:T(8,128)(2,1)} %all-gather.8.cloned.1.call-done, bf16[1536,2048]{1,0:T(8,128)(2,1)} %param.9), kind=kOutput, calls=%fused_computation.3 | convolution fusion | flops 2415919104 | bytes 10223616 | tf_op jit(solution)/shard_map/dot_general | solution.py:20
  96.3 3.1 copy.11
  99.4 4.9 %fusion = f32[24,128,384]{2,0,1:T(8,128)S(1)} fusion(f32[12,128,384]{2,1,0:T(8,128)} %bitcast.33, s32[12]{0:T(128)S(1)} %subtract_bitcast_fusion), kind=kOutput, calls=%fused_computation | convolution fusion | flops 169869600 | bytes 7077936 | tf_op jit(solution)/shard_map/kj,jcn->kcn/dot_general | solution.py:32
  104.3 3.0 copy.13
  107.3 0.0 reduce-scatter.4.cloned.1.call-update
  107.3 0.0 all-gather.10.cloned.1.call-start
  107.3 52.9 %reduce-scatter.4.cloned.1.call-done = f32[384,384]{1,0:T(8,128)} async-done(((f32[3072,384]{1,0:T(8,128)}), f32[384,384]{1,0:T(8,128)}) %reduce-scatter.4.cloned.1.call-update) | async-done | bytes 589840 | tf_op jit(solution)/shard_map/reduce_scatter | solution.py:38
  160.2 2.0 subtract_convert_fusion
  162.2 0.0 all-gather.10.cloned.1.call-update
  162.2 0.2 reduce-scatter.6.cloned.1.call-start
  162.5 29.2 %all-gather.10.cloned.1.call-done = bf16[3072,384]{1,0:T(8,128)(2,1)} async-done(((bf16[384,384]{1,0:T(8,128)(2,1)}), bf16[3072,384]{1,0:T(8,128)(2,1)}) %all-gather.10.cloned.1.call-update) | async-done | bytes 2359312 | tf_op jit(solution)/shard_map/all_gather | solution.py:41
  191.7 9.7 %convolution_bitcast_fusion.2 = f32[1536,384]{0,1:T(8,128)} fusion(bf16[3072,384]{1,0:T(8,128)(2,1)} %all-gather.10.cloned.1.call-done, bf16[1536,3072]{1,0:T(8,128)(2,1)} %param.10), kind=kOutput, calls=%fused_computation.4 | convolution fusion | flops 3623878656 | bytes 14155776 | tf_op jit(solution)/shard_map/dot_general | solution.py:43
  201.4 0.0 reduce-scatter.6.cloned.1.call-update
  201.4 0.0 all-gather.12.cloned.1.call-start
  201.5 48.1 %reduce-scatter.6.cloned.1.call-done = f32[384,384]{0,1:T(8,128)} async-done(((f32[1536,384]{0,1:T(8,128)}), f32[384,384]{0,1:T(8,128)}) %reduce-scatter.6.cloned.1.call-update) | async-done | bytes 589840 | tf_op jit(solution)/shard_map/reduce_scatter | solution.py:42
  249.6 1.8 convert_element_type.25
  251.4 0.0 all-gather.12.cloned.1.call-update
  251.4 0.0 reduce-scatter.8.cloned.1.call-start
  251.5 86.8 %all-gather.12.cloned.1.call-done = bf16[12288,384]{0,1:T(8,128)(2,1)} async-done(((bf16[384,384]{0,1:T(8,128)(2,1)}), bf16[12288,384]{0,1:T(8,128)(2,1)}) %all-gather.12.cloned.1.call-update) | async-done | bytes 9437200 | tf_op jit(solution)/shard_map/all_gather | solution.py:49
  338.3 3.2 constant_dynamic-slice_fusion
  341.5 4.3 copy.14
  345.8 3.5 fusion.4
  349.2 0.3 copy.16
  349.5 7.1 %convolution_bitcast_fusion = f32[2048,384]{0,1:T(8,128)} fusion(bf16[1536,384]{1,0:T(8,128)(2,1)S(1)} %bitcast.35, bf16[1536,2048]{1,0:T(8,128)(2,1)} %param.9), kind=kOutput, calls=%fused_computation.2 | convolution fusion | flops 2415919104 | bytes 10616832 | tf_op jit(solution)/shard_map/dot_general | solution.py:60
  356.6 0.0 copy-start.1
  356.6 0.0 reduce-scatter.8.cloned.1.call-update
  356.6 0.0 all-gather.14.cloned.1.call-start
  356.7 58.5 %reduce-scatter.8.cloned.1.call-done = f32[512,384]{0,1:T(8,128)} async-done(((f32[2048,384]{0,1:T(8,128)}), f32[512,384]{0,1:T(8,128)}) %reduce-scatter.8.cloned.1.call-update) | async-done | bytes 786448 | tf_op jit(solution)/shard_map/reduce_scatter | solution.py:59
  415.2 1.9 convert_element_type.27
  417.2 0.0 all-gather.14.cloned.1.call-update
  417.2 0.0 copy-done.1
  417.2 1.1 copy.18
  418.2 36.4 %all-gather.14.cloned.1.call-done = bf16[2048,384]{0,1:T(8,128)(2,1)} async-done(((bf16[512,384]{0,1:T(8,128)(2,1)}), bf16[2048,384]{0,1:T(8,128)(2,1)}) %all-gather.14.cloned.1.call-update) | async-done | bytes 1572880 | tf_op jit(solution)/shard_map/all_gather | solution.py:67
  454.6 3.6 fusion.7
  (1 shorter events, 0.0 us)
Async XLA Ops:
  7.2 42.2 %copy-start = (bf16[512,2048]{1,0:T(8,128)(2,1)S(1)}, bf16[512,2048]{1,0:T(8,128)(2,1)}, u32[]{:S(2)}) copy-start(bf16[512,2048]{1,0:T(8,128)(2,1)} %param.8) | copy-start | bytes 6291460
  7.2 42.2 %all-gather.6.cloned.1.call-start = ((), (), s32[]{:S(2)}) async-start(), calls=%async_computation.3 | async-start | bytes 1966080 | tf_op jit(solution)/shard_map/all_gather | solution.py:17
  7.9 45.0 %copy-start.2 = (s32[1,12]{1,0:T(1,128)S(1)}, s32[1,12]{1,0:T(1,128)}, u32[]{:S(2)}) copy-start(s32[1,12]{1,0:T(1,128)} %param.11) | copy-start | bytes 148
  7.9 81.0 %all-gather.8.cloned.1.call-start = ((), (), s32[]{:S(2)}) async-start(), calls=%async_computation.4 | async-start | bytes 1966080 | tf_op jit(solution)/shard_map/all_gather | solution.py:22
  52.8 107.3 %reduce-scatter.4.cloned.1.call-start = ((), (), s32[]{:S(2)}) async-start(), calls=%async_computation.5 | async-start | bytes 5308416 | tf_op jit(solution)/shard_map/reduce_scatter | solution.py:38
  107.3 84.4 %all-gather.10.cloned.1.call-start = ((), (), s32[]{:S(2)}) async-start(), calls=%async_computation.6 | async-start | bytes 2654208 | tf_op jit(solution)/shard_map/all_gather | solution.py:41
  162.2 87.4 %reduce-scatter.6.cloned.1.call-start = ((), (), s32[]{:S(2)}) async-start(), calls=%async_computation.7 | async-start | bytes 2949120 | tf_op jit(solution)/shard_map/reduce_scatter | solution.py:42
  201.4 136.9 %all-gather.12.cloned.1.call-start = ((), (), s32[]{:S(2)}) async-start(), calls=%async_computation.8 | async-start | bytes 9732096 | tf_op jit(solution)/shard_map/all_gather | solution.py:49
  251.4 163.8 %reduce-scatter.8.cloned.1.call-start = ((), (), s32[]{:S(2)}) async-start(), calls=%async_computation.9 | async-start | bytes 3932160 | tf_op jit(solution)/shard_map/reduce_scatter | solution.py:59
  356.6 60.6 %copy-start.1 = (f32[384,384]{0,1:T(8,128)S(1)}, f32[384,384]{0,1:T(8,128)}, u32[]{:S(2)}) copy-start(f32[384,384]{0,1:T(8,128)} %reduce-scatter.6.cloned.1.call-done) | copy-start | bytes 1769476
  356.6 98.0 %all-gather.14.cloned.1.call-start = ((), (), s32[]{:S(2)}) async-start(), calls=%async_computation.10 | async-start | bytes 1966080 | tf_op jit(solution)/shard_map/all_gather | solution.py:67
Sparse Core Ops, SparseCore 0:
  9.6 39.7 all-gather.5
  53.0 35.9 all-gather.7
  107.4 52.7 reduce-scatter.3
  162.7 28.9 all-gather.9
  201.5 48.0 reduce-scatter.5
  253.3 84.9 all-gather.11
  356.8 58.4 reduce-scatter.7
  417.5 37.1 all-gather.13
where the time goes:
time: 466 us; the launch traced here: 465 us
  waiting for transfers between devices  390 us (84%)
  matrix products  39.5 us (8%)
  local copies, waits for them, and re-layouts  14.8 us (3%)
  between operations  14.2 us (3%)
  other arithmetic  5.75 us (1%)
    all_gather x1, waiting for transfers between devices, per_device(): gathered = lax.all_gather(root_half, ('front', 'row'), axis=0, tiled=True)  86.8 us
    reduce_scatter x1, waiting for transfers between devices, per_device(): lax.psum_scatter(lax.dot_general(columns, picked, (((0,), (0,)), ((), ())...  58.5 us
    reduce_scatter x1, waiting for transfers between devices, per_device(): shares = lax.psum_scatter(dense, 'front', scatter_dimension=0, tiled=True)  52.9 us
    reduce_scatter x1, waiting for transfers between devices, per_device(): lax.psum_scatter(jnp.dot(root_inverse, schur_rhs, preferred_element_type=...  48.1 us
    all_gather x1, waiting for transfers between devices, per_device(): inner = pivot_step(lax.all_gather(rhs_front, 'row', axis=0, tiled=True))  41.4 us
    all_gather x1, waiting for transfers between devices, per_device(): correction = pivot_step(lax.all_gather(pulled, 'row', axis=0, tiled=True))  36.4 us
    all_gather x1, waiting for transfers between devices, per_device(): lax.all_gather(inner_half, 'row', axis=0, tiled=True)  36 us
    all_gather x1, waiting for transfers between devices, per_device(): schur_rhs = lax.all_gather(schur_piece, 'front', axis=0, tiled=True)  29.2 us
  transfers between devices with their start and end apart: 8, of which 8 were waited for; matrix products, arithmetic and copies ran while one was open for 0% of the time, Pallas kernels for 0%

commit v1 on v0

v1 whole, which is shorter than its diff:
```python
import functools

import jax
import jax.numpy as jnp
from jax import lax
from jax.sharding import PartitionSpec as P

BLK = 128
F32 = jnp.float32
BF16 = jnp.bfloat16


def shift(x, axis, size, by):
    return lax.ppermute(x, axis, [(i, (i + by) % size) for i in range(size)])


def gather_row(x, n, at):
    length = x.shape[0]
    whole = lax.dynamic_update_slice_in_dim(
        jnp.zeros((n * length,) + x.shape[1:], x.dtype), x, at * length, 0
    )
    up, down = x, x
    for step in range(1, n // 2 + 1):
        up = shift(up, "row", n, 1)
        whole = lax.dynamic_update_slice_in_dim(whole, up, (at - step) % n * length, 0)
        if step < n - step:
            down = shift(down, "row", n, -1)
            whole = lax.dynamic_update_slice_in_dim(whole, down, (at + step) % n * length, 0)
    return whole


def scatter_row(partial, n, at):
    length = partial.shape[0] // n

    def block(offset):
        return lax.dynamic_slice_in_dim(partial, (at + offset) % n * length, length, 0)

    total = block(0)
    for sign, far in ((-1, n // 2), (1, (n - 1) // 2)):
        running = None
        for step in range(far, 0, -1):
            mine = block(sign * step)
            running = mine if running is None else running.astype(F32) + mine
            running = shift(running.astype(BF16), "row", n, sign)
        if running is not None:
            total = total + running.astype(F32)
    return total


def per_device(n_front, n_row, rhs_front, rhs_root, pivot_inverse, border_coupling, root_inverse, border_map):
    row_at = lax.axis_index("row")
    front_at = lax.axis_index("front")
    width = rhs_front.shape[1]

    inner = jnp.dot(pivot_inverse, gather_row(rhs_front, n_row, row_at), preferred_element_type=F32)
    inner_half = inner.astype(BF16)
    contrib = jnp.dot(
        border_coupling, gather_row(inner_half, n_row, row_at), preferred_element_type=F32
    ).astype(BF16)
    block_local = border_map.shape[1]
    span_rows = root_inverse.shape[1]
    span_blocks = span_rows // BLK
    local_index = border_map[0] - row_at * span_blocks
    select = (local_index[None, :] == jnp.arange(span_blocks, dtype=jnp.int32)[:, None]).astype(BF16)
    dense = jnp.einsum(
        "kj,jcn->kcn", select, contrib.reshape(block_local, BLK, width), preferred_element_type=F32
    ).astype(BF16).reshape(span_rows, width)
    shares = lax.psum_scatter(dense, "front", scatter_dimension=0, tiled=True).astype(F32)
    own_rhs = lax.dynamic_slice_in_dim(rhs_root, front_at * shares.shape[0], shares.shape[0], 0)
    schur_piece = (own_rhs - shares).astype(BF16)
    schur_rhs = lax.all_gather(schur_piece, "front", axis=0, tiled=True)
    root_solution = scatter_row(
        jnp.dot(root_inverse, schur_rhs, preferred_element_type=F32), n_row, row_at
    )
    root_half = root_solution.astype(BF16)
    if n_front == 2 * n_row:
        perm = [
            ((chip * 2 + core) * n_row + row, (row * 2 + core) * n_row + chip)
            for chip in range(n_row)
            for core in range(2)
            for row in range(n_row)
        ]
        moved = lax.ppermute(root_half, ("front", "row"), perm)
        ranged = lax.all_gather(moved, "front", axis=0, tiled=True)
        ranged = ranged.reshape(n_row, 2, root_half.shape[0], width).swapaxes(0, 1)
        ranged = ranged.reshape(span_rows, width)
    else:
        gathered = lax.all_gather(root_half, ("front", "row"), axis=0, tiled=True)
        ranged = lax.dynamic_slice_in_dim(gathered, row_at * span_rows, span_rows, 0)
    picked = jnp.einsum(
        "kj,kcn->jcn", select, ranged.reshape(span_blocks, BLK, width), preferred_element_type=F32
    )
    picked = picked.astype(BF16).reshape(block_local * BLK, width)
    pulled = scatter_row(
        lax.dot_general(border_coupling, picked, (((0,), (0,)), ((), ())), preferred_element_type=F32),
        n_row,
        row_at,
    ).astype(BF16)
    correction = jnp.dot(pivot_inverse, gather_row(pulled, n_row, row_at), preferred_element_type=F32)
    return (inner - correction, root_solution)


def solution(mesh):
    in_specs = (
        P(("front", "row"), None),
        P("row", None),
        P(("front", "row"), None),
        P(("front", "row"), None),
        P("front", "row"),
        P("front", "row"),
    )
    out_specs = (P(("front", "row"), None), P(("front", "row"), None))
    body = functools.partial(per_device, mesh.shape["front"], mesh.shape["row"])
    return jax.shard_map(body, mesh=mesh, in_specs=in_specs, out_specs=out_specs, check_vma=False)
```

time: 466 us -> 346 us (0.74)
  waiting for transfers between devices: 390 us -> 223 us
  starting transfers between devices: 0.51 us -> 29.2 us
  local copies, waits for them, and re-layouts: 14.8 us -> 41.8 us
  matrix products: 39.5 us -> 29.2 us
    all_gather x4 -> x1, waiting for transfers between devices: 201 us -> 52 us  [per_device(): ranged = lax.all_gather(moved, 'front', axis=0, tiled=True)]
    reduce_scatter x3 -> x1, waiting for transfers between devices: 160 us -> 40.8 us  [per_device(): lax.psum_scatter(dense, 'front', scatter_dimension=0, tiled=True)]
    ppermute x0 -> x16, waiting for transfers between devices: none -> 101 us  [the longest x15 101 us: shift(): return lax.ppermute(x, axis, [(i, (i + by) % size) for i in range(size)])]
    ppermute x0 -> x16, starting transfers between devices: none -> 29.1 us  [the longest x15 28.3 us: shift(): return lax.ppermute(x, axis, [(i, (i + by) % size) for i in range(size)])]
    reshape x0 -> x2, local copies, waits for them, and re-layouts: none -> 13.4 us  [per_device(): ranged = ranged.reshape(n_row, 2, root_half.shape[0], width).swapaxes(0, 1)]
    dynamic_update_slice x0 -> x10, local copies, waits for them, and re-layouts: none -> 11.1 us  [the longest x6 6.86 us: gather_row(): lax.dynamic_update_slice_in_dim(whole, up, (at - step) % n * length, 0)]
    dynamic_slice x2 -> x0, local copies, waits for them, and re-layouts: 7.47 us -> none  [per_device(): lax.dynamic_slice_in_dim(gathered, row_at * span_rows, span_rows, 0)]
    dot_general x6, matrix products: 34.6 us -> 28.1 us  [the longest x1 7.22 us: per_device(): jnp.dot(root_inverse, schur_rhs, preferred_element_type=F32)]
  transfers between devices with their start and end apart: 8 -> 19, of which waited for: 8 -> 18; matrix products, arithmetic and copies ran while one was open for 0% -> 4% of each run, Pallas kernels for 0% -> 0%
where the time goes in v1:
time: 346 us; the launch traced here: 345 us
  waiting for transfers between devices  223 us (64%)
  local copies, waits for them, and re-layouts  41.8 us (12%)
  starting transfers between devices  29.2 us (8%)
  matrix products  29.2 us (8%)
  between operations  14 us (4%)
  other arithmetic  7.65 us (2%)
    ppermute x15, waiting for transfers between devices, shift(): return lax.ppermute(x, axis, [(i, (i + by) % size) for i in range(size)])  101 us
    all_gather x1, waiting for transfers between devices, per_device(): ranged = lax.all_gather(moved, 'front', axis=0, tiled=True)  52 us
    reduce_scatter x1, waiting for transfers between devices, per_device(): lax.psum_scatter(dense, 'front', scatter_dimension=0, tiled=True)  40.8 us
    all_gather x1, waiting for transfers between devices, per_device(): schur_rhs = lax.all_gather(schur_piece, 'front', axis=0, tiled=True)  29.6 us
    ppermute x15, starting transfers between devices, shift(): return lax.ppermute(x, axis, [(i, (i + by) % size) for i in range(size)])  28.3 us
    reshape x2, local copies, waits for them, and re-layouts, per_device(): ranged = ranged.reshape(n_row, 2, root_half.shape[0], width).swapaxes(0, 1)  13.4 us
    dot_general x1, matrix products, per_device(): jnp.dot(root_inverse, schur_rhs, preferred_element_type=F32)  7.22 us
    dot_general x1, matrix products, per_device(): jnp.dot(border_coupling, gather_row(inner_half, n_row, row_at), preferred...  6.94 us
  transfers between devices with their start and end apart: 19, of which 18 were waited for; matrix products, arithmetic and copies ran while one was open for 4% of the time, Pallas kernels for 0%

profile of v1, /device:TPU:0, one launch (start us, length us, event | category | flops | bytes accessed | tf_op | source)
XLA Modules:
  0.0 345.0 jit_solution(16372614285510980296)
XLA Ops:
  7.2 3.1 collective-permute-start
  10.3 2.1 collective-permute-start.1
  12.4 10.1 %collective-permute-done = bf16[512,384]{1,0:T(8,128)(2,1)S(1)} collective-permute-done((bf16[512,384]{1,0:T(8,128)(2,1)}, bf16[512,384]{1,0:T(8,128)(2,1)S(1)}, u32[]{:S(2)}, u32[]{:S(2)}) %collective-permute-start) | collective-permute-done | bytes 393248 | tf_op jit(solution)/shard_map/ppermute | solution.py:14
  22.5 1.2 copy.15
  23.7 1.4 broadcast.8.clone
  25.1 0.8 constant_dynamic-update-slice_fusion.11
  26.1 3.8 %collective-permute-done.1 = bf16[512,384]{1,0:T(8,128)(2,1)} collective-permute-done((bf16[512,384]{1,0:T(8,128)(2,1)}, bf16[512,384]{1,0:T(8,128)(2,1)}, u32[]{:S(2)}, u32[]{:S(2)}) %collective-permute-start.1) | collective-permute-done | bytes 393248 | tf_op jit(solution)/shard_map/ppermute | solution.py:14
  29.8 1.2 copy.17
  31.0 0.8 constant_dynamic-update-slice_fusion.10
  31.8 0.8 constant_dynamic-update-slice_fusion.9
  32.6 6.0 %collective-permute-done.2 = bf16[512,384]{1,0:T(8,128)(2,1)} collective-permute-done((bf16[512,384]{1,0:T(8,128)(2,1)S(1)}, bf16[512,384]{1,0:T(8,128)(2,1)}, u32[]{:S(2)}, u32[]{:S(2)}) %collective-permute-start.2) | collective-permute-done | bytes 393248 | tf_op jit(solution)/shard_map/ppermute | solution.py:14
  38.7 1.2 copy.18
  39.8 0.8 constant_dynamic-update-slice_fusion.8
  40.7 2.4 fusion.25
  43.1 1.4 broadcast.8.clone.1
  44.5 0.8 constant_dynamic-update-slice_fusion.7
  45.4 3.8 %collective-permute-start.4 = (bf16[512,384]{0,1:T(8,128)(2,1)S(1)}, bf16[512,384]{0,1:T(8,128)(2,1)S(1)}, u32[]{:S(2)}, u32[]{:S(2)}) collective-permute-start(bf16[512,384]{0,1:T(8,128)(2,1)S(1)} %get-tuple-element.11), channel_id=1, source_target_pairs={{0,3},{1,0},{2,1},{3,2},{4,7},{5,4},{6,5},{7,6},{8,11},{9,8},{10,9... | collective-permute-start | bytes 1179656 | tf_op jit(solution)/shard_map/ppermute | solution.py:14
  49.2 10.0 %collective-permute-done.3 = bf16[512,384]{0,1:T(8,128)(2,1)S(1)} collective-permute-done((bf16[512,384]{0,1:T(8,128)(2,1)S(1)}, bf16[512,384]{0,1:T(8,128)(2,1)S(1)}, u32[]{:S(2)}, u32[]{:S(2)}) %collective-permute-start.3) | collective-permute-done | bytes 393248 | tf_op jit(solution)/shard_map/ppermute | solution.py:14
  59.2 0.8 constant_dynamic-update-slice_fusion.6
  60.0 5.1 %collective-permute-done.4 = bf16[512,384]{0,1:T(8,128)(2,1)S(1)} collective-permute-done((bf16[512,384]{0,1:T(8,128)(2,1)S(1)}, bf16[512,384]{0,1:T(8,128)(2,1)S(1)}, u32[]{:S(2)}, u32[]{:S(2)}) %collective-permute-start.4) | collective-permute-done | bytes 393248 | tf_op jit(solution)/shard_map/ppermute | solution.py:14
  65.2 0.8 constant_dynamic-update-slice_fusion.5
  66.0 6.9 %collective-permute-done.5 = bf16[512,384]{0,1:T(8,128)(2,1)S(1)} collective-permute-done((bf16[512,384]{0,1:T(8,128)(2,1)S(1)}, bf16[512,384]{0,1:T(8,128)(2,1)S(1)}, u32[]{:S(2)}, u32[]{:S(2)}) %collective-permute-start.5) | collective-permute-done | bytes 393248 | tf_op jit(solution)/shard_map/ppermute | solution.py:14
  72.9 0.8 constant_dynamic-update-slice_fusion.4
  73.7 6.9 %fusion = bf16[1536,384]{0,1:T(8,128)(2,1)} fusion(bf16[2048,384]{0,1:T(8,128)(2,1)} %constant_dynamic-update-slice_fusion.4, bf16[1536,2048]{1,0:T(8,128)(2,1)} %param.9), kind=kOutput, calls=%fused_computation.1 | convolution fusion | flops 2416508928 | bytes 9043968 | tf_op jit(solution)/shard_map/dot_general | solution.py:57
  80.6 1.7 copy.19
  82.3 1.0 convolution_convert_fusion.1
  83.4 1.8 copy.21
  85.3 40.8 %reduce-scatter.2.cloned.1.call-done = bf16[384,384]{1,0:T(8,128)(2,1)} async-done(((bf16[3072,384]{1,0:T(8,128)(2,1)}), bf16[384,384]{1,0:T(8,128)(2,1)}) %reduce-scatter.2.cloned.1.call-update) | async-done | bytes 294928 | tf_op jit(solution)/shard_map/reduce_scatter | solution.py:68
  126.1 1.9 subtract_convert_fusion
  128.2 29.6 %all-gather.3.cloned.1.call-done = bf16[3072,384]{1,0:T(8,128)(2,1)} async-done(((bf16[384,384]{1,0:T(8,128)(2,1)}), bf16[3072,384]{1,0:T(8,128)(2,1)}) %all-gather.3.cloned.1.call-update) | async-done | bytes 2359312 | tf_op jit(solution)/shard_map/all_gather | solution.py:71
  157.8 7.2 %fusion.26 = f32[384,1536]{1,0:T(8,128)S(1)} fusion(bf16[3072,384]{1,0:T(8,128)(2,1)} %all-gather.3.cloned.1.call-done, bf16[1536,3072]{1,0:T(8,128)(2,1)} %param.10), kind=kOutput, calls=%fused_computation.47 | convolution fusion | flops 3623878656 | bytes 14155776 | tf_op jit(solution)/shard_map/dot_general | solution.py:73
  165.0 1.4 copy-done.2
  166.6 3.4 collective-permute-start.6
  169.9 7.4 %collective-permute-done.6 = bf16[384,384]{0,1:T(8,128)(2,1)S(1)} collective-permute-done((bf16[384,384]{0,1:T(8,128)(2,1)S(1)}, bf16[384,384]{0,1:T(8,128)(2,1)S(1)}, u32[]{:S(2)}, u32[]{:S(2)}) %collective-permute-start.6) | collective-permute-done | bytes 294944 | tf_op jit(solution)/shard_map/ppermute | solution.py:14
  177.3 1.1 fusion.11
  178.5 4.3 %collective-permute-start.7 = (bf16[384,384]{0,1:T(8,128)(2,1)S(1)}, bf16[384,384]{0,1:T(8,128)(2,1)S(1)}, u32[]{:S(2)}, u32[]{:S(2)}) collective-permute-start(bf16[384,384]{0,1:T(8,128)(2,1)S(1)} %fusion.11), channel_id=1, source_target_pairs={{0,3},{1,0},{2,1},{3,2},{4,7},{5,4},{6,5},{7,6},{8,11},{9,8},{10,9... | collective-permute-start | bytes 884744 | tf_op jit(solution)/shard_map/ppermute | solution.py:14
  182.8 1.9 collective-permute-done.8
  184.7 5.6 %collective-permute-done.7 = bf16[384,384]{0,1:T(8,128)(2,1)S(1)} collective-permute-done((bf16[384,384]{0,1:T(8,128)(2,1)S(1)}, bf16[384,384]{0,1:T(8,128)(2,1)S(1)}, u32[]{:S(2)}, u32[]{:S(2)}) %collective-permute-start.7) | collective-permute-done | bytes 294944 | tf_op jit(solution)/shard_map/ppermute | solution.py:14
  190.3 1.2 fusion.23
  191.4 0.9 collective-permute-start.9
  192.3 0.7 copy-done.5
  193.0 52.0 %all-gather.5.cloned.1.call-done = bf16[3072,384]{0,1:T(8,128)(2,1)} async-done(((bf16[384,384]{0,1:T(8,128)(2,1)}), bf16[3072,384]{0,1:T(8,128)(2,1)}) %all-gather.5.cloned.1.call-update) | async-done | bytes 2359312 | tf_op jit(solution)/shard_map/all_gather | solution.py:84
  245.1 6.5 %reshape.18 = bf16[4,2,384,384]{2,1,0,3:T(2,128)(2,1)} reshape(bf16[3072,384]{0,1:T(8,128)(2,1)} %all-gather.5.cloned.1.call-done) | data formatting | bytes 4718592 | tf_op jit(solution)/shard_map/reshape | solution.py:85
  251.5 6.9 %copy.22 = bf16[4,2,384,384]{3,2,0,1:T(8,128)(2,1)} copy(bf16[4,2,384,384]{2,1,0,3:T(2,128)(2,1)} %reshape.18) | data formatting | bytes 4718592 | tf_op jit(solution)/shard_map/reshape | solution.py:85
  258.4 3.5 %fusion.3 = bf16[12,128,384]{2,0,1:T(8,128)(2,1)S(1)} fusion(bf16[24,128,384]{2,1,0:T(8,128)(2,1)} %bitcast.60, s32[12]{0:T(128)S(1)} %subtract_bitcast_fusion), kind=kOutput, calls=%fused_computation.5 | convolution fusion | flops 28901664 | bytes 3538992 | tf_op jit(solution)/shard_map/kj,kcn->jcn/dot_general | solution.py:90
  262.2 4.8 %fusion.27 = f32[384,2048]{1,0:T(8,128)S(1)} fusion(bf16[1536,384]{1,0:T(8,128)(2,1)S(1)} %bitcast.61, bf16[1536,2048]{1,0:T(8,128)(2,1)} %param.9), kind=kOutput, calls=%fused_computation.48 | convolution fusion | flops 2415919104 | bytes 10616832 | tf_op jit(solution)/shard_map/dot_general | solution.py:95
  267.1 3.4 collective-permute-start.10
  270.5 9.5 %collective-permute-done.10 = bf16[512,384]{0,1:T(8,128)(2,1)S(1)} collective-permute-done((bf16[512,384]{0,1:T(8,128)(2,1)S(1)}, bf16[512,384]{0,1:T(8,128)(2,1)S(1)}, u32[]{:S(2)}, u32[]{:S(2)}) %collective-permute-start.10) | collective-permute-done | bytes 393248 | tf_op jit(solution)/shard_map/ppermute | solution.py:14
  280.1 4.3 %collective-permute-start.11 = (bf16[512,384]{0,1:T(8,128)(2,1)S(1)}, bf16[512,384]{0,1:T(8,128)(2,1)}, u32[]{:S(2)}, u32[]{:S(2)}) collective-permute-start(bf16[512,384]{0,1:T(8,128)(2,1)S(1)} %fusion.8), channel_id=1, source_target_pairs={{0,3},{1,0},{2,1},{3,2},{4,7},{5,4},{6,5},{7,6},{8,11},{9,8},{10,9... | collective-permute-start | bytes 1179656 | tf_op jit(solution)/shard_map/ppermute | solution.py:14
  284.5 5.0 %collective-permute-done.12 = bf16[512,384]{0,1:T(8,128)(2,1)} collective-permute-done((bf16[512,384]{0,1:T(8,128)(2,1)S(1)}, bf16[512,384]{0,1:T(8,128)(2,1)}, u32[]{:S(2)}, u32[]{:S(2)}) %collective-permute-start.12) | collective-permute-done | bytes 393248 | tf_op jit(solution)/shard_map/ppermute | solution.py:14
  289.5 7.7 %collective-permute-done.11 = bf16[512,384]{0,1:T(8,128)(2,1)} collective-permute-done((bf16[512,384]{0,1:T(8,128)(2,1)S(1)}, bf16[512,384]{0,1:T(8,128)(2,1)}, u32[]{:S(2)}, u32[]{:S(2)}) %collective-permute-start.11) | collective-permute-done | bytes 393248 | tf_op jit(solution)/shard_map/ppermute | solution.py:14
  297.2 1.3 broadcast.8
  298.6 2.5 constant_dynamic-update-slice_fusion.3
  301.0 0.5 collective-permute-start.13
  301.6 3.3 collective-permute-start.14
  304.9 10.3 %collective-permute-done.13 = bf16[512,384]{0,1:T(8,128)(2,1)} collective-permute-done((bf16[512,384]{0,1:T(8,128)(2,1)}, bf16[512,384]{0,1:T(8,128)(2,1)}, u32[]{:S(2)}, u32[]{:S(2)}) %collective-permute-start.13) | collective-permute-done | bytes 393248 | tf_op jit(solution)/shard_map/ppermute | solution.py:14
  315.1 1.1 copy.26
  316.2 1.8 constant_dynamic-update-slice_fusion.2
  318.0 3.1 collective-permute-done.14
  321.1 1.8 constant_dynamic-update-slice_fusion.1
  322.8 8.2 %collective-permute-done.15 = bf16[512,384]{0,1:T(8,128)(2,1)} collective-permute-done((bf16[512,384]{0,1:T(8,128)(2,1)}, bf16[512,384]{0,1:T(8,128)(2,1)}, u32[]{:S(2)}, u32[]{:S(2)}) %collective-permute-start.15) | collective-permute-done | bytes 393248 | tf_op jit(solution)/shard_map/ppermute | solution.py:14
  331.0 1.8 constant_dynamic-update-slice_fusion
  332.8 3.3 fusion.7
  336.1 2.3 copy.25
  (31 shorter events, 1.0 us)
Async XLA Ops:
  7.2 33.5 %copy-start = (bf16[512,2048]{1,0:T(8,128)(2,1)S(1)}, bf16[512,2048]{1,0:T(8,128)(2,1)}, u32[]{:S(2)}) copy-start(bf16[512,2048]{1,0:T(8,128)(2,1)} %param.8) | copy-start | bytes 6291460
  7.2 119.0 %reduce-scatter.2.cloned.1.call-start = ((), (), s32[]{:S(2)}) async-start(), calls=%async_computation.1 | async-start | bytes 2654208 | tf_op jit(solution)/shard_map/reduce_scatter | solution.py:68
  7.2 15.3 %collective-permute-start = (bf16[512,384]{1,0:T(8,128)(2,1)}, bf16[512,384]{1,0:T(8,128)(2,1)S(1)}, u32[]{:S(2)}, u32[]{:S(2)}) collective-permute-start(bf16[512,384]{1,0:T(8,128)(2,1)} %param.6), channel_id=1, source_target_pairs={{0,1},{1,2},{2,3},{3,0},{4,5},{5,6},{6,7},{7,4},{8,9},{9,10},{10,1... | collective-permute-start | bytes 1179656 | tf_op jit(solution)/shard_map/ppermute | solution.py:14
  10.3 19.5 %collective-permute-start.1 = (bf16[512,384]{1,0:T(8,128)(2,1)}, bf16[512,384]{1,0:T(8,128)(2,1)}, u32[]{:S(2)}, u32[]{:S(2)}) collective-permute-start(bf16[512,384]{1,0:T(8,128)(2,1)} %param.6), channel_id=1, source_target_pairs={{0,3},{1,0},{2,1},{3,2},{4,7},{5,4},{6,5},{7,6},{8,11},{9,8},{10,9... | collective-permute-start | bytes 1179656 | tf_op jit(solution)/shard_map/ppermute | solution.py:14
  22.5 16.1 %collective-permute-start.2 = (bf16[512,384]{1,0:T(8,128)(2,1)S(1)}, bf16[512,384]{1,0:T(8,128)(2,1)}, u32[]{:S(2)}, u32[]{:S(2)}) collective-permute-start(bf16[512,384]{1,0:T(8,128)(2,1)S(1)} %collective-permute-done), channel_id=1, source_target_pairs={{0,1},{1,2},{2,3},{3,0},{4,5},{5,6},{6,7},{7,4},{8,9},{9,10},{10,1... | collective-permute-start | bytes 1179656 | tf_op jit(solution)/shard_map/ppermute | solution.py:14
  43.1 2.3 copy-start.3
  43.1 16.1 %copy-start.6 = (s32[1,12]{1,0:T(1,128)S(1)}, s32[1,12]{1,0:T(1,128)}, u32[]{:S(2)}) copy-start(s32[1,12]{1,0:T(1,128)} %param.11) | copy-start | bytes 148
  45.4 13.8 %collective-permute-start.3 = (bf16[512,384]{0,1:T(8,128)(2,1)S(1)}, bf16[512,384]{0,1:T(8,128)(2,1)S(1)}, u32[]{:S(2)}, u32[]{:S(2)}) collective-permute-start(bf16[512,384]{0,1:T(8,128)(2,1)S(1)} %get-tuple-element.11), channel_id=1, source_target_pairs={{0,1},{1,2},{2,3},{3,0},{4,5},{5,6},{6,7},{7,4},{8,9},{9,10},{10,1... | collective-permute-start | bytes 1179656 | tf_op jit(solution)/shard_map/ppermute | solution.py:14
  45.4 19.8 %collective-permute-start.4 = (bf16[512,384]{0,1:T(8,128)(2,1)S(1)}, bf16[512,384]{0,1:T(8,128)(2,1)S(1)}, u32[]{:S(2)}, u32[]{:S(2)}) collective-permute-start(bf16[512,384]{0,1:T(8,128)(2,1)S(1)} %get-tuple-element.11), channel_id=1, source_target_pairs={{0,3},{1,0},{2,1},{3,2},{4,7},{5,4},{6,5},{7,6},{8,11},{9,8},{10,9... | collective-permute-start | bytes 1179656 | tf_op jit(solution)/shard_map/ppermute | solution.py:14
  59.2 13.6 %collective-permute-start.5 = (bf16[512,384]{0,1:T(8,128)(2,1)S(1)}, bf16[512,384]{0,1:T(8,128)(2,1)S(1)}, u32[]{:S(2)}, u32[]{:S(2)}) collective-permute-start(bf16[512,384]{0,1:T(8,128)(2,1)S(1)} %collective-permute-done.3), channel_id=1, source_target_pairs={{0,1},{1,2},{2,3},{3,0},{4,5},{5,6},{6,7},{7,4},{8,9},{9,10},{10,1... | collective-permute-start | bytes 1179656 | tf_op jit(solution)/shard_map/ppermute | solution.py:14
  85.3 72.5 %all-gather.3.cloned.1.call-start = ((), (), s32[]{:S(2)}) async-start(), calls=%async_computation.2 | async-start | bytes 2654208 | tf_op jit(solution)/shard_map/all_gather | solution.py:71
  128.1 116.9 %all-gather.5.cloned.1.call-start = ((), (), s32[]{:S(2)}) async-start(), calls=%async_computation.3 | async-start | bytes 2654208 | tf_op jit(solution)/shard_map/all_gather | solution.py:84
  165.0 1.4 copy-start.2
  166.6 10.8 %collective-permute-start.6 = (bf16[384,384]{0,1:T(8,128)(2,1)S(1)}, bf16[384,384]{0,1:T(8,128)(2,1)S(1)}, u32[]{:S(2)}, u32[]{:S(2)}) collective-permute-start(bf16[384,384]{0,1:T(8,128)(2,1)S(1)} %get-tuple-element.14), channel_id=1, source_target_pairs={{0,3},{1,0},{2,1},{3,2},{4,7},{5,4},{6,5},{7,6},{8,11},{9,8},{10,9... | collective-permute-start | bytes 884744 | tf_op jit(solution)/shard_map/ppermute | solution.py:14
  169.9 14.7 %collective-permute-start.8 = (bf16[384,384]{0,1:T(8,128)(2,1)S(1)}, bf16[384,384]{0,1:T(8,128)(2,1)S(1)}, u32[]{:S(2)}, u32[]{:S(2)}) collective-permute-start(bf16[384,384]{0,1:T(8,128)(2,1)S(1)} %get-tuple-element.15), channel_id=1, source_target_pairs={{0,1},{1,2},{2,3},{3,0},{4,5},{5,6},{6,7},{7,4},{8,9},{9,10},{10,1... | collective-permute-start | bytes 884744 | tf_op jit(solution)/shard_map/ppermute | solution.py:14
  178.5 11.8 %collective-permute-start.7 = (bf16[384,384]{0,1:T(8,128)(2,1)S(1)}, bf16[384,384]{0,1:T(8,128)(2,1)S(1)}, u32[]{:S(2)}, u32[]{:S(2)}) collective-permute-start(bf16[384,384]{0,1:T(8,128)(2,1)S(1)} %fusion.11), channel_id=1, source_target_pairs={{0,3},{1,0},{2,1},{3,2},{4,7},{5,4},{6,5},{7,6},{8,11},{9,8},{10,9... | collective-permute-start | bytes 884744 | tf_op jit(solution)/shard_map/ppermute | solution.py:14
  191.4 0.9 collective-permute-start.9
  192.3 0.7 copy-start.5
  267.0 13.2 %copy-start.1 = (f32[384,2048]{1,0:T(8,128)}, f32[384,2048]{1,0:T(8,128)S(1)}, u32[]{:S(2)}) copy-start(f32[384,2048]{1,0:T(8,128)S(1)} %fusion.27) | copy-start | bytes 9437188
  267.1 12.9 %collective-permute-start.10 = (bf16[512,384]{0,1:T(8,128)(2,1)S(1)}, bf16[512,384]{0,1:T(8,128)(2,1)S(1)}, u32[]{:S(2)}, u32[]{:S(2)}) collective-permute-start(bf16[512,384]{0,1:T(8,128)(2,1)S(1)} %get-tuple-element.12), channel_id=1, source_target_pairs={{0,3},{1,0},{2,1},{3,2},{4,7},{5,4},{6,5},{7,6},{8,11},{9,8},{10,9... | collective-permute-start | bytes 1179656 | tf_op jit(solution)/shard_map/ppermute | solution.py:14
  270.5 19.0 %collective-permute-start.12 = (bf16[512,384]{0,1:T(8,128)(2,1)S(1)}, bf16[512,384]{0,1:T(8,128)(2,1)}, u32[]{:S(2)}, u32[]{:S(2)}) collective-permute-start(bf16[512,384]{0,1:T(8,128)(2,1)S(1)} %get-tuple-element.13), channel_id=1, source_target_pairs={{0,1},{1,2},{2,3},{3,0},{4,5},{5,6},{6,7},{7,4},{8,9},{9,10},{10,1... | collective-permute-start | bytes 1179656 | tf_op jit(solution)/shard_map/ppermute | solution.py:14
  280.1 17.1 %collective-permute-start.11 = (bf16[512,384]{0,1:T(8,128)(2,1)S(1)}, bf16[512,384]{0,1:T(8,128)(2,1)}, u32[]{:S(2)}, u32[]{:S(2)}) collective-permute-start(bf16[512,384]{0,1:T(8,128)(2,1)S(1)} %fusion.8), channel_id=1, source_target_pairs={{0,3},{1,0},{2,1},{3,2},{4,7},{5,4},{6,5},{7,6},{8,11},{9,8},{10,9... | collective-permute-start | bytes 1179656 | tf_op jit(solution)/shard_map/ppermute | solution.py:14
  301.0 14.1 %collective-permute-start.13 = (bf16[512,384]{0,1:T(8,128)(2,1)}, bf16[512,384]{0,1:T(8,128)(2,1)}, u32[]{:S(2)}, u32[]{:S(2)}) collective-permute-start(bf16[512,384]{0,1:T(8,128)(2,1)} %get-tuple-element.7), channel_id=1, source_target_pairs={{0,1},{1,2},{2,3},{3,0},{4,5},{5,6},{6,7},{7,4},{8,9},{9,10},{10,1... | collective-permute-start | bytes 1179656 | tf_op jit(solution)/shard_map/ppermute | solution.py:14
  301.6 19.5 %collective-permute-start.14 = (bf16[512,384]{0,1:T(8,128)(2,1)}, bf16[512,384]{0,1:T(8,128)(2,1)}, u32[]{:S(2)}, u32[]{:S(2)}) collective-permute-start(bf16[512,384]{0,1:T(8,128)(2,1)} %get-tuple-element.7), channel_id=1, source_target_pairs={{0,3},{1,0},{2,1},{3,2},{4,7},{5,4},{6,5},{7,6},{8,11},{9,8},{10,9... | collective-permute-start | bytes 1179656 | tf_op jit(solution)/shard_map/ppermute | solution.py:14
  315.1 15.9 %collective-permute-start.15 = (bf16[512,384]{0,1:T(8,128)(2,1)}, bf16[512,384]{0,1:T(8,128)(2,1)}, u32[]{:S(2)}, u32[]{:S(2)}) collective-permute-start(bf16[512,384]{0,1:T(8,128)(2,1)} %collective-permute-done.13), channel_id=1, source_target_pairs={{0,1},{1,2},{2,3},{3,0},{4,5},{5,6},{6,7},{7,4},{8,9},{9,10},{10,1... | collective-permute-start | bytes 1179656 | tf_op jit(solution)/shard_map/ppermute | solution.py:14
  315.1 17.7 %copy-start.4 = (f32[384,512]{1,0:T(8,128)S(1)}, f32[384,512]{1,0:T(8,128)}, u32[]{:S(2)}) copy-start(f32[384,512]{1,0:T(8,128)} %copy-done.3) | copy-start | bytes 2359300
Sparse Core Ops, SparseCore 0:
  85.4 40.7 reduce-scatter.1
  128.8 28.9 all-gather.2
  193.2 51.8 all-gather.4

commit v2 on v0

v2 whole, which is shorter than its diff:
```python
import functools

import jax
import jax.numpy as jnp
from jax import lax
from jax.experimental import pallas as pl
from jax.experimental.pallas import tpu as pltpu
from jax.sharding import PartitionSpec as P

BLK = 128
F32 = jnp.float32
BF16 = jnp.bfloat16
VMEM = pl.BlockSpec(memory_space=pltpu.VMEM)
ANY = pl.BlockSpec(memory_space=pl.ANY)
VMEM_LIMIT = 56 * 1024 * 1024


def dot(a, b, contract=((1,), (0,))):
    return lax.dot_general(a, b, (contract, ((), ())), preferred_element_type=F32)


def kernel_call(body, out_shape, grid, n_scalars, in_specs, out_specs, scratch, flops, nbytes):
    return pl.pallas_call(
        body,
        out_shape=out_shape,
        grid_spec=pltpu.PrefetchScalarGridSpec(
            num_scalar_prefetch=n_scalars,
            grid=grid,
            in_specs=in_specs,
            out_specs=out_specs,
            scratch_shapes=scratch,
        ),
        compiler_params=pltpu.CompilerParams(vmem_limit_bytes=VMEM_LIMIT),
        cost_estimate=pl.CostEstimate(flops=flops, bytes_accessed=nbytes, transcendentals=0),
    )


def whole(shape):
    return pl.BlockSpec(shape, lambda *_: (0,) * len(shape))


def shift(x, size, by):
    return lax.ppermute(x, "row", [(i, (i + by) % size) for i in range(size)])


def swap(x, size, by):
    return lax.ppermute(x, "front", [(i, i ^ by) for i in range(size)])


def gather_row(x, n):
    found = [(0, x)]
    up, down = x, x
    for step in range(1, n // 2 + 1):
        up = shift(up, n, 1)
        found.append((-step, up))
        if step < n - step:
            down = shift(down, n, -1)
            found.append((step, down))
    return found


def gather_front(x, n):
    found = {0: x, 1: swap(x, n, 1)}
    for d in range(2, n, 2):
        found[d] = swap(x, n, d)
    for d in range(2, n, 2):
        found[d + 1] = swap(found[d], n, 1)
    return [found[d] for d in range(n)]


def far_offsets(n):
    first = [-(n // 2)] + ([(n - 1) // 2] if n > 2 else [])
    later = [o for o in range(-(n // 2) + 1, (n - 1) // 2) if o]
    return first, later


def scatter_row(first, later, own, n):
    total = own
    for sign, far in ((-1, n // 2), (1, (n - 1) // 2)):
        running = None
        for step in range(far, 0, -1):
            if running is None:
                running = first[sign * step]
            else:
                running = (running.astype(F32) + later[sign * step]).astype(BF16)
            running = shift(running, n, sign)
        if running is not None:
            total = total + running.astype(F32)
    return total


def accumulate(at_ref, a_ref, offsets, x_refs, n_row, contract=((1,), (0,))):
    depth = a_ref.shape[1] // n_row
    total = None
    for offset, x_ref in zip(offsets, x_refs):
        owner = lax.rem(at_ref[0] + (offset + n_row), n_row)
        columns = pl.ds(pl.multiple_of(owner * depth, depth), depth)
        part = dot(a_ref[:, columns], x_ref[...], contract)
        total = part if total is None else total + part
    return total


def pivot_forward(at, pivot, found, n_row):
    rows, width = pivot.shape[0], found[0][1].shape[1]
    offsets = [o for o, _ in found]

    def body(at_ref, a_ref, *refs):
        total = accumulate(at_ref, a_ref, offsets, refs[: len(offsets)], n_row)
        refs[-2][...] = total
        refs[-1][...] = total.astype(BF16)

    return kernel_call(
        body,
        [jax.ShapeDtypeStruct((rows, width), F32), jax.ShapeDtypeStruct((rows, width), BF16)],
        (1,),
        1,
        [whole(pivot.shape)] + [whole(x.shape) for _, x in found],
        [whole((rows, width))] * 2,
        [],
        2 * pivot.size * width,
        2 * pivot.size,
    )(at, pivot, *[x for _, x in found])


def pivot_backward(at, pivot, found, inner, n_row):
    rows, width = inner.shape
    offsets = [o for o, _ in found]

    def body(at_ref, a_ref, inner_ref, *refs):
        total = accumulate(at_ref, a_ref, offsets, refs[: len(offsets)], n_row, ((1,), (1,)))
        refs[-1][...] = inner_ref[...] - total

    return kernel_call(
        body,
        jax.ShapeDtypeStruct((rows, width), F32),
        (1,),
        1,
        [whole(pivot.shape), whole(inner.shape)] + [whole(x.shape) for _, x in found],
        whole((rows, width)),
        [],
        2 * pivot.size * width,
        2 * pivot.size,
    )(at, pivot, inner, *[x for _, x in found])


def border_forward(at, local_index, coupling, found, n_row, n_front, span_rows):
    rows, depth = coupling.shape
    width = found[0][1].shape[1]
    offsets = [o for o, _ in found]
    blocks = rows // BLK
    per_step = next(k for k in (4, 3, 2, 1) if blocks % k == 0)
    piece_blocks = span_rows // n_front // BLK

    def body(at_ref, index_ref, a_ref, *refs):
        send_ref, keep_ref = refs[-2], refs[-1]
        step = pl.program_id(0)

        @pl.when(step == 0)
        def _():
            send_ref[...] = jnp.zeros_like(send_ref)
            keep_ref[...] = jnp.zeros_like(keep_ref)

        total = accumulate(at_ref, a_ref, offsets, refs[: len(offsets)], n_row).astype(BF16)
        for j in range(per_step):
            target = index_ref[step * per_step + j]
            away = lax.bitwise_xor(lax.div(target, piece_blocks), at_ref[1])
            slot = lax.shift_right_logical(away, 1) * piece_blocks + lax.rem(target, piece_blocks)
            place = pl.ds(pl.multiple_of(slot * BLK, BLK), BLK)
            block = total[j * BLK : (j + 1) * BLK]

            @pl.when(lax.rem(away, 2) == 1)
            def _():
                send_ref[place, :] = block

            @pl.when(lax.rem(away, 2) == 0)
            def _():
                keep_ref[place, :] = block

    half = jax.ShapeDtypeStruct((span_rows // 2, width), BF16)
    return kernel_call(
        body,
        [half, half],
        (blocks // per_step,),
        2,
        [pl.BlockSpec((per_step * BLK, depth), lambda i, *_: (i, 0))] + [whole(x.shape) for _, x in found],
        [whole(half.shape)] * 2,
        [],
        2 * coupling.size * width,
        2 * coupling.size,
    )(at, local_index, coupling, *[x for _, x in found])


def root_products(at, inverse, pieces, offsets, kinds, n_row, n_front):
    span_rows = inverse.shape[1]
    rows = inverse.shape[0] // n_row
    width = pieces[0].shape[1]
    piece_rows = pieces[0].shape[0]
    count = len(offsets)
    owners = (at[0] + jnp.array([o + n_row for o in offsets], jnp.int32)) % n_row

    def body(at_ref, owner_ref, a_ref, *refs):
        piece_refs, out_refs = refs[:n_front], refs[n_front : n_front + count]
        x_ref, sems = refs[-2], refs[-1]
        step = pl.program_id(0)

        @pl.when(step == 0)
        def _():
            copies = []
            for d in range(n_front):
                start = lax.bitwise_xor(at_ref[1], d) * piece_rows
                place = pl.ds(pl.multiple_of(start, piece_rows), piece_rows)
                copies.append(pltpu.make_async_copy(piece_refs[d], x_ref.at[place], sems.at[d]))
            for copy in copies:
                copy.start()
            for copy in copies:
                copy.wait()

        total = dot(a_ref[...], x_ref[...])
        for i in range(count):

            @pl.when(step == i)
            def _():
                out_refs[i][...] = total.astype(out_refs[i].dtype)

    return kernel_call(
        body,
        [jax.ShapeDtypeStruct((rows, width), kind) for kind in kinds],
        (count,),
        2,
        [pl.BlockSpec((rows, span_rows), lambda i, at_ref, owner_ref: (owner_ref[i], 0))] + [ANY] * n_front,
        [whole((rows, width))] * count,
        [pltpu.VMEM((span_rows, width), BF16), pltpu.SemaphoreType.DMA((n_front,))],
        2 * rows * span_rows * width * count,
        2 * rows * span_rows * count,
    )(at, owners, inverse, *pieces)


def border_backward(at, local_index, coupling, pieces, offsets, kinds, n_row, n_front):
    rows, depth = coupling.shape
    width = pieces[0].shape[1]
    piece_rows = pieces[0].shape[0]
    quarter = piece_rows // n_row
    span_rows = piece_rows * n_front
    columns = depth // n_row
    blocks = rows // BLK
    count = len(offsets)
    owners = (at[0] + jnp.array([o + n_row for o in offsets], jnp.int32)) % n_row

    def body(at_ref, index_ref, owner_ref, a_ref, *refs):
        piece_refs, out_refs = refs[:n_front], refs[n_front : n_front + count]
        span_ref, picked_ref, sems = refs[-3], refs[-2], refs[-1]
        step = pl.program_id(0)

        @pl.when(step == 0)
        def _():
            copies = []
            for d in range(n_front):
                there = lax.bitwise_xor(at_ref[1], d)
                chip, core = lax.shift_right_logical(there, 1), lax.rem(there, 2)
                for k in range(n_row):
                    start = core * (span_rows // 2) + lax.bitwise_xor(chip, k) * piece_rows + k * quarter
                    place = pl.ds(pl.multiple_of(start, quarter), quarter)
                    copies.append(
                        pltpu.make_async_copy(
                            piece_refs[d].at[pl.ds(k * quarter, quarter)],
                            span_ref.at[place],
                            sems.at[d * n_row + k],
                        )
                    )
            for copy in copies:
                copy.start()
            for copy in copies:
                copy.wait()
            for j in range(blocks):
                source = pl.ds(pl.multiple_of(index_ref[j] * BLK, BLK), BLK)
                picked_ref[pl.ds(j * BLK, BLK), :] = span_ref[source, :]

        total = dot(picked_ref[...], a_ref[...], ((0,), (0,)))
        for i in range(count):

            @pl.when(step == i)
            def _():
                out_refs[i][...] = total.astype(out_refs[i].dtype)

    return kernel_call(
        body,
        [jax.ShapeDtypeStruct((width, columns), kind) for kind in kinds],
        (count,),
        3,
        [pl.BlockSpec((rows, columns), lambda i, at_ref, index_ref, owner_ref: (0, owner_ref[i]))]
        + [ANY] * n_front,
        [whole((width, columns))] * count,
        [
            pltpu.VMEM((span_rows, width), BF16),
            pltpu.VMEM((rows, width), BF16),
            pltpu.SemaphoreType.DMA((n_front * n_row,)),
        ],
        2 * rows * columns * width * count,
        2 * rows * columns * count,
    )(at, local_index, owners, coupling, *pieces)


def solve(n_front, n_row, rhs_front, rhs_root, pivot_inverse, border_coupling, root_inverse, border_map):
    row_at = lax.axis_index("row").astype(jnp.int32)
    front_at = lax.axis_index("front").astype(jnp.int32)
    at = jnp.stack([row_at, front_at])
    span_rows = root_inverse.shape[1]
    piece_rows = span_rows // n_front
    local_index = border_map[0] - row_at * (span_rows // BLK)
    first_at, later_at = far_offsets(n_row)

    inner, inner_half = pivot_forward(at, pivot_inverse, gather_row(rhs_front, n_row), n_row)
    send, keep = border_forward(
        at, local_index, border_coupling, gather_row(inner_half, n_row), n_row, n_front, span_rows
    )
    came = swap(send, n_front, 1)

    def pair(i):
        rows = slice(i * piece_rows, (i + 1) * piece_rows)
        return keep[rows].astype(F32) + came[rows].astype(F32)

    shares = pair(0)
    for d in range(2, n_front, 2):
        shares = shares + swap(pair(d // 2).astype(BF16), n_front, d).astype(F32)
    own_rhs = lax.dynamic_slice_in_dim(rhs_root, front_at * piece_rows, piece_rows, 0)
    pieces = gather_front((own_rhs - shares).astype(BF16), n_front)

    def root(offsets, kind):
        outs = root_products(at, root_inverse, pieces, offsets, [kind] * len(offsets), n_row, n_front)
        return dict(zip(offsets, outs))

    first = root(first_at, BF16)
    rest = root(later_at + [0], F32)
    root_solution = scatter_row(first, rest, rest[0], n_row)
    root_half = root_solution.astype(BF16)
    quarter = root_half.shape[0] // n_row
    moved = []
    for k in range(n_row):
        perm = [
            ((chip * 2 + core) * n_row + row, ((row ^ k) * 2 + core) * n_row + chip)
            for chip in range(n_row)
            for core in range(2)
            for row in range(n_row)
        ]
        moved.append(lax.ppermute(root_half[k * quarter : (k + 1) * quarter], ("front", "row"), perm))
    spans = gather_front(jnp.concatenate(moved, axis=0), n_front)

    def border(offsets, kind):
        outs = border_backward(
            at, local_index, border_coupling, spans, offsets, [kind] * len(offsets), n_row, n_front
        )
        return dict(zip(offsets, outs))

    first = border(first_at, BF16)
    rest = border(later_at + [0], F32)
    pulled = scatter_row(first, rest, rest[0], n_row).astype(BF16)
    front_solution = pivot_backward(at, pivot_inverse, gather_row(pulled, n_row), inner, n_row)
    return front_solution, root_solution


def solve_plain(n_front, n_row, rhs_front, rhs_root, pivot_inverse, border_coupling, root_inverse, border_map):
    row_at = lax.axis_index("row")
    front_at = lax.axis_index("front")
    width = rhs_front.shape[1]
    inner = dot(pivot_inverse, lax.all_gather(rhs_front, "row", axis=0, tiled=True))
    contrib = dot(border_coupling, lax.all_gather(inner.astype(BF16), "row", axis=0, tiled=True))
    block_local = border_map.shape[1]
    span_rows = root_inverse.shape[1]
    span_blocks = span_rows // BLK
    local_index = border_map[0] - row_at * span_blocks
    select = (local_index[None, :] == jnp.arange(span_blocks, dtype=jnp.int32)[:, None]).astype(F32)
    dense = jnp.einsum(
        "kj,jcn->kcn", select, contrib.reshape(block_local, BLK, width), precision=lax.Precision.HIGHEST
    ).reshape(span_rows, width)
    shares = lax.psum_scatter(dense, "front", scatter_dimension=0, tiled=True)
    own_rhs = lax.dynamic_slice_in_dim(rhs_root, front_at * shares.shape[0], shares.shape[0], 0)
    schur_rhs = lax.all_gather((own_rhs - shares).astype(BF16), "front", axis=0, tiled=True)
    root_solution = lax.psum_scatter(dot(root_inverse, schur_rhs), "row", scatter_dimension=0, tiled=True)
    gathered = lax.all_gather(root_solution.astype(BF16), ("front", "row"), axis=0, tiled=True)
    ranged = lax.dynamic_slice_in_dim(gathered, row_at * span_rows, span_rows, 0)
    picked = jnp.take(ranged.reshape(span_blocks, BLK, width), local_index, axis=0)
    picked = picked.reshape(block_local * BLK, width)
    pulled = lax.psum_scatter(
        dot(border_coupling, picked, ((0,), (0,))), "row", scatter_dimension=0, tiled=True
    ).astype(BF16)
    correction = dot(pivot_inverse, lax.all_gather(pulled, "row", axis=0, tiled=True))
    return inner - correction, root_solution


def solution(mesh):
    in_specs = (
        P(("front", "row"), None),
        P("row", None),
        P(("front", "row"), None),
        P(("front", "row"), None),
        P("front", "row"),
        P("front", "row"),
    )
    out_specs = (P(("front", "row"), None), P(("front", "row"), None))
    n_front, n_row = mesh.shape["front"], mesh.shape["row"]

    def per_device(*arrays):
        root_inverse, width = arrays[4], arrays[0].shape[1]
        fits = (
            n_front == 2 * n_row
            and n_front & (n_front - 1) == 0
            and n_row > 2
            and root_inverse.shape[1] % (n_front * BLK) == 0
            and root_inverse.shape[0] == n_row * (root_inverse.shape[1] // n_front)
            and root_inverse.shape[1] % (n_front * n_row * 16) == 0
            and arrays[2].shape[1] % (n_row * BLK) == 0
            and width % BLK == 0
        )
        return (solve if fits else solve_plain)(n_front, n_row, *arrays)

    return jax.shard_map(per_device, mesh=mesh, in_specs=in_specs, out_specs=out_specs, check_vma=False)
```

time: 466 us -> 258 us (0.55)
  waiting for transfers between devices: 390 us -> 160 us
  Pallas kernels: 0 us -> 48.3 us
  matrix products: 39.5 us -> 0 us
  starting transfers between devices: 0.51 us -> 35.2 us
  between operations: 14.2 us -> 0.97 us
  local copies, waits for them, and re-layouts: 14.8 us -> 4.06 us
    all_gather x5 -> x0, waiting for transfers between devices: 230 us -> none  [the longest x1 86.8 us: per_device(): gathered = lax.all_gather(root_half, ('front', 'row'), axis=0, tiled=True)]
    ppermute x0 -> x37, waiting for transfers between devices: none -> 160 us  [the longest x15 103 us: shift(): return lax.ppermute(x, 'row', [(i, (i + by) % size) for i in range(size)])]
    reduce_scatter x3 -> x0, waiting for transfers between devices: 160 us -> none  [the longest x1 58.5 us: per_device(): lax.psum_scatter(lax.dot_general(columns, picked, (((0,), (0,)), ((), ())...]
    pallas_call x0 -> x7, Pallas kernels: none -> 48.3 us  [the longest x2 15.9 us: root_products(): kernel_call(body, [jax.ShapeDtypeStruct((rows, width), kind) for kind in...]
    dot_general x7 -> x0, matrix products: 39.5 us -> none  [the longest x1 9.69 us: per_device(): jnp.dot(root_inverse, schur_rhs, preferred_element_type=jnp.float32)]
    ppermute x0 -> x37, starting transfers between devices: none -> 35.2 us  [the longest x15 17.1 us: shift(): return lax.ppermute(x, 'row', [(i, (i + by) % size) for i in range(size)])]
    dynamic_slice x2 -> x0, local copies, waits for them, and re-layouts: 7.47 us -> none  [per_device(): lax.dynamic_slice_in_dim(gathered, row_at * span_rows, span_rows, 0)]
    dot_general x2 -> x0, local copies, waits for them, and re-layouts: 6.03 us -> none  [the longest x1 3.06 us: per_device(): jnp.dot(columns, lax.all_gather(inner_half, 'row', axis=0, tiled=True), p...]
  transfers between devices with their start and end apart: 8 -> 37, of which waited for: 8 -> 26; matrix products, arithmetic and copies ran while one was open for 0% -> 2% of each run, Pallas kernels for 0% -> 6%
where the time goes in v2:
time: 258 us; the launch traced here: 256 us
  waiting for transfers between devices  160 us (62%)
  Pallas kernels  48.3 us (19%)
  starting transfers between devices  35.2 us (14%)
  other arithmetic  7.87 us (3%)
  local copies, waits for them, and re-layouts  4.06 us (2%)
    ppermute x15, waiting for transfers between devices, shift(): return lax.ppermute(x, 'row', [(i, (i + by) % size) for i in range(size)])  103 us
    ppermute x18, waiting for transfers between devices, swap(): return lax.ppermute(x, 'front', [(i, i ^ by) for i in range(size)])  41.4 us
    ppermute x15, starting transfers between devices, shift(): return lax.ppermute(x, 'row', [(i, (i + by) % size) for i in range(size)])  17.1 us
    pallas_call x2, Pallas kernels, root_products(): kernel_call(body, [jax.ShapeDtypeStruct((rows, width), kind) for kind in...  15.9 us
    ppermute x4, waiting for transfers between devices, solve(): lax.ppermute(root_half[k * quarter:(k + 1) * quarter], ('front', 'row'),...  15.6 us
    pallas_call x2, Pallas kernels, border_backward(): kernel_call(body, [jax.ShapeDtypeStruct((width, columns), kind) for kind...  13.9 us
    ppermute x18, starting transfers between devices, swap(): return lax.ppermute(x, 'front', [(i, i ^ by) for i in range(size)])  11.7 us
    pallas_call x1, Pallas kernels, border_forward(): kernel_call(body, [half, half], (blocks // per_step,), 2, [pl.BlockSpec((...  8.58 us
  transfers between devices with their start and end apart: 37, of which 26 were waited for; matrix products, arithmetic and copies ran while one was open for 2% of the time, Pallas kernels for 6%

profile of v2, /device:TPU:0, one launch (start us, length us, event | category | flops | bytes accessed | tf_op | source)
XLA Modules:
  0.0 256.0 jit_solution(10118648994466023201)
XLA Ops:
  0.6 3.1 %collective-permute-start = (bf16[512,384]{1,0:T(8,128)(2,1)}, bf16[512,384]{1,0:T(8,128)(2,1)S(1)}, u32[]{:S(2)}, u32[]{:S(2)}) collective-permute-start(bf16[512,384]{1,0:T(8,128)(2,1)} %refs_0_.1), channel_id=1, source_target_pairs={{0,1},{1,2},{2,3},{3,0},{4,5},{5,6},{6,7},{7,4},{8,9},{9,10},{10,1... | collective-permute-start | bytes 1179656 | tf_op jit(solution)/shard_map/ppermute | solution.py:43
  3.7 2.1 collective-permute-start.1
  5.8 10.1 %collective-permute-done.refs_1_ = bf16[512,384]{1,0:T(8,128)(2,1)S(1)} collective-permute-done((bf16[512,384]{1,0:T(8,128)(2,1)}, bf16[512,384]{1,0:T(8,128)(2,1)S(1)}, u32[]{:S(2)}, u32[]{:S(2)}) %collective-permute-start) | collective-permute-done | bytes 393248 | tf_op jit(solution)/shard_map/ppermute | solution.py:43
  15.9 0.6 pad_add_fusion.at_ref
  16.6 6.6 %collective-permute-done.1.refs_2_ = bf16[512,384]{1,0:T(8,128)(2,1)S(1)} collective-permute-done((bf16[512,384]{1,0:T(8,128)(2,1)}, bf16[512,384]{1,0:T(8,128)(2,1)S(1)}, u32[]{:S(2)}, u32[]{:S(2)}) %collective-permute-start.1) | collective-permute-done | bytes 393248 | tf_op jit(solution)/shard_map/ppermute | solution.py:43
  23.1 8.8 %collective-permute-done.2.refs_3_ = bf16[512,384]{1,0:T(8,128)(2,1)S(1)} collective-permute-done((bf16[512,384]{1,0:T(8,128)(2,1)S(1)}, bf16[512,384]{1,0:T(8,128)(2,1)S(1)}, u32[]{:S(2)}, u32[]{:S(2)}) %collective-permute-start.2) | collective-permute-done | bytes 393248 | tf_op jit(solution)/shard_map/ppermute | solution.py:43
  32.0 0.7 copy-done.21
  32.7 4.9 %shard_map.113 = (f32[512,384]{1,0:T(8,128)}, bf16[512,384]{1,0:T(8,128)(2,1)}) custom-call(s32[2]{0:T(128)} %pad_add_fusion.at_ref, bf16[512,2048]{1,0:T(8,128)(2,1)} %a_ref.13, bf16[512,384]{1,0:T(8,128)(2,1)} %refs_0_.1, bf16[512,384]{1,0:T(8,128)(2,1)} %copy-done.19, bf16[512,384]{1,0:T(8,128)(2,1)} %copy-done.20, bf16[512,384]{1,0:T(8,128)(2,1)} %copy-done.21), custom_call_target="tpu_custom_call" | custom-call | flops 805306368 | bytes 2097152 | tf_op jit(solution)/shard_map/pallas_call | solution.py:112
  37.7 3.8 %collective-permute-start.4 = (bf16[512,384]{1,0:T(8,128)(2,1)}, bf16[512,384]{1,0:T(8,128)(2,1)S(1)}, u32[]{:S(2)}, u32[]{:S(2)}) collective-permute-start(bf16[512,384]{1,0:T(8,128)(2,1)} %get-tuple-element.15.refs_0_), channel_id=1, source_target_pairs={{0,3},{1,0},{2,1},{3,2},{4,7},{5,4},{6,5},{7,6},{8,11},{9,8},{10,9... | collective-permute-start | bytes 1179656 | tf_op jit(solution)/shard_map/ppermute | solution.py:43
  41.5 10.2 %collective-permute-done.3.refs_1_ = bf16[512,384]{1,0:T(8,128)(2,1)S(1)} collective-permute-done((bf16[512,384]{1,0:T(8,128)(2,1)}, bf16[512,384]{1,0:T(8,128)(2,1)S(1)}, u32[]{:S(2)}, u32[]{:S(2)}) %collective-permute-start.3) | collective-permute-done | bytes 393248 | tf_op jit(solution)/shard_map/ppermute | solution.py:43
  51.7 0.6 subtract_bitcast_fusion.index_ref
  52.3 5.4 %collective-permute-done.4.refs_2_ = bf16[512,384]{1,0:T(8,128)(2,1)S(1)} collective-permute-done((bf16[512,384]{1,0:T(8,128)(2,1)}, bf16[512,384]{1,0:T(8,128)(2,1)S(1)}, u32[]{:S(2)}, u32[]{:S(2)}) %collective-permute-start.4) | collective-permute-done | bytes 393248 | tf_op jit(solution)/shard_map/ppermute | solution.py:43
  57.7 7.6 %collective-permute-done.5.refs_3_ = bf16[512,384]{1,0:T(8,128)(2,1)S(1)} collective-permute-done((bf16[512,384]{1,0:T(8,128)(2,1)S(1)}, bf16[512,384]{1,0:T(8,128)(2,1)S(1)}, u32[]{:S(2)}, u32[]{:S(2)}) %collective-permute-start.5) | collective-permute-done | bytes 393248 | tf_op jit(solution)/shard_map/ppermute | solution.py:43
  65.4 0.8 copy-done.29
  66.1 8.6 %shard_map.114 = (bf16[1536,384]{1,0:T(8,128)(2,1)}, bf16[1536,384]{1,0:T(8,128)(2,1)}) custom-call(s32[2]{0:T(128)} %pad_add_fusion.at_ref, s32[12]{0:T(128)} %subtract_bitcast_fusion.index_ref, bf16[1536,2048]{1,0:T(8,128)(2,1)} %a_ref.12, bf16[512,384]{1,0:T(8,128)(2,1)} %get-tuple-element.15.refs_0_, bf16[512,384]{1,0:T(8,128)(2,1)} %copy-done.27, ...), custom_call_target="tpu_custom_call" | custom-call | flops 2415919104 | bytes 6291456 | tf_op jit(solution)/shard_map/pallas_call | solution.py:180
  74.7 3.1 %collective-permute-done.6 = bf16[1536,384]{1,0:T(8,128)(2,1)S(1)} collective-permute-done((bf16[1536,384]{1,0:T(8,128)(2,1)}, bf16[1536,384]{1,0:T(8,128)(2,1)S(1)}, u32[]{:S(2)}, u32[]{:S(2)}) %collective-permute-start.6) | collective-permute-done | bytes 1179680 | tf_op jit(solution)/shard_map/ppermute | solution.py:47
  77.8 1.4 add_convert_fusion.5
  79.1 1.6 collective-permute-start.7
  80.7 1.5 collective-permute-start.9
  82.2 0.5 collective-permute-start.8
  82.7 6.4 %collective-permute-done.7 = bf16[384,384]{1,0:T(8,128)(2,1)S(1)} collective-permute-done((bf16[384,384]{1,0:T(8,128)(2,1)S(1)}, bf16[384,384]{1,0:T(8,128)(2,1)S(1)}, u32[]{:S(2)}, u32[]{:S(2)}) %collective-permute-start.7) | collective-permute-done | bytes 294944 | tf_op jit(solution)/shard_map/ppermute | solution.py:47
  89.1 6.6 %collective-permute-done.9 = bf16[384,384]{1,0:T(8,128)(2,1)S(1)} collective-permute-done((bf16[384,384]{1,0:T(8,128)(2,1)S(1)}, bf16[384,384]{1,0:T(8,128)(2,1)S(1)}, u32[]{:S(2)}, u32[]{:S(2)}) %collective-permute-start.9) | collective-permute-done | bytes 294944 | tf_op jit(solution)/shard_map/ppermute | solution.py:47
  95.6 1.4 collective-permute-done.8
  97.0 1.3 subtract_convert_fusion.refs_0_
  98.4 1.5 collective-permute-start.15
  99.8 1.5 collective-permute-start.13
  101.4 0.5 collective-permute-start.11
  101.9 7.4 %collective-permute-done.15.refs_6_ = bf16[384,384]{1,0:T(8,128)(2,1)S(1)} collective-permute-done((bf16[384,384]{1,0:T(8,128)(2,1)S(1)}, bf16[384,384]{1,0:T(8,128)(2,1)S(1)}, u32[]{:S(2)}, u32[]{:S(2)}) %collective-permute-start.15) | collective-permute-done | bytes 294944 | tf_op jit(solution)/shard_map/ppermute | solution.py:47
  109.3 3.2 %collective-permute-done.13.refs_4_ = bf16[384,384]{1,0:T(8,128)(2,1)S(1)} collective-permute-done((bf16[384,384]{1,0:T(8,128)(2,1)S(1)}, bf16[384,384]{1,0:T(8,128)(2,1)S(1)}, u32[]{:S(2)}, u32[]{:S(2)}) %collective-permute-start.13) | collective-permute-done | bytes 294944 | tf_op jit(solution)/shard_map/ppermute | solution.py:47
  112.5 0.5 collective-permute-start.12
  113.0 0.6 and_select_fusion
  113.5 0.5 collective-permute-done.14.refs_5_
  114.0 0.4 collective-permute-done.12.refs_3_
  115.2 7.9 %shard_map.116 = (bf16[384,384]{1,0:T(8,128)(2,1)}, bf16[384,384]{1,0:T(8,128)(2,1)}) custom-call(s32[2]{0:T(128)} %pad_add_fusion.at_ref, s32[2]{0:T(128)} %get-tuple-element.35.owner_ref, bf16[1536,3072]{1,0:T(8,128)(2,1)} %a_ref.10, bf16[384,384]{1,0:T(8,128)(2,1)} %copy-done, bf16[384,384]{1,0:T(8,128)(2,1)} %copy-done.8, bf16[384,384]{1,0:T(8,128)(2,1)} %copy-done.6, ...), custom_call_target="tpu_custom_call" | custom-call | flops 1811939328 | bytes 4718592 | tf_op jit(solution)/shard_map/pallas_call | solution.py:225
  123.1 2.0 collective-permute-start.19
  125.1 8.1 %shard_map.115 = (f32[384,384]{1,0:T(8,128)}, f32[384,384]{1,0:T(8,128)}) custom-call(s32[2]{0:T(128)} %pad_add_fusion.at_ref, s32[2]{0:T(128)} %get-tuple-element.36.owner_ref, bf16[1536,3072]{1,0:T(8,128)(2,1)} %a_ref.10, bf16[384,384]{1,0:T(8,128)(2,1)} %copy-done, bf16[384,384]{1,0:T(8,128)(2,1)} %copy-done.8, bf16[384,384]{1,0:T(8,128)(2,1)} %copy-done.6, ...), custom_call_target="tpu_custom_call" | custom-call | flops 1811939328 | bytes 4718592 | tf_op jit(solution)/shard_map/pallas_call | solution.py:225
  133.2 5.5 %collective-permute-done.17 = bf16[384,384]{1,0:T(8,128)(2,1)S(1)} collective-permute-done((bf16[384,384]{1,0:T(8,128)(2,1)}, bf16[384,384]{1,0:T(8,128)(2,1)S(1)}, u32[]{:S(2)}, u32[]{:S(2)}) %collective-permute-start.17) | collective-permute-done | bytes 294944 | tf_op jit(solution)/shard_map/ppermute | solution.py:43
  138.7 1.1 add_convert_fusion.2
  139.9 8.2 %collective-permute-done.18 = bf16[384,384]{1,0:T(8,128)(2,1)S(1)} collective-permute-done((bf16[384,384]{1,0:T(8,128)(2,1)S(1)}, bf16[384,384]{1,0:T(8,128)(2,1)S(1)}, u32[]{:S(2)}, u32[]{:S(2)}) %collective-permute-start.18) | collective-permute-done | bytes 294944 | tf_op jit(solution)/shard_map/ppermute | solution.py:43
  148.1 0.9 fusion.2
  149.0 0.7 collective-permute-start.20
  149.7 5.7 %collective-permute-start.23 = (bf16[96,384]{1,0:T(8,128)(2,1)S(1)}, bf16[96,384]{1,0:T(8,128)(2,1)S(1)}, u32[]{:S(2)}, u32[]{:S(2)}) collective-permute-start(bf16[96,384]{1,0:T(8,128)(2,1)S(1)} %get-tuple-element.31), channel_id=1, source_target_pairs={{0,24},{1,16},{2,8},{3,0},{4,28},{5,20},{6,12},{7,4},{8,25},{9,17}... | collective-permute-start | bytes 221192 | tf_op jit(solution)/shard_map/ppermute | solution.py:345
  155.5 15.6 %collective-permute-done.21 = bf16[96,384]{1,0:T(8,128)(2,1)S(1)} collective-permute-done((bf16[96,384]{1,0:T(8,128)(2,1)S(1)}, bf16[96,384]{1,0:T(8,128)(2,1)S(1)}, u32[]{:S(2)}, u32[]{:S(2)}) %collective-permute-start.21) | collective-permute-done | bytes 73760 | tf_op jit(solution)/shard_map/ppermute | solution.py:345
  171.2 1.6 collective-permute-start.29
  172.8 1.9 collective-permute-start.25
  174.7 7.3 %collective-permute-done.29.refs_6_ = bf16[384,384]{1,0:T(8,128)(2,1)S(1)} collective-permute-done((bf16[384,384]{1,0:T(8,128)(2,1)S(1)}, bf16[384,384]{1,0:T(8,128)(2,1)S(1)}, u32[]{:S(2)}, u32[]{:S(2)}) %collective-permute-start.29) | collective-permute-done | bytes 294944 | tf_op jit(solution)/shard_map/ppermute | solution.py:47
  182.1 3.7 %collective-permute-done.27.refs_4_ = bf16[384,384]{1,0:T(8,128)(2,1)S(1)} collective-permute-done((bf16[384,384]{1,0:T(8,128)(2,1)S(1)}, bf16[384,384]{1,0:T(8,128)(2,1)S(1)}, u32[]{:S(2)}, u32[]{:S(2)}) %collective-permute-start.27) | collective-permute-done | bytes 294944 | tf_op jit(solution)/shard_map/ppermute | solution.py:47
  185.8 0.5 collective-permute-start.26
  186.4 1.0 collective-permute-done.28.refs_5_
  187.4 0.4 collective-permute-done.26.refs_3_
  188.1 0.7 copy-done.16
  188.8 6.8 %shard_map.118 = (bf16[384,512]{1,0:T(8,128)(2,1)}, bf16[384,512]{1,0:T(8,128)(2,1)}) custom-call(s32[2]{0:T(128)} %pad_add_fusion.at_ref, s32[12]{0:T(128)} %subtract_bitcast_fusion.index_ref, s32[2]{0:T(128)} %get-tuple-element.35.owner_ref, bf16[1536,2048]{1,0:T(8,128)(2,1)} %a_ref.12, bf16[384,384]{1,0:T(8,128)(2,1)} %copy-done.2, ...), custom_call_target="tpu_custom_call" | custom-call | flops 1207959552 | bytes 3145728 | tf_op jit(solution)/shard_map/pallas_call | solution.py:285
  195.6 1.4 collective-permute-start.31
  197.1 0.6 collective-permute-start.33
  197.7 7.1 %shard_map.117 = (f32[384,512]{1,0:T(8,128)}, f32[384,512]{1,0:T(8,128)}) custom-call(s32[2]{0:T(128)} %pad_add_fusion.at_ref, s32[12]{0:T(128)} %subtract_bitcast_fusion.index_ref, s32[2]{0:T(128)} %get-tuple-element.36.owner_ref, bf16[1536,2048]{1,0:T(8,128)(2,1)} %a_ref.12, bf16[384,384]{1,0:T(8,128)(2,1)} %copy-done.2, bf16[384,384]{1,0:T(8,128)(2,1)} %copy-done.10, ...), custom_call_target="tpu_custom_call" | custom-call | flops 1207959552 | bytes 3145728 | tf_op jit(solution)/shard_map/pallas_call | solution.py:285
  204.8 10.6 %collective-permute-done.31 = bf16[384,512]{1,0:T(8,128)(2,1)S(1)} collective-permute-done((bf16[384,512]{1,0:T(8,128)(2,1)}, bf16[384,512]{1,0:T(8,128)(2,1)S(1)}, u32[]{:S(2)}, u32[]{:S(2)}) %collective-permute-start.31) | collective-permute-done | bytes 393248 | tf_op jit(solution)/shard_map/ppermute | solution.py:43
  215.4 1.3 add_convert_fusion.1
  216.8 7.8 %collective-permute-done.32 = bf16[384,512]{1,0:T(8,128)(2,1)S(1)} collective-permute-done((bf16[384,512]{1,0:T(8,128)(2,1)S(1)}, bf16[384,512]{1,0:T(8,128)(2,1)S(1)}, u32[]{:S(2)}, u32[]{:S(2)}) %collective-permute-start.32) | collective-permute-done | bytes 393248 | tf_op jit(solution)/shard_map/ppermute | solution.py:43
  224.8 3.8 %collective-permute-start.35 = (bf16[384,512]{1,0:T(8,128)(2,1)S(1)}, bf16[384,512]{1,0:T(8,128)(2,1)S(1)}, u32[]{:S(2)}, u32[]{:S(2)}) collective-permute-start(bf16[384,512]{1,0:T(8,128)(2,1)S(1)} %add_convert_fusion.refs_0_), channel_id=1, source_target_pairs={{0,3},{1,0},{2,1},{3,2},{4,7},{5,4},{6,5},{7,6},{8,11},{9,8},{10,9... | collective-permute-start | bytes 1179656 | tf_op jit(solution)/shard_map/ppermute | solution.py:43
  228.6 10.2 %collective-permute-done.34.refs_1_ = bf16[384,512]{1,0:T(8,128)(2,1)S(1)} collective-permute-done((bf16[384,512]{1,0:T(8,128)(2,1)S(1)}, bf16[384,512]{1,0:T(8,128)(2,1)S(1)}, u32[]{:S(2)}, u32[]{:S(2)}) %collective-permute-start.34) | collective-permute-done | bytes 393248 | tf_op jit(solution)/shard_map/ppermute | solution.py:43
  238.8 7.2 %collective-permute-done.35.refs_2_ = bf16[384,512]{1,0:T(8,128)(2,1)S(1)} collective-permute-done((bf16[384,512]{1,0:T(8,128)(2,1)S(1)}, bf16[384,512]{1,0:T(8,128)(2,1)S(1)}, u32[]{:S(2)}, u32[]{:S(2)}) %collective-permute-start.35) | collective-permute-done | bytes 393248 | tf_op jit(solution)/shard_map/ppermute | solution.py:43
  245.9 4.3 %collective-permute-done.36.refs_3_ = bf16[384,512]{1,0:T(8,128)(2,1)S(1)} collective-permute-done((bf16[384,512]{1,0:T(8,128)(2,1)S(1)}, bf16[384,512]{1,0:T(8,128)(2,1)S(1)}, u32[]{:S(2)}, u32[]{:S(2)}) %collective-permute-start.36) | collective-permute-done | bytes 393248 | tf_op jit(solution)/shard_map/ppermute | solution.py:43
  250.2 0.7 copy-done.24
  251.0 5.0 %shard_map.119 = f32[512,384]{1,0:T(8,128)} custom-call(s32[2]{0:T(128)} %pad_add_fusion.at_ref, bf16[512,2048]{1,0:T(8,128)(2,1)} %a_ref.13, f32[512,384]{1,0:T(8,128)} %get-tuple-element.14.inner_ref, bf16[384,512]{1,0:T(8,128)(2,1)} %copy-done.1, bf16[384,512]{1,0:T(8,128)(2,1)} %copy-done.22, bf16[384,512]{1,0:T(8,128)(2,1)} %copy-done.23, ...), custom_call_target="tpu_custom_call" | custom-call | flops 805306368 | bytes 2097152 | tf_op jit(solution)/shard_map/pallas_call | solution.py:133
  (93 shorter events, 1.6 us)
Async XLA Ops:
  0.6 15.3 %collective-permute-start = (bf16[512,384]{1,0:T(8,128)(2,1)}, bf16[512,384]{1,0:T(8,128)(2,1)S(1)}, u32[]{:S(2)}, u32[]{:S(2)}) collective-permute-start(bf16[512,384]{1,0:T(8,128)(2,1)} %refs_0_.1), channel_id=1, source_target_pairs={{0,1},{1,2},{2,3},{3,0},{4,5},{5,6},{6,7},{7,4},{8,9},{9,10},{10,1... | collective-permute-start | bytes 1179656 | tf_op jit(solution)/shard_map/ppermute | solution.py:43
  3.7 19.4 %collective-permute-start.1 = (bf16[512,384]{1,0:T(8,128)(2,1)}, bf16[512,384]{1,0:T(8,128)(2,1)S(1)}, u32[]{:S(2)}, u32[]{:S(2)}) collective-permute-start(bf16[512,384]{1,0:T(8,128)(2,1)} %refs_0_.1), channel_id=1, source_target_pairs={{0,3},{1,0},{2,1},{3,2},{4,7},{5,4},{6,5},{7,6},{8,11},{9,8},{10,9... | collective-permute-start | bytes 1179656 | tf_op jit(solution)/shard_map/ppermute | solution.py:43
  15.9 16.0 %copy-start.19 = (bf16[512,384]{1,0:T(8,128)(2,1)}, bf16[512,384]{1,0:T(8,128)(2,1)S(1)}, u32[]{:S(2)}) copy-start(bf16[512,384]{1,0:T(8,128)(2,1)S(1)} %collective-permute-done.refs_1_) | copy-start | bytes 1179652
  15.9 16.0 %collective-permute-start.2 = (bf16[512,384]{1,0:T(8,128)(2,1)S(1)}, bf16[512,384]{1,0:T(8,128)(2,1)S(1)}, u32[]{:S(2)}, u32[]{:S(2)}) collective-permute-start(bf16[512,384]{1,0:T(8,128)(2,1)S(1)} %collective-permute-done.refs_1_), channel_id=1, source_target_pairs={{0,1},{1,2},{2,3},{3,0},{4,5},{5,6},{6,7},{7,4},{8,9},{9,10},{10,1... | collective-permute-start | bytes 1179656 | tf_op jit(solution)/shard_map/ppermute | solution.py:43
  16.6 35.2 %copy-start.30 = (s32[1,12]{1,0:T(1,128)S(1)}, s32[1,12]{1,0:T(1,128)}, u32[]{:S(2)}) copy-start(s32[1,12]{1,0:T(1,128)} %param.15) | copy-start | bytes 148
  23.1 8.8 %copy-start.20 = (bf16[512,384]{1,0:T(8,128)(2,1)}, bf16[512,384]{1,0:T(8,128)(2,1)S(1)}, u32[]{:S(2)}) copy-start(bf16[512,384]{1,0:T(8,128)(2,1)S(1)} %collective-permute-done.1.refs_2_) | copy-start | bytes 1179652
  32.0 0.7 copy-start.21
  37.7 14.1 %collective-permute-start.3 = (bf16[512,384]{1,0:T(8,128)(2,1)}, bf16[512,384]{1,0:T(8,128)(2,1)S(1)}, u32[]{:S(2)}, u32[]{:S(2)}) collective-permute-start(bf16[512,384]{1,0:T(8,128)(2,1)} %get-tuple-element.15.refs_0_), channel_id=1, source_target_pairs={{0,1},{1,2},{2,3},{3,0},{4,5},{5,6},{6,7},{7,4},{8,9},{9,10},{10,1... | collective-permute-start | bytes 1179656 | tf_op jit(solution)/shard_map/ppermute | solution.py:43
  37.7 20.0 %collective-permute-start.4 = (bf16[512,384]{1,0:T(8,128)(2,1)}, bf16[512,384]{1,0:T(8,128)(2,1)S(1)}, u32[]{:S(2)}, u32[]{:S(2)}) collective-permute-start(bf16[512,384]{1,0:T(8,128)(2,1)} %get-tuple-element.15.refs_0_), channel_id=1, source_target_pairs={{0,3},{1,0},{2,1},{3,2},{4,7},{5,4},{6,5},{7,6},{8,11},{9,8},{10,9... | collective-permute-start | bytes 1179656 | tf_op jit(solution)/shard_map/ppermute | solution.py:43
  51.7 13.6 %copy-start.27 = (bf16[512,384]{1,0:T(8,128)(2,1)}, bf16[512,384]{1,0:T(8,128)(2,1)S(1)}, u32[]{:S(2)}) copy-start(bf16[512,384]{1,0:T(8,128)(2,1)S(1)} %collective-permute-done.3.refs_1_) | copy-start | bytes 1179652
  51.7 13.6 %collective-permute-start.5 = (bf16[512,384]{1,0:T(8,128)(2,1)S(1)}, bf16[512,384]{1,0:T(8,128)(2,1)S(1)}, u32[]{:S(2)}, u32[]{:S(2)}) collective-permute-start(bf16[512,384]{1,0:T(8,128)(2,1)S(1)} %collective-permute-done.3.refs_1_), channel_id=1, source_target_pairs={{0,1},{1,2},{2,3},{3,0},{4,5},{5,6},{6,7},{7,4},{8,9},{9,10},{10,1... | collective-permute-start | bytes 1179656 | tf_op jit(solution)/shard_map/ppermute | solution.py:43
  57.7 7.7 %copy-start.28 = (bf16[512,384]{1,0:T(8,128)(2,1)}, bf16[512,384]{1,0:T(8,128)(2,1)S(1)}, u32[]{:S(2)}) copy-start(bf16[512,384]{1,0:T(8,128)(2,1)S(1)} %collective-permute-done.4.refs_2_) | copy-start | bytes 1179652
  65.4 0.8 copy-start.29
  74.7 3.1 %collective-permute-start.6 = (bf16[1536,384]{1,0:T(8,128)(2,1)}, bf16[1536,384]{1,0:T(8,128)(2,1)S(1)}, u32[]{:S(2)}, u32[]{:S(2)}) collective-permute-start(bf16[1536,384]{1,0:T(8,128)(2,1)} %get-tuple-element.17), channel_id=1, source_target_pairs={{0,4},{4,0},{8,12},{12,8},{16,20},{20,16},{24,28},{28,24},{1,5},{5... | collective-permute-start | bytes 3538952 | tf_op jit(solution)/shard_map/ppermute | solution.py:47
  79.1 9.9 %collective-permute-start.7 = (bf16[384,384]{1,0:T(8,128)(2,1)S(1)}, bf16[384,384]{1,0:T(8,128)(2,1)S(1)}, u32[]{:S(2)}, u32[]{:S(2)}) collective-permute-start(bf16[384,384]{1,0:T(8,128)(2,1)S(1)} %get-tuple-element.28), channel_id=1, source_target_pairs={{0,8},{4,12},{8,0},{12,4},{16,24},{20,28},{24,16},{28,20},{1,9},{5... | collective-permute-start | bytes 884744 | tf_op jit(solution)/shard_map/ppermute | solution.py:47
  80.7 14.9 %collective-permute-start.9 = (bf16[384,384]{1,0:T(8,128)(2,1)S(1)}, bf16[384,384]{1,0:T(8,128)(2,1)S(1)}, u32[]{:S(2)}, u32[]{:S(2)}) collective-permute-start(bf16[384,384]{1,0:T(8,128)(2,1)S(1)} %get-tuple-element.29), channel_id=1, source_target_pairs={{0,24},{4,28},{8,16},{12,20},{16,8},{20,12},{24,0},{28,4},{1,25},{... | collective-permute-start | bytes 884744 | tf_op jit(solution)/shard_map/ppermute | solution.py:47
  82.2 14.8 %collective-permute-start.8 = (bf16[384,384]{1,0:T(8,128)(2,1)S(1)}, bf16[384,384]{1,0:T(8,128)(2,1)S(1)}, u32[]{:S(2)}, u32[]{:S(2)}) collective-permute-start(bf16[384,384]{1,0:T(8,128)(2,1)S(1)} %get-tuple-element.30), channel_id=1, source_target_pairs={{0,16},{4,20},{8,24},{12,28},{16,0},{20,4},{24,8},{28,12},{1,17},{... | collective-permute-start | bytes 884744 | tf_op jit(solution)/shard_map/ppermute | solution.py:47
  82.7 30.3 %copy-start.25 = (s32[2]{0:T(128)S(1)}, s32[2]{0:T(128)}, u32[]{:S(2)}) copy-start(s32[2]{0:T(128)} %constant.51.clone) | copy-start | bytes 28
  82.7 30.3 %copy-start.26 = (s32[2]{0:T(128)S(1)}, s32[2]{0:T(128)}, u32[]{:S(2)}) copy-start(s32[2]{0:T(128)} %constant.50.clone) | copy-start | bytes 28
  98.3 16.1 %copy-start = (bf16[384,384]{1,0:T(8,128)(2,1)}, bf16[384,384]{1,0:T(8,128)(2,1)S(1)}, u32[]{:S(2)}) copy-start(bf16[384,384]{1,0:T(8,128)(2,1)S(1)} %subtract_convert_fusion.refs_0_) | copy-start | bytes 884740
  98.4 10.9 %collective-permute-start.15 = (bf16[384,384]{1,0:T(8,128)(2,1)S(1)}, bf16[384,384]{1,0:T(8,128)(2,1)S(1)}, u32[]{:S(2)}, u32[]{:S(2)}) collective-permute-start(bf16[384,384]{1,0:T(8,128)(2,1)S(1)} %subtract_convert_fusion.refs_0_), channel_id=1, source_target_pairs={{0,24},{4,28},{8,16},{12,20},{16,8},{20,12},{24,0},{28,4},{1,25},{... | collective-permute-start | bytes 884744 | tf_op jit(solution)/shard_map/ppermute | solution.py:47
  99.8 12.6 %collective-permute-start.13 = (bf16[384,384]{1,0:T(8,128)(2,1)S(1)}, bf16[384,384]{1,0:T(8,128)(2,1)S(1)}, u32[]{:S(2)}, u32[]{:S(2)}) collective-permute-start(bf16[384,384]{1,0:T(8,128)(2,1)S(1)} %subtract_convert_fusion.refs_0_), channel_id=1, source_target_pairs={{0,16},{4,20},{8,24},{12,28},{16,0},{20,4},{24,8},{28,12},{1,17},{... | collective-permute-start | bytes 884744 | tf_op jit(solution)/shard_map/ppermute | solution.py:47
  101.4 11.1 %collective-permute-start.11 = (bf16[384,384]{1,0:T(8,128)(2,1)S(1)}, bf16[384,384]{1,0:T(8,128)(2,1)S(1)}, u32[]{:S(2)}, u32[]{:S(2)}) collective-permute-start(bf16[384,384]{1,0:T(8,128)(2,1)S(1)} %subtract_convert_fusion.refs_0_), channel_id=1, source_target_pairs={{0,8},{4,12},{8,0},{12,4},{16,24},{20,28},{24,16},{28,20},{1,9},{5... | collective-permute-start | bytes 884744 | tf_op jit(solution)/shard_map/ppermute | solution.py:47
  101.9 11.6 %collective-permute-start.10 = (bf16[384,384]{1,0:T(8,128)(2,1)S(1)}, bf16[384,384]{1,0:T(8,128)(2,1)S(1)}, u32[]{:S(2)}, u32[]{:S(2)}) collective-permute-start(bf16[384,384]{1,0:T(8,128)(2,1)S(1)} %subtract_convert_fusion.refs_0_), channel_id=1, source_target_pairs={{0,4},{4,0},{8,12},{12,8},{16,20},{20,16},{24,28},{28,24},{1,5},{5... | collective-permute-start | bytes 884744 | tf_op jit(solution)/shard_map/ppermute | solution.py:47
  109.3 5.2 %copy-start.3 = (bf16[384,384]{1,0:T(8,128)(2,1)}, bf16[384,384]{1,0:T(8,128)(2,1)S(1)}, u32[]{:S(2)}) copy-start(bf16[384,384]{1,0:T(8,128)(2,1)S(1)} %collective-permute-done.15.refs_6_) | copy-start | bytes 884740
  109.3 4.3 %collective-permute-start.16 = (bf16[384,384]{1,0:T(8,128)(2,1)S(1)}, bf16[384,384]{1,0:T(8,128)(2,1)S(1)}, u32[]{:S(2)}, u32[]{:S(2)}) collective-permute-start(bf16[384,384]{1,0:T(8,128)(2,1)S(1)} %collective-permute-done.15.refs_6_), channel_id=1, source_target_pairs={{0,4},{4,0},{8,12},{12,8},{16,20},{20,16},{24,28},{28,24},{1,5},{5... | collective-permute-start | bytes 884744 | tf_op jit(solution)/shard_map/ppermute | solution.py:47
  112.4 2.0 copy-start.4
  112.4 1.6 collective-permute-start.14
  112.5 2.0 copy-start.6
  112.5 2.0 collective-permute-start.12
  113.5 1.0 copy-start.8
  113.5 1.0 copy-start.11
  123.0 15.6 %collective-permute-start.17 = (bf16[384,384]{1,0:T(8,128)(2,1)}, bf16[384,384]{1,0:T(8,128)(2,1)S(1)}, u32[]{:S(2)}, u32[]{:S(2)}) collective-permute-start(bf16[384,384]{1,0:T(8,128)(2,1)} %get-tuple-element.19), channel_id=1, source_target_pairs={{0,3},{1,0},{2,1},{3,2},{4,7},{5,4},{6,5},{7,6},{8,11},{9,8},{10,9... | collective-permute-start | bytes 884744 | tf_op jit(solution)/shard_map/ppermute | solution.py:43
  123.1 16.8 %collective-permute-start.19 = (bf16[384,384]{1,0:T(8,128)(2,1)}, bf16[384,384]{1,0:T(8,128)(2,1)S(1)}, u32[]{:S(2)}, u32[]{:S(2)}) collective-permute-start(bf16[384,384]{1,0:T(8,128)(2,1)} %get-tuple-element.21), channel_id=1, source_target_pairs={{0,1},{1,2},{2,3},{3,0},{4,5},{5,6},{6,7},{7,4},{8,9},{9,10},{10,1... | collective-permute-start | bytes 884744 | tf_op jit(solution)/shard_map/ppermute | solution.py:43
  133.2 14.9 %copy-start.18 = (f32[384,384]{1,0:T(8,128)S(1)}, f32[384,384]{1,0:T(8,128)}, u32[]{:S(2)}) copy-start(f32[384,384]{1,0:T(8,128)} %get-tuple-element.18) | copy-start | bytes 1769476
  139.8 8.3 %collective-permute-start.18 = (bf16[384,384]{1,0:T(8,128)(2,1)S(1)}, bf16[384,384]{1,0:T(8,128)(2,1)S(1)}, u32[]{:S(2)}, u32[]{:S(2)}) collective-permute-start(bf16[384,384]{1,0:T(8,128)(2,1)S(1)} %add_convert_fusion.2), channel_id=1, source_target_pairs={{0,3},{1,0},{2,1},{3,2},{4,7},{5,4},{6,5},{7,6},{8,11},{9,8},{10,9... | collective-permute-start | bytes 884744 | tf_op jit(solution)/shard_map/ppermute | solution.py:43
  149.0 6.4 %collective-permute-start.20 = (bf16[96,384]{1,0:T(8,128)(2,1)S(1)}, bf16[96,384]{1,0:T(8,128)(2,1)S(1)}, u32[]{:S(2)}, u32[]{:S(2)}) collective-permute-start(bf16[96,384]{1,0:T(8,128)(2,1)S(1)} %get-tuple-element.34), channel_id=1, source_target_pairs={{0,0},{1,8},{2,16},{3,24},{4,4},{5,12},{6,20},{7,28},{8,1},{9,9},{... | collective-permute-start | bytes 221192 | tf_op jit(solution)/shard_map/ppermute | solution.py:345
  149.7 21.4 %collective-permute-start.23 = (bf16[96,384]{1,0:T(8,128)(2,1)S(1)}, bf16[96,384]{1,0:T(8,128)(2,1)S(1)}, u32[]{:S(2)}, u32[]{:S(2)}) collective-permute-start(bf16[96,384]{1,0:T(8,128)(2,1)S(1)} %get-tuple-element.31), channel_id=1, source_target_pairs={{0,24},{1,16},{2,8},{3,0},{4,28},{5,20},{6,12},{7,4},{8,25},{9,17}... | collective-permute-start | bytes 221192 | tf_op jit(solution)/shard_map/ppermute | solution.py:345
  155.4 15.7 %collective-permute-start.22 = (bf16[96,384]{1,0:T(8,128)(2,1)S(1)}, bf16[96,384]{1,0:T(8,128)(2,1)S(1)}, u32[]{:S(2)}, u32[]{:S(2)}) collective-permute-start(bf16[96,384]{1,0:T(8,128)(2,1)S(1)} %get-tuple-element.32), channel_id=1, source_target_pairs={{0,16},{1,24},{2,0},{3,8},{4,20},{5,28},{6,4},{7,12},{8,17},{9,25}... | collective-permute-start | bytes 221192 | tf_op jit(solution)/shard_map/ppermute | solution.py:345
  155.4 15.6 %collective-permute-start.21 = (bf16[96,384]{1,0:T(8,128)(2,1)S(1)}, bf16[96,384]{1,0:T(8,128)(2,1)S(1)}, u32[]{:S(2)}, u32[]{:S(2)}) collective-permute-start(bf16[96,384]{1,0:T(8,128)(2,1)S(1)} %get-tuple-element.33), channel_id=1, source_target_pairs={{0,8},{1,0},{2,24},{3,16},{4,12},{5,4},{6,28},{7,20},{8,9},{9,1},{... | collective-permute-start | bytes 221192 | tf_op jit(solution)/shard_map/ppermute | solution.py:345
  171.2 16.7 %copy-start.2 = (bf16[384,384]{1,0:T(8,128)(2,1)}, bf16[384,384]{1,0:T(8,128)(2,1)S(1)}, u32[]{:S(2)}) copy-start(bf16[384,384]{1,0:T(8,128)(2,1)S(1)} %constant_dynamic-update-slice_fusion.refs_0_) | copy-start | bytes 884740
  171.2 10.9 %collective-permute-start.29 = (bf16[384,384]{1,0:T(8,128)(2,1)S(1)}, bf16[384,384]{1,0:T(8,128)(2,1)S(1)}, u32[]{:S(2)}, u32[]{:S(2)}) collective-permute-start(bf16[384,384]{1,0:T(8,128)(2,1)S(1)} %constant_dynamic-update-slice_fusion.refs_0_), channel_id=1, source_target_pairs={{0,24},{4,28},{8,16},{12,20},{16,8},{20,12},{24,0},{28,4},{1,25},{... | collective-permute-start | bytes 884744 | tf_op jit(solution)/shard_map/ppermute | solution.py:47
  172.8 13.1 %collective-permute-start.27 = (bf16[384,384]{1,0:T(8,128)(2,1)S(1)}, bf16[384,384]{1,0:T(8,128)(2,1)S(1)}, u32[]{:S(2)}, u32[]{:S(2)}) collective-permute-start(bf16[384,384]{1,0:T(8,128)(2,1)S(1)} %constant_dynamic-update-slice_fusion.refs_0_), channel_id=1, source_target_pairs={{0,16},{4,20},{8,24},{12,28},{16,0},{20,4},{24,8},{28,12},{1,17},{... | collective-permute-start | bytes 884744 | tf_op jit(solution)/shard_map/ppermute | solution.py:47
  172.8 13.1 %collective-permute-start.25 = (bf16[384,384]{1,0:T(8,128)(2,1)S(1)}, bf16[384,384]{1,0:T(8,128)(2,1)S(1)}, u32[]{:S(2)}, u32[]{:S(2)}) collective-permute-start(bf16[384,384]{1,0:T(8,128)(2,1)S(1)} %constant_dynamic-update-slice_fusion.refs_0_), channel_id=1, source_target_pairs={{0,8},{4,12},{8,0},{12,4},{16,24},{20,28},{24,16},{28,20},{1,9},{5... | collective-permute-start | bytes 884744 | tf_op jit(solution)/shard_map/ppermute | solution.py:47
  174.7 11.6 %collective-permute-start.24 = (bf16[384,384]{1,0:T(8,128)(2,1)S(1)}, bf16[384,384]{1,0:T(8,128)(2,1)S(1)}, u32[]{:S(2)}, u32[]{:S(2)}) collective-permute-start(bf16[384,384]{1,0:T(8,128)(2,1)S(1)} %constant_dynamic-update-slice_fusion.refs_0_), channel_id=1, source_target_pairs={{0,4},{4,0},{8,12},{12,8},{16,20},{20,16},{24,28},{28,24},{1,5},{5... | collective-permute-start | bytes 884744 | tf_op jit(solution)/shard_map/ppermute | solution.py:47
  182.1 5.8 %copy-start.5 = (bf16[384,384]{1,0:T(8,128)(2,1)}, bf16[384,384]{1,0:T(8,128)(2,1)S(1)}, u32[]{:S(2)}) copy-start(bf16[384,384]{1,0:T(8,128)(2,1)S(1)} %collective-permute-done.29.refs_6_) | copy-start | bytes 884740
  182.1 4.3 %collective-permute-start.30 = (bf16[384,384]{1,0:T(8,128)(2,1)S(1)}, bf16[384,384]{1,0:T(8,128)(2,1)S(1)}, u32[]{:S(2)}, u32[]{:S(2)}) collective-permute-start(bf16[384,384]{1,0:T(8,128)(2,1)S(1)} %collective-permute-done.29.refs_6_), channel_id=1, source_target_pairs={{0,4},{4,0},{8,12},{12,8},{16,20},{20,16},{24,28},{28,24},{1,5},{5... | collective-permute-start | bytes 884744 | tf_op jit(solution)/shard_map/ppermute | solution.py:47
  185.8 2.0 copy-start.7
  185.8 1.6 collective-permute-start.28
  185.8 2.0 copy-start.9
  185.8 2.0 collective-permute-start.26
  186.3 1.5 copy-start.10
  186.4 1.5 copy-start.12
  195.6 19.8 %collective-permute-start.31 = (bf16[384,512]{1,0:T(8,128)(2,1)}, bf16[384,512]{1,0:T(8,128)(2,1)S(1)}, u32[]{:S(2)}, u32[]{:S(2)}) collective-permute-start(bf16[384,512]{1,0:T(8,128)(2,1)} %get-tuple-element.23), channel_id=1, source_target_pairs={{0,3},{1,0},{2,1},{3,2},{4,7},{5,4},{6,5},{7,6},{8,11},{9,8},{10,9... | collective-permute-start | bytes 1179656 | tf_op jit(solution)/shard_map/ppermute | solution.py:43
  197.1 19.7 %collective-permute-start.33 = (bf16[384,512]{1,0:T(8,128)(2,1)}, bf16[384,512]{1,0:T(8,128)(2,1)S(1)}, u32[]{:S(2)}, u32[]{:S(2)}) collective-permute-start(bf16[384,512]{1,0:T(8,128)(2,1)} %get-tuple-element.25), channel_id=1, source_target_pairs={{0,1},{1,2},{2,3},{3,0},{4,5},{5,6},{6,7},{7,4},{8,9},{9,10},{10,1... | collective-permute-start | bytes 1179656 | tf_op jit(solution)/shard_map/ppermute | solution.py:43
  204.8 19.7 %copy-start.17 = (f32[384,512]{1,0:T(8,128)S(1)}, f32[384,512]{1,0:T(8,128)}, u32[]{:S(2)}) copy-start(f32[384,512]{1,0:T(8,128)} %get-tuple-element.22) | copy-start | bytes 2359300
  216.7 7.8 %collective-permute-start.32 = (bf16[384,512]{1,0:T(8,128)(2,1)S(1)}, bf16[384,512]{1,0:T(8,128)(2,1)S(1)}, u32[]{:S(2)}, u32[]{:S(2)}) collective-permute-start(bf16[384,512]{1,0:T(8,128)(2,1)S(1)} %add_convert_fusion.1), channel_id=1, source_target_pairs={{0,3},{1,0},{2,1},{3,2},{4,7},{5,4},{6,5},{7,6},{8,11},{9,8},{10,9... | collective-permute-start | bytes 1179656 | tf_op jit(solution)/shard_map/ppermute | solution.py:43
  224.7 25.6 %copy-start.1 = (bf16[384,512]{1,0:T(8,128)(2,1)}, bf16[384,512]{1,0:T(8,128)(2,1)S(1)}, u32[]{:S(2)}) copy-start(bf16[384,512]{1,0:T(8,128)(2,1)S(1)} %add_convert_fusion.refs_0_) | copy-start | bytes 1179652
  224.7 14.1 %collective-permute-start.34 = (bf16[384,512]{1,0:T(8,128)(2,1)S(1)}, bf16[384,512]{1,0:T(8,128)(2,1)S(1)}, u32[]{:S(2)}, u32[]{:S(2)}) collective-permute-start(bf16[384,512]{1,0:T(8,128)(2,1)S(1)} %add_convert_fusion.refs_0_), channel_id=1, source_target_pairs={{0,1},{1,2},{2,3},{3,0},{4,5},{5,6},{6,7},{7,4},{8,9},{9,10},{10,1... | collective-permute-start | bytes 1179656 | tf_op jit(solution)/shard_map/ppermute | solution.py:43
  224.8 21.2 %collective-permute-start.35 = (bf16[384,512]{1,0:T(8,128)(2,1)S(1)}, bf16[384,512]{1,0:T(8,128)(2,1)S(1)}, u32[]{:S(2)}, u32[]{:S(2)}) collective-permute-start(bf16[384,512]{1,0:T(8,128)(2,1)S(1)} %add_convert_fusion.refs_0_), channel_id=1, source_target_pairs={{0,3},{1,0},{2,1},{3,2},{4,7},{5,4},{6,5},{7,6},{8,11},{9,8},{10,9... | collective-permute-start | bytes 1179656 | tf_op jit(solution)/shard_map/ppermute | solution.py:43
  238.8 11.5 %copy-start.22 = (bf16[384,512]{1,0:T(8,128)(2,1)}, bf16[384,512]{1,0:T(8,128)(2,1)S(1)}, u32[]{:S(2)}) copy-start(bf16[384,512]{1,0:T(8,128)(2,1)S(1)} %collective-permute-done.34.refs_1_) | copy-start | bytes 1179652
  238.8 11.5 %collective-permute-start.36 = (bf16[384,512]{1,0:T(8,128)(2,1)S(1)}, bf16[384,512]{1,0:T(8,128)(2,1)S(1)}, u32[]{:S(2)}, u32[]{:S(2)}) collective-permute-start(bf16[384,512]{1,0:T(8,128)(2,1)S(1)} %collective-permute-done.34.refs_1_), channel_id=1, source_target_pairs={{0,1},{1,2},{2,3},{3,0},{4,5},{5,6},{6,7},{7,4},{8,9},{9,10},{10,1... | collective-permute-start | bytes 1179656 | tf_op jit(solution)/shard_map/ppermute | solution.py:43
  245.9 4.3 %copy-start.23 = (bf16[384,512]{1,0:T(8,128)(2,1)}, bf16[384,512]{1,0:T(8,128)(2,1)S(1)}, u32[]{:S(2)}) copy-start(bf16[384,512]{1,0:T(8,128)(2,1)S(1)} %collective-permute-done.35.refs_2_) | copy-start | bytes 1179652
  250.2 0.7 copy-start.24
  (4 other events, 2.9 us)

commit v3 on v2

--- a/solution.py
+++ b/solution.py
@@ -411,6 +411,14 @@
             and arrays[2].shape[1] % (n_row * BLK) == 0
             and width % BLK == 0
         )
-        return (solve if fits else solve_plain)(n_front, n_row, *arrays)
+        if not fits:
+            return solve_plain(n_front, n_row, *arrays)
+        cut = width * 2 // 3 // BLK * BLK
+        parts = [
+            solve(n_front, n_row, arrays[0][:, low:high], arrays[1][:, low:high], *arrays[2:])
+            for low, high in ((0, cut), (cut, width))
+            if high > low
+        ]
+        return tuple(jnp.concatenate(outs, axis=1) for outs in zip(*parts))
 
     return jax.shard_map(per_device, mesh=mesh, in_specs=in_specs, out_specs=out_specs, check_vma=False)

time: 258 us -> 277 us (1.074)
  waiting for transfers between devices: 160 us -> 89.7 us
  starting transfers between devices: 35.2 us -> 84 us
  Pallas kernels: 48.3 us -> 76.7 us
  local copies, waits for them, and re-layouts: 4.06 us -> 11.9 us
  other arithmetic: 7.87 us -> 12.4 us
    ppermute x15 -> x30, waiting for transfers between devices: 103 us -> 54.7 us  [shift(): return lax.ppermute(x, 'row', [(i, (i + by) % size) for i in range(size)])]
    ppermute x15 -> x30, starting transfers between devices: 17.1 us -> 46.6 us  [shift(): return lax.ppermute(x, 'row', [(i, (i + by) % size) for i in range(size)])]
    ppermute x18 -> x36, waiting for transfers between devices: 41.4 us -> 21.2 us  [swap(): return lax.ppermute(x, 'front', [(i, i ^ by) for i in range(size)])]
    ppermute x18 -> x36, starting transfers between devices: 11.7 us -> 24.8 us  [swap(): return lax.ppermute(x, 'front', [(i, i ^ by) for i in range(size)])]
    pallas_call x2 -> x4, Pallas kernels: 15.9 us -> 24.9 us  [root_products(): kernel_call(body, [jax.ShapeDtypeStruct((rows, width), kind) for kind in...]
    pallas_call x2 -> x4, Pallas kernels: 13.9 us -> 22.3 us  [border_backward(): kernel_call(body, [jax.ShapeDtypeStruct((width, columns), kind) for kind...]
    ppermute x4 -> x8, starting transfers between devices: 6.41 us -> 12.7 us  [solve(): lax.ppermute(root_half[k * quarter:(k + 1) * quarter], ('front', 'row'),...]
    unnamed x65 -> x136, local copies, waits for them, and re-layouts: 4.01 us -> 9.95 us
  transfers between devices with their start and end apart: 37 -> 74, of which waited for: 26 -> 30; matrix products, arithmetic and copies ran while one was open for 2% -> 4% of each run, Pallas kernels for 6% -> 25%
where the time goes in v3:
time: 277 us; the launch traced here: 276 us
  waiting for transfers between devices  89.7 us (32%)
  starting transfers between devices  84 us (30%)
  Pallas kernels  76.7 us (28%)
  other arithmetic  12.4 us (4%)
  local copies, waits for them, and re-layouts  11.9 us (4%)
    ppermute x30, waiting for transfers between devices, shift(): return lax.ppermute(x, 'row', [(i, (i + by) % size) for i in range(size)])  54.7 us
    ppermute x30, starting transfers between devices, shift(): return lax.ppermute(x, 'row', [(i, (i + by) % size) for i in range(size)])  46.6 us
    pallas_call x4, Pallas kernels, root_products(): kernel_call(body, [jax.ShapeDtypeStruct((rows, width), kind) for kind in...  24.9 us
    ppermute x36, starting transfers between devices, swap(): return lax.ppermute(x, 'front', [(i, i ^ by) for i in range(size)])  24.8 us
    pallas_call x4, Pallas kernels, border_backward(): kernel_call(body, [jax.ShapeDtypeStruct((width, columns), kind) for kind...  22.3 us
    ppermute x36, waiting for transfers between devices, swap(): return lax.ppermute(x, 'front', [(i, i ^ by) for i in range(size)])  21.2 us
    ppermute x8, waiting for transfers between devices, solve(): lax.ppermute(root_half[k * quarter:(k + 1) * quarter], ('front', 'row'),...  13.8 us
    pallas_call x2, Pallas kernels, border_forward(): kernel_call(body, [half, half], (blocks // per_step,), 2, [pl.BlockSpec((...  13.4 us
  transfers between devices with their start and end apart: 74, of which 30 were waited for; matrix products, arithmetic and copies ran while one was open for 4% of the time, Pallas kernels for 25%

profile of v3, /device:TPU:0, one launch (start us, length us, event | category | flops | bytes accessed | tf_op | source)
XLA Modules:
  0.0 276.1 jit_solution(5084809342317995570)
XLA Ops:
  1.6 3.1 %collective-permute-start = (bf16[512,256]{1,0:T(8,128)(2,1)S(1)}, bf16[512,256]{1,0:T(8,128)(2,1)S(1)}, u32[]{:S(2)}, u32[]{:S(2)}) collective-permute-start(bf16[512,256]{1,0:T(8,128)(2,1)S(1)} %slice.84.refs_0_), channel_id=1, source_target_pairs={{0,1},{1,2},{2,3},{3,0},{4,5},{5,6},{6,7},{7,4},{8,9},{9,10},{10,1... | collective-permute-start | bytes 786440 | tf_op jit(solution)/shard_map/ppermute | solution.py:43
  4.7 2.1 collective-permute-start.1
  6.8 7.1 %collective-permute-done.refs_1_ = bf16[512,256]{1,0:T(8,128)(2,1)S(1)} collective-permute-done((bf16[512,256]{1,0:T(8,128)(2,1)S(1)}, bf16[512,256]{1,0:T(8,128)(2,1)S(1)}, u32[]{:S(2)}, u32[]{:S(2)}) %collective-permute-start) | collective-permute-done | bytes 262176 | tf_op jit(solution)/shard_map/ppermute | solution.py:43
  14.6 3.7 %collective-permute-done.1.refs_2_ = bf16[512,256]{1,0:T(8,128)(2,1)S(1)} collective-permute-done((bf16[512,256]{1,0:T(8,128)(2,1)S(1)}, bf16[512,256]{1,0:T(8,128)(2,1)S(1)}, u32[]{:S(2)}, u32[]{:S(2)}) %collective-permute-start.1) | collective-permute-done | bytes 262176 | tf_op jit(solution)/shard_map/ppermute | solution.py:43
  18.3 6.0 %collective-permute-done.2.refs_3_ = bf16[512,256]{1,0:T(8,128)(2,1)S(1)} collective-permute-done((bf16[512,256]{1,0:T(8,128)(2,1)S(1)}, bf16[512,256]{1,0:T(8,128)(2,1)S(1)}, u32[]{:S(2)}, u32[]{:S(2)}) %collective-permute-start.2) | collective-permute-done | bytes 262176 | tf_op jit(solution)/shard_map/ppermute | solution.py:43
  25.0 4.1 %shard_map.149 = (f32[512,256]{1,0:T(8,128)}, bf16[512,256]{1,0:T(8,128)(2,1)}) custom-call(s32[2]{0:T(128)} %pad_add_fusion.at_ref, bf16[512,2048]{1,0:T(8,128)(2,1)} %a_ref.27, bf16[512,256]{1,0:T(8,128)(2,1)} %copy-done.2, bf16[512,256]{1,0:T(8,128)(2,1)} %copy-done.46, bf16[512,256]{1,0:T(8,128)(2,1)} %copy-done.47, bf16[512,256]{1,0:T(8,128)(2,1)} %copy-done.48), custom_call_target="tpu_custom_call" | custom-call | flops 536870912 | bytes 2097152 | tf_op jit(solution)/shard_map/pallas_call | solution.py:112
  30.1 1.3 collective-permute-start.37
  31.4 2.6 collective-permute-start.38
  34.0 7.5 %collective-permute-done.37.refs_1_ = bf16[512,128]{1,0:T(8,128)(2,1)S(1)} collective-permute-done((bf16[512,128]{1,0:T(8,128)(2,1)S(1)}, bf16[512,128]{1,0:T(8,128)(2,1)S(1)}, u32[]{:S(2)}, u32[]{:S(2)}) %collective-permute-start.37) | collective-permute-done | bytes 131104 | tf_op jit(solution)/shard_map/ppermute | solution.py:43
  41.6 3.8 %collective-permute-start.4 = (bf16[512,256]{1,0:T(8,128)(2,1)}, bf16[512,256]{1,0:T(8,128)(2,1)S(1)}, u32[]{:S(2)}, u32[]{:S(2)}) collective-permute-start(bf16[512,256]{1,0:T(8,128)(2,1)} %get-tuple-element.27.refs_0_), channel_id=1, source_target_pairs={{0,3},{1,0},{2,1},{3,2},{4,7},{5,4},{6,5},{7,6},{8,11},{9,8},{10,9... | collective-permute-start | bytes 786440 | tf_op jit(solution)/shard_map/ppermute | solution.py:43
  45.4 4.5 %collective-permute-done.39.refs_3_ = bf16[512,128]{1,0:T(8,128)(2,1)S(1)} collective-permute-done((bf16[512,128]{1,0:T(8,128)(2,1)S(1)}, bf16[512,128]{1,0:T(8,128)(2,1)S(1)}, u32[]{:S(2)}, u32[]{:S(2)}) %collective-permute-start.39) | collective-permute-done | bytes 131104 | tf_op jit(solution)/shard_map/ppermute | solution.py:43
  50.6 3.9 %shard_map.156 = (f32[512,128]{1,0:T(8,128)}, bf16[512,128]{1,0:T(8,128)(2,1)}) custom-call(s32[2]{0:T(128)} %pad_add_fusion.at_ref, bf16[512,2048]{1,0:T(8,128)(2,1)} %a_ref.27, bf16[512,128]{1,0:T(8,128)(2,1)} %copy-done.21, bf16[512,128]{1,0:T(8,128)(2,1)} %copy-done.53, bf16[512,128]{1,0:T(8,128)(2,1)} %copy-done.54, bf16[512,128]{1,0:T(8,128)(2,1)} %copy-done.56), custom_call_target="tpu_custom_call" | custom-call | flops 268435456 | bytes 2097152 | tf_op jit(solution)/shard_map/pallas_call | solution.py:112
  55.0 3.8 %collective-permute-start.41 = (bf16[512,128]{1,0:T(8,128)(2,1)}, bf16[512,128]{1,0:T(8,128)(2,1)S(1)}, u32[]{:S(2)}, u32[]{:S(2)}) collective-permute-start(bf16[512,128]{1,0:T(8,128)(2,1)} %get-tuple-element.39.refs_0_), channel_id=1, source_target_pairs={{0,3},{1,0},{2,1},{3,2},{4,7},{5,4},{6,5},{7,6},{8,11},{9,8},{10,9... | collective-permute-start | bytes 393224 | tf_op jit(solution)/shard_map/ppermute | solution.py:43
  58.9 3.6 %collective-permute-done.40.refs_1_ = bf16[512,128]{1,0:T(8,128)(2,1)S(1)} collective-permute-done((bf16[512,128]{1,0:T(8,128)(2,1)}, bf16[512,128]{1,0:T(8,128)(2,1)S(1)}, u32[]{:S(2)}, u32[]{:S(2)}) %collective-permute-start.40) | collective-permute-done | bytes 131104 | tf_op jit(solution)/shard_map/ppermute | solution.py:43
  63.9 7.0 %shard_map.150 = (bf16[1536,256]{1,0:T(8,128)(2,1)}, bf16[1536,256]{1,0:T(8,128)(2,1)}) custom-call(s32[2]{0:T(128)} %pad_add_fusion.at_ref, s32[12]{0:T(128)} %subtract_bitcast_fusion.index_ref, bf16[1536,2048]{1,0:T(8,128)(2,1)} %a_ref.26, bf16[512,256]{1,0:T(8,128)(2,1)} %get-tuple-element.27.refs_0_, bf16[512,256]{1,0:T(8,128)(2,1)} %copy-done.40, ...), custom_call_target="tpu_custom_call" | custom-call | flops 1610612736 | bytes 6291456 | tf_op jit(solution)/shard_map/pallas_call | solution.py:180
  72.2 6.5 %shard_map.157 = (bf16[1536,128]{1,0:T(8,128)(2,1)}, bf16[1536,128]{1,0:T(8,128)(2,1)}) custom-call(s32[2]{0:T(128)} %pad_add_fusion.at_ref, s32[12]{0:T(128)} %subtract_bitcast_fusion.index_ref, bf16[1536,2048]{1,0:T(8,128)(2,1)} %a_ref.26, bf16[512,128]{1,0:T(8,128)(2,1)} %get-tuple-element.39.refs_0_, bf16[512,128]{1,0:T(8,128)(2,1)} %copy-done.51, ...), custom_call_target="tpu_custom_call" | custom-call | flops 805306368 | bytes 6291456 | tf_op jit(solution)/shard_map/pallas_call | solution.py:180
  79.2 1.7 collective-permute-done.43
  82.0 1.6 collective-permute-start.44
  83.6 1.5 collective-permute-start.45
  85.7 1.6 collective-permute-start.7
  87.3 1.5 collective-permute-start.8
  88.8 1.4 collective-permute-start.9
  90.2 1.5 collective-permute-done.46
  95.0 1.5 collective-permute-start.52
  96.5 2.4 collective-permute-done.8
  98.9 1.4 collective-permute-done.9
  101.2 1.5 collective-permute-start.13
  102.6 1.9 collective-permute-start.15
  106.6 4.2 %collective-permute-done.13.refs_4_ = bf16[384,256]{1,0:T(8,128)(2,1)S(1)} collective-permute-done((bf16[384,256]{1,0:T(8,128)(2,1)S(1)}, bf16[384,256]{1,0:T(8,128)(2,1)S(1)}, u32[]{:S(2)}, u32[]{:S(2)}) %collective-permute-start.13) | collective-permute-done | bytes 196640 | tf_op jit(solution)/shard_map/ppermute | solution.py:47
  110.8 1.8 collective-permute-done.15.refs_6_
  113.9 6.0 %shard_map.159 = (bf16[384,128]{1,0:T(8,128)(2,1)}, bf16[384,128]{1,0:T(8,128)(2,1)}) custom-call(s32[2]{0:T(128)} %pad_add_fusion.at_ref, s32[2]{0:T(128)} %get-tuple-element.68.owner_ref, bf16[1536,3072]{1,0:T(8,128)(2,1)} %a_ref.24, bf16[384,128]{1,0:T(8,128)(2,1)} %copy-done.5, bf16[384,128]{1,0:T(8,128)(2,1)} %copy-done.28, ...), custom_call_target="tpu_custom_call" | custom-call | flops 603979776 | bytes 4718592 | tf_op jit(solution)/shard_map/pallas_call | solution.py:225
  119.9 3.8 %collective-permute-start.54 = (bf16[384,128]{1,0:T(8,128)(2,1)}, bf16[384,128]{1,0:T(8,128)(2,1)S(1)}, u32[]{:S(2)}, u32[]{:S(2)}) collective-permute-start(bf16[384,128]{1,0:T(8,128)(2,1)} %get-tuple-element.43), channel_id=1, source_target_pairs={{0,3},{1,0},{2,1},{3,2},{4,7},{5,4},{6,5},{7,6},{8,11},{9,8},{10,9... | collective-permute-start | bytes 294920 | tf_op jit(solution)/shard_map/ppermute | solution.py:43
  123.7 6.2 %shard_map.158 = (f32[384,128]{1,0:T(8,128)}, f32[384,128]{1,0:T(8,128)}) custom-call(s32[2]{0:T(128)} %pad_add_fusion.at_ref, s32[2]{0:T(128)} %get-tuple-element.69.owner_ref, bf16[1536,3072]{1,0:T(8,128)(2,1)} %a_ref.24, bf16[384,128]{1,0:T(8,128)(2,1)} %copy-done.5, bf16[384,128]{1,0:T(8,128)(2,1)} %copy-done.28, bf16[384,128]{1,0:T(8,128)(2,1)} %copy-done.25, ...), custom_call_target="tpu_custom_call" | custom-call | flops 603979776 | bytes 4718592 | tf_op jit(solution)/shard_map/pallas_call | solution.py:225
  131.5 6.3 %shard_map.152 = (bf16[384,256]{1,0:T(8,128)(2,1)}, bf16[384,256]{1,0:T(8,128)(2,1)}) custom-call(s32[2]{0:T(128)} %pad_add_fusion.at_ref, s32[2]{0:T(128)} %get-tuple-element.68.owner_ref, bf16[1536,3072]{1,0:T(8,128)(2,1)} %a_ref.24, bf16[384,256]{1,0:T(8,128)(2,1)} %copy-done, bf16[384,256]{1,0:T(8,128)(2,1)} %copy-done.17, bf16[384,256]{1,0:T(8,128)(2,1)} %copy-done.10, ...), custom_call_target="tpu_custom_call" | custom-call | flops 1207959552 | bytes 4718592 | tf_op jit(solution)/shard_map/pallas_call | solution.py:225
  137.8 3.9 %collective-permute-start.17 = (bf16[384,256]{1,0:T(8,128)(2,1)}, bf16[384,256]{1,0:T(8,128)(2,1)S(1)}, u32[]{:S(2)}, u32[]{:S(2)}) collective-permute-start(bf16[384,256]{1,0:T(8,128)(2,1)} %get-tuple-element.31), channel_id=1, source_target_pairs={{0,3},{1,0},{2,1},{3,2},{4,7},{5,4},{6,5},{7,6},{8,11},{9,8},{10,9... | collective-permute-start | bytes 589832 | tf_op jit(solution)/shard_map/ppermute | solution.py:43
  141.8 2.0 collective-permute-start.19
  143.8 6.4 %shard_map.151 = (f32[384,256]{1,0:T(8,128)}, f32[384,256]{1,0:T(8,128)}) custom-call(s32[2]{0:T(128)} %pad_add_fusion.at_ref, s32[2]{0:T(128)} %get-tuple-element.69.owner_ref, bf16[1536,3072]{1,0:T(8,128)(2,1)} %a_ref.24, bf16[384,256]{1,0:T(8,128)(2,1)} %copy-done, bf16[384,256]{1,0:T(8,128)(2,1)} %copy-done.17, bf16[384,256]{1,0:T(8,128)(2,1)} %copy-done.10, ...), custom_call_target="tpu_custom_call" | custom-call | flops 1207959552 | bytes 4718592 | tf_op jit(solution)/shard_map/pallas_call | solution.py:225
  151.3 1.9 collective-permute-start.18
  153.3 4.1 %collective-permute-done.18 = bf16[384,256]{1,0:T(8,128)(2,1)S(1)} collective-permute-done((bf16[384,256]{1,0:T(8,128)(2,1)S(1)}, bf16[384,256]{1,0:T(8,128)(2,1)S(1)}, u32[]{:S(2)}, u32[]{:S(2)}) %collective-permute-start.18) | collective-permute-done | bytes 196640 | tf_op jit(solution)/shard_map/ppermute | solution.py:43
  159.8 6.1 %collective-permute-start.58 = (bf16[96,128]{1,0:T(8,128)(2,1)S(1)}, bf16[96,128]{1,0:T(8,128)(2,1)S(1)}, u32[]{:S(2)}, u32[]{:S(2)}) collective-permute-start(bf16[96,128]{1,0:T(8,128)(2,1)S(1)} %get-tuple-element.66), channel_id=1, source_target_pairs={{0,8},{1,0},{2,24},{3,16},{4,12},{5,4},{6,28},{7,20},{8,9},{9,1},{... | collective-permute-start | bytes 73736 | tf_op jit(solution)/shard_map/ppermute | solution.py:345
  166.0 2.6 collective-permute-start.59
  168.6 1.4 collective-permute-start.21
  171.0 7.9 %collective-permute-done.21 = bf16[96,256]{1,0:T(8,128)(2,1)S(1)} collective-permute-done((bf16[96,256]{1,0:T(8,128)(2,1)S(1)}, bf16[96,256]{1,0:T(8,128)(2,1)S(1)}, u32[]{:S(2)}, u32[]{:S(2)}) %collective-permute-start.21) | collective-permute-done | bytes 49184 | tf_op jit(solution)/shard_map/ppermute | solution.py:345
  178.9 5.9 %collective-permute-done.23 = bf16[96,256]{1,0:T(8,128)(2,1)S(1)} collective-permute-done((bf16[96,256]{1,0:T(8,128)(2,1)S(1)}, bf16[96,256]{1,0:T(8,128)(2,1)S(1)}, u32[]{:S(2)}, u32[]{:S(2)}) %collective-permute-start.23) | collective-permute-done | bytes 49184 | tf_op jit(solution)/shard_map/ppermute | solution.py:345
  185.3 3.0 %collective-permute-start.29 = (bf16[384,256]{1,0:T(8,128)(2,1)S(1)}, bf16[384,256]{1,0:T(8,128)(2,1)S(1)}, u32[]{:S(2)}, u32[]{:S(2)}) collective-permute-start(bf16[384,256]{1,0:T(8,128)(2,1)S(1)} %constant_dynamic-update-slice_fusion.refs_0_), channel_id=1, source_target_pairs={{0,24},{4,28},{8,16},{12,20},{16,8},{20,12},{24,0},{28,4},{1,25},{... | collective-permute-start | bytes 589832 | tf_op jit(solution)/shard_map/ppermute | solution.py:47
  188.6 2.8 %collective-permute-done.25.refs_2_ = bf16[384,256]{1,0:T(8,128)(2,1)S(1)} collective-permute-done((bf16[384,256]{1,0:T(8,128)(2,1)S(1)}, bf16[384,256]{1,0:T(8,128)(2,1)S(1)}, u32[]{:S(2)}, u32[]{:S(2)}) %collective-permute-start.25) | collective-permute-done | bytes 196640 | tf_op jit(solution)/shard_map/ppermute | solution.py:47
  191.4 2.2 collective-permute-done.27.refs_4_
  194.1 1.7 collective-permute-start.62
  199.0 5.9 %shard_map.154 = (bf16[256,512]{1,0:T(8,128)(2,1)}, bf16[256,512]{1,0:T(8,128)(2,1)}) custom-call(s32[2]{0:T(128)} %pad_add_fusion.at_ref, s32[12]{0:T(128)} %subtract_bitcast_fusion.index_ref, s32[2]{0:T(128)} %get-tuple-element.68.owner_ref, bf16[1536,2048]{1,0:T(8,128)(2,1)} %a_ref.26, bf16[384,256]{1,0:T(8,128)(2,1)} %copy-done.4, ...), custom_call_target="tpu_custom_call" | custom-call | flops 805306368 | bytes 3145728 | tf_op jit(solution)/shard_map/pallas_call | solution.py:285
  204.9 2.5 collective-permute-start.31
  210.5 5.1 %shard_map.161 = (bf16[128,512]{1,0:T(8,128)(2,1)}, bf16[128,512]{1,0:T(8,128)(2,1)}) custom-call(s32[2]{0:T(128)} %pad_add_fusion.at_ref, s32[12]{0:T(128)} %subtract_bitcast_fusion.index_ref, s32[2]{0:T(128)} %get-tuple-element.68.owner_ref, bf16[1536,2048]{1,0:T(8,128)(2,1)} %a_ref.26, bf16[384,128]{1,0:T(8,128)(2,1)} %copy-done.24, ...), custom_call_target="tpu_custom_call" | custom-call | flops 402653184 | bytes 3145728 | tf_op jit(solution)/shard_map/pallas_call | solution.py:285
  215.8 1.9 collective-permute-start.70
  217.8 6.1 %shard_map.153 = (f32[256,512]{1,0:T(8,128)}, f32[256,512]{1,0:T(8,128)}) custom-call(s32[2]{0:T(128)} %pad_add_fusion.at_ref, s32[12]{0:T(128)} %subtract_bitcast_fusion.index_ref, s32[2]{0:T(128)} %get-tuple-element.69.owner_ref, bf16[1536,2048]{1,0:T(8,128)(2,1)} %a_ref.26, bf16[384,256]{1,0:T(8,128)(2,1)} %copy-done.4, bf16[384,256]{1,0:T(8,128)(2,1)} %copy-done.12, ...), custom_call_target="tpu_custom_call" | custom-call | flops 805306368 | bytes 3145728 | tf_op jit(solution)/shard_map/pallas_call | solution.py:285
  225.0 3.8 %collective-permute-start.32 = (bf16[256,512]{1,0:T(8,128)(2,1)S(1)}, bf16[256,512]{1,0:T(8,128)(2,1)S(1)}, u32[]{:S(2)}, u32[]{:S(2)}) collective-permute-start(bf16[256,512]{1,0:T(8,128)(2,1)S(1)} %add_convert_fusion.1), channel_id=1, source_target_pairs={{0,3},{1,0},{2,1},{3,2},{4,7},{5,4},{6,5},{7,6},{8,11},{9,8},{10,9... | collective-permute-start | bytes 786440 | tf_op jit(solution)/shard_map/ppermute | solution.py:43
  228.8 5.2 %shard_map.160 = (f32[128,512]{1,0:T(8,128)}, f32[128,512]{1,0:T(8,128)}) custom-call(s32[2]{0:T(128)} %pad_add_fusion.at_ref, s32[12]{0:T(128)} %subtract_bitcast_fusion.index_ref, s32[2]{0:T(128)} %get-tuple-element.69.owner_ref, bf16[1536,2048]{1,0:T(8,128)(2,1)} %a_ref.26, bf16[384,128]{1,0:T(8,128)(2,1)} %copy-done.24, bf16[384,128]{1,0:T(8,128)(2,1)} %copy-done.36, ...), custom_call_target="tpu_custom_call" | custom-call | flops 402653184 | bytes 3145728 | tf_op jit(solution)/shard_map/pallas_call | solution.py:285
  235.6 1.7 collective-permute-start.34
  237.3 10.3 %collective-permute-done.69 = bf16[128,512]{1,0:T(8,128)(2,1)S(1)} collective-permute-done((bf16[128,512]{1,0:T(8,128)(2,1)S(1)}, bf16[128,512]{1,0:T(8,128)(2,1)S(1)}, u32[]{:S(2)}, u32[]{:S(2)}) %collective-permute-start.69) | collective-permute-done | bytes 131104 | tf_op jit(solution)/shard_map/ppermute | solution.py:43
  248.7 3.8 %collective-permute-start.72 = (bf16[128,512]{1,0:T(8,128)(2,1)S(1)}, bf16[128,512]{1,0:T(8,128)(2,1)S(1)}, u32[]{:S(2)}, u32[]{:S(2)}) collective-permute-start(bf16[128,512]{1,0:T(8,128)(2,1)S(1)} %add_convert_fusion.6.refs_0_), channel_id=1, source_target_pairs={{0,3},{1,0},{2,1},{3,2},{4,7},{5,4},{6,5},{7,6},{8,11},{9,8},{10,9... | collective-permute-start | bytes 393224 | tf_op jit(solution)/shard_map/ppermute | solution.py:43
  252.5 4.3 %collective-permute-done.71.refs_1_ = bf16[128,512]{1,0:T(8,128)(2,1)S(1)} collective-permute-done((bf16[128,512]{1,0:T(8,128)(2,1)S(1)}, bf16[128,512]{1,0:T(8,128)(2,1)S(1)}, u32[]{:S(2)}, u32[]{:S(2)}) %collective-permute-start.71) | collective-permute-done | bytes 131104 | tf_op jit(solution)/shard_map/ppermute | solution.py:43
  256.8 3.8 %collective-permute-start.35 = (bf16[256,512]{1,0:T(8,128)(2,1)S(1)}, bf16[256,512]{1,0:T(8,128)(2,1)S(1)}, u32[]{:S(2)}, u32[]{:S(2)}) collective-permute-start(bf16[256,512]{1,0:T(8,128)(2,1)S(1)} %add_convert_fusion.refs_0_), channel_id=1, source_target_pairs={{0,3},{1,0},{2,1},{3,2},{4,7},{5,4},{6,5},{7,6},{8,11},{9,8},{10,9... | collective-permute-start | bytes 786440 | tf_op jit(solution)/shard_map/ppermute | solution.py:43
  260.6 3.1 %collective-permute-done.73.refs_3_ = bf16[128,512]{1,0:T(8,128)(2,1)S(1)} collective-permute-done((bf16[128,512]{1,0:T(8,128)(2,1)S(1)}, bf16[128,512]{1,0:T(8,128)(2,1)S(1)}, u32[]{:S(2)}, u32[]{:S(2)}) %collective-permute-start.73) | collective-permute-done | bytes 131104 | tf_op jit(solution)/shard_map/ppermute | solution.py:43
  264.4 3.8 %shard_map.162 = f32[512,128]{1,0:T(8,128)} custom-call(s32[2]{0:T(128)} %pad_add_fusion.at_ref, bf16[512,2048]{1,0:T(8,128)(2,1)} %a_ref.27, f32[512,128]{1,0:T(8,128)} %get-tuple-element.38.inner_ref, bf16[128,512]{1,0:T(8,128)(2,1)} %copy-done.23, bf16[128,512]{1,0:T(8,128)(2,1)} %copy-done.57, bf16[128,512]{1,0:T(8,128)(2,1)} %copy-done.58, ...), custom_call_target="tpu_custom_call" | custom-call | flops 268435456 | bytes 2097152 | tf_op jit(solution)/shard_map/pallas_call | solution.py:133
  269.9 4.2 %shard_map.155 = f32[512,256]{1,0:T(8,128)} custom-call(s32[2]{0:T(128)} %pad_add_fusion.at_ref, bf16[512,2048]{1,0:T(8,128)(2,1)} %a_ref.27, f32[512,256]{1,0:T(8,128)} %get-tuple-element.26.inner_ref, bf16[256,512]{1,0:T(8,128)(2,1)} %copy-done.1, bf16[256,512]{1,0:T(8,128)(2,1)} %copy-done.41, bf16[256,512]{1,0:T(8,128)(2,1)} %copy-done.44, ...), custom_call_target="tpu_custom_call" | custom-call | flops 536870912 | bytes 2097152 | tf_op jit(solution)/shard_map/pallas_call | solution.py:133
  274.1 2.0 pad_maximum_fusion
  (261 shorter events, 37.0 us)
Async XLA Ops:
  1.6 12.3 %collective-permute-start = (bf16[512,256]{1,0:T(8,128)(2,1)S(1)}, bf16[512,256]{1,0:T(8,128)(2,1)S(1)}, u32[]{:S(2)}, u32[]{:S(2)}) collective-permute-start(bf16[512,256]{1,0:T(8,128)(2,1)S(1)} %slice.84.refs_0_), channel_id=1, source_target_pairs={{0,1},{1,2},{2,3},{3,0},{4,5},{5,6},{6,7},{7,4},{8,9},{9,10},{10,1... | collective-permute-start | bytes 786440 | tf_op jit(solution)/shard_map/ppermute | solution.py:43
  4.7 13.6 %collective-permute-start.1 = (bf16[512,256]{1,0:T(8,128)(2,1)S(1)}, bf16[512,256]{1,0:T(8,128)(2,1)S(1)}, u32[]{:S(2)}, u32[]{:S(2)}) collective-permute-start(bf16[512,256]{1,0:T(8,128)(2,1)S(1)} %slice.84.refs_0_), channel_id=1, source_target_pairs={{0,3},{1,0},{2,1},{3,2},{4,7},{5,4},{6,5},{7,6},{8,11},{9,8},{10,9... | collective-permute-start | bytes 786440 | tf_op jit(solution)/shard_map/ppermute | solution.py:43
  13.9 10.4 %collective-permute-start.2 = (bf16[512,256]{1,0:T(8,128)(2,1)S(1)}, bf16[512,256]{1,0:T(8,128)(2,1)S(1)}, u32[]{:S(2)}, u32[]{:S(2)}) collective-permute-start(bf16[512,256]{1,0:T(8,128)(2,1)S(1)} %collective-permute-done.refs_1_), channel_id=1, source_target_pairs={{0,1},{1,2},{2,3},{3,0},{4,5},{5,6},{6,7},{7,4},{8,9},{9,10},{10,1... | collective-permute-start | bytes 786440 | tf_op jit(solution)/shard_map/ppermute | solution.py:43
  29.2 16.2 %collective-permute-start.3 = (bf16[512,256]{1,0:T(8,128)(2,1)}, bf16[512,256]{1,0:T(8,128)(2,1)S(1)}, u32[]{:S(2)}, u32[]{:S(2)}) collective-permute-start(bf16[512,256]{1,0:T(8,128)(2,1)} %get-tuple-element.27.refs_0_), channel_id=1, source_target_pairs={{0,1},{1,2},{2,3},{3,0},{4,5},{5,6},{6,7},{7,4},{8,9},{9,10},{10,1... | collective-permute-start | bytes 786440 | tf_op jit(solution)/shard_map/ppermute | solution.py:43
  30.1 11.5 %collective-permute-start.37 = (bf16[512,128]{1,0:T(8,128)(2,1)S(1)}, bf16[512,128]{1,0:T(8,128)(2,1)S(1)}, u32[]{:S(2)}, u32[]{:S(2)}) collective-permute-start(bf16[512,128]{1,0:T(8,128)(2,1)S(1)} %slice.98.refs_0_), channel_id=1, source_target_pairs={{0,1},{1,2},{2,3},{3,0},{4,5},{5,6},{6,7},{7,4},{8,9},{9,10},{10,1... | collective-permute-start | bytes 393224 | tf_op jit(solution)/shard_map/ppermute | solution.py:43
  31.4 14.0 %collective-permute-start.38 = (bf16[512,128]{1,0:T(8,128)(2,1)S(1)}, bf16[512,128]{1,0:T(8,128)(2,1)S(1)}, u32[]{:S(2)}, u32[]{:S(2)}) collective-permute-start(bf16[512,128]{1,0:T(8,128)(2,1)S(1)} %slice.98.refs_0_), channel_id=1, source_target_pairs={{0,3},{1,0},{2,1},{3,2},{4,7},{5,4},{6,5},{7,6},{8,11},{9,8},{10,9... | collective-permute-start | bytes 393224 | tf_op jit(solution)/shard_map/ppermute | solution.py:43
  41.6 8.4 %collective-permute-start.39 = (bf16[512,128]{1,0:T(8,128)(2,1)S(1)}, bf16[512,128]{1,0:T(8,128)(2,1)S(1)}, u32[]{:S(2)}, u32[]{:S(2)}) collective-permute-start(bf16[512,128]{1,0:T(8,128)(2,1)S(1)} %collective-permute-done.37.refs_1_), channel_id=1, source_target_pairs={{0,1},{1,2},{2,3},{3,0},{4,5},{5,6},{6,7},{7,4},{8,9},{9,10},{10,1... | collective-permute-start | bytes 393224 | tf_op jit(solution)/shard_map/ppermute | solution.py:43
  41.6 20.9 %collective-permute-start.4 = (bf16[512,256]{1,0:T(8,128)(2,1)}, bf16[512,256]{1,0:T(8,128)(2,1)S(1)}, u32[]{:S(2)}, u32[]{:S(2)}) collective-permute-start(bf16[512,256]{1,0:T(8,128)(2,1)} %get-tuple-element.27.refs_0_), channel_id=1, source_target_pairs={{0,3},{1,0},{2,1},{3,2},{4,7},{5,4},{6,5},{7,6},{8,11},{9,8},{10,9... | collective-permute-start | bytes 786440 | tf_op jit(solution)/shard_map/ppermute | solution.py:43
  45.4 17.1 %collective-permute-start.5 = (bf16[512,256]{1,0:T(8,128)(2,1)S(1)}, bf16[512,256]{1,0:T(8,128)(2,1)S(1)}, u32[]{:S(2)}, u32[]{:S(2)}) collective-permute-start(bf16[512,256]{1,0:T(8,128)(2,1)S(1)} %collective-permute-done.3.refs_1_), channel_id=1, source_target_pairs={{0,1},{1,2},{2,3},{3,0},{4,5},{5,6},{6,7},{7,4},{8,9},{9,10},{10,1... | collective-permute-start | bytes 786440 | tf_op jit(solution)/shard_map/ppermute | solution.py:43
  54.5 8.0 %collective-permute-start.40 = (bf16[512,128]{1,0:T(8,128)(2,1)}, bf16[512,128]{1,0:T(8,128)(2,1)S(1)}, u32[]{:S(2)}, u32[]{:S(2)}) collective-permute-start(bf16[512,128]{1,0:T(8,128)(2,1)} %get-tuple-element.39.refs_0_), channel_id=1, source_target_pairs={{0,1},{1,2},{2,3},{3,0},{4,5},{5,6},{6,7},{7,4},{8,9},{9,10},{10,1... | collective-permute-start | bytes 393224 | tf_op jit(solution)/shard_map/ppermute | solution.py:43
  55.0 15.8 %collective-permute-start.41 = (bf16[512,128]{1,0:T(8,128)(2,1)}, bf16[512,128]{1,0:T(8,128)(2,1)S(1)}, u32[]{:S(2)}, u32[]{:S(2)}) collective-permute-start(bf16[512,128]{1,0:T(8,128)(2,1)} %get-tuple-element.39.refs_0_), channel_id=1, source_target_pairs={{0,3},{1,0},{2,1},{3,2},{4,7},{5,4},{6,5},{7,6},{8,11},{9,8},{10,9... | collective-permute-start | bytes 393224 | tf_op jit(solution)/shard_map/ppermute | solution.py:43
  62.5 8.4 %collective-permute-start.42 = (bf16[512,128]{1,0:T(8,128)(2,1)S(1)}, bf16[512,128]{1,0:T(8,128)(2,1)S(1)}, u32[]{:S(2)}, u32[]{:S(2)}) collective-permute-start(bf16[512,128]{1,0:T(8,128)(2,1)S(1)} %collective-permute-done.40.refs_1_), channel_id=1, source_target_pairs={{0,1},{1,2},{2,3},{3,0},{4,5},{5,6},{6,7},{7,4},{8,9},{9,10},{10,1... | collective-permute-start | bytes 393224 | tf_op jit(solution)/shard_map/ppermute | solution.py:43
  70.9 14.7 %collective-permute-start.6 = (bf16[1536,256]{1,0:T(8,128)(2,1)}, bf16[1536,256]{1,0:T(8,128)(2,1)S(1)}, u32[]{:S(2)}, u32[]{:S(2)}) collective-permute-start(bf16[1536,256]{1,0:T(8,128)(2,1)} %get-tuple-element.29), channel_id=1, source_target_pairs={{0,4},{4,0},{8,12},{12,8},{16,20},{20,16},{24,28},{28,24},{1,5},{5... | collective-permute-start | bytes 2359304 | tf_op jit(solution)/shard_map/ppermute | solution.py:47
  82.0 6.8 %collective-permute-start.44 = (bf16[384,128]{1,0:T(8,128)(2,1)S(1)}, bf16[384,128]{1,0:T(8,128)(2,1)S(1)}, u32[]{:S(2)}, u32[]{:S(2)}) collective-permute-start(bf16[384,128]{1,0:T(8,128)(2,1)S(1)} %get-tuple-element.57), channel_id=1, source_target_pairs={{0,8},{4,12},{8,0},{12,4},{16,24},{20,28},{24,16},{28,20},{1,9},{5... | collective-permute-start | bytes 294920 | tf_op jit(solution)/shard_map/ppermute | solution.py:47
  83.6 6.6 %collective-permute-start.45 = (bf16[384,128]{1,0:T(8,128)(2,1)S(1)}, bf16[384,128]{1,0:T(8,128)(2,1)S(1)}, u32[]{:S(2)}, u32[]{:S(2)}) collective-permute-start(bf16[384,128]{1,0:T(8,128)(2,1)S(1)} %get-tuple-element.59), channel_id=1, source_target_pairs={{0,16},{4,20},{8,24},{12,28},{16,0},{20,4},{24,8},{28,12},{1,17},{... | collective-permute-start | bytes 294920 | tf_op jit(solution)/shard_map/ppermute | solution.py:47
  85.1 6.6 %collective-permute-start.46 = (bf16[384,128]{1,0:T(8,128)(2,1)S(1)}, bf16[384,128]{1,0:T(8,128)(2,1)S(1)}, u32[]{:S(2)}, u32[]{:S(2)}) collective-permute-start(bf16[384,128]{1,0:T(8,128)(2,1)S(1)} %get-tuple-element.58), channel_id=1, source_target_pairs={{0,24},{4,28},{8,16},{12,20},{16,8},{20,12},{24,0},{28,4},{1,25},{... | collective-permute-start | bytes 294920 | tf_op jit(solution)/shard_map/ppermute | solution.py:47
  85.7 9.3 %collective-permute-start.7 = (bf16[384,256]{1,0:T(8,128)(2,1)S(1)}, bf16[384,256]{1,0:T(8,128)(2,1)S(1)}, u32[]{:S(2)}, u32[]{:S(2)}) collective-permute-start(bf16[384,256]{1,0:T(8,128)(2,1)S(1)} %get-tuple-element.54), channel_id=1, source_target_pairs={{0,8},{4,12},{8,0},{12,4},{16,24},{20,28},{24,16},{28,20},{1,9},{5... | collective-permute-start | bytes 589832 | tf_op jit(solution)/shard_map/ppermute | solution.py:47
  87.3 11.6 %collective-permute-start.8 = (bf16[384,256]{1,0:T(8,128)(2,1)S(1)}, bf16[384,256]{1,0:T(8,128)(2,1)S(1)}, u32[]{:S(2)}, u32[]{:S(2)}) collective-permute-start(bf16[384,256]{1,0:T(8,128)(2,1)S(1)} %get-tuple-element.56), channel_id=1, source_target_pairs={{0,16},{4,20},{8,24},{12,28},{16,0},{20,4},{24,8},{28,12},{1,17},{... | collective-permute-start | bytes 589832 | tf_op jit(solution)/shard_map/ppermute | solution.py:47
  88.8 11.4 %collective-permute-start.9 = (bf16[384,256]{1,0:T(8,128)(2,1)S(1)}, bf16[384,256]{1,0:T(8,128)(2,1)S(1)}, u32[]{:S(2)}, u32[]{:S(2)}) collective-permute-start(bf16[384,256]{1,0:T(8,128)(2,1)S(1)} %get-tuple-element.55), channel_id=1, source_target_pairs={{0,24},{4,28},{8,16},{12,20},{16,8},{20,12},{24,0},{28,4},{1,25},{... | collective-permute-start | bytes 589832 | tf_op jit(solution)/shard_map/ppermute | solution.py:47
  92.7 8.5 %collective-permute-start.48 = (bf16[384,128]{1,0:T(8,128)(2,1)S(1)}, bf16[384,128]{1,0:T(8,128)(2,1)S(1)}, u32[]{:S(2)}, u32[]{:S(2)}) collective-permute-start(bf16[384,128]{1,0:T(8,128)(2,1)S(1)} %subtract_convert_fusion.1.refs_0_), channel_id=1, source_target_pairs={{0,8},{4,12},{8,0},{12,4},{16,24},{20,28},{24,16},{28,20},{1,9},{5... | collective-permute-start | bytes 294920 | tf_op jit(solution)/shard_map/ppermute | solution.py:47
  93.3 9.3 %collective-permute-start.50 = (bf16[384,128]{1,0:T(8,128)(2,1)S(1)}, bf16[384,128]{1,0:T(8,128)(2,1)S(1)}, u32[]{:S(2)}, u32[]{:S(2)}) collective-permute-start(bf16[384,128]{1,0:T(8,128)(2,1)S(1)} %subtract_convert_fusion.1.refs_0_), channel_id=1, source_target_pairs={{0,16},{4,20},{8,24},{12,28},{16,0},{20,4},{24,8},{28,12},{1,17},{... | collective-permute-start | bytes 294920 | tf_op jit(solution)/shard_map/ppermute | solution.py:47
  95.0 9.5 %collective-permute-start.52 = (bf16[384,128]{1,0:T(8,128)(2,1)S(1)}, bf16[384,128]{1,0:T(8,128)(2,1)S(1)}, u32[]{:S(2)}, u32[]{:S(2)}) collective-permute-start(bf16[384,128]{1,0:T(8,128)(2,1)S(1)} %subtract_convert_fusion.1.refs_0_), channel_id=1, source_target_pairs={{0,24},{4,28},{8,16},{12,20},{16,8},{20,12},{24,0},{28,4},{1,25},{... | collective-permute-start | bytes 294920 | tf_op jit(solution)/shard_map/ppermute | solution.py:47
  98.9 5.7 %collective-permute-start.47 = (bf16[384,128]{1,0:T(8,128)(2,1)S(1)}, bf16[384,128]{1,0:T(8,128)(2,1)S(1)}, u32[]{:S(2)}, u32[]{:S(2)}) collective-permute-start(bf16[384,128]{1,0:T(8,128)(2,1)S(1)} %subtract_convert_fusion.1.refs_0_), channel_id=1, source_target_pairs={{0,4},{4,0},{8,12},{12,8},{16,20},{20,16},{24,28},{28,24},{1,5},{5... | collective-permute-start | bytes 294920 | tf_op jit(solution)/shard_map/ppermute | solution.py:47
  100.4 6.2 %collective-permute-start.11 = (bf16[384,256]{1,0:T(8,128)(2,1)S(1)}, bf16[384,256]{1,0:T(8,128)(2,1)S(1)}, u32[]{:S(2)}, u32[]{:S(2)}) collective-permute-start(bf16[384,256]{1,0:T(8,128)(2,1)S(1)} %subtract_convert_fusion.refs_0_), channel_id=1, source_target_pairs={{0,8},{4,12},{8,0},{12,4},{16,24},{20,28},{24,16},{28,20},{1,9},{5... | collective-permute-start | bytes 589832 | tf_op jit(solution)/shard_map/ppermute | solution.py:47
  101.2 9.6 %collective-permute-start.13 = (bf16[384,256]{1,0:T(8,128)(2,1)S(1)}, bf16[384,256]{1,0:T(8,128)(2,1)S(1)}, u32[]{:S(2)}, u32[]{:S(2)}) collective-permute-start(bf16[384,256]{1,0:T(8,128)(2,1)S(1)} %subtract_convert_fusion.refs_0_), channel_id=1, source_target_pairs={{0,16},{4,20},{8,24},{12,28},{16,0},{20,4},{24,8},{28,12},{1,17},{... | collective-permute-start | bytes 589832 | tf_op jit(solution)/shard_map/ppermute | solution.py:47
  102.6 10.0 %collective-permute-start.15 = (bf16[384,256]{1,0:T(8,128)(2,1)S(1)}, bf16[384,256]{1,0:T(8,128)(2,1)S(1)}, u32[]{:S(2)}, u32[]{:S(2)}) collective-permute-start(bf16[384,256]{1,0:T(8,128)(2,1)S(1)} %subtract_convert_fusion.refs_0_), channel_id=1, source_target_pairs={{0,24},{4,28},{8,16},{12,20},{16,8},{20,12},{24,0},{28,4},{1,25},{... | collective-permute-start | bytes 589832 | tf_op jit(solution)/shard_map/ppermute | solution.py:47
  105.8 7.4 %collective-permute-start.53 = (bf16[384,128]{1,0:T(8,128)(2,1)S(1)}, bf16[384,128]{1,0:T(8,128)(2,1)S(1)}, u32[]{:S(2)}, u32[]{:S(2)}) collective-permute-start(bf16[384,128]{1,0:T(8,128)(2,1)S(1)} %collective-permute-done.52.refs_6_), channel_id=1, source_target_pairs={{0,4},{4,0},{8,12},{12,8},{16,20},{20,16},{24,28},{28,24},{1,5},{5... | collective-permute-start | bytes 294920 | tf_op jit(solution)/shard_map/ppermute | solution.py:47
  106.0 23.9 %collective-permute-start.10 = (bf16[384,256]{1,0:T(8,128)(2,1)S(1)}, bf16[384,256]{1,0:T(8,128)(2,1)S(1)}, u32[]{:S(2)}, u32[]{:S(2)}) collective-permute-start(bf16[384,256]{1,0:T(8,128)(2,1)S(1)} %subtract_convert_fusion.refs_0_), channel_id=1, source_target_pairs={{0,4},{4,0},{8,12},{12,8},{16,20},{20,16},{24,28},{28,24},{1,5},{5... | collective-permute-start | bytes 589832 | tf_op jit(solution)/shard_map/ppermute | solution.py:47
  106.6 23.4 %collective-permute-start.12 = (bf16[384,256]{1,0:T(8,128)(2,1)S(1)}, bf16[384,256]{1,0:T(8,128)(2,1)S(1)}, u32[]{:S(2)}, u32[]{:S(2)}) collective-permute-start(bf16[384,256]{1,0:T(8,128)(2,1)S(1)} %collective-permute-done.11.refs_2_), channel_id=1, source_target_pairs={{0,4},{4,0},{8,12},{12,8},{16,20},{20,16},{24,28},{28,24},{1,5},{5... | collective-permute-start | bytes 589832 | tf_op jit(solution)/shard_map/ppermute | solution.py:47
  110.8 19.3 %collective-permute-start.14 = (bf16[384,256]{1,0:T(8,128)(2,1)S(1)}, bf16[384,256]{1,0:T(8,128)(2,1)S(1)}, u32[]{:S(2)}, u32[]{:S(2)}) collective-permute-start(bf16[384,256]{1,0:T(8,128)(2,1)S(1)} %collective-permute-done.13.refs_4_), channel_id=1, source_target_pairs={{0,4},{4,0},{8,12},{12,8},{16,20},{20,16},{24,28},{28,24},{1,5},{5... | collective-permute-start | bytes 589832 | tf_op jit(solution)/shard_map/ppermute | solution.py:47
  112.6 17.5 %collective-permute-start.16 = (bf16[384,256]{1,0:T(8,128)(2,1)S(1)}, bf16[384,256]{1,0:T(8,128)(2,1)S(1)}, u32[]{:S(2)}, u32[]{:S(2)}) collective-permute-start(bf16[384,256]{1,0:T(8,128)(2,1)S(1)} %collective-permute-done.15.refs_6_), channel_id=1, source_target_pairs={{0,4},{4,0},{8,12},{12,8},{16,20},{20,16},{24,28},{28,24},{1,5},{5... | collective-permute-start | bytes 589832 | tf_op jit(solution)/shard_map/ppermute | solution.py:47
  119.9 21.7 %collective-permute-start.54 = (bf16[384,128]{1,0:T(8,128)(2,1)}, bf16[384,128]{1,0:T(8,128)(2,1)S(1)}, u32[]{:S(2)}, u32[]{:S(2)}) collective-permute-start(bf16[384,128]{1,0:T(8,128)(2,1)} %get-tuple-element.43), channel_id=1, source_target_pairs={{0,3},{1,0},{2,1},{3,2},{4,7},{5,4},{6,5},{7,6},{8,11},{9,8},{10,9... | collective-permute-start | bytes 294920 | tf_op jit(solution)/shard_map/ppermute | solution.py:43
  130.0 23.2 %collective-permute-start.56 = (bf16[384,128]{1,0:T(8,128)(2,1)S(1)}, bf16[384,128]{1,0:T(8,128)(2,1)S(1)}, u32[]{:S(2)}, u32[]{:S(2)}) collective-permute-start(bf16[384,128]{1,0:T(8,128)(2,1)S(1)} %copy-done.63), channel_id=1, source_target_pairs={{0,1},{1,2},{2,3},{3,0},{4,5},{5,6},{6,7},{7,4},{8,9},{9,10},{10,1... | collective-permute-start | bytes 294920 | tf_op jit(solution)/shard_map/ppermute | solution.py:43
  137.8 12.4 %collective-permute-start.17 = (bf16[384,256]{1,0:T(8,128)(2,1)}, bf16[384,256]{1,0:T(8,128)(2,1)S(1)}, u32[]{:S(2)}, u32[]{:S(2)}) collective-permute-start(bf16[384,256]{1,0:T(8,128)(2,1)} %get-tuple-element.31), channel_id=1, source_target_pairs={{0,3},{1,0},{2,1},{3,2},{4,7},{5,4},{6,5},{7,6},{8,11},{9,8},{10,9... | collective-permute-start | bytes 589832 | tf_op jit(solution)/shard_map/ppermute | solution.py:43
  141.7 11.5 %collective-permute-start.55 = (bf16[384,128]{1,0:T(8,128)(2,1)S(1)}, bf16[384,128]{1,0:T(8,128)(2,1)S(1)}, u32[]{:S(2)}, u32[]{:S(2)}) collective-permute-start(bf16[384,128]{1,0:T(8,128)(2,1)S(1)} %add_convert_fusion.8), channel_id=1, source_target_pairs={{0,3},{1,0},{2,1},{3,2},{4,7},{5,4},{6,5},{7,6},{8,11},{9,8},{10,9... | collective-permute-start | bytes 294920 | tf_op jit(solution)/shard_map/ppermute | solution.py:43
  141.8 11.5 %collective-permute-start.19 = (bf16[384,256]{1,0:T(8,128)(2,1)}, bf16[384,256]{1,0:T(8,128)(2,1)S(1)}, u32[]{:S(2)}, u32[]{:S(2)}) collective-permute-start(bf16[384,256]{1,0:T(8,128)(2,1)} %get-tuple-element.33), channel_id=1, source_target_pairs={{0,1},{1,2},{2,3},{3,0},{4,5},{5,6},{6,7},{7,4},{8,9},{9,10},{10,1... | collective-permute-start | bytes 589832 | tf_op jit(solution)/shard_map/ppermute | solution.py:43
  151.3 6.1 %collective-permute-start.18 = (bf16[384,256]{1,0:T(8,128)(2,1)S(1)}, bf16[384,256]{1,0:T(8,128)(2,1)S(1)}, u32[]{:S(2)}, u32[]{:S(2)}) collective-permute-start(bf16[384,256]{1,0:T(8,128)(2,1)S(1)} %add_convert_fusion.2), channel_id=1, source_target_pairs={{0,3},{1,0},{2,1},{3,2},{4,7},{5,4},{6,5},{7,6},{8,11},{9,8},{10,9... | collective-permute-start | bytes 589832 | tf_op jit(solution)/shard_map/ppermute | solution.py:43
  158.5 11.5 %collective-permute-start.20 = (bf16[96,256]{1,0:T(8,128)(2,1)S(1)}, bf16[96,256]{1,0:T(8,128)(2,1)S(1)}, u32[]{:S(2)}, u32[]{:S(2)}) collective-permute-start(bf16[96,256]{1,0:T(8,128)(2,1)S(1)} %get-tuple-element.63), channel_id=1, source_target_pairs={{0,0},{1,8},{2,16},{3,24},{4,4},{5,12},{6,20},{7,28},{8,1},{9,9},{... | collective-permute-start | bytes 147464 | tf_op jit(solution)/shard_map/ppermute | solution.py:345
  159.2 26.1 %collective-permute-start.57 = (bf16[96,128]{1,0:T(8,128)(2,1)S(1)}, bf16[96,128]{1,0:T(8,128)(2,1)S(1)}, u32[]{:S(2)}, u32[]{:S(2)}) collective-permute-start(bf16[96,128]{1,0:T(8,128)(2,1)S(1)} %get-tuple-element.67), channel_id=1, source_target_pairs={{0,0},{1,8},{2,16},{3,24},{4,4},{5,12},{6,20},{7,28},{8,1},{9,9},{... | collective-permute-start | bytes 73736 | tf_op jit(solution)/shard_map/ppermute | solution.py:345
  159.8 28.4 %collective-permute-start.58 = (bf16[96,128]{1,0:T(8,128)(2,1)S(1)}, bf16[96,128]{1,0:T(8,128)(2,1)S(1)}, u32[]{:S(2)}, u32[]{:S(2)}) collective-permute-start(bf16[96,128]{1,0:T(8,128)(2,1)S(1)} %get-tuple-element.66), channel_id=1, source_target_pairs={{0,8},{1,0},{2,24},{3,16},{4,12},{5,4},{6,28},{7,20},{8,9},{9,1},{... | collective-permute-start | bytes 73736 | tf_op jit(solution)/shard_map/ppermute | solution.py:345
  166.0 22.6 %collective-permute-start.59 = (bf16[96,128]{1,0:T(8,128)(2,1)S(1)}, bf16[96,128]{1,0:T(8,128)(2,1)S(1)}, u32[]{:S(2)}, u32[]{:S(2)}) collective-permute-start(bf16[96,128]{1,0:T(8,128)(2,1)S(1)} %get-tuple-element.65), channel_id=1, source_target_pairs={{0,16},{1,24},{2,0},{3,8},{4,20},{5,28},{6,4},{7,12},{8,17},{9,25}... | collective-permute-start | bytes 73736 | tf_op jit(solution)/shard_map/ppermute | solution.py:345
  168.6 10.3 %collective-permute-start.21 = (bf16[96,256]{1,0:T(8,128)(2,1)S(1)}, bf16[96,256]{1,0:T(8,128)(2,1)S(1)}, u32[]{:S(2)}, u32[]{:S(2)}) collective-permute-start(bf16[96,256]{1,0:T(8,128)(2,1)S(1)} %get-tuple-element.62), channel_id=1, source_target_pairs={{0,8},{1,0},{2,24},{3,16},{4,12},{5,4},{6,28},{7,20},{8,9},{9,1},{... | collective-permute-start | bytes 147464 | tf_op jit(solution)/shard_map/ppermute | solution.py:345
  169.9 9.0 %collective-permute-start.22 = (bf16[96,256]{1,0:T(8,128)(2,1)S(1)}, bf16[96,256]{1,0:T(8,128)(2,1)S(1)}, u32[]{:S(2)}, u32[]{:S(2)}) collective-permute-start(bf16[96,256]{1,0:T(8,128)(2,1)S(1)} %get-tuple-element.61), channel_id=1, source_target_pairs={{0,16},{1,24},{2,0},{3,8},{4,20},{5,28},{6,4},{7,12},{8,17},{9,25}... | collective-permute-start | bytes 147464 | tf_op jit(solution)/shard_map/ppermute | solution.py:345
  178.9 5.9 %collective-permute-start.23 = (bf16[96,256]{1,0:T(8,128)(2,1)S(1)}, bf16[96,256]{1,0:T(8,128)(2,1)S(1)}, u32[]{:S(2)}, u32[]{:S(2)}) collective-permute-start(bf16[96,256]{1,0:T(8,128)(2,1)S(1)} %get-tuple-element.60), channel_id=1, source_target_pairs={{0,24},{1,16},{2,8},{3,0},{4,28},{5,20},{6,12},{7,4},{8,25},{9,17}... | collective-permute-start | bytes 147464 | tf_op jit(solution)/shard_map/ppermute | solution.py:345
  184.8 6.6 %collective-permute-start.25 = (bf16[384,256]{1,0:T(8,128)(2,1)S(1)}, bf16[384,256]{1,0:T(8,128)(2,1)S(1)}, u32[]{:S(2)}, u32[]{:S(2)}) collective-permute-start(bf16[384,256]{1,0:T(8,128)(2,1)S(1)} %constant_dynamic-update-slice_fusion.refs_0_), channel_id=1, source_target_pairs={{0,8},{4,12},{8,0},{12,4},{16,24},{20,28},{24,16},{28,20},{1,9},{5... | collective-permute-start | bytes 589832 | tf_op jit(solution)/shard_map/ppermute | solution.py:47
  184.8 8.8 %collective-permute-start.27 = (bf16[384,256]{1,0:T(8,128)(2,1)S(1)}, bf16[384,256]{1,0:T(8,128)(2,1)S(1)}, u32[]{:S(2)}, u32[]{:S(2)}) collective-permute-start(bf16[384,256]{1,0:T(8,128)(2,1)S(1)} %constant_dynamic-update-slice_fusion.refs_0_), channel_id=1, source_target_pairs={{0,16},{4,20},{8,24},{12,28},{16,0},{20,4},{24,8},{28,12},{1,17},{... | collective-permute-start | bytes 589832 | tf_op jit(solution)/shard_map/ppermute | solution.py:47
  185.3 8.3 %collective-permute-start.29 = (bf16[384,256]{1,0:T(8,128)(2,1)S(1)}, bf16[384,256]{1,0:T(8,128)(2,1)S(1)}, u32[]{:S(2)}, u32[]{:S(2)}) collective-permute-start(bf16[384,256]{1,0:T(8,128)(2,1)S(1)} %constant_dynamic-update-slice_fusion.refs_0_), channel_id=1, source_target_pairs={{0,24},{4,28},{8,16},{12,20},{16,8},{20,12},{24,0},{28,4},{1,25},{... | collective-permute-start | bytes 589832 | tf_op jit(solution)/shard_map/ppermute | solution.py:47
  188.3 5.8 %collective-permute-start.60 = (bf16[96,128]{1,0:T(8,128)(2,1)S(1)}, bf16[96,128]{1,0:T(8,128)(2,1)S(1)}, u32[]{:S(2)}, u32[]{:S(2)}) collective-permute-start(bf16[96,128]{1,0:T(8,128)(2,1)S(1)} %get-tuple-element.64), channel_id=1, source_target_pairs={{0,24},{1,16},{2,8},{3,0},{4,28},{5,20},{6,12},{7,4},{8,25},{9,17}... | collective-permute-start | bytes 73736 | tf_op jit(solution)/shard_map/ppermute | solution.py:345
  188.5 7.2 %collective-permute-start.24 = (bf16[384,256]{1,0:T(8,128)(2,1)S(1)}, bf16[384,256]{1,0:T(8,128)(2,1)S(1)}, u32[]{:S(2)}, u32[]{:S(2)}) collective-permute-start(bf16[384,256]{1,0:T(8,128)(2,1)S(1)} %constant_dynamic-update-slice_fusion.refs_0_), channel_id=1, source_target_pairs={{0,4},{4,0},{8,12},{12,8},{16,20},{20,16},{24,28},{28,24},{1,5},{5... | collective-permute-start | bytes 589832 | tf_op jit(solution)/shard_map/ppermute | solution.py:47
  194.1 13.3 %collective-permute-start.62 = (bf16[384,128]{1,0:T(8,128)(2,1)S(1)}, bf16[384,128]{1,0:T(8,128)(2,1)S(1)}, u32[]{:S(2)}, u32[]{:S(2)}) collective-permute-start(bf16[384,128]{1,0:T(8,128)(2,1)S(1)} %constant_dynamic-update-slice_fusion.4.refs_0_), channel_id=1, source_target_pairs={{0,8},{4,12},{8,0},{12,4},{16,24},{20,28},{24,16},{28,20},{1,9},{5... | collective-permute-start | bytes 294920 | tf_op jit(solution)/shard_map/ppermute | solution.py:47
  195.8 12.2 %collective-permute-start.64 = (bf16[384,128]{1,0:T(8,128)(2,1)S(1)}, bf16[384,128]{1,0:T(8,128)(2,1)S(1)}, u32[]{:S(2)}, u32[]{:S(2)}) collective-permute-start(bf16[384,128]{1,0:T(8,128)(2,1)S(1)} %constant_dynamic-update-slice_fusion.4.refs_0_), channel_id=1, source_target_pairs={{0,16},{4,20},{8,24},{12,28},{16,0},{20,4},{24,8},{28,12},{1,17},{... | collective-permute-start | bytes 294920 | tf_op jit(solution)/shard_map/ppermute | solution.py:47
  196.8 11.2 %collective-permute-start.66 = (bf16[384,128]{1,0:T(8,128)(2,1)S(1)}, bf16[384,128]{1,0:T(8,128)(2,1)S(1)}, u32[]{:S(2)}, u32[]{:S(2)}) collective-permute-start(bf16[384,128]{1,0:T(8,128)(2,1)S(1)} %constant_dynamic-update-slice_fusion.4.refs_0_), channel_id=1, source_target_pairs={{0,24},{4,28},{8,16},{12,20},{16,8},{20,12},{24,0},{28,4},{1,25},{... | collective-permute-start | bytes 294920 | tf_op jit(solution)/shard_map/ppermute | solution.py:47
  204.9 18.9 %collective-permute-start.31 = (bf16[256,512]{1,0:T(8,128)(2,1)}, bf16[256,512]{1,0:T(8,128)(2,1)S(1)}, u32[]{:S(2)}, u32[]{:S(2)}) collective-permute-start(bf16[256,512]{1,0:T(8,128)(2,1)} %get-tuple-element.35), channel_id=1, source_target_pairs={{0,3},{1,0},{2,1},{3,2},{4,7},{5,4},{6,5},{7,6},{8,11},{9,8},{10,9... | collective-permute-start | bytes 786440 | tf_op jit(solution)/shard_map/ppermute | solution.py:43
  215.7 18.4 %collective-permute-start.68 = (bf16[128,512]{1,0:T(8,128)(2,1)}, bf16[128,512]{1,0:T(8,128)(2,1)S(1)}, u32[]{:S(2)}, u32[]{:S(2)}) collective-permute-start(bf16[128,512]{1,0:T(8,128)(2,1)} %get-tuple-element.47), channel_id=1, source_target_pairs={{0,3},{1,0},{2,1},{3,2},{4,7},{5,4},{6,5},{7,6},{8,11},{9,8},{10,9... | collective-permute-start | bytes 393224 | tf_op jit(solution)/shard_map/ppermute | solution.py:43
  215.8 21.5 %collective-permute-start.70 = (bf16[128,512]{1,0:T(8,128)(2,1)}, bf16[128,512]{1,0:T(8,128)(2,1)S(1)}, u32[]{:S(2)}, u32[]{:S(2)}) collective-permute-start(bf16[128,512]{1,0:T(8,128)(2,1)} %get-tuple-element.49), channel_id=1, source_target_pairs={{0,1},{1,2},{2,3},{3,0},{4,5},{5,6},{6,7},{7,4},{8,9},{9,10},{10,1... | collective-permute-start | bytes 393224 | tf_op jit(solution)/shard_map/ppermute | solution.py:43
  217.7 17.6 %collective-permute-start.33 = (bf16[256,512]{1,0:T(8,128)(2,1)S(1)}, bf16[256,512]{1,0:T(8,128)(2,1)S(1)}, u32[]{:S(2)}, u32[]{:S(2)}) collective-permute-start(bf16[256,512]{1,0:T(8,128)(2,1)S(1)} %copy-done.62), channel_id=1, source_target_pairs={{0,1},{1,2},{2,3},{3,0},{4,5},{5,6},{6,7},{7,4},{8,9},{9,10},{10,1... | collective-permute-start | bytes 786440 | tf_op jit(solution)/shard_map/ppermute | solution.py:43
  225.0 10.5 %collective-permute-start.32 = (bf16[256,512]{1,0:T(8,128)(2,1)S(1)}, bf16[256,512]{1,0:T(8,128)(2,1)S(1)}, u32[]{:S(2)}, u32[]{:S(2)}) collective-permute-start(bf16[256,512]{1,0:T(8,128)(2,1)S(1)} %add_convert_fusion.1), channel_id=1, source_target_pairs={{0,3},{1,0},{2,1},{3,2},{4,7},{5,4},{6,5},{7,6},{8,11},{9,8},{10,9... | collective-permute-start | bytes 786440 | tf_op jit(solution)/shard_map/ppermute | solution.py:43
  235.0 12.5 %collective-permute-start.69 = (bf16[128,512]{1,0:T(8,128)(2,1)S(1)}, bf16[128,512]{1,0:T(8,128)(2,1)S(1)}, u32[]{:S(2)}, u32[]{:S(2)}) collective-permute-start(bf16[128,512]{1,0:T(8,128)(2,1)S(1)} %add_convert_fusion.7), channel_id=1, source_target_pairs={{0,3},{1,0},{2,1},{3,2},{4,7},{5,4},{6,5},{7,6},{8,11},{9,8},{10,9... | collective-permute-start | bytes 393224 | tf_op jit(solution)/shard_map/ppermute | solution.py:43
  235.6 25.0 %collective-permute-start.34 = (bf16[256,512]{1,0:T(8,128)(2,1)S(1)}, bf16[256,512]{1,0:T(8,128)(2,1)S(1)}, u32[]{:S(2)}, u32[]{:S(2)}) collective-permute-start(bf16[256,512]{1,0:T(8,128)(2,1)S(1)} %add_convert_fusion.refs_0_), channel_id=1, source_target_pairs={{0,1},{1,2},{2,3},{3,0},{4,5},{5,6},{6,7},{7,4},{8,9},{9,10},{10,1... | collective-permute-start | bytes 786440 | tf_op jit(solution)/shard_map/ppermute | solution.py:43
  248.6 8.2 %collective-permute-start.71 = (bf16[128,512]{1,0:T(8,128)(2,1)S(1)}, bf16[128,512]{1,0:T(8,128)(2,1)S(1)}, u32[]{:S(2)}, u32[]{:S(2)}) collective-permute-start(bf16[128,512]{1,0:T(8,128)(2,1)S(1)} %add_convert_fusion.6.refs_0_), channel_id=1, source_target_pairs={{0,1},{1,2},{2,3},{3,0},{4,5},{5,6},{6,7},{7,4},{8,9},{9,10},{10,1... | collective-permute-start | bytes 393224 | tf_op jit(solution)/shard_map/ppermute | solution.py:43
  248.7 12.0 %collective-permute-start.72 = (bf16[128,512]{1,0:T(8,128)(2,1)S(1)}, bf16[128,512]{1,0:T(8,128)(2,1)S(1)}, u32[]{:S(2)}, u32[]{:S(2)}) collective-permute-start(bf16[128,512]{1,0:T(8,128)(2,1)S(1)} %add_convert_fusion.6.refs_0_), channel_id=1, source_target_pairs={{0,3},{1,0},{2,1},{3,2},{4,7},{5,4},{6,5},{7,6},{8,11},{9,8},{10,9... | collective-permute-start | bytes 393224 | tf_op jit(solution)/shard_map/ppermute | solution.py:43
  256.8 6.9 %collective-permute-start.73 = (bf16[128,512]{1,0:T(8,128)(2,1)S(1)}, bf16[128,512]{1,0:T(8,128)(2,1)S(1)}, u32[]{:S(2)}, u32[]{:S(2)}) collective-permute-start(bf16[128,512]{1,0:T(8,128)(2,1)S(1)} %collective-permute-done.71.refs_1_), channel_id=1, source_target_pairs={{0,1},{1,2},{2,3},{3,0},{4,5},{5,6},{6,7},{7,4},{8,9},{9,10},{10,1... | collective-permute-start | bytes 393224 | tf_op jit(solution)/shard_map/ppermute | solution.py:43
  256.8 12.3 %collective-permute-start.35 = (bf16[256,512]{1,0:T(8,128)(2,1)S(1)}, bf16[256,512]{1,0:T(8,128)(2,1)S(1)}, u32[]{:S(2)}, u32[]{:S(2)}) collective-permute-start(bf16[256,512]{1,0:T(8,128)(2,1)S(1)} %add_convert_fusion.refs_0_), channel_id=1, source_target_pairs={{0,3},{1,0},{2,1},{3,2},{4,7},{5,4},{6,5},{7,6},{8,11},{9,8},{10,9... | collective-permute-start | bytes 786440 | tf_op jit(solution)/shard_map/ppermute | solution.py:43
  260.6 8.6 %collective-permute-start.36 = (bf16[256,512]{1,0:T(8,128)(2,1)S(1)}, bf16[256,512]{1,0:T(8,128)(2,1)S(1)}, u32[]{:S(2)}, u32[]{:S(2)}) collective-permute-start(bf16[256,512]{1,0:T(8,128)(2,1)S(1)} %collective-permute-done.34.refs_1_), channel_id=1, source_target_pairs={{0,1},{1,2},{2,3},{3,0},{4,5},{5,6},{6,7},{7,4},{8,9},{9,10},{10,1... | collective-permute-start | bytes 786440 | tf_op jit(solution)/shard_map/ppermute | solution.py:43
  (77 other events, 598.2 us)

commit v4 on v2

v4 whole, which is shorter than its diff:
```python
import math

import jax
import jax.numpy as jnp
from jax import lax
from jax.experimental import pallas as pl
from jax.experimental.pallas import tpu as pltpu
from jax.sharding import PartitionSpec as P

BLK = 128
F32 = jnp.float32
BF16 = jnp.bfloat16
VMEM = pl.BlockSpec(memory_space=pltpu.VMEM)
ANY = pl.BlockSpec(memory_space=pl.ANY)


def dot(a, b, contract=((1,), (0,))):
    return lax.dot_general(a, b, (contract, ((), ())), preferred_element_type=F32)


def spec_bytes(specs):
    return sum(4 * math.prod(s.block_shape) for s in jax.tree.leaves(specs) if s.block_shape is not None)


def kernel_call(body, out_shape, grid, n_scalars, in_specs, out_specs, scratch, flops, nbytes):
    held = sum(2 * math.prod(s.shape) for s in scratch if s.dtype == BF16)
    limit = spec_bytes(in_specs) + 3 * spec_bytes(out_specs) + held + 4 * 1024 * 1024
    return pl.pallas_call(
        body,
        out_shape=out_shape,
        grid_spec=pltpu.PrefetchScalarGridSpec(
            num_scalar_prefetch=n_scalars,
            grid=grid,
            in_specs=in_specs,
            out_specs=out_specs,
            scratch_shapes=scratch,
        ),
        compiler_params=pltpu.CompilerParams(vmem_limit_bytes=limit),
        cost_estimate=pl.CostEstimate(flops=flops, bytes_accessed=nbytes, transcendentals=0),
    )


def whole(shape):
    return pl.BlockSpec(shape, lambda *_: (0,) * len(shape))


def shift(x, size, by):
    return lax.ppermute(x, "row", [(i, (i + by) % size) for i in range(size)])


def swap(x, size, by):
    return lax.ppermute(x, "front", [(i, i ^ by) for i in range(size)])


def gather_row(x, n):
    found = [(0, x)]
    up, down = x, x
    for step in range(1, n // 2 + 1):
        up = shift(up, n, 1)
        found.append((-step, up))
        if step < n - step:
            down = shift(down, n, -1)
            found.append((step, down))
    return found


def gather_front(x, n):
    found = {0: x, 1: swap(x, n, 1)}
    for d in range(2, n, 2):
        found[d] = swap(x, n, d)
    for d in range(2, n, 2):
        found[d + 1] = swap(found[d], n, 1)
    return [found[d] for d in range(n)]


def far_offsets(n):
    first = [-(n // 2)] + ([(n - 1) // 2] if n > 2 else [])
    later = [o for o in range(-(n // 2) + 1, (n - 1) // 2) if o]
    return first, later


def scatter_row(first, later, own, n):
    total = own
    for sign, far in ((-1, n // 2), (1, (n - 1) // 2)):
        running = None
        for step in range(far, 0, -1):
            if running is None:
                running = first[sign * step]
            else:
                running = (running.astype(F32) + later[sign * step]).astype(BF16)
            running = shift(running, n, sign)
        if running is not None:
            total = total + running.astype(F32)
    return total


def owner(at_ref, offset, n_row):
    return lax.rem(at_ref[0] + (offset + n_row), n_row)


def column_specs(rows, depth, offsets, n_row, moving=False):
    return [
        pl.BlockSpec((rows, depth), lambda i, at_ref, *_, o=o: (i if moving else 0, owner(at_ref, o, n_row)))
        for o in offsets
    ]


def products(a_refs, x_refs, contract):
    total = None
    for a_ref, x_ref in zip(a_refs, x_refs):
        part = dot(a_ref[...], x_ref[...], contract)
        total = part if total is None else total + part
    return total


def pivot_products(at, pivot, found, n_row, contract, finish, outs, extra=()):
    rows, depth = pivot.shape[0], pivot.shape[1] // n_row
    count = len(found)
    width = outs[0].shape[1]

    def body(at_ref, *refs):
        total = products(refs[:count], refs[count : 2 * count], contract)
        extras = refs[2 * count : 2 * count + len(extra)]
        for ref, value in zip(refs[2 * count + len(extra) :], finish(total, *[e[...] for e in extras])):
            ref[...] = value

    return kernel_call(
        body,
        outs,
        (1,),
        1,
        column_specs(rows, depth, [o for o, _ in found], n_row)
        + [whole(x.shape) for _, x in found]
        + [whole(e.shape) for e in extra],
        [whole(o.shape) for o in outs],
        [],
        2 * rows * depth * width * count,
        2 * rows * depth * count,
    )(at, *[pivot] * count, *[x for _, x in found], *extra)


def border_partial(at, coupling, found, n_row):
    rows, depth = coupling.shape[0], coupling.shape[1] // n_row
    count, width = len(found), found[0][1].shape[1]
    tile = rows // border_steps(rows)

    def body(at_ref, *refs):
        refs[-1][...] = products(refs[:count], refs[count : 2 * count], ((1,), (0,)))

    return kernel_call(
        body,
        jax.ShapeDtypeStruct((rows, width), F32),
        (rows // tile,),
        1,
        column_specs(tile, depth, [o for o, _ in found], n_row, True) + [whole(x.shape) for _, x in found],
        pl.BlockSpec((tile, width), lambda i, *_: (i, 0)),
        [],
        2 * rows * depth * width * count,
        2 * rows * depth * count,
    )(at, *[coupling] * count, *[x for _, x in found])


def border_steps(rows):
    blocks = rows // BLK
    return blocks // next(k for k in (4, 3, 2, 1) if blocks % k == 0)


def border_scatter(at, local_index, coupling, found, partial, n_row, n_front, span_rows):
    rows, depth = coupling.shape[0], coupling.shape[1] // n_row
    count, width = len(found), found[0][1].shape[1]
    tile = rows // border_steps(rows)
    piece_blocks = span_rows // n_front // BLK

    def body(at_ref, index_ref, *refs):
        partial_ref, send_ref, keep_ref = refs[-3], refs[-2], refs[-1]
        step = pl.program_id(0)

        @pl.when(step == 0)
        def _():
            send_ref[...] = jnp.zeros_like(send_ref)
            keep_ref[...] = jnp.zeros_like(keep_ref)

        total = products(refs[:count], refs[count : 2 * count], ((1,), (0,)))
        total = (partial_ref[...] + total).astype(BF16)
        for j in range(tile // BLK):
            target = index_ref[step * (tile // BLK) + j]
            there = lax.div(target, piece_blocks)
            slot = lax.shift_right_logical(there, 1) * piece_blocks + lax.rem(target, piece_blocks)
            place = pl.ds(pl.multiple_of(slot * BLK, BLK), BLK)
            block = total[j * BLK : (j + 1) * BLK]
            away = lax.rem(there + at_ref[1], 2)

            @pl.when(away == 1)
            def _():
                send_ref[place, :] = block

            @pl.when(away == 0)
            def _():
                keep_ref[place, :] = block

    half = jax.ShapeDtypeStruct((span_rows // 2, width), BF16)
    return kernel_call(
        body,
        [half, half],
        (rows // tile,),
        2,
        column_specs(tile, depth, [o for o, _ in found], n_row, True)
        + [whole(x.shape) for _, x in found]
        + [pl.BlockSpec((tile, width), lambda i, *_: (i, 0))],
        [whole(half.shape)] * 2,
        [],
        2 * rows * depth * width * count,
        2 * rows * depth * count,
    )(at, local_index, *[coupling] * count, *[x for _, x in found], partial)


def root_products(at, inverse, pieces, offsets, kinds, n_row, n_front):
    span_rows = inverse.shape[1]
    rows = inverse.shape[0] // n_row
    piece_rows, width = pieces[0].shape
    count = len(offsets)

    def row_block(i, at_ref):
        offset = offsets[0]
        for k in range(1, count):
            offset = jnp.where(i == k, offsets[k], offset)
        return owner(at_ref, offset, n_row), 0

    def body(at_ref, a_ref, *refs):
        piece_refs, out_refs = refs[:n_front], refs[n_front : n_front + count]
        x_ref, sems = refs[-2], refs[-1]
        step = pl.program_id(0)

        @pl.when(step == 0)
        def _():
            copies = []
            for d in range(n_front):
                start = lax.bitwise_xor(at_ref[1], d) * piece_rows
                place = pl.ds(pl.multiple_of(start, piece_rows), piece_rows)
                copies.append(pltpu.make_async_copy(piece_refs[d], x_ref.at[place], sems.at[d]))
            for copy in copies:
                copy.start()
            for copy in copies:
                copy.wait()

        total = dot(a_ref[...], x_ref[...])
        for i in range(count):

            @pl.when(step == i)
            def _():
                out_refs[i][...] = total.astype(out_refs[i].dtype)

    return kernel_call(
        body,
        [jax.ShapeDtypeStruct((rows, width), kind) for kind in kinds],
        (count,),
        1,
        [pl.BlockSpec((rows, span_rows), row_block)] + [ANY] * n_front,
        [whole((rows, width))] * count,
        [pltpu.VMEM((span_rows, width), BF16), pltpu.SemaphoreType.DMA((n_front,))],
        2 * rows * span_rows * width * count,
        2 * rows * span_rows * count,
    )(at, inverse, *pieces)


def border_pick(at, local_index, coupling, pieces, offset, n_row, n_front):
    rows, depth = coupling.shape[0], coupling.shape[1] // n_row
    piece_rows, width = pieces[0].shape
    quarter = piece_rows // n_row
    span_rows = piece_rows * n_front

    def body(at_ref, index_ref, a_ref, *refs):
        piece_refs, out_ref, picked_ref = refs[:n_front], refs[n_front], refs[n_front + 1]
        span_ref, sems = refs[-2], refs[-1]
        copies = []
        for d in range(n_front):
            there = lax.bitwise_xor(at_ref[1], d)
            chip, core = lax.shift_right_logical(there, 1), lax.rem(there, 2)
            for k in range(n_row):
                start = core * (span_rows // 2) + k * piece_rows + chip * quarter
                place = pl.ds(pl.multiple_of(start, quarter), quarter)
                copies.append(
                    pltpu.make_async_copy(
                        piece_refs[d].at[pl.ds(k * quarter, quarter)], span_ref.at[place], sems.at[d * n_row + k]
                    )
                )
        for copy in copies:
            copy.start()
        for copy in copies:
            copy.wait()
        for j in range(rows // BLK):
            source = pl.ds(pl.multiple_of(index_ref[j] * BLK, BLK), BLK)
            picked_ref[:, pl.ds(j * BLK, BLK)] = jnp.transpose(span_ref[source, :])
        out_ref[...] = dot(picked_ref[...], a_ref[...]).astype(BF16)

    return kernel_call(
        body,
        [jax.ShapeDtypeStruct((width, depth), BF16), jax.ShapeDtypeStruct((width, rows), BF16)],
        (1,),
        2,
        column_specs(rows, depth, [offset], n_row) + [ANY] * n_front,
        [whole((width, depth)), whole((width, rows))],
        [pltpu.VMEM((span_rows, width), BF16), pltpu.SemaphoreType.DMA((n_front * n_row,))],
        2 * rows * depth * width,
        2 * rows * depth,
    )(at, local_index, coupling, *pieces)


def border_backward(at, coupling, picked, offsets, kinds, n_row):
    rows, depth = coupling.shape[0], coupling.shape[1] // n_row
    width, count = picked.shape[0], len(offsets)

    def body(at_ref, x_ref, *refs):
        for a_ref, out_ref in zip(refs[:count], refs[count:]):
            out_ref[...] = dot(x_ref[...], a_ref[...]).astype(out_ref.dtype)

    return kernel_call(
        body,
        [jax.ShapeDtypeStruct((width, depth), kind) for kind in kinds],
        (1,),
        1,
        [whole(picked.shape)] + column_specs(rows, depth, offsets, n_row),
        [whole((width, depth))] * count,
        [],
        2 * rows * depth * width * count,
        2 * rows * depth * count,
    )(at, picked, *[coupling] * count)


def solve(n_front, n_row, rhs_front, rhs_root, pivot_inverse, border_coupling, root_inverse, border_map):
    row_at = lax.axis_index("row").astype(jnp.int32)
    front_at = lax.axis_index("front").astype(jnp.int32)
    at = jnp.stack([row_at, front_at])
    span_rows = root_inverse.shape[1]
    piece_rows, width = span_rows // n_front, rhs_front.shape[1]
    local_index = border_map[0] - row_at * (span_rows // BLK)
    first_at, later_at = far_offsets(n_row)
    chips = [[2 * chip + core for chip in range(n_front // 2)] for core in range(2)]
    block = jax.ShapeDtypeStruct((pivot_inverse.shape[0], width), F32)
    half = jax.ShapeDtypeStruct(block.shape, BF16)
    straight, across = ((1,), (0,)), ((1,), (1,))

    found = gather_row(rhs_front, n_row)
    early, last = found[:-1], found[-1:]
    partial = pivot_products(at, pivot_inverse, early, n_row, straight, lambda t: [t], [block])
    inner, inner_half = pivot_products(
        at,
        pivot_inverse,
        last,
        n_row,
        straight,
        lambda t, p: [t + p, (t + p).astype(BF16)],
        [block, half],
        partial,
    )
    found = gather_row(inner_half, n_row)
    early, last = found[:-1], found[-1:]
    partial = border_partial(at, border_coupling, early, n_row)
    send, keep = border_scatter(
        at, local_index, border_coupling, last, partial, n_row, n_front, span_rows
    )
    both = (keep.astype(F32) + swap(send, n_front, 1).astype(F32)).astype(BF16)
    shares = lax.all_to_all(
        both.reshape(n_front // 2, piece_rows, width), "front", 0, 0, axis_index_groups=chips
    )
    own_rhs = lax.dynamic_slice_in_dim(rhs_root, front_at * piece_rows, piece_rows, 0)
    pieces = gather_front((own_rhs - shares.astype(F32).sum(axis=0)).astype(BF16), n_front)

    def root(offsets, kind):
        outs = root_products(at, root_inverse, pieces, offsets, [kind] * len(offsets), n_row, n_front)
        return dict(zip(offsets, outs))

    first = {}
    for offset in first_at:
        first.update(root([offset], BF16))
    rest = root(later_at + [0], F32)
    root_solution = scatter_row(first, rest, rest[0], n_row)
    quarters = root_solution.astype(BF16).reshape(n_row, piece_rows // n_row, width)
    quarters = lax.all_to_all(quarters, "front", 0, 0, axis_index_groups=chips)
    quarters = lax.all_to_all(quarters, "row", 0, 0)
    spans = gather_front(quarters.reshape(piece_rows, width), n_front)

    out, picked = border_pick(at, local_index, border_coupling, spans, first_at[0], n_row, n_front)
    first = {first_at[0]: out}
    for offset in first_at[1:]:
        first[offset] = border_backward(at, border_coupling, picked, [offset], [BF16], n_row)[0]
    offsets = later_at + [0]
    rest = dict(zip(offsets, border_backward(at, border_coupling, picked, offsets, [F32] * len(offsets), n_row)))
    pulled = scatter_row(first, rest, rest[0], n_row).astype(BF16)
    found = gather_row(pulled, n_row)
    early, last = found[:-1], found[-1:]
    partial = pivot_products(
        at, pivot_inverse, early, n_row, across, lambda t, i: [i - t], [block], [inner]
    )
    front_solution = pivot_products(
        at, pivot_inverse, last, n_row, across, lambda t, p: [p - t], [block], partial
    )
    return front_solution[0], root_solution


def solve_plain(n_front, n_row, rhs_front, rhs_root, pivot_inverse, border_coupling, root_inverse, border_map):
    row_at = lax.axis_index("row")
    front_at = lax.axis_index("front")
    width = rhs_front.shape[1]
    inner = dot(pivot_inverse, lax.all_gather(rhs_front, "row", axis=0, tiled=True))
    contrib = dot(border_coupling, lax.all_gather(inner.astype(BF16), "row", axis=0, tiled=True))
    block_local = border_map.shape[1]
    span_rows = root_inverse.shape[1]
    span_blocks = span_rows // BLK
    local_index = border_map[0] - row_at * span_blocks
    select = (local_index[None, :] == jnp.arange(span_blocks, dtype=jnp.int32)[:, None]).astype(F32)
    dense = jnp.einsum(
        "kj,jcn->kcn", select, contrib.reshape(block_local, BLK, width), precision=lax.Precision.HIGHEST
    ).reshape(span_rows, width)
    shares = lax.psum_scatter(dense, "front", scatter_dimension=0, tiled=True)
    own_rhs = lax.dynamic_slice_in_dim(rhs_root, front_at * shares.shape[0], shares.shape[0], 0)
    schur_rhs = lax.all_gather((own_rhs - shares).astype(BF16), "front", axis=0, tiled=True)
    root_solution = lax.psum_scatter(dot(root_inverse, schur_rhs), "row", scatter_dimension=0, tiled=True)
    gathered = lax.all_gather(root_solution.astype(BF16), ("front", "row"), axis=0, tiled=True)
    ranged = lax.dynamic_slice_in_dim(gathered, row_at * span_rows, span_rows, 0)
    picked = jnp.take(ranged.reshape(span_blocks, BLK, width), local_index, axis=0)
    picked = picked.reshape(block_local * BLK, width)
    pulled = lax.psum_scatter(
        dot(border_coupling, picked, ((0,), (0,))), "row", scatter_dimension=0, tiled=True
    ).astype(BF16)
    correction = dot(pivot_inverse, lax.all_gather(pulled, "row", axis=0, tiled=True))
    return inner - correction, root_solution


def solution(mesh):
    in_specs = (
        P(("front", "row"), None),
        P("row", None),
        P(("front", "row"), None),
        P(("front", "row"), None),
        P("front", "row"),
        P("front", "row"),
    )
    out_specs = (P(("front", "row"), None), P(("front", "row"), None))
    n_front, n_row = mesh.shape["front"], mesh.shape["row"]

    def per_device(*arrays):
        root_inverse, width = arrays[4], arrays[0].shape[1]
        fits = (
            n_front == 2 * n_row
            and n_front & (n_front - 1) == 0
            and n_row > 2
            and root_inverse.shape[1] % (n_front * BLK) == 0
            and root_inverse.shape[0] == n_row * (root_inverse.shape[1] // n_front)
            and root_inverse.shape[1] % (n_front * n_row * 16) == 0
            and arrays[2].shape[1] % (n_row * BLK) == 0
            and width % BLK == 0
        )
        return (solve if fits else solve_plain)(n_front, n_row, *arrays)

    return jax.shard_map(per_device, mesh=mesh, in_specs=in_specs, out_specs=out_specs, check_vma=False)
```

time: 258 us -> 241 us (0.934)
  waiting for transfers between devices: 160 us -> 134 us
  blocking collectives: 0 us -> 19.7 us
  Pallas kernels: 48.3 us -> 32.1 us
  local copies, waits for them, and re-layouts: 4.06 us -> 9.09 us
  starting transfers between devices: 35.2 us -> 39.6 us
    all_to_all x0 -> x2, blocking collectives: none -> 19.7 us  [the longest x1 10.9 us: solve(): quarters = lax.all_to_all(quarters, 'row', 0, 0)]
    all_to_all x0 -> x1, waiting for transfers between devices: none -> 15.7 us  [solve(): lax.all_to_all(both.reshape(n_front // 2, piece_rows, width), 'front', 0,...]
    ppermute x4 -> x0, waiting for transfers between devices: 15.6 us -> none  [solve(): lax.ppermute(root_half[k * quarter:(k + 1) * quarter], ('front', 'row'),...]
    ppermute x18 -> x15, waiting for transfers between devices: 41.4 us -> 26.5 us  [swap(): return lax.ppermute(x, 'front', [(i, i ^ by) for i in range(size)])]
    ppermute x15, waiting for transfers between devices: 103 us -> 91.4 us  [shift(): return lax.ppermute(x, 'row', [(i, (i + by) % size) for i in range(size)])]
    ppermute x15, starting transfers between devices: 17.1 us -> 27.2 us  [shift(): return lax.ppermute(x, 'row', [(i, (i + by) % size) for i in range(size)])]
    pallas_call x5 -> x9, Pallas kernels: 32.4 us -> 23 us  [the longest x4 6.67 us: pivot_products(): kernel_call(body, outs, (1,), 1, column_specs(rows, depth, [o for o, _ in...]
    pallas_call x2 -> x3, Pallas kernels: 15.9 us -> 9.1 us  [root_products(): kernel_call(body, [jax.ShapeDtypeStruct((rows, width), kind) for kind in...]
  transfers between devices with their start and end apart: 37 -> 31, of which waited for: 26 -> 24; matrix products, arithmetic and copies ran while one was open for 2% -> 0% of each run, Pallas kernels for 6% -> 8%
where the time goes in v4:
time: 241 us; the launch traced here: 240 us
  waiting for transfers between devices  134 us (56%)
  starting transfers between devices  39.6 us (16%)
  Pallas kernels  32.1 us (13%)
  blocking collectives  19.7 us (8%)
  local copies, waits for them, and re-layouts  9.09 us (4%)
  other arithmetic  5.37 us (2%)
    ppermute x15, waiting for transfers between devices, shift(): return lax.ppermute(x, 'row', [(i, (i + by) % size) for i in range(size)])  91.4 us
    ppermute x15, starting transfers between devices, shift(): return lax.ppermute(x, 'row', [(i, (i + by) % size) for i in range(size)])  27.2 us
    ppermute x15, waiting for transfers between devices, swap(): return lax.ppermute(x, 'front', [(i, i ^ by) for i in range(size)])  26.5 us
    all_to_all x1, waiting for transfers between devices, solve(): lax.all_to_all(both.reshape(n_front // 2, piece_rows, width), 'front', 0,...  15.7 us
    all_to_all x1, blocking collectives, solve(): quarters = lax.all_to_all(quarters, 'row', 0, 0)  10.9 us
    pallas_call x3, Pallas kernels, root_products(): kernel_call(body, [jax.ShapeDtypeStruct((rows, width), kind) for kind in...  9.1 us
    unnamed x24, local copies, waits for them, and re-layouts  9.09 us
    all_to_all x1, blocking collectives, solve(): quarters = lax.all_to_all(quarters, 'front', 0, 0, axis_index_groups=chips)  8.78 us
  transfers between devices with their start and end apart: 31, of which 24 were waited for; matrix products, arithmetic and copies ran while one was open for 0% of the time, Pallas kernels for 8%

profile of v4, /device:TPU:0, one launch (start us, length us, event | category | flops | bytes accessed | tf_op | source)
XLA Modules:
  0.0 240.3 jit_solution(12538640229671190242)
XLA Ops:
  0.6 3.1 %collective-permute-start = (bf16[512,384]{1,0:T(8,128)(2,1)}, bf16[512,384]{1,0:T(8,128)(2,1)S(1)}, u32[]{:S(2)}, u32[]{:S(2)}) collective-permute-start(bf16[512,384]{1,0:T(8,128)(2,1)} %refs_3_.1), channel_id=1, source_target_pairs={{0,1},{1,2},{2,3},{3,0},{4,5},{5,6},{6,7},{7,4},{8,9},{9,10},{10,1... | collective-permute-start | bytes 1179656 | tf_op jit(solution)/shard_map/ppermute | solution.py:48
  3.7 2.1 collective-permute-start.2
  5.8 10.1 %collective-permute-done.refs_4_ = bf16[512,384]{1,0:T(8,128)(2,1)S(1)} collective-permute-done((bf16[512,384]{1,0:T(8,128)(2,1)}, bf16[512,384]{1,0:T(8,128)(2,1)S(1)}, u32[]{:S(2)}, u32[]{:S(2)}) %collective-permute-start) | collective-permute-done | bytes 393248 | tf_op jit(solution)/shard_map/ppermute | solution.py:48
  16.0 7.1 %collective-permute-done.2.refs_5_ = bf16[512,384]{1,0:T(8,128)(2,1)S(1)} collective-permute-done((bf16[512,384]{1,0:T(8,128)(2,1)}, bf16[512,384]{1,0:T(8,128)(2,1)S(1)}, u32[]{:S(2)}, u32[]{:S(2)}) %collective-permute-start.2) | collective-permute-done | bytes 393248 | tf_op jit(solution)/shard_map/ppermute | solution.py:48
  23.1 1.6 copy-done.2
  24.7 1.0 copy-done.5
  25.7 1.5 shard_map.77.refs_2_
  27.3 4.7 %collective-permute-done.1.refs_1_ = bf16[512,384]{1,0:T(8,128)(2,1)S(1)} collective-permute-done((bf16[512,384]{1,0:T(8,128)(2,1)S(1)}, bf16[512,384]{1,0:T(8,128)(2,1)S(1)}, u32[]{:S(2)}, u32[]{:S(2)}) %collective-permute-start.1) | collective-permute-done | bytes 393248 | tf_op jit(solution)/shard_map/ppermute | solution.py:48
  32.0 1.7 shard_map.78
  33.7 3.8 %collective-permute-start.5 = (bf16[512,384]{1,0:T(8,128)(2,1)}, bf16[512,384]{1,0:T(8,128)(2,1)}, u32[]{:S(2)}, u32[]{:S(2)}) collective-permute-start(bf16[512,384]{1,0:T(8,128)(2,1)} %get-tuple-element.12.refs_3_), channel_id=1, source_target_pairs={{0,3},{1,0},{2,1},{3,2},{4,7},{5,4},{6,5},{7,6},{8,11},{9,8},{10,9... | collective-permute-start | bytes 1179656 | tf_op jit(solution)/shard_map/ppermute | solution.py:48
  37.5 10.2 %collective-permute-done.3.refs_4_ = bf16[512,384]{1,0:T(8,128)(2,1)S(1)} collective-permute-done((bf16[512,384]{1,0:T(8,128)(2,1)}, bf16[512,384]{1,0:T(8,128)(2,1)S(1)}, u32[]{:S(2)}, u32[]{:S(2)}) %collective-permute-start.3) | collective-permute-done | bytes 393248 | tf_op jit(solution)/shard_map/ppermute | solution.py:48
  47.8 6.1 %collective-permute-done.5.refs_5_ = bf16[512,384]{1,0:T(8,128)(2,1)} collective-permute-done((bf16[512,384]{1,0:T(8,128)(2,1)}, bf16[512,384]{1,0:T(8,128)(2,1)}, u32[]{:S(2)}, u32[]{:S(2)}) %collective-permute-start.5) | collective-permute-done | bytes 393248 | tf_op jit(solution)/shard_map/ppermute | solution.py:48
  53.9 2.8 %copy-done = bf16[1536,2048]{1,0:T(8,128)(2,1)S(1)} copy-done((bf16[1536,2048]{1,0:T(8,128)(2,1)S(1)}, bf16[1536,2048]{1,0:T(8,128)(2,1)}, u32[]{:S(2)}) %copy-start) | copy-done | bytes 6291480
  56.6 5.2 %shard_map.79.refs_2_ = f32[1536,384]{1,0:T(8,128)S(1)} custom-call(s32[2]{0:T(128)S(1)} %pad_add_fusion.at_ref, bf16[1536,2048]{1,0:T(8,128)(2,1)S(1)} %copy-done, bf16[1536,2048]{1,0:T(8,128)(2,1)S(1)} %copy-done, bf16[1536,2048]{1,0:T(8,128)(2,1)S(1)} %copy-done, bf16[512,384]{1,0:T(8,128)(2,1)} %get-tuple-element.12.refs_3_, ...), custom_call_target="tpu_custom_call" | custom-call | flops 1811939328 | bytes 4718592 | tf_op jit(solution)/shard_map/pallas_call | solution.py:150
  61.9 2.6 %shard_map.80 = (bf16[1536,384]{1,0:T(8,128)(2,1)S(1)}, bf16[1536,384]{1,0:T(8,128)(2,1)S(1)}) custom-call(s32[2]{0:T(128)S(1)} %pad_add_fusion.at_ref, s32[12]{0:T(128)S(1)} %subtract_bitcast_fusion.index_ref, bf16[1536,2048]{1,0:T(8,128)(2,1)S(1)} %copy-done.1, bf16[512,384]{1,0:T(8,128)(2,1)S(1)} %collective-permute-done.4.refs_1_, ...), custom_call_target="tpu_custom_call" | custom-call | flops 603979776 | bytes 1572864 | tf_op jit(solution)/shard_map/pallas_call | solution.py:202
  64.6 2.8 %collective-permute-done.6 = bf16[1536,384]{1,0:T(8,128)(2,1)S(1)} collective-permute-done((bf16[1536,384]{1,0:T(8,128)(2,1)S(1)}, bf16[1536,384]{1,0:T(8,128)(2,1)S(1)}, u32[]{:S(2)}, u32[]{:S(2)}) %collective-permute-start.6) | collective-permute-done | bytes 1179680 | tf_op jit(solution)/shard_map/ppermute | solution.py:52
  67.4 1.4 add_convert_fusion
  68.8 4.3 %all-to-all-start = ((bf16[4,384,384]{2,1,0:T(8,128)(2,1)}), bf16[4,384,384]{2,1,0:T(8,128)(2,1)}, u32[]{:S(2)}, u32[]{:S(2)}) async-start(bf16[4,384,384]{2,1,0:T(8,128)(2,1)} %bitcast.16), calls=%async_computation | async-start | bytes 2359296 | tf_op jit(solution)/shard_map/all_to_all | solution.py:363
  73.0 15.7 %all-to-all-done = bf16[4,384,384]{2,1,0:T(8,128)(2,1)} async-done(((bf16[4,384,384]{2,1,0:T(8,128)(2,1)}), bf16[4,384,384]{2,1,0:T(8,128)(2,1)}, u32[]{:S(2)}, u32[]{:S(2)}) %all-to-all-start) | async-done | bytes 1179680 | tf_op jit(solution)/shard_map/all_to_all | solution.py:363
  88.7 1.5 convert_reduce_fusion
  90.2 1.2 subtract_convert_fusion.refs_0_
  91.4 1.5 collective-permute-start.12
  92.9 1.5 collective-permute-start.10
  94.3 0.6 collective-permute-start.8
  94.9 7.4 %collective-permute-done.12.refs_6_ = bf16[384,384]{1,0:T(8,128)(2,1)S(1)} collective-permute-done((bf16[384,384]{1,0:T(8,128)(2,1)S(1)}, bf16[384,384]{1,0:T(8,128)(2,1)S(1)}, u32[]{:S(2)}, u32[]{:S(2)}) %collective-permute-start.12) | collective-permute-done | bytes 294944 | tf_op jit(solution)/shard_map/ppermute | solution.py:52
  102.3 4.5 %collective-permute-done.10.refs_4_ = bf16[384,384]{1,0:T(8,128)(2,1)S(1)} collective-permute-done((bf16[384,384]{1,0:T(8,128)(2,1)S(1)}, bf16[384,384]{1,0:T(8,128)(2,1)S(1)}, u32[]{:S(2)}, u32[]{:S(2)}) %collective-permute-start.10) | collective-permute-done | bytes 294944 | tf_op jit(solution)/shard_map/ppermute | solution.py:52
  106.9 0.5 collective-permute-start.9
  107.4 1.1 collective-permute-done.11.refs_5_
  108.5 0.4 collective-permute-done.9.refs_3_
  108.9 3.7 %copy-done.4 = bf16[1536,3072]{1,0:T(8,128)(2,1)S(1)} copy-done((bf16[1536,3072]{1,0:T(8,128)(2,1)S(1)}, bf16[1536,3072]{1,0:T(8,128)(2,1)}, u32[]{:S(2)}) %copy-start.4) | copy-done | bytes 9437208
  112.6 2.5 %shard_map.82 = bf16[384,384]{1,0:T(8,128)(2,1)S(1)} custom-call(s32[2]{0:T(128)S(1)} %pad_add_fusion.at_ref, bf16[1536,3072]{1,0:T(8,128)(2,1)S(1)} %copy-done.4, bf16[384,384]{1,0:T(8,128)(2,1)S(1)} %subtract_convert_fusion.refs_0_, bf16[384,384]{1,0:T(8,128)(2,1)S(1)} %collective-permute-done.7.refs_1_, ...), custom_call_target="tpu_custom_call" | custom-call | flops 905969664 | bytes 2359296 | tf_op jit(solution)/shard_map/pallas_call | solution.py:253
  115.1 2.5 %collective-permute-start.14 = (bf16[384,384]{1,0:T(8,128)(2,1)S(1)}, bf16[384,384]{1,0:T(8,128)(2,1)S(1)}, u32[]{:S(2)}, u32[]{:S(2)}) collective-permute-start(bf16[384,384]{1,0:T(8,128)(2,1)S(1)} %shard_map.82), channel_id=1, source_target_pairs={{0,3},{1,0},{2,1},{3,2},{4,7},{5,4},{6,5},{7,6},{8,11},{9,8},{10,9... | collective-permute-start | bytes 884744 | tf_op jit(solution)/shard_map/ppermute | solution.py:48
  117.7 2.5 %shard_map.83 = bf16[384,384]{1,0:T(8,128)(2,1)S(1)} custom-call(s32[2]{0:T(128)S(1)} %pad_add_fusion.at_ref, bf16[1536,3072]{1,0:T(8,128)(2,1)S(1)} %copy-done.4, bf16[384,384]{1,0:T(8,128)(2,1)S(1)} %subtract_convert_fusion.refs_0_, bf16[384,384]{1,0:T(8,128)(2,1)S(1)} %collective-permute-done.7.refs_1_, ...), custom_call_target="tpu_custom_call" | custom-call | flops 905969664 | bytes 2359296 | tf_op jit(solution)/shard_map/pallas_call | solution.py:253
  120.3 4.1 %shard_map.81 = (f32[384,384]{1,0:T(8,128)S(1)}, f32[384,384]{1,0:T(8,128)S(1)}) custom-call(s32[2]{0:T(128)S(1)} %pad_add_fusion.at_ref, bf16[1536,3072]{1,0:T(8,128)(2,1)S(1)} %bitcast.10, bf16[384,384]{1,0:T(8,128)(2,1)S(1)} %subtract_convert_fusion.refs_0_, bf16[384,384]{1,0:T(8,128)(2,1)S(1)} %collective-permute-done.7.refs_1_, ...), custom_call_target="tpu_custom_call" | custom-call | flops 1811939328 | bytes 4718592 | tf_op jit(solution)/shard_map/pallas_call | solution.py:253
  124.4 0.7 collective-permute-done.14
  125.1 4.3 %collective-permute-start.15 = (bf16[384,384]{1,0:T(8,128)(2,1)S(1)}, bf16[384,384]{1,0:T(8,128)(2,1)S(1)}, u32[]{:S(2)}, u32[]{:S(2)}) collective-permute-start(bf16[384,384]{1,0:T(8,128)(2,1)S(1)} %add_convert_fusion.3), channel_id=1, source_target_pairs={{0,3},{1,0},{2,1},{3,2},{4,7},{5,4},{6,5},{7,6},{8,11},{9,8},{10,9... | collective-permute-start | bytes 884744 | tf_op jit(solution)/shard_map/ppermute | solution.py:48
  129.5 4.3 %collective-permute-done.16 = bf16[384,384]{1,0:T(8,128)(2,1)S(1)} collective-permute-done((bf16[384,384]{1,0:T(8,128)(2,1)S(1)}, bf16[384,384]{1,0:T(8,128)(2,1)S(1)}, u32[]{:S(2)}, u32[]{:S(2)}) %collective-permute-start.16) | collective-permute-done | bytes 294944 | tf_op jit(solution)/shard_map/ppermute | solution.py:48
  133.8 5.2 %collective-permute-done.15 = bf16[384,384]{1,0:T(8,128)(2,1)S(1)} collective-permute-done((bf16[384,384]{1,0:T(8,128)(2,1)S(1)}, bf16[384,384]{1,0:T(8,128)(2,1)S(1)}, u32[]{:S(2)}, u32[]{:S(2)}) %collective-permute-start.15) | collective-permute-done | bytes 294944 | tf_op jit(solution)/shard_map/ppermute | solution.py:48
  139.0 0.9 fusion
  140.0 8.8 %all_to_all.15 = bf16[4,96,384]{2,1,0:T(8,128)(2,1)S(1)} all-to-all(bf16[4,96,384]{2,1,0:T(8,128)(2,1)S(1)} %bitcast.17), channel_id=1, replica_groups={{0,8,16,24},{4,12,20,28},{1,9,17,25},{5,13,21,29},{2,10,18,26},{6,14,22..., dimensions={0} | all-to-all | bytes 589824 | tf_op jit(solution)/shard_map/all_to_all | solution.py:379
  148.7 10.9 %all_to_all.16 = bf16[4,96,384]{2,1,0:T(8,128)(2,1)S(1)} all-to-all(bf16[4,96,384]{2,1,0:T(8,128)(2,1)S(1)} %all_to_all.15), channel_id=1, replica_groups=mesh['front'=8,'row'=4] {'row'}, dimensions={0} | all-to-all | bytes 589824 | tf_op jit(solution)/shard_map/all_to_all | solution.py:380
  159.7 0.6 collective-permute-start.22
  160.3 1.6 collective-permute-start.20
  161.8 1.3 collective-permute-start.18
  163.2 6.1 %collective-permute-done.22.refs_6_ = bf16[384,384]{1,0:T(8,128)(2,1)S(1)} collective-permute-done((bf16[384,384]{1,0:T(8,128)(2,1)S(1)}, bf16[384,384]{1,0:T(8,128)(2,1)S(1)}, u32[]{:S(2)}, u32[]{:S(2)}) %collective-permute-start.22) | collective-permute-done | bytes 294944 | tf_op jit(solution)/shard_map/ppermute | solution.py:52
  169.3 2.6 %collective-permute-done.20.refs_4_ = bf16[384,384]{1,0:T(8,128)(2,1)S(1)} collective-permute-done((bf16[384,384]{1,0:T(8,128)(2,1)S(1)}, bf16[384,384]{1,0:T(8,128)(2,1)S(1)}, u32[]{:S(2)}, u32[]{:S(2)}) %collective-permute-start.20) | collective-permute-done | bytes 294944 | tf_op jit(solution)/shard_map/ppermute | solution.py:52
  171.9 0.5 collective-permute-start.19
  172.4 1.1 collective-permute-done.21.refs_5_
  173.5 0.4 collective-permute-done.19.refs_3_
  173.9 5.3 %shard_map.84 = (bf16[384,512]{1,0:T(8,128)(2,1)S(1)}, bf16[384,1536]{1,0:T(8,128)(2,1)S(1)}) custom-call(s32[2]{0:T(128)S(1)} %pad_add_fusion.at_ref, s32[12]{0:T(128)S(1)} %subtract_bitcast_fusion.index_ref, bf16[1536,2048]{1,0:T(8,128)(2,1)S(1)} %bitcast.8, bf16[384,384]{1,0:T(8,128)(2,1)S(1)} %bitcast.15, ...), custom_call_target="tpu_custom_call" | custom-call | flops 603979776 | bytes 1572864 | tf_op jit(solution)/shard_map/pallas_call | solution.py:296
  179.2 3.0 %collective-permute-start.24 = (bf16[384,512]{1,0:T(8,128)(2,1)S(1)}, bf16[384,512]{1,0:T(8,128)(2,1)S(1)}, u32[]{:S(2)}, u32[]{:S(2)}) collective-permute-start(bf16[384,512]{1,0:T(8,128)(2,1)S(1)} %get-tuple-element.19), channel_id=1, source_target_pairs={{0,3},{1,0},{2,1},{3,2},{4,7},{5,4},{6,5},{7,6},{8,11},{9,8},{10,9... | collective-permute-start | bytes 1179656 | tf_op jit(solution)/shard_map/ppermute | solution.py:48
  182.2 1.3 shard_map.86
  183.6 1.9 shard_map.85
  185.5 6.2 %collective-permute-done.24 = bf16[384,512]{1,0:T(8,128)(2,1)S(1)} collective-permute-done((bf16[384,512]{1,0:T(8,128)(2,1)S(1)}, bf16[384,512]{1,0:T(8,128)(2,1)S(1)}, u32[]{:S(2)}, u32[]{:S(2)}) %collective-permute-start.24) | collective-permute-done | bytes 393248 | tf_op jit(solution)/shard_map/ppermute | solution.py:48
  191.9 4.3 %collective-permute-start.25 = (bf16[384,512]{1,0:T(8,128)(2,1)S(1)}, bf16[384,512]{1,0:T(8,128)(2,1)S(1)}, u32[]{:S(2)}, u32[]{:S(2)}) collective-permute-start(bf16[384,512]{1,0:T(8,128)(2,1)S(1)} %add_convert_fusion.2), channel_id=1, source_target_pairs={{0,3},{1,0},{2,1},{3,2},{4,7},{5,4},{6,5},{7,6},{8,11},{9,8},{10,9... | collective-permute-start | bytes 1179656 | tf_op jit(solution)/shard_map/ppermute | solution.py:48
  196.2 4.4 %collective-permute-done.26 = bf16[384,512]{1,0:T(8,128)(2,1)S(1)} collective-permute-done((bf16[384,512]{1,0:T(8,128)(2,1)S(1)}, bf16[384,512]{1,0:T(8,128)(2,1)S(1)}, u32[]{:S(2)}, u32[]{:S(2)}) %collective-permute-start.26) | collective-permute-done | bytes 393248 | tf_op jit(solution)/shard_map/ppermute | solution.py:48
  200.6 7.9 %collective-permute-done.25 = bf16[384,512]{1,0:T(8,128)(2,1)S(1)} collective-permute-done((bf16[384,512]{1,0:T(8,128)(2,1)S(1)}, bf16[384,512]{1,0:T(8,128)(2,1)S(1)}, u32[]{:S(2)}, u32[]{:S(2)}) %collective-permute-start.25) | collective-permute-done | bytes 393248 | tf_op jit(solution)/shard_map/ppermute | solution.py:48
  208.7 0.6 collective-permute-start.27
  209.3 3.3 %collective-permute-start.29 = (bf16[384,512]{1,0:T(8,128)(2,1)S(1)}, bf16[384,512]{1,0:T(8,128)(2,1)S(1)}, u32[]{:S(2)}, u32[]{:S(2)}) collective-permute-start(bf16[384,512]{1,0:T(8,128)(2,1)S(1)} %add_convert_fusion.1.refs_3_), channel_id=1, source_target_pairs={{0,3},{1,0},{2,1},{3,2},{4,7},{5,4},{6,5},{7,6},{8,11},{9,8},{10,9... | collective-permute-start | bytes 1179656 | tf_op jit(solution)/shard_map/ppermute | solution.py:48
  212.5 10.0 %collective-permute-done.27.refs_4_ = bf16[384,512]{1,0:T(8,128)(2,1)S(1)} collective-permute-done((bf16[384,512]{1,0:T(8,128)(2,1)S(1)}, bf16[384,512]{1,0:T(8,128)(2,1)S(1)}, u32[]{:S(2)}, u32[]{:S(2)}) %collective-permute-start.27) | collective-permute-done | bytes 393248 | tf_op jit(solution)/shard_map/ppermute | solution.py:48
  222.5 5.9 %collective-permute-done.29.refs_5_ = bf16[384,512]{1,0:T(8,128)(2,1)S(1)} collective-permute-done((bf16[384,512]{1,0:T(8,128)(2,1)S(1)}, bf16[384,512]{1,0:T(8,128)(2,1)S(1)}, u32[]{:S(2)}, u32[]{:S(2)}) %collective-permute-start.29) | collective-permute-done | bytes 393248 | tf_op jit(solution)/shard_map/ppermute | solution.py:48
  228.5 1.5 shard_map.87.refs_2_
  230.0 8.4 %collective-permute-done.28.refs_1_ = bf16[384,512]{1,0:T(8,128)(2,1)S(1)} collective-permute-done((bf16[384,512]{1,0:T(8,128)(2,1)S(1)}, bf16[384,512]{1,0:T(8,128)(2,1)S(1)}, u32[]{:S(2)}, u32[]{:S(2)}) %collective-permute-start.28) | collective-permute-done | bytes 393248 | tf_op jit(solution)/shard_map/ppermute | solution.py:48
  238.4 1.9 shard_map.88
  (47 shorter events, 0.8 us)
Async XLA Ops:
  0.6 15.3 %collective-permute-start = (bf16[512,384]{1,0:T(8,128)(2,1)}, bf16[512,384]{1,0:T(8,128)(2,1)S(1)}, u32[]{:S(2)}, u32[]{:S(2)}) collective-permute-start(bf16[512,384]{1,0:T(8,128)(2,1)} %refs_3_.1), channel_id=1, source_target_pairs={{0,1},{1,2},{2,3},{3,0},{4,5},{5,6},{6,7},{7,4},{8,9},{9,10},{10,1... | collective-permute-start | bytes 1179656 | tf_op jit(solution)/shard_map/ppermute | solution.py:48
  3.7 19.4 %collective-permute-start.2 = (bf16[512,384]{1,0:T(8,128)(2,1)}, bf16[512,384]{1,0:T(8,128)(2,1)S(1)}, u32[]{:S(2)}, u32[]{:S(2)}) collective-permute-start(bf16[512,384]{1,0:T(8,128)(2,1)} %refs_3_.1), channel_id=1, source_target_pairs={{0,3},{1,0},{2,1},{3,2},{4,7},{5,4},{6,5},{7,6},{8,11},{9,8},{10,9... | collective-permute-start | bytes 1179656 | tf_op jit(solution)/shard_map/ppermute | solution.py:48
  15.9 16.0 %collective-permute-start.1 = (bf16[512,384]{1,0:T(8,128)(2,1)S(1)}, bf16[512,384]{1,0:T(8,128)(2,1)S(1)}, u32[]{:S(2)}, u32[]{:S(2)}) collective-permute-start(bf16[512,384]{1,0:T(8,128)(2,1)S(1)} %collective-permute-done.refs_4_), channel_id=1, source_target_pairs={{0,1},{1,2},{2,3},{3,0},{4,5},{5,6},{6,7},{7,4},{8,9},{9,10},{10,1... | collective-permute-start | bytes 1179656 | tf_op jit(solution)/shard_map/ppermute | solution.py:48
  23.1 1.6 copy-start.2
  24.7 1.0 copy-start.5
  25.7 6.2 %copy-start.3 = (bf16[512,2048]{1,0:T(8,128)(2,1)S(1)}, bf16[512,2048]{1,0:T(8,128)(2,1)}, u32[]{:S(2)}) copy-start(bf16[512,2048]{1,0:T(8,128)(2,1)} %refs_0_.15) | copy-start | bytes 6291460
  27.2 20.5 %copy-start.6 = (s32[1,12]{1,0:T(1,128)S(1)}, s32[1,12]{1,0:T(1,128)}, u32[]{:S(2)}) copy-start(s32[1,12]{1,0:T(1,128)} %param.11) | copy-start | bytes 148
  33.7 14.1 %collective-permute-start.3 = (bf16[512,384]{1,0:T(8,128)(2,1)}, bf16[512,384]{1,0:T(8,128)(2,1)S(1)}, u32[]{:S(2)}, u32[]{:S(2)}) collective-permute-start(bf16[512,384]{1,0:T(8,128)(2,1)} %get-tuple-element.12.refs_3_), channel_id=1, source_target_pairs={{0,1},{1,2},{2,3},{3,0},{4,5},{5,6},{6,7},{7,4},{8,9},{9,10},{10,1... | collective-permute-start | bytes 1179656 | tf_op jit(solution)/shard_map/ppermute | solution.py:48
  33.7 20.2 %collective-permute-start.5 = (bf16[512,384]{1,0:T(8,128)(2,1)}, bf16[512,384]{1,0:T(8,128)(2,1)}, u32[]{:S(2)}, u32[]{:S(2)}) collective-permute-start(bf16[512,384]{1,0:T(8,128)(2,1)} %get-tuple-element.12.refs_3_), channel_id=1, source_target_pairs={{0,3},{1,0},{2,1},{3,2},{4,7},{5,4},{6,5},{7,6},{8,11},{9,8},{10,9... | collective-permute-start | bytes 1179656 | tf_op jit(solution)/shard_map/ppermute | solution.py:48
  47.8 14.1 %collective-permute-start.4 = (bf16[512,384]{1,0:T(8,128)(2,1)S(1)}, bf16[512,384]{1,0:T(8,128)(2,1)S(1)}, u32[]{:S(2)}, u32[]{:S(2)}) collective-permute-start(bf16[512,384]{1,0:T(8,128)(2,1)S(1)} %collective-permute-done.3.refs_4_), channel_id=1, source_target_pairs={{0,1},{1,2},{2,3},{3,0},{4,5},{5,6},{6,7},{7,4},{8,9},{9,10},{10,1... | collective-permute-start | bytes 1179656 | tf_op jit(solution)/shard_map/ppermute | solution.py:48
  53.9 2.8 %copy-start = (bf16[1536,2048]{1,0:T(8,128)(2,1)S(1)}, bf16[1536,2048]{1,0:T(8,128)(2,1)}, u32[]{:S(2)}) copy-start(bf16[1536,2048]{1,0:T(8,128)(2,1)} %refs_0_.13) | copy-start | bytes 18874372
  56.6 5.3 %copy-start.1 = (bf16[1536,2048]{1,0:T(8,128)(2,1)S(1)}, bf16[1536,2048]{1,0:T(8,128)(2,1)}, u32[]{:S(2)}) copy-start(bf16[1536,2048]{1,0:T(8,128)(2,1)} %refs_0_.13) | copy-start | bytes 18874372
  64.5 2.9 %collective-permute-start.6 = (bf16[1536,384]{1,0:T(8,128)(2,1)S(1)}, bf16[1536,384]{1,0:T(8,128)(2,1)S(1)}, u32[]{:S(2)}, u32[]{:S(2)}) collective-permute-start(bf16[1536,384]{1,0:T(8,128)(2,1)S(1)} %get-tuple-element.14), channel_id=1, source_target_pairs={{0,4},{4,0},{8,12},{12,8},{16,20},{20,16},{24,28},{28,24},{1,5},{5... | collective-permute-start | bytes 3538952 | tf_op jit(solution)/shard_map/ppermute | solution.py:52
  68.8 20.0 %all-to-all-start = ((bf16[4,384,384]{2,1,0:T(8,128)(2,1)}), bf16[4,384,384]{2,1,0:T(8,128)(2,1)}, u32[]{:S(2)}, u32[]{:S(2)}) async-start(bf16[4,384,384]{2,1,0:T(8,128)(2,1)} %bitcast.16), calls=%async_computation | async-start | bytes 2359296 | tf_op jit(solution)/shard_map/all_to_all | solution.py:363
  91.4 11.0 %collective-permute-start.12 = (bf16[384,384]{1,0:T(8,128)(2,1)S(1)}, bf16[384,384]{1,0:T(8,128)(2,1)S(1)}, u32[]{:S(2)}, u32[]{:S(2)}) collective-permute-start(bf16[384,384]{1,0:T(8,128)(2,1)S(1)} %subtract_convert_fusion.refs_0_), channel_id=1, source_target_pairs={{0,24},{4,28},{8,16},{12,20},{16,8},{20,12},{24,0},{28,4},{1,25},{... | collective-permute-start | bytes 884744 | tf_op jit(solution)/shard_map/ppermute | solution.py:52
  92.9 14.0 %collective-permute-start.10 = (bf16[384,384]{1,0:T(8,128)(2,1)S(1)}, bf16[384,384]{1,0:T(8,128)(2,1)S(1)}, u32[]{:S(2)}, u32[]{:S(2)}) collective-permute-start(bf16[384,384]{1,0:T(8,128)(2,1)S(1)} %subtract_convert_fusion.refs_0_), channel_id=1, source_target_pairs={{0,16},{4,20},{8,24},{12,28},{16,0},{20,4},{24,8},{28,12},{1,17},{... | collective-permute-start | bytes 884744 | tf_op jit(solution)/shard_map/ppermute | solution.py:52
  94.3 12.6 %collective-permute-start.8 = (bf16[384,384]{1,0:T(8,128)(2,1)S(1)}, bf16[384,384]{1,0:T(8,128)(2,1)S(1)}, u32[]{:S(2)}, u32[]{:S(2)}) collective-permute-start(bf16[384,384]{1,0:T(8,128)(2,1)S(1)} %subtract_convert_fusion.refs_0_), channel_id=1, source_target_pairs={{0,8},{4,12},{8,0},{12,4},{16,24},{20,28},{24,16},{28,20},{1,9},{5... | collective-permute-start | bytes 884744 | tf_op jit(solution)/shard_map/ppermute | solution.py:52
  94.9 12.5 %collective-permute-start.7 = (bf16[384,384]{1,0:T(8,128)(2,1)S(1)}, bf16[384,384]{1,0:T(8,128)(2,1)S(1)}, u32[]{:S(2)}, u32[]{:S(2)}) collective-permute-start(bf16[384,384]{1,0:T(8,128)(2,1)S(1)} %subtract_convert_fusion.refs_0_), channel_id=1, source_target_pairs={{0,4},{4,0},{8,12},{12,8},{16,20},{20,16},{24,28},{28,24},{1,5},{5... | collective-permute-start | bytes 884744 | tf_op jit(solution)/shard_map/ppermute | solution.py:52
  102.3 5.1 %collective-permute-start.13 = (bf16[384,384]{1,0:T(8,128)(2,1)S(1)}, bf16[384,384]{1,0:T(8,128)(2,1)S(1)}, u32[]{:S(2)}, u32[]{:S(2)}) collective-permute-start(bf16[384,384]{1,0:T(8,128)(2,1)S(1)} %collective-permute-done.12.refs_6_), channel_id=1, source_target_pairs={{0,4},{4,0},{8,12},{12,8},{16,20},{20,16},{24,28},{28,24},{1,5},{5... | collective-permute-start | bytes 884744 | tf_op jit(solution)/shard_map/ppermute | solution.py:52
  106.9 1.6 collective-permute-start.11
  106.9 2.0 collective-permute-start.9
  108.9 3.7 %copy-start.4 = (bf16[1536,3072]{1,0:T(8,128)(2,1)S(1)}, bf16[1536,3072]{1,0:T(8,128)(2,1)}, u32[]{:S(2)}) copy-start(bf16[1536,3072]{1,0:T(8,128)(2,1)} %a_ref.6) | copy-start | bytes 28311556
  112.6 7.7 %slice-start.2 = ((s8[9437184]{0:T(1024)(128)(4,1)}), s8[4194304]{0:T(1024)(128)(4,1)S(1)}, s32[]{:S(2)}) async-start(s8[9437184]{0:T(1024)(128)(4,1)} %bitcast.9), calls=%async_computation.5 | async-start | bytes 8388608
  112.6 7.7 %slice-start.3 = ((s8[9437184]{0:T(1024)(128)(4,1)}), s8[4194304]{0:T(1024)(128)(4,1)S(1)}, s32[]{:S(2)}) async-start(s8[9437184]{0:T(1024)(128)(4,1)} %bitcast.9), calls=%async_computation.6 | async-start | bytes 8388608
  115.1 5.2 %slice-start.4 = ((s8[9437184]{0:T(1024)(128)(4,1)}), s8[1048576]{0:T(1024)(128)(4,1)S(1)}, s32[]{:S(2)}) async-start(s8[9437184]{0:T(1024)(128)(4,1)} %bitcast.9), calls=%async_computation.7 | async-start | bytes 2097152
  115.1 10.0 %collective-permute-start.14 = (bf16[384,384]{1,0:T(8,128)(2,1)S(1)}, bf16[384,384]{1,0:T(8,128)(2,1)S(1)}, u32[]{:S(2)}, u32[]{:S(2)}) collective-permute-start(bf16[384,384]{1,0:T(8,128)(2,1)S(1)} %shard_map.82), channel_id=1, source_target_pairs={{0,3},{1,0},{2,1},{3,2},{4,7},{5,4},{6,5},{7,6},{8,11},{9,8},{10,9... | collective-permute-start | bytes 884744 | tf_op jit(solution)/shard_map/ppermute | solution.py:48
  117.7 56.2 %slice-start = ((s8[6291456]{0:T(1024)(128)(4,1)}), s8[4194304]{0:T(1024)(128)(4,1)S(1)}, s32[]{:S(2)}) async-start(s8[6291456]{0:T(1024)(128)(4,1)} %bitcast.7), calls=%async_computation.3 | async-start | bytes 8388608
  120.2 53.7 %slice-start.1 = ((s8[6291456]{0:T(1024)(128)(4,1)}), s8[2097152]{0:T(1024)(128)(4,1)S(1)}, s32[]{:S(2)}) async-start(s8[6291456]{0:T(1024)(128)(4,1)} %bitcast.7), calls=%async_computation.4 | async-start | bytes 4194304
  120.2 13.6 %collective-permute-start.16 = (bf16[384,384]{1,0:T(8,128)(2,1)S(1)}, bf16[384,384]{1,0:T(8,128)(2,1)S(1)}, u32[]{:S(2)}, u32[]{:S(2)}) collective-permute-start(bf16[384,384]{1,0:T(8,128)(2,1)S(1)} %shard_map.83), channel_id=1, source_target_pairs={{0,1},{1,2},{2,3},{3,0},{4,5},{5,6},{6,7},{7,4},{8,9},{9,10},{10,1... | collective-permute-start | bytes 884744 | tf_op jit(solution)/shard_map/ppermute | solution.py:48
  125.1 13.9 %collective-permute-start.15 = (bf16[384,384]{1,0:T(8,128)(2,1)S(1)}, bf16[384,384]{1,0:T(8,128)(2,1)S(1)}, u32[]{:S(2)}, u32[]{:S(2)}) collective-permute-start(bf16[384,384]{1,0:T(8,128)(2,1)S(1)} %add_convert_fusion.3), channel_id=1, source_target_pairs={{0,3},{1,0},{2,1},{3,2},{4,7},{5,4},{6,5},{7,6},{8,11},{9,8},{10,9... | collective-permute-start | bytes 884744 | tf_op jit(solution)/shard_map/ppermute | solution.py:48
  159.7 9.6 %collective-permute-start.22 = (bf16[384,384]{1,0:T(8,128)(2,1)S(1)}, bf16[384,384]{1,0:T(8,128)(2,1)S(1)}, u32[]{:S(2)}, u32[]{:S(2)}) collective-permute-start(bf16[384,384]{1,0:T(8,128)(2,1)S(1)} %bitcast.11), channel_id=1, source_target_pairs={{0,24},{4,28},{8,16},{12,20},{16,8},{20,12},{24,0},{28,4},{1,25},{... | collective-permute-start | bytes 884744 | tf_op jit(solution)/shard_map/ppermute | solution.py:52
  160.3 11.6 %collective-permute-start.20 = (bf16[384,384]{1,0:T(8,128)(2,1)S(1)}, bf16[384,384]{1,0:T(8,128)(2,1)S(1)}, u32[]{:S(2)}, u32[]{:S(2)}) collective-permute-start(bf16[384,384]{1,0:T(8,128)(2,1)S(1)} %bitcast.12), channel_id=1, source_target_pairs={{0,16},{4,20},{8,24},{12,28},{16,0},{20,4},{24,8},{28,12},{1,17},{... | collective-permute-start | bytes 884744 | tf_op jit(solution)/shard_map/ppermute | solution.py:52
  161.8 10.0 %collective-permute-start.18 = (bf16[384,384]{1,0:T(8,128)(2,1)S(1)}, bf16[384,384]{1,0:T(8,128)(2,1)S(1)}, u32[]{:S(2)}, u32[]{:S(2)}) collective-permute-start(bf16[384,384]{1,0:T(8,128)(2,1)S(1)} %bitcast.13), channel_id=1, source_target_pairs={{0,8},{4,12},{8,0},{12,4},{16,24},{20,28},{24,16},{28,20},{1,9},{5... | collective-permute-start | bytes 884744 | tf_op jit(solution)/shard_map/ppermute | solution.py:52
  163.1 9.2 %collective-permute-start.17 = (bf16[384,384]{1,0:T(8,128)(2,1)S(1)}, bf16[384,384]{1,0:T(8,128)(2,1)S(1)}, u32[]{:S(2)}, u32[]{:S(2)}) collective-permute-start(bf16[384,384]{1,0:T(8,128)(2,1)S(1)} %bitcast.14), channel_id=1, source_target_pairs={{0,4},{4,0},{8,12},{12,8},{16,20},{20,16},{24,28},{28,24},{1,5},{5... | collective-permute-start | bytes 884744 | tf_op jit(solution)/shard_map/ppermute | solution.py:52
  169.3 3.1 %collective-permute-start.23 = (bf16[384,384]{1,0:T(8,128)(2,1)S(1)}, bf16[384,384]{1,0:T(8,128)(2,1)S(1)}, u32[]{:S(2)}, u32[]{:S(2)}) collective-permute-start(bf16[384,384]{1,0:T(8,128)(2,1)S(1)} %collective-permute-done.22.refs_6_), channel_id=1, source_target_pairs={{0,4},{4,0},{8,12},{12,8},{16,20},{20,16},{24,28},{28,24},{1,5},{5... | collective-permute-start | bytes 884744 | tf_op jit(solution)/shard_map/ppermute | solution.py:52
  171.9 1.6 collective-permute-start.21
  171.9 2.0 collective-permute-start.19
  179.2 12.5 %collective-permute-start.24 = (bf16[384,512]{1,0:T(8,128)(2,1)S(1)}, bf16[384,512]{1,0:T(8,128)(2,1)S(1)}, u32[]{:S(2)}, u32[]{:S(2)}) collective-permute-start(bf16[384,512]{1,0:T(8,128)(2,1)S(1)} %get-tuple-element.19), channel_id=1, source_target_pairs={{0,3},{1,0},{2,1},{3,2},{4,7},{5,4},{6,5},{7,6},{8,11},{9,8},{10,9... | collective-permute-start | bytes 1179656 | tf_op jit(solution)/shard_map/ppermute | solution.py:48
  183.5 17.1 %collective-permute-start.26 = (bf16[384,512]{1,0:T(8,128)(2,1)S(1)}, bf16[384,512]{1,0:T(8,128)(2,1)S(1)}, u32[]{:S(2)}, u32[]{:S(2)}) collective-permute-start(bf16[384,512]{1,0:T(8,128)(2,1)S(1)} %shard_map.86), channel_id=1, source_target_pairs={{0,1},{1,2},{2,3},{3,0},{4,5},{5,6},{6,7},{7,4},{8,9},{9,10},{10,1... | collective-permute-start | bytes 1179656 | tf_op jit(solution)/shard_map/ppermute | solution.py:48
  191.9 16.6 %collective-permute-start.25 = (bf16[384,512]{1,0:T(8,128)(2,1)S(1)}, bf16[384,512]{1,0:T(8,128)(2,1)S(1)}, u32[]{:S(2)}, u32[]{:S(2)}) collective-permute-start(bf16[384,512]{1,0:T(8,128)(2,1)S(1)} %add_convert_fusion.2), channel_id=1, source_target_pairs={{0,3},{1,0},{2,1},{3,2},{4,7},{5,4},{6,5},{7,6},{8,11},{9,8},{10,9... | collective-permute-start | bytes 1179656 | tf_op jit(solution)/shard_map/ppermute | solution.py:48
  208.7 13.9 %collective-permute-start.27 = (bf16[384,512]{1,0:T(8,128)(2,1)S(1)}, bf16[384,512]{1,0:T(8,128)(2,1)S(1)}, u32[]{:S(2)}, u32[]{:S(2)}) collective-permute-start(bf16[384,512]{1,0:T(8,128)(2,1)S(1)} %add_convert_fusion.1.refs_3_), channel_id=1, source_target_pairs={{0,1},{1,2},{2,3},{3,0},{4,5},{5,6},{6,7},{7,4},{8,9},{9,10},{10,1... | collective-permute-start | bytes 1179656 | tf_op jit(solution)/shard_map/ppermute | solution.py:48
  209.3 19.2 %collective-permute-start.29 = (bf16[384,512]{1,0:T(8,128)(2,1)S(1)}, bf16[384,512]{1,0:T(8,128)(2,1)S(1)}, u32[]{:S(2)}, u32[]{:S(2)}) collective-permute-start(bf16[384,512]{1,0:T(8,128)(2,1)S(1)} %add_convert_fusion.1.refs_3_), channel_id=1, source_target_pairs={{0,3},{1,0},{2,1},{3,2},{4,7},{5,4},{6,5},{7,6},{8,11},{9,8},{10,9... | collective-permute-start | bytes 1179656 | tf_op jit(solution)/shard_map/ppermute | solution.py:48
  222.5 15.9 %collective-permute-start.28 = (bf16[384,512]{1,0:T(8,128)(2,1)S(1)}, bf16[384,512]{1,0:T(8,128)(2,1)S(1)}, u32[]{:S(2)}, u32[]{:S(2)}) collective-permute-start(bf16[384,512]{1,0:T(8,128)(2,1)S(1)} %collective-permute-done.27.refs_4_), channel_id=1, source_target_pairs={{0,1},{1,2},{2,3},{3,0},{4,5},{5,6},{6,7},{7,4},{8,9},{9,10},{10,1... | collective-permute-start | bytes 1179656 | tf_op jit(solution)/shard_map/ppermute | solution.py:48

commit v5 on v4

--- a/solution.py
+++ b/solution.py
@@ -451,6 +451,14 @@
             and arrays[2].shape[1] % (n_row * BLK) == 0
             and width % BLK == 0
         )
-        return (solve if fits else solve_plain)(n_front, n_row, *arrays)
+        if not fits:
+            return solve_plain(n_front, n_row, *arrays)
+        cut = width * 2 // 3 // BLK * BLK
+        parts = [
+            solve(n_front, n_row, arrays[0][:, low:high], arrays[1][:, low:high], *arrays[2:])
+            for low, high in ((0, cut), (cut, width))
+            if high > low
+        ]
+        return tuple(jnp.concatenate(outs, axis=1) for outs in zip(*parts))
 
     return jax.shard_map(per_device, mesh=mesh, in_specs=in_specs, out_specs=out_specs, check_vma=False)

time: 241 us -> 276 us (1.15)
  waiting for transfers between devices: 134 us -> 82.6 us
  starting transfers between devices: 39.6 us -> 81.6 us
  local copies, waits for them, and re-layouts: 9.09 us -> 43.1 us
  Pallas kernels: 32.1 us -> 49 us
  blocking collectives: 19.7 us -> 9.36 us
    ppermute x15 -> x30, waiting for transfers between devices: 91.4 us -> 59.6 us  [shift(): return lax.ppermute(x, 'row', [(i, (i + by) % size) for i in range(size)])]
    unnamed x24 -> x46, local copies, waits for them, and re-layouts: 9.09 us -> 37.4 us
    ppermute x15 -> x30, starting transfers between devices: 27.2 us -> 44.8 us  [shift(): return lax.ppermute(x, 'row', [(i, (i + by) % size) for i in range(size)])]
    all_to_all x1 -> x2, waiting for transfers between devices: 15.7 us -> 0.01 us  [solve(): lax.all_to_all(both.reshape(n_front // 2, piece_rows, width), 'front', 0,...]
    all_to_all x0 -> x3, starting transfers between devices: none -> 11.2 us  [the longest x2 7.84 us: solve(): quarters = lax.all_to_all(quarters, 'front', 0, 0, axis_index_groups=chips)]
    pallas_call x3 -> x6, Pallas kernels: 9.1 us -> 19.7 us  [root_products(): kernel_call(body, [jax.ShapeDtypeStruct((rows, width), kind) for kind in...]
    ppermute x15 -> x30, waiting for transfers between devices: 26.5 us -> 16 us  [swap(): return lax.ppermute(x, 'front', [(i, i ^ by) for i in range(size)])]
    ppermute x15 -> x30, starting transfers between devices: 8.11 us -> 17.3 us  [swap(): return lax.ppermute(x, 'front', [(i, i ^ by) for i in range(size)])]
  transfers between devices with their start and end apart: 31 -> 65, of which waited for: 24 -> 31; matrix products, arithmetic and copies ran while one was open for 0% -> 4% of each run, Pallas kernels for 8% -> 16%
where the time goes in v5:
time: 276 us; the launch traced here: 275 us
  waiting for transfers between devices  82.6 us (30%)
  starting transfers between devices  81.6 us (30%)
  Pallas kernels  49 us (18%)
  local copies, waits for them, and re-layouts  43.1 us (16%)
  blocking collectives  9.36 us (3%)
  other arithmetic  8.01 us (3%)
    ppermute x30, waiting for transfers between devices, shift(): return lax.ppermute(x, 'row', [(i, (i + by) % size) for i in range(size)])  59.6 us
    ppermute x30, starting transfers between devices, shift(): return lax.ppermute(x, 'row', [(i, (i + by) % size) for i in range(size)])  44.8 us
    unnamed x46, local copies, waits for them, and re-layouts  37.4 us
    pallas_call x6, Pallas kernels, root_products(): kernel_call(body, [jax.ShapeDtypeStruct((rows, width), kind) for kind in...  19.7 us
    ppermute x30, starting transfers between devices, swap(): return lax.ppermute(x, 'front', [(i, i ^ by) for i in range(size)])  17.3 us
    ppermute x30, waiting for transfers between devices, swap(): return lax.ppermute(x, 'front', [(i, i ^ by) for i in range(size)])  16 us
    all_to_all x1, blocking collectives, solve(): quarters = lax.all_to_all(quarters, 'row', 0, 0)  9.36 us
    all_to_all x2, starting transfers between devices, solve(): lax.all_to_all(both.reshape(n_front // 2, piece_rows, width), 'front', 0,...  8.33 us
  transfers between devices with their start and end apart: 65, of which 31 were waited for; matrix products, arithmetic and copies ran while one was open for 4% of the time, Pallas kernels for 16%

profile of v5, /device:TPU:0, one launch (start us, length us, event | category | flops | bytes accessed | tf_op | source)
XLA Modules:
  0.0 274.8 jit_solution(958096347896345255)
XLA Ops:
  1.6 3.1 %collective-permute-start = (bf16[512,256]{1,0:T(8,128)(2,1)S(1)}, bf16[512,256]{1,0:T(8,128)(2,1)S(1)}, u32[]{:S(2)}, u32[]{:S(2)}) collective-permute-start(bf16[512,256]{1,0:T(8,128)(2,1)S(1)} %slice.13.refs_3_), channel_id=1, source_target_pairs={{0,1},{1,2},{2,3},{3,0},{4,5},{5,6},{6,7},{7,4},{8,9},{9,10},{10,1... | collective-permute-start | bytes 786440 | tf_op jit(solution)/shard_map/ppermute | solution.py:48
  4.7 2.1 collective-permute-start.2
  6.8 7.1 %collective-permute-done.refs_4_ = bf16[512,256]{1,0:T(8,128)(2,1)S(1)} collective-permute-done((bf16[512,256]{1,0:T(8,128)(2,1)S(1)}, bf16[512,256]{1,0:T(8,128)(2,1)S(1)}, u32[]{:S(2)}, u32[]{:S(2)}) %collective-permute-start) | collective-permute-done | bytes 262176 | tf_op jit(solution)/shard_map/ppermute | solution.py:48
  14.0 4.3 %collective-permute-done.2.refs_5_ = bf16[512,256]{1,0:T(8,128)(2,1)S(1)} collective-permute-done((bf16[512,256]{1,0:T(8,128)(2,1)S(1)}, bf16[512,256]{1,0:T(8,128)(2,1)S(1)}, u32[]{:S(2)}, u32[]{:S(2)}) %collective-permute-start.2) | collective-permute-done | bytes 262176 | tf_op jit(solution)/shard_map/ppermute | solution.py:48
  21.0 3.3 %collective-permute-done.1.refs_1_ = bf16[512,256]{1,0:T(8,128)(2,1)S(1)} collective-permute-done((bf16[512,256]{1,0:T(8,128)(2,1)S(1)}, bf16[512,256]{1,0:T(8,128)(2,1)S(1)}, u32[]{:S(2)}, u32[]{:S(2)}) %collective-permute-start.1) | collective-permute-done | bytes 262176 | tf_op jit(solution)/shard_map/ppermute | solution.py:48
  25.2 3.8 %collective-permute-start.5 = (bf16[512,256]{1,0:T(8,128)(2,1)S(1)}, bf16[512,256]{1,0:T(8,128)(2,1)S(1)}, u32[]{:S(2)}, u32[]{:S(2)}) collective-permute-start(bf16[512,256]{1,0:T(8,128)(2,1)S(1)} %get-tuple-element.22.refs_3_), channel_id=1, source_target_pairs={{0,3},{1,0},{2,1},{3,2},{4,7},{5,4},{6,5},{7,6},{8,11},{9,8},{10,9... | collective-permute-start | bytes 786440 | tf_op jit(solution)/shard_map/ppermute | solution.py:48
  29.0 7.3 %collective-permute-done.3.refs_4_ = bf16[512,256]{1,0:T(8,128)(2,1)S(1)} collective-permute-done((bf16[512,256]{1,0:T(8,128)(2,1)S(1)}, bf16[512,256]{1,0:T(8,128)(2,1)S(1)}, u32[]{:S(2)}, u32[]{:S(2)}) %collective-permute-start.3) | collective-permute-done | bytes 262176 | tf_op jit(solution)/shard_map/ppermute | solution.py:48
  36.3 3.3 %collective-permute-done.5.refs_5_ = bf16[512,256]{1,0:T(8,128)(2,1)S(1)} collective-permute-done((bf16[512,256]{1,0:T(8,128)(2,1)S(1)}, bf16[512,256]{1,0:T(8,128)(2,1)S(1)}, u32[]{:S(2)}, u32[]{:S(2)}) %collective-permute-start.5) | collective-permute-done | bytes 262176 | tf_op jit(solution)/shard_map/ppermute | solution.py:48
  39.6 2.8 %copy-done = bf16[1536,2048]{1,0:T(8,128)(2,1)S(1)} copy-done((bf16[1536,2048]{1,0:T(8,128)(2,1)S(1)}, bf16[1536,2048]{1,0:T(8,128)(2,1)}, u32[]{:S(2)}) %copy-start) | copy-done | bytes 6291480
  42.4 2.8 %shard_map.79.refs_2_ = f32[1536,256]{1,0:T(8,128)S(1)} custom-call(s32[2]{0:T(128)S(1)} %pad_add_fusion.at_ref, bf16[1536,2048]{1,0:T(8,128)(2,1)S(1)} %copy-done, bf16[1536,2048]{1,0:T(8,128)(2,1)S(1)} %copy-done, bf16[1536,2048]{1,0:T(8,128)(2,1)S(1)} %copy-done, bf16[512,256]{1,0:T(8,128)(2,1)S(1)} %get-tuple-element.22.refs_3_, ...), custom_call_target="tpu_custom_call" | custom-call | flops 1207959552 | bytes 4718592 | tf_op jit(solution)/shard_map/pallas_call | solution.py:150
  45.2 2.0 shard_map.80
  47.3 2.3 collective-permute-done.6
  50.7 4.2 %all-to-all-start = ((bf16[4,384,256]{2,1,0:T(8,128)(2,1)}), bf16[4,384,256]{2,1,0:T(8,128)(2,1)}, u32[]{:S(2)}, u32[]{:S(2)}) async-start(bf16[4,384,256]{2,1,0:T(8,128)(2,1)} %bitcast.24), calls=%async_computation | async-start | bytes 1572864 | tf_op jit(solution)/shard_map/all_to_all | solution.py:363
  56.0 3.7 %collective-permute-start.32 = (bf16[512,128]{1,0:T(8,128)(2,1)S(1)}, bf16[512,128]{1,0:T(8,128)(2,1)S(1)}, u32[]{:S(2)}, u32[]{:S(2)}) collective-permute-start(bf16[512,128]{1,0:T(8,128)(2,1)S(1)} %slice.15.refs_3_), channel_id=1, source_target_pairs={{0,3},{1,0},{2,1},{3,2},{4,7},{5,4},{6,5},{7,6},{8,11},{9,8},{10,9... | collective-permute-start | bytes 393224 | tf_op jit(solution)/shard_map/ppermute | solution.py:48
  59.7 4.3 %collective-permute-done.30.refs_4_ = bf16[512,128]{1,0:T(8,128)(2,1)S(1)} collective-permute-done((bf16[512,128]{1,0:T(8,128)(2,1)S(1)}, bf16[512,128]{1,0:T(8,128)(2,1)S(1)}, u32[]{:S(2)}, u32[]{:S(2)}) %collective-permute-start.30) | collective-permute-done | bytes 131104 | tf_op jit(solution)/shard_map/ppermute | solution.py:48
  68.0 2.8 %collective-permute-done.31.refs_1_ = bf16[512,128]{1,0:T(8,128)(2,1)S(1)} collective-permute-done((bf16[512,128]{1,0:T(8,128)(2,1)S(1)}, bf16[512,128]{1,0:T(8,128)(2,1)S(1)}, u32[]{:S(2)}, u32[]{:S(2)}) %collective-permute-start.31) | collective-permute-done | bytes 131104 | tf_op jit(solution)/shard_map/ppermute | solution.py:48
  71.8 3.7 %collective-permute-start.35 = (bf16[512,128]{1,0:T(8,128)(2,1)S(1)}, bf16[512,128]{1,0:T(8,128)(2,1)S(1)}, u32[]{:S(2)}, u32[]{:S(2)}) collective-permute-start(bf16[512,128]{1,0:T(8,128)(2,1)S(1)} %get-tuple-element.32.refs_3_), channel_id=1, source_target_pairs={{0,3},{1,0},{2,1},{3,2},{4,7},{5,4},{6,5},{7,6},{8,11},{9,8},{10,9... | collective-permute-start | bytes 393224 | tf_op jit(solution)/shard_map/ppermute | solution.py:48
  75.5 3.1 %collective-permute-done.33.refs_4_ = bf16[512,128]{1,0:T(8,128)(2,1)S(1)} collective-permute-done((bf16[512,128]{1,0:T(8,128)(2,1)S(1)}, bf16[512,128]{1,0:T(8,128)(2,1)S(1)}, u32[]{:S(2)}, u32[]{:S(2)}) %collective-permute-start.33) | collective-permute-done | bytes 131104 | tf_op jit(solution)/shard_map/ppermute | solution.py:48
  78.7 2.7 shard_map.91.refs_2_
  81.5 3.9 %collective-permute-done.34.refs_1_ = bf16[512,128]{1,0:T(8,128)(2,1)S(1)} collective-permute-done((bf16[512,128]{1,0:T(8,128)(2,1)S(1)}, bf16[512,128]{1,0:T(8,128)(2,1)S(1)}, u32[]{:S(2)}, u32[]{:S(2)}) %collective-permute-start.34) | collective-permute-done | bytes 131104 | tf_op jit(solution)/shard_map/ppermute | solution.py:48
  85.4 2.6 shard_map.92
  88.0 3.7 %slice.12 = f32[3072,256]{1,0:T(8,128)} slice(f32[3072,384]{1,0:T(8,128)} %param.7), slice={[0:3072], [0:256]} | slice | bytes 6291456 | tf_op jit(solution)/shard_map/slice | solution.py:458
  94.2 2.0 collective-permute-start.10
  98.6 4.1 %all-to-all-start.3 = ((bf16[4,384,128]{2,1,0:T(8,128)(2,1)}), bf16[4,384,128]{2,1,0:T(8,128)(2,1)S(1)}, u32[]{:S(2)}, u32[]{:S(2)}) async-start(bf16[4,384,128]{2,1,0:T(8,128)(2,1)} %bitcast.6), calls=%async_computation.3 | async-start | bytes 786432 | tf_op jit(solution)/shard_map/all_to_all | solution.py:363
  102.7 3.5 %collective-permute-done.10.refs_4_ = bf16[384,256]{1,0:T(8,128)(2,1)S(1)} collective-permute-done((bf16[384,256]{1,0:T(8,128)(2,1)S(1)}, bf16[384,256]{1,0:T(8,128)(2,1)S(1)}, u32[]{:S(2)}, u32[]{:S(2)}) %collective-permute-start.10) | collective-permute-done | bytes 196640 | tf_op jit(solution)/shard_map/ppermute | solution.py:52
  109.1 3.7 %copy-done.13 = bf16[1536,3072]{1,0:T(8,128)(2,1)S(1)} copy-done((bf16[1536,3072]{1,0:T(8,128)(2,1)S(1)}, bf16[1536,3072]{1,0:T(8,128)(2,1)}, u32[]{:S(2)}) %copy-start.13) | copy-done | bytes 9437208
  112.8 3.5 %shard_map.82 = bf16[384,256]{1,0:T(8,128)(2,1)S(1)} custom-call(s32[2]{0:T(128)S(1)} %pad_add_fusion.at_ref, bf16[1536,3072]{1,0:T(8,128)(2,1)S(1)} %copy-done.13, bf16[384,256]{1,0:T(8,128)(2,1)S(1)} %subtract_convert_fusion.refs_0_, bf16[384,256]{1,0:T(8,128)(2,1)S(1)} %collective-permute-done.7.refs_1_, ...), custom_call_target="tpu_custom_call" | custom-call | flops 603979776 | bytes 2359296 | tf_op jit(solution)/shard_map/pallas_call | solution.py:253
  116.6 3.7 %copy-done.14 = bf16[1536,3072]{1,0:T(8,128)(2,1)S(1)} copy-done((bf16[1536,3072]{1,0:T(8,128)(2,1)S(1)}, bf16[1536,3072]{1,0:T(8,128)(2,1)}, u32[]{:S(2)}) %copy-start.14) | copy-done | bytes 9437208
  120.2 3.5 %shard_map.83 = bf16[384,256]{1,0:T(8,128)(2,1)S(1)} custom-call(s32[2]{0:T(128)S(1)} %pad_add_fusion.at_ref, bf16[1536,3072]{1,0:T(8,128)(2,1)S(1)} %copy-done.14, bf16[384,256]{1,0:T(8,128)(2,1)S(1)} %subtract_convert_fusion.refs_0_, bf16[384,256]{1,0:T(8,128)(2,1)S(1)} %collective-permute-done.7.refs_1_, ...), custom_call_target="tpu_custom_call" | custom-call | flops 603979776 | bytes 2359296 | tf_op jit(solution)/shard_map/pallas_call | solution.py:253
  123.8 2.0 collective-permute-start.16
  125.8 3.7 %copy-done.15 = bf16[1536,3072]{1,0:T(8,128)(2,1)S(1)} copy-done((bf16[1536,3072]{1,0:T(8,128)(2,1)S(1)}, bf16[1536,3072]{1,0:T(8,128)(2,1)}, u32[]{:S(2)}) %copy-start.15) | copy-done | bytes 9437208
  129.4 4.3 %shard_map.81 = (f32[384,256]{1,0:T(8,128)S(1)}, f32[384,256]{1,0:T(8,128)S(1)}) custom-call(s32[2]{0:T(128)S(1)} %pad_add_fusion.at_ref, bf16[1536,3072]{1,0:T(8,128)(2,1)S(1)} %copy-done.15, bf16[384,256]{1,0:T(8,128)(2,1)S(1)} %subtract_convert_fusion.refs_0_, bf16[384,256]{1,0:T(8,128)(2,1)S(1)} %collective-permute-done.7.refs_1_, ...), custom_call_target="tpu_custom_call" | custom-call | flops 1207959552 | bytes 4718592 | tf_op jit(solution)/shard_map/pallas_call | solution.py:253
  135.8 2.0 collective-permute-start.38
  140.8 2.6 collective-permute-done.40.refs_4_
  146.0 4.0 %all-to-all-start.1 = ((bf16[4,96,256]{2,1,0:T(8,128)(2,1)}), bf16[4,96,256]{2,1,0:T(8,128)(2,1)}, u32[]{:S(2)}, u32[]{:S(2)}) async-start(bf16[4,96,256]{2,1,0:T(8,128)(2,1)} %bitcast.4), calls=%async_computation.1 | async-start | bytes 393216 | tf_op jit(solution)/shard_map/all_to_all | solution.py:379
  150.1 3.7 %copy-done.16 = bf16[1536,3072]{1,0:T(8,128)(2,1)S(1)} copy-done((bf16[1536,3072]{1,0:T(8,128)(2,1)S(1)}, bf16[1536,3072]{1,0:T(8,128)(2,1)}, u32[]{:S(2)}) %copy-start.16) | copy-done | bytes 9437208
  153.8 2.5 shard_map.94
  156.3 2.5 shard_map.95
  158.8 2.1 collective-permute-start.46
  160.9 3.3 %shard_map.93 = (f32[384,128]{1,0:T(8,128)S(1)}, f32[384,128]{1,0:T(8,128)S(1)}) custom-call(s32[2]{0:T(128)S(1)} %pad_add_fusion.at_ref, bf16[1536,3072]{1,0:T(8,128)(2,1)S(1)} %bitcast.13, bf16[384,128]{1,0:T(8,128)(2,1)S(1)} %subtract_convert_fusion.1.refs_0_, bf16[384,128]{1,0:T(8,128)(2,1)S(1)} %collective-permute-done.37.refs_1_, ...), custom_call_target="tpu_custom_call" | custom-call | flops 603979776 | bytes 4718592 | tf_op jit(solution)/shard_map/pallas_call | solution.py:253
  164.2 3.4 %all-to-all-start.2 = ((bf16[4,96,256]{2,1,0:T(8,128)(2,1)}), bf16[4,96,256]{2,1,0:T(8,128)(2,1)S(1)}, u32[]{:S(2)}, u32[]{:S(2)}) async-start(bf16[4,96,256]{2,1,0:T(8,128)(2,1)} %all-to-all-done.1), calls=%async_computation.2 | async-start | bytes 393216 | tf_op jit(solution)/shard_map/all_to_all | solution.py:380
  167.6 3.8 %collective-permute-start.45 = (bf16[384,128]{1,0:T(8,128)(2,1)S(1)}, bf16[384,128]{1,0:T(8,128)(2,1)S(1)}, u32[]{:S(2)}, u32[]{:S(2)}) collective-permute-start(bf16[384,128]{1,0:T(8,128)(2,1)S(1)} %add_convert_fusion.7), channel_id=1, source_target_pairs={{0,3},{1,0},{2,1},{3,2},{4,7},{5,4},{6,5},{7,6},{8,11},{9,8},{10,9... | collective-permute-start | bytes 294920 | tf_op jit(solution)/shard_map/ppermute | solution.py:48
  171.5 4.6 %all-to-all-done.2 = bf16[4,96,256]{2,1,0:T(8,128)(2,1)S(1)} async-done(((bf16[4,96,256]{2,1,0:T(8,128)(2,1)}), bf16[4,96,256]{2,1,0:T(8,128)(2,1)S(1)}, u32[]{:S(2)}, u32[]{:S(2)}) %all-to-all-start.2) | async-done | bytes 196640 | tf_op jit(solution)/shard_map/all_to_all | solution.py:380
  180.2 3.8 %all-to-all-start.4 = ((bf16[4,96,128]{2,1,0:T(8,128)(2,1)}), bf16[4,96,128]{2,1,0:T(8,128)(2,1)S(1)}, u32[]{:S(2)}, u32[]{:S(2)}) async-start(bf16[4,96,128]{2,1,0:T(8,128)(2,1)} %bitcast.7), calls=%async_computation.4 | async-start | bytes 196608 | tf_op jit(solution)/shard_map/all_to_all | solution.py:379
  186.5 2.5 all-to-all-done.4
  189.0 9.4 %all_to_all.30 = bf16[4,96,128]{2,1,0:T(8,128)(2,1)S(1)} all-to-all(bf16[4,96,128]{2,1,0:T(8,128)(2,1)S(1)} %all-to-all-done.4), channel_id=1, replica_groups=mesh['front'=8,'row'=4] {'row'}, dimensions={0} | all-to-all | bytes 196608 | tf_op jit(solution)/shard_map/all_to_all | solution.py:380
  199.5 2.4 collective-permute-start.52
  201.8 2.8 %copy-done.2 = bf16[1536,2048]{1,0:T(8,128)(2,1)S(1)} copy-done((bf16[1536,2048]{1,0:T(8,128)(2,1)S(1)}, bf16[1536,2048]{1,0:T(8,128)(2,1)}, u32[]{:S(2)}) %copy-start.2) | copy-done | bytes 6291480
  204.6 4.0 %shard_map.84 = (bf16[256,512]{1,0:T(8,128)(2,1)S(1)}, bf16[256,1536]{1,0:T(8,128)(2,1)S(1)}) custom-call(s32[2]{0:T(128)S(1)} %pad_add_fusion.at_ref, s32[12]{0:T(128)S(1)} %subtract_bitcast_fusion.index_ref, bf16[1536,2048]{1,0:T(8,128)(2,1)S(1)} %copy-done.2, bf16[384,256]{1,0:T(8,128)(2,1)S(1)} %bitcast.18, ...), custom_call_target="tpu_custom_call" | custom-call | flops 402653184 | bytes 1572864 | tf_op jit(solution)/shard_map/pallas_call | solution.py:296
  211.7 2.8 %copy-done.3 = bf16[1536,2048]{1,0:T(8,128)(2,1)S(1)} copy-done((bf16[1536,2048]{1,0:T(8,128)(2,1)S(1)}, bf16[1536,2048]{1,0:T(8,128)(2,1)}, u32[]{:S(2)}) %copy-start.3) | copy-done | bytes 6291480
  214.5 2.7 shard_map.96
  218.4 2.8 %copy-done.4 = bf16[1536,2048]{1,0:T(8,128)(2,1)S(1)} copy-done((bf16[1536,2048]{1,0:T(8,128)(2,1)S(1)}, bf16[1536,2048]{1,0:T(8,128)(2,1)}, u32[]{:S(2)}) %copy-start.4) | copy-done | bytes 6291480
  223.0 2.8 %copy-done.5 = bf16[1536,2048]{1,0:T(8,128)(2,1)S(1)} copy-done((bf16[1536,2048]{1,0:T(8,128)(2,1)S(1)}, bf16[1536,2048]{1,0:T(8,128)(2,1)}, u32[]{:S(2)}) %copy-start.5) | copy-done | bytes 6291480
  227.9 2.8 %copy-done.6 = bf16[1536,2048]{1,0:T(8,128)(2,1)S(1)} copy-done((bf16[1536,2048]{1,0:T(8,128)(2,1)S(1)}, bf16[1536,2048]{1,0:T(8,128)(2,1)}, u32[]{:S(2)}) %copy-start.6) | copy-done | bytes 6291480
  232.3 2.9 %collective-permute-start.25 = (bf16[256,512]{1,0:T(8,128)(2,1)S(1)}, bf16[256,512]{1,0:T(8,128)(2,1)S(1)}, u32[]{:S(2)}, u32[]{:S(2)}) collective-permute-start(bf16[256,512]{1,0:T(8,128)(2,1)S(1)} %add_convert_fusion.3), channel_id=1, source_target_pairs={{0,3},{1,0},{2,1},{3,2},{4,7},{5,4},{6,5},{7,6},{8,11},{9,8},{10,9... | collective-permute-start | bytes 786440 | tf_op jit(solution)/shard_map/ppermute | solution.py:48
  235.2 2.8 %copy-done.7 = bf16[1536,2048]{1,0:T(8,128)(2,1)S(1)} copy-done((bf16[1536,2048]{1,0:T(8,128)(2,1)S(1)}, bf16[1536,2048]{1,0:T(8,128)(2,1)}, u32[]{:S(2)}) %copy-start.7) | copy-done | bytes 6291480
  240.5 2.0 collective-permute-done.25
  243.2 2.0 collective-permute-done.55
  245.8 3.3 %collective-permute-start.59 = (bf16[128,512]{1,0:T(8,128)(2,1)S(1)}, bf16[128,512]{1,0:T(8,128)(2,1)S(1)}, u32[]{:S(2)}, u32[]{:S(2)}) collective-permute-start(bf16[128,512]{1,0:T(8,128)(2,1)S(1)} %add_convert_fusion.5.refs_3_), channel_id=1, source_target_pairs={{0,3},{1,0},{2,1},{3,2},{4,7},{5,4},{6,5},{7,6},{8,11},{9,8},{10,9... | collective-permute-start | bytes 393224 | tf_op jit(solution)/shard_map/ppermute | solution.py:48
  249.1 7.4 %collective-permute-done.57.refs_4_ = bf16[128,512]{1,0:T(8,128)(2,1)S(1)} collective-permute-done((bf16[128,512]{1,0:T(8,128)(2,1)S(1)}, bf16[128,512]{1,0:T(8,128)(2,1)S(1)}, u32[]{:S(2)}, u32[]{:S(2)}) %collective-permute-start.57) | collective-permute-done | bytes 131104 | tf_op jit(solution)/shard_map/ppermute | solution.py:48
  256.5 3.8 %collective-permute-start.29 = (bf16[256,512]{1,0:T(8,128)(2,1)S(1)}, bf16[256,512]{1,0:T(8,128)(2,1)S(1)}, u32[]{:S(2)}, u32[]{:S(2)}) collective-permute-start(bf16[256,512]{1,0:T(8,128)(2,1)S(1)} %add_convert_fusion.2.refs_3_), channel_id=1, source_target_pairs={{0,3},{1,0},{2,1},{3,2},{4,7},{5,4},{6,5},{7,6},{8,11},{9,8},{10,9... | collective-permute-start | bytes 786440 | tf_op jit(solution)/shard_map/ppermute | solution.py:48
  261.4 3.4 %collective-permute-done.58.refs_1_ = bf16[128,512]{1,0:T(8,128)(2,1)S(1)} collective-permute-done((bf16[128,512]{1,0:T(8,128)(2,1)S(1)}, bf16[128,512]{1,0:T(8,128)(2,1)S(1)}, u32[]{:S(2)}, u32[]{:S(2)}) %collective-permute-start.58) | collective-permute-done | bytes 131104 | tf_op jit(solution)/shard_map/ppermute | solution.py:48
  266.5 2.4 collective-permute-done.29.refs_5_
  270.1 2.9 %collective-permute-done.28.refs_1_ = bf16[256,512]{1,0:T(8,128)(2,1)S(1)} collective-permute-done((bf16[256,512]{1,0:T(8,128)(2,1)S(1)}, bf16[256,512]{1,0:T(8,128)(2,1)S(1)}, u32[]{:S(2)}, u32[]{:S(2)}) %collective-permute-start.28) | collective-permute-done | bytes 262176 | tf_op jit(solution)/shard_map/ppermute | solution.py:48
  (162 shorter events, 54.9 us)
Async XLA Ops:
  1.6 12.3 %collective-permute-start = (bf16[512,256]{1,0:T(8,128)(2,1)S(1)}, bf16[512,256]{1,0:T(8,128)(2,1)S(1)}, u32[]{:S(2)}, u32[]{:S(2)}) collective-permute-start(bf16[512,256]{1,0:T(8,128)(2,1)S(1)} %slice.13.refs_3_), channel_id=1, source_target_pairs={{0,1},{1,2},{2,3},{3,0},{4,5},{5,6},{6,7},{7,4},{8,9},{9,10},{10,1... | collective-permute-start | bytes 786440 | tf_op jit(solution)/shard_map/ppermute | solution.py:48
  4.7 13.6 %collective-permute-start.2 = (bf16[512,256]{1,0:T(8,128)(2,1)S(1)}, bf16[512,256]{1,0:T(8,128)(2,1)S(1)}, u32[]{:S(2)}, u32[]{:S(2)}) collective-permute-start(bf16[512,256]{1,0:T(8,128)(2,1)S(1)} %slice.13.refs_3_), channel_id=1, source_target_pairs={{0,3},{1,0},{2,1},{3,2},{4,7},{5,4},{6,5},{7,6},{8,11},{9,8},{10,9... | collective-permute-start | bytes 786440 | tf_op jit(solution)/shard_map/ppermute | solution.py:48
  13.9 10.4 %collective-permute-start.1 = (bf16[512,256]{1,0:T(8,128)(2,1)S(1)}, bf16[512,256]{1,0:T(8,128)(2,1)S(1)}, u32[]{:S(2)}, u32[]{:S(2)}) collective-permute-start(bf16[512,256]{1,0:T(8,128)(2,1)S(1)} %collective-permute-done.refs_4_), channel_id=1, source_target_pairs={{0,1},{1,2},{2,3},{3,0},{4,5},{5,6},{6,7},{7,4},{8,9},{9,10},{10,1... | collective-permute-start | bytes 786440 | tf_op jit(solution)/shard_map/ppermute | solution.py:48
  25.1 11.2 %collective-permute-start.3 = (bf16[512,256]{1,0:T(8,128)(2,1)S(1)}, bf16[512,256]{1,0:T(8,128)(2,1)S(1)}, u32[]{:S(2)}, u32[]{:S(2)}) collective-permute-start(bf16[512,256]{1,0:T(8,128)(2,1)S(1)} %get-tuple-element.22.refs_3_), channel_id=1, source_target_pairs={{0,1},{1,2},{2,3},{3,0},{4,5},{5,6},{6,7},{7,4},{8,9},{9,10},{10,1... | collective-permute-start | bytes 786440 | tf_op jit(solution)/shard_map/ppermute | solution.py:48
  25.2 14.4 %collective-permute-start.5 = (bf16[512,256]{1,0:T(8,128)(2,1)S(1)}, bf16[512,256]{1,0:T(8,128)(2,1)S(1)}, u32[]{:S(2)}, u32[]{:S(2)}) collective-permute-start(bf16[512,256]{1,0:T(8,128)(2,1)S(1)} %get-tuple-element.22.refs_3_), channel_id=1, source_target_pairs={{0,3},{1,0},{2,1},{3,2},{4,7},{5,4},{6,5},{7,6},{8,11},{9,8},{10,9... | collective-permute-start | bytes 786440 | tf_op jit(solution)/shard_map/ppermute | solution.py:48
  36.3 8.9 %collective-permute-start.4 = (bf16[512,256]{1,0:T(8,128)(2,1)S(1)}, bf16[512,256]{1,0:T(8,128)(2,1)S(1)}, u32[]{:S(2)}, u32[]{:S(2)}) collective-permute-start(bf16[512,256]{1,0:T(8,128)(2,1)S(1)} %collective-permute-done.3.refs_4_), channel_id=1, source_target_pairs={{0,1},{1,2},{2,3},{3,0},{4,5},{5,6},{6,7},{7,4},{8,9},{9,10},{10,1... | collective-permute-start | bytes 786440 | tf_op jit(solution)/shard_map/ppermute | solution.py:48
  47.2 2.4 collective-permute-start.6
  50.7 41.1 %all-to-all-start = ((bf16[4,384,256]{2,1,0:T(8,128)(2,1)}), bf16[4,384,256]{2,1,0:T(8,128)(2,1)}, u32[]{:S(2)}, u32[]{:S(2)}) async-start(bf16[4,384,256]{2,1,0:T(8,128)(2,1)} %bitcast.24), calls=%async_computation | async-start | bytes 1572864 | tf_op jit(solution)/shard_map/all_to_all | solution.py:363
  55.8 8.2 %collective-permute-start.30 = (bf16[512,128]{1,0:T(8,128)(2,1)S(1)}, bf16[512,128]{1,0:T(8,128)(2,1)S(1)}, u32[]{:S(2)}, u32[]{:S(2)}) collective-permute-start(bf16[512,128]{1,0:T(8,128)(2,1)S(1)} %slice.15.refs_3_), channel_id=1, source_target_pairs={{0,1},{1,2},{2,3},{3,0},{4,5},{5,6},{6,7},{7,4},{8,9},{9,10},{10,1... | collective-permute-start | bytes 393224 | tf_op jit(solution)/shard_map/ppermute | solution.py:48
  56.0 9.3 %collective-permute-start.32 = (bf16[512,128]{1,0:T(8,128)(2,1)S(1)}, bf16[512,128]{1,0:T(8,128)(2,1)S(1)}, u32[]{:S(2)}, u32[]{:S(2)}) collective-permute-start(bf16[512,128]{1,0:T(8,128)(2,1)S(1)} %slice.15.refs_3_), channel_id=1, source_target_pairs={{0,3},{1,0},{2,1},{3,2},{4,7},{5,4},{6,5},{7,6},{8,11},{9,8},{10,9... | collective-permute-start | bytes 393224 | tf_op jit(solution)/shard_map/ppermute | solution.py:48
  64.0 6.8 %collective-permute-start.31 = (bf16[512,128]{1,0:T(8,128)(2,1)S(1)}, bf16[512,128]{1,0:T(8,128)(2,1)S(1)}, u32[]{:S(2)}, u32[]{:S(2)}) collective-permute-start(bf16[512,128]{1,0:T(8,128)(2,1)S(1)} %collective-permute-done.30.refs_4_), channel_id=1, source_target_pairs={{0,1},{1,2},{2,3},{3,0},{4,5},{5,6},{6,7},{7,4},{8,9},{9,10},{10,1... | collective-permute-start | bytes 393224 | tf_op jit(solution)/shard_map/ppermute | solution.py:48
  71.6 7.0 %collective-permute-start.33 = (bf16[512,128]{1,0:T(8,128)(2,1)S(1)}, bf16[512,128]{1,0:T(8,128)(2,1)S(1)}, u32[]{:S(2)}, u32[]{:S(2)}) collective-permute-start(bf16[512,128]{1,0:T(8,128)(2,1)S(1)} %get-tuple-element.32.refs_3_), channel_id=1, source_target_pairs={{0,1},{1,2},{2,3},{3,0},{4,5},{5,6},{6,7},{7,4},{8,9},{9,10},{10,1... | collective-permute-start | bytes 393224 | tf_op jit(solution)/shard_map/ppermute | solution.py:48
  71.8 6.9 %collective-permute-start.35 = (bf16[512,128]{1,0:T(8,128)(2,1)S(1)}, bf16[512,128]{1,0:T(8,128)(2,1)S(1)}, u32[]{:S(2)}, u32[]{:S(2)}) collective-permute-start(bf16[512,128]{1,0:T(8,128)(2,1)S(1)} %get-tuple-element.32.refs_3_), channel_id=1, source_target_pairs={{0,3},{1,0},{2,1},{3,2},{4,7},{5,4},{6,5},{7,6},{8,11},{9,8},{10,9... | collective-permute-start | bytes 393224 | tf_op jit(solution)/shard_map/ppermute | solution.py:48
  78.6 6.8 %collective-permute-start.34 = (bf16[512,128]{1,0:T(8,128)(2,1)S(1)}, bf16[512,128]{1,0:T(8,128)(2,1)S(1)}, u32[]{:S(2)}, u32[]{:S(2)}) collective-permute-start(bf16[512,128]{1,0:T(8,128)(2,1)S(1)} %collective-permute-done.33.refs_4_), channel_id=1, source_target_pairs={{0,1},{1,2},{2,3},{3,0},{4,5},{5,6},{6,7},{7,4},{8,9},{9,10},{10,1... | collective-permute-start | bytes 393224 | tf_op jit(solution)/shard_map/ppermute | solution.py:48
  88.0 9.7 %collective-permute-start.36 = (bf16[1536,128]{1,0:T(8,128)(2,1)}, bf16[1536,128]{1,0:T(8,128)(2,1)S(1)}, u32[]{:S(2)}, u32[]{:S(2)}) collective-permute-start(bf16[1536,128]{1,0:T(8,128)(2,1)} %get-tuple-element.34), channel_id=1, source_target_pairs={{0,4},{4,0},{8,12},{12,8},{16,20},{20,16},{24,28},{28,24},{1,5},{5... | collective-permute-start | bytes 1179656 | tf_op jit(solution)/shard_map/ppermute | solution.py:52
  94.2 12.1 %collective-permute-start.10 = (bf16[384,256]{1,0:T(8,128)(2,1)S(1)}, bf16[384,256]{1,0:T(8,128)(2,1)S(1)}, u32[]{:S(2)}, u32[]{:S(2)}) collective-permute-start(bf16[384,256]{1,0:T(8,128)(2,1)S(1)} %subtract_convert_fusion.refs_0_), channel_id=1, source_target_pairs={{0,16},{4,20},{8,24},{12,28},{16,0},{20,4},{24,8},{28,12},{1,17},{... | collective-permute-start | bytes 589832 | tf_op jit(solution)/shard_map/ppermute | solution.py:52
  96.2 10.0 %collective-permute-start.12 = (bf16[384,256]{1,0:T(8,128)(2,1)S(1)}, bf16[384,256]{1,0:T(8,128)(2,1)S(1)}, u32[]{:S(2)}, u32[]{:S(2)}) collective-permute-start(bf16[384,256]{1,0:T(8,128)(2,1)S(1)} %subtract_convert_fusion.refs_0_), channel_id=1, source_target_pairs={{0,24},{4,28},{8,16},{12,20},{16,8},{20,12},{24,0},{28,4},{1,25},{... | collective-permute-start | bytes 589832 | tf_op jit(solution)/shard_map/ppermute | solution.py:52
  97.6 10.0 %collective-permute-start.8 = (bf16[384,256]{1,0:T(8,128)(2,1)S(1)}, bf16[384,256]{1,0:T(8,128)(2,1)S(1)}, u32[]{:S(2)}, u32[]{:S(2)}) collective-permute-start(bf16[384,256]{1,0:T(8,128)(2,1)S(1)} %subtract_convert_fusion.refs_0_), channel_id=1, source_target_pairs={{0,8},{4,12},{8,0},{12,4},{16,24},{20,28},{24,16},{28,20},{1,9},{5... | collective-permute-start | bytes 589832 | tf_op jit(solution)/shard_map/ppermute | solution.py:52
  98.6 17.9 %all-to-all-start.3 = ((bf16[4,384,128]{2,1,0:T(8,128)(2,1)}), bf16[4,384,128]{2,1,0:T(8,128)(2,1)S(1)}, u32[]{:S(2)}, u32[]{:S(2)}) async-start(bf16[4,384,128]{2,1,0:T(8,128)(2,1)} %bitcast.6), calls=%async_computation.3 | async-start | bytes 786432 | tf_op jit(solution)/shard_map/all_to_all | solution.py:363
  102.7 5.0 %collective-permute-start.7 = (bf16[384,256]{1,0:T(8,128)(2,1)S(1)}, bf16[384,256]{1,0:T(8,128)(2,1)S(1)}, u32[]{:S(2)}, u32[]{:S(2)}) collective-permute-start(bf16[384,256]{1,0:T(8,128)(2,1)S(1)} %subtract_convert_fusion.refs_0_), channel_id=1, source_target_pairs={{0,4},{4,0},{8,12},{12,8},{16,20},{20,16},{24,28},{28,24},{1,5},{5... | collective-permute-start | bytes 589832 | tf_op jit(solution)/shard_map/ppermute | solution.py:52
  106.2 1.5 collective-permute-start.11
  106.2 1.7 collective-permute-start.13
  107.7 1.4 collective-permute-start.9
  116.3 17.4 %collective-permute-start.14 = (bf16[384,256]{1,0:T(8,128)(2,1)S(1)}, bf16[384,256]{1,0:T(8,128)(2,1)S(1)}, u32[]{:S(2)}, u32[]{:S(2)}) collective-permute-start(bf16[384,256]{1,0:T(8,128)(2,1)S(1)} %shard_map.82), channel_id=1, source_target_pairs={{0,3},{1,0},{2,1},{3,2},{4,7},{5,4},{6,5},{7,6},{8,11},{9,8},{10,9... | collective-permute-start | bytes 589832 | tf_op jit(solution)/shard_map/ppermute | solution.py:48
  123.8 21.0 %collective-permute-start.16 = (bf16[384,256]{1,0:T(8,128)(2,1)S(1)}, bf16[384,256]{1,0:T(8,128)(2,1)S(1)}, u32[]{:S(2)}, u32[]{:S(2)}) collective-permute-start(bf16[384,256]{1,0:T(8,128)(2,1)S(1)} %shard_map.83), channel_id=1, source_target_pairs={{0,1},{1,2},{2,3},{3,0},{4,5},{5,6},{6,7},{7,4},{8,9},{9,10},{10,1... | collective-permute-start | bytes 589832 | tf_op jit(solution)/shard_map/ppermute | solution.py:48
  133.8 11.4 %collective-permute-start.15 = (bf16[384,256]{1,0:T(8,128)(2,1)S(1)}, bf16[384,256]{1,0:T(8,128)(2,1)S(1)}, u32[]{:S(2)}, u32[]{:S(2)}) collective-permute-start(bf16[384,256]{1,0:T(8,128)(2,1)S(1)} %add_convert_fusion.4), channel_id=1, source_target_pairs={{0,3},{1,0},{2,1},{3,2},{4,7},{5,4},{6,5},{7,6},{8,11},{9,8},{10,9... | collective-permute-start | bytes 589832 | tf_op jit(solution)/shard_map/ppermute | solution.py:48
  135.8 5.0 %collective-permute-start.38 = (bf16[384,128]{1,0:T(8,128)(2,1)S(1)}, bf16[384,128]{1,0:T(8,128)(2,1)S(1)}, u32[]{:S(2)}, u32[]{:S(2)}) collective-permute-start(bf16[384,128]{1,0:T(8,128)(2,1)S(1)} %subtract_convert_fusion.1.refs_0_), channel_id=1, source_target_pairs={{0,8},{4,12},{8,0},{12,4},{16,24},{20,28},{24,16},{28,20},{1,9},{5... | collective-permute-start | bytes 294920 | tf_op jit(solution)/shard_map/ppermute | solution.py:52
  137.8 5.7 %collective-permute-start.40 = (bf16[384,128]{1,0:T(8,128)(2,1)S(1)}, bf16[384,128]{1,0:T(8,128)(2,1)S(1)}, u32[]{:S(2)}, u32[]{:S(2)}) collective-permute-start(bf16[384,128]{1,0:T(8,128)(2,1)S(1)} %subtract_convert_fusion.1.refs_0_), channel_id=1, source_target_pairs={{0,16},{4,20},{8,24},{12,28},{16,0},{20,4},{24,8},{28,12},{1,17},{... | collective-permute-start | bytes 294920 | tf_op jit(solution)/shard_map/ppermute | solution.py:52
  139.3 5.5 %collective-permute-start.42 = (bf16[384,128]{1,0:T(8,128)(2,1)S(1)}, bf16[384,128]{1,0:T(8,128)(2,1)S(1)}, u32[]{:S(2)}, u32[]{:S(2)}) collective-permute-start(bf16[384,128]{1,0:T(8,128)(2,1)S(1)} %subtract_convert_fusion.1.refs_0_), channel_id=1, source_target_pairs={{0,24},{4,28},{8,16},{12,20},{16,8},{20,12},{24,0},{28,4},{1,25},{... | collective-permute-start | bytes 294920 | tf_op jit(solution)/shard_map/ppermute | solution.py:52
  140.8 9.2 %collective-permute-start.37 = (bf16[384,128]{1,0:T(8,128)(2,1)S(1)}, bf16[384,128]{1,0:T(8,128)(2,1)S(1)}, u32[]{:S(2)}, u32[]{:S(2)}) collective-permute-start(bf16[384,128]{1,0:T(8,128)(2,1)S(1)} %subtract_convert_fusion.1.refs_0_), channel_id=1, source_target_pairs={{0,4},{4,0},{8,12},{12,8},{16,20},{20,16},{24,28},{28,24},{1,5},{5... | collective-permute-start | bytes 294920 | tf_op jit(solution)/shard_map/ppermute | solution.py:52
  143.4 6.6 %collective-permute-start.39 = (bf16[384,128]{1,0:T(8,128)(2,1)S(1)}, bf16[384,128]{1,0:T(8,128)(2,1)S(1)}, u32[]{:S(2)}, u32[]{:S(2)}) collective-permute-start(bf16[384,128]{1,0:T(8,128)(2,1)S(1)} %collective-permute-done.38.refs_2_), channel_id=1, source_target_pairs={{0,4},{4,0},{8,12},{12,8},{16,20},{20,16},{24,28},{28,24},{1,5},{5... | collective-permute-start | bytes 294920 | tf_op jit(solution)/shard_map/ppermute | solution.py:52
  144.8 5.3 %collective-permute-start.41 = (bf16[384,128]{1,0:T(8,128)(2,1)S(1)}, bf16[384,128]{1,0:T(8,128)(2,1)S(1)}, u32[]{:S(2)}, u32[]{:S(2)}) collective-permute-start(bf16[384,128]{1,0:T(8,128)(2,1)S(1)} %collective-permute-done.40.refs_4_), channel_id=1, source_target_pairs={{0,4},{4,0},{8,12},{12,8},{16,20},{20,16},{24,28},{28,24},{1,5},{5... | collective-permute-start | bytes 294920 | tf_op jit(solution)/shard_map/ppermute | solution.py:52
  144.8 5.3 %collective-permute-start.43 = (bf16[384,128]{1,0:T(8,128)(2,1)S(1)}, bf16[384,128]{1,0:T(8,128)(2,1)S(1)}, u32[]{:S(2)}, u32[]{:S(2)}) collective-permute-start(bf16[384,128]{1,0:T(8,128)(2,1)S(1)} %collective-permute-done.42.refs_6_), channel_id=1, source_target_pairs={{0,4},{4,0},{8,12},{12,8},{16,20},{20,16},{24,28},{28,24},{1,5},{5... | collective-permute-start | bytes 294920 | tf_op jit(solution)/shard_map/ppermute | solution.py:52
  146.0 18.2 %all-to-all-start.1 = ((bf16[4,96,256]{2,1,0:T(8,128)(2,1)}), bf16[4,96,256]{2,1,0:T(8,128)(2,1)}, u32[]{:S(2)}, u32[]{:S(2)}) async-start(bf16[4,96,256]{2,1,0:T(8,128)(2,1)} %bitcast.4), calls=%async_computation.1 | async-start | bytes 393216 | tf_op jit(solution)/shard_map/all_to_all | solution.py:379
  156.3 11.3 %collective-permute-start.44 = (bf16[384,128]{1,0:T(8,128)(2,1)S(1)}, bf16[384,128]{1,0:T(8,128)(2,1)S(1)}, u32[]{:S(2)}, u32[]{:S(2)}) collective-permute-start(bf16[384,128]{1,0:T(8,128)(2,1)S(1)} %shard_map.94), channel_id=1, source_target_pairs={{0,3},{1,0},{2,1},{3,2},{4,7},{5,4},{6,5},{7,6},{8,11},{9,8},{10,9... | collective-permute-start | bytes 294920 | tf_op jit(solution)/shard_map/ppermute | solution.py:48
  158.8 20.7 %collective-permute-start.46 = (bf16[384,128]{1,0:T(8,128)(2,1)S(1)}, bf16[384,128]{1,0:T(8,128)(2,1)S(1)}, u32[]{:S(2)}, u32[]{:S(2)}) collective-permute-start(bf16[384,128]{1,0:T(8,128)(2,1)S(1)} %shard_map.95), channel_id=1, source_target_pairs={{0,1},{1,2},{2,3},{3,0},{4,5},{5,6},{6,7},{7,4},{8,9},{9,10},{10,1... | collective-permute-start | bytes 294920 | tf_op jit(solution)/shard_map/ppermute | solution.py:48
  164.2 11.8 %all-to-all-start.2 = ((bf16[4,96,256]{2,1,0:T(8,128)(2,1)}), bf16[4,96,256]{2,1,0:T(8,128)(2,1)S(1)}, u32[]{:S(2)}, u32[]{:S(2)}) async-start(bf16[4,96,256]{2,1,0:T(8,128)(2,1)} %all-to-all-done.1), calls=%async_computation.2 | async-start | bytes 393216 | tf_op jit(solution)/shard_map/all_to_all | solution.py:380
  167.6 11.9 %collective-permute-start.45 = (bf16[384,128]{1,0:T(8,128)(2,1)S(1)}, bf16[384,128]{1,0:T(8,128)(2,1)S(1)}, u32[]{:S(2)}, u32[]{:S(2)}) collective-permute-start(bf16[384,128]{1,0:T(8,128)(2,1)S(1)} %add_convert_fusion.7), channel_id=1, source_target_pairs={{0,3},{1,0},{2,1},{3,2},{4,7},{5,4},{6,5},{7,6},{8,11},{9,8},{10,9... | collective-permute-start | bytes 294920 | tf_op jit(solution)/shard_map/ppermute | solution.py:48
  176.0 8.0 %collective-permute-start.18 = (bf16[384,256]{1,0:T(8,128)(2,1)S(1)}, bf16[384,256]{1,0:T(8,128)(2,1)S(1)}, u32[]{:S(2)}, u32[]{:S(2)}) collective-permute-start(bf16[384,256]{1,0:T(8,128)(2,1)S(1)} %bitcast.14), channel_id=1, source_target_pairs={{0,8},{4,12},{8,0},{12,4},{16,24},{20,28},{24,16},{28,20},{1,9},{5... | collective-permute-start | bytes 589832 | tf_op jit(solution)/shard_map/ppermute | solution.py:52
  177.7 8.3 %collective-permute-start.20 = (bf16[384,256]{1,0:T(8,128)(2,1)S(1)}, bf16[384,256]{1,0:T(8,128)(2,1)S(1)}, u32[]{:S(2)}, u32[]{:S(2)}) collective-permute-start(bf16[384,256]{1,0:T(8,128)(2,1)S(1)} %bitcast.15), channel_id=1, source_target_pairs={{0,16},{4,20},{8,24},{12,28},{16,0},{20,4},{24,8},{28,12},{1,17},{... | collective-permute-start | bytes 589832 | tf_op jit(solution)/shard_map/ppermute | solution.py:52
  179.1 6.8 %collective-permute-start.22 = (bf16[384,256]{1,0:T(8,128)(2,1)S(1)}, bf16[384,256]{1,0:T(8,128)(2,1)S(1)}, u32[]{:S(2)}, u32[]{:S(2)}) collective-permute-start(bf16[384,256]{1,0:T(8,128)(2,1)S(1)} %bitcast.16), channel_id=1, source_target_pairs={{0,24},{4,28},{8,16},{12,20},{16,8},{20,12},{24,0},{28,4},{1,25},{... | collective-permute-start | bytes 589832 | tf_op jit(solution)/shard_map/ppermute | solution.py:52
  180.2 8.8 %all-to-all-start.4 = ((bf16[4,96,128]{2,1,0:T(8,128)(2,1)}), bf16[4,96,128]{2,1,0:T(8,128)(2,1)S(1)}, u32[]{:S(2)}, u32[]{:S(2)}) async-start(bf16[4,96,128]{2,1,0:T(8,128)(2,1)} %bitcast.7), calls=%async_computation.4 | async-start | bytes 196608 | tf_op jit(solution)/shard_map/all_to_all | solution.py:379
  184.0 15.1 %collective-permute-start.17 = (bf16[384,256]{1,0:T(8,128)(2,1)S(1)}, bf16[384,256]{1,0:T(8,128)(2,1)S(1)}, u32[]{:S(2)}, u32[]{:S(2)}) collective-permute-start(bf16[384,256]{1,0:T(8,128)(2,1)S(1)} %bitcast.17), channel_id=1, source_target_pairs={{0,4},{4,0},{8,12},{12,8},{16,20},{20,16},{24,28},{28,24},{1,5},{5... | collective-permute-start | bytes 589832 | tf_op jit(solution)/shard_map/ppermute | solution.py:52
  184.0 15.4 %collective-permute-start.19 = (bf16[384,256]{1,0:T(8,128)(2,1)S(1)}, bf16[384,256]{1,0:T(8,128)(2,1)S(1)}, u32[]{:S(2)}, u32[]{:S(2)}) collective-permute-start(bf16[384,256]{1,0:T(8,128)(2,1)S(1)} %collective-permute-done.18.refs_2_), channel_id=1, source_target_pairs={{0,4},{4,0},{8,12},{12,8},{16,20},{20,16},{24,28},{28,24},{1,5},{5... | collective-permute-start | bytes 589832 | tf_op jit(solution)/shard_map/ppermute | solution.py:52
  186.0 15.8 %collective-permute-start.21 = (bf16[384,256]{1,0:T(8,128)(2,1)S(1)}, bf16[384,256]{1,0:T(8,128)(2,1)S(1)}, u32[]{:S(2)}, u32[]{:S(2)}) collective-permute-start(bf16[384,256]{1,0:T(8,128)(2,1)S(1)} %collective-permute-done.20.refs_4_), channel_id=1, source_target_pairs={{0,4},{4,0},{8,12},{12,8},{16,20},{20,16},{24,28},{28,24},{1,5},{5... | collective-permute-start | bytes 589832 | tf_op jit(solution)/shard_map/ppermute | solution.py:52
  186.0 15.8 %collective-permute-start.23 = (bf16[384,256]{1,0:T(8,128)(2,1)S(1)}, bf16[384,256]{1,0:T(8,128)(2,1)S(1)}, u32[]{:S(2)}, u32[]{:S(2)}) collective-permute-start(bf16[384,256]{1,0:T(8,128)(2,1)S(1)} %collective-permute-done.22.refs_6_), channel_id=1, source_target_pairs={{0,4},{4,0},{8,12},{12,8},{16,20},{20,16},{24,28},{28,24},{1,5},{5... | collective-permute-start | bytes 589832 | tf_op jit(solution)/shard_map/ppermute | solution.py:52
  198.3 11.4 %collective-permute-start.48 = (bf16[384,128]{1,0:T(8,128)(2,1)S(1)}, bf16[384,128]{1,0:T(8,128)(2,1)S(1)}, u32[]{:S(2)}, u32[]{:S(2)}) collective-permute-start(bf16[384,128]{1,0:T(8,128)(2,1)S(1)} %bitcast.19), channel_id=1, source_target_pairs={{0,8},{4,12},{8,0},{12,4},{16,24},{20,28},{24,16},{28,20},{1,9},{5... | collective-permute-start | bytes 294920 | tf_op jit(solution)/shard_map/ppermute | solution.py:52
  199.1 11.1 %collective-permute-start.50 = (bf16[384,128]{1,0:T(8,128)(2,1)S(1)}, bf16[384,128]{1,0:T(8,128)(2,1)S(1)}, u32[]{:S(2)}, u32[]{:S(2)}) collective-permute-start(bf16[384,128]{1,0:T(8,128)(2,1)S(1)} %bitcast.20), channel_id=1, source_target_pairs={{0,16},{4,20},{8,24},{12,28},{16,0},{20,4},{24,8},{28,12},{1,17},{... | collective-permute-start | bytes 294920 | tf_op jit(solution)/shard_map/ppermute | solution.py:52
  199.5 10.8 %collective-permute-start.52 = (bf16[384,128]{1,0:T(8,128)(2,1)S(1)}, bf16[384,128]{1,0:T(8,128)(2,1)S(1)}, u32[]{:S(2)}, u32[]{:S(2)}) collective-permute-start(bf16[384,128]{1,0:T(8,128)(2,1)S(1)} %bitcast.21), channel_id=1, source_target_pairs={{0,24},{4,28},{8,16},{12,20},{16,8},{20,12},{24,0},{28,4},{1,25},{... | collective-permute-start | bytes 294920 | tf_op jit(solution)/shard_map/ppermute | solution.py:52
  208.6 23.7 %collective-permute-start.24 = (bf16[256,512]{1,0:T(8,128)(2,1)S(1)}, bf16[256,512]{1,0:T(8,128)(2,1)S(1)}, u32[]{:S(2)}, u32[]{:S(2)}) collective-permute-start(bf16[256,512]{1,0:T(8,128)(2,1)S(1)} %get-tuple-element.29), channel_id=1, source_target_pairs={{0,3},{1,0},{2,1},{3,2},{4,7},{5,4},{6,5},{7,6},{8,11},{9,8},{10,9... | collective-permute-start | bytes 786440 | tf_op jit(solution)/shard_map/ppermute | solution.py:48
  209.7 1.5 collective-permute-start.49
  210.2 1.3 collective-permute-start.51
  210.3 1.4 collective-permute-start.53
  217.1 22.0 %collective-permute-start.54 = (bf16[128,512]{1,0:T(8,128)(2,1)S(1)}, bf16[128,512]{1,0:T(8,128)(2,1)S(1)}, u32[]{:S(2)}, u32[]{:S(2)}) collective-permute-start(bf16[128,512]{1,0:T(8,128)(2,1)S(1)} %get-tuple-element.39), channel_id=1, source_target_pairs={{0,3},{1,0},{2,1},{3,2},{4,7},{5,4},{6,5},{7,6},{8,11},{9,8},{10,9... | collective-permute-start | bytes 393224 | tf_op jit(solution)/shard_map/ppermute | solution.py:48
  222.2 21.0 %collective-permute-start.56 = (bf16[128,512]{1,0:T(8,128)(2,1)S(1)}, bf16[128,512]{1,0:T(8,128)(2,1)S(1)}, u32[]{:S(2)}, u32[]{:S(2)}) collective-permute-start(bf16[128,512]{1,0:T(8,128)(2,1)S(1)} %shard_map.98), channel_id=1, source_target_pairs={{0,1},{1,2},{2,3},{3,0},{4,5},{5,6},{6,7},{7,4},{8,9},{9,10},{10,1... | collective-permute-start | bytes 393224 | tf_op jit(solution)/shard_map/ppermute | solution.py:48
  226.9 13.6 %collective-permute-start.26 = (bf16[256,512]{1,0:T(8,128)(2,1)S(1)}, bf16[256,512]{1,0:T(8,128)(2,1)S(1)}, u32[]{:S(2)}, u32[]{:S(2)}) collective-permute-start(bf16[256,512]{1,0:T(8,128)(2,1)S(1)} %shard_map.86), channel_id=1, source_target_pairs={{0,1},{1,2},{2,3},{3,0},{4,5},{5,6},{6,7},{7,4},{8,9},{9,10},{10,1... | collective-permute-start | bytes 786440 | tf_op jit(solution)/shard_map/ppermute | solution.py:48
  232.3 10.1 %collective-permute-start.25 = (bf16[256,512]{1,0:T(8,128)(2,1)S(1)}, bf16[256,512]{1,0:T(8,128)(2,1)S(1)}, u32[]{:S(2)}, u32[]{:S(2)}) collective-permute-start(bf16[256,512]{1,0:T(8,128)(2,1)S(1)} %add_convert_fusion.3), channel_id=1, source_target_pairs={{0,3},{1,0},{2,1},{3,2},{4,7},{5,4},{6,5},{7,6},{8,11},{9,8},{10,9... | collective-permute-start | bytes 786440 | tf_op jit(solution)/shard_map/ppermute | solution.py:48
  239.2 6.0 %collective-permute-start.55 = (bf16[128,512]{1,0:T(8,128)(2,1)S(1)}, bf16[128,512]{1,0:T(8,128)(2,1)S(1)}, u32[]{:S(2)}, u32[]{:S(2)}) collective-permute-start(bf16[128,512]{1,0:T(8,128)(2,1)S(1)} %add_convert_fusion.6), channel_id=1, source_target_pairs={{0,3},{1,0},{2,1},{3,2},{4,7},{5,4},{6,5},{7,6},{8,11},{9,8},{10,9... | collective-permute-start | bytes 393224 | tf_op jit(solution)/shard_map/ppermute | solution.py:48
  242.6 17.7 %collective-permute-start.27 = (bf16[256,512]{1,0:T(8,128)(2,1)S(1)}, bf16[256,512]{1,0:T(8,128)(2,1)S(1)}, u32[]{:S(2)}, u32[]{:S(2)}) collective-permute-start(bf16[256,512]{1,0:T(8,128)(2,1)S(1)} %add_convert_fusion.2.refs_3_), channel_id=1, source_target_pairs={{0,1},{1,2},{2,3},{3,0},{4,5},{5,6},{6,7},{7,4},{8,9},{9,10},{10,1... | collective-permute-start | bytes 786440 | tf_op jit(solution)/shard_map/ppermute | solution.py:48
  245.2 11.2 %collective-permute-start.57 = (bf16[128,512]{1,0:T(8,128)(2,1)S(1)}, bf16[128,512]{1,0:T(8,128)(2,1)S(1)}, u32[]{:S(2)}, u32[]{:S(2)}) collective-permute-start(bf16[128,512]{1,0:T(8,128)(2,1)S(1)} %add_convert_fusion.5.refs_3_), channel_id=1, source_target_pairs={{0,1},{1,2},{2,3},{3,0},{4,5},{5,6},{6,7},{7,4},{8,9},{9,10},{10,1... | collective-permute-start | bytes 393224 | tf_op jit(solution)/shard_map/ppermute | solution.py:48
  245.8 14.5 %collective-permute-start.59 = (bf16[128,512]{1,0:T(8,128)(2,1)S(1)}, bf16[128,512]{1,0:T(8,128)(2,1)S(1)}, u32[]{:S(2)}, u32[]{:S(2)}) collective-permute-start(bf16[128,512]{1,0:T(8,128)(2,1)S(1)} %add_convert_fusion.5.refs_3_), channel_id=1, source_target_pairs={{0,3},{1,0},{2,1},{3,2},{4,7},{5,4},{6,5},{7,6},{8,11},{9,8},{10,9... | collective-permute-start | bytes 393224 | tf_op jit(solution)/shard_map/ppermute | solution.py:48
  256.5 8.4 %collective-permute-start.58 = (bf16[128,512]{1,0:T(8,128)(2,1)S(1)}, bf16[128,512]{1,0:T(8,128)(2,1)S(1)}, u32[]{:S(2)}, u32[]{:S(2)}) collective-permute-start(bf16[128,512]{1,0:T(8,128)(2,1)S(1)} %collective-permute-done.57.refs_4_), channel_id=1, source_target_pairs={{0,1},{1,2},{2,3},{3,0},{4,5},{5,6},{6,7},{7,4},{8,9},{9,10},{10,1... | collective-permute-start | bytes 393224 | tf_op jit(solution)/shard_map/ppermute | solution.py:48
  256.5 12.4 %collective-permute-start.29 = (bf16[256,512]{1,0:T(8,128)(2,1)S(1)}, bf16[256,512]{1,0:T(8,128)(2,1)S(1)}, u32[]{:S(2)}, u32[]{:S(2)}) collective-permute-start(bf16[256,512]{1,0:T(8,128)(2,1)S(1)} %add_convert_fusion.2.refs_3_), channel_id=1, source_target_pairs={{0,3},{1,0},{2,1},{3,2},{4,7},{5,4},{6,5},{7,6},{8,11},{9,8},{10,9... | collective-permute-start | bytes 786440 | tf_op jit(solution)/shard_map/ppermute | solution.py:48
  260.3 12.6 %collective-permute-start.28 = (bf16[256,512]{1,0:T(8,128)(2,1)S(1)}, bf16[256,512]{1,0:T(8,128)(2,1)S(1)}, u32[]{:S(2)}, u32[]{:S(2)}) collective-permute-start(bf16[256,512]{1,0:T(8,128)(2,1)S(1)} %collective-permute-done.27.refs_4_), channel_id=1, source_target_pairs={{0,1},{1,2},{2,3},{3,0},{4,5},{5,6},{6,7},{7,4},{8,9},{9,10},{10,1... | collective-permute-start | bytes 786440 | tf_op jit(solution)/shard_map/ppermute | solution.py:48
  (25 other events, 163.7 us)

commit v6 on v4

--- a/solution.py
+++ b/solution.py
@@ -40,6 +40,10 @@
     )
 
 
+def in_hbm(x):
+    return pltpu.with_memory_space_constraint(x, pltpu.HBM)
+
+
 def whole(shape):
     return pl.BlockSpec(shape, lambda *_: (0,) * len(shape))
 
@@ -65,12 +69,13 @@
 
 
 def gather_front(x, n):
-    found = {0: x, 1: swap(x, n, 1)}
-    for d in range(2, n, 2):
-        found[d] = swap(x, n, d)
-    for d in range(2, n, 2):
-        found[d + 1] = swap(found[d], n, 1)
-    return [found[d] for d in range(n)]
+    rows = x.shape[0]
+    by_x, by_y = swap(x, n, 2), swap(x, n, 4)
+    corner_low = swap(by_y[: rows // 2], n, 2)
+    corner_high = swap(by_x[rows // 2 :], n, 4)
+    mine = [(0, 0, x), (1, 0, by_x), (2, 0, by_y), (3, 0, corner_low), (3, rows // 2, corner_high)]
+    found = [(chip, 0, low, block) for chip, low, block in mine]
+    return found + [(chip, 1, low, swap(block, n, 1)) for chip, low, block in mine]
 
 
 def far_offsets(n):
@@ -136,28 +141,33 @@
         [],
         2 * rows * depth * width * count,
         2 * rows * depth * count,
-    )(at, *[pivot] * count, *[x for _, x in found], *extra)
-
-
-def border_partial(at, coupling, found, n_row):
+    )(at, *[in_hbm(pivot)] * count, *[x for _, x in found], *extra)
+
+
+def border_partial(at, coupling, found, partial, n_row):
     rows, depth = coupling.shape[0], coupling.shape[1] // n_row
     count, width = len(found), found[0][1].shape[1]
     tile = rows // border_steps(rows)
 
+    moving = pl.BlockSpec((tile, width), lambda i, *_: (i, 0))
+
     def body(at_ref, *refs):
-        refs[-1][...] = products(refs[:count], refs[count : 2 * count], ((1,), (0,)))
+        total = products(refs[:count], refs[count : 2 * count], ((1,), (0,)))
+        refs[-1][...] = total if partial is None else refs[-2][...] + total
 
     return kernel_call(
         body,
         jax.ShapeDtypeStruct((rows, width), F32),
         (rows // tile,),
         1,
-        column_specs(tile, depth, [o for o, _ in found], n_row, True) + [whole(x.shape) for _, x in found],
-        pl.BlockSpec((tile, width), lambda i, *_: (i, 0)),
+        column_specs(tile, depth, [o for o, _ in found], n_row, True)
+        + [whole(x.shape) for _, x in found]
+        + [moving] * (partial is not None),
+        moving,
         [],
         2 * rows * depth * width * count,
         2 * rows * depth * count,
-    )(at, *[coupling] * count, *[x for _, x in found])
+    )(at, *[in_hbm(coupling)] * count, *[x for _, x in found], *([] if partial is None else [partial]))
 
 
 def border_steps(rows):
@@ -185,7 +195,8 @@
         for j in range(tile // BLK):
             target = index_ref[step * (tile // BLK) + j]
             there = lax.div(target, piece_blocks)
-            slot = lax.shift_right_logical(there, 1) * piece_blocks + lax.rem(target, piece_blocks)
+            chip = lax.shift_right_logical(lax.bitwise_xor(there, at_ref[1]), 1)
+            slot = chip * piece_blocks + lax.rem(target, piece_blocks)
             place = pl.ds(pl.multiple_of(slot * BLK, BLK), BLK)
             block = total[j * BLK : (j + 1) * BLK]
             away = lax.rem(there + at_ref[1], 2)
@@ -211,79 +222,143 @@
         [],
         2 * rows * depth * width * count,
         2 * rows * depth * count,
-    )(at, local_index, *[coupling] * count, *[x for _, x in found], partial)
+    )(at, local_index, *[in_hbm(coupling)] * count, *[x for _, x in found], partial)
+
+
+def corner_parts(at, send, came):
+    rows, width = send.shape[0] // 4, send.shape[1]
+    half = jax.ShapeDtypeStruct((rows // 2, width), BF16)
+
+    def body(at_ref, keep_ref, came_ref, low_ref, high_ref):
+        total = (keep_ref[...].astype(F32) + came_ref[...].astype(F32)).astype(BF16)
+        low_ref[...] = total[: rows // 2]
+        high_ref[...] = total[rows // 2 :]
+
+    block = pl.BlockSpec((rows, width), lambda i, *_: (3, 0))
+    return kernel_call(
+        body, [half, half], (1,), 1, [block] * 2, [whole(half.shape)] * 2, [], send.size, send.size
+    )(at, send, came)
+
+
+def side_parts(at, keep, came, low, high):
+    rows, width = keep.shape[0] // 4, keep.shape[1]
+    part = jax.ShapeDtypeStruct((rows, width), BF16)
+
+    def body(at_ref, keep_x, came_x, keep_y, came_y, low_ref, high_ref, x_ref, y_ref):
+        first, second = slice(0, rows // 2), slice(rows // 2, rows)
+        for keep_ref, came_ref, add_ref, here, other, out_ref in (
+            (keep_x, came_x, high_ref, second, first, x_ref),
+            (keep_y, came_y, low_ref, first, second, y_ref),
+        ):
+            out_ref[other, :] = (keep_ref[other, :].astype(F32) + came_ref[other, :].astype(F32)).astype(BF16)
+            both = keep_ref[here, :].astype(F32) + came_ref[here, :].astype(F32)
+            out_ref[here, :] = (both + add_ref[...].astype(F32)).astype(BF16)
+
+    one, two = (pl.BlockSpec((rows, width), lambda i, *_, k=k: (k, 0)) for k in (1, 2))
+    return kernel_call(
+        body,
+        [part, part],
+        (1,),
+        1,
+        [one, one, two, two] + [whole(low.shape)] * 2,
+        [whole(part.shape)] * 2,
+        [],
+        2 * keep.size,
+        3 * keep.size,
+    )(at, keep, came, keep, came, low, high)
+
+
+def own_part(at, rhs_root, keep, came, by_x, by_y):
+    rows, width = by_x.shape
+
+    def body(at_ref, rhs_ref, keep_ref, came_ref, x_ref, y_ref, out_ref):
+        total = keep_ref[...].astype(F32) + came_ref[...].astype(F32)
+        total = total + x_ref[...].astype(F32) + y_ref[...].astype(F32)
+        out_ref[...] = (rhs_ref[...] - total).astype(BF16)
+
+    block = pl.BlockSpec((rows, width), lambda i, *_: (0, 0))
+    return kernel_call(
+        body,
+        jax.ShapeDtypeStruct((rows, width), BF16),
+        (1,),
+        1,
+        [pl.BlockSpec((rows, width), lambda i, at_ref: (at_ref[1], 0)), block, block] + [whole(by_x.shape)] * 2,
+        whole(by_x.shape),
+        [],
+        keep.size,
+        2 * keep.size,
+    )(at, in_hbm(rhs_root), keep, came, by_x, by_y)
 
 
 def root_products(at, inverse, pieces, offsets, kinds, n_row, n_front):
     span_rows = inverse.shape[1]
     rows = inverse.shape[0] // n_row
-    piece_rows, width = pieces[0].shape
-    count = len(offsets)
-
-    def row_block(i, at_ref):
-        offset = offsets[0]
-        for k in range(1, count):
-            offset = jnp.where(i == k, offsets[k], offset)
-        return owner(at_ref, offset, n_row), 0
-
-    def body(at_ref, a_ref, *refs):
-        piece_refs, out_refs = refs[:n_front], refs[n_front : n_front + count]
-        x_ref, sems = refs[-2], refs[-1]
-        step = pl.program_id(0)
-
-        @pl.when(step == 0)
-        def _():
-            copies = []
-            for d in range(n_front):
-                start = lax.bitwise_xor(at_ref[1], d) * piece_rows
-                place = pl.ds(pl.multiple_of(start, piece_rows), piece_rows)
-                copies.append(pltpu.make_async_copy(piece_refs[d], x_ref.at[place], sems.at[d]))
-            for copy in copies:
-                copy.start()
-            for copy in copies:
-                copy.wait()
-
-        total = dot(a_ref[...], x_ref[...])
+    width = pieces[0][3].shape[1]
+    piece_rows = span_rows // n_front
+    count, many = len(offsets), len(pieces)
+
+    def body(at_ref, a_hbm, *refs):
+        piece_refs, out_refs = refs[:many], refs[many : many + count]
+        a_ref, x_ref, sems = refs[-3:]
+        copies = []
+        for (chip, core, low, block), ref in zip(pieces, piece_refs):
+            start = lax.bitwise_xor(at_ref[1], 2 * chip + core) * piece_rows + low
+            place = pl.ds(pl.multiple_of(start, block.shape[0]), block.shape[0])
+            copies.append(pltpu.make_async_copy(ref, x_ref.at[place], sems.at[len(copies)]))
+        loads = []
+        for i, offset in enumerate(offsets):
+            place = pl.ds(pl.multiple_of(owner(at_ref, offset, n_row) * rows, rows), rows)
+            loads.append(pltpu.make_async_copy(a_hbm.at[place], a_ref.at[i], sems.at[many + i]))
+        for copy in loads[:1] + copies + loads[1:]:
+            copy.start()
+        for copy in copies:
+            copy.wait()
         for i in range(count):
-
-            @pl.when(step == i)
-            def _():
-                out_refs[i][...] = total.astype(out_refs[i].dtype)
+            loads[i].wait()
+            out_refs[i][...] = dot(a_ref[i], x_ref[...]).astype(out_refs[i].dtype)
 
     return kernel_call(
         body,
         [jax.ShapeDtypeStruct((rows, width), kind) for kind in kinds],
-        (count,),
+        (1,),
         1,
-        [pl.BlockSpec((rows, span_rows), row_block)] + [ANY] * n_front,
+        [ANY] * (1 + many),
         [whole((rows, width))] * count,
-        [pltpu.VMEM((span_rows, width), BF16), pltpu.SemaphoreType.DMA((n_front,))],
+        [
+            pltpu.VMEM((count, rows, span_rows), BF16),
+            pltpu.VMEM((span_rows, width), BF16),
+            pltpu.SemaphoreType.DMA((many + count,)),
+        ],
         2 * rows * span_rows * width * count,
         2 * rows * span_rows * count,
-    )(at, inverse, *pieces)
+    )(at, in_hbm(inverse), *[block for *_, block in pieces])
 
 
 def border_pick(at, local_index, coupling, pieces, offset, n_row, n_front):
     rows, depth = coupling.shape[0], coupling.shape[1] // n_row
-    piece_rows, width = pieces[0].shape
+    piece_rows, width = pieces[0][3].shape
     quarter = piece_rows // n_row
     span_rows = piece_rows * n_front
-
-    def body(at_ref, index_ref, a_ref, *refs):
-        piece_refs, out_ref, picked_ref = refs[:n_front], refs[n_front], refs[n_front + 1]
-        span_ref, sems = refs[-2], refs[-1]
+    many = len(pieces)
+
+    def body(at_ref, index_ref, a_hbm, *refs):
+        piece_refs, out_ref, picked_ref = refs[:many], refs[many], refs[many + 1]
+        a_ref, span_ref, sems = refs[-3:]
+        columns = pl.ds(pl.multiple_of(owner(at_ref, offset, n_row) * depth, depth), depth)
+        load = pltpu.make_async_copy(a_hbm.at[:, columns], a_ref, sems.at[0])
         copies = []
-        for d in range(n_front):
-            there = lax.bitwise_xor(at_ref[1], d)
-            chip, core = lax.shift_right_logical(there, 1), lax.rem(there, 2)
-            for k in range(n_row):
-                start = core * (span_rows // 2) + k * piece_rows + chip * quarter
+        for (chip, core, low, block), ref in zip(pieces, piece_refs):
+            there = lax.bitwise_xor(at_ref[1], 2 * chip + core)
+            base = lax.rem(there, 2) * (span_rows // 2) + lax.shift_right_logical(there, 1) * quarter
+            for k in range(block.shape[0] // quarter):
+                start = base + (low // quarter + k) * piece_rows
                 place = pl.ds(pl.multiple_of(start, quarter), quarter)
                 copies.append(
                     pltpu.make_async_copy(
-                        piece_refs[d].at[pl.ds(k * quarter, quarter)], span_ref.at[place], sems.at[d * n_row + k]
+                        ref.at[pl.ds(k * quarter, quarter)], span_ref.at[place], sems.at[1 + len(copies)]
                     )
                 )
+        load.start()
         for copy in copies:
             copy.start()
         for copy in copies:
@@ -291,6 +366,7 @@
         for j in range(rows // BLK):
             source = pl.ds(pl.multiple_of(index_ref[j] * BLK, BLK), BLK)
             picked_ref[:, pl.ds(j * BLK, BLK)] = jnp.transpose(span_ref[source, :])
+        load.wait()
         out_ref[...] = dot(picked_ref[...], a_ref[...]).astype(BF16)
 
     return kernel_call(
@@ -298,12 +374,16 @@
         [jax.ShapeDtypeStruct((width, depth), BF16), jax.ShapeDtypeStruct((width, rows), BF16)],
         (1,),
         2,
-        column_specs(rows, depth, [offset], n_row) + [ANY] * n_front,
+        [ANY] * (1 + many),
         [whole((width, depth)), whole((width, rows))],
-        [pltpu.VMEM((span_rows, width), BF16), pltpu.SemaphoreType.DMA((n_front * n_row,))],
+        [
+            pltpu.VMEM((rows, depth), BF16),
+            pltpu.VMEM((span_rows, width), BF16),
+            pltpu.SemaphoreType.DMA((1 + n_front * n_row,)),
+        ],
         2 * rows * depth * width,
         2 * rows * depth,
-    )(at, local_index, coupling, *pieces)
+    )(at, local_index, in_hbm(coupling), *[block for *_, block in pieces])
 
 
 def border_backward(at, coupling, picked, offsets, kinds, n_row):
@@ -324,7 +404,7 @@
         [],
         2 * rows * depth * width * count,
         2 * rows * depth * count,
-    )(at, picked, *[coupling] * count)
+    )(at, picked, *[in_hbm(coupling)] * count)
 
 
 def solve(n_front, n_row, rhs_front, rhs_root, pivot_inverse, border_coupling, root_inverse, border_map):
@@ -354,17 +434,18 @@
         partial,
     )
     found = gather_row(inner_half, n_row)
-    early, last = found[:-1], found[-1:]
-    partial = border_partial(at, border_coupling, early, n_row)
+    partial = None
+    for some in (found[:2], found[2:-1]):
+        if some:
+            partial = border_partial(at, border_coupling, some, partial, n_row)
     send, keep = border_scatter(
-        at, local_index, border_coupling, last, partial, n_row, n_front, span_rows
+        at, local_index, border_coupling, found[-1:], partial, n_row, n_front, span_rows
     )
-    both = (keep.astype(F32) + swap(send, n_front, 1).astype(F32)).astype(BF16)
-    shares = lax.all_to_all(
-        both.reshape(n_front // 2, piece_rows, width), "front", 0, 0, axis_index_groups=chips
-    )
-    own_rhs = lax.dynamic_slice_in_dim(rhs_root, front_at * piece_rows, piece_rows, 0)
-    pieces = gather_front((own_rhs - shares.astype(F32).sum(axis=0)).astype(BF16), n_front)
+    came = swap(send, n_front, 1)
+    low, high = corner_parts(at, keep, came)
+    by_x, by_y = side_parts(at, keep, came, swap(low, n_front, 2), swap(high, n_front, 4))
+    piece = own_part(at, rhs_root, keep, came, swap(by_x, n_front, 2), swap(by_y, n_front, 4))
+    pieces = gather_front(piece, n_front)
 
     def root(offsets, kind):
         outs = root_products(at, root_inverse, pieces, offsets, [kind] * len(offsets), n_row, n_front)
@@ -442,9 +523,8 @@
     def per_device(*arrays):
         root_inverse, width = arrays[4], arrays[0].shape[1]
         fits = (
-            n_front == 2 * n_row
-            and n_front & (n_front - 1) == 0
-            and n_row > 2
+            n_front == 8
+            and n_front == 2 * n_row
             and root_inverse.shape[1] % (n_front * BLK) == 0
             and root_inverse.shape[0] == n_row * (root_inverse.shape[1] // n_front)
             and root_inverse.shape[1] % (n_front * n_row * 16) == 0

time: 241 us -> 233 us (0.967)
  Pallas kernels: 32.1 us -> 50.4 us
  waiting for transfers between devices: 134 us -> 125 us
  local copies, waits for them, and re-layouts: 9.09 us -> 1.07 us
  starting transfers between devices: 39.6 us -> 34.9 us
  other arithmetic: 5.37 us -> 1.43 us
    all_to_all x1 -> x0, waiting for transfers between devices: 15.7 us -> none  [solve(): lax.all_to_all(both.reshape(n_front // 2, piece_rows, width), 'front', 0,...]
    ppermute x15 -> x23, waiting for transfers between devices: 26.5 us -> 36 us  [swap(): return lax.ppermute(x, 'front', [(i, i ^ by) for i in range(size)])]
    unnamed x24 -> x4, local copies, waits for them, and re-layouts: 9.09 us -> 1 us
    ppermute x15, starting transfers between devices: 27.2 us -> 20.5 us  [shift(): return lax.ppermute(x, 'row', [(i, (i + by) % size) for i in range(size)])]
    ppermute x15 -> x23, starting transfers between devices: 8.11 us -> 14.3 us  [swap(): return lax.ppermute(x, 'front', [(i, i ^ by) for i in range(size)])]
    all_to_all x1 -> x0, starting transfers between devices: 4.26 us -> none  [solve(): lax.all_to_all(both.reshape(n_front // 2, piece_rows, width), 'front', 0,...]
    pallas_call x4, Pallas kernels: 6.67 us -> 10.7 us  [pivot_products(): kernel_call(body, outs, (1,), 1, column_specs(rows, depth, [o for o, _ in...]
    pallas_call x3, Pallas kernels: 9.1 us -> 12.5 us  [root_products(): kernel_call(body, [jax.ShapeDtypeStruct((rows, width), kind) for kind in...]
  transfers between devices with their start and end apart: 31 -> 38, of which waited for: 24 -> 30; matrix products, arithmetic and copies ran while one was open for 0% -> 0% of each run, Pallas kernels for 8% -> 12%
where the time goes in v6:
time: 233 us
  waiting for transfers between devices  125 us (54%)
  Pallas kernels  50.4 us (22%)
  starting transfers between devices  34.9 us (15%)
  blocking collectives  19.3 us (8%)
    ppermute x15, waiting for transfers between devices, shift(): return lax.ppermute(x, 'row', [(i, (i + by) % size) for i in range(size)])  88.8 us
    ppermute x23, waiting for transfers between devices, swap(): return lax.ppermute(x, 'front', [(i, i ^ by) for i in range(size)])  36 us
    ppermute x15, starting transfers between devices, shift(): return lax.ppermute(x, 'row', [(i, (i + by) % size) for i in range(size)])  20.5 us
    ppermute x23, starting transfers between devices, swap(): return lax.ppermute(x, 'front', [(i, i ^ by) for i in range(size)])  14.3 us
    pallas_call x3, Pallas kernels, root_products(): kernel_call(body, [jax.ShapeDtypeStruct((rows, width), kind) for kind in...  12.5 us
    pallas_call x4, Pallas kernels, pivot_products(): kernel_call(body, outs, (1,), 1, column_specs(rows, depth, [o for o, _ in...  10.7 us
    all_to_all x1, blocking collectives, solve(): quarters = lax.all_to_all(quarters, 'row', 0, 0)  10.6 us
    all_to_all x1, blocking collectives, solve(): quarters = lax.all_to_all(quarters, 'front', 0, 0, axis_index_groups=chips)  8.64 us
  transfers between devices with their start and end apart: 38, of which 30 were waited for; matrix products, arithmetic and copies ran while one was open for 0% of the time, Pallas kernels for 12%

profile of v6, /device:TPU:0, one launch (start us, length us, event | category | flops | bytes accessed | tf_op | source)
XLA Modules:
  0.0 232.6 jit_solution(14546489261498234519)
XLA Ops:
  0.6 3.1 %collective-permute-start = (bf16[512,384]{1,0:T(8,128)(2,1)}, bf16[512,384]{1,0:T(8,128)(2,1)S(1)}, u32[]{:S(2)}, u32[]{:S(2)}) collective-permute-start(bf16[512,384]{1,0:T(8,128)(2,1)} %refs_3_.1), channel_id=1, source_target_pairs={{0,1},{1,2},{2,3},{3,0},{4,5},{5,6},{6,7},{7,4},{8,9},{9,10},{10,1... | collective-permute-start | bytes 1179656 | tf_op jit(solution)/shard_map/ppermute | solution.py:52
  3.7 2.1 collective-permute-start.2
  5.8 10.1 %collective-permute-done.refs_4_ = bf16[512,384]{1,0:T(8,128)(2,1)S(1)} collective-permute-done((bf16[512,384]{1,0:T(8,128)(2,1)}, bf16[512,384]{1,0:T(8,128)(2,1)S(1)}, u32[]{:S(2)}, u32[]{:S(2)}) %collective-permute-start) | collective-permute-done | bytes 393248 | tf_op jit(solution)/shard_map/ppermute | solution.py:52
  16.0 7.1 %collective-permute-done.2.refs_5_ = bf16[512,384]{1,0:T(8,128)(2,1)S(1)} collective-permute-done((bf16[512,384]{1,0:T(8,128)(2,1)}, bf16[512,384]{1,0:T(8,128)(2,1)S(1)}, u32[]{:S(2)}, u32[]{:S(2)}) %collective-permute-start.2) | collective-permute-done | bytes 393248 | tf_op jit(solution)/shard_map/ppermute | solution.py:52
  23.1 1.0 copy-done
  24.1 2.9 %shard_map.77.refs_2_ = f32[512,384]{1,0:T(8,128)S(1)} custom-call(s32[2]{0:T(128)S(1)} %pad_add_fusion.at_ref, bf16[512,2048]{1,0:T(8,128)(2,1)} %refs_0_.17, bf16[512,2048]{1,0:T(8,128)(2,1)} %refs_0_.17, bf16[512,2048]{1,0:T(8,128)(2,1)} %refs_0_.17, bf16[512,384]{1,0:T(8,128)(2,1)S(1)} %copy-done, bf16[512,384]{1,0:T(8,128)(2,1)S(1)} %collective-permute-done.refs_4_, ...), custom_call_target="tpu_custom_call" | custom-call | flops 603979776 | bytes 1572864 | tf_op jit(solution)/shard_map/pallas_call | solution.py:132
  27.0 4.9 %collective-permute-done.1.refs_1_ = bf16[512,384]{1,0:T(8,128)(2,1)S(1)} collective-permute-done((bf16[512,384]{1,0:T(8,128)(2,1)S(1)}, bf16[512,384]{1,0:T(8,128)(2,1)S(1)}, u32[]{:S(2)}, u32[]{:S(2)}) %collective-permute-start.1) | collective-permute-done | bytes 393248 | tf_op jit(solution)/shard_map/ppermute | solution.py:52
  32.0 2.0 shard_map.78
  34.1 3.8 %collective-permute-start.5 = (bf16[512,384]{1,0:T(8,128)(2,1)S(1)}, bf16[512,384]{1,0:T(8,128)(2,1)S(1)}, u32[]{:S(2)}, u32[]{:S(2)}) collective-permute-start(bf16[512,384]{1,0:T(8,128)(2,1)S(1)} %get-tuple-element.16.refs_2_), channel_id=1, source_target_pairs={{0,3},{1,0},{2,1},{3,2},{4,7},{5,4},{6,5},{7,6},{8,11},{9,8},{10,9... | collective-permute-start | bytes 1179656 | tf_op jit(solution)/shard_map/ppermute | solution.py:52
  37.9 10.0 %collective-permute-done.3.refs_3_ = bf16[512,384]{1,0:T(8,128)(2,1)S(1)} collective-permute-done((bf16[512,384]{1,0:T(8,128)(2,1)S(1)}, bf16[512,384]{1,0:T(8,128)(2,1)S(1)}, u32[]{:S(2)}, u32[]{:S(2)}) %collective-permute-start.3) | collective-permute-done | bytes 393248 | tf_op jit(solution)/shard_map/ppermute | solution.py:52
  47.9 4.4 %shard_map.79.refs_2_ = f32[1536,384]{1,0:T(8,128)S(1)} custom-call(s32[2]{0:T(128)S(1)} %pad_add_fusion.at_ref, bf16[1536,2048]{1,0:T(8,128)(2,1)} %refs_0_.15, bf16[1536,2048]{1,0:T(8,128)(2,1)} %refs_0_.15, bf16[512,384]{1,0:T(8,128)(2,1)S(1)} %get-tuple-element.16.refs_2_, bf16[512,384]{1,0:T(8,128)(2,1)S(1)} %collective-permute-done.3.refs_3_), custom_call_target="tpu_custom_call" | custom-call | flops 1207959552 | bytes 3145728 | tf_op jit(solution)/shard_map/pallas_call | solution.py:158
  52.3 1.5 collective-permute-done.5.refs_1_
  53.9 3.5 %shard_map.80.refs_2_ = f32[1536,384]{1,0:T(8,128)S(1)} custom-call(s32[2]{0:T(128)S(1)} %pad_add_fusion.at_ref, bf16[1536,2048]{1,0:T(8,128)(2,1)} %refs_0_.15, bf16[512,384]{1,0:T(8,128)(2,1)S(1)} %collective-permute-done.5.refs_1_, f32[1536,384]{1,0:T(8,128)S(1)} %shard_map.79.refs_2_), custom_call_target="tpu_custom_call" | custom-call | flops 603979776 | bytes 1572864 | tf_op jit(solution)/shard_map/pallas_call | solution.py:158
  57.4 4.1 %collective-permute-done.4.refs_1_ = bf16[512,384]{1,0:T(8,128)(2,1)S(1)} collective-permute-done((bf16[512,384]{1,0:T(8,128)(2,1)S(1)}, bf16[512,384]{1,0:T(8,128)(2,1)S(1)}, u32[]{:S(2)}, u32[]{:S(2)}) %collective-permute-start.4) | collective-permute-done | bytes 393248 | tf_op jit(solution)/shard_map/ppermute | solution.py:52
  61.5 3.9 %shard_map.81 = (bf16[1536,384]{1,0:T(8,128)(2,1)S(1)}, bf16[1536,384]{1,0:T(8,128)(2,1)S(1)}) custom-call(s32[2]{0:T(128)S(1)} %pad_add_fusion.at_ref, s32[12]{0:T(128)S(1)} %subtract_bitcast_fusion.index_ref, bf16[1536,2048]{1,0:T(8,128)(2,1)} %refs_0_.15, bf16[512,384]{1,0:T(8,128)(2,1)S(1)} %collective-permute-done.4.refs_1_, ...), custom_call_target="tpu_custom_call" | custom-call | flops 603979776 | bytes 1572864 | tf_op jit(solution)/shard_map/pallas_call | solution.py:213
  65.6 2.8 %collective-permute-done.6.came_ref.came_x.came_y = bf16[1536,384]{1,0:T(8,128)(2,1)S(1)} collective-permute-done((bf16[1536,384]{1,0:T(8,128)(2,1)S(1)}, bf16[1536,384]{1,0:T(8,128)(2,1)S(1)}, u32[]{:S(2)}, u32[]{:S(2)}) %collective-permute-start.6) | collective-permute-done | bytes 1179680 | tf_op jit(solution)/shard_map/ppermute | solution.py:56
  68.4 0.6 shard_map.82
  69.0 1.6 collective-permute-start.7
  70.6 1.5 collective-permute-start.8
  72.1 2.9 %collective-permute-done.7.low_ref = bf16[192,384]{1,0:T(8,128)(2,1)S(1)} collective-permute-done((bf16[192,384]{1,0:T(8,128)(2,1)S(1)}, bf16[192,384]{1,0:T(8,128)(2,1)S(1)}, u32[]{:S(2)}, u32[]{:S(2)}) %collective-permute-start.7) | collective-permute-done | bytes 147488 | tf_op jit(solution)/shard_map/ppermute | solution.py:56
  75.0 1.2 collective-permute-done.8.high_ref
  76.2 0.7 shard_map.83
  77.5 1.5 collective-permute-start.10
  79.0 5.8 %collective-permute-done.9.x_ref = bf16[384,384]{1,0:T(8,128)(2,1)S(1)} collective-permute-done((bf16[384,384]{1,0:T(8,128)(2,1)S(1)}, bf16[384,384]{1,0:T(8,128)(2,1)S(1)}, u32[]{:S(2)}, u32[]{:S(2)}) %collective-permute-start.9) | collective-permute-done | bytes 294944 | tf_op jit(solution)/shard_map/ppermute | solution.py:56
  85.2 1.8 shard_map.84.refs_0_
  87.0 1.6 collective-permute-start.12
  88.6 1.4 collective-permute-start.11
  90.0 3.8 %collective-permute-done.12.refs_2_ = bf16[384,384]{1,0:T(8,128)(2,1)S(1)} collective-permute-done((bf16[384,384]{1,0:T(8,128)(2,1)S(1)}, bf16[384,384]{1,0:T(8,128)(2,1)S(1)}, u32[]{:S(2)}, u32[]{:S(2)}) %collective-permute-start.12) | collective-permute-done | bytes 294944 | tf_op jit(solution)/shard_map/ppermute | solution.py:56
  93.9 1.4 collective-permute-start.13
  95.3 1.6 collective-permute-done.11.refs_1_
  97.6 1.5 collective-permute-done.13.refs_3_
  99.1 3.0 %collective-permute-done.14.refs_4_ = bf16[192,384]{1,0:T(8,128)(2,1)S(1)} collective-permute-done((bf16[192,384]{1,0:T(8,128)(2,1)S(1)}, bf16[192,384]{1,0:T(8,128)(2,1)S(1)}, u32[]{:S(2)}, u32[]{:S(2)}) %collective-permute-start.14) | collective-permute-done | bytes 147488 | tf_op jit(solution)/shard_map/ppermute | solution.py:56
  102.2 1.4 collective-permute-done.19.refs_9_
  103.5 3.7 %shard_map.86 = bf16[384,384]{1,0:T(8,128)(2,1)S(1)} custom-call(s32[2]{0:T(128)S(1)} %pad_add_fusion.at_ref, bf16[1536,3072]{1,0:T(8,128)(2,1)} %a_hbm.6, bf16[384,384]{1,0:T(8,128)(2,1)S(1)} %shard_map.84.refs_0_, bf16[384,384]{1,0:T(8,128)(2,1)S(1)} %collective-permute-done.11.refs_1_, bf16[384,384]{1,0:T(8,128)(2,1)S(1)} %collective-permute-done.12.refs_2_, ...), custom_call_target="tpu_custom_call" | custom-call | flops 905969664 | bytes 2359296 | tf_op jit(solution)/shard_map/pallas_call | solution.py:320
  107.3 3.7 %shard_map.87 = bf16[384,384]{1,0:T(8,128)(2,1)S(1)} custom-call(s32[2]{0:T(128)S(1)} %pad_add_fusion.at_ref, bf16[1536,3072]{1,0:T(8,128)(2,1)} %a_hbm.6, bf16[384,384]{1,0:T(8,128)(2,1)S(1)} %shard_map.84.refs_0_, bf16[384,384]{1,0:T(8,128)(2,1)S(1)} %collective-permute-done.11.refs_1_, bf16[384,384]{1,0:T(8,128)(2,1)S(1)} %collective-permute-done.12.refs_2_, ...), custom_call_target="tpu_custom_call" | custom-call | flops 905969664 | bytes 2359296 | tf_op jit(solution)/shard_map/pallas_call | solution.py:320
  111.0 2.1 collective-permute-start.22
  113.1 5.1 %shard_map.85 = (f32[384,384]{1,0:T(8,128)S(1)}, f32[384,384]{1,0:T(8,128)S(1)}) custom-call(s32[2]{0:T(128)S(1)} %pad_add_fusion.at_ref, bf16[1536,3072]{1,0:T(8,128)(2,1)} %a_hbm.6, bf16[384,384]{1,0:T(8,128)(2,1)S(1)} %shard_map.84.refs_0_, bf16[384,384]{1,0:T(8,128)(2,1)S(1)} %collective-permute-done.11.refs_1_, ...), custom_call_target="tpu_custom_call" | custom-call | flops 1811939328 | bytes 4718592 | tf_op jit(solution)/shard_map/pallas_call | solution.py:320
  118.2 5.1 %collective-permute-done.20 = bf16[384,384]{1,0:T(8,128)(2,1)S(1)} collective-permute-done((bf16[384,384]{1,0:T(8,128)(2,1)S(1)}, bf16[384,384]{1,0:T(8,128)(2,1)S(1)}, u32[]{:S(2)}, u32[]{:S(2)}) %collective-permute-start.20) | collective-permute-done | bytes 294944 | tf_op jit(solution)/shard_map/ppermute | solution.py:52
  123.4 6.7 %collective-permute-done.21 = bf16[384,384]{1,0:T(8,128)(2,1)S(1)} collective-permute-done((bf16[384,384]{1,0:T(8,128)(2,1)S(1)}, bf16[384,384]{1,0:T(8,128)(2,1)S(1)}, u32[]{:S(2)}, u32[]{:S(2)}) %collective-permute-start.21) | collective-permute-done | bytes 294944 | tf_op jit(solution)/shard_map/ppermute | solution.py:52
  130.1 0.9 fusion
  131.0 8.6 %all_to_all.10 = bf16[4,96,384]{2,1,0:T(8,128)(2,1)S(1)} all-to-all(bf16[4,96,384]{2,1,0:T(8,128)(2,1)S(1)} %bitcast.10), channel_id=1, replica_groups={{0,8,16,24},{4,12,20,28},{1,9,17,25},{5,13,21,29},{2,10,18,26},{6,14,22..., dimensions={0} | all-to-all | bytes 589824 | tf_op jit(solution)/shard_map/all_to_all | solution.py:460
  139.7 10.6 %all_to_all.11 = bf16[4,96,384]{2,1,0:T(8,128)(2,1)S(1)} all-to-all(bf16[4,96,384]{2,1,0:T(8,128)(2,1)S(1)} %all_to_all.10), channel_id=1, replica_groups=mesh['front'=8,'row'=4] {'row'}, dimensions={0} | all-to-all | bytes 589824 | tf_op jit(solution)/shard_map/all_to_all | solution.py:461
  150.3 0.7 collective-permute-start.24
  151.4 6.6 %collective-permute-done.24.refs_2_ = bf16[384,384]{1,0:T(8,128)(2,1)S(1)} collective-permute-done((bf16[384,384]{1,0:T(8,128)(2,1)S(1)}, bf16[384,384]{1,0:T(8,128)(2,1)S(1)}, u32[]{:S(2)}, u32[]{:S(2)}) %collective-permute-start.24) | collective-permute-done | bytes 294944 | tf_op jit(solution)/shard_map/ppermute | solution.py:56
  158.0 0.9 collective-permute-start.25
  159.3 1.4 collective-permute-start.26
  161.2 2.0 collective-permute-done.25.refs_3_
  163.2 1.3 collective-permute-done.26.refs_4_
  164.6 1.3 collective-permute-done.31.refs_9_
  165.8 5.6 %shard_map.88 = (bf16[384,512]{1,0:T(8,128)(2,1)S(1)}, bf16[384,1536]{1,0:T(8,128)(2,1)S(1)}) custom-call(s32[2]{0:T(128)S(1)} %pad_add_fusion.at_ref, s32[12]{0:T(128)S(1)} %subtract_bitcast_fusion.index_ref, bf16[1536,2048]{1,0:T(8,128)(2,1)} %refs_0_.15, bf16[384,384]{1,0:T(8,128)(2,1)S(1)} %bitcast.9, ...), custom_call_target="tpu_custom_call" | custom-call | flops 603979776 | bytes 1572864 | tf_op jit(solution)/shard_map/pallas_call | solution.py:372
  171.4 1.4 collective-permute-start.32
  172.8 2.7 %shard_map.90 = bf16[384,512]{1,0:T(8,128)(2,1)S(1)} custom-call(s32[2]{0:T(128)S(1)} %pad_add_fusion.at_ref, bf16[384,1536]{1,0:T(8,128)(2,1)S(1)} %get-tuple-element.25.x_ref, bf16[1536,2048]{1,0:T(8,128)(2,1)} %refs_0_.15), custom_call_target="tpu_custom_call" | custom-call | flops 603979776 | bytes 1572864 | tf_op jit(solution)/shard_map/pallas_call | solution.py:397
  175.5 0.8 collective-permute-start.34
  176.3 3.8 %shard_map.89 = (f32[384,512]{1,0:T(8,128)S(1)}, f32[384,512]{1,0:T(8,128)S(1)}) custom-call(s32[2]{0:T(128)S(1)} %pad_add_fusion.at_ref, bf16[384,1536]{1,0:T(8,128)(2,1)S(1)} %get-tuple-element.25.x_ref, bf16[1536,2048]{1,0:T(8,128)(2,1)} %refs_0_.15, bf16[1536,2048]{1,0:T(8,128)(2,1)} %refs_0_.15), custom_call_target="tpu_custom_call" | custom-call | flops 1207959552 | bytes 3145728 | tf_op jit(solution)/shard_map/pallas_call | solution.py:397
  180.1 3.2 %collective-permute-done.32 = bf16[384,512]{1,0:T(8,128)(2,1)S(1)} collective-permute-done((bf16[384,512]{1,0:T(8,128)(2,1)S(1)}, bf16[384,512]{1,0:T(8,128)(2,1)S(1)}, u32[]{:S(2)}, u32[]{:S(2)}) %collective-permute-start.32) | collective-permute-done | bytes 393248 | tf_op jit(solution)/shard_map/ppermute | solution.py:52
  183.5 3.3 %collective-permute-start.33 = (bf16[384,512]{1,0:T(8,128)(2,1)S(1)}, bf16[384,512]{1,0:T(8,128)(2,1)S(1)}, u32[]{:S(2)}, u32[]{:S(2)}) collective-permute-start(bf16[384,512]{1,0:T(8,128)(2,1)S(1)} %add_convert_fusion.1), channel_id=1, source_target_pairs={{0,3},{1,0},{2,1},{3,2},{4,7},{5,4},{6,5},{7,6},{8,11},{9,8},{10,9... | collective-permute-start | bytes 1179656 | tf_op jit(solution)/shard_map/ppermute | solution.py:52
  186.8 5.2 %collective-permute-done.34 = bf16[384,512]{1,0:T(8,128)(2,1)S(1)} collective-permute-done((bf16[384,512]{1,0:T(8,128)(2,1)S(1)}, bf16[384,512]{1,0:T(8,128)(2,1)S(1)}, u32[]{:S(2)}, u32[]{:S(2)}) %collective-permute-start.34) | collective-permute-done | bytes 393248 | tf_op jit(solution)/shard_map/ppermute | solution.py:52
  192.0 7.6 %collective-permute-done.33 = bf16[384,512]{1,0:T(8,128)(2,1)S(1)} collective-permute-done((bf16[384,512]{1,0:T(8,128)(2,1)S(1)}, bf16[384,512]{1,0:T(8,128)(2,1)S(1)}, u32[]{:S(2)}, u32[]{:S(2)}) %collective-permute-start.33) | collective-permute-done | bytes 393248 | tf_op jit(solution)/shard_map/ppermute | solution.py:52
  200.5 3.3 %collective-permute-start.37 = (bf16[384,512]{1,0:T(8,128)(2,1)S(1)}, bf16[384,512]{1,0:T(8,128)(2,1)S(1)}, u32[]{:S(2)}, u32[]{:S(2)}) collective-permute-start(bf16[384,512]{1,0:T(8,128)(2,1)S(1)} %add_convert_fusion.refs_3_), channel_id=1, source_target_pairs={{0,3},{1,0},{2,1},{3,2},{4,7},{5,4},{6,5},{7,6},{8,11},{9,8},{10,9... | collective-permute-start | bytes 1179656 | tf_op jit(solution)/shard_map/ppermute | solution.py:52
  203.7 10.0 %collective-permute-done.35.refs_4_ = bf16[384,512]{1,0:T(8,128)(2,1)S(1)} collective-permute-done((bf16[384,512]{1,0:T(8,128)(2,1)S(1)}, bf16[384,512]{1,0:T(8,128)(2,1)S(1)}, u32[]{:S(2)}, u32[]{:S(2)}) %collective-permute-start.35) | collective-permute-done | bytes 393248 | tf_op jit(solution)/shard_map/ppermute | solution.py:52
  213.7 6.0 %collective-permute-done.37.refs_5_ = bf16[384,512]{1,0:T(8,128)(2,1)S(1)} collective-permute-done((bf16[384,512]{1,0:T(8,128)(2,1)S(1)}, bf16[384,512]{1,0:T(8,128)(2,1)S(1)}, u32[]{:S(2)}, u32[]{:S(2)}) %collective-permute-start.37) | collective-permute-done | bytes 393248 | tf_op jit(solution)/shard_map/ppermute | solution.py:52
  219.7 2.9 %shard_map.91.refs_2_ = f32[512,384]{1,0:T(8,128)S(1)} custom-call(s32[2]{0:T(128)S(1)} %pad_add_fusion.at_ref, bf16[512,2048]{1,0:T(8,128)(2,1)} %refs_0_.17, bf16[512,2048]{1,0:T(8,128)(2,1)} %refs_0_.17, bf16[512,2048]{1,0:T(8,128)(2,1)} %refs_0_.17, bf16[384,512]{1,0:T(8,128)(2,1)S(1)} %add_convert_fusion.refs_3_, ...), custom_call_target="tpu_custom_call" | custom-call | flops 603979776 | bytes 1572864 | tf_op jit(solution)/shard_map/pallas_call | solution.py:132
  222.6 7.0 %collective-permute-done.36.refs_1_ = bf16[384,512]{1,0:T(8,128)(2,1)S(1)} collective-permute-done((bf16[384,512]{1,0:T(8,128)(2,1)S(1)}, bf16[384,512]{1,0:T(8,128)(2,1)S(1)}, u32[]{:S(2)}, u32[]{:S(2)}) %collective-permute-start.36) | collective-permute-done | bytes 393248 | tf_op jit(solution)/shard_map/ppermute | solution.py:52
  229.6 2.9 %shard_map.92 = f32[512,384]{1,0:T(8,128)} custom-call(s32[2]{0:T(128)S(1)} %pad_add_fusion.at_ref, bf16[512,2048]{1,0:T(8,128)(2,1)} %refs_0_.17, bf16[384,512]{1,0:T(8,128)(2,1)S(1)} %collective-permute-done.36.refs_1_, f32[512,384]{1,0:T(8,128)S(1)} %shard_map.91.refs_2_), custom_call_target="tpu_custom_call" | custom-call | flops 201326592 | bytes 524288 | tf_op jit(solution)/shard_map/pallas_call | solution.py:132
  (44 shorter events, 4.5 us)
Async XLA Ops:
  0.6 15.3 %collective-permute-start = (bf16[512,384]{1,0:T(8,128)(2,1)}, bf16[512,384]{1,0:T(8,128)(2,1)S(1)}, u32[]{:S(2)}, u32[]{:S(2)}) collective-permute-start(bf16[512,384]{1,0:T(8,128)(2,1)} %refs_3_.1), channel_id=1, source_target_pairs={{0,1},{1,2},{2,3},{3,0},{4,5},{5,6},{6,7},{7,4},{8,9},{9,10},{10,1... | collective-permute-start | bytes 1179656 | tf_op jit(solution)/shard_map/ppermute | solution.py:52
  3.7 19.4 %collective-permute-start.2 = (bf16[512,384]{1,0:T(8,128)(2,1)}, bf16[512,384]{1,0:T(8,128)(2,1)S(1)}, u32[]{:S(2)}, u32[]{:S(2)}) collective-permute-start(bf16[512,384]{1,0:T(8,128)(2,1)} %refs_3_.1), channel_id=1, source_target_pairs={{0,3},{1,0},{2,1},{3,2},{4,7},{5,4},{6,5},{7,6},{8,11},{9,8},{10,9... | collective-permute-start | bytes 1179656 | tf_op jit(solution)/shard_map/ppermute | solution.py:52
  15.9 16.0 %collective-permute-start.1 = (bf16[512,384]{1,0:T(8,128)(2,1)S(1)}, bf16[512,384]{1,0:T(8,128)(2,1)S(1)}, u32[]{:S(2)}, u32[]{:S(2)}) collective-permute-start(bf16[512,384]{1,0:T(8,128)(2,1)S(1)} %collective-permute-done.refs_4_), channel_id=1, source_target_pairs={{0,1},{1,2},{2,3},{3,0},{4,5},{5,6},{6,7},{7,4},{8,9},{9,10},{10,1... | collective-permute-start | bytes 1179656 | tf_op jit(solution)/shard_map/ppermute | solution.py:52
  23.1 1.0 copy-start
  27.0 20.9 %copy-start.1 = (s32[1,12]{1,0:T(1,128)S(1)}, s32[1,12]{1,0:T(1,128)}, u32[]{:S(2)}) copy-start(s32[1,12]{1,0:T(1,128)} %param.11) | copy-start | bytes 148
  34.0 13.9 %collective-permute-start.3 = (bf16[512,384]{1,0:T(8,128)(2,1)S(1)}, bf16[512,384]{1,0:T(8,128)(2,1)S(1)}, u32[]{:S(2)}, u32[]{:S(2)}) collective-permute-start(bf16[512,384]{1,0:T(8,128)(2,1)S(1)} %get-tuple-element.16.refs_2_), channel_id=1, source_target_pairs={{0,1},{1,2},{2,3},{3,0},{4,5},{5,6},{6,7},{7,4},{8,9},{9,10},{10,1... | collective-permute-start | bytes 1179656 | tf_op jit(solution)/shard_map/ppermute | solution.py:52
  34.1 19.8 %collective-permute-start.5 = (bf16[512,384]{1,0:T(8,128)(2,1)S(1)}, bf16[512,384]{1,0:T(8,128)(2,1)S(1)}, u32[]{:S(2)}, u32[]{:S(2)}) collective-permute-start(bf16[512,384]{1,0:T(8,128)(2,1)S(1)} %get-tuple-element.16.refs_2_), channel_id=1, source_target_pairs={{0,3},{1,0},{2,1},{3,2},{4,7},{5,4},{6,5},{7,6},{8,11},{9,8},{10,9... | collective-permute-start | bytes 1179656 | tf_op jit(solution)/shard_map/ppermute | solution.py:52
  47.9 13.6 %collective-permute-start.4 = (bf16[512,384]{1,0:T(8,128)(2,1)S(1)}, bf16[512,384]{1,0:T(8,128)(2,1)S(1)}, u32[]{:S(2)}, u32[]{:S(2)}) collective-permute-start(bf16[512,384]{1,0:T(8,128)(2,1)S(1)} %collective-permute-done.3.refs_3_), channel_id=1, source_target_pairs={{0,1},{1,2},{2,3},{3,0},{4,5},{5,6},{6,7},{7,4},{8,9},{9,10},{10,1... | collective-permute-start | bytes 1179656 | tf_op jit(solution)/shard_map/ppermute | solution.py:52
  65.5 2.9 %collective-permute-start.6 = (bf16[1536,384]{1,0:T(8,128)(2,1)S(1)}, bf16[1536,384]{1,0:T(8,128)(2,1)S(1)}, u32[]{:S(2)}, u32[]{:S(2)}) collective-permute-start(bf16[1536,384]{1,0:T(8,128)(2,1)S(1)} %get-tuple-element.18), channel_id=1, source_target_pairs={{0,4},{4,0},{8,12},{12,8},{16,20},{20,16},{24,28},{28,24},{1,5},{5... | collective-permute-start | bytes 3538952 | tf_op jit(solution)/shard_map/ppermute | solution.py:56
  69.0 6.0 %collective-permute-start.7 = (bf16[192,384]{1,0:T(8,128)(2,1)S(1)}, bf16[192,384]{1,0:T(8,128)(2,1)S(1)}, u32[]{:S(2)}, u32[]{:S(2)}) collective-permute-start(bf16[192,384]{1,0:T(8,128)(2,1)S(1)} %get-tuple-element.19), channel_id=1, source_target_pairs={{0,8},{4,12},{8,0},{12,4},{16,24},{20,28},{24,16},{28,20},{1,9},{5... | collective-permute-start | bytes 442376 | tf_op jit(solution)/shard_map/ppermute | solution.py:56
  70.6 5.6 %collective-permute-start.8 = (bf16[192,384]{1,0:T(8,128)(2,1)S(1)}, bf16[192,384]{1,0:T(8,128)(2,1)S(1)}, u32[]{:S(2)}, u32[]{:S(2)}) collective-permute-start(bf16[192,384]{1,0:T(8,128)(2,1)S(1)} %get-tuple-element.20), channel_id=1, source_target_pairs={{0,16},{4,20},{8,24},{12,28},{16,0},{20,4},{24,8},{28,12},{1,17},{... | collective-permute-start | bytes 442376 | tf_op jit(solution)/shard_map/ppermute | solution.py:56
  76.9 8.0 %collective-permute-start.9 = (bf16[384,384]{1,0:T(8,128)(2,1)S(1)}, bf16[384,384]{1,0:T(8,128)(2,1)S(1)}, u32[]{:S(2)}, u32[]{:S(2)}) collective-permute-start(bf16[384,384]{1,0:T(8,128)(2,1)S(1)} %get-tuple-element.21), channel_id=1, source_target_pairs={{0,8},{4,12},{8,0},{12,4},{16,24},{20,28},{24,16},{28,20},{1,9},{5... | collective-permute-start | bytes 884744 | tf_op jit(solution)/shard_map/ppermute | solution.py:56
  77.5 7.7 %collective-permute-start.10 = (bf16[384,384]{1,0:T(8,128)(2,1)S(1)}, bf16[384,384]{1,0:T(8,128)(2,1)S(1)}, u32[]{:S(2)}, u32[]{:S(2)}) collective-permute-start(bf16[384,384]{1,0:T(8,128)(2,1)S(1)} %get-tuple-element.22), channel_id=1, source_target_pairs={{0,16},{4,20},{8,24},{12,28},{16,0},{20,4},{24,8},{28,12},{1,17},{... | collective-permute-start | bytes 884744 | tf_op jit(solution)/shard_map/ppermute | solution.py:56
  87.0 6.8 %collective-permute-start.12 = (bf16[384,384]{1,0:T(8,128)(2,1)S(1)}, bf16[384,384]{1,0:T(8,128)(2,1)S(1)}, u32[]{:S(2)}, u32[]{:S(2)}) collective-permute-start(bf16[384,384]{1,0:T(8,128)(2,1)S(1)} %shard_map.84.refs_0_), channel_id=1, source_target_pairs={{0,16},{4,20},{8,24},{12,28},{16,0},{20,4},{24,8},{28,12},{1,17},{... | collective-permute-start | bytes 884744 | tf_op jit(solution)/shard_map/ppermute | solution.py:56
  88.6 8.3 %collective-permute-start.11 = (bf16[384,384]{1,0:T(8,128)(2,1)S(1)}, bf16[384,384]{1,0:T(8,128)(2,1)S(1)}, u32[]{:S(2)}, u32[]{:S(2)}) collective-permute-start(bf16[384,384]{1,0:T(8,128)(2,1)S(1)} %shard_map.84.refs_0_), channel_id=1, source_target_pairs={{0,8},{4,12},{8,0},{12,4},{16,24},{20,28},{24,16},{28,20},{1,9},{5... | collective-permute-start | bytes 884744 | tf_op jit(solution)/shard_map/ppermute | solution.py:56
  90.0 12.1 %collective-permute-start.15 = (bf16[384,384]{1,0:T(8,128)(2,1)S(1)}, bf16[384,384]{1,0:T(8,128)(2,1)S(1)}, u32[]{:S(2)}, u32[]{:S(2)}) collective-permute-start(bf16[384,384]{1,0:T(8,128)(2,1)S(1)} %shard_map.84.refs_0_), channel_id=1, source_target_pairs={{0,4},{4,0},{8,12},{12,8},{16,20},{20,16},{24,28},{28,24},{1,5},{5... | collective-permute-start | bytes 884744 | tf_op jit(solution)/shard_map/ppermute | solution.py:56
  93.9 5.2 %collective-permute-start.13 = (bf16[192,384]{1,0:T(8,128)(2,1)S(1)}, bf16[192,384]{1,0:T(8,128)(2,1)S(1)}, u32[]{:S(2)}, u32[]{:S(2)}) collective-permute-start(bf16[192,384]{1,0:T(8,128)(2,1)S(1)} %slice.16), channel_id=1, source_target_pairs={{0,8},{4,12},{8,0},{12,4},{16,24},{20,28},{24,16},{28,20},{1,9},{5... | collective-permute-start | bytes 442376 | tf_op jit(solution)/shard_map/ppermute | solution.py:56
  96.9 5.2 %collective-permute-start.14 = (bf16[192,384]{1,0:T(8,128)(2,1)S(1)}, bf16[192,384]{1,0:T(8,128)(2,1)S(1)}, u32[]{:S(2)}, u32[]{:S(2)}) collective-permute-start(bf16[192,384]{1,0:T(8,128)(2,1)S(1)} %slice.17), channel_id=1, source_target_pairs={{0,16},{4,20},{8,24},{12,28},{16,0},{20,4},{24,8},{28,12},{1,17},{... | collective-permute-start | bytes 442376 | tf_op jit(solution)/shard_map/ppermute | solution.py:56
  97.0 6.5 %collective-permute-start.17 = (bf16[384,384]{1,0:T(8,128)(2,1)S(1)}, bf16[384,384]{1,0:T(8,128)(2,1)S(1)}, u32[]{:S(2)}, u32[]{:S(2)}) collective-permute-start(bf16[384,384]{1,0:T(8,128)(2,1)S(1)} %collective-permute-done.12.refs_2_), channel_id=1, source_target_pairs={{0,4},{4,0},{8,12},{12,8},{16,20},{20,16},{24,28},{28,24},{1,5},{5... | collective-permute-start | bytes 884744 | tf_op jit(solution)/shard_map/ppermute | solution.py:56
  97.1 6.4 %collective-permute-start.16 = (bf16[384,384]{1,0:T(8,128)(2,1)S(1)}, bf16[384,384]{1,0:T(8,128)(2,1)S(1)}, u32[]{:S(2)}, u32[]{:S(2)}) collective-permute-start(bf16[384,384]{1,0:T(8,128)(2,1)S(1)} %collective-permute-done.11.refs_1_), channel_id=1, source_target_pairs={{0,4},{4,0},{8,12},{12,8},{16,20},{20,16},{24,28},{28,24},{1,5},{5... | collective-permute-start | bytes 884744 | tf_op jit(solution)/shard_map/ppermute | solution.py:56
  99.1 3.1 %collective-permute-start.18 = (bf16[192,384]{1,0:T(8,128)(2,1)S(1)}, bf16[192,384]{1,0:T(8,128)(2,1)S(1)}, u32[]{:S(2)}, u32[]{:S(2)}) collective-permute-start(bf16[192,384]{1,0:T(8,128)(2,1)S(1)} %collective-permute-done.13.refs_3_), channel_id=1, source_target_pairs={{0,4},{4,0},{8,12},{12,8},{16,20},{20,16},{24,28},{28,24},{1,5},{5... | collective-permute-start | bytes 442376 | tf_op jit(solution)/shard_map/ppermute | solution.py:56
  102.1 1.4 collective-permute-start.19
  107.2 16.0 %collective-permute-start.20 = (bf16[384,384]{1,0:T(8,128)(2,1)S(1)}, bf16[384,384]{1,0:T(8,128)(2,1)S(1)}, u32[]{:S(2)}, u32[]{:S(2)}) collective-permute-start(bf16[384,384]{1,0:T(8,128)(2,1)S(1)} %shard_map.86), channel_id=1, source_target_pairs={{0,3},{1,0},{2,1},{3,2},{4,7},{5,4},{6,5},{7,6},{8,11},{9,8},{10,9... | collective-permute-start | bytes 884744 | tf_op jit(solution)/shard_map/ppermute | solution.py:52
  111.0 12.4 %collective-permute-start.22 = (bf16[384,384]{1,0:T(8,128)(2,1)S(1)}, bf16[384,384]{1,0:T(8,128)(2,1)S(1)}, u32[]{:S(2)}, u32[]{:S(2)}) collective-permute-start(bf16[384,384]{1,0:T(8,128)(2,1)S(1)} %shard_map.87), channel_id=1, source_target_pairs={{0,1},{1,2},{2,3},{3,0},{4,5},{5,6},{6,7},{7,4},{8,9},{9,10},{10,1... | collective-permute-start | bytes 884744 | tf_op jit(solution)/shard_map/ppermute | solution.py:52
  123.3 6.8 %collective-permute-start.21 = (bf16[384,384]{1,0:T(8,128)(2,1)S(1)}, bf16[384,384]{1,0:T(8,128)(2,1)S(1)}, u32[]{:S(2)}, u32[]{:S(2)}) collective-permute-start(bf16[384,384]{1,0:T(8,128)(2,1)S(1)} %add_convert_fusion.2), channel_id=1, source_target_pairs={{0,3},{1,0},{2,1},{3,2},{4,7},{5,4},{6,5},{7,6},{8,11},{9,8},{10,9... | collective-permute-start | bytes 884744 | tf_op jit(solution)/shard_map/ppermute | solution.py:52
  150.3 7.7 %collective-permute-start.24 = (bf16[384,384]{1,0:T(8,128)(2,1)S(1)}, bf16[384,384]{1,0:T(8,128)(2,1)S(1)}, u32[]{:S(2)}, u32[]{:S(2)}) collective-permute-start(bf16[384,384]{1,0:T(8,128)(2,1)S(1)} %bitcast.6), channel_id=1, source_target_pairs={{0,16},{4,20},{8,24},{12,28},{16,0},{20,4},{24,8},{28,12},{1,17},{... | collective-permute-start | bytes 884744 | tf_op jit(solution)/shard_map/ppermute | solution.py:56
  150.9 8.3 %collective-permute-start.23 = (bf16[384,384]{1,0:T(8,128)(2,1)S(1)}, bf16[384,384]{1,0:T(8,128)(2,1)S(1)}, u32[]{:S(2)}, u32[]{:S(2)}) collective-permute-start(bf16[384,384]{1,0:T(8,128)(2,1)S(1)} %bitcast.7), channel_id=1, source_target_pairs={{0,8},{4,12},{8,0},{12,4},{16,24},{20,28},{24,16},{28,20},{1,9},{5... | collective-permute-start | bytes 884744 | tf_op jit(solution)/shard_map/ppermute | solution.py:56
  151.4 13.1 %collective-permute-start.27 = (bf16[384,384]{1,0:T(8,128)(2,1)S(1)}, bf16[384,384]{1,0:T(8,128)(2,1)S(1)}, u32[]{:S(2)}, u32[]{:S(2)}) collective-permute-start(bf16[384,384]{1,0:T(8,128)(2,1)S(1)} %bitcast.8), channel_id=1, source_target_pairs={{0,4},{4,0},{8,12},{12,8},{16,20},{20,16},{24,28},{28,24},{1,5},{5... | collective-permute-start | bytes 884744 | tf_op jit(solution)/shard_map/ppermute | solution.py:56
  158.0 5.2 %collective-permute-start.25 = (bf16[192,384]{1,0:T(8,128)(2,1)S(1)}, bf16[192,384]{1,0:T(8,128)(2,1)S(1)}, u32[]{:S(2)}, u32[]{:S(2)}) collective-permute-start(bf16[192,384]{1,0:T(8,128)(2,1)S(1)} %slice.18), channel_id=1, source_target_pairs={{0,8},{4,12},{8,0},{12,4},{16,24},{20,28},{24,16},{28,20},{1,9},{5... | collective-permute-start | bytes 442376 | tf_op jit(solution)/shard_map/ppermute | solution.py:56
  159.3 5.2 %collective-permute-start.26 = (bf16[192,384]{1,0:T(8,128)(2,1)S(1)}, bf16[192,384]{1,0:T(8,128)(2,1)S(1)}, u32[]{:S(2)}, u32[]{:S(2)}) collective-permute-start(bf16[192,384]{1,0:T(8,128)(2,1)S(1)} %slice.19), channel_id=1, source_target_pairs={{0,16},{4,20},{8,24},{12,28},{16,0},{20,4},{24,8},{28,12},{1,17},{... | collective-permute-start | bytes 442376 | tf_op jit(solution)/shard_map/ppermute | solution.py:56
  160.7 5.1 %collective-permute-start.29 = (bf16[384,384]{1,0:T(8,128)(2,1)S(1)}, bf16[384,384]{1,0:T(8,128)(2,1)S(1)}, u32[]{:S(2)}, u32[]{:S(2)}) collective-permute-start(bf16[384,384]{1,0:T(8,128)(2,1)S(1)} %collective-permute-done.24.refs_2_), channel_id=1, source_target_pairs={{0,4},{4,0},{8,12},{12,8},{16,20},{20,16},{24,28},{28,24},{1,5},{5... | collective-permute-start | bytes 884744 | tf_op jit(solution)/shard_map/ppermute | solution.py:56
  160.7 5.1 %collective-permute-start.28 = (bf16[384,384]{1,0:T(8,128)(2,1)S(1)}, bf16[384,384]{1,0:T(8,128)(2,1)S(1)}, u32[]{:S(2)}, u32[]{:S(2)}) collective-permute-start(bf16[384,384]{1,0:T(8,128)(2,1)S(1)} %collective-permute-done.23.refs_1_), channel_id=1, source_target_pairs={{0,4},{4,0},{8,12},{12,8},{16,20},{20,16},{24,28},{28,24},{1,5},{5... | collective-permute-start | bytes 884744 | tf_op jit(solution)/shard_map/ppermute | solution.py:56
  163.2 1.4 collective-permute-start.30
  164.5 1.4 collective-permute-start.31
  171.4 11.9 %collective-permute-start.32 = (bf16[384,512]{1,0:T(8,128)(2,1)S(1)}, bf16[384,512]{1,0:T(8,128)(2,1)S(1)}, u32[]{:S(2)}, u32[]{:S(2)}) collective-permute-start(bf16[384,512]{1,0:T(8,128)(2,1)S(1)} %get-tuple-element.27), channel_id=1, source_target_pairs={{0,3},{1,0},{2,1},{3,2},{4,7},{5,4},{6,5},{7,6},{8,11},{9,8},{10,9... | collective-permute-start | bytes 1179656 | tf_op jit(solution)/shard_map/ppermute | solution.py:52
  175.5 16.5 %collective-permute-start.34 = (bf16[384,512]{1,0:T(8,128)(2,1)S(1)}, bf16[384,512]{1,0:T(8,128)(2,1)S(1)}, u32[]{:S(2)}, u32[]{:S(2)}) collective-permute-start(bf16[384,512]{1,0:T(8,128)(2,1)S(1)} %shard_map.90), channel_id=1, source_target_pairs={{0,1},{1,2},{2,3},{3,0},{4,5},{5,6},{6,7},{7,4},{8,9},{9,10},{10,1... | collective-permute-start | bytes 1179656 | tf_op jit(solution)/shard_map/ppermute | solution.py:52
  183.5 16.2 %collective-permute-start.33 = (bf16[384,512]{1,0:T(8,128)(2,1)S(1)}, bf16[384,512]{1,0:T(8,128)(2,1)S(1)}, u32[]{:S(2)}, u32[]{:S(2)}) collective-permute-start(bf16[384,512]{1,0:T(8,128)(2,1)S(1)} %add_convert_fusion.1), channel_id=1, source_target_pairs={{0,3},{1,0},{2,1},{3,2},{4,7},{5,4},{6,5},{7,6},{8,11},{9,8},{10,9... | collective-permute-start | bytes 1179656 | tf_op jit(solution)/shard_map/ppermute | solution.py:52
  199.9 13.9 %collective-permute-start.35 = (bf16[384,512]{1,0:T(8,128)(2,1)S(1)}, bf16[384,512]{1,0:T(8,128)(2,1)S(1)}, u32[]{:S(2)}, u32[]{:S(2)}) collective-permute-start(bf16[384,512]{1,0:T(8,128)(2,1)S(1)} %add_convert_fusion.refs_3_), channel_id=1, source_target_pairs={{0,1},{1,2},{2,3},{3,0},{4,5},{5,6},{6,7},{7,4},{8,9},{9,10},{10,1... | collective-permute-start | bytes 1179656 | tf_op jit(solution)/shard_map/ppermute | solution.py:52
  200.5 19.2 %collective-permute-start.37 = (bf16[384,512]{1,0:T(8,128)(2,1)S(1)}, bf16[384,512]{1,0:T(8,128)(2,1)S(1)}, u32[]{:S(2)}, u32[]{:S(2)}) collective-permute-start(bf16[384,512]{1,0:T(8,128)(2,1)S(1)} %add_convert_fusion.refs_3_), channel_id=1, source_target_pairs={{0,3},{1,0},{2,1},{3,2},{4,7},{5,4},{6,5},{7,6},{8,11},{9,8},{10,9... | collective-permute-start | bytes 1179656 | tf_op jit(solution)/shard_map/ppermute | solution.py:52
  213.7 15.9 %collective-permute-start.36 = (bf16[384,512]{1,0:T(8,128)(2,1)S(1)}, bf16[384,512]{1,0:T(8,128)(2,1)S(1)}, u32[]{:S(2)}, u32[]{:S(2)}) collective-permute-start(bf16[384,512]{1,0:T(8,128)(2,1)S(1)} %collective-permute-done.35.refs_4_), channel_id=1, source_target_pairs={{0,1},{1,2},{2,3},{3,0},{4,5},{5,6},{6,7},{7,4},{8,9},{9,10},{10,1... | collective-permute-start | bytes 1179656 | tf_op jit(solution)/shard_map/ppermute | solution.py:52

commit v7 on v0

v7 whole, which is shorter than its diff:
```python
import math

import jax
import jax.numpy as jnp
from jax import lax
from jax.experimental import pallas as pl
from jax.experimental.pallas import tpu as pltpu
from jax.sharding import PartitionSpec as P

BLK = 128
F32 = jnp.float32
BF16 = jnp.bfloat16
VMEM = pl.BlockSpec(memory_space=pltpu.VMEM)
ANY = pl.BlockSpec(memory_space=pl.ANY)


def dot(a, b, contract=((1,), (0,))):
    return lax.dot_general(a, b, (contract, ((), ())), preferred_element_type=F32)


def in_hbm(x):
    return pltpu.with_memory_space_constraint(x, pltpu.HBM)


def kernel_call(body, outs, scalars, held, placed, scratch, flops, nbytes, final=False):
    size = sum(2 * math.prod(s.shape) for s in scratch if s.dtype == BF16)
    single = not isinstance(outs, list)
    out_shape = [o if final else pltpu.VMEM(o.shape, o.dtype) for o in ([outs] if single else outs)]
    results = pl.pallas_call(
        body,
        out_shape=out_shape,
        grid_spec=pltpu.PrefetchScalarGridSpec(
            num_scalar_prefetch=len(scalars),
            grid=(1,),
            in_specs=[VMEM] * len(held) + [ANY] * len(placed),
            out_specs=[VMEM] * len(out_shape),
            scratch_shapes=scratch,
        ),
        compiler_params=pltpu.CompilerParams(vmem_limit_bytes=size + 12 * 1024 * 1024),
        cost_estimate=pl.CostEstimate(flops=flops, bytes_accessed=nbytes, transcendentals=0),
    )(*scalars, *[pltpu.with_memory_space_constraint(x, pltpu.VMEM) for x in held], *placed)
    return results[0] if single else results


def shift(x, size, by):
    return lax.ppermute(x, "row", [(i, (i + by) % size) for i in range(size)])


def swap(x, size, by):
    return lax.ppermute(x, "front", [(i, i ^ by) for i in range(size)])


def gather_row(x, n):
    found = [(0, x)]
    up, down = x, x
    for step in range(1, n // 2 + 1):
        up = shift(up, n, 1)
        found.append((-step, up))
        if step < n - step:
            down = shift(down, n, -1)
            found.append((step, down))
    return found


def gather_front(x, n):
    rows = x.shape[0]
    by_x, by_y = swap(x, n, 2), swap(x, n, 4)
    corner_low = swap(by_y[: rows // 2], n, 2)
    corner_high = swap(by_x[rows // 2 :], n, 4)
    mine = [(0, 0, x), (1, 0, by_x), (2, 0, by_y), (3, 0, corner_low), (3, rows // 2, corner_high)]
    found = [(chip, 0, low, block) for chip, low, block in mine]
    return found + [(chip, 1, low, swap(block, n, 1)) for chip, low, block in mine]


def to_plane(x, n):
    rows = x.shape[0] // n
    moved = []
    for k in range(n):
        quarter = x[k * rows : (k + 1) * rows]
        if k:
            quarter = swap(quarter, 2 * n, 2 * k)
        perm = [
            ((chip * 2 + core) * n + row, (row * 2 + core) * n + (chip ^ k))
            for chip in range(n)
            for core in range(2)
            for row in range(n)
        ]
        moved.append(lax.ppermute(quarter, ("front", "row"), perm))
    return jnp.concatenate(moved, axis=0)


def far_offsets(n):
    first = [-(n // 2)] + ([(n - 1) // 2] if n > 2 else [])
    later = [o for o in range(-(n // 2) + 1, (n - 1) // 2) if o]
    return first, later


def scatter_row(first, later, own, n):
    total = own
    for sign, far in ((-1, n // 2), (1, (n - 1) // 2)):
        running = None
        for step in range(far, 0, -1):
            if running is None:
                running = first[sign * step]
            else:
                running = (running.astype(F32) + later[sign * step]).astype(BF16)
            running = shift(running, n, sign)
        if running is not None:
            total = total + running.astype(F32)
    return total


def owner(at_ref, offset, n_row):
    return lax.rem(at_ref[0] + (offset + n_row), n_row)


def products(at_ref, a_ref, rows, offsets, x_refs, n_row, contract):
    depth = a_ref.shape[1] // n_row
    total = None
    for offset, x_ref in zip(offsets, x_refs):
        columns = pl.ds(pl.multiple_of(owner(at_ref, offset, n_row) * depth, depth), depth)
        part = dot(a_ref[rows, columns], x_ref[...], contract)
        total = part if total is None else total + part
    return total


def pivot_products(at, pivot, found, n_row, contract, finish, outs, extra=(), final=False):
    count = len(found)
    offsets = [o for o, _ in found]

    def body(at_ref, a_ref, *refs):
        total = products(at_ref, a_ref, slice(None), offsets, refs[:count], n_row, contract)
        extras = refs[count : count + len(extra)]
        for ref, value in zip(refs[count + len(extra) :], finish(total, *[e[...] for e in extras])):
            ref[...] = value

    share = 2 * pivot.size * count // n_row
    held = [pivot] + [x for _, x in found] + list(extra)
    return kernel_call(body, outs, [at], held, [], [], share * outs[0].shape[1], share, final)


def border_tile(rows):
    return BLK * next(k for k in (4, 3, 2, 1) if rows // BLK % k == 0)


def border_partial(at, coupling, found, n_row, partial, rhs_root, piece_rows):
    rows, count, width = coupling.shape[0], len(found), found[0][1].shape[1]
    offsets = [o for o, _ in found]
    tile = border_tile(rows)
    held = [coupling] + [x for _, x in found] + ([] if partial is None else [partial])

    def body(at_ref, a_ref, *refs):
        if partial is None:
            rhs_hbm, out_ref, own_ref, sem = refs[count:]
            place = pl.ds(pl.multiple_of(at_ref[1] * piece_rows, piece_rows), piece_rows)
            copy = pltpu.make_async_copy(rhs_hbm.at[place], own_ref, sem)
            copy.start()
        else:
            partial_ref, out_ref = refs[count:]

        @pl.loop(0, rows // tile)
        def _(i):
            place = pl.ds(pl.multiple_of(i * tile, tile), tile)
            total = products(at_ref, a_ref, place, offsets, refs[:count], n_row, ((1,), (0,)))
            out_ref[place, :] = total if partial is None else partial_ref[place, :] + total

        if partial is None:
            copy.wait()

    share = 2 * coupling.size * count // n_row
    out = jax.ShapeDtypeStruct((rows, width), F32)
    if partial is None:
        outs = [out, jax.ShapeDtypeStruct((piece_rows, width), F32)]
        scratch = [pltpu.SemaphoreType.DMA]
        return kernel_call(body, outs, [at], held, [in_hbm(rhs_root)], scratch, share * width, share)
    return kernel_call(body, out, [at], held, [], [], share * width, share)


def border_scatter(at, local_index, coupling, found, partial, n_row, n_front, span_rows):
    rows, count, width = coupling.shape[0], len(found), found[0][1].shape[1]
    offsets = [o for o, _ in found]
    tile = border_tile(rows)
    piece_blocks = span_rows // n_front // BLK

    def body(at_ref, index_ref, a_ref, *refs):
        partial_ref, send_ref, keep_ref = refs[count:]
        send_ref[...] = jnp.zeros_like(send_ref)
        keep_ref[...] = jnp.zeros_like(keep_ref)

        @pl.loop(0, rows // tile)
        def _(i):
            place = pl.ds(pl.multiple_of(i * tile, tile), tile)
            total = products(at_ref, a_ref, place, offsets, refs[:count], n_row, ((1,), (0,)))
            total = (partial_ref[place, :] + total).astype(BF16)
            for j in range(tile // BLK):
                target = index_ref[i * (tile // BLK) + j]
                there = lax.div(target, piece_blocks)
                chip = lax.shift_right_logical(lax.bitwise_xor(there, at_ref[1]), 1)
                slot = chip * piece_blocks + lax.rem(target, piece_blocks)
                goal = pl.ds(pl.multiple_of(slot * BLK, BLK), BLK)
                block = total[j * BLK : (j + 1) * BLK]
                away = lax.rem(there + at_ref[1], 2)

                @pl.when(away == 1)
                def _():
                    send_ref[goal, :] = block

                @pl.when(away == 0)
                def _():
                    keep_ref[goal, :] = block

    half = jax.ShapeDtypeStruct((span_rows // 2, width), BF16)
    share = 2 * coupling.size * count // n_row
    held = [coupling] + [x for _, x in found] + [partial]
    return kernel_call(body, [half, half], [at, local_index], held, [], [], share * width, share)


def added(*parts):
    total = parts[0].astype(F32)
    for part in parts[1:]:
        total = total + part.astype(F32)
    return total


def corner_parts(keep, came):
    rows, width = keep.shape[0] // 4, keep.shape[1]
    half = jax.ShapeDtypeStruct((rows // 2, width), BF16)

    def body(keep_ref, came_ref, low_ref, high_ref):
        for start, out_ref in ((3 * rows, low_ref), (3 * rows + rows // 2, high_ref)):
            place = slice(start, start + rows // 2)
            out_ref[...] = added(keep_ref[place, :], came_ref[place, :]).astype(BF16)

    return kernel_call(body, [half, half], [], [keep, came], [], [], keep.size, keep.size)


def side_parts(keep, came, low, high):
    rows, width = keep.shape[0] // 4, keep.shape[1]
    part = jax.ShapeDtypeStruct((rows, width), BF16)

    def body(keep_ref, came_ref, low_ref, high_ref, x_ref, y_ref):
        first, second = (0, rows // 2), (rows // 2, rows)
        for slot, add_ref, here, other, out_ref in (
            (1, high_ref, second, first, x_ref),
            (2, low_ref, first, second, y_ref),
        ):
            place = slice(slot * rows + other[0], slot * rows + other[1])
            out_ref[other[0] : other[1], :] = added(keep_ref[place, :], came_ref[place, :]).astype(BF16)
            place = slice(slot * rows + here[0], slot * rows + here[1])
            total = added(keep_ref[place, :], came_ref[place, :], add_ref[...])
            out_ref[here[0] : here[1], :] = total.astype(BF16)

    return kernel_call(body, [part, part], [], [keep, came, low, high], [], [], 2 * keep.size, 2 * keep.size)


def own_part(own_rhs, keep, came, by_x, by_y):
    rows, width = by_x.shape

    def body(rhs_ref, keep_ref, came_ref, x_ref, y_ref, out_ref):
        total = added(keep_ref[:rows, :], came_ref[:rows, :], x_ref[...], y_ref[...])
        out_ref[...] = (rhs_ref[...] - total).astype(BF16)

    out = jax.ShapeDtypeStruct((rows, width), BF16)
    return kernel_call(body, out, [], [own_rhs, keep, came, by_x, by_y], [], [], keep.size, keep.size)


def assemble(pieces, piece_refs, target_ref, sems, base):
    copies = []
    for (chip, core, low, block), ref in zip(pieces, piece_refs):
        start = base(2 * chip + core) + low
        place = pl.ds(pl.multiple_of(start, block.shape[0]), block.shape[0])
        copies.append(pltpu.make_async_copy(ref, target_ref.at[place], sems.at[len(copies)]))
    return copies


def root_products(at, inverse, pieces, offsets, kinds, n_row, n_front):
    span_rows = inverse.shape[1]
    rows = inverse.shape[0] // n_row
    width = pieces[0][3].shape[1]
    piece_rows = span_rows // n_front
    count, many = len(offsets), len(pieces)

    def body(at_ref, *refs):
        piece_refs, a_hbm, out_refs = refs[:many], refs[many], refs[many + 1 : many + 1 + count]
        a_ref, x_ref, sems = refs[-3:]
        copies = assemble(
            pieces, piece_refs, x_ref, sems, lambda d: lax.bitwise_xor(at_ref[1], d) * piece_rows
        )
        loads = []
        for i, offset in enumerate(offsets):
            place = pl.ds(pl.multiple_of(owner(at_ref, offset, n_row) * rows, rows), rows)
            loads.append(pltpu.make_async_copy(a_hbm.at[place], a_ref.at[i], sems.at[many + i]))
        for copy in loads[:1] + copies + loads[1:]:
            copy.start()
        for copy in copies:
            copy.wait()
        for i in range(count):
            loads[i].wait()
            out_refs[i][...] = dot(a_ref[i], x_ref[...]).astype(out_refs[i].dtype)

    outs = [jax.ShapeDtypeStruct((rows, width), kind) for kind in kinds]
    scratch = [
        pltpu.VMEM((count, rows, span_rows), BF16),
        pltpu.VMEM((span_rows, width), BF16),
        pltpu.SemaphoreType.DMA((many + count,)),
    ]
    share = 2 * rows * span_rows * count
    held = [block for *_, block in pieces]
    return kernel_call(body, outs, [at], held, [in_hbm(inverse)], scratch, share * width, share)


def border_pick(at, local_index, coupling, pieces, offset, n_row, n_front):
    rows, depth = coupling.shape[0], coupling.shape[1] // n_row
    piece_rows, width = pieces[0][3].shape
    span_rows = piece_rows * n_front
    many = len(pieces)

    def body(at_ref, index_ref, a_ref, *refs):
        piece_refs, (out_ref, picked_ref, span_ref, sems) = refs[:many], refs[many:]

        def base(d):
            there = lax.bitwise_xor(at_ref[1], d)
            return lax.rem(there, 2) * (span_rows // 2) + lax.shift_right_logical(there, 1) * piece_rows

        copies = assemble(pieces, piece_refs, span_ref, sems, base)
        for copy in copies:
            copy.start()
        for copy in copies:
            copy.wait()
        for j in range(rows // BLK):
            source = pl.ds(pl.multiple_of(index_ref[j] * BLK, BLK), BLK)
            picked_ref[:, pl.ds(j * BLK, BLK)] = jnp.transpose(span_ref[source, :])
        columns = pl.ds(pl.multiple_of(owner(at_ref, offset, n_row) * depth, depth), depth)
        out_ref[...] = dot(picked_ref[...], a_ref[:, columns]).astype(BF16)

    outs = [jax.ShapeDtypeStruct((width, depth), BF16), jax.ShapeDtypeStruct((width, rows), BF16)]
    scratch = [pltpu.VMEM((span_rows, width), BF16), pltpu.SemaphoreType.DMA((many,))]
    share = 2 * rows * depth
    held = [coupling] + [block for *_, block in pieces]
    return kernel_call(body, outs, [at, local_index], held, [], scratch, share * width, share)


def border_backward(at, coupling, picked, offsets, kinds, n_row):
    rows, depth = coupling.shape[0], coupling.shape[1] // n_row
    width, count = picked.shape[0], len(offsets)

    def body(at_ref, x_ref, a_ref, *out_refs):
        for offset, out_ref in zip(offsets, out_refs):
            columns = pl.ds(pl.multiple_of(owner(at_ref, offset, n_row) * depth, depth), depth)
            out_ref[...] = dot(x_ref[...], a_ref[:, columns]).astype(out_ref.dtype)

    outs = [jax.ShapeDtypeStruct((width, depth), kind) for kind in kinds]
    share = 2 * rows * depth * count
    return kernel_call(body, outs, [at], [picked, coupling], [], [], share * width, share)


def solve(n_front, n_row, rhs_front, rhs_root, pivot_inverse, border_coupling, root_inverse, border_map):
    row_at = lax.axis_index("row").astype(jnp.int32)
    front_at = lax.axis_index("front").astype(jnp.int32)
    at = jnp.stack([row_at, front_at])
    span_rows = root_inverse.shape[1]
    piece_rows, width = span_rows // n_front, rhs_front.shape[1]
    local_index = border_map[0] - row_at * (span_rows // BLK)
    first_at, later_at = far_offsets(n_row)
    block = jax.ShapeDtypeStruct((pivot_inverse.shape[0], width), F32)
    half = jax.ShapeDtypeStruct(block.shape, BF16)
    straight, across = ((1,), (0,)), ((1,), (1,))

    found = gather_row(rhs_front, n_row)
    early, last = found[:-1], found[-1:]
    partial = pivot_products(at, pivot_inverse, early, n_row, straight, lambda t: [t], [block])
    inner, inner_half = pivot_products(
        at,
        pivot_inverse,
        last,
        n_row,
        straight,
        lambda t, p: [t + p, (t + p).astype(BF16)],
        [block, half],
        partial,
    )
    found = gather_row(inner_half, n_row)
    partial, own_rhs = border_partial(at, border_coupling, found[:2], n_row, None, rhs_root, piece_rows)
    if found[2:-1]:
        partial = border_partial(at, border_coupling, found[2:-1], n_row, partial, rhs_root, piece_rows)
    send, keep = border_scatter(
        at, local_index, border_coupling, found[-1:], partial, n_row, n_front, span_rows
    )
    came = swap(send, n_front, 1)
    low, high = corner_parts(keep, came)
    by_x, by_y = side_parts(keep, came, swap(low, n_front, 2), swap(high, n_front, 4))
    piece = own_part(own_rhs, keep, came, swap(by_x, n_front, 2), swap(by_y, n_front, 4))
    pieces = gather_front(piece, n_front)

    def root(offsets, kind):
        outs = root_products(at, root_inverse, pieces, offsets, [kind] * len(offsets), n_row, n_front)
        return dict(zip(offsets, outs))

    first = {}
    for offset in first_at:
        first.update(root([offset], BF16))
    rest = root(later_at + [0], F32)
    root_solution = scatter_row(first, rest, rest[0], n_row)
    spans = gather_front(to_plane(root_solution.astype(BF16), n_row), n_front)

    out, picked = border_pick(at, local_index, border_coupling, spans, first_at[0], n_row, n_front)
    first = {first_at[0]: out}
    for offset in first_at[1:]:
        first[offset] = border_backward(at, border_coupling, picked, [offset], [BF16], n_row)[0]
    offsets = later_at + [0]
    rest = dict(zip(offsets, border_backward(at, border_coupling, picked, offsets, [F32] * len(offsets), n_row)))
    pulled = scatter_row(first, rest, rest[0], n_row).astype(BF16)
    found = gather_row(pulled, n_row)
    early, last = found[:-1], found[-1:]
    partial = pivot_products(
        at, pivot_inverse, early, n_row, across, lambda t, i: [i - t], [block], [inner]
    )
    front_solution = pivot_products(
        at, pivot_inverse, last, n_row, across, lambda t, p: [p - t], [block], partial, True
    )
    return front_solution[0], root_solution


def solve_plain(n_front, n_row, rhs_front, rhs_root, pivot_inverse, border_coupling, root_inverse, border_map):
    row_at = lax.axis_index("row")
    front_at = lax.axis_index("front")
    width = rhs_front.shape[1]
    inner = dot(pivot_inverse, lax.all_gather(rhs_front, "row", axis=0, tiled=True))
    contrib = dot(border_coupling, lax.all_gather(inner.astype(BF16), "row", axis=0, tiled=True))
    block_local = border_map.shape[1]
    span_rows = root_inverse.shape[1]
    span_blocks = span_rows // BLK
    local_index = border_map[0] - row_at * span_blocks
    select = (local_index[None, :] == jnp.arange(span_blocks, dtype=jnp.int32)[:, None]).astype(F32)
    dense = jnp.einsum(
        "kj,jcn->kcn", select, contrib.reshape(block_local, BLK, width), precision=lax.Precision.HIGHEST
    ).reshape(span_rows, width)
    shares = lax.psum_scatter(dense, "front", scatter_dimension=0, tiled=True)
    own_rhs = lax.dynamic_slice_in_dim(rhs_root, front_at * shares.shape[0], shares.shape[0], 0)
    schur_rhs = lax.all_gather((own_rhs - shares).astype(BF16), "front", axis=0, tiled=True)
    root_solution = lax.psum_scatter(dot(root_inverse, schur_rhs), "row", scatter_dimension=0, tiled=True)
    gathered = lax.all_gather(root_solution.astype(BF16), ("front", "row"), axis=0, tiled=True)
    ranged = lax.dynamic_slice_in_dim(gathered, row_at * span_rows, span_rows, 0)
    picked = jnp.take(ranged.reshape(span_blocks, BLK, width), local_index, axis=0)
    picked = picked.reshape(block_local * BLK, width)
    pulled = lax.psum_scatter(
        dot(border_coupling, picked, ((0,), (0,))), "row", scatter_dimension=0, tiled=True
    ).astype(BF16)
    correction = dot(pivot_inverse, lax.all_gather(pulled, "row", axis=0, tiled=True))
    return inner - correction, root_solution


def solution(mesh):
    in_specs = (
        P(("front", "row"), None),
        P("row", None),
        P(("front", "row"), None),
        P(("front", "row"), None),
        P("front", "row"),
        P("front", "row"),
    )
    out_specs = (P(("front", "row"), None), P(("front", "row"), None))
    n_front, n_row = mesh.shape["front"], mesh.shape["row"]

    def per_device(*arrays):
        root_inverse, width = arrays[4], arrays[0].shape[1]
        fits = (
            n_front == 8
            and n_front == 2 * n_row
            and root_inverse.shape[1] % (n_front * BLK) == 0
            and root_inverse.shape[0] == n_row * (root_inverse.shape[1] // n_front)
            and root_inverse.shape[1] % (n_front * n_row * 16) == 0
            and arrays[2].shape[1] % (n_row * BLK) == 0
            and width % BLK == 0
        )
        return (solve if fits else solve_plain)(n_front, n_row, *arrays)

    return jax.shard_map(per_device, mesh=mesh, in_specs=in_specs, out_specs=out_specs, check_vma=False)
```

time: 466 us -> 225 us (0.48)
  waiting for transfers between devices: 390 us -> 134 us
  starting transfers between devices: 0.51 us -> 46.5 us
  matrix products: 39.5 us -> 0 us
  Pallas kernels: 0 us -> 34.1 us
  between operations: 14.2 us -> 0.98 us
  local copies, waits for them, and re-layouts: 14.8 us -> 7.28 us
    all_gather x5 -> x0, waiting for transfers between devices: 230 us -> none  [the longest x1 86.8 us: per_device(): gathered = lax.all_gather(root_half, ('front', 'row'), axis=0, tiled=True)]
    reduce_scatter x3 -> x0, waiting for transfers between devices: 160 us -> none  [the longest x1 58.5 us: per_device(): lax.psum_scatter(lax.dot_general(columns, picked, (((0,), (0,)), ((), ())...]
    ppermute x0 -> x45, waiting for transfers between devices: none -> 134 us  [the longest x15 90.4 us: shift(): return lax.ppermute(x, 'row', [(i, (i + by) % size) for i in range(size)])]
    ppermute x0 -> x45, starting transfers between devices: none -> 46.5 us  [the longest x15 21.6 us: shift(): return lax.ppermute(x, 'row', [(i, (i + by) % size) for i in range(size)])]
    dot_general x7 -> x0, matrix products: 39.5 us -> none  [the longest x1 9.69 us: per_device(): jnp.dot(root_inverse, schur_rhs, preferred_element_type=jnp.float32)]
    pallas_call x0 -> x16, Pallas kernels: none -> 34.1 us  [kernel_call(): pl.pallas_call(body, out_shape=out_shape, grid_spec=pltpu.PrefetchScalarG...]
    dynamic_slice x2 -> x0, local copies, waits for them, and re-layouts: 7.47 us -> none  [per_device(): lax.dynamic_slice_in_dim(gathered, row_at * span_rows, span_rows, 0)]
    unnamed x7 -> x21, local copies, waits for them, and re-layouts: 1.07 us -> 7.17 us
  transfers between devices with their start and end apart: 8 -> 45, of which waited for: 8 -> 30; matrix products, arithmetic and copies ran while one was open for 0% -> 0% of each run, Pallas kernels for 0% -> 10%
where the time goes in v7:
time: 225 us
  waiting for transfers between devices  134 us (60%)
  starting transfers between devices  46.5 us (21%)
  Pallas kernels  34.1 us (15%)
  local copies, waits for them, and re-layouts  7.28 us (3%)
    ppermute x15, waiting for transfers between devices, shift(): return lax.ppermute(x, 'row', [(i, (i + by) % size) for i in range(size)])  90.4 us
    ppermute x26, waiting for transfers between devices, swap(): return lax.ppermute(x, 'front', [(i, i ^ by) for i in range(size)])  39.7 us
    pallas_call x16, Pallas kernels, kernel_call(): pl.pallas_call(body, out_shape=out_shape, grid_spec=pltpu.PrefetchScalarG...  34.1 us
    ppermute x15, starting transfers between devices, shift(): return lax.ppermute(x, 'row', [(i, (i + by) % size) for i in range(size)])  21.6 us
    ppermute x26, starting transfers between devices, swap(): return lax.ppermute(x, 'front', [(i, i ^ by) for i in range(size)])  19.9 us
    unnamed x21, local copies, waits for them, and re-layouts  7.17 us
    ppermute x4, starting transfers between devices, to_plane(): moved.append(lax.ppermute(quarter, ('front', 'row'), perm))  5.01 us
  transfers between devices with their start and end apart: 45, of which 30 were waited for; matrix products, arithmetic and copies ran while one was open for 0% of the time, Pallas kernels for 10%

profile of v7, /device:TPU:0, one launch (start us, length us, event | category | flops | bytes accessed | tf_op | source)
XLA Modules:
  0.0 224.6 jit_solution(13540935457880249857)
XLA Ops:
  0.6 3.1 %collective-permute-start = (bf16[512,384]{1,0:T(8,128)(2,1)}, bf16[512,384]{1,0:T(8,128)(2,1)S(1)}, u32[]{:S(2)}, u32[]{:S(2)}) collective-permute-start(bf16[512,384]{1,0:T(8,128)(2,1)} %refs_0_.1), channel_id=1, source_target_pairs={{0,1},{1,2},{2,3},{3,0},{4,5},{5,6},{6,7},{7,4},{8,9},{9,10},{10,1... | collective-permute-start | bytes 1179656 | tf_op jit(solution)/shard_map/ppermute | solution.py:46
  3.7 2.1 collective-permute-start.2
  5.8 10.1 %collective-permute-done.refs_1_ = bf16[512,384]{1,0:T(8,128)(2,1)S(1)} collective-permute-done((bf16[512,384]{1,0:T(8,128)(2,1)}, bf16[512,384]{1,0:T(8,128)(2,1)S(1)}, u32[]{:S(2)}, u32[]{:S(2)}) %collective-permute-start) | collective-permute-done | bytes 393248 | tf_op jit(solution)/shard_map/ppermute | solution.py:46
  16.0 7.1 %collective-permute-done.2.refs_2_ = bf16[512,384]{1,0:T(8,128)(2,1)S(1)} collective-permute-done((bf16[512,384]{1,0:T(8,128)(2,1)}, bf16[512,384]{1,0:T(8,128)(2,1)S(1)}, u32[]{:S(2)}, u32[]{:S(2)}) %collective-permute-start.2) | collective-permute-done | bytes 393248 | tf_op jit(solution)/shard_map/ppermute | solution.py:46
  23.1 1.6 copy-done.1
  24.7 1.0 copy-done.3
  25.7 1.5 shard_map.77.refs_1_
  27.2 4.7 %collective-permute-done.1.refs_0_ = bf16[512,384]{1,0:T(8,128)(2,1)S(1)} collective-permute-done((bf16[512,384]{1,0:T(8,128)(2,1)S(1)}, bf16[512,384]{1,0:T(8,128)(2,1)S(1)}, u32[]{:S(2)}, u32[]{:S(2)}) %collective-permute-start.1) | collective-permute-done | bytes 393248 | tf_op jit(solution)/shard_map/ppermute | solution.py:46
  32.7 1.0 copy-done.5
  33.7 1.0 shard_map.78
  34.7 3.8 %collective-permute-start.5 = (bf16[512,384]{1,0:T(8,128)(2,1)S(1)}, bf16[512,384]{1,0:T(8,128)(2,1)}, u32[]{:S(2)}, u32[]{:S(2)}) collective-permute-start(bf16[512,384]{1,0:T(8,128)(2,1)S(1)} %get-tuple-element.18.refs_0_), channel_id=1, source_target_pairs={{0,3},{1,0},{2,1},{3,2},{4,7},{5,4},{6,5},{7,6},{8,11},{9,8},{10,9... | collective-permute-start | bytes 1179656 | tf_op jit(solution)/shard_map/ppermute | solution.py:46
  38.6 10.1 %collective-permute-done.3.refs_1_ = bf16[512,384]{1,0:T(8,128)(2,1)} collective-permute-done((bf16[512,384]{1,0:T(8,128)(2,1)S(1)}, bf16[512,384]{1,0:T(8,128)(2,1)}, u32[]{:S(2)}, u32[]{:S(2)}) %collective-permute-start.3) | collective-permute-done | bytes 393248 | tf_op jit(solution)/shard_map/ppermute | solution.py:46
  48.7 2.8 %copy-done = bf16[1536,2048]{1,0:T(8,128)(2,1)S(1)} copy-done((bf16[1536,2048]{1,0:T(8,128)(2,1)S(1)}, bf16[1536,2048]{1,0:T(8,128)(2,1)}, u32[]{:S(2)}) %copy-start) | copy-done | bytes 6291480
  51.5 4.0 %shard_map.79 = (f32[1536,384]{1,0:T(8,128)S(1)}, f32[384,384]{1,0:T(8,128)S(1)}) custom-call(s32[2]{0:T(128)S(1)} %pad_add_fusion.at_ref, bf16[1536,2048]{1,0:T(8,128)(2,1)S(1)} %copy-done, bf16[512,384]{1,0:T(8,128)(2,1)S(1)} %get-tuple-element.18.refs_0_, bf16[512,384]{1,0:T(8,128)(2,1)} %collective-permute-done.3.refs_1_, f32[3072,384]{1,0:T(8,128)} %refs_2_.1), custom_call_target="tpu_custom_call" | custom-call | flops 1207959552 | bytes 3145728 | tf_op jit(solution)/shard_map/pallas_call | solution.py:29
  55.5 2.9 %shard_map.80.refs_1_ = f32[1536,384]{1,0:T(8,128)S(1)} custom-call(s32[2]{0:T(128)S(1)} %pad_add_fusion.at_ref, bf16[1536,2048]{1,0:T(8,128)(2,1)S(1)} %bitcast.5, bf16[512,384]{1,0:T(8,128)(2,1)} %collective-permute-done.5.refs_0_, f32[1536,384]{1,0:T(8,128)S(1)} %get-tuple-element.20.refs_1_), custom_call_target="tpu_custom_call" | custom-call | flops 603979776 | bytes 1572864 | tf_op jit(solution)/shard_map/pallas_call | solution.py:29
  58.4 3.9 %collective-permute-done.4.refs_0_ = bf16[512,384]{1,0:T(8,128)(2,1)S(1)} collective-permute-done((bf16[512,384]{1,0:T(8,128)(2,1)}, bf16[512,384]{1,0:T(8,128)(2,1)S(1)}, u32[]{:S(2)}, u32[]{:S(2)}) %collective-permute-start.4) | collective-permute-done | bytes 393248 | tf_op jit(solution)/shard_map/ppermute | solution.py:46
  62.2 2.4 %shard_map.81 = (bf16[1536,384]{1,0:T(8,128)(2,1)S(1)}, bf16[1536,384]{1,0:T(8,128)(2,1)S(1)}) custom-call(s32[2]{0:T(128)S(1)} %pad_add_fusion.at_ref, s32[12]{0:T(128)S(1)} %subtract_bitcast_fusion.index_ref, bf16[1536,2048]{1,0:T(8,128)(2,1)S(1)} %bitcast.5, bf16[512,384]{1,0:T(8,128)(2,1)S(1)} %collective-permute-done.4.refs_0_, ...), custom_call_target="tpu_custom_call" | custom-call | flops 603979776 | bytes 1572864 | tf_op jit(solution)/shard_map/pallas_call | solution.py:29
  64.7 2.8 %collective-permute-done.6.came_ref = bf16[1536,384]{1,0:T(8,128)(2,1)S(1)} collective-permute-done((bf16[1536,384]{1,0:T(8,128)(2,1)S(1)}, bf16[1536,384]{1,0:T(8,128)(2,1)S(1)}, u32[]{:S(2)}, u32[]{:S(2)}) %collective-permute-start.6) | collective-permute-done | bytes 1179680 | tf_op jit(solution)/shard_map/ppermute | solution.py:50
  67.6 1.6 collective-permute-start.7
  69.2 1.5 collective-permute-start.8
  70.7 2.9 %collective-permute-done.7.low_ref = bf16[192,384]{1,0:T(8,128)(2,1)S(1)} collective-permute-done((bf16[192,384]{1,0:T(8,128)(2,1)S(1)}, bf16[192,384]{1,0:T(8,128)(2,1)S(1)}, u32[]{:S(2)}, u32[]{:S(2)}) %collective-permute-start.7) | collective-permute-done | bytes 147488 | tf_op jit(solution)/shard_map/ppermute | solution.py:50
  73.6 1.2 collective-permute-done.8.high_ref
  75.6 1.5 collective-permute-start.10
  77.1 5.8 %collective-permute-done.9.x_ref = bf16[384,384]{1,0:T(8,128)(2,1)S(1)} collective-permute-done((bf16[384,384]{1,0:T(8,128)(2,1)S(1)}, bf16[384,384]{1,0:T(8,128)(2,1)S(1)}, u32[]{:S(2)}, u32[]{:S(2)}) %collective-permute-start.9) | collective-permute-done | bytes 294944 | tf_op jit(solution)/shard_map/ppermute | solution.py:50
  83.4 1.6 collective-permute-start.12
  85.0 1.4 collective-permute-start.11
  86.4 3.8 %collective-permute-done.12.refs_2_ = bf16[384,384]{1,0:T(8,128)(2,1)S(1)} collective-permute-done((bf16[384,384]{1,0:T(8,128)(2,1)S(1)}, bf16[384,384]{1,0:T(8,128)(2,1)S(1)}, u32[]{:S(2)}, u32[]{:S(2)}) %collective-permute-start.12) | collective-permute-done | bytes 294944 | tf_op jit(solution)/shard_map/ppermute | solution.py:50
  90.3 1.4 collective-permute-start.13
  91.7 1.6 collective-permute-done.11.refs_1_
  94.0 1.5 collective-permute-done.13.refs_3_
  95.5 3.0 %collective-permute-done.14.refs_4_ = bf16[192,384]{1,0:T(8,128)(2,1)S(1)} collective-permute-done((bf16[192,384]{1,0:T(8,128)(2,1)S(1)}, bf16[192,384]{1,0:T(8,128)(2,1)S(1)}, u32[]{:S(2)}, u32[]{:S(2)}) %collective-permute-start.14) | collective-permute-done | bytes 147488 | tf_op jit(solution)/shard_map/ppermute | solution.py:50
  98.6 1.4 collective-permute-done.19.refs_9_
  99.9 3.7 %shard_map.86 = bf16[384,384]{1,0:T(8,128)(2,1)S(1)} custom-call(s32[2]{0:T(128)S(1)} %pad_add_fusion.at_ref, bf16[384,384]{1,0:T(8,128)(2,1)S(1)} %shard_map.84.refs_0_, bf16[384,384]{1,0:T(8,128)(2,1)S(1)} %collective-permute-done.11.refs_1_, bf16[384,384]{1,0:T(8,128)(2,1)S(1)} %collective-permute-done.12.refs_2_, ...), custom_call_target="tpu_custom_call" | custom-call | flops 905969664 | bytes 2359296 | tf_op jit(solution)/shard_map/pallas_call | solution.py:29
  103.7 3.7 %shard_map.87 = bf16[384,384]{1,0:T(8,128)(2,1)S(1)} custom-call(s32[2]{0:T(128)S(1)} %pad_add_fusion.at_ref, bf16[384,384]{1,0:T(8,128)(2,1)S(1)} %shard_map.84.refs_0_, bf16[384,384]{1,0:T(8,128)(2,1)S(1)} %collective-permute-done.11.refs_1_, bf16[384,384]{1,0:T(8,128)(2,1)S(1)} %collective-permute-done.12.refs_2_, ...), custom_call_target="tpu_custom_call" | custom-call | flops 905969664 | bytes 2359296 | tf_op jit(solution)/shard_map/pallas_call | solution.py:29
  107.4 2.1 collective-permute-start.22
  109.5 5.1 %shard_map.85 = (f32[384,384]{1,0:T(8,128)S(1)}, f32[384,384]{1,0:T(8,128)S(1)}) custom-call(s32[2]{0:T(128)S(1)} %pad_add_fusion.at_ref, bf16[384,384]{1,0:T(8,128)(2,1)S(1)} %shard_map.84.refs_0_, bf16[384,384]{1,0:T(8,128)(2,1)S(1)} %collective-permute-done.11.refs_1_, bf16[384,384]{1,0:T(8,128)(2,1)S(1)} %collective-permute-done.12.refs_2_, ...), custom_call_target="tpu_custom_call" | custom-call | flops 1811939328 | bytes 4718592 | tf_op jit(solution)/shard_map/pallas_call | solution.py:29
  114.6 5.1 %collective-permute-done.20 = bf16[384,384]{1,0:T(8,128)(2,1)S(1)} collective-permute-done((bf16[384,384]{1,0:T(8,128)(2,1)S(1)}, bf16[384,384]{1,0:T(8,128)(2,1)S(1)}, u32[]{:S(2)}, u32[]{:S(2)}) %collective-permute-start.20) | collective-permute-done | bytes 294944 | tf_op jit(solution)/shard_map/ppermute | solution.py:46
  119.8 6.7 %collective-permute-done.21 = bf16[384,384]{1,0:T(8,128)(2,1)S(1)} collective-permute-done((bf16[384,384]{1,0:T(8,128)(2,1)S(1)}, bf16[384,384]{1,0:T(8,128)(2,1)S(1)}, u32[]{:S(2)}, u32[]{:S(2)}) %collective-permute-start.21) | collective-permute-done | bytes 294944 | tf_op jit(solution)/shard_map/ppermute | solution.py:46
  126.5 0.9 fusion
  127.4 1.0 collective-permute-start.28
  128.4 2.0 collective-permute-start.26
  131.6 1.2 collective-permute-done.28
  132.8 4.3 %collective-permute-start.29 = (bf16[96,384]{1,0:T(8,128)(2,1)S(1)}, bf16[96,384]{1,0:T(8,128)(2,1)S(1)}, u32[]{:S(2)}, u32[]{:S(2)}) collective-permute-start(bf16[96,384]{1,0:T(8,128)(2,1)S(1)} %collective-permute-done.28), channel_id=1, source_target_pairs={{0,3},{1,11},{2,19},{3,27},{4,7},{5,15},{6,23},{7,31},{8,2},{9,10}... | collective-permute-start | bytes 221192 | tf_op jit(solution)/shard_map/ppermute | solution.py:88
  137.2 4.3 %collective-permute-done.25 = bf16[96,384]{1,0:T(8,128)(2,1)S(1)} collective-permute-done((bf16[96,384]{1,0:T(8,128)(2,1)S(1)}, bf16[96,384]{1,0:T(8,128)(2,1)S(1)}, u32[]{:S(2)}, u32[]{:S(2)}) %collective-permute-start.25) | collective-permute-done | bytes 73760 | tf_op jit(solution)/shard_map/ppermute | solution.py:88
  141.6 5.3 %collective-permute-start.31 = (bf16[384,384]{1,0:T(8,128)(2,1)S(1)}, bf16[384,384]{1,0:T(8,128)(2,1)S(1)}, u32[]{:S(2)}, u32[]{:S(2)}) collective-permute-start(bf16[384,384]{1,0:T(8,128)(2,1)S(1)} %constant_dynamic-update-slice_fusion.refs_0_), channel_id=1, source_target_pairs={{0,16},{4,20},{8,24},{12,28},{16,0},{20,4},{24,8},{28,12},{1,17},{... | collective-permute-start | bytes 884744 | tf_op jit(solution)/shard_map/ppermute | solution.py:50
  146.9 5.6 %collective-permute-done.31.refs_2_ = bf16[384,384]{1,0:T(8,128)(2,1)S(1)} collective-permute-done((bf16[384,384]{1,0:T(8,128)(2,1)S(1)}, bf16[384,384]{1,0:T(8,128)(2,1)S(1)}, u32[]{:S(2)}, u32[]{:S(2)}) %collective-permute-start.31) | collective-permute-done | bytes 294944 | tf_op jit(solution)/shard_map/ppermute | solution.py:50
  152.6 2.5 %collective-permute-done.30.refs_1_ = bf16[384,384]{1,0:T(8,128)(2,1)S(1)} collective-permute-done((bf16[384,384]{1,0:T(8,128)(2,1)S(1)}, bf16[384,384]{1,0:T(8,128)(2,1)S(1)}, u32[]{:S(2)}, u32[]{:S(2)}) %collective-permute-start.30) | collective-permute-done | bytes 294944 | tf_op jit(solution)/shard_map/ppermute | solution.py:50
  155.8 1.9 collective-permute-done.32.refs_3_
  157.7 2.6 %collective-permute-done.33.refs_4_ = bf16[192,384]{1,0:T(8,128)(2,1)S(1)} collective-permute-done((bf16[192,384]{1,0:T(8,128)(2,1)S(1)}, bf16[192,384]{1,0:T(8,128)(2,1)S(1)}, u32[]{:S(2)}, u32[]{:S(2)}) %collective-permute-start.33) | collective-permute-done | bytes 147488 | tf_op jit(solution)/shard_map/ppermute | solution.py:50
  160.4 1.4 collective-permute-done.38.refs_9_
  161.7 2.7 %shard_map.88 = (bf16[384,512]{1,0:T(8,128)(2,1)S(1)}, bf16[384,1536]{1,0:T(8,128)(2,1)S(1)}) custom-call(s32[2]{0:T(128)S(1)} %pad_add_fusion.at_ref, s32[12]{0:T(128)S(1)} %subtract_bitcast_fusion.index_ref, bf16[1536,2048]{1,0:T(8,128)(2,1)S(1)} %bitcast.5, bf16[384,384]{1,0:T(8,128)(2,1)S(1)} %constant_dynamic-update-slice_fusion.refs_0_, ...), custom_call_target="tpu_custom_call" | custom-call | flops 603979776 | bytes 1572864 | tf_op jit(solution)/shard_map/pallas_call | solution.py:29
  164.5 1.9 collective-permute-start.39
  166.4 1.3 shard_map.90
  168.1 2.0 shard_map.89
  170.1 5.9 %collective-permute-done.39 = bf16[384,512]{1,0:T(8,128)(2,1)S(1)} collective-permute-done((bf16[384,512]{1,0:T(8,128)(2,1)S(1)}, bf16[384,512]{1,0:T(8,128)(2,1)S(1)}, u32[]{:S(2)}, u32[]{:S(2)}) %collective-permute-start.39) | collective-permute-done | bytes 393248 | tf_op jit(solution)/shard_map/ppermute | solution.py:46
  176.2 4.2 %collective-permute-start.40 = (bf16[384,512]{1,0:T(8,128)(2,1)S(1)}, bf16[384,512]{1,0:T(8,128)(2,1)S(1)}, u32[]{:S(2)}, u32[]{:S(2)}) collective-permute-start(bf16[384,512]{1,0:T(8,128)(2,1)S(1)} %add_convert_fusion.1), channel_id=1, source_target_pairs={{0,3},{1,0},{2,1},{3,2},{4,7},{5,4},{6,5},{7,6},{8,11},{9,8},{10,9... | collective-permute-start | bytes 1179656 | tf_op jit(solution)/shard_map/ppermute | solution.py:46
  180.4 4.4 %collective-permute-done.41 = bf16[384,512]{1,0:T(8,128)(2,1)S(1)} collective-permute-done((bf16[384,512]{1,0:T(8,128)(2,1)S(1)}, bf16[384,512]{1,0:T(8,128)(2,1)S(1)}, u32[]{:S(2)}, u32[]{:S(2)}) %collective-permute-start.41) | collective-permute-done | bytes 393248 | tf_op jit(solution)/shard_map/ppermute | solution.py:46
  184.8 8.0 %collective-permute-done.40 = bf16[384,512]{1,0:T(8,128)(2,1)S(1)} collective-permute-done((bf16[384,512]{1,0:T(8,128)(2,1)S(1)}, bf16[384,512]{1,0:T(8,128)(2,1)S(1)}, u32[]{:S(2)}, u32[]{:S(2)}) %collective-permute-start.40) | collective-permute-done | bytes 393248 | tf_op jit(solution)/shard_map/ppermute | solution.py:46
  193.5 3.3 %collective-permute-start.44 = (bf16[384,512]{1,0:T(8,128)(2,1)S(1)}, bf16[384,512]{1,0:T(8,128)(2,1)S(1)}, u32[]{:S(2)}, u32[]{:S(2)}) collective-permute-start(bf16[384,512]{1,0:T(8,128)(2,1)S(1)} %add_convert_fusion.refs_0_), channel_id=1, source_target_pairs={{0,3},{1,0},{2,1},{3,2},{4,7},{5,4},{6,5},{7,6},{8,11},{9,8},{10,9... | collective-permute-start | bytes 1179656 | tf_op jit(solution)/shard_map/ppermute | solution.py:46
  196.8 10.0 %collective-permute-done.42.refs_1_ = bf16[384,512]{1,0:T(8,128)(2,1)S(1)} collective-permute-done((bf16[384,512]{1,0:T(8,128)(2,1)S(1)}, bf16[384,512]{1,0:T(8,128)(2,1)S(1)}, u32[]{:S(2)}, u32[]{:S(2)}) %collective-permute-start.42) | collective-permute-done | bytes 393248 | tf_op jit(solution)/shard_map/ppermute | solution.py:46
  206.8 5.9 %collective-permute-done.44.refs_2_ = bf16[384,512]{1,0:T(8,128)(2,1)S(1)} collective-permute-done((bf16[384,512]{1,0:T(8,128)(2,1)S(1)}, bf16[384,512]{1,0:T(8,128)(2,1)S(1)}, u32[]{:S(2)}, u32[]{:S(2)}) %collective-permute-start.44) | collective-permute-done | bytes 393248 | tf_op jit(solution)/shard_map/ppermute | solution.py:46
  212.7 1.5 shard_map.91.refs_1_
  214.2 8.5 %collective-permute-done.43.refs_0_ = bf16[384,512]{1,0:T(8,128)(2,1)S(1)} collective-permute-done((bf16[384,512]{1,0:T(8,128)(2,1)S(1)}, bf16[384,512]{1,0:T(8,128)(2,1)S(1)}, u32[]{:S(2)}, u32[]{:S(2)}) %collective-permute-start.43) | collective-permute-done | bytes 393248 | tf_op jit(solution)/shard_map/ppermute | solution.py:46
  222.7 1.9 shard_map.92
  (76 shorter events, 6.7 us)
Async XLA Ops:
  0.6 15.3 %collective-permute-start = (bf16[512,384]{1,0:T(8,128)(2,1)}, bf16[512,384]{1,0:T(8,128)(2,1)S(1)}, u32[]{:S(2)}, u32[]{:S(2)}) collective-permute-start(bf16[512,384]{1,0:T(8,128)(2,1)} %refs_0_.1), channel_id=1, source_target_pairs={{0,1},{1,2},{2,3},{3,0},{4,5},{5,6},{6,7},{7,4},{8,9},{9,10},{10,1... | collective-permute-start | bytes 1179656 | tf_op jit(solution)/shard_map/ppermute | solution.py:46
  3.7 19.4 %collective-permute-start.2 = (bf16[512,384]{1,0:T(8,128)(2,1)}, bf16[512,384]{1,0:T(8,128)(2,1)S(1)}, u32[]{:S(2)}, u32[]{:S(2)}) collective-permute-start(bf16[512,384]{1,0:T(8,128)(2,1)} %refs_0_.1), channel_id=1, source_target_pairs={{0,3},{1,0},{2,1},{3,2},{4,7},{5,4},{6,5},{7,6},{8,11},{9,8},{10,9... | collective-permute-start | bytes 1179656 | tf_op jit(solution)/shard_map/ppermute | solution.py:46
  15.9 16.0 %collective-permute-start.1 = (bf16[512,384]{1,0:T(8,128)(2,1)S(1)}, bf16[512,384]{1,0:T(8,128)(2,1)S(1)}, u32[]{:S(2)}, u32[]{:S(2)}) collective-permute-start(bf16[512,384]{1,0:T(8,128)(2,1)S(1)} %collective-permute-done.refs_1_), channel_id=1, source_target_pairs={{0,1},{1,2},{2,3},{3,0},{4,5},{5,6},{6,7},{7,4},{8,9},{9,10},{10,1... | collective-permute-start | bytes 1179656 | tf_op jit(solution)/shard_map/ppermute | solution.py:46
  23.1 1.6 copy-start.1
  24.7 1.0 copy-start.3
  25.7 29.8 %slice-start = ((s8[6291456]{0:T(1024)(128)(4,1)}), s8[2097152]{0:T(1024)(128)(4,1)S(1)}, s32[]{:S(2)}) async-start(s8[6291456]{0:T(1024)(128)(4,1)} %bitcast.4), calls=%async_computation | async-start | bytes 4194304
  32.0 0.7 copy-start.4
  32.7 1.0 copy-start.5
  33.7 15.0 %copy-start.6 = (s32[1,12]{1,0:T(1,128)S(1)}, s32[1,12]{1,0:T(1,128)}, u32[]{:S(2)}) copy-start(s32[1,12]{1,0:T(1,128)} %param.11) | copy-start | bytes 148
  34.7 14.0 %collective-permute-start.3 = (bf16[512,384]{1,0:T(8,128)(2,1)S(1)}, bf16[512,384]{1,0:T(8,128)(2,1)}, u32[]{:S(2)}, u32[]{:S(2)}) collective-permute-start(bf16[512,384]{1,0:T(8,128)(2,1)S(1)} %get-tuple-element.18.refs_0_), channel_id=1, source_target_pairs={{0,1},{1,2},{2,3},{3,0},{4,5},{5,6},{6,7},{7,4},{8,9},{9,10},{10,1... | collective-permute-start | bytes 1179656 | tf_op jit(solution)/shard_map/ppermute | solution.py:46
  34.7 20.7 %collective-permute-start.5 = (bf16[512,384]{1,0:T(8,128)(2,1)S(1)}, bf16[512,384]{1,0:T(8,128)(2,1)}, u32[]{:S(2)}, u32[]{:S(2)}) collective-permute-start(bf16[512,384]{1,0:T(8,128)(2,1)S(1)} %get-tuple-element.18.refs_0_), channel_id=1, source_target_pairs={{0,3},{1,0},{2,1},{3,2},{4,7},{5,4},{6,5},{7,6},{8,11},{9,8},{10,9... | collective-permute-start | bytes 1179656 | tf_op jit(solution)/shard_map/ppermute | solution.py:46
  48.7 13.5 %collective-permute-start.4 = (bf16[512,384]{1,0:T(8,128)(2,1)}, bf16[512,384]{1,0:T(8,128)(2,1)S(1)}, u32[]{:S(2)}, u32[]{:S(2)}) collective-permute-start(bf16[512,384]{1,0:T(8,128)(2,1)} %collective-permute-done.3.refs_1_), channel_id=1, source_target_pairs={{0,1},{1,2},{2,3},{3,0},{4,5},{5,6},{6,7},{7,4},{8,9},{9,10},{10,1... | collective-permute-start | bytes 1179656 | tf_op jit(solution)/shard_map/ppermute | solution.py:46
  48.7 2.8 %copy-start = (bf16[1536,2048]{1,0:T(8,128)(2,1)S(1)}, bf16[1536,2048]{1,0:T(8,128)(2,1)}, u32[]{:S(2)}) copy-start(bf16[1536,2048]{1,0:T(8,128)(2,1)} %a_ref.17) | copy-start | bytes 18874372
  51.5 4.0 %slice-start.1 = ((s8[6291456]{0:T(1024)(128)(4,1)}), s8[4194304]{0:T(1024)(128)(4,1)S(1)}, s32[]{:S(2)}) async-start(s8[6291456]{0:T(1024)(128)(4,1)} %bitcast.4), calls=%async_computation.1 | async-start | bytes 8388608
  64.6 2.9 %collective-permute-start.6 = (bf16[1536,384]{1,0:T(8,128)(2,1)S(1)}, bf16[1536,384]{1,0:T(8,128)(2,1)S(1)}, u32[]{:S(2)}, u32[]{:S(2)}) collective-permute-start(bf16[1536,384]{1,0:T(8,128)(2,1)S(1)} %get-tuple-element.22), channel_id=1, source_target_pairs={{0,4},{4,0},{8,12},{12,8},{16,20},{20,16},{24,28},{28,24},{1,5},{5... | collective-permute-start | bytes 3538952 | tf_op jit(solution)/shard_map/ppermute | solution.py:50
  67.6 6.0 %collective-permute-start.7 = (bf16[192,384]{1,0:T(8,128)(2,1)S(1)}, bf16[192,384]{1,0:T(8,128)(2,1)S(1)}, u32[]{:S(2)}, u32[]{:S(2)}) collective-permute-start(bf16[192,384]{1,0:T(8,128)(2,1)S(1)} %get-tuple-element.23), channel_id=1, source_target_pairs={{0,8},{4,12},{8,0},{12,4},{16,24},{20,28},{24,16},{28,20},{1,9},{5... | collective-permute-start | bytes 442376 | tf_op jit(solution)/shard_map/ppermute | solution.py:50
  69.2 5.6 %collective-permute-start.8 = (bf16[192,384]{1,0:T(8,128)(2,1)S(1)}, bf16[192,384]{1,0:T(8,128)(2,1)S(1)}, u32[]{:S(2)}, u32[]{:S(2)}) collective-permute-start(bf16[192,384]{1,0:T(8,128)(2,1)S(1)} %get-tuple-element.24), channel_id=1, source_target_pairs={{0,16},{4,20},{8,24},{12,28},{16,0},{20,4},{24,8},{28,12},{1,17},{... | collective-permute-start | bytes 442376 | tf_op jit(solution)/shard_map/ppermute | solution.py:50
  75.0 8.0 %collective-permute-start.9 = (bf16[384,384]{1,0:T(8,128)(2,1)S(1)}, bf16[384,384]{1,0:T(8,128)(2,1)S(1)}, u32[]{:S(2)}, u32[]{:S(2)}) collective-permute-start(bf16[384,384]{1,0:T(8,128)(2,1)S(1)} %get-tuple-element.25), channel_id=1, source_target_pairs={{0,8},{4,12},{8,0},{12,4},{16,24},{20,28},{24,16},{28,20},{1,9},{5... | collective-permute-start | bytes 884744 | tf_op jit(solution)/shard_map/ppermute | solution.py:50
  75.6 7.7 %collective-permute-start.10 = (bf16[384,384]{1,0:T(8,128)(2,1)S(1)}, bf16[384,384]{1,0:T(8,128)(2,1)S(1)}, u32[]{:S(2)}, u32[]{:S(2)}) collective-permute-start(bf16[384,384]{1,0:T(8,128)(2,1)S(1)} %get-tuple-element.26), channel_id=1, source_target_pairs={{0,16},{4,20},{8,24},{12,28},{16,0},{20,4},{24,8},{28,12},{1,17},{... | collective-permute-start | bytes 884744 | tf_op jit(solution)/shard_map/ppermute | solution.py:50
  83.4 6.8 %collective-permute-start.12 = (bf16[384,384]{1,0:T(8,128)(2,1)S(1)}, bf16[384,384]{1,0:T(8,128)(2,1)S(1)}, u32[]{:S(2)}, u32[]{:S(2)}) collective-permute-start(bf16[384,384]{1,0:T(8,128)(2,1)S(1)} %shard_map.84.refs_0_), channel_id=1, source_target_pairs={{0,16},{4,20},{8,24},{12,28},{16,0},{20,4},{24,8},{28,12},{1,17},{... | collective-permute-start | bytes 884744 | tf_op jit(solution)/shard_map/ppermute | solution.py:50
  85.0 8.3 %collective-permute-start.11 = (bf16[384,384]{1,0:T(8,128)(2,1)S(1)}, bf16[384,384]{1,0:T(8,128)(2,1)S(1)}, u32[]{:S(2)}, u32[]{:S(2)}) collective-permute-start(bf16[384,384]{1,0:T(8,128)(2,1)S(1)} %shard_map.84.refs_0_), channel_id=1, source_target_pairs={{0,8},{4,12},{8,0},{12,4},{16,24},{20,28},{24,16},{28,20},{1,9},{5... | collective-permute-start | bytes 884744 | tf_op jit(solution)/shard_map/ppermute | solution.py:50
  86.4 12.1 %collective-permute-start.15 = (bf16[384,384]{1,0:T(8,128)(2,1)S(1)}, bf16[384,384]{1,0:T(8,128)(2,1)S(1)}, u32[]{:S(2)}, u32[]{:S(2)}) collective-permute-start(bf16[384,384]{1,0:T(8,128)(2,1)S(1)} %shard_map.84.refs_0_), channel_id=1, source_target_pairs={{0,4},{4,0},{8,12},{12,8},{16,20},{20,16},{24,28},{28,24},{1,5},{5... | collective-permute-start | bytes 884744 | tf_op jit(solution)/shard_map/ppermute | solution.py:50
  90.3 5.2 %collective-permute-start.13 = (bf16[192,384]{1,0:T(8,128)(2,1)S(1)}, bf16[192,384]{1,0:T(8,128)(2,1)S(1)}, u32[]{:S(2)}, u32[]{:S(2)}) collective-permute-start(bf16[192,384]{1,0:T(8,128)(2,1)S(1)} %slice.32), channel_id=1, source_target_pairs={{0,8},{4,12},{8,0},{12,4},{16,24},{20,28},{24,16},{28,20},{1,9},{5... | collective-permute-start | bytes 442376 | tf_op jit(solution)/shard_map/ppermute | solution.py:50
  93.3 5.2 %collective-permute-start.14 = (bf16[192,384]{1,0:T(8,128)(2,1)S(1)}, bf16[192,384]{1,0:T(8,128)(2,1)S(1)}, u32[]{:S(2)}, u32[]{:S(2)}) collective-permute-start(bf16[192,384]{1,0:T(8,128)(2,1)S(1)} %slice.33), channel_id=1, source_target_pairs={{0,16},{4,20},{8,24},{12,28},{16,0},{20,4},{24,8},{28,12},{1,17},{... | collective-permute-start | bytes 442376 | tf_op jit(solution)/shard_map/ppermute | solution.py:50
  93.4 6.5 %collective-permute-start.17 = (bf16[384,384]{1,0:T(8,128)(2,1)S(1)}, bf16[384,384]{1,0:T(8,128)(2,1)S(1)}, u32[]{:S(2)}, u32[]{:S(2)}) collective-permute-start(bf16[384,384]{1,0:T(8,128)(2,1)S(1)} %collective-permute-done.12.refs_2_), channel_id=1, source_target_pairs={{0,4},{4,0},{8,12},{12,8},{16,20},{20,16},{24,28},{28,24},{1,5},{5... | collective-permute-start | bytes 884744 | tf_op jit(solution)/shard_map/ppermute | solution.py:50
  93.5 6.4 %collective-permute-start.16 = (bf16[384,384]{1,0:T(8,128)(2,1)S(1)}, bf16[384,384]{1,0:T(8,128)(2,1)S(1)}, u32[]{:S(2)}, u32[]{:S(2)}) collective-permute-start(bf16[384,384]{1,0:T(8,128)(2,1)S(1)} %collective-permute-done.11.refs_1_), channel_id=1, source_target_pairs={{0,4},{4,0},{8,12},{12,8},{16,20},{20,16},{24,28},{28,24},{1,5},{5... | collective-permute-start | bytes 884744 | tf_op jit(solution)/shard_map/ppermute | solution.py:50
  95.5 3.1 %collective-permute-start.18 = (bf16[192,384]{1,0:T(8,128)(2,1)S(1)}, bf16[192,384]{1,0:T(8,128)(2,1)S(1)}, u32[]{:S(2)}, u32[]{:S(2)}) collective-permute-start(bf16[192,384]{1,0:T(8,128)(2,1)S(1)} %collective-permute-done.13.refs_3_), channel_id=1, source_target_pairs={{0,4},{4,0},{8,12},{12,8},{16,20},{20,16},{24,28},{28,24},{1,5},{5... | collective-permute-start | bytes 442376 | tf_op jit(solution)/shard_map/ppermute | solution.py:50
  98.6 1.4 collective-permute-start.19
  103.6 16.0 %collective-permute-start.20 = (bf16[384,384]{1,0:T(8,128)(2,1)S(1)}, bf16[384,384]{1,0:T(8,128)(2,1)S(1)}, u32[]{:S(2)}, u32[]{:S(2)}) collective-permute-start(bf16[384,384]{1,0:T(8,128)(2,1)S(1)} %shard_map.86), channel_id=1, source_target_pairs={{0,3},{1,0},{2,1},{3,2},{4,7},{5,4},{6,5},{7,6},{8,11},{9,8},{10,9... | collective-permute-start | bytes 884744 | tf_op jit(solution)/shard_map/ppermute | solution.py:46
  107.4 12.4 %collective-permute-start.22 = (bf16[384,384]{1,0:T(8,128)(2,1)S(1)}, bf16[384,384]{1,0:T(8,128)(2,1)S(1)}, u32[]{:S(2)}, u32[]{:S(2)}) collective-permute-start(bf16[384,384]{1,0:T(8,128)(2,1)S(1)} %shard_map.87), channel_id=1, source_target_pairs={{0,1},{1,2},{2,3},{3,0},{4,5},{5,6},{6,7},{7,4},{8,9},{9,10},{10,1... | collective-permute-start | bytes 884744 | tf_op jit(solution)/shard_map/ppermute | solution.py:46
  119.7 6.8 %collective-permute-start.21 = (bf16[384,384]{1,0:T(8,128)(2,1)S(1)}, bf16[384,384]{1,0:T(8,128)(2,1)S(1)}, u32[]{:S(2)}, u32[]{:S(2)}) collective-permute-start(bf16[384,384]{1,0:T(8,128)(2,1)S(1)} %add_convert_fusion.2), channel_id=1, source_target_pairs={{0,3},{1,0},{2,1},{3,2},{4,7},{5,4},{6,5},{7,6},{8,11},{9,8},{10,9... | collective-permute-start | bytes 884744 | tf_op jit(solution)/shard_map/ppermute | solution.py:46
  127.4 5.4 %collective-permute-start.28 = (bf16[96,384]{1,0:T(8,128)(2,1)S(1)}, bf16[96,384]{1,0:T(8,128)(2,1)S(1)}, u32[]{:S(2)}, u32[]{:S(2)}) collective-permute-start(bf16[96,384]{1,0:T(8,128)(2,1)S(1)} %get-tuple-element.36), channel_id=1, source_target_pairs={{0,24},{4,28},{8,16},{12,20},{16,8},{20,12},{24,0},{28,4},{1,25},{... | collective-permute-start | bytes 221192 | tf_op jit(solution)/shard_map/ppermute | solution.py:50
  128.4 8.7 %collective-permute-start.26 = (bf16[96,384]{1,0:T(8,128)(2,1)S(1)}, bf16[96,384]{1,0:T(8,128)(2,1)S(1)}, u32[]{:S(2)}, u32[]{:S(2)}) collective-permute-start(bf16[96,384]{1,0:T(8,128)(2,1)S(1)} %get-tuple-element.37), channel_id=1, source_target_pairs={{0,16},{4,20},{8,24},{12,28},{16,0},{20,4},{24,8},{28,12},{1,17},{... | collective-permute-start | bytes 221192 | tf_op jit(solution)/shard_map/ppermute | solution.py:50
  130.4 6.8 %collective-permute-start.24 = (bf16[96,384]{1,0:T(8,128)(2,1)S(1)}, bf16[96,384]{1,0:T(8,128)(2,1)S(1)}, u32[]{:S(2)}, u32[]{:S(2)}) collective-permute-start(bf16[96,384]{1,0:T(8,128)(2,1)S(1)} %get-tuple-element.38), channel_id=1, source_target_pairs={{0,8},{4,12},{8,0},{12,4},{16,24},{20,28},{24,16},{28,20},{1,9},{5... | collective-permute-start | bytes 221192 | tf_op jit(solution)/shard_map/ppermute | solution.py:50
  131.0 6.2 %collective-permute-start.23 = (bf16[96,384]{1,0:T(8,128)(2,1)S(1)}, bf16[96,384]{1,0:T(8,128)(2,1)S(1)}, u32[]{:S(2)}, u32[]{:S(2)}) collective-permute-start(bf16[96,384]{1,0:T(8,128)(2,1)S(1)} %get-tuple-element.39), channel_id=1, source_target_pairs={{0,0},{1,8},{2,16},{3,24},{4,4},{5,12},{6,20},{7,28},{8,1},{9,9},{... | collective-permute-start | bytes 221192 | tf_op jit(solution)/shard_map/ppermute | solution.py:88
  132.8 8.8 %collective-permute-start.29 = (bf16[96,384]{1,0:T(8,128)(2,1)S(1)}, bf16[96,384]{1,0:T(8,128)(2,1)S(1)}, u32[]{:S(2)}, u32[]{:S(2)}) collective-permute-start(bf16[96,384]{1,0:T(8,128)(2,1)S(1)} %collective-permute-done.28), channel_id=1, source_target_pairs={{0,3},{1,11},{2,19},{3,27},{4,7},{5,15},{6,23},{7,31},{8,2},{9,10}... | collective-permute-start | bytes 221192 | tf_op jit(solution)/shard_map/ppermute | solution.py:88
  137.1 4.4 %collective-permute-start.27 = (bf16[96,384]{1,0:T(8,128)(2,1)S(1)}, bf16[96,384]{1,0:T(8,128)(2,1)S(1)}, u32[]{:S(2)}, u32[]{:S(2)}) collective-permute-start(bf16[96,384]{1,0:T(8,128)(2,1)S(1)} %collective-permute-done.26), channel_id=1, source_target_pairs={{0,2},{1,10},{2,18},{3,26},{4,6},{5,14},{6,22},{7,30},{8,3},{9,11}... | collective-permute-start | bytes 221192 | tf_op jit(solution)/shard_map/ppermute | solution.py:88
  137.1 4.4 %collective-permute-start.25 = (bf16[96,384]{1,0:T(8,128)(2,1)S(1)}, bf16[96,384]{1,0:T(8,128)(2,1)S(1)}, u32[]{:S(2)}, u32[]{:S(2)}) collective-permute-start(bf16[96,384]{1,0:T(8,128)(2,1)S(1)} %collective-permute-done.24), channel_id=1, source_target_pairs={{0,1},{1,9},{2,17},{3,25},{4,5},{5,13},{6,21},{7,29},{8,0},{9,8},{... | collective-permute-start | bytes 221192 | tf_op jit(solution)/shard_map/ppermute | solution.py:88
  141.6 10.8 %collective-permute-start.31 = (bf16[384,384]{1,0:T(8,128)(2,1)S(1)}, bf16[384,384]{1,0:T(8,128)(2,1)S(1)}, u32[]{:S(2)}, u32[]{:S(2)}) collective-permute-start(bf16[384,384]{1,0:T(8,128)(2,1)S(1)} %constant_dynamic-update-slice_fusion.refs_0_), channel_id=1, source_target_pairs={{0,16},{4,20},{8,24},{12,28},{16,0},{20,4},{24,8},{28,12},{1,17},{... | collective-permute-start | bytes 884744 | tf_op jit(solution)/shard_map/ppermute | solution.py:50
  146.9 8.2 %collective-permute-start.30 = (bf16[384,384]{1,0:T(8,128)(2,1)S(1)}, bf16[384,384]{1,0:T(8,128)(2,1)S(1)}, u32[]{:S(2)}, u32[]{:S(2)}) collective-permute-start(bf16[384,384]{1,0:T(8,128)(2,1)S(1)} %constant_dynamic-update-slice_fusion.refs_0_), channel_id=1, source_target_pairs={{0,8},{4,12},{8,0},{12,4},{16,24},{20,28},{24,16},{28,20},{1,9},{5... | collective-permute-start | bytes 884744 | tf_op jit(solution)/shard_map/ppermute | solution.py:50
  146.9 13.4 %collective-permute-start.34 = (bf16[384,384]{1,0:T(8,128)(2,1)S(1)}, bf16[384,384]{1,0:T(8,128)(2,1)S(1)}, u32[]{:S(2)}, u32[]{:S(2)}) collective-permute-start(bf16[384,384]{1,0:T(8,128)(2,1)S(1)} %constant_dynamic-update-slice_fusion.refs_0_), channel_id=1, source_target_pairs={{0,4},{4,0},{8,12},{12,8},{16,20},{20,16},{24,28},{28,24},{1,5},{5... | collective-permute-start | bytes 884744 | tf_op jit(solution)/shard_map/ppermute | solution.py:50
  152.5 5.2 %collective-permute-start.32 = (bf16[192,384]{1,0:T(8,128)(2,1)S(1)}, bf16[192,384]{1,0:T(8,128)(2,1)S(1)}, u32[]{:S(2)}, u32[]{:S(2)}) collective-permute-start(bf16[192,384]{1,0:T(8,128)(2,1)S(1)} %slice.38), channel_id=1, source_target_pairs={{0,8},{4,12},{8,0},{12,4},{16,24},{20,28},{24,16},{28,20},{1,9},{5... | collective-permute-start | bytes 442376 | tf_op jit(solution)/shard_map/ppermute | solution.py:50
  155.1 5.2 %collective-permute-start.33 = (bf16[192,384]{1,0:T(8,128)(2,1)S(1)}, bf16[192,384]{1,0:T(8,128)(2,1)S(1)}, u32[]{:S(2)}, u32[]{:S(2)}) collective-permute-start(bf16[192,384]{1,0:T(8,128)(2,1)S(1)} %slice.39), channel_id=1, source_target_pairs={{0,16},{4,20},{8,24},{12,28},{16,0},{20,4},{24,8},{28,12},{1,17},{... | collective-permute-start | bytes 442376 | tf_op jit(solution)/shard_map/ppermute | solution.py:50
  155.3 6.4 %collective-permute-start.36 = (bf16[384,384]{1,0:T(8,128)(2,1)S(1)}, bf16[384,384]{1,0:T(8,128)(2,1)S(1)}, u32[]{:S(2)}, u32[]{:S(2)}) collective-permute-start(bf16[384,384]{1,0:T(8,128)(2,1)S(1)} %collective-permute-done.31.refs_2_), channel_id=1, source_target_pairs={{0,4},{4,0},{8,12},{12,8},{16,20},{20,16},{24,28},{28,24},{1,5},{5... | collective-permute-start | bytes 884744 | tf_op jit(solution)/shard_map/ppermute | solution.py:50
  155.3 6.4 %collective-permute-start.35 = (bf16[384,384]{1,0:T(8,128)(2,1)S(1)}, bf16[384,384]{1,0:T(8,128)(2,1)S(1)}, u32[]{:S(2)}, u32[]{:S(2)}) collective-permute-start(bf16[384,384]{1,0:T(8,128)(2,1)S(1)} %collective-permute-done.30.refs_1_), channel_id=1, source_target_pairs={{0,4},{4,0},{8,12},{12,8},{16,20},{20,16},{24,28},{28,24},{1,5},{5... | collective-permute-start | bytes 884744 | tf_op jit(solution)/shard_map/ppermute | solution.py:50
  157.7 2.6 %collective-permute-start.37 = (bf16[192,384]{1,0:T(8,128)(2,1)S(1)}, bf16[192,384]{1,0:T(8,128)(2,1)S(1)}, u32[]{:S(2)}, u32[]{:S(2)}) collective-permute-start(bf16[192,384]{1,0:T(8,128)(2,1)S(1)} %collective-permute-done.32.refs_3_), channel_id=1, source_target_pairs={{0,4},{4,0},{8,12},{12,8},{16,20},{20,16},{24,28},{28,24},{1,5},{5... | collective-permute-start | bytes 442376 | tf_op jit(solution)/shard_map/ppermute | solution.py:50
  160.3 1.4 collective-permute-start.38
  164.5 11.6 %collective-permute-start.39 = (bf16[384,512]{1,0:T(8,128)(2,1)S(1)}, bf16[384,512]{1,0:T(8,128)(2,1)S(1)}, u32[]{:S(2)}, u32[]{:S(2)}) collective-permute-start(bf16[384,512]{1,0:T(8,128)(2,1)S(1)} %get-tuple-element.31), channel_id=1, source_target_pairs={{0,3},{1,0},{2,1},{3,2},{4,7},{5,4},{6,5},{7,6},{8,11},{9,8},{10,9... | collective-permute-start | bytes 1179656 | tf_op jit(solution)/shard_map/ppermute | solution.py:46
  167.7 17.0 %collective-permute-start.41 = (bf16[384,512]{1,0:T(8,128)(2,1)S(1)}, bf16[384,512]{1,0:T(8,128)(2,1)S(1)}, u32[]{:S(2)}, u32[]{:S(2)}) collective-permute-start(bf16[384,512]{1,0:T(8,128)(2,1)S(1)} %shard_map.90), channel_id=1, source_target_pairs={{0,1},{1,2},{2,3},{3,0},{4,5},{5,6},{6,7},{7,4},{8,9},{9,10},{10,1... | collective-permute-start | bytes 1179656 | tf_op jit(solution)/shard_map/ppermute | solution.py:46
  170.1 42.6 %copy-start.2 = (bf16[512,2048]{1,0:T(8,128)(2,1)S(1)}, bf16[512,2048]{1,0:T(8,128)(2,1)}, u32[]{:S(2)}) copy-start(bf16[512,2048]{1,0:T(8,128)(2,1)} %a_ref.19) | copy-start | bytes 6291460
  176.2 16.6 %collective-permute-start.40 = (bf16[384,512]{1,0:T(8,128)(2,1)S(1)}, bf16[384,512]{1,0:T(8,128)(2,1)S(1)}, u32[]{:S(2)}, u32[]{:S(2)}) collective-permute-start(bf16[384,512]{1,0:T(8,128)(2,1)S(1)} %add_convert_fusion.1), channel_id=1, source_target_pairs={{0,3},{1,0},{2,1},{3,2},{4,7},{5,4},{6,5},{7,6},{8,11},{9,8},{10,9... | collective-permute-start | bytes 1179656 | tf_op jit(solution)/shard_map/ppermute | solution.py:46
  192.9 13.9 %collective-permute-start.42 = (bf16[384,512]{1,0:T(8,128)(2,1)S(1)}, bf16[384,512]{1,0:T(8,128)(2,1)S(1)}, u32[]{:S(2)}, u32[]{:S(2)}) collective-permute-start(bf16[384,512]{1,0:T(8,128)(2,1)S(1)} %add_convert_fusion.refs_0_), channel_id=1, source_target_pairs={{0,1},{1,2},{2,3},{3,0},{4,5},{5,6},{6,7},{7,4},{8,9},{9,10},{10,1... | collective-permute-start | bytes 1179656 | tf_op jit(solution)/shard_map/ppermute | solution.py:46
  193.5 19.2 %collective-permute-start.44 = (bf16[384,512]{1,0:T(8,128)(2,1)S(1)}, bf16[384,512]{1,0:T(8,128)(2,1)S(1)}, u32[]{:S(2)}, u32[]{:S(2)}) collective-permute-start(bf16[384,512]{1,0:T(8,128)(2,1)S(1)} %add_convert_fusion.refs_0_), channel_id=1, source_target_pairs={{0,3},{1,0},{2,1},{3,2},{4,7},{5,4},{6,5},{7,6},{8,11},{9,8},{10,9... | collective-permute-start | bytes 1179656 | tf_op jit(solution)/shard_map/ppermute | solution.py:46
  206.8 15.9 %collective-permute-start.43 = (bf16[384,512]{1,0:T(8,128)(2,1)S(1)}, bf16[384,512]{1,0:T(8,128)(2,1)S(1)}, u32[]{:S(2)}, u32[]{:S(2)}) collective-permute-start(bf16[384,512]{1,0:T(8,128)(2,1)S(1)} %collective-permute-done.42.refs_1_), channel_id=1, source_target_pairs={{0,1},{1,2},{2,3},{3,0},{4,5},{5,6},{6,7},{7,4},{8,9},{9,10},{10,1... | collective-permute-start | bytes 1179656 | tf_op jit(solution)/shard_map/ppermute | solution.py:46

commit v8 on v7

--- a/solution.py
+++ b/solution.py
@@ -473,6 +473,14 @@
             and arrays[2].shape[1] % (n_row * BLK) == 0
             and width % BLK == 0
         )
-        return (solve if fits else solve_plain)(n_front, n_row, *arrays)
+        if not fits:
+            return solve_plain(n_front, n_row, *arrays)
+        cut = width * 2 // 3 // BLK * BLK
+        parts = [
+            solve(n_front, n_row, arrays[0][:, low:high], arrays[1][:, low:high], *arrays[2:])
+            for low, high in ((0, cut), (cut, width))
+            if high > low
+        ]
+        return tuple(jnp.concatenate(outs, axis=1) for outs in zip(*parts))
 
     return jax.shard_map(per_device, mesh=mesh, in_specs=in_specs, out_specs=out_specs, check_vma=False)

time: 225 us -> 272 us (1.21)
  starting transfers between devices: 46.5 us -> 106 us
  waiting for transfers between devices: 134 us -> 98.2 us
  Pallas kernels: 34.1 us -> 53.3 us
  local copies, waits for them, and re-layouts: 7.28 us -> 11.1 us
    ppermute x15 -> x30, starting transfers between devices: 21.6 us -> 47.1 us  [shift(): return lax.ppermute(x, 'row', [(i, (i + by) % size) for i in range(size)])]
    ppermute x15 -> x30, waiting for transfers between devices: 90.4 us -> 66.5 us  [shift(): return lax.ppermute(x, 'row', [(i, (i + by) % size) for i in range(size)])]
    ppermute x26 -> x52, starting transfers between devices: 19.9 us -> 42.8 us  [swap(): return lax.ppermute(x, 'front', [(i, i ^ by) for i in range(size)])]
    pallas_call x16 -> x32, Pallas kernels: 34.1 us -> 53.3 us  [kernel_call(): pl.pallas_call(body, out_shape=out_shape, grid_spec=pltpu.PrefetchScalarG...]
    ppermute x26 -> x52, waiting for transfers between devices: 39.7 us -> 28.8 us  [swap(): return lax.ppermute(x, 'front', [(i, i ^ by) for i in range(size)])]
    ppermute x4 -> x8, starting transfers between devices: 5.01 us -> 15.6 us  [to_plane(): moved.append(lax.ppermute(quarter, ('front', 'row'), perm))]
    slice x0 -> x4, local copies, waits for them, and re-layouts: none -> 6.59 us  [the longest x2 4.57 us: per_device(): arrays[1][:, low:high]]
    unnamed x21 -> x20, local copies, waits for them, and re-layouts: 7.17 us -> 4.43 us
  transfers between devices with their start and end apart: 45 -> 90, of which waited for: 30 -> 39; matrix products, arithmetic and copies ran while one was open for 0% -> 3% of each run, Pallas kernels for 10% -> 18%
where the time goes in v8:
time: 272 us
  starting transfers between devices  106 us (39%)
  waiting for transfers between devices  98.2 us (36%)
  Pallas kernels  53.3 us (20%)
  local copies, waits for them, and re-layouts  11.1 us (4%)
    ppermute x30, waiting for transfers between devices, shift(): return lax.ppermute(x, 'row', [(i, (i + by) % size) for i in range(size)])  66.5 us
    pallas_call x32, Pallas kernels, kernel_call(): pl.pallas_call(body, out_shape=out_shape, grid_spec=pltpu.PrefetchScalarG...  53.3 us
    ppermute x30, starting transfers between devices, shift(): return lax.ppermute(x, 'row', [(i, (i + by) % size) for i in range(size)])  47.1 us
    ppermute x52, starting transfers between devices, swap(): return lax.ppermute(x, 'front', [(i, i ^ by) for i in range(size)])  42.8 us
    ppermute x52, waiting for transfers between devices, swap(): return lax.ppermute(x, 'front', [(i, i ^ by) for i in range(size)])  28.8 us
    ppermute x8, starting transfers between devices, to_plane(): moved.append(lax.ppermute(quarter, ('front', 'row'), perm))  15.6 us
  transfers between devices with their start and end apart: 90, of which 39 were waited for; matrix products, arithmetic and copies ran while one was open for 3% of the time, Pallas kernels for 18%

profile of v8, /device:TPU:0, one launch (start us, length us, event | category | flops | bytes accessed | tf_op | source)
XLA Modules:
  0.0 271.8 jit_solution(14239624343119847931)
XLA Ops:
  1.6 3.1 %collective-permute-start = (bf16[512,256]{1,0:T(8,128)(2,1)S(1)}, bf16[512,256]{1,0:T(8,128)(2,1)S(1)}, u32[]{:S(2)}, u32[]{:S(2)}) collective-permute-start(bf16[512,256]{1,0:T(8,128)(2,1)S(1)} %slice.60.refs_0_), channel_id=1, source_target_pairs={{0,1},{1,2},{2,3},{3,0},{4,5},{5,6},{6,7},{7,4},{8,9},{9,10},{10,1... | collective-permute-start | bytes 786440 | tf_op jit(solution)/shard_map/ppermute | solution.py:46
  4.7 2.1 collective-permute-start.2
  6.8 7.1 %collective-permute-done.refs_1_ = bf16[512,256]{1,0:T(8,128)(2,1)S(1)} collective-permute-done((bf16[512,256]{1,0:T(8,128)(2,1)S(1)}, bf16[512,256]{1,0:T(8,128)(2,1)S(1)}, u32[]{:S(2)}, u32[]{:S(2)}) %collective-permute-start) | collective-permute-done | bytes 262176 | tf_op jit(solution)/shard_map/ppermute | solution.py:46
  14.0 4.3 %collective-permute-done.2.refs_2_ = bf16[512,256]{1,0:T(8,128)(2,1)S(1)} collective-permute-done((bf16[512,256]{1,0:T(8,128)(2,1)S(1)}, bf16[512,256]{1,0:T(8,128)(2,1)S(1)}, u32[]{:S(2)}, u32[]{:S(2)}) %collective-permute-start.2) | collective-permute-done | bytes 262176 | tf_op jit(solution)/shard_map/ppermute | solution.py:46
  18.3 1.6 copy-done.1
  21.0 3.3 %collective-permute-done.1.refs_0_ = bf16[512,256]{1,0:T(8,128)(2,1)S(1)} collective-permute-done((bf16[512,256]{1,0:T(8,128)(2,1)S(1)}, bf16[512,256]{1,0:T(8,128)(2,1)S(1)}, u32[]{:S(2)}, u32[]{:S(2)}) %collective-permute-start.1) | collective-permute-done | bytes 262176 | tf_op jit(solution)/shard_map/ppermute | solution.py:46
  25.2 1.9 slice.61.refs_2_
  27.1 3.8 %collective-permute-start.5 = (bf16[512,256]{1,0:T(8,128)(2,1)S(1)}, bf16[512,256]{1,0:T(8,128)(2,1)S(1)}, u32[]{:S(2)}, u32[]{:S(2)}) collective-permute-start(bf16[512,256]{1,0:T(8,128)(2,1)S(1)} %get-tuple-element.34.refs_0_), channel_id=1, source_target_pairs={{0,3},{1,0},{2,1},{3,2},{4,7},{5,4},{6,5},{7,6},{8,11},{9,8},{10,9... | collective-permute-start | bytes 786440 | tf_op jit(solution)/shard_map/ppermute | solution.py:46
  30.9 5.4 %collective-permute-done.3.refs_1_ = bf16[512,256]{1,0:T(8,128)(2,1)S(1)} collective-permute-done((bf16[512,256]{1,0:T(8,128)(2,1)S(1)}, bf16[512,256]{1,0:T(8,128)(2,1)S(1)}, u32[]{:S(2)}, u32[]{:S(2)}) %collective-permute-start.3) | collective-permute-done | bytes 262176 | tf_op jit(solution)/shard_map/ppermute | solution.py:46
  36.3 2.8 %copy-done = bf16[1536,2048]{1,0:T(8,128)(2,1)S(1)} copy-done((bf16[1536,2048]{1,0:T(8,128)(2,1)S(1)}, bf16[1536,2048]{1,0:T(8,128)(2,1)}, u32[]{:S(2)}) %copy-start) | copy-done | bytes 6291480
  39.1 1.9 shard_map.79
  42.9 1.6 collective-permute-done.4.refs_0_
  44.5 1.8 shard_map.81
  47.5 3.8 %collective-permute-start.47 = (bf16[512,128]{1,0:T(8,128)(2,1)S(1)}, bf16[512,128]{1,0:T(8,128)(2,1)S(1)}, u32[]{:S(2)}, u32[]{:S(2)}) collective-permute-start(bf16[512,128]{1,0:T(8,128)(2,1)S(1)} %slice.70.refs_0_), channel_id=1, source_target_pairs={{0,3},{1,0},{2,1},{3,2},{4,7},{5,4},{6,5},{7,6},{8,11},{9,8},{10,9... | collective-permute-start | bytes 393224 | tf_op jit(solution)/shard_map/ppermute | solution.py:46
  51.3 4.3 %collective-permute-done.45.refs_1_ = bf16[512,128]{1,0:T(8,128)(2,1)S(1)} collective-permute-done((bf16[512,128]{1,0:T(8,128)(2,1)S(1)}, bf16[512,128]{1,0:T(8,128)(2,1)S(1)}, u32[]{:S(2)}, u32[]{:S(2)}) %collective-permute-start.45) | collective-permute-done | bytes 131104 | tf_op jit(solution)/shard_map/ppermute | solution.py:46
  57.2 5.2 %collective-permute-done.46.refs_0_ = bf16[512,128]{1,0:T(8,128)(2,1)S(1)} collective-permute-done((bf16[512,128]{1,0:T(8,128)(2,1)S(1)}, bf16[512,128]{1,0:T(8,128)(2,1)S(1)}, u32[]{:S(2)}, u32[]{:S(2)}) %collective-permute-start.46) | collective-permute-done | bytes 131104 | tf_op jit(solution)/shard_map/ppermute | solution.py:46
  63.3 3.8 %collective-permute-start.50 = (bf16[512,128]{1,0:T(8,128)(2,1)S(1)}, bf16[512,128]{1,0:T(8,128)(2,1)S(1)}, u32[]{:S(2)}, u32[]{:S(2)}) collective-permute-start(bf16[512,128]{1,0:T(8,128)(2,1)S(1)} %get-tuple-element.50.refs_0_), channel_id=1, source_target_pairs={{0,3},{1,0},{2,1},{3,2},{4,7},{5,4},{6,5},{7,6},{8,11},{9,8},{10,9... | collective-permute-start | bytes 393224 | tf_op jit(solution)/shard_map/ppermute | solution.py:46
  67.1 2.9 %collective-permute-done.48.refs_1_ = bf16[512,128]{1,0:T(8,128)(2,1)S(1)} collective-permute-done((bf16[512,128]{1,0:T(8,128)(2,1)S(1)}, bf16[512,128]{1,0:T(8,128)(2,1)S(1)}, u32[]{:S(2)}, u32[]{:S(2)}) %collective-permute-start.48) | collective-permute-done | bytes 131104 | tf_op jit(solution)/shard_map/ppermute | solution.py:46
  70.1 2.6 slice.71.refs_2_
  72.7 1.9 shard_map.95
  76.8 1.7 shard_map.97
  81.8 2.2 collective-permute-done.7.low_ref
  89.5 4.3 %collective-permute-done.52.low_ref = bf16[192,128]{1,0:T(8,128)(2,1)S(1)} collective-permute-done((bf16[192,128]{1,0:T(8,128)(2,1)S(1)}, bf16[192,128]{1,0:T(8,128)(2,1)S(1)}, u32[]{:S(2)}, u32[]{:S(2)}) %collective-permute-start.52) | collective-permute-done | bytes 49184 | tf_op jit(solution)/shard_map/ppermute | solution.py:50
  102.4 2.4 collective-permute-done.57.refs_2_
  107.1 1.8 collective-permute-done.58.refs_3_
  114.8 1.9 collective-permute-done.13.refs_3_
  117.8 3.1 %shard_map.102 = bf16[384,128]{1,0:T(8,128)(2,1)S(1)} custom-call(s32[2]{0:T(128)S(1)} %pad_add_fusion.at_ref, bf16[384,128]{1,0:T(8,128)(2,1)S(1)} %shard_map.100.refs_0_, bf16[384,128]{1,0:T(8,128)(2,1)S(1)} %collective-permute-done.56.refs_1_, bf16[384,128]{1,0:T(8,128)(2,1)S(1)} %collective-permute-done.57.refs_2_, ...), custom_call_target="tpu_custom_call" | custom-call | flops 301989888 | bytes 2359296 | tf_op jit(solution)/shard_map/pallas_call | solution.py:29
  120.9 3.1 %collective-permute-start.65 = (bf16[384,128]{1,0:T(8,128)(2,1)S(1)}, bf16[384,128]{1,0:T(8,128)(2,1)S(1)}, u32[]{:S(2)}, u32[]{:S(2)}) collective-permute-start(bf16[384,128]{1,0:T(8,128)(2,1)S(1)} %shard_map.102), channel_id=1, source_target_pairs={{0,3},{1,0},{2,1},{3,2},{4,7},{5,4},{6,5},{7,6},{8,11},{9,8},{10,9... | collective-permute-start | bytes 294920 | tf_op jit(solution)/shard_map/ppermute | solution.py:46
  124.0 5.0 %shard_map.101 = (f32[384,128]{1,0:T(8,128)S(1)}, f32[384,128]{1,0:T(8,128)S(1)}) custom-call(s32[2]{0:T(128)S(1)} %pad_add_fusion.at_ref, bf16[384,128]{1,0:T(8,128)(2,1)S(1)} %shard_map.100.refs_0_, bf16[384,128]{1,0:T(8,128)(2,1)S(1)} %collective-permute-done.56.refs_1_, bf16[384,128]{1,0:T(8,128)(2,1)S(1)} %collective-permute-done.57.refs_2_, ...), custom_call_target="tpu_custom_call" | custom-call | flops 603979776 | bytes 4718592 | tf_op jit(solution)/shard_map/pallas_call | solution.py:29
  129.1 3.1 %shard_map.103 = bf16[384,128]{1,0:T(8,128)(2,1)S(1)} custom-call(s32[2]{0:T(128)S(1)} %pad_add_fusion.at_ref, bf16[384,128]{1,0:T(8,128)(2,1)S(1)} %shard_map.100.refs_0_, bf16[384,128]{1,0:T(8,128)(2,1)S(1)} %collective-permute-done.56.refs_1_, bf16[384,128]{1,0:T(8,128)(2,1)S(1)} %collective-permute-done.57.refs_2_, ...), custom_call_target="tpu_custom_call" | custom-call | flops 301989888 | bytes 2359296 | tf_op jit(solution)/shard_map/pallas_call | solution.py:29
  132.3 3.6 %shard_map.86 = bf16[384,256]{1,0:T(8,128)(2,1)S(1)} custom-call(s32[2]{0:T(128)S(1)} %pad_add_fusion.at_ref, bf16[384,256]{1,0:T(8,128)(2,1)S(1)} %shard_map.84.refs_0_, bf16[384,256]{1,0:T(8,128)(2,1)S(1)} %collective-permute-done.11.refs_1_, bf16[384,256]{1,0:T(8,128)(2,1)S(1)} %collective-permute-done.12.refs_2_, ...), custom_call_target="tpu_custom_call" | custom-call | flops 603979776 | bytes 2359296 | tf_op jit(solution)/shard_map/pallas_call | solution.py:29
  135.9 3.8 %collective-permute-start.20 = (bf16[384,256]{1,0:T(8,128)(2,1)S(1)}, bf16[384,256]{1,0:T(8,128)(2,1)S(1)}, u32[]{:S(2)}, u32[]{:S(2)}) collective-permute-start(bf16[384,256]{1,0:T(8,128)(2,1)S(1)} %shard_map.86), channel_id=1, source_target_pairs={{0,3},{1,0},{2,1},{3,2},{4,7},{5,4},{6,5},{7,6},{8,11},{9,8},{10,9... | collective-permute-start | bytes 589832 | tf_op jit(solution)/shard_map/ppermute | solution.py:46
  139.9 3.6 %shard_map.87 = bf16[384,256]{1,0:T(8,128)(2,1)S(1)} custom-call(s32[2]{0:T(128)S(1)} %pad_add_fusion.at_ref, bf16[384,256]{1,0:T(8,128)(2,1)S(1)} %shard_map.84.refs_0_, bf16[384,256]{1,0:T(8,128)(2,1)S(1)} %collective-permute-done.11.refs_1_, bf16[384,256]{1,0:T(8,128)(2,1)S(1)} %collective-permute-done.12.refs_2_, ...), custom_call_target="tpu_custom_call" | custom-call | flops 603979776 | bytes 2359296 | tf_op jit(solution)/shard_map/pallas_call | solution.py:29
  143.5 2.2 collective-permute-start.22
  145.8 5.9 %shard_map.85 = (f32[384,256]{1,0:T(8,128)S(1)}, f32[384,256]{1,0:T(8,128)S(1)}) custom-call(s32[2]{0:T(128)S(1)} %pad_add_fusion.at_ref, bf16[384,256]{1,0:T(8,128)(2,1)S(1)} %shard_map.84.refs_0_, bf16[384,256]{1,0:T(8,128)(2,1)S(1)} %collective-permute-done.11.refs_1_, bf16[384,256]{1,0:T(8,128)(2,1)S(1)} %collective-permute-done.12.refs_2_, ...), custom_call_target="tpu_custom_call" | custom-call | flops 1207959552 | bytes 4718592 | tf_op jit(solution)/shard_map/pallas_call | solution.py:29
  151.7 1.9 collective-permute-start.21
  153.6 4.0 %collective-permute-done.21 = bf16[384,256]{1,0:T(8,128)(2,1)S(1)} collective-permute-done((bf16[384,256]{1,0:T(8,128)(2,1)S(1)}, bf16[384,256]{1,0:T(8,128)(2,1)S(1)}, u32[]{:S(2)}, u32[]{:S(2)}) %collective-permute-start.21) | collective-permute-done | bytes 196640 | tf_op jit(solution)/shard_map/ppermute | solution.py:46
  158.4 3.1 %collective-permute-start.24 = (bf16[96,256]{1,0:T(8,128)(2,1)S(1)}, bf16[96,256]{1,0:T(8,128)(2,1)S(1)}, u32[]{:S(2)}, u32[]{:S(2)}) collective-permute-start(bf16[96,256]{1,0:T(8,128)(2,1)S(1)} %get-tuple-element.72), channel_id=1, source_target_pairs={{0,8},{4,12},{8,0},{12,4},{16,24},{20,28},{24,16},{28,20},{1,9},{5... | collective-permute-start | bytes 147464 | tf_op jit(solution)/shard_map/ppermute | solution.py:50
  162.2 3.2 %collective-permute-start.69 = (bf16[96,128]{1,0:T(8,128)(2,1)S(1)}, bf16[96,128]{1,0:T(8,128)(2,1)S(1)}, u32[]{:S(2)}, u32[]{:S(2)}) collective-permute-start(bf16[96,128]{1,0:T(8,128)(2,1)S(1)} %get-tuple-element.76), channel_id=1, source_target_pairs={{0,8},{4,12},{8,0},{12,4},{16,24},{20,28},{24,16},{28,20},{1,9},{5... | collective-permute-start | bytes 73736 | tf_op jit(solution)/shard_map/ppermute | solution.py:50
  165.4 3.9 %collective-permute-start.71 = (bf16[96,128]{1,0:T(8,128)(2,1)S(1)}, bf16[96,128]{1,0:T(8,128)(2,1)S(1)}, u32[]{:S(2)}, u32[]{:S(2)}) collective-permute-start(bf16[96,128]{1,0:T(8,128)(2,1)S(1)} %get-tuple-element.75), channel_id=1, source_target_pairs={{0,16},{4,20},{8,24},{12,28},{16,0},{20,4},{24,8},{28,12},{1,17},{... | collective-permute-start | bytes 73736 | tf_op jit(solution)/shard_map/ppermute | solution.py:50
  170.3 3.7 %collective-permute-done.26 = bf16[96,256]{1,0:T(8,128)(2,1)S(1)} collective-permute-done((bf16[96,256]{1,0:T(8,128)(2,1)S(1)}, bf16[96,256]{1,0:T(8,128)(2,1)S(1)}, u32[]{:S(2)}, u32[]{:S(2)}) %collective-permute-start.26) | collective-permute-done | bytes 49184 | tf_op jit(solution)/shard_map/ppermute | solution.py:50
  175.5 4.6 %collective-permute-start.27 = (bf16[96,256]{1,0:T(8,128)(2,1)S(1)}, bf16[96,256]{1,0:T(8,128)(2,1)S(1)}, u32[]{:S(2)}, u32[]{:S(2)}) collective-permute-start(bf16[96,256]{1,0:T(8,128)(2,1)S(1)} %collective-permute-done.26), channel_id=1, source_target_pairs={{0,2},{1,10},{2,18},{3,26},{4,6},{5,14},{6,22},{7,30},{8,3},{9,11}... | collective-permute-start | bytes 147464 | tf_op jit(solution)/shard_map/ppermute | solution.py:88
  181.8 5.3 %collective-permute-start.29 = (bf16[96,256]{1,0:T(8,128)(2,1)S(1)}, bf16[96,256]{1,0:T(8,128)(2,1)S(1)}, u32[]{:S(2)}, u32[]{:S(2)}) collective-permute-start(bf16[96,256]{1,0:T(8,128)(2,1)S(1)} %collective-permute-done.28), channel_id=1, source_target_pairs={{0,3},{1,11},{2,19},{3,27},{4,7},{5,15},{6,23},{7,31},{8,2},{9,10}... | collective-permute-start | bytes 147464 | tf_op jit(solution)/shard_map/ppermute | solution.py:88
  187.1 1.7 collective-permute-done.29
  189.7 2.9 %collective-permute-start.30 = (bf16[384,256]{1,0:T(8,128)(2,1)S(1)}, bf16[384,256]{1,0:T(8,128)(2,1)S(1)}, u32[]{:S(2)}, u32[]{:S(2)}) collective-permute-start(bf16[384,256]{1,0:T(8,128)(2,1)S(1)} %constant_dynamic-update-slice_fusion.refs_0_), channel_id=1, source_target_pairs={{0,8},{4,12},{8,0},{12,4},{16,24},{20,28},{24,16},{28,20},{1,9},{5... | collective-permute-start | bytes 589832 | tf_op jit(solution)/shard_map/ppermute | solution.py:50
  192.6 3.0 %collective-permute-start.74 = (bf16[96,128]{1,0:T(8,128)(2,1)S(1)}, bf16[96,128]{1,0:T(8,128)(2,1)S(1)}, u32[]{:S(2)}, u32[]{:S(2)}) collective-permute-start(bf16[96,128]{1,0:T(8,128)(2,1)S(1)} %collective-permute-done.73), channel_id=1, source_target_pairs={{0,3},{1,11},{2,19},{3,27},{4,7},{5,15},{6,23},{7,31},{8,2},{9,10}... | collective-permute-start | bytes 73736 | tf_op jit(solution)/shard_map/ppermute | solution.py:88
  196.5 1.9 collective-permute-start.33
  198.9 2.0 collective-permute-done.32.refs_3_
  201.5 1.6 collective-permute-start.76
  203.5 3.6 %shard_map.88 = (bf16[256,512]{1,0:T(8,128)(2,1)S(1)}, bf16[256,1536]{1,0:T(8,128)(2,1)S(1)}) custom-call(s32[2]{0:T(128)S(1)} %pad_add_fusion.at_ref, s32[12]{0:T(128)S(1)} %subtract_bitcast_fusion.index_ref, bf16[1536,2048]{1,0:T(8,128)(2,1)S(1)} %bitcast.5, bf16[384,256]{1,0:T(8,128)(2,1)S(1)} %constant_dynamic-update-slice_fusion.refs_0_, ...), custom_call_target="tpu_custom_call" | custom-call | flops 402653184 | bytes 1572864 | tf_op jit(solution)/shard_map/pallas_call | solution.py:29
  207.1 4.7 %collective-permute-start.39 = (bf16[256,512]{1,0:T(8,128)(2,1)S(1)}, bf16[256,512]{1,0:T(8,128)(2,1)S(1)}, u32[]{:S(2)}, u32[]{:S(2)}) collective-permute-start(bf16[256,512]{1,0:T(8,128)(2,1)S(1)} %get-tuple-element.47), channel_id=1, source_target_pairs={{0,3},{1,0},{2,1},{3,2},{4,7},{5,4},{6,5},{7,6},{8,11},{9,8},{10,9... | collective-permute-start | bytes 786440 | tf_op jit(solution)/shard_map/ppermute | solution.py:46
  213.8 2.2 collective-permute-done.77.refs_3_
  217.6 2.2 shard_map.104
  220.8 2.0 collective-permute-start.86
  225.7 3.9 %collective-permute-start.40 = (bf16[256,512]{1,0:T(8,128)(2,1)S(1)}, bf16[256,512]{1,0:T(8,128)(2,1)S(1)}, u32[]{:S(2)}, u32[]{:S(2)}) collective-permute-start(bf16[256,512]{1,0:T(8,128)(2,1)S(1)} %add_convert_fusion.1), channel_id=1, source_target_pairs={{0,3},{1,0},{2,1},{3,2},{4,7},{5,4},{6,5},{7,6},{8,11},{9,8},{10,9... | collective-permute-start | bytes 786440 | tf_op jit(solution)/shard_map/ppermute | solution.py:46
  230.9 4.3 %collective-permute-done.41 = bf16[256,512]{1,0:T(8,128)(2,1)S(1)} collective-permute-done((bf16[256,512]{1,0:T(8,128)(2,1)S(1)}, bf16[256,512]{1,0:T(8,128)(2,1)S(1)}, u32[]{:S(2)}, u32[]{:S(2)}) %collective-permute-start.41) | collective-permute-done | bytes 262176 | tf_op jit(solution)/shard_map/ppermute | solution.py:46
  235.1 4.5 %collective-permute-done.40 = bf16[256,512]{1,0:T(8,128)(2,1)S(1)} collective-permute-done((bf16[256,512]{1,0:T(8,128)(2,1)S(1)}, bf16[256,512]{1,0:T(8,128)(2,1)S(1)}, u32[]{:S(2)}, u32[]{:S(2)}) %collective-permute-start.40) | collective-permute-done | bytes 262176 | tf_op jit(solution)/shard_map/ppermute | solution.py:46
  240.3 2.0 collective-permute-done.85
  243.0 3.3 %collective-permute-start.89 = (bf16[128,512]{1,0:T(8,128)(2,1)S(1)}, bf16[128,512]{1,0:T(8,128)(2,1)S(1)}, u32[]{:S(2)}, u32[]{:S(2)}) collective-permute-start(bf16[128,512]{1,0:T(8,128)(2,1)S(1)} %add_convert_fusion.3.refs_0_), channel_id=1, source_target_pairs={{0,3},{1,0},{2,1},{3,2},{4,7},{5,4},{6,5},{7,6},{8,11},{9,8},{10,9... | collective-permute-start | bytes 393224 | tf_op jit(solution)/shard_map/ppermute | solution.py:46
  246.2 7.4 %collective-permute-done.87.refs_1_ = bf16[128,512]{1,0:T(8,128)(2,1)S(1)} collective-permute-done((bf16[128,512]{1,0:T(8,128)(2,1)S(1)}, bf16[128,512]{1,0:T(8,128)(2,1)S(1)}, u32[]{:S(2)}, u32[]{:S(2)}) %collective-permute-start.87) | collective-permute-done | bytes 131104 | tf_op jit(solution)/shard_map/ppermute | solution.py:46
  253.6 3.8 %collective-permute-start.44 = (bf16[256,512]{1,0:T(8,128)(2,1)S(1)}, bf16[256,512]{1,0:T(8,128)(2,1)S(1)}, u32[]{:S(2)}, u32[]{:S(2)}) collective-permute-start(bf16[256,512]{1,0:T(8,128)(2,1)S(1)} %add_convert_fusion.refs_0_), channel_id=1, source_target_pairs={{0,3},{1,0},{2,1},{3,2},{4,7},{5,4},{6,5},{7,6},{8,11},{9,8},{10,9... | collective-permute-start | bytes 786440 | tf_op jit(solution)/shard_map/ppermute | solution.py:46
  258.6 3.4 %collective-permute-done.88.refs_0_ = bf16[128,512]{1,0:T(8,128)(2,1)S(1)} collective-permute-done((bf16[128,512]{1,0:T(8,128)(2,1)S(1)}, bf16[128,512]{1,0:T(8,128)(2,1)S(1)}, u32[]{:S(2)}, u32[]{:S(2)}) %collective-permute-start.88) | collective-permute-done | bytes 131104 | tf_op jit(solution)/shard_map/ppermute | solution.py:46
  263.7 2.4 collective-permute-done.44.refs_2_
  267.3 2.7 %collective-permute-done.43.refs_0_ = bf16[256,512]{1,0:T(8,128)(2,1)S(1)} collective-permute-done((bf16[256,512]{1,0:T(8,128)(2,1)S(1)}, bf16[256,512]{1,0:T(8,128)(2,1)S(1)}, u32[]{:S(2)}, u32[]{:S(2)}) %collective-permute-start.43) | collective-permute-done | bytes 262176 | tf_op jit(solution)/shard_map/ppermute | solution.py:46
  (197 shorter events, 62.2 us)
Async XLA Ops:
  1.6 12.3 %collective-permute-start = (bf16[512,256]{1,0:T(8,128)(2,1)S(1)}, bf16[512,256]{1,0:T(8,128)(2,1)S(1)}, u32[]{:S(2)}, u32[]{:S(2)}) collective-permute-start(bf16[512,256]{1,0:T(8,128)(2,1)S(1)} %slice.60.refs_0_), channel_id=1, source_target_pairs={{0,1},{1,2},{2,3},{3,0},{4,5},{5,6},{6,7},{7,4},{8,9},{9,10},{10,1... | collective-permute-start | bytes 786440 | tf_op jit(solution)/shard_map/ppermute | solution.py:46
  4.7 13.6 %collective-permute-start.2 = (bf16[512,256]{1,0:T(8,128)(2,1)S(1)}, bf16[512,256]{1,0:T(8,128)(2,1)S(1)}, u32[]{:S(2)}, u32[]{:S(2)}) collective-permute-start(bf16[512,256]{1,0:T(8,128)(2,1)S(1)} %slice.60.refs_0_), channel_id=1, source_target_pairs={{0,3},{1,0},{2,1},{3,2},{4,7},{5,4},{6,5},{7,6},{8,11},{9,8},{10,9... | collective-permute-start | bytes 786440 | tf_op jit(solution)/shard_map/ppermute | solution.py:46
  13.9 10.4 %collective-permute-start.1 = (bf16[512,256]{1,0:T(8,128)(2,1)S(1)}, bf16[512,256]{1,0:T(8,128)(2,1)S(1)}, u32[]{:S(2)}, u32[]{:S(2)}) collective-permute-start(bf16[512,256]{1,0:T(8,128)(2,1)S(1)} %collective-permute-done.refs_1_), channel_id=1, source_target_pairs={{0,1},{1,2},{2,3},{3,0},{4,5},{5,6},{6,7},{7,4},{8,9},{9,10},{10,1... | collective-permute-start | bytes 786440 | tf_op jit(solution)/shard_map/ppermute | solution.py:46
  25.1 11.2 %collective-permute-start.3 = (bf16[512,256]{1,0:T(8,128)(2,1)S(1)}, bf16[512,256]{1,0:T(8,128)(2,1)S(1)}, u32[]{:S(2)}, u32[]{:S(2)}) collective-permute-start(bf16[512,256]{1,0:T(8,128)(2,1)S(1)} %get-tuple-element.34.refs_0_), channel_id=1, source_target_pairs={{0,1},{1,2},{2,3},{3,0},{4,5},{5,6},{6,7},{7,4},{8,9},{9,10},{10,1... | collective-permute-start | bytes 786440 | tf_op jit(solution)/shard_map/ppermute | solution.py:46
  27.1 14.3 %collective-permute-start.5 = (bf16[512,256]{1,0:T(8,128)(2,1)S(1)}, bf16[512,256]{1,0:T(8,128)(2,1)S(1)}, u32[]{:S(2)}, u32[]{:S(2)}) collective-permute-start(bf16[512,256]{1,0:T(8,128)(2,1)S(1)} %get-tuple-element.34.refs_0_), channel_id=1, source_target_pairs={{0,3},{1,0},{2,1},{3,2},{4,7},{5,4},{6,5},{7,6},{8,11},{9,8},{10,9... | collective-permute-start | bytes 786440 | tf_op jit(solution)/shard_map/ppermute | solution.py:46
  36.3 8.2 %collective-permute-start.4 = (bf16[512,256]{1,0:T(8,128)(2,1)S(1)}, bf16[512,256]{1,0:T(8,128)(2,1)S(1)}, u32[]{:S(2)}, u32[]{:S(2)}) collective-permute-start(bf16[512,256]{1,0:T(8,128)(2,1)S(1)} %collective-permute-done.3.refs_1_), channel_id=1, source_target_pairs={{0,1},{1,2},{2,3},{3,0},{4,5},{5,6},{6,7},{7,4},{8,9},{9,10},{10,1... | collective-permute-start | bytes 786440 | tf_op jit(solution)/shard_map/ppermute | solution.py:46
  46.3 32.4 %collective-permute-start.6 = (bf16[1536,256]{1,0:T(8,128)(2,1)S(1)}, bf16[1536,256]{1,0:T(8,128)(2,1)S(1)}, u32[]{:S(2)}, u32[]{:S(2)}) collective-permute-start(bf16[1536,256]{1,0:T(8,128)(2,1)S(1)} %get-tuple-element.38), channel_id=1, source_target_pairs={{0,4},{4,0},{8,12},{12,8},{16,20},{20,16},{24,28},{28,24},{1,5},{5... | collective-permute-start | bytes 2359304 | tf_op jit(solution)/shard_map/ppermute | solution.py:50
  47.4 8.2 %collective-permute-start.45 = (bf16[512,128]{1,0:T(8,128)(2,1)S(1)}, bf16[512,128]{1,0:T(8,128)(2,1)S(1)}, u32[]{:S(2)}, u32[]{:S(2)}) collective-permute-start(bf16[512,128]{1,0:T(8,128)(2,1)S(1)} %slice.70.refs_0_), channel_id=1, source_target_pairs={{0,1},{1,2},{2,3},{3,0},{4,5},{5,6},{6,7},{7,4},{8,9},{9,10},{10,1... | collective-permute-start | bytes 393224 | tf_op jit(solution)/shard_map/ppermute | solution.py:46
  47.5 8.6 %collective-permute-start.47 = (bf16[512,128]{1,0:T(8,128)(2,1)S(1)}, bf16[512,128]{1,0:T(8,128)(2,1)S(1)}, u32[]{:S(2)}, u32[]{:S(2)}) collective-permute-start(bf16[512,128]{1,0:T(8,128)(2,1)S(1)} %slice.70.refs_0_), channel_id=1, source_target_pairs={{0,3},{1,0},{2,1},{3,2},{4,7},{5,4},{6,5},{7,6},{8,11},{9,8},{10,9... | collective-permute-start | bytes 393224 | tf_op jit(solution)/shard_map/ppermute | solution.py:46
  55.6 6.8 %collective-permute-start.46 = (bf16[512,128]{1,0:T(8,128)(2,1)S(1)}, bf16[512,128]{1,0:T(8,128)(2,1)S(1)}, u32[]{:S(2)}, u32[]{:S(2)}) collective-permute-start(bf16[512,128]{1,0:T(8,128)(2,1)S(1)} %collective-permute-done.45.refs_1_), channel_id=1, source_target_pairs={{0,1},{1,2},{2,3},{3,0},{4,5},{5,6},{6,7},{7,4},{8,9},{9,10},{10,1... | collective-permute-start | bytes 393224 | tf_op jit(solution)/shard_map/ppermute | solution.py:46
  63.2 6.8 %collective-permute-start.48 = (bf16[512,128]{1,0:T(8,128)(2,1)S(1)}, bf16[512,128]{1,0:T(8,128)(2,1)S(1)}, u32[]{:S(2)}, u32[]{:S(2)}) collective-permute-start(bf16[512,128]{1,0:T(8,128)(2,1)S(1)} %get-tuple-element.50.refs_0_), channel_id=1, source_target_pairs={{0,1},{1,2},{2,3},{3,0},{4,5},{5,6},{6,7},{7,4},{8,9},{9,10},{10,1... | collective-permute-start | bytes 393224 | tf_op jit(solution)/shard_map/ppermute | solution.py:46
  63.3 11.3 %collective-permute-start.50 = (bf16[512,128]{1,0:T(8,128)(2,1)S(1)}, bf16[512,128]{1,0:T(8,128)(2,1)S(1)}, u32[]{:S(2)}, u32[]{:S(2)}) collective-permute-start(bf16[512,128]{1,0:T(8,128)(2,1)S(1)} %get-tuple-element.50.refs_0_), channel_id=1, source_target_pairs={{0,3},{1,0},{2,1},{3,2},{4,7},{5,4},{6,5},{7,6},{8,11},{9,8},{10,9... | collective-permute-start | bytes 393224 | tf_op jit(solution)/shard_map/ppermute | solution.py:46
  70.1 6.8 %collective-permute-start.49 = (bf16[512,128]{1,0:T(8,128)(2,1)S(1)}, bf16[512,128]{1,0:T(8,128)(2,1)S(1)}, u32[]{:S(2)}, u32[]{:S(2)}) collective-permute-start(bf16[512,128]{1,0:T(8,128)(2,1)S(1)} %collective-permute-done.48.refs_1_), channel_id=1, source_target_pairs={{0,1},{1,2},{2,3},{3,0},{4,5},{5,6},{6,7},{7,4},{8,9},{9,10},{10,1... | collective-permute-start | bytes 393224 | tf_op jit(solution)/shard_map/ppermute | solution.py:46
  78.6 8.8 %collective-permute-start.51 = (bf16[1536,128]{1,0:T(8,128)(2,1)S(1)}, bf16[1536,128]{1,0:T(8,128)(2,1)S(1)}, u32[]{:S(2)}, u32[]{:S(2)}) collective-permute-start(bf16[1536,128]{1,0:T(8,128)(2,1)S(1)} %get-tuple-element.54), channel_id=1, source_target_pairs={{0,4},{4,0},{8,12},{12,8},{16,20},{20,16},{24,28},{28,24},{1,5},{5... | collective-permute-start | bytes 1179656 | tf_op jit(solution)/shard_map/ppermute | solution.py:50
  85.3 9.8 %collective-permute-start.10 = (bf16[384,256]{1,0:T(8,128)(2,1)S(1)}, bf16[384,256]{1,0:T(8,128)(2,1)S(1)}, u32[]{:S(2)}, u32[]{:S(2)}) collective-permute-start(bf16[384,256]{1,0:T(8,128)(2,1)S(1)} %get-tuple-element.42), channel_id=1, source_target_pairs={{0,16},{4,20},{8,24},{12,28},{16,0},{20,4},{24,8},{28,12},{1,17},{... | collective-permute-start | bytes 589832 | tf_op jit(solution)/shard_map/ppermute | solution.py:50
  86.9 8.2 %collective-permute-start.9 = (bf16[384,256]{1,0:T(8,128)(2,1)S(1)}, bf16[384,256]{1,0:T(8,128)(2,1)S(1)}, u32[]{:S(2)}, u32[]{:S(2)}) collective-permute-start(bf16[384,256]{1,0:T(8,128)(2,1)S(1)} %get-tuple-element.41), channel_id=1, source_target_pairs={{0,8},{4,12},{8,0},{12,4},{16,24},{20,28},{24,16},{28,20},{1,9},{5... | collective-permute-start | bytes 589832 | tf_op jit(solution)/shard_map/ppermute | solution.py:50
  87.5 6.4 %collective-permute-start.52 = (bf16[192,128]{1,0:T(8,128)(2,1)S(1)}, bf16[192,128]{1,0:T(8,128)(2,1)S(1)}, u32[]{:S(2)}, u32[]{:S(2)}) collective-permute-start(bf16[192,128]{1,0:T(8,128)(2,1)S(1)} %get-tuple-element.55), channel_id=1, source_target_pairs={{0,8},{4,12},{8,0},{12,4},{16,24},{20,28},{24,16},{28,20},{1,9},{5... | collective-permute-start | bytes 147464 | tf_op jit(solution)/shard_map/ppermute | solution.py:50
  93.9 5.7 %collective-permute-start.54 = (bf16[384,128]{1,0:T(8,128)(2,1)S(1)}, bf16[384,128]{1,0:T(8,128)(2,1)S(1)}, u32[]{:S(2)}, u32[]{:S(2)}) collective-permute-start(bf16[384,128]{1,0:T(8,128)(2,1)S(1)} %get-tuple-element.57), channel_id=1, source_target_pairs={{0,8},{4,12},{8,0},{12,4},{16,24},{20,28},{24,16},{28,20},{1,9},{5... | collective-permute-start | bytes 294920 | tf_op jit(solution)/shard_map/ppermute | solution.py:50
  94.6 5.5 %collective-permute-start.55 = (bf16[384,128]{1,0:T(8,128)(2,1)S(1)}, bf16[384,128]{1,0:T(8,128)(2,1)S(1)}, u32[]{:S(2)}, u32[]{:S(2)}) collective-permute-start(bf16[384,128]{1,0:T(8,128)(2,1)S(1)} %get-tuple-element.58), channel_id=1, source_target_pairs={{0,16},{4,20},{8,24},{12,28},{16,0},{20,4},{24,8},{28,12},{1,17},{... | collective-permute-start | bytes 294920 | tf_op jit(solution)/shard_map/ppermute | solution.py:50
  95.2 15.1 %collective-permute-start.12 = (bf16[384,256]{1,0:T(8,128)(2,1)S(1)}, bf16[384,256]{1,0:T(8,128)(2,1)S(1)}, u32[]{:S(2)}, u32[]{:S(2)}) collective-permute-start(bf16[384,256]{1,0:T(8,128)(2,1)S(1)} %shard_map.84.refs_0_), channel_id=1, source_target_pairs={{0,16},{4,20},{8,24},{12,28},{16,0},{20,4},{24,8},{28,12},{1,17},{... | collective-permute-start | bytes 589832 | tf_op jit(solution)/shard_map/ppermute | solution.py:50
  96.8 14.0 %collective-permute-start.11 = (bf16[384,256]{1,0:T(8,128)(2,1)S(1)}, bf16[384,256]{1,0:T(8,128)(2,1)S(1)}, u32[]{:S(2)}, u32[]{:S(2)}) collective-permute-start(bf16[384,256]{1,0:T(8,128)(2,1)S(1)} %shard_map.84.refs_0_), channel_id=1, source_target_pairs={{0,8},{4,12},{8,0},{12,4},{16,24},{20,28},{24,16},{28,20},{1,9},{5... | collective-permute-start | bytes 589832 | tf_op jit(solution)/shard_map/ppermute | solution.py:50
  107.1 7.2 %collective-permute-start.61 = (bf16[384,128]{1,0:T(8,128)(2,1)S(1)}, bf16[384,128]{1,0:T(8,128)(2,1)S(1)}, u32[]{:S(2)}, u32[]{:S(2)}) collective-permute-start(bf16[384,128]{1,0:T(8,128)(2,1)S(1)} %collective-permute-done.56.refs_1_), channel_id=1, source_target_pairs={{0,4},{4,0},{8,12},{12,8},{16,20},{20,16},{24,28},{28,24},{1,5},{5... | collective-permute-start | bytes 294920 | tf_op jit(solution)/shard_map/ppermute | solution.py:50
  110.3 10.6 %collective-permute-start.15 = (bf16[384,256]{1,0:T(8,128)(2,1)S(1)}, bf16[384,256]{1,0:T(8,128)(2,1)S(1)}, u32[]{:S(2)}, u32[]{:S(2)}) collective-permute-start(bf16[384,256]{1,0:T(8,128)(2,1)S(1)} %shard_map.84.refs_0_), channel_id=1, source_target_pairs={{0,4},{4,0},{8,12},{12,8},{16,20},{20,16},{24,28},{28,24},{1,5},{5... | collective-permute-start | bytes 589832 | tf_op jit(solution)/shard_map/ppermute | solution.py:50
  114.3 17.9 %collective-permute-start.16 = (bf16[384,256]{1,0:T(8,128)(2,1)S(1)}, bf16[384,256]{1,0:T(8,128)(2,1)S(1)}, u32[]{:S(2)}, u32[]{:S(2)}) collective-permute-start(bf16[384,256]{1,0:T(8,128)(2,1)S(1)} %collective-permute-done.11.refs_1_), channel_id=1, source_target_pairs={{0,4},{4,0},{8,12},{12,8},{16,20},{20,16},{24,28},{28,24},{1,5},{5... | collective-permute-start | bytes 589832 | tf_op jit(solution)/shard_map/ppermute | solution.py:50
  114.3 17.9 %collective-permute-start.17 = (bf16[384,256]{1,0:T(8,128)(2,1)S(1)}, bf16[384,256]{1,0:T(8,128)(2,1)S(1)}, u32[]{:S(2)}, u32[]{:S(2)}) collective-permute-start(bf16[384,256]{1,0:T(8,128)(2,1)S(1)} %collective-permute-done.12.refs_2_), channel_id=1, source_target_pairs={{0,4},{4,0},{8,12},{12,8},{16,20},{20,16},{24,28},{28,24},{1,5},{5... | collective-permute-start | bytes 589832 | tf_op jit(solution)/shard_map/ppermute | solution.py:50
  116.8 15.4 %collective-permute-start.18 = (bf16[192,256]{1,0:T(8,128)(2,1)S(1)}, bf16[192,256]{1,0:T(8,128)(2,1)S(1)}, u32[]{:S(2)}, u32[]{:S(2)}) collective-permute-start(bf16[192,256]{1,0:T(8,128)(2,1)S(1)} %collective-permute-done.13.refs_3_), channel_id=1, source_target_pairs={{0,4},{4,0},{8,12},{12,8},{16,20},{20,16},{24,28},{28,24},{1,5},{5... | collective-permute-start | bytes 294920 | tf_op jit(solution)/shard_map/ppermute | solution.py:50
  117.8 14.4 %collective-permute-start.19 = (bf16[192,256]{1,0:T(8,128)(2,1)S(1)}, bf16[192,256]{1,0:T(8,128)(2,1)S(1)}, u32[]{:S(2)}, u32[]{:S(2)}) collective-permute-start(bf16[192,256]{1,0:T(8,128)(2,1)S(1)} %collective-permute-done.14.refs_4_), channel_id=1, source_target_pairs={{0,4},{4,0},{8,12},{12,8},{16,20},{20,16},{24,28},{28,24},{1,5},{5... | collective-permute-start | bytes 294920 | tf_op jit(solution)/shard_map/ppermute | solution.py:50
  120.9 18.9 %collective-permute-start.65 = (bf16[384,128]{1,0:T(8,128)(2,1)S(1)}, bf16[384,128]{1,0:T(8,128)(2,1)S(1)}, u32[]{:S(2)}, u32[]{:S(2)}) collective-permute-start(bf16[384,128]{1,0:T(8,128)(2,1)S(1)} %shard_map.102), channel_id=1, source_target_pairs={{0,3},{1,0},{2,1},{3,2},{4,7},{5,4},{6,5},{7,6},{8,11},{9,8},{10,9... | collective-permute-start | bytes 294920 | tf_op jit(solution)/shard_map/ppermute | solution.py:46
  132.2 21.4 %collective-permute-start.67 = (bf16[384,128]{1,0:T(8,128)(2,1)S(1)}, bf16[384,128]{1,0:T(8,128)(2,1)S(1)}, u32[]{:S(2)}, u32[]{:S(2)}) collective-permute-start(bf16[384,128]{1,0:T(8,128)(2,1)S(1)} %shard_map.103), channel_id=1, source_target_pairs={{0,1},{1,2},{2,3},{3,0},{4,5},{5,6},{6,7},{7,4},{8,9},{9,10},{10,1... | collective-permute-start | bytes 294920 | tf_op jit(solution)/shard_map/ppermute | solution.py:46
  135.9 15.7 %collective-permute-start.20 = (bf16[384,256]{1,0:T(8,128)(2,1)S(1)}, bf16[384,256]{1,0:T(8,128)(2,1)S(1)}, u32[]{:S(2)}, u32[]{:S(2)}) collective-permute-start(bf16[384,256]{1,0:T(8,128)(2,1)S(1)} %shard_map.86), channel_id=1, source_target_pairs={{0,3},{1,0},{2,1},{3,2},{4,7},{5,4},{6,5},{7,6},{8,11},{9,8},{10,9... | collective-permute-start | bytes 589832 | tf_op jit(solution)/shard_map/ppermute | solution.py:46
  139.8 13.8 %collective-permute-start.66 = (bf16[384,128]{1,0:T(8,128)(2,1)S(1)}, bf16[384,128]{1,0:T(8,128)(2,1)S(1)}, u32[]{:S(2)}, u32[]{:S(2)}) collective-permute-start(bf16[384,128]{1,0:T(8,128)(2,1)S(1)} %add_convert_fusion.5), channel_id=1, source_target_pairs={{0,3},{1,0},{2,1},{3,2},{4,7},{5,4},{6,5},{7,6},{8,11},{9,8},{10,9... | collective-permute-start | bytes 294920 | tf_op jit(solution)/shard_map/ppermute | solution.py:46
  143.5 10.1 %collective-permute-start.22 = (bf16[384,256]{1,0:T(8,128)(2,1)S(1)}, bf16[384,256]{1,0:T(8,128)(2,1)S(1)}, u32[]{:S(2)}, u32[]{:S(2)}) collective-permute-start(bf16[384,256]{1,0:T(8,128)(2,1)S(1)} %shard_map.87), channel_id=1, source_target_pairs={{0,1},{1,2},{2,3},{3,0},{4,5},{5,6},{6,7},{7,4},{8,9},{9,10},{10,1... | collective-permute-start | bytes 589832 | tf_op jit(solution)/shard_map/ppermute | solution.py:46
  151.7 6.0 %collective-permute-start.21 = (bf16[384,256]{1,0:T(8,128)(2,1)S(1)}, bf16[384,256]{1,0:T(8,128)(2,1)S(1)}, u32[]{:S(2)}, u32[]{:S(2)}) collective-permute-start(bf16[384,256]{1,0:T(8,128)(2,1)S(1)} %add_convert_fusion.2), channel_id=1, source_target_pairs={{0,3},{1,0},{2,1},{3,2},{4,7},{5,4},{6,5},{7,6},{8,11},{9,8},{10,9... | collective-permute-start | bytes 589832 | tf_op jit(solution)/shard_map/ppermute | solution.py:46
  157.8 11.5 %collective-permute-start.23 = (bf16[96,256]{1,0:T(8,128)(2,1)S(1)}, bf16[96,256]{1,0:T(8,128)(2,1)S(1)}, u32[]{:S(2)}, u32[]{:S(2)}) collective-permute-start(bf16[96,256]{1,0:T(8,128)(2,1)S(1)} %get-tuple-element.73), channel_id=1, source_target_pairs={{0,0},{1,8},{2,16},{3,24},{4,4},{5,12},{6,20},{7,28},{8,1},{9,9},{... | collective-permute-start | bytes 147464 | tf_op jit(solution)/shard_map/ppermute | solution.py:88
  158.4 10.9 %collective-permute-start.24 = (bf16[96,256]{1,0:T(8,128)(2,1)S(1)}, bf16[96,256]{1,0:T(8,128)(2,1)S(1)}, u32[]{:S(2)}, u32[]{:S(2)}) collective-permute-start(bf16[96,256]{1,0:T(8,128)(2,1)S(1)} %get-tuple-element.72), channel_id=1, source_target_pairs={{0,8},{4,12},{8,0},{12,4},{16,24},{20,28},{24,16},{28,20},{1,9},{5... | collective-permute-start | bytes 147464 | tf_op jit(solution)/shard_map/ppermute | solution.py:50
  161.5 28.2 %collective-permute-start.68 = (bf16[96,128]{1,0:T(8,128)(2,1)S(1)}, bf16[96,128]{1,0:T(8,128)(2,1)S(1)}, u32[]{:S(2)}, u32[]{:S(2)}) collective-permute-start(bf16[96,128]{1,0:T(8,128)(2,1)S(1)} %get-tuple-element.77), channel_id=1, source_target_pairs={{0,0},{1,8},{2,16},{3,24},{4,4},{5,12},{6,20},{7,28},{8,1},{9,9},{... | collective-permute-start | bytes 73736 | tf_op jit(solution)/shard_map/ppermute | solution.py:88
  162.2 17.8 %collective-permute-start.69 = (bf16[96,128]{1,0:T(8,128)(2,1)S(1)}, bf16[96,128]{1,0:T(8,128)(2,1)S(1)}, u32[]{:S(2)}, u32[]{:S(2)}) collective-permute-start(bf16[96,128]{1,0:T(8,128)(2,1)S(1)} %get-tuple-element.76), channel_id=1, source_target_pairs={{0,8},{4,12},{8,0},{12,4},{16,24},{20,28},{24,16},{28,20},{1,9},{5... | collective-permute-start | bytes 73736 | tf_op jit(solution)/shard_map/ppermute | solution.py:50
  165.4 27.2 %collective-permute-start.71 = (bf16[96,128]{1,0:T(8,128)(2,1)S(1)}, bf16[96,128]{1,0:T(8,128)(2,1)S(1)}, u32[]{:S(2)}, u32[]{:S(2)}) collective-permute-start(bf16[96,128]{1,0:T(8,128)(2,1)S(1)} %get-tuple-element.75), channel_id=1, source_target_pairs={{0,16},{4,20},{8,24},{12,28},{16,0},{20,4},{24,8},{28,12},{1,17},{... | collective-permute-start | bytes 73736 | tf_op jit(solution)/shard_map/ppermute | solution.py:50
  169.3 6.1 %collective-permute-start.25 = (bf16[96,256]{1,0:T(8,128)(2,1)S(1)}, bf16[96,256]{1,0:T(8,128)(2,1)S(1)}, u32[]{:S(2)}, u32[]{:S(2)}) collective-permute-start(bf16[96,256]{1,0:T(8,128)(2,1)S(1)} %collective-permute-done.24), channel_id=1, source_target_pairs={{0,1},{1,9},{2,17},{3,25},{4,5},{5,13},{6,21},{7,29},{8,0},{9,8},{... | collective-permute-start | bytes 147464 | tf_op jit(solution)/shard_map/ppermute | solution.py:88
  173.9 6.2 %collective-permute-start.28 = (bf16[96,256]{1,0:T(8,128)(2,1)S(1)}, bf16[96,256]{1,0:T(8,128)(2,1)S(1)}, u32[]{:S(2)}, u32[]{:S(2)}) collective-permute-start(bf16[96,256]{1,0:T(8,128)(2,1)S(1)} %get-tuple-element.70), channel_id=1, source_target_pairs={{0,24},{4,28},{8,16},{12,20},{16,8},{20,12},{24,0},{28,4},{1,25},{... | collective-permute-start | bytes 147464 | tf_op jit(solution)/shard_map/ppermute | solution.py:50
  175.5 6.3 %collective-permute-start.27 = (bf16[96,256]{1,0:T(8,128)(2,1)S(1)}, bf16[96,256]{1,0:T(8,128)(2,1)S(1)}, u32[]{:S(2)}, u32[]{:S(2)}) collective-permute-start(bf16[96,256]{1,0:T(8,128)(2,1)S(1)} %collective-permute-done.26), channel_id=1, source_target_pairs={{0,2},{1,10},{2,18},{3,26},{4,6},{5,14},{6,22},{7,30},{8,3},{9,11}... | collective-permute-start | bytes 147464 | tf_op jit(solution)/shard_map/ppermute | solution.py:88
  180.0 12.6 %collective-permute-start.73 = (bf16[96,128]{1,0:T(8,128)(2,1)S(1)}, bf16[96,128]{1,0:T(8,128)(2,1)S(1)}, u32[]{:S(2)}, u32[]{:S(2)}) collective-permute-start(bf16[96,128]{1,0:T(8,128)(2,1)S(1)} %get-tuple-element.74), channel_id=1, source_target_pairs={{0,24},{4,28},{8,16},{12,20},{16,8},{20,12},{24,0},{28,4},{1,25},{... | collective-permute-start | bytes 73736 | tf_op jit(solution)/shard_map/ppermute | solution.py:50
  180.1 15.5 %collective-permute-start.70 = (bf16[96,128]{1,0:T(8,128)(2,1)S(1)}, bf16[96,128]{1,0:T(8,128)(2,1)S(1)}, u32[]{:S(2)}, u32[]{:S(2)}) collective-permute-start(bf16[96,128]{1,0:T(8,128)(2,1)S(1)} %collective-permute-done.69), channel_id=1, source_target_pairs={{0,1},{1,9},{2,17},{3,25},{4,5},{5,13},{6,21},{7,29},{8,0},{9,8},{... | collective-permute-start | bytes 73736 | tf_op jit(solution)/shard_map/ppermute | solution.py:88
  181.8 7.1 %collective-permute-start.29 = (bf16[96,256]{1,0:T(8,128)(2,1)S(1)}, bf16[96,256]{1,0:T(8,128)(2,1)S(1)}, u32[]{:S(2)}, u32[]{:S(2)}) collective-permute-start(bf16[96,256]{1,0:T(8,128)(2,1)S(1)} %collective-permute-done.28), channel_id=1, source_target_pairs={{0,3},{1,11},{2,19},{3,27},{4,7},{5,15},{6,23},{7,31},{8,2},{9,10}... | collective-permute-start | bytes 147464 | tf_op jit(solution)/shard_map/ppermute | solution.py:88
  188.8 6.8 %collective-permute-start.31 = (bf16[384,256]{1,0:T(8,128)(2,1)S(1)}, bf16[384,256]{1,0:T(8,128)(2,1)S(1)}, u32[]{:S(2)}, u32[]{:S(2)}) collective-permute-start(bf16[384,256]{1,0:T(8,128)(2,1)S(1)} %constant_dynamic-update-slice_fusion.refs_0_), channel_id=1, source_target_pairs={{0,16},{4,20},{8,24},{12,28},{16,0},{20,4},{24,8},{28,12},{1,17},{... | collective-permute-start | bytes 589832 | tf_op jit(solution)/shard_map/ppermute | solution.py:50
  189.7 6.8 %collective-permute-start.30 = (bf16[384,256]{1,0:T(8,128)(2,1)S(1)}, bf16[384,256]{1,0:T(8,128)(2,1)S(1)}, u32[]{:S(2)}, u32[]{:S(2)}) collective-permute-start(bf16[384,256]{1,0:T(8,128)(2,1)S(1)} %constant_dynamic-update-slice_fusion.refs_0_), channel_id=1, source_target_pairs={{0,8},{4,12},{8,0},{12,4},{16,24},{20,28},{24,16},{28,20},{1,9},{5... | collective-permute-start | bytes 589832 | tf_op jit(solution)/shard_map/ppermute | solution.py:50
  192.6 5.8 %collective-permute-start.72 = (bf16[96,128]{1,0:T(8,128)(2,1)S(1)}, bf16[96,128]{1,0:T(8,128)(2,1)S(1)}, u32[]{:S(2)}, u32[]{:S(2)}) collective-permute-start(bf16[96,128]{1,0:T(8,128)(2,1)S(1)} %collective-permute-done.71), channel_id=1, source_target_pairs={{0,2},{1,10},{2,18},{3,26},{4,6},{5,14},{6,22},{7,30},{8,3},{9,11}... | collective-permute-start | bytes 73736 | tf_op jit(solution)/shard_map/ppermute | solution.py:88
  192.6 5.8 %collective-permute-start.74 = (bf16[96,128]{1,0:T(8,128)(2,1)S(1)}, bf16[96,128]{1,0:T(8,128)(2,1)S(1)}, u32[]{:S(2)}, u32[]{:S(2)}) collective-permute-start(bf16[96,128]{1,0:T(8,128)(2,1)S(1)} %collective-permute-done.73), channel_id=1, source_target_pairs={{0,3},{1,11},{2,19},{3,27},{4,7},{5,15},{6,23},{7,31},{8,2},{9,10}... | collective-permute-start | bytes 73736 | tf_op jit(solution)/shard_map/ppermute | solution.py:88
  195.6 5.9 %collective-permute-start.34 = (bf16[384,256]{1,0:T(8,128)(2,1)S(1)}, bf16[384,256]{1,0:T(8,128)(2,1)S(1)}, u32[]{:S(2)}, u32[]{:S(2)}) collective-permute-start(bf16[384,256]{1,0:T(8,128)(2,1)S(1)} %constant_dynamic-update-slice_fusion.refs_0_), channel_id=1, source_target_pairs={{0,4},{4,0},{8,12},{12,8},{16,20},{20,16},{24,28},{28,24},{1,5},{5... | collective-permute-start | bytes 589832 | tf_op jit(solution)/shard_map/ppermute | solution.py:50
  201.5 10.4 %collective-permute-start.76 = (bf16[384,128]{1,0:T(8,128)(2,1)S(1)}, bf16[384,128]{1,0:T(8,128)(2,1)S(1)}, u32[]{:S(2)}, u32[]{:S(2)}) collective-permute-start(bf16[384,128]{1,0:T(8,128)(2,1)S(1)} %constant_dynamic-update-slice_fusion.4.refs_0_), channel_id=1, source_target_pairs={{0,16},{4,20},{8,24},{12,28},{16,0},{20,4},{24,8},{28,12},{1,17},{... | collective-permute-start | bytes 294920 | tf_op jit(solution)/shard_map/ppermute | solution.py:50
  203.1 9.1 %collective-permute-start.75 = (bf16[384,128]{1,0:T(8,128)(2,1)S(1)}, bf16[384,128]{1,0:T(8,128)(2,1)S(1)}, u32[]{:S(2)}, u32[]{:S(2)}) collective-permute-start(bf16[384,128]{1,0:T(8,128)(2,1)S(1)} %constant_dynamic-update-slice_fusion.4.refs_0_), channel_id=1, source_target_pairs={{0,8},{4,12},{8,0},{12,4},{16,24},{20,28},{24,16},{28,20},{1,9},{5... | collective-permute-start | bytes 294920 | tf_op jit(solution)/shard_map/ppermute | solution.py:50
  203.5 9.8 %collective-permute-start.79 = (bf16[384,128]{1,0:T(8,128)(2,1)S(1)}, bf16[384,128]{1,0:T(8,128)(2,1)S(1)}, u32[]{:S(2)}, u32[]{:S(2)}) collective-permute-start(bf16[384,128]{1,0:T(8,128)(2,1)S(1)} %constant_dynamic-update-slice_fusion.4.refs_0_), channel_id=1, source_target_pairs={{0,4},{4,0},{8,12},{12,8},{16,20},{20,16},{24,28},{28,24},{1,5},{5... | collective-permute-start | bytes 294920 | tf_op jit(solution)/shard_map/ppermute | solution.py:50
  207.1 18.5 %collective-permute-start.39 = (bf16[256,512]{1,0:T(8,128)(2,1)S(1)}, bf16[256,512]{1,0:T(8,128)(2,1)S(1)}, u32[]{:S(2)}, u32[]{:S(2)}) collective-permute-start(bf16[256,512]{1,0:T(8,128)(2,1)S(1)} %get-tuple-element.47), channel_id=1, source_target_pairs={{0,3},{1,0},{2,1},{3,2},{4,7},{5,4},{6,5},{7,6},{8,11},{9,8},{10,9... | collective-permute-start | bytes 786440 | tf_op jit(solution)/shard_map/ppermute | solution.py:46
  219.8 10.9 %collective-permute-start.84 = (bf16[128,512]{1,0:T(8,128)(2,1)S(1)}, bf16[128,512]{1,0:T(8,128)(2,1)S(1)}, u32[]{:S(2)}, u32[]{:S(2)}) collective-permute-start(bf16[128,512]{1,0:T(8,128)(2,1)S(1)} %get-tuple-element.63), channel_id=1, source_target_pairs={{0,3},{1,0},{2,1},{3,2},{4,7},{5,4},{6,5},{7,6},{8,11},{9,8},{10,9... | collective-permute-start | bytes 393224 | tf_op jit(solution)/shard_map/ppermute | solution.py:46
  220.8 19.5 %collective-permute-start.86 = (bf16[128,512]{1,0:T(8,128)(2,1)S(1)}, bf16[128,512]{1,0:T(8,128)(2,1)S(1)}, u32[]{:S(2)}, u32[]{:S(2)}) collective-permute-start(bf16[128,512]{1,0:T(8,128)(2,1)S(1)} %shard_map.106), channel_id=1, source_target_pairs={{0,1},{1,2},{2,3},{3,0},{4,5},{5,6},{6,7},{7,4},{8,9},{9,10},{10,1... | collective-permute-start | bytes 393224 | tf_op jit(solution)/shard_map/ppermute | solution.py:46
  224.0 11.1 %collective-permute-start.41 = (bf16[256,512]{1,0:T(8,128)(2,1)S(1)}, bf16[256,512]{1,0:T(8,128)(2,1)S(1)}, u32[]{:S(2)}, u32[]{:S(2)}) collective-permute-start(bf16[256,512]{1,0:T(8,128)(2,1)S(1)} %shard_map.90), channel_id=1, source_target_pairs={{0,1},{1,2},{2,3},{3,0},{4,5},{5,6},{6,7},{7,4},{8,9},{9,10},{10,1... | collective-permute-start | bytes 786440 | tf_op jit(solution)/shard_map/ppermute | solution.py:46
  225.7 13.9 %collective-permute-start.40 = (bf16[256,512]{1,0:T(8,128)(2,1)S(1)}, bf16[256,512]{1,0:T(8,128)(2,1)S(1)}, u32[]{:S(2)}, u32[]{:S(2)}) collective-permute-start(bf16[256,512]{1,0:T(8,128)(2,1)S(1)} %add_convert_fusion.1), channel_id=1, source_target_pairs={{0,3},{1,0},{2,1},{3,2},{4,7},{5,4},{6,5},{7,6},{8,11},{9,8},{10,9... | collective-permute-start | bytes 786440 | tf_op jit(solution)/shard_map/ppermute | solution.py:46
  230.8 11.5 %collective-permute-start.85 = (bf16[128,512]{1,0:T(8,128)(2,1)S(1)}, bf16[128,512]{1,0:T(8,128)(2,1)S(1)}, u32[]{:S(2)}, u32[]{:S(2)}) collective-permute-start(bf16[128,512]{1,0:T(8,128)(2,1)S(1)} %add_convert_fusion.4), channel_id=1, source_target_pairs={{0,3},{1,0},{2,1},{3,2},{4,7},{5,4},{6,5},{7,6},{8,11},{9,8},{10,9... | collective-permute-start | bytes 393224 | tf_op jit(solution)/shard_map/ppermute | solution.py:46
  239.7 17.7 %collective-permute-start.42 = (bf16[256,512]{1,0:T(8,128)(2,1)S(1)}, bf16[256,512]{1,0:T(8,128)(2,1)S(1)}, u32[]{:S(2)}, u32[]{:S(2)}) collective-permute-start(bf16[256,512]{1,0:T(8,128)(2,1)S(1)} %add_convert_fusion.refs_0_), channel_id=1, source_target_pairs={{0,1},{1,2},{2,3},{3,0},{4,5},{5,6},{6,7},{7,4},{8,9},{9,10},{10,1... | collective-permute-start | bytes 786440 | tf_op jit(solution)/shard_map/ppermute | solution.py:46
  242.4 11.3 %collective-permute-start.87 = (bf16[128,512]{1,0:T(8,128)(2,1)S(1)}, bf16[128,512]{1,0:T(8,128)(2,1)S(1)}, u32[]{:S(2)}, u32[]{:S(2)}) collective-permute-start(bf16[128,512]{1,0:T(8,128)(2,1)S(1)} %add_convert_fusion.3.refs_0_), channel_id=1, source_target_pairs={{0,1},{1,2},{2,3},{3,0},{4,5},{5,6},{6,7},{7,4},{8,9},{9,10},{10,1... | collective-permute-start | bytes 393224 | tf_op jit(solution)/shard_map/ppermute | solution.py:46
  243.0 14.5 %collective-permute-start.89 = (bf16[128,512]{1,0:T(8,128)(2,1)S(1)}, bf16[128,512]{1,0:T(8,128)(2,1)S(1)}, u32[]{:S(2)}, u32[]{:S(2)}) collective-permute-start(bf16[128,512]{1,0:T(8,128)(2,1)S(1)} %add_convert_fusion.3.refs_0_), channel_id=1, source_target_pairs={{0,3},{1,0},{2,1},{3,2},{4,7},{5,4},{6,5},{7,6},{8,11},{9,8},{10,9... | collective-permute-start | bytes 393224 | tf_op jit(solution)/shard_map/ppermute | solution.py:46
  253.6 8.4 %collective-permute-start.88 = (bf16[128,512]{1,0:T(8,128)(2,1)S(1)}, bf16[128,512]{1,0:T(8,128)(2,1)S(1)}, u32[]{:S(2)}, u32[]{:S(2)}) collective-permute-start(bf16[128,512]{1,0:T(8,128)(2,1)S(1)} %collective-permute-done.87.refs_1_), channel_id=1, source_target_pairs={{0,1},{1,2},{2,3},{3,0},{4,5},{5,6},{6,7},{7,4},{8,9},{9,10},{10,1... | collective-permute-start | bytes 393224 | tf_op jit(solution)/shard_map/ppermute | solution.py:46
  253.6 12.5 %collective-permute-start.44 = (bf16[256,512]{1,0:T(8,128)(2,1)S(1)}, bf16[256,512]{1,0:T(8,128)(2,1)S(1)}, u32[]{:S(2)}, u32[]{:S(2)}) collective-permute-start(bf16[256,512]{1,0:T(8,128)(2,1)S(1)} %add_convert_fusion.refs_0_), channel_id=1, source_target_pairs={{0,3},{1,0},{2,1},{3,2},{4,7},{5,4},{6,5},{7,6},{8,11},{9,8},{10,9... | collective-permute-start | bytes 786440 | tf_op jit(solution)/shard_map/ppermute | solution.py:46
  257.4 12.6 %collective-permute-start.43 = (bf16[256,512]{1,0:T(8,128)(2,1)S(1)}, bf16[256,512]{1,0:T(8,128)(2,1)S(1)}, u32[]{:S(2)}, u32[]{:S(2)}) collective-permute-start(bf16[256,512]{1,0:T(8,128)(2,1)S(1)} %collective-permute-done.42.refs_1_), channel_id=1, source_target_pairs={{0,1},{1,2},{2,3},{3,0},{4,5},{5,6},{6,7},{7,4},{8,9},{9,10},{10,1... | collective-permute-start | bytes 786440 | tf_op jit(solution)/shard_map/ppermute | solution.py:46
  (33 other events, 194.0 us)

commit v9 on v7

--- a/solution.py
+++ b/solution.py
@@ -22,7 +22,7 @@
     return pltpu.with_memory_space_constraint(x, pltpu.HBM)
 
 
-def kernel_call(body, outs, scalars, held, placed, scratch, flops, nbytes, final=False):
+def kernel_call(body, outs, scalars, held, placed, scratch, flops, nbytes, final=False, loose=()):
     size = sum(2 * math.prod(s.shape) for s in scratch if s.dtype == BF16)
     single = not isinstance(outs, list)
     out_shape = [o if final else pltpu.VMEM(o.shape, o.dtype) for o in ([outs] if single else outs)]
@@ -32,13 +32,13 @@
         grid_spec=pltpu.PrefetchScalarGridSpec(
             num_scalar_prefetch=len(scalars),
             grid=(1,),
-            in_specs=[VMEM] * len(held) + [ANY] * len(placed),
+            in_specs=[VMEM] * (len(held) + len(loose)) + [ANY] * len(placed),
             out_specs=[VMEM] * len(out_shape),
             scratch_shapes=scratch,
         ),
         compiler_params=pltpu.CompilerParams(vmem_limit_bytes=size + 12 * 1024 * 1024),
         cost_estimate=pl.CostEstimate(flops=flops, bytes_accessed=nbytes, transcendentals=0),
-    )(*scalars, *[pltpu.with_memory_space_constraint(x, pltpu.VMEM) for x in held], *placed)
+    )(*scalars, *[pltpu.with_memory_space_constraint(x, pltpu.VMEM) for x in held], *loose, *placed)
     return results[0] if single else results
 
 
@@ -62,14 +62,18 @@
     return found
 
 
-def gather_front(x, n):
-    rows = x.shape[0]
-    by_x, by_y = swap(x, n, 2), swap(x, n, 4)
-    corner_low = swap(by_y[: rows // 2], n, 2)
-    corner_high = swap(by_x[rows // 2 :], n, 4)
-    mine = [(0, 0, x), (1, 0, by_x), (2, 0, by_y), (3, 0, corner_low), (3, rows // 2, corner_high)]
-    found = [(chip, 0, low, block) for chip, low, block in mine]
-    return found + [(chip, 1, low, swap(block, n, 1)) for chip, low, block in mine]
+def gather_front(low, high, n):
+    rows = low.shape[0]
+    x_high, y_low = swap(high, n, 2), swap(low, n, 4)
+    own, low, high = regroup(low, high)
+    x_low, y_high = swap(low, n, 2), swap(high, n, 4)
+    corner_low, corner_high = swap(y_low, n, 2), swap(x_high, n, 4)
+    sides = stack([x_low, x_high, y_low, y_high, corner_low, corner_high])
+    found = []
+    for core, block, others in ((0, own, sides), (1, swap(own, n, 1), swap(sides, n, 1))):
+        found.append((0, core, 0, 2 * rows, block))
+        found += [(chip, core, (chip - 1) * 2 * rows, 2 * rows, others) for chip in (1, 2, 3)]
+    return found
 
 
 def to_plane(x, n):
@@ -86,7 +90,8 @@
             for row in range(n)
         ]
         moved.append(lax.ppermute(quarter, ("front", "row"), perm))
-    return jnp.concatenate(moved, axis=0)
+    half = n // 2
+    return [jnp.concatenate(some, axis=0) for some in (moved[:half], moved[half:])]
 
 
 def far_offsets(n):
@@ -129,51 +134,49 @@
     offsets = [o for o, _ in found]
 
     def body(at_ref, a_ref, *refs):
-        total = products(at_ref, a_ref, slice(None), offsets, refs[:count], n_row, contract)
-        extras = refs[count : count + len(extra)]
+        extras, x_refs = refs[: len(extra)], refs[len(extra) : len(extra) + count]
+        total = products(at_ref, a_ref, slice(None), offsets, x_refs, n_row, contract)
         for ref, value in zip(refs[count + len(extra) :], finish(total, *[e[...] for e in extras])):
             ref[...] = value
 
     share = 2 * pivot.size * count // n_row
-    held = [pivot] + [x for _, x in found] + list(extra)
-    return kernel_call(body, outs, [at], held, [], [], share * outs[0].shape[1], share, final)
+    held = [pivot] + list(extra)
+    blocks = [x for _, x in found]
+    return kernel_call(body, outs, [at], held, [], [], share * outs[0].shape[1], share, final, blocks)
 
 
 def border_tile(rows):
     return BLK * next(k for k in (4, 3, 2, 1) if rows // BLK % k == 0)
 
 
-def border_partial(at, coupling, found, n_row, partial, rhs_root, piece_rows):
+def border_partial(at, coupling, found, n_row, partial, source, fetch_rows):
     rows, count, width = coupling.shape[0], len(found), found[0][1].shape[1]
     offsets = [o for o, _ in found]
     tile = border_tile(rows)
     held = [coupling] + [x for _, x in found] + ([] if partial is None else [partial])
 
     def body(at_ref, a_ref, *refs):
-        if partial is None:
-            rhs_hbm, out_ref, own_ref, sem = refs[count:]
-            place = pl.ds(pl.multiple_of(at_ref[1] * piece_rows, piece_rows), piece_rows)
-            copy = pltpu.make_async_copy(rhs_hbm.at[place], own_ref, sem)
-            copy.start()
-        else:
-            partial_ref, out_ref = refs[count:]
+        source_hbm, out_ref, own_ref, sem = refs[-4:]
+        if fetch_rows < source.shape[0]:
+            source_hbm = source_hbm.at[pl.ds(pl.multiple_of(at_ref[1] * fetch_rows, fetch_rows), fetch_rows)]
+        copy = pltpu.make_async_copy(source_hbm, own_ref, sem)
+        copy.start()
 
         @pl.loop(0, rows // tile)
         def _(i):
             place = pl.ds(pl.multiple_of(i * tile, tile), tile)
             total = products(at_ref, a_ref, place, offsets, refs[:count], n_row, ((1,), (0,)))
-            out_ref[place, :] = total if partial is None else partial_ref[place, :] + total
-
-        if partial is None:
-            copy.wait()
+            out_ref[place, :] = total if partial is None else refs[count][place, :] + total
+
+        copy.wait()
 
     share = 2 * coupling.size * count // n_row
-    out = jax.ShapeDtypeStruct((rows, width), F32)
-    if partial is None:
-        outs = [out, jax.ShapeDtypeStruct((piece_rows, width), F32)]
-        scratch = [pltpu.SemaphoreType.DMA]
-        return kernel_call(body, outs, [at], held, [in_hbm(rhs_root)], scratch, share * width, share)
-    return kernel_call(body, out, [at], held, [], [], share * width, share)
+    outs = [
+        jax.ShapeDtypeStruct((rows, width), F32),
+        jax.ShapeDtypeStruct((fetch_rows, source.shape[1]), source.dtype),
+    ]
+    scratch = [pltpu.SemaphoreType.DMA]
+    return kernel_call(body, outs, [at], held, [in_hbm(source)], scratch, share * width, share)
 
 
 def border_scatter(at, local_index, coupling, found, partial, n_row, n_front, span_rows):
@@ -222,96 +225,106 @@
     return total
 
 
-def corner_parts(keep, came):
-    rows, width = keep.shape[0] // 4, keep.shape[1]
-    half = jax.ShapeDtypeStruct((rows // 2, width), BF16)
-
-    def body(keep_ref, came_ref, low_ref, high_ref):
-        for start, out_ref in ((3 * rows, low_ref), (3 * rows + rows // 2, high_ref)):
-            place = slice(start, start + rows // 2)
+def sum_halves(keep, came, halves):
+    rows, width = keep.shape[0] // 8, keep.shape[1]
+    outs = [jax.ShapeDtypeStruct((rows, width), BF16)] * len(halves)
+
+    def body(keep_ref, came_ref, *out_refs):
+        for (chip, which), out_ref in zip(halves, out_refs):
+            place = slice((2 * chip + which) * rows, (2 * chip + which + 1) * rows)
             out_ref[...] = added(keep_ref[place, :], came_ref[place, :]).astype(BF16)
 
-    return kernel_call(body, [half, half], [], [keep, came], [], [], keep.size, keep.size)
-
-
-def side_parts(keep, came, low, high):
-    rows, width = keep.shape[0] // 4, keep.shape[1]
-    part = jax.ShapeDtypeStruct((rows, width), BF16)
+    return kernel_call(body, outs, [], [keep, came], [], [], keep.size, keep.size)
+
+
+def sum_relayed(keep, came, low, high):
+    rows, width = low.shape
 
     def body(keep_ref, came_ref, low_ref, high_ref, x_ref, y_ref):
-        first, second = (0, rows // 2), (rows // 2, rows)
-        for slot, add_ref, here, other, out_ref in (
-            (1, high_ref, second, first, x_ref),
-            (2, low_ref, first, second, y_ref),
-        ):
-            place = slice(slot * rows + other[0], slot * rows + other[1])
-            out_ref[other[0] : other[1], :] = added(keep_ref[place, :], came_ref[place, :]).astype(BF16)
-            place = slice(slot * rows + here[0], slot * rows + here[1])
-            total = added(keep_ref[place, :], came_ref[place, :], add_ref[...])
-            out_ref[here[0] : here[1], :] = total.astype(BF16)
-
-    return kernel_call(body, [part, part], [], [keep, came, low, high], [], [], 2 * keep.size, 2 * keep.size)
-
-
-def own_part(own_rhs, keep, came, by_x, by_y):
-    rows, width = by_x.shape
-
-    def body(rhs_ref, keep_ref, came_ref, x_ref, y_ref, out_ref):
-        total = added(keep_ref[:rows, :], came_ref[:rows, :], x_ref[...], y_ref[...])
-        out_ref[...] = (rhs_ref[...] - total).astype(BF16)
-
-    out = jax.ShapeDtypeStruct((rows, width), BF16)
-    return kernel_call(body, out, [], [own_rhs, keep, came, by_x, by_y], [], [], keep.size, keep.size)
+        for half, add_ref, out_ref in ((3, high_ref, x_ref), (4, low_ref, y_ref)):
+            place = slice(half * rows, (half + 1) * rows)
+            out_ref[...] = added(keep_ref[place, :], came_ref[place, :], add_ref[...]).astype(BF16)
+
+    outs = [jax.ShapeDtypeStruct((rows, width), BF16)] * 2
+    return kernel_call(body, outs, [], [keep, came, low, high], [], [], 2 * keep.size, 2 * keep.size)
+
+
+def own_part(own_rhs, keep, came, low, high):
+    half, width = own_rhs.shape[0] // 2, own_rhs.shape[1]
+
+    def body(rhs_ref, keep_ref, came_ref, *refs):
+        *add_refs, low_ref, high_ref = refs
+        for start, adds, out_ref in ((0, add_refs[:2], low_ref), (half, add_refs[2:], high_ref)):
+            place = slice(start, start + half)
+            total = added(keep_ref[place, :], came_ref[place, :], *[ref[...] for ref in adds])
+            out_ref[...] = (rhs_ref[place, :] - total).astype(BF16)
+
+    outs = [jax.ShapeDtypeStruct((half, width), BF16)] * 2
+    return kernel_call(body, outs, [], [own_rhs, keep, came, *low, *high], [], [], keep.size, keep.size)
+
+
+def stack(blocks):
+    rows, width = blocks[0].shape
+
+    def body(*refs):
+        for i, ref in enumerate(refs[:-1]):
+            refs[-1][i * rows : (i + 1) * rows, :] = ref[...]
+
+    out = jax.ShapeDtypeStruct((len(blocks) * rows, width), BF16)
+    return kernel_call(body, out, [], blocks, [], [], 0, 4 * len(blocks) * rows * width)
+
+
+def regroup(low, high):
+    rows, width = low.shape
+
+    def body(low_ref, high_ref, whole_ref, low_out_ref, high_out_ref):
+        for start, half_ref, out_ref in ((0, low_ref, low_out_ref), (rows, high_ref, high_out_ref)):
+            out_ref[...] = half_ref[...]
+            whole_ref[start : start + rows, :] = half_ref[...]
+
+    outs = [jax.ShapeDtypeStruct((n * rows, width), BF16) for n in (2, 1, 1)]
+    return kernel_call(body, outs, [], [low, high], [], [], 0, 8 * low.size)
 
 
 def assemble(pieces, piece_refs, target_ref, sems, base):
     copies = []
-    for (chip, core, low, block), ref in zip(pieces, piece_refs):
-        start = base(2 * chip + core) + low
-        place = pl.ds(pl.multiple_of(start, block.shape[0]), block.shape[0])
-        copies.append(pltpu.make_async_copy(ref, target_ref.at[place], sems.at[len(copies)]))
+    for (chip, core, row, rows, _), ref in zip(pieces, piece_refs):
+        place = pl.ds(pl.multiple_of(base(2 * chip + core), rows), rows)
+        source = ref.at[pl.ds(row, rows)]
+        copies.append(pltpu.make_async_copy(source, target_ref.at[place], sems.at[len(copies)]))
     return copies
 
 
 def root_products(at, inverse, pieces, offsets, kinds, n_row, n_front):
     span_rows = inverse.shape[1]
     rows = inverse.shape[0] // n_row
-    width = pieces[0][3].shape[1]
+    width = pieces[0][-1].shape[1]
     piece_rows = span_rows // n_front
     count, many = len(offsets), len(pieces)
 
-    def body(at_ref, *refs):
-        piece_refs, a_hbm, out_refs = refs[:many], refs[many], refs[many + 1 : many + 1 + count]
-        a_ref, x_ref, sems = refs[-3:]
+    def body(at_ref, a_ref, *refs):
+        piece_refs, out_refs, (x_ref, sems) = refs[:many], refs[many : many + count], refs[many + count :]
         copies = assemble(
             pieces, piece_refs, x_ref, sems, lambda d: lax.bitwise_xor(at_ref[1], d) * piece_rows
         )
-        loads = []
-        for i, offset in enumerate(offsets):
-            place = pl.ds(pl.multiple_of(owner(at_ref, offset, n_row) * rows, rows), rows)
-            loads.append(pltpu.make_async_copy(a_hbm.at[place], a_ref.at[i], sems.at[many + i]))
-        for copy in loads[:1] + copies + loads[1:]:
+        for copy in copies:
             copy.start()
         for copy in copies:
             copy.wait()
-        for i in range(count):
-            loads[i].wait()
-            out_refs[i][...] = dot(a_ref[i], x_ref[...]).astype(out_refs[i].dtype)
+        for offset, out_ref in zip(offsets, out_refs):
+            place = pl.ds(pl.multiple_of(owner(at_ref, offset, n_row) * rows, rows), rows)
+            out_ref[...] = dot(a_ref[place, :], x_ref[...]).astype(out_ref.dtype)
 
     outs = [jax.ShapeDtypeStruct((rows, width), kind) for kind in kinds]
-    scratch = [
-        pltpu.VMEM((count, rows, span_rows), BF16),
-        pltpu.VMEM((span_rows, width), BF16),
-        pltpu.SemaphoreType.DMA((many + count,)),
-    ]
+    scratch = [pltpu.VMEM((span_rows, width), BF16), pltpu.SemaphoreType.DMA((many,))]
     share = 2 * rows * span_rows * count
-    held = [block for *_, block in pieces]
-    return kernel_call(body, outs, [at], held, [in_hbm(inverse)], scratch, share * width, share)
+    held = [inverse] + [block for *_, block in pieces]
+    return kernel_call(body, outs, [at], held, [], scratch, share * width, share)
 
 
 def border_pick(at, local_index, coupling, pieces, offset, n_row, n_front):
     rows, depth = coupling.shape[0], coupling.shape[1] // n_row
-    piece_rows, width = pieces[0][3].shape
+    piece_rows, width = pieces[0][-1].shape
     span_rows = piece_rows * n_front
     many = len(pieces)
 
@@ -381,19 +394,23 @@
     )
     found = gather_row(inner_half, n_row)
     partial, own_rhs = border_partial(at, border_coupling, found[:2], n_row, None, rhs_root, piece_rows)
-    if found[2:-1]:
-        partial = border_partial(at, border_coupling, found[2:-1], n_row, partial, rhs_root, piece_rows)
+    partial, inverse = border_partial(
+        at, border_coupling, found[2:-1], n_row, partial, root_inverse, root_inverse.shape[0]
+    )
     send, keep = border_scatter(
         at, local_index, border_coupling, found[-1:], partial, n_row, n_front, span_rows
     )
     came = swap(send, n_front, 1)
-    low, high = corner_parts(keep, came)
-    by_x, by_y = side_parts(keep, came, swap(low, n_front, 2), swap(high, n_front, 4))
-    piece = own_part(own_rhs, keep, came, swap(by_x, n_front, 2), swap(by_y, n_front, 4))
-    pieces = gather_front(piece, n_front)
+    low, high = sum_halves(keep, came, [(3, 0), (3, 1)])
+    low, high = swap(low, n_front, 2), swap(high, n_front, 4)
+    x_low, y_high = sum_halves(keep, came, [(1, 0), (2, 1)])
+    x_low, y_high = swap(x_low, n_front, 2), swap(y_high, n_front, 4)
+    x_high, y_low = sum_relayed(keep, came, low, high)
+    x_high, y_low = swap(x_high, n_front, 2), swap(y_low, n_front, 4)
+    pieces = gather_front(*own_part(own_rhs, keep, came, (x_low, y_low), (x_high, y_high)), n_front)
 
     def root(offsets, kind):
-        outs = root_products(at, root_inverse, pieces, offsets, [kind] * len(offsets), n_row, n_front)
+        outs = root_products(at, inverse, pieces, offsets, [kind] * len(offsets), n_row, n_front)
         return dict(zip(offsets, outs))
 
     first = {}
@@ -401,7 +418,7 @@
         first.update(root([offset], BF16))
     rest = root(later_at + [0], F32)
     root_solution = scatter_row(first, rest, rest[0], n_row)
-    spans = gather_front(to_plane(root_solution.astype(BF16), n_row), n_front)
+    spans = gather_front(*to_plane(root_solution.astype(BF16), n_row), n_front)
 
     out, picked = border_pick(at, local_index, border_coupling, spans, first_at[0], n_row, n_front)
     first = {first_at[0]: out}

time: 225 us -> 221 us (0.982)
  waiting for transfers between devices: 134 us -> 121 us
  starting transfers between devices: 46.5 us -> 59.2 us
    ppermute x26, waiting for transfers between devices: 39.7 us -> 30.1 us  [swap(): return lax.ppermute(x, 'front', [(i, i ^ by) for i in range(size)])]
    ppermute x15, starting transfers between devices: 21.6 us -> 28.2 us  [shift(): return lax.ppermute(x, 'row', [(i, (i + by) % size) for i in range(size)])]
    ppermute x26, starting transfers between devices: 19.9 us -> 25.6 us  [swap(): return lax.ppermute(x, 'front', [(i, i ^ by) for i in range(size)])]
    ppermute x15, waiting for transfers between devices: 90.4 us -> 85.6 us  [shift(): return lax.ppermute(x, 'row', [(i, (i + by) % size) for i in range(size)])]
    unnamed x21 -> x16, local copies, waits for them, and re-layouts: 7.17 us -> 5.4 us
    pallas_call x16 -> x21, Pallas kernels: 34.1 us -> 33 us  [kernel_call(): pl.pallas_call(body, out_shape=out_shape, grid_spec=pltpu.PrefetchScalarG...]
  transfers between devices with their start and end apart: 45 -> 45, of which waited for: 30 -> 34; matrix products, arithmetic and copies ran while one was open for 0% -> 0% of each run, Pallas kernels for 10% -> 10%
where the time goes in v9:
time: 221 us
  waiting for transfers between devices  121 us (55%)
  starting transfers between devices  59.2 us (27%)
  Pallas kernels  33 us (15%)
  local copies, waits for them, and re-layouts  5.47 us (2%)
    ppermute x15, waiting for transfers between devices, shift(): return lax.ppermute(x, 'row', [(i, (i + by) % size) for i in range(size)])  85.6 us
    pallas_call x21, Pallas kernels, kernel_call(): pl.pallas_call(body, out_shape=out_shape, grid_spec=pltpu.PrefetchScalarG...  33 us
    ppermute x26, waiting for transfers between devices, swap(): return lax.ppermute(x, 'front', [(i, i ^ by) for i in range(size)])  30.1 us
    ppermute x15, starting transfers between devices, shift(): return lax.ppermute(x, 'row', [(i, (i + by) % size) for i in range(size)])  28.2 us
    ppermute x26, starting transfers between devices, swap(): return lax.ppermute(x, 'front', [(i, i ^ by) for i in range(size)])  25.6 us
    ppermute x4, starting transfers between devices, to_plane(): moved.append(lax.ppermute(quarter, ('front', 'row'), perm))  5.51 us
    unnamed x16, local copies, waits for them, and re-layouts  5.4 us
    ppermute x4, waiting for transfers between devices, to_plane(): moved.append(lax.ppermute(quarter, ('front', 'row'), perm))  4.86 us
  transfers between devices with their start and end apart: 45, of which 34 were waited for; matrix products, arithmetic and copies ran while one was open for 0% of the time, Pallas kernels for 10%

profile of v9, /device:TPU:0, one launch (start us, length us, event | category | flops | bytes accessed | tf_op | source)
XLA Modules:
  0.0 220.6 jit_solution(8993961266682131895)
XLA Ops:
  0.6 3.1 %collective-permute-start = (bf16[512,384]{1,0:T(8,128)(2,1)}, bf16[512,384]{1,0:T(8,128)(2,1)S(1)}, u32[]{:S(2)}, u32[]{:S(2)}) collective-permute-start(bf16[512,384]{1,0:T(8,128)(2,1)} %refs_0_.1), channel_id=1, source_target_pairs={{0,1},{1,2},{2,3},{3,0},{4,5},{5,6},{6,7},{7,4},{8,9},{9,10},{10,1... | collective-permute-start | bytes 1179656 | tf_op jit(solution)/shard_map/ppermute | solution.py:46
  3.7 2.1 collective-permute-start.1
  5.8 10.1 %collective-permute-done.refs_1_ = bf16[512,384]{1,0:T(8,128)(2,1)S(1)} collective-permute-done((bf16[512,384]{1,0:T(8,128)(2,1)}, bf16[512,384]{1,0:T(8,128)(2,1)S(1)}, u32[]{:S(2)}, u32[]{:S(2)}) %collective-permute-start) | collective-permute-done | bytes 393248 | tf_op jit(solution)/shard_map/ppermute | solution.py:46
  16.0 7.1 %collective-permute-done.1.refs_2_ = bf16[512,384]{1,0:T(8,128)(2,1)S(1)} collective-permute-done((bf16[512,384]{1,0:T(8,128)(2,1)}, bf16[512,384]{1,0:T(8,128)(2,1)S(1)}, u32[]{:S(2)}, u32[]{:S(2)}) %collective-permute-start.1) | collective-permute-done | bytes 393248 | tf_op jit(solution)/shard_map/ppermute | solution.py:46
  23.1 1.6 copy-done.1
  25.7 1.5 shard_map.77.refs_0_
  27.3 4.7 %collective-permute-done.2.refs_1_ = bf16[512,384]{1,0:T(8,128)(2,1)S(1)} collective-permute-done((bf16[512,384]{1,0:T(8,128)(2,1)S(1)}, bf16[512,384]{1,0:T(8,128)(2,1)S(1)}, u32[]{:S(2)}, u32[]{:S(2)}) %collective-permute-start.2) | collective-permute-done | bytes 393248 | tf_op jit(solution)/shard_map/ppermute | solution.py:46
  32.0 1.7 shard_map.78
  33.7 3.8 %collective-permute-start.3 = (bf16[512,384]{1,0:T(8,128)(2,1)}, bf16[512,384]{1,0:T(8,128)(2,1)}, u32[]{:S(2)}, u32[]{:S(2)}) collective-permute-start(bf16[512,384]{1,0:T(8,128)(2,1)} %get-tuple-element.31.refs_0_), channel_id=1, source_target_pairs={{0,3},{1,0},{2,1},{3,2},{4,7},{5,4},{6,5},{7,6},{8,11},{9,8},{10,9... | collective-permute-start | bytes 1179656 | tf_op jit(solution)/shard_map/ppermute | solution.py:46
  37.5 10.2 %collective-permute-done.4.refs_1_ = bf16[512,384]{1,0:T(8,128)(2,1)S(1)} collective-permute-done((bf16[512,384]{1,0:T(8,128)(2,1)}, bf16[512,384]{1,0:T(8,128)(2,1)S(1)}, u32[]{:S(2)}, u32[]{:S(2)}) %collective-permute-start.4) | collective-permute-done | bytes 393248 | tf_op jit(solution)/shard_map/ppermute | solution.py:46
  47.8 2.8 %copy-done = bf16[1536,2048]{1,0:T(8,128)(2,1)S(1)} copy-done((bf16[1536,2048]{1,0:T(8,128)(2,1)S(1)}, bf16[1536,2048]{1,0:T(8,128)(2,1)}, u32[]{:S(2)}) %copy-start) | copy-done | bytes 6291480
  50.6 4.0 %shard_map.79 = (f32[1536,384]{1,0:T(8,128)S(1)}, f32[384,384]{1,0:T(8,128)S(1)}) custom-call(s32[2]{0:T(128)S(1)} %pad_add_fusion.at_ref, bf16[1536,2048]{1,0:T(8,128)(2,1)S(1)} %copy-done, bf16[512,384]{1,0:T(8,128)(2,1)} %get-tuple-element.31.refs_0_, bf16[512,384]{1,0:T(8,128)(2,1)S(1)} %collective-permute-done.4.refs_1_, f32[3072,384]{1,0:T(8,128)} %refs_2_.2), custom_call_target="tpu_custom_call" | custom-call | flops 1207959552 | bytes 3145728 | tf_op jit(solution)/shard_map/pallas_call | solution.py:29
  54.6 5.2 %shard_map.80 = (f32[1536,384]{1,0:T(8,128)S(1)}, bf16[1536,3072]{1,0:T(8,128)(2,1)S(1)}) custom-call(s32[2]{0:T(128)S(1)} %pad_add_fusion.at_ref, bf16[1536,2048]{1,0:T(8,128)(2,1)S(1)} %bitcast.5, bf16[512,384]{1,0:T(8,128)(2,1)} %collective-permute-done.3.refs_0_, f32[1536,384]{1,0:T(8,128)S(1)} %get-tuple-element.32.refs_1_, bf16[1536,3072]{1,0:T(8,128)(2,1)} %refs_2_.3), custom_call_target="tpu_custom_call" | custom-call | flops 603979776 | bytes 1572864 | tf_op jit(solution)/shard_map/pallas_call | solution.py:29
  59.8 1.6 collective-permute-done.5.refs_0_
  61.4 2.4 %shard_map.81 = (bf16[1536,384]{1,0:T(8,128)(2,1)S(1)}, bf16[1536,384]{1,0:T(8,128)(2,1)S(1)}) custom-call(s32[2]{0:T(128)S(1)} %pad_add_fusion.at_ref, s32[12]{0:T(128)S(1)} %subtract_bitcast_fusion.index_ref, bf16[1536,2048]{1,0:T(8,128)(2,1)S(1)} %bitcast.5, bf16[512,384]{1,0:T(8,128)(2,1)S(1)} %collective-permute-done.5.refs_0_, ...), custom_call_target="tpu_custom_call" | custom-call | flops 603979776 | bytes 1572864 | tf_op jit(solution)/shard_map/pallas_call | solution.py:29
  63.9 2.8 %collective-permute-done.6.came_ref = bf16[1536,384]{1,0:T(8,128)(2,1)S(1)} collective-permute-done((bf16[1536,384]{1,0:T(8,128)(2,1)S(1)}, bf16[1536,384]{1,0:T(8,128)(2,1)S(1)}, u32[]{:S(2)}, u32[]{:S(2)}) %collective-permute-start.6) | collective-permute-done | bytes 1179680 | tf_op jit(solution)/shard_map/ppermute | solution.py:50
  66.8 1.6 collective-permute-start.8
  68.3 1.5 collective-permute-start.9
  71.0 2.2 collective-permute-done.8.low_ref
  73.2 1.8 collective-permute-done.9.high_ref
  75.2 1.6 collective-permute-start.10
  78.2 2.2 collective-permute-done.10.refs_1_
  80.4 1.5 collective-permute-done.11.refs_2_
  82.8 2.0 collective-permute-start.13
  84.8 1.5 collective-permute-start.16
  86.3 1.8 collective-permute-done.15.refs_2_
  88.9 1.1 collective-permute-start.18
  90.5 2.8 %collective-permute-done.17.refs_4_ = bf16[192,384]{1,0:T(8,128)(2,1)S(1)} collective-permute-done((bf16[192,384]{1,0:T(8,128)(2,1)S(1)}, bf16[192,384]{1,0:T(8,128)(2,1)S(1)}, u32[]{:S(2)}, u32[]{:S(2)}) %collective-permute-start.17) | collective-permute-done | bytes 147488 | tf_op jit(solution)/shard_map/ppermute | solution.py:50
  94.7 2.3 %collective-permute-done.19.refs_4_ = bf16[384,384]{1,0:T(8,128)(2,1)S(1)} collective-permute-done((bf16[384,384]{1,0:T(8,128)(2,1)S(1)}, bf16[384,384]{1,0:T(8,128)(2,1)S(1)}, u32[]{:S(2)}, u32[]{:S(2)}) %collective-permute-start.19) | collective-permute-done | bytes 294944 | tf_op jit(solution)/shard_map/ppermute | solution.py:50
  97.0 2.5 %shard_map.89 = bf16[384,384]{1,0:T(8,128)(2,1)S(1)} custom-call(s32[2]{0:T(128)S(1)} %pad_add_fusion.at_ref, bf16[1536,3072]{1,0:T(8,128)(2,1)S(1)} %get-tuple-element.33.a_ref, bf16[384,384]{1,0:T(8,128)(2,1)S(1)} %get-tuple-element.46.refs_0_, bf16[1152,384]{1,0:T(8,128)(2,1)S(1)} %shard_map.87.refs_1_.refs_2_.refs_3_, ...), custom_call_target="tpu_custom_call" | custom-call | flops 905969664 | bytes 2359296 | tf_op jit(solution)/shard_map/pallas_call | solution.py:29
  99.6 2.3 %collective-permute-start.21 = (bf16[384,384]{1,0:T(8,128)(2,1)S(1)}, bf16[384,384]{1,0:T(8,128)(2,1)S(1)}, u32[]{:S(2)}, u32[]{:S(2)}) collective-permute-start(bf16[384,384]{1,0:T(8,128)(2,1)S(1)} %shard_map.89), channel_id=1, source_target_pairs={{0,3},{1,0},{2,1},{3,2},{4,7},{5,4},{6,5},{7,6},{8,11},{9,8},{10,9... | collective-permute-start | bytes 884744 | tf_op jit(solution)/shard_map/ppermute | solution.py:46
  101.8 2.5 %shard_map.90 = bf16[384,384]{1,0:T(8,128)(2,1)S(1)} custom-call(s32[2]{0:T(128)S(1)} %pad_add_fusion.at_ref, bf16[1536,3072]{1,0:T(8,128)(2,1)S(1)} %get-tuple-element.33.a_ref, bf16[384,384]{1,0:T(8,128)(2,1)S(1)} %get-tuple-element.46.refs_0_, bf16[1152,384]{1,0:T(8,128)(2,1)S(1)} %shard_map.87.refs_1_.refs_2_.refs_3_, ...), custom_call_target="tpu_custom_call" | custom-call | flops 905969664 | bytes 2359296 | tf_op jit(solution)/shard_map/pallas_call | solution.py:29
  104.4 3.8 %shard_map.88 = (f32[384,384]{1,0:T(8,128)S(1)}, f32[384,384]{1,0:T(8,128)S(1)}) custom-call(s32[2]{0:T(128)S(1)} %pad_add_fusion.at_ref, bf16[1536,3072]{1,0:T(8,128)(2,1)S(1)} %get-tuple-element.33.a_ref, bf16[384,384]{1,0:T(8,128)(2,1)S(1)} %get-tuple-element.46.refs_0_, bf16[1152,384]{1,0:T(8,128)(2,1)S(1)} %shard_map.87.refs_1_.refs_2_.refs_3_, ...), custom_call_target="tpu_custom_call" | custom-call | flops 1811939328 | bytes 4718592 | tf_op jit(solution)/shard_map/pallas_call | solution.py:29
  108.2 1.1 collective-permute-done.21
  109.3 4.3 %collective-permute-start.22 = (bf16[384,384]{1,0:T(8,128)(2,1)S(1)}, bf16[384,384]{1,0:T(8,128)(2,1)S(1)}, u32[]{:S(2)}, u32[]{:S(2)}) collective-permute-start(bf16[384,384]{1,0:T(8,128)(2,1)S(1)} %add_convert_fusion.2), channel_id=1, source_target_pairs={{0,3},{1,0},{2,1},{3,2},{4,7},{5,4},{6,5},{7,6},{8,11},{9,8},{10,9... | collective-permute-start | bytes 884744 | tf_op jit(solution)/shard_map/ppermute | solution.py:46
  113.7 2.5 %collective-permute-done.23 = bf16[384,384]{1,0:T(8,128)(2,1)S(1)} collective-permute-done((bf16[384,384]{1,0:T(8,128)(2,1)S(1)}, bf16[384,384]{1,0:T(8,128)(2,1)S(1)}, u32[]{:S(2)}, u32[]{:S(2)}) %collective-permute-start.23) | collective-permute-done | bytes 294944 | tf_op jit(solution)/shard_map/ppermute | solution.py:46
  116.2 5.7 %collective-permute-done.22 = bf16[384,384]{1,0:T(8,128)(2,1)S(1)} collective-permute-done((bf16[384,384]{1,0:T(8,128)(2,1)S(1)}, bf16[384,384]{1,0:T(8,128)(2,1)S(1)}, u32[]{:S(2)}, u32[]{:S(2)}) %collective-permute-start.22) | collective-permute-done | bytes 294944 | tf_op jit(solution)/shard_map/ppermute | solution.py:46
  122.8 1.2 collective-permute-start.29
  124.0 1.6 collective-permute-start.27
  127.0 1.7 collective-permute-done.29
  128.7 4.0 %collective-permute-start.30 = (bf16[96,384]{1,0:T(8,128)(2,1)S(1)}, bf16[96,384]{1,0:T(8,128)(2,1)S(1)}, u32[]{:S(2)}, u32[]{:S(2)}) collective-permute-start(bf16[96,384]{1,0:T(8,128)(2,1)S(1)} %collective-permute-done.29), channel_id=1, source_target_pairs={{0,3},{1,11},{2,19},{3,27},{4,7},{5,15},{6,23},{7,31},{8,2},{9,10}... | collective-permute-start | bytes 221192 | tf_op jit(solution)/shard_map/ppermute | solution.py:92
  133.6 4.9 %collective-permute-done.26 = bf16[96,384]{1,0:T(8,128)(2,1)S(1)} collective-permute-done((bf16[96,384]{1,0:T(8,128)(2,1)S(1)}, bf16[96,384]{1,0:T(8,128)(2,1)S(1)}, u32[]{:S(2)}, u32[]{:S(2)}) %collective-permute-start.26) | collective-permute-done | bytes 73760 | tf_op jit(solution)/shard_map/ppermute | solution.py:92
  138.5 3.4 %collective-permute-start.33 = (bf16[192,384]{1,0:T(8,128)(2,1)S(1)}, bf16[192,384]{1,0:T(8,128)(2,1)S(1)}, u32[]{:S(2)}, u32[]{:S(2)}) collective-permute-start(bf16[192,384]{1,0:T(8,128)(2,1)S(1)} %constant_dynamic-update-slice_fusion.low_ref), channel_id=1, source_target_pairs={{0,16},{4,20},{8,24},{12,28},{16,0},{20,4},{24,8},{28,12},{1,17},{... | collective-permute-start | bytes 442376 | tf_op jit(solution)/shard_map/ppermute | solution.py:50
  141.9 1.8 collective-permute-start.32
  144.2 2.3 %collective-permute-done.33.refs_2_ = bf16[192,384]{1,0:T(8,128)(2,1)S(1)} collective-permute-done((bf16[192,384]{1,0:T(8,128)(2,1)S(1)}, bf16[192,384]{1,0:T(8,128)(2,1)S(1)}, u32[]{:S(2)}, u32[]{:S(2)}) %collective-permute-start.33) | collective-permute-done | bytes 147488 | tf_op jit(solution)/shard_map/ppermute | solution.py:50
  146.5 1.8 collective-permute-start.35
  148.3 1.3 collective-permute-start.36
  149.9 1.7 collective-permute-done.35.refs_4_
  151.6 1.8 collective-permute-done.36.refs_5_
  154.1 2.3 %collective-permute-done.37.refs_4_ = bf16[384,384]{1,0:T(8,128)(2,1)S(1)} collective-permute-done((bf16[384,384]{1,0:T(8,128)(2,1)S(1)}, bf16[384,384]{1,0:T(8,128)(2,1)S(1)}, u32[]{:S(2)}, u32[]{:S(2)}) %collective-permute-start.37) | collective-permute-done | bytes 294944 | tf_op jit(solution)/shard_map/ppermute | solution.py:50
  156.4 2.0 shard_map.93
  158.4 4.1 %collective-permute-start.39 = (bf16[384,512]{1,0:T(8,128)(2,1)S(1)}, bf16[384,512]{1,0:T(8,128)(2,1)S(1)}, u32[]{:S(2)}, u32[]{:S(2)}) collective-permute-start(bf16[384,512]{1,0:T(8,128)(2,1)S(1)} %get-tuple-element.56), channel_id=1, source_target_pairs={{0,3},{1,0},{2,1},{3,2},{4,7},{5,4},{6,5},{7,6},{8,11},{9,8},{10,9... | collective-permute-start | bytes 1179656 | tf_op jit(solution)/shard_map/ppermute | solution.py:46
  162.5 1.3 shard_map.95
  164.1 2.0 shard_map.94
  166.0 6.0 %collective-permute-done.39 = bf16[384,512]{1,0:T(8,128)(2,1)S(1)} collective-permute-done((bf16[384,512]{1,0:T(8,128)(2,1)S(1)}, bf16[384,512]{1,0:T(8,128)(2,1)S(1)}, u32[]{:S(2)}, u32[]{:S(2)}) %collective-permute-start.39) | collective-permute-done | bytes 393248 | tf_op jit(solution)/shard_map/ppermute | solution.py:46
  172.1 4.3 %collective-permute-start.40 = (bf16[384,512]{1,0:T(8,128)(2,1)S(1)}, bf16[384,512]{1,0:T(8,128)(2,1)S(1)}, u32[]{:S(2)}, u32[]{:S(2)}) collective-permute-start(bf16[384,512]{1,0:T(8,128)(2,1)S(1)} %add_convert_fusion.1), channel_id=1, source_target_pairs={{0,3},{1,0},{2,1},{3,2},{4,7},{5,4},{6,5},{7,6},{8,11},{9,8},{10,9... | collective-permute-start | bytes 1179656 | tf_op jit(solution)/shard_map/ppermute | solution.py:46
  176.5 4.4 %collective-permute-done.41 = bf16[384,512]{1,0:T(8,128)(2,1)S(1)} collective-permute-done((bf16[384,512]{1,0:T(8,128)(2,1)S(1)}, bf16[384,512]{1,0:T(8,128)(2,1)S(1)}, u32[]{:S(2)}, u32[]{:S(2)}) %collective-permute-start.41) | collective-permute-done | bytes 393248 | tf_op jit(solution)/shard_map/ppermute | solution.py:46
  180.9 7.9 %collective-permute-done.40 = bf16[384,512]{1,0:T(8,128)(2,1)S(1)} collective-permute-done((bf16[384,512]{1,0:T(8,128)(2,1)S(1)}, bf16[384,512]{1,0:T(8,128)(2,1)S(1)}, u32[]{:S(2)}, u32[]{:S(2)}) %collective-permute-start.40) | collective-permute-done | bytes 393248 | tf_op jit(solution)/shard_map/ppermute | solution.py:46
  189.6 3.3 %collective-permute-start.43 = (bf16[384,512]{1,0:T(8,128)(2,1)S(1)}, bf16[384,512]{1,0:T(8,128)(2,1)S(1)}, u32[]{:S(2)}, u32[]{:S(2)}) collective-permute-start(bf16[384,512]{1,0:T(8,128)(2,1)S(1)} %add_convert_fusion.refs_1_), channel_id=1, source_target_pairs={{0,3},{1,0},{2,1},{3,2},{4,7},{5,4},{6,5},{7,6},{8,11},{9,8},{10,9... | collective-permute-start | bytes 1179656 | tf_op jit(solution)/shard_map/ppermute | solution.py:46
  192.9 10.0 %collective-permute-done.42.refs_2_ = bf16[384,512]{1,0:T(8,128)(2,1)S(1)} collective-permute-done((bf16[384,512]{1,0:T(8,128)(2,1)S(1)}, bf16[384,512]{1,0:T(8,128)(2,1)S(1)}, u32[]{:S(2)}, u32[]{:S(2)}) %collective-permute-start.42) | collective-permute-done | bytes 393248 | tf_op jit(solution)/shard_map/ppermute | solution.py:46
  202.8 5.9 %collective-permute-done.43.refs_3_ = bf16[384,512]{1,0:T(8,128)(2,1)S(1)} collective-permute-done((bf16[384,512]{1,0:T(8,128)(2,1)S(1)}, bf16[384,512]{1,0:T(8,128)(2,1)S(1)}, u32[]{:S(2)}, u32[]{:S(2)}) %collective-permute-start.43) | collective-permute-done | bytes 393248 | tf_op jit(solution)/shard_map/ppermute | solution.py:46
  208.8 1.5 shard_map.96.refs_0_
  210.3 8.4 %collective-permute-done.44.refs_1_ = bf16[384,512]{1,0:T(8,128)(2,1)S(1)} collective-permute-done((bf16[384,512]{1,0:T(8,128)(2,1)S(1)}, bf16[384,512]{1,0:T(8,128)(2,1)S(1)}, u32[]{:S(2)}, u32[]{:S(2)}) %collective-permute-start.44) | collective-permute-done | bytes 393248 | tf_op jit(solution)/shard_map/ppermute | solution.py:46
  218.7 1.9 shard_map.97
  (73 shorter events, 13.7 us)
Async XLA Ops:
  0.6 15.3 %collective-permute-start = (bf16[512,384]{1,0:T(8,128)(2,1)}, bf16[512,384]{1,0:T(8,128)(2,1)S(1)}, u32[]{:S(2)}, u32[]{:S(2)}) collective-permute-start(bf16[512,384]{1,0:T(8,128)(2,1)} %refs_0_.1), channel_id=1, source_target_pairs={{0,1},{1,2},{2,3},{3,0},{4,5},{5,6},{6,7},{7,4},{8,9},{9,10},{10,1... | collective-permute-start | bytes 1179656 | tf_op jit(solution)/shard_map/ppermute | solution.py:46
  3.7 19.4 %collective-permute-start.1 = (bf16[512,384]{1,0:T(8,128)(2,1)}, bf16[512,384]{1,0:T(8,128)(2,1)S(1)}, u32[]{:S(2)}, u32[]{:S(2)}) collective-permute-start(bf16[512,384]{1,0:T(8,128)(2,1)} %refs_0_.1), channel_id=1, source_target_pairs={{0,3},{1,0},{2,1},{3,2},{4,7},{5,4},{6,5},{7,6},{8,11},{9,8},{10,9... | collective-permute-start | bytes 1179656 | tf_op jit(solution)/shard_map/ppermute | solution.py:46
  15.9 16.0 %collective-permute-start.2 = (bf16[512,384]{1,0:T(8,128)(2,1)S(1)}, bf16[512,384]{1,0:T(8,128)(2,1)S(1)}, u32[]{:S(2)}, u32[]{:S(2)}) collective-permute-start(bf16[512,384]{1,0:T(8,128)(2,1)S(1)} %collective-permute-done.refs_1_), channel_id=1, source_target_pairs={{0,1},{1,2},{2,3},{3,0},{4,5},{5,6},{6,7},{7,4},{8,9},{9,10},{10,1... | collective-permute-start | bytes 1179656 | tf_op jit(solution)/shard_map/ppermute | solution.py:46
  23.1 1.6 copy-start.1
  24.7 1.0 copy-start.3
  25.7 28.8 %slice-start = ((s8[6291456]{0:T(1024)(128)(4,1)}), s8[2097152]{0:T(1024)(128)(4,1)S(1)}, s32[]{:S(2)}) async-start(s8[6291456]{0:T(1024)(128)(4,1)} %bitcast.4), calls=%async_computation | async-start | bytes 4194304
  27.2 20.5 %copy-start.4 = (s32[1,12]{1,0:T(1,128)S(1)}, s32[1,12]{1,0:T(1,128)}, u32[]{:S(2)}) copy-start(s32[1,12]{1,0:T(1,128)} %param.11) | copy-start | bytes 148
  33.7 14.1 %collective-permute-start.4 = (bf16[512,384]{1,0:T(8,128)(2,1)}, bf16[512,384]{1,0:T(8,128)(2,1)S(1)}, u32[]{:S(2)}, u32[]{:S(2)}) collective-permute-start(bf16[512,384]{1,0:T(8,128)(2,1)} %get-tuple-element.31.refs_0_), channel_id=1, source_target_pairs={{0,1},{1,2},{2,3},{3,0},{4,5},{5,6},{6,7},{7,4},{8,9},{9,10},{10,1... | collective-permute-start | bytes 1179656 | tf_op jit(solution)/shard_map/ppermute | solution.py:46
  33.7 20.8 %collective-permute-start.3 = (bf16[512,384]{1,0:T(8,128)(2,1)}, bf16[512,384]{1,0:T(8,128)(2,1)}, u32[]{:S(2)}, u32[]{:S(2)}) collective-permute-start(bf16[512,384]{1,0:T(8,128)(2,1)} %get-tuple-element.31.refs_0_), channel_id=1, source_target_pairs={{0,3},{1,0},{2,1},{3,2},{4,7},{5,4},{6,5},{7,6},{8,11},{9,8},{10,9... | collective-permute-start | bytes 1179656 | tf_op jit(solution)/shard_map/ppermute | solution.py:46
  47.8 13.6 %collective-permute-start.5 = (bf16[512,384]{1,0:T(8,128)(2,1)S(1)}, bf16[512,384]{1,0:T(8,128)(2,1)S(1)}, u32[]{:S(2)}, u32[]{:S(2)}) collective-permute-start(bf16[512,384]{1,0:T(8,128)(2,1)S(1)} %collective-permute-done.4.refs_1_), channel_id=1, source_target_pairs={{0,1},{1,2},{2,3},{3,0},{4,5},{5,6},{6,7},{7,4},{8,9},{9,10},{10,1... | collective-permute-start | bytes 1179656 | tf_op jit(solution)/shard_map/ppermute | solution.py:46
  47.8 2.8 %copy-start = (bf16[1536,2048]{1,0:T(8,128)(2,1)S(1)}, bf16[1536,2048]{1,0:T(8,128)(2,1)}, u32[]{:S(2)}) copy-start(bf16[1536,2048]{1,0:T(8,128)(2,1)} %a_ref.17) | copy-start | bytes 18874372
  50.6 4.0 %slice-start.1 = ((s8[6291456]{0:T(1024)(128)(4,1)}), s8[4194304]{0:T(1024)(128)(4,1)S(1)}, s32[]{:S(2)}) async-start(s8[6291456]{0:T(1024)(128)(4,1)} %bitcast.4), calls=%async_computation.1 | async-start | bytes 8388608
  63.8 2.9 %collective-permute-start.6 = (bf16[1536,384]{1,0:T(8,128)(2,1)S(1)}, bf16[1536,384]{1,0:T(8,128)(2,1)S(1)}, u32[]{:S(2)}, u32[]{:S(2)}) collective-permute-start(bf16[1536,384]{1,0:T(8,128)(2,1)S(1)} %get-tuple-element.37), channel_id=1, source_target_pairs={{0,4},{4,0},{8,12},{12,8},{16,20},{20,16},{24,28},{28,24},{1,5},{5... | collective-permute-start | bytes 3538952 | tf_op jit(solution)/shard_map/ppermute | solution.py:50
  66.8 6.5 %collective-permute-start.8 = (bf16[192,384]{1,0:T(8,128)(2,1)S(1)}, bf16[192,384]{1,0:T(8,128)(2,1)S(1)}, u32[]{:S(2)}, u32[]{:S(2)}) collective-permute-start(bf16[192,384]{1,0:T(8,128)(2,1)S(1)} %get-tuple-element.39), channel_id=1, source_target_pairs={{0,8},{4,12},{8,0},{12,4},{16,24},{20,28},{24,16},{28,20},{1,9},{5... | collective-permute-start | bytes 442376 | tf_op jit(solution)/shard_map/ppermute | solution.py:50
  68.3 6.7 %collective-permute-start.9 = (bf16[192,384]{1,0:T(8,128)(2,1)S(1)}, bf16[192,384]{1,0:T(8,128)(2,1)S(1)}, u32[]{:S(2)}, u32[]{:S(2)}) collective-permute-start(bf16[192,384]{1,0:T(8,128)(2,1)S(1)} %get-tuple-element.40), channel_id=1, source_target_pairs={{0,16},{4,20},{8,24},{12,28},{16,0},{20,4},{24,8},{28,12},{1,17},{... | collective-permute-start | bytes 442376 | tf_op jit(solution)/shard_map/ppermute | solution.py:50
  69.9 7.4 %collective-permute-start.7 = (bf16[192,384]{1,0:T(8,128)(2,1)S(1)}, bf16[192,384]{1,0:T(8,128)(2,1)S(1)}, u32[]{:S(2)}, u32[]{:S(2)}) collective-permute-start(bf16[192,384]{1,0:T(8,128)(2,1)S(1)} %get-tuple-element.38), channel_id=1, source_target_pairs={{0,8},{4,12},{8,0},{12,4},{16,24},{20,28},{24,16},{28,20},{1,9},{5... | collective-permute-start | bytes 442376 | tf_op jit(solution)/shard_map/ppermute | solution.py:50
  70.5 7.7 %collective-permute-start.12 = (bf16[192,384]{1,0:T(8,128)(2,1)S(1)}, bf16[192,384]{1,0:T(8,128)(2,1)S(1)}, u32[]{:S(2)}, u32[]{:S(2)}) collective-permute-start(bf16[192,384]{1,0:T(8,128)(2,1)S(1)} %get-tuple-element.43), channel_id=1, source_target_pairs={{0,16},{4,20},{8,24},{12,28},{16,0},{20,4},{24,8},{28,12},{1,17},{... | collective-permute-start | bytes 442376 | tf_op jit(solution)/shard_map/ppermute | solution.py:50
  75.2 5.2 %collective-permute-start.10 = (bf16[192,384]{1,0:T(8,128)(2,1)S(1)}, bf16[192,384]{1,0:T(8,128)(2,1)S(1)}, u32[]{:S(2)}, u32[]{:S(2)}) collective-permute-start(bf16[192,384]{1,0:T(8,128)(2,1)S(1)} %get-tuple-element.41), channel_id=1, source_target_pairs={{0,16},{4,20},{8,24},{12,28},{16,0},{20,4},{24,8},{28,12},{1,17},{... | collective-permute-start | bytes 442376 | tf_op jit(solution)/shard_map/ppermute | solution.py:50
  76.8 5.1 %collective-permute-start.11 = (bf16[192,384]{1,0:T(8,128)(2,1)S(1)}, bf16[192,384]{1,0:T(8,128)(2,1)S(1)}, u32[]{:S(2)}, u32[]{:S(2)}) collective-permute-start(bf16[192,384]{1,0:T(8,128)(2,1)S(1)} %get-tuple-element.42), channel_id=1, source_target_pairs={{0,8},{4,12},{8,0},{12,4},{16,24},{20,28},{24,16},{28,20},{1,9},{5... | collective-permute-start | bytes 442376 | tf_op jit(solution)/shard_map/ppermute | solution.py:50
  82.1 6.0 %collective-permute-start.15 = (bf16[192,384]{1,0:T(8,128)(2,1)S(1)}, bf16[192,384]{1,0:T(8,128)(2,1)S(1)}, u32[]{:S(2)}, u32[]{:S(2)}) collective-permute-start(bf16[192,384]{1,0:T(8,128)(2,1)S(1)} %get-tuple-element.44.low_ref), channel_id=1, source_target_pairs={{0,16},{4,20},{8,24},{12,28},{16,0},{20,4},{24,8},{28,12},{1,17},{... | collective-permute-start | bytes 442376 | tf_op jit(solution)/shard_map/ppermute | solution.py:50
  82.7 6.2 %collective-permute-start.14 = (bf16[192,384]{1,0:T(8,128)(2,1)S(1)}, bf16[192,384]{1,0:T(8,128)(2,1)S(1)}, u32[]{:S(2)}, u32[]{:S(2)}) collective-permute-start(bf16[192,384]{1,0:T(8,128)(2,1)S(1)} %get-tuple-element.45.high_ref), channel_id=1, source_target_pairs={{0,8},{4,12},{8,0},{12,4},{16,24},{20,28},{24,16},{28,20},{1,9},{5... | collective-permute-start | bytes 442376 | tf_op jit(solution)/shard_map/ppermute | solution.py:50
  82.8 7.7 %collective-permute-start.13 = (bf16[192,384]{1,0:T(8,128)(2,1)S(1)}, bf16[192,384]{1,0:T(8,128)(2,1)S(1)}, u32[]{:S(2)}, u32[]{:S(2)}) collective-permute-start(bf16[192,384]{1,0:T(8,128)(2,1)S(1)} %get-tuple-element.47), channel_id=1, source_target_pairs={{0,8},{4,12},{8,0},{12,4},{16,24},{20,28},{24,16},{28,20},{1,9},{5... | collective-permute-start | bytes 442376 | tf_op jit(solution)/shard_map/ppermute | solution.py:50
  84.8 5.7 %collective-permute-start.16 = (bf16[192,384]{1,0:T(8,128)(2,1)S(1)}, bf16[192,384]{1,0:T(8,128)(2,1)S(1)}, u32[]{:S(2)}, u32[]{:S(2)}) collective-permute-start(bf16[192,384]{1,0:T(8,128)(2,1)S(1)} %get-tuple-element.48), channel_id=1, source_target_pairs={{0,16},{4,20},{8,24},{12,28},{16,0},{20,4},{24,8},{28,12},{1,17},{... | collective-permute-start | bytes 442376 | tf_op jit(solution)/shard_map/ppermute | solution.py:50
  88.1 5.1 %collective-permute-start.17 = (bf16[192,384]{1,0:T(8,128)(2,1)S(1)}, bf16[192,384]{1,0:T(8,128)(2,1)S(1)}, u32[]{:S(2)}, u32[]{:S(2)}) collective-permute-start(bf16[192,384]{1,0:T(8,128)(2,1)S(1)} %collective-permute-done.15.refs_2_), channel_id=1, source_target_pairs={{0,8},{4,12},{8,0},{12,4},{16,24},{20,28},{24,16},{28,20},{1,9},{5... | collective-permute-start | bytes 442376 | tf_op jit(solution)/shard_map/ppermute | solution.py:50
  88.9 5.1 %collective-permute-start.18 = (bf16[192,384]{1,0:T(8,128)(2,1)S(1)}, bf16[192,384]{1,0:T(8,128)(2,1)S(1)}, u32[]{:S(2)}, u32[]{:S(2)}) collective-permute-start(bf16[192,384]{1,0:T(8,128)(2,1)S(1)} %collective-permute-done.14.refs_1_), channel_id=1, source_target_pairs={{0,16},{4,20},{8,24},{12,28},{16,0},{20,4},{24,8},{28,12},{1,17},{... | collective-permute-start | bytes 442376 | tf_op jit(solution)/shard_map/ppermute | solution.py:50
  94.1 2.9 %collective-permute-start.20 = (bf16[1152,384]{1,0:T(8,128)(2,1)S(1)}, bf16[1152,384]{1,0:T(8,128)(2,1)S(1)}, u32[]{:S(2)}, u32[]{:S(2)}) collective-permute-start(bf16[1152,384]{1,0:T(8,128)(2,1)S(1)} %shard_map.87.refs_1_.refs_2_.refs_3_), channel_id=1, source_target_pairs={{0,4},{4,0},{8,12},{12,8},{16,20},{20,16},{24,28},{28,24},{1,5},{5... | collective-permute-start | bytes 2654216 | tf_op jit(solution)/shard_map/ppermute | solution.py:50
  94.2 2.8 %collective-permute-start.19 = (bf16[384,384]{1,0:T(8,128)(2,1)S(1)}, bf16[384,384]{1,0:T(8,128)(2,1)S(1)}, u32[]{:S(2)}, u32[]{:S(2)}) collective-permute-start(bf16[384,384]{1,0:T(8,128)(2,1)S(1)} %get-tuple-element.46.refs_0_), channel_id=1, source_target_pairs={{0,4},{4,0},{8,12},{12,8},{16,20},{20,16},{24,28},{28,24},{1,5},{5... | collective-permute-start | bytes 884744 | tf_op jit(solution)/shard_map/ppermute | solution.py:50
  99.6 9.7 %collective-permute-start.21 = (bf16[384,384]{1,0:T(8,128)(2,1)S(1)}, bf16[384,384]{1,0:T(8,128)(2,1)S(1)}, u32[]{:S(2)}, u32[]{:S(2)}) collective-permute-start(bf16[384,384]{1,0:T(8,128)(2,1)S(1)} %shard_map.89), channel_id=1, source_target_pairs={{0,3},{1,0},{2,1},{3,2},{4,7},{5,4},{6,5},{7,6},{8,11},{9,8},{10,9... | collective-permute-start | bytes 884744 | tf_op jit(solution)/shard_map/ppermute | solution.py:46
  104.4 11.8 %collective-permute-start.23 = (bf16[384,384]{1,0:T(8,128)(2,1)S(1)}, bf16[384,384]{1,0:T(8,128)(2,1)S(1)}, u32[]{:S(2)}, u32[]{:S(2)}) collective-permute-start(bf16[384,384]{1,0:T(8,128)(2,1)S(1)} %shard_map.90), channel_id=1, source_target_pairs={{0,1},{1,2},{2,3},{3,0},{4,5},{5,6},{6,7},{7,4},{8,9},{9,10},{10,1... | collective-permute-start | bytes 884744 | tf_op jit(solution)/shard_map/ppermute | solution.py:46
  109.3 12.5 %collective-permute-start.22 = (bf16[384,384]{1,0:T(8,128)(2,1)S(1)}, bf16[384,384]{1,0:T(8,128)(2,1)S(1)}, u32[]{:S(2)}, u32[]{:S(2)}) collective-permute-start(bf16[384,384]{1,0:T(8,128)(2,1)S(1)} %add_convert_fusion.2), channel_id=1, source_target_pairs={{0,3},{1,0},{2,1},{3,2},{4,7},{5,4},{6,5},{7,6},{8,11},{9,8},{10,9... | collective-permute-start | bytes 884744 | tf_op jit(solution)/shard_map/ppermute | solution.py:46
  122.8 5.9 %collective-permute-start.29 = (bf16[96,384]{1,0:T(8,128)(2,1)S(1)}, bf16[96,384]{1,0:T(8,128)(2,1)S(1)}, u32[]{:S(2)}, u32[]{:S(2)}) collective-permute-start(bf16[96,384]{1,0:T(8,128)(2,1)S(1)} %get-tuple-element.60), channel_id=1, source_target_pairs={{0,24},{4,28},{8,16},{12,20},{16,8},{20,12},{24,0},{28,4},{1,25},{... | collective-permute-start | bytes 221192 | tf_op jit(solution)/shard_map/ppermute | solution.py:50
  124.0 8.7 %collective-permute-start.27 = (bf16[96,384]{1,0:T(8,128)(2,1)S(1)}, bf16[96,384]{1,0:T(8,128)(2,1)S(1)}, u32[]{:S(2)}, u32[]{:S(2)}) collective-permute-start(bf16[96,384]{1,0:T(8,128)(2,1)S(1)} %get-tuple-element.61), channel_id=1, source_target_pairs={{0,16},{4,20},{8,24},{12,28},{16,0},{20,4},{24,8},{28,12},{1,17},{... | collective-permute-start | bytes 221192 | tf_op jit(solution)/shard_map/ppermute | solution.py:50
  125.6 8.0 %collective-permute-start.25 = (bf16[96,384]{1,0:T(8,128)(2,1)S(1)}, bf16[96,384]{1,0:T(8,128)(2,1)S(1)}, u32[]{:S(2)}, u32[]{:S(2)}) collective-permute-start(bf16[96,384]{1,0:T(8,128)(2,1)S(1)} %get-tuple-element.62), channel_id=1, source_target_pairs={{0,8},{4,12},{8,0},{12,4},{16,24},{20,28},{24,16},{28,20},{1,9},{5... | collective-permute-start | bytes 221192 | tf_op jit(solution)/shard_map/ppermute | solution.py:50
  126.4 7.3 %collective-permute-start.24 = (bf16[96,384]{1,0:T(8,128)(2,1)S(1)}, bf16[96,384]{1,0:T(8,128)(2,1)S(1)}, u32[]{:S(2)}, u32[]{:S(2)}) collective-permute-start(bf16[96,384]{1,0:T(8,128)(2,1)S(1)} %get-tuple-element.63), channel_id=1, source_target_pairs={{0,0},{1,8},{2,16},{3,24},{4,4},{5,12},{6,20},{7,28},{8,1},{9,9},{... | collective-permute-start | bytes 221192 | tf_op jit(solution)/shard_map/ppermute | solution.py:92
  128.7 13.2 %collective-permute-start.30 = (bf16[96,384]{1,0:T(8,128)(2,1)S(1)}, bf16[96,384]{1,0:T(8,128)(2,1)S(1)}, u32[]{:S(2)}, u32[]{:S(2)}) collective-permute-start(bf16[96,384]{1,0:T(8,128)(2,1)S(1)} %collective-permute-done.29), channel_id=1, source_target_pairs={{0,3},{1,11},{2,19},{3,27},{4,7},{5,15},{6,23},{7,31},{8,2},{9,10}... | collective-permute-start | bytes 221192 | tf_op jit(solution)/shard_map/ppermute | solution.py:92
  132.7 9.2 %collective-permute-start.28 = (bf16[96,384]{1,0:T(8,128)(2,1)S(1)}, bf16[96,384]{1,0:T(8,128)(2,1)S(1)}, u32[]{:S(2)}, u32[]{:S(2)}) collective-permute-start(bf16[96,384]{1,0:T(8,128)(2,1)S(1)} %collective-permute-done.27), channel_id=1, source_target_pairs={{0,2},{1,10},{2,18},{3,26},{4,6},{5,14},{6,22},{7,30},{8,3},{9,11}... | collective-permute-start | bytes 221192 | tf_op jit(solution)/shard_map/ppermute | solution.py:92
  133.6 4.9 %collective-permute-start.26 = (bf16[96,384]{1,0:T(8,128)(2,1)S(1)}, bf16[96,384]{1,0:T(8,128)(2,1)S(1)}, u32[]{:S(2)}, u32[]{:S(2)}) collective-permute-start(bf16[96,384]{1,0:T(8,128)(2,1)S(1)} %collective-permute-done.25), channel_id=1, source_target_pairs={{0,1},{1,9},{2,17},{3,25},{4,5},{5,13},{6,21},{7,29},{8,0},{9,8},{... | collective-permute-start | bytes 221192 | tf_op jit(solution)/shard_map/ppermute | solution.py:92
  138.5 8.0 %collective-permute-start.33 = (bf16[192,384]{1,0:T(8,128)(2,1)S(1)}, bf16[192,384]{1,0:T(8,128)(2,1)S(1)}, u32[]{:S(2)}, u32[]{:S(2)}) collective-permute-start(bf16[192,384]{1,0:T(8,128)(2,1)S(1)} %constant_dynamic-update-slice_fusion.low_ref), channel_id=1, source_target_pairs={{0,16},{4,20},{8,24},{12,28},{16,0},{20,4},{24,8},{28,12},{1,17},{... | collective-permute-start | bytes 442376 | tf_op jit(solution)/shard_map/ppermute | solution.py:50
  141.9 6.4 %collective-permute-start.32 = (bf16[192,384]{1,0:T(8,128)(2,1)S(1)}, bf16[192,384]{1,0:T(8,128)(2,1)S(1)}, u32[]{:S(2)}, u32[]{:S(2)}) collective-permute-start(bf16[192,384]{1,0:T(8,128)(2,1)S(1)} %constant_dynamic-update-slice_fusion.2.high_ref), channel_id=1, source_target_pairs={{0,8},{4,12},{8,0},{12,4},{16,24},{20,28},{24,16},{28,20},{1,9},{5... | collective-permute-start | bytes 442376 | tf_op jit(solution)/shard_map/ppermute | solution.py:50
  143.7 6.1 %collective-permute-start.31 = (bf16[192,384]{1,0:T(8,128)(2,1)S(1)}, bf16[192,384]{1,0:T(8,128)(2,1)S(1)}, u32[]{:S(2)}, u32[]{:S(2)}) collective-permute-start(bf16[192,384]{1,0:T(8,128)(2,1)S(1)} %get-tuple-element.52), channel_id=1, source_target_pairs={{0,8},{4,12},{8,0},{12,4},{16,24},{20,28},{24,16},{28,20},{1,9},{5... | collective-permute-start | bytes 442376 | tf_op jit(solution)/shard_map/ppermute | solution.py:50
  144.1 5.7 %collective-permute-start.34 = (bf16[192,384]{1,0:T(8,128)(2,1)S(1)}, bf16[192,384]{1,0:T(8,128)(2,1)S(1)}, u32[]{:S(2)}, u32[]{:S(2)}) collective-permute-start(bf16[192,384]{1,0:T(8,128)(2,1)S(1)} %get-tuple-element.53), channel_id=1, source_target_pairs={{0,16},{4,20},{8,24},{12,28},{16,0},{20,4},{24,8},{28,12},{1,17},{... | collective-permute-start | bytes 442376 | tf_op jit(solution)/shard_map/ppermute | solution.py:50
  146.5 5.1 %collective-permute-start.35 = (bf16[192,384]{1,0:T(8,128)(2,1)S(1)}, bf16[192,384]{1,0:T(8,128)(2,1)S(1)}, u32[]{:S(2)}, u32[]{:S(2)}) collective-permute-start(bf16[192,384]{1,0:T(8,128)(2,1)S(1)} %collective-permute-done.33.refs_2_), channel_id=1, source_target_pairs={{0,8},{4,12},{8,0},{12,4},{16,24},{20,28},{24,16},{28,20},{1,9},{5... | collective-permute-start | bytes 442376 | tf_op jit(solution)/shard_map/ppermute | solution.py:50
  148.3 5.1 %collective-permute-start.36 = (bf16[192,384]{1,0:T(8,128)(2,1)S(1)}, bf16[192,384]{1,0:T(8,128)(2,1)S(1)}, u32[]{:S(2)}, u32[]{:S(2)}) collective-permute-start(bf16[192,384]{1,0:T(8,128)(2,1)S(1)} %collective-permute-done.32.refs_1_), channel_id=1, source_target_pairs={{0,16},{4,20},{8,24},{12,28},{16,0},{20,4},{24,8},{28,12},{1,17},{... | collective-permute-start | bytes 442376 | tf_op jit(solution)/shard_map/ppermute | solution.py:50
  153.5 2.9 %collective-permute-start.38 = (bf16[1152,384]{1,0:T(8,128)(2,1)S(1)}, bf16[1152,384]{1,0:T(8,128)(2,1)S(1)}, u32[]{:S(2)}, u32[]{:S(2)}) collective-permute-start(bf16[1152,384]{1,0:T(8,128)(2,1)S(1)} %shard_map.92.refs_1_.refs_2_.refs_3_), channel_id=1, source_target_pairs={{0,4},{4,0},{8,12},{12,8},{16,20},{20,16},{24,28},{28,24},{1,5},{5... | collective-permute-start | bytes 2654216 | tf_op jit(solution)/shard_map/ppermute | solution.py:50
  153.6 2.8 %collective-permute-start.37 = (bf16[384,384]{1,0:T(8,128)(2,1)S(1)}, bf16[384,384]{1,0:T(8,128)(2,1)S(1)}, u32[]{:S(2)}, u32[]{:S(2)}) collective-permute-start(bf16[384,384]{1,0:T(8,128)(2,1)S(1)} %get-tuple-element.51.refs_0_), channel_id=1, source_target_pairs={{0,4},{4,0},{8,12},{12,8},{16,20},{20,16},{24,28},{28,24},{1,5},{5... | collective-permute-start | bytes 884744 | tf_op jit(solution)/shard_map/ppermute | solution.py:50
  158.4 13.6 %collective-permute-start.39 = (bf16[384,512]{1,0:T(8,128)(2,1)S(1)}, bf16[384,512]{1,0:T(8,128)(2,1)S(1)}, u32[]{:S(2)}, u32[]{:S(2)}) collective-permute-start(bf16[384,512]{1,0:T(8,128)(2,1)S(1)} %get-tuple-element.56), channel_id=1, source_target_pairs={{0,3},{1,0},{2,1},{3,2},{4,7},{5,4},{6,5},{7,6},{8,11},{9,8},{10,9... | collective-permute-start | bytes 1179656 | tf_op jit(solution)/shard_map/ppermute | solution.py:46
  163.8 17.0 %collective-permute-start.41 = (bf16[384,512]{1,0:T(8,128)(2,1)S(1)}, bf16[384,512]{1,0:T(8,128)(2,1)S(1)}, u32[]{:S(2)}, u32[]{:S(2)}) collective-permute-start(bf16[384,512]{1,0:T(8,128)(2,1)S(1)} %shard_map.95), channel_id=1, source_target_pairs={{0,1},{1,2},{2,3},{3,0},{4,5},{5,6},{6,7},{7,4},{8,9},{9,10},{10,1... | collective-permute-start | bytes 1179656 | tf_op jit(solution)/shard_map/ppermute | solution.py:46
  166.0 42.7 %copy-start.2 = (bf16[512,2048]{1,0:T(8,128)(2,1)S(1)}, bf16[512,2048]{1,0:T(8,128)(2,1)}, u32[]{:S(2)}) copy-start(bf16[512,2048]{1,0:T(8,128)(2,1)} %a_ref.19) | copy-start | bytes 6291460
  172.1 16.6 %collective-permute-start.40 = (bf16[384,512]{1,0:T(8,128)(2,1)S(1)}, bf16[384,512]{1,0:T(8,128)(2,1)S(1)}, u32[]{:S(2)}, u32[]{:S(2)}) collective-permute-start(bf16[384,512]{1,0:T(8,128)(2,1)S(1)} %add_convert_fusion.1), channel_id=1, source_target_pairs={{0,3},{1,0},{2,1},{3,2},{4,7},{5,4},{6,5},{7,6},{8,11},{9,8},{10,9... | collective-permute-start | bytes 1179656 | tf_op jit(solution)/shard_map/ppermute | solution.py:46
  189.0 13.9 %collective-permute-start.42 = (bf16[384,512]{1,0:T(8,128)(2,1)S(1)}, bf16[384,512]{1,0:T(8,128)(2,1)S(1)}, u32[]{:S(2)}, u32[]{:S(2)}) collective-permute-start(bf16[384,512]{1,0:T(8,128)(2,1)S(1)} %add_convert_fusion.refs_1_), channel_id=1, source_target_pairs={{0,1},{1,2},{2,3},{3,0},{4,5},{5,6},{6,7},{7,4},{8,9},{9,10},{10,1... | collective-permute-start | bytes 1179656 | tf_op jit(solution)/shard_map/ppermute | solution.py:46
  189.6 19.2 %collective-permute-start.43 = (bf16[384,512]{1,0:T(8,128)(2,1)S(1)}, bf16[384,512]{1,0:T(8,128)(2,1)S(1)}, u32[]{:S(2)}, u32[]{:S(2)}) collective-permute-start(bf16[384,512]{1,0:T(8,128)(2,1)S(1)} %add_convert_fusion.refs_1_), channel_id=1, source_target_pairs={{0,3},{1,0},{2,1},{3,2},{4,7},{5,4},{6,5},{7,6},{8,11},{9,8},{10,9... | collective-permute-start | bytes 1179656 | tf_op jit(solution)/shard_map/ppermute | solution.py:46
  202.8 15.9 %collective-permute-start.44 = (bf16[384,512]{1,0:T(8,128)(2,1)S(1)}, bf16[384,512]{1,0:T(8,128)(2,1)S(1)}, u32[]{:S(2)}, u32[]{:S(2)}) collective-permute-start(bf16[384,512]{1,0:T(8,128)(2,1)S(1)} %collective-permute-done.42.refs_2_), channel_id=1, source_target_pairs={{0,1},{1,2},{2,3},{3,0},{4,5},{5,6},{6,7},{7,4},{8,9},{9,10},{10,1... | collective-permute-start | bytes 1179656 | tf_op jit(solution)/shard_map/ppermute | solution.py:46

commit v10 on v9

--- a/solution.py
+++ b/solution.py
@@ -65,15 +65,15 @@
 def gather_front(low, high, n):
     rows = low.shape[0]
     x_high, y_low = swap(high, n, 2), swap(low, n, 4)
-    own, low, high = regroup(low, high)
+    low, high = again(low, high)
     x_low, y_high = swap(low, n, 2), swap(high, n, 4)
     corner_low, corner_high = swap(y_low, n, 2), swap(x_high, n, 4)
-    sides = stack([x_low, x_high, y_low, y_high, corner_low, corner_high])
-    found = []
-    for core, block, others in ((0, own, sides), (1, swap(own, n, 1), swap(sides, n, 1))):
-        found.append((0, core, 0, 2 * rows, block))
-        found += [(chip, core, (chip - 1) * 2 * rows, 2 * rows, others) for chip in (1, 2, 3)]
-    return found
+    mine = stack([low, high, x_low, x_high, y_low, y_high, corner_low, corner_high])
+    return [
+        (chip, core, chip * 2 * rows, 2 * rows, blocks)
+        for core, blocks in ((0, mine), (1, swap(mine, n, 1)))
+        for chip in range(4)
+    ]
 
 
 def to_plane(x, n):
@@ -274,15 +274,12 @@
     return kernel_call(body, out, [], blocks, [], [], 0, 4 * len(blocks) * rows * width)
 
 
-def regroup(low, high):
-    rows, width = low.shape
-
-    def body(low_ref, high_ref, whole_ref, low_out_ref, high_out_ref):
-        for start, half_ref, out_ref in ((0, low_ref, low_out_ref), (rows, high_ref, high_out_ref)):
-            out_ref[...] = half_ref[...]
-            whole_ref[start : start + rows, :] = half_ref[...]
-
-    outs = [jax.ShapeDtypeStruct((n * rows, width), BF16) for n in (2, 1, 1)]
+def again(low, high):
+    def body(low_ref, high_ref, low_out_ref, high_out_ref):
+        low_out_ref[...] = low_ref[...]
+        high_out_ref[...] = high_ref[...]
+
+    outs = [jax.ShapeDtypeStruct(low.shape, BF16)] * 2
     return kernel_call(body, outs, [], [low, high], [], [], 0, 8 * low.size)
 
 
@@ -324,7 +321,7 @@
 
 def border_pick(at, local_index, coupling, pieces, offset, n_row, n_front):
     rows, depth = coupling.shape[0], coupling.shape[1] // n_row
-    piece_rows, width = pieces[0][-1].shape
+    piece_rows, width = pieces[0][3], pieces[0][-1].shape[1]
     span_rows = piece_rows * n_front
     many = len(pieces)
 

time: 221 us -> 221 us (level)
    ppermute x26 -> x24, waiting for transfers between devices: 30.1 us -> 31.1 us  [swap(): return lax.ppermute(x, 'front', [(i, i ^ by) for i in range(size)])]
    ppermute x26 -> x24, starting transfers between devices: 25.6 us -> 24.7 us  [swap(): return lax.ppermute(x, 'front', [(i, i ^ by) for i in range(size)])]
  transfers between devices with their start and end apart: 45 -> 43, of which waited for: 34 -> 33; matrix products, arithmetic and copies ran while one was open for 0% -> 0% of each run, Pallas kernels for 10% -> 10%
where the time goes in v10:
time: 221 us
  waiting for transfers between devices  122 us (55%)
  starting transfers between devices  58.3 us (26%)
  Pallas kernels  32.9 us (15%)
  local copies, waits for them, and re-layouts  5.47 us (2%)
    ppermute x15, waiting for transfers between devices, shift(): return lax.ppermute(x, 'row', [(i, (i + by) % size) for i in range(size)])  85.6 us
    pallas_call x21, Pallas kernels, kernel_call(): pl.pallas_call(body, out_shape=out_shape, grid_spec=pltpu.PrefetchScalarG...  32.9 us
    ppermute x24, waiting for transfers between devices, swap(): return lax.ppermute(x, 'front', [(i, i ^ by) for i in range(size)])  31.1 us
    ppermute x15, starting transfers between devices, shift(): return lax.ppermute(x, 'row', [(i, (i + by) % size) for i in range(size)])  28.2 us
    ppermute x24, starting transfers between devices, swap(): return lax.ppermute(x, 'front', [(i, i ^ by) for i in range(size)])  24.7 us
    ppermute x4, starting transfers between devices, to_plane(): moved.append(lax.ppermute(quarter, ('front', 'row'), perm))  5.41 us
    unnamed x16, local copies, waits for them, and re-layouts  5.4 us
    ppermute x4, waiting for transfers between devices, to_plane(): moved.append(lax.ppermute(quarter, ('front', 'row'), perm))  4.88 us
  transfers between devices with their start and end apart: 43, of which 33 were waited for; matrix products, arithmetic and copies ran while one was open for 0% of the time, Pallas kernels for 10%

profile of v10, /device:TPU:0, one launch (start us, length us, event | category | flops | bytes accessed | tf_op | source)
XLA Modules:
  0.0 220.6 jit_solution(5986261776771213677)
XLA Ops:
  0.6 3.1 %collective-permute-start = (bf16[512,384]{1,0:T(8,128)(2,1)}, bf16[512,384]{1,0:T(8,128)(2,1)S(1)}, u32[]{:S(2)}, u32[]{:S(2)}) collective-permute-start(bf16[512,384]{1,0:T(8,128)(2,1)} %refs_0_.1), channel_id=1, source_target_pairs={{0,1},{1,2},{2,3},{3,0},{4,5},{5,6},{6,7},{7,4},{8,9},{9,10},{10,1... | collective-permute-start | bytes 1179656 | tf_op jit(solution)/shard_map/ppermute | solution.py:46
  3.7 2.1 collective-permute-start.1
  5.8 10.1 %collective-permute-done.refs_1_ = bf16[512,384]{1,0:T(8,128)(2,1)S(1)} collective-permute-done((bf16[512,384]{1,0:T(8,128)(2,1)}, bf16[512,384]{1,0:T(8,128)(2,1)S(1)}, u32[]{:S(2)}, u32[]{:S(2)}) %collective-permute-start) | collective-permute-done | bytes 393248 | tf_op jit(solution)/shard_map/ppermute | solution.py:46
  16.0 7.1 %collective-permute-done.1.refs_2_ = bf16[512,384]{1,0:T(8,128)(2,1)S(1)} collective-permute-done((bf16[512,384]{1,0:T(8,128)(2,1)}, bf16[512,384]{1,0:T(8,128)(2,1)S(1)}, u32[]{:S(2)}, u32[]{:S(2)}) %collective-permute-start.1) | collective-permute-done | bytes 393248 | tf_op jit(solution)/shard_map/ppermute | solution.py:46
  23.1 1.6 copy-done.1
  25.7 1.5 shard_map.77.refs_0_
  27.3 4.7 %collective-permute-done.2.refs_1_ = bf16[512,384]{1,0:T(8,128)(2,1)S(1)} collective-permute-done((bf16[512,384]{1,0:T(8,128)(2,1)S(1)}, bf16[512,384]{1,0:T(8,128)(2,1)S(1)}, u32[]{:S(2)}, u32[]{:S(2)}) %collective-permute-start.2) | collective-permute-done | bytes 393248 | tf_op jit(solution)/shard_map/ppermute | solution.py:46
  32.0 1.7 shard_map.78
  33.7 3.8 %collective-permute-start.3 = (bf16[512,384]{1,0:T(8,128)(2,1)}, bf16[512,384]{1,0:T(8,128)(2,1)}, u32[]{:S(2)}, u32[]{:S(2)}) collective-permute-start(bf16[512,384]{1,0:T(8,128)(2,1)} %get-tuple-element.29.refs_0_), channel_id=1, source_target_pairs={{0,3},{1,0},{2,1},{3,2},{4,7},{5,4},{6,5},{7,6},{8,11},{9,8},{10,9... | collective-permute-start | bytes 1179656 | tf_op jit(solution)/shard_map/ppermute | solution.py:46
  37.5 10.2 %collective-permute-done.4.refs_1_ = bf16[512,384]{1,0:T(8,128)(2,1)S(1)} collective-permute-done((bf16[512,384]{1,0:T(8,128)(2,1)}, bf16[512,384]{1,0:T(8,128)(2,1)S(1)}, u32[]{:S(2)}, u32[]{:S(2)}) %collective-permute-start.4) | collective-permute-done | bytes 393248 | tf_op jit(solution)/shard_map/ppermute | solution.py:46
  47.8 2.8 %copy-done = bf16[1536,2048]{1,0:T(8,128)(2,1)S(1)} copy-done((bf16[1536,2048]{1,0:T(8,128)(2,1)S(1)}, bf16[1536,2048]{1,0:T(8,128)(2,1)}, u32[]{:S(2)}) %copy-start) | copy-done | bytes 6291480
  50.6 4.0 %shard_map.79 = (f32[1536,384]{1,0:T(8,128)S(1)}, f32[384,384]{1,0:T(8,128)S(1)}) custom-call(s32[2]{0:T(128)S(1)} %pad_add_fusion.at_ref, bf16[1536,2048]{1,0:T(8,128)(2,1)S(1)} %copy-done, bf16[512,384]{1,0:T(8,128)(2,1)} %get-tuple-element.29.refs_0_, bf16[512,384]{1,0:T(8,128)(2,1)S(1)} %collective-permute-done.4.refs_1_, f32[3072,384]{1,0:T(8,128)} %refs_2_.2), custom_call_target="tpu_custom_call" | custom-call | flops 1207959552 | bytes 3145728 | tf_op jit(solution)/shard_map/pallas_call | solution.py:29
  54.6 5.2 %shard_map.80 = (f32[1536,384]{1,0:T(8,128)S(1)}, bf16[1536,3072]{1,0:T(8,128)(2,1)S(1)}) custom-call(s32[2]{0:T(128)S(1)} %pad_add_fusion.at_ref, bf16[1536,2048]{1,0:T(8,128)(2,1)S(1)} %bitcast.5, bf16[512,384]{1,0:T(8,128)(2,1)} %collective-permute-done.3.refs_0_, f32[1536,384]{1,0:T(8,128)S(1)} %get-tuple-element.30.refs_1_, bf16[1536,3072]{1,0:T(8,128)(2,1)} %refs_2_.3), custom_call_target="tpu_custom_call" | custom-call | flops 603979776 | bytes 1572864 | tf_op jit(solution)/shard_map/pallas_call | solution.py:29
  59.8 1.6 collective-permute-done.5.refs_0_
  61.4 2.4 %shard_map.81 = (bf16[1536,384]{1,0:T(8,128)(2,1)S(1)}, bf16[1536,384]{1,0:T(8,128)(2,1)S(1)}) custom-call(s32[2]{0:T(128)S(1)} %pad_add_fusion.at_ref, s32[12]{0:T(128)S(1)} %subtract_bitcast_fusion.index_ref, bf16[1536,2048]{1,0:T(8,128)(2,1)S(1)} %bitcast.5, bf16[512,384]{1,0:T(8,128)(2,1)S(1)} %collective-permute-done.5.refs_0_, ...), custom_call_target="tpu_custom_call" | custom-call | flops 603979776 | bytes 1572864 | tf_op jit(solution)/shard_map/pallas_call | solution.py:29
  63.9 2.8 %collective-permute-done.6.came_ref = bf16[1536,384]{1,0:T(8,128)(2,1)S(1)} collective-permute-done((bf16[1536,384]{1,0:T(8,128)(2,1)S(1)}, bf16[1536,384]{1,0:T(8,128)(2,1)S(1)}, u32[]{:S(2)}, u32[]{:S(2)}) %collective-permute-start.6) | collective-permute-done | bytes 1179680 | tf_op jit(solution)/shard_map/ppermute | solution.py:50
  66.8 1.6 collective-permute-start.8
  68.3 1.5 collective-permute-start.9
  71.0 2.2 collective-permute-done.8.low_ref
  73.2 1.9 collective-permute-done.9.high_ref
  75.2 1.6 collective-permute-start.10
  78.2 2.2 collective-permute-done.10.refs_1_
  80.4 1.5 collective-permute-done.11.refs_2_
  82.8 2.0 collective-permute-start.13
  84.8 1.5 collective-permute-start.16
  86.3 1.7 collective-permute-done.15.refs_4_
  88.9 1.1 collective-permute-start.18
  90.5 2.7 %collective-permute-done.17.refs_6_ = bf16[192,384]{1,0:T(8,128)(2,1)S(1)} collective-permute-done((bf16[192,384]{1,0:T(8,128)(2,1)S(1)}, bf16[192,384]{1,0:T(8,128)(2,1)S(1)}, u32[]{:S(2)}, u32[]{:S(2)}) %collective-permute-start.17) | collective-permute-done | bytes 147488 | tf_op jit(solution)/shard_map/ppermute | solution.py:50
  94.2 2.8 %collective-permute-done.19.refs_4_.refs_5_.refs_6_.refs_7_ = bf16[1536,384]{1,0:T(8,128)(2,1)S(1)} collective-permute-done((bf16[1536,384]{1,0:T(8,128)(2,1)S(1)}, bf16[1536,384]{1,0:T(8,128)(2,1)S(1)}, u32[]{:S(2)}, u32[]{:S(2)}) %collective-permute-start.19) | collective-permute-done | bytes 1179680 | tf_op jit(solution)/shard_map/ppermute | solution.py:50
  97.1 2.5 %shard_map.89 = bf16[384,384]{1,0:T(8,128)(2,1)S(1)} custom-call(s32[2]{0:T(128)S(1)} %pad_add_fusion.at_ref, bf16[1536,3072]{1,0:T(8,128)(2,1)S(1)} %get-tuple-element.31.a_ref, bf16[1536,384]{1,0:T(8,128)(2,1)S(1)} %shard_map.87.refs_0_.refs_1_.refs_2_.refs_3_, bf16[1536,384]{1,0:T(8,128)(2,1)S(1)} %shard_map.87.refs_0_.refs_1_.refs_2_.refs_3_, ...), custom_call_target="tpu_custom_call" | custom-call | flops 905969664 | bytes 2359296 | tf_op jit(solution)/shard_map/pallas_call | solution.py:29
  99.6 2.3 %collective-permute-start.20 = (bf16[384,384]{1,0:T(8,128)(2,1)S(1)}, bf16[384,384]{1,0:T(8,128)(2,1)S(1)}, u32[]{:S(2)}, u32[]{:S(2)}) collective-permute-start(bf16[384,384]{1,0:T(8,128)(2,1)S(1)} %shard_map.89), channel_id=1, source_target_pairs={{0,3},{1,0},{2,1},{3,2},{4,7},{5,4},{6,5},{7,6},{8,11},{9,8},{10,9... | collective-permute-start | bytes 884744 | tf_op jit(solution)/shard_map/ppermute | solution.py:46
  101.9 2.5 %shard_map.90 = bf16[384,384]{1,0:T(8,128)(2,1)S(1)} custom-call(s32[2]{0:T(128)S(1)} %pad_add_fusion.at_ref, bf16[1536,3072]{1,0:T(8,128)(2,1)S(1)} %get-tuple-element.31.a_ref, bf16[1536,384]{1,0:T(8,128)(2,1)S(1)} %shard_map.87.refs_0_.refs_1_.refs_2_.refs_3_, bf16[1536,384]{1,0:T(8,128)(2,1)S(1)} %shard_map.87.refs_0_.refs_1_.refs_2_.refs_3_, ...), custom_call_target="tpu_custom_call" | custom-call | flops 905969664 | bytes 2359296 | tf_op jit(solution)/shard_map/pallas_call | solution.py:29
  104.5 3.8 %shard_map.88 = (f32[384,384]{1,0:T(8,128)S(1)}, f32[384,384]{1,0:T(8,128)S(1)}) custom-call(s32[2]{0:T(128)S(1)} %pad_add_fusion.at_ref, bf16[1536,3072]{1,0:T(8,128)(2,1)S(1)} %get-tuple-element.31.a_ref, bf16[1536,384]{1,0:T(8,128)(2,1)S(1)} %shard_map.87.refs_0_.refs_1_.refs_2_.refs_3_, bf16[1536,384]{1,0:T(8,128)(2,1)S(1)} %shard_map.87.refs_0_.refs_1_.refs_2_.refs_3_, ...), custom_call_target="tpu_custom_call" | custom-call | flops 1811939328 | bytes 4718592 | tf_op jit(solution)/shard_map/pallas_call | solution.py:29
  108.2 1.1 collective-permute-done.20
  109.4 4.3 %collective-permute-start.21 = (bf16[384,384]{1,0:T(8,128)(2,1)S(1)}, bf16[384,384]{1,0:T(8,128)(2,1)S(1)}, u32[]{:S(2)}, u32[]{:S(2)}) collective-permute-start(bf16[384,384]{1,0:T(8,128)(2,1)S(1)} %add_convert_fusion.2), channel_id=1, source_target_pairs={{0,3},{1,0},{2,1},{3,2},{4,7},{5,4},{6,5},{7,6},{8,11},{9,8},{10,9... | collective-permute-start | bytes 884744 | tf_op jit(solution)/shard_map/ppermute | solution.py:46
  113.7 2.5 %collective-permute-done.22 = bf16[384,384]{1,0:T(8,128)(2,1)S(1)} collective-permute-done((bf16[384,384]{1,0:T(8,128)(2,1)S(1)}, bf16[384,384]{1,0:T(8,128)(2,1)S(1)}, u32[]{:S(2)}, u32[]{:S(2)}) %collective-permute-start.22) | collective-permute-done | bytes 294944 | tf_op jit(solution)/shard_map/ppermute | solution.py:46
  116.2 5.7 %collective-permute-done.21 = bf16[384,384]{1,0:T(8,128)(2,1)S(1)} collective-permute-done((bf16[384,384]{1,0:T(8,128)(2,1)S(1)}, bf16[384,384]{1,0:T(8,128)(2,1)S(1)}, u32[]{:S(2)}, u32[]{:S(2)}) %collective-permute-start.21) | collective-permute-done | bytes 294944 | tf_op jit(solution)/shard_map/ppermute | solution.py:46
  122.8 1.2 collective-permute-start.28
  124.0 1.6 collective-permute-start.26
  127.0 1.8 collective-permute-done.28
  128.8 3.9 %collective-permute-start.29 = (bf16[96,384]{1,0:T(8,128)(2,1)S(1)}, bf16[96,384]{1,0:T(8,128)(2,1)S(1)}, u32[]{:S(2)}, u32[]{:S(2)}) collective-permute-start(bf16[96,384]{1,0:T(8,128)(2,1)S(1)} %collective-permute-done.28), channel_id=1, source_target_pairs={{0,3},{1,11},{2,19},{3,27},{4,7},{5,15},{6,23},{7,31},{8,2},{9,10}... | collective-permute-start | bytes 221192 | tf_op jit(solution)/shard_map/ppermute | solution.py:92
  133.6 4.9 %collective-permute-done.25 = bf16[96,384]{1,0:T(8,128)(2,1)S(1)} collective-permute-done((bf16[96,384]{1,0:T(8,128)(2,1)S(1)}, bf16[96,384]{1,0:T(8,128)(2,1)S(1)}, u32[]{:S(2)}, u32[]{:S(2)}) %collective-permute-start.25) | collective-permute-done | bytes 73760 | tf_op jit(solution)/shard_map/ppermute | solution.py:92
  138.5 3.4 %collective-permute-start.32 = (bf16[192,384]{1,0:T(8,128)(2,1)S(1)}, bf16[192,384]{1,0:T(8,128)(2,1)S(1)}, u32[]{:S(2)}, u32[]{:S(2)}) collective-permute-start(bf16[192,384]{1,0:T(8,128)(2,1)S(1)} %constant_dynamic-update-slice_fusion.low_ref), channel_id=1, source_target_pairs={{0,16},{4,20},{8,24},{12,28},{16,0},{20,4},{24,8},{28,12},{1,17},{... | collective-permute-start | bytes 442376 | tf_op jit(solution)/shard_map/ppermute | solution.py:50
  141.9 1.8 collective-permute-start.31
  144.1 2.3 %collective-permute-done.32.refs_4_ = bf16[192,384]{1,0:T(8,128)(2,1)S(1)} collective-permute-done((bf16[192,384]{1,0:T(8,128)(2,1)S(1)}, bf16[192,384]{1,0:T(8,128)(2,1)S(1)}, u32[]{:S(2)}, u32[]{:S(2)}) %collective-permute-start.32) | collective-permute-done | bytes 147488 | tf_op jit(solution)/shard_map/ppermute | solution.py:50
  146.4 1.8 collective-permute-start.34
  148.3 1.4 collective-permute-start.35
  149.9 1.7 collective-permute-done.34.refs_6_
  151.6 1.9 collective-permute-done.35.refs_7_
  153.6 2.8 %collective-permute-done.36.refs_4_.refs_5_.refs_6_.refs_7_ = bf16[1536,384]{1,0:T(8,128)(2,1)S(1)} collective-permute-done((bf16[1536,384]{1,0:T(8,128)(2,1)S(1)}, bf16[1536,384]{1,0:T(8,128)(2,1)S(1)}, u32[]{:S(2)}, u32[]{:S(2)}) %collective-permute-start.36) | collective-permute-done | bytes 1179680 | tf_op jit(solution)/shard_map/ppermute | solution.py:50
  156.5 2.0 shard_map.93
  158.4 4.1 %collective-permute-start.37 = (bf16[384,512]{1,0:T(8,128)(2,1)S(1)}, bf16[384,512]{1,0:T(8,128)(2,1)S(1)}, u32[]{:S(2)}, u32[]{:S(2)}) collective-permute-start(bf16[384,512]{1,0:T(8,128)(2,1)S(1)} %get-tuple-element.52), channel_id=1, source_target_pairs={{0,3},{1,0},{2,1},{3,2},{4,7},{5,4},{6,5},{7,6},{8,11},{9,8},{10,9... | collective-permute-start | bytes 1179656 | tf_op jit(solution)/shard_map/ppermute | solution.py:46
  162.5 1.3 shard_map.95
  164.1 1.9 shard_map.94
  166.0 6.0 %collective-permute-done.37 = bf16[384,512]{1,0:T(8,128)(2,1)S(1)} collective-permute-done((bf16[384,512]{1,0:T(8,128)(2,1)S(1)}, bf16[384,512]{1,0:T(8,128)(2,1)S(1)}, u32[]{:S(2)}, u32[]{:S(2)}) %collective-permute-start.37) | collective-permute-done | bytes 393248 | tf_op jit(solution)/shard_map/ppermute | solution.py:46
  172.2 4.3 %collective-permute-start.38 = (bf16[384,512]{1,0:T(8,128)(2,1)S(1)}, bf16[384,512]{1,0:T(8,128)(2,1)S(1)}, u32[]{:S(2)}, u32[]{:S(2)}) collective-permute-start(bf16[384,512]{1,0:T(8,128)(2,1)S(1)} %add_convert_fusion.1), channel_id=1, source_target_pairs={{0,3},{1,0},{2,1},{3,2},{4,7},{5,4},{6,5},{7,6},{8,11},{9,8},{10,9... | collective-permute-start | bytes 1179656 | tf_op jit(solution)/shard_map/ppermute | solution.py:46
  176.5 4.4 %collective-permute-done.39 = bf16[384,512]{1,0:T(8,128)(2,1)S(1)} collective-permute-done((bf16[384,512]{1,0:T(8,128)(2,1)S(1)}, bf16[384,512]{1,0:T(8,128)(2,1)S(1)}, u32[]{:S(2)}, u32[]{:S(2)}) %collective-permute-start.39) | collective-permute-done | bytes 393248 | tf_op jit(solution)/shard_map/ppermute | solution.py:46
  180.9 7.9 %collective-permute-done.38 = bf16[384,512]{1,0:T(8,128)(2,1)S(1)} collective-permute-done((bf16[384,512]{1,0:T(8,128)(2,1)S(1)}, bf16[384,512]{1,0:T(8,128)(2,1)S(1)}, u32[]{:S(2)}, u32[]{:S(2)}) %collective-permute-start.38) | collective-permute-done | bytes 393248 | tf_op jit(solution)/shard_map/ppermute | solution.py:46
  189.6 3.3 %collective-permute-start.41 = (bf16[384,512]{1,0:T(8,128)(2,1)S(1)}, bf16[384,512]{1,0:T(8,128)(2,1)S(1)}, u32[]{:S(2)}, u32[]{:S(2)}) collective-permute-start(bf16[384,512]{1,0:T(8,128)(2,1)S(1)} %add_convert_fusion.refs_1_), channel_id=1, source_target_pairs={{0,3},{1,0},{2,1},{3,2},{4,7},{5,4},{6,5},{7,6},{8,11},{9,8},{10,9... | collective-permute-start | bytes 1179656 | tf_op jit(solution)/shard_map/ppermute | solution.py:46
  192.8 10.0 %collective-permute-done.40.refs_2_ = bf16[384,512]{1,0:T(8,128)(2,1)S(1)} collective-permute-done((bf16[384,512]{1,0:T(8,128)(2,1)S(1)}, bf16[384,512]{1,0:T(8,128)(2,1)S(1)}, u32[]{:S(2)}, u32[]{:S(2)}) %collective-permute-start.40) | collective-permute-done | bytes 393248 | tf_op jit(solution)/shard_map/ppermute | solution.py:46
  202.8 5.9 %collective-permute-done.41.refs_3_ = bf16[384,512]{1,0:T(8,128)(2,1)S(1)} collective-permute-done((bf16[384,512]{1,0:T(8,128)(2,1)S(1)}, bf16[384,512]{1,0:T(8,128)(2,1)S(1)}, u32[]{:S(2)}, u32[]{:S(2)}) %collective-permute-start.41) | collective-permute-done | bytes 393248 | tf_op jit(solution)/shard_map/ppermute | solution.py:46
  208.7 1.5 shard_map.96.refs_0_
  210.3 8.4 %collective-permute-done.42.refs_1_ = bf16[384,512]{1,0:T(8,128)(2,1)S(1)} collective-permute-done((bf16[384,512]{1,0:T(8,128)(2,1)S(1)}, bf16[384,512]{1,0:T(8,128)(2,1)S(1)}, u32[]{:S(2)}, u32[]{:S(2)}) %collective-permute-start.42) | collective-permute-done | bytes 393248 | tf_op jit(solution)/shard_map/ppermute | solution.py:46
  218.7 1.9 shard_map.97
  (69 shorter events, 12.7 us)
Async XLA Ops:
  0.6 15.3 %collective-permute-start = (bf16[512,384]{1,0:T(8,128)(2,1)}, bf16[512,384]{1,0:T(8,128)(2,1)S(1)}, u32[]{:S(2)}, u32[]{:S(2)}) collective-permute-start(bf16[512,384]{1,0:T(8,128)(2,1)} %refs_0_.1), channel_id=1, source_target_pairs={{0,1},{1,2},{2,3},{3,0},{4,5},{5,6},{6,7},{7,4},{8,9},{9,10},{10,1... | collective-permute-start | bytes 1179656 | tf_op jit(solution)/shard_map/ppermute | solution.py:46
  3.7 19.4 %collective-permute-start.1 = (bf16[512,384]{1,0:T(8,128)(2,1)}, bf16[512,384]{1,0:T(8,128)(2,1)S(1)}, u32[]{:S(2)}, u32[]{:S(2)}) collective-permute-start(bf16[512,384]{1,0:T(8,128)(2,1)} %refs_0_.1), channel_id=1, source_target_pairs={{0,3},{1,0},{2,1},{3,2},{4,7},{5,4},{6,5},{7,6},{8,11},{9,8},{10,9... | collective-permute-start | bytes 1179656 | tf_op jit(solution)/shard_map/ppermute | solution.py:46
  15.9 16.0 %collective-permute-start.2 = (bf16[512,384]{1,0:T(8,128)(2,1)S(1)}, bf16[512,384]{1,0:T(8,128)(2,1)S(1)}, u32[]{:S(2)}, u32[]{:S(2)}) collective-permute-start(bf16[512,384]{1,0:T(8,128)(2,1)S(1)} %collective-permute-done.refs_1_), channel_id=1, source_target_pairs={{0,1},{1,2},{2,3},{3,0},{4,5},{5,6},{6,7},{7,4},{8,9},{9,10},{10,1... | collective-permute-start | bytes 1179656 | tf_op jit(solution)/shard_map/ppermute | solution.py:46
  23.1 1.6 copy-start.1
  24.7 1.0 copy-start.3
  25.7 28.8 %slice-start = ((s8[6291456]{0:T(1024)(128)(4,1)}), s8[2097152]{0:T(1024)(128)(4,1)S(1)}, s32[]{:S(2)}) async-start(s8[6291456]{0:T(1024)(128)(4,1)} %bitcast.4), calls=%async_computation | async-start | bytes 4194304
  27.2 20.5 %copy-start.4 = (s32[1,12]{1,0:T(1,128)S(1)}, s32[1,12]{1,0:T(1,128)}, u32[]{:S(2)}) copy-start(s32[1,12]{1,0:T(1,128)} %param.11) | copy-start | bytes 148
  33.7 14.1 %collective-permute-start.4 = (bf16[512,384]{1,0:T(8,128)(2,1)}, bf16[512,384]{1,0:T(8,128)(2,1)S(1)}, u32[]{:S(2)}, u32[]{:S(2)}) collective-permute-start(bf16[512,384]{1,0:T(8,128)(2,1)} %get-tuple-element.29.refs_0_), channel_id=1, source_target_pairs={{0,1},{1,2},{2,3},{3,0},{4,5},{5,6},{6,7},{7,4},{8,9},{9,10},{10,1... | collective-permute-start | bytes 1179656 | tf_op jit(solution)/shard_map/ppermute | solution.py:46
  33.7 20.8 %collective-permute-start.3 = (bf16[512,384]{1,0:T(8,128)(2,1)}, bf16[512,384]{1,0:T(8,128)(2,1)}, u32[]{:S(2)}, u32[]{:S(2)}) collective-permute-start(bf16[512,384]{1,0:T(8,128)(2,1)} %get-tuple-element.29.refs_0_), channel_id=1, source_target_pairs={{0,3},{1,0},{2,1},{3,2},{4,7},{5,4},{6,5},{7,6},{8,11},{9,8},{10,9... | collective-permute-start | bytes 1179656 | tf_op jit(solution)/shard_map/ppermute | solution.py:46
  47.8 13.6 %collective-permute-start.5 = (bf16[512,384]{1,0:T(8,128)(2,1)S(1)}, bf16[512,384]{1,0:T(8,128)(2,1)S(1)}, u32[]{:S(2)}, u32[]{:S(2)}) collective-permute-start(bf16[512,384]{1,0:T(8,128)(2,1)S(1)} %collective-permute-done.4.refs_1_), channel_id=1, source_target_pairs={{0,1},{1,2},{2,3},{3,0},{4,5},{5,6},{6,7},{7,4},{8,9},{9,10},{10,1... | collective-permute-start | bytes 1179656 | tf_op jit(solution)/shard_map/ppermute | solution.py:46
  47.8 2.8 %copy-start = (bf16[1536,2048]{1,0:T(8,128)(2,1)S(1)}, bf16[1536,2048]{1,0:T(8,128)(2,1)}, u32[]{:S(2)}) copy-start(bf16[1536,2048]{1,0:T(8,128)(2,1)} %a_ref.17) | copy-start | bytes 18874372
  50.6 4.0 %slice-start.1 = ((s8[6291456]{0:T(1024)(128)(4,1)}), s8[4194304]{0:T(1024)(128)(4,1)S(1)}, s32[]{:S(2)}) async-start(s8[6291456]{0:T(1024)(128)(4,1)} %bitcast.4), calls=%async_computation.1 | async-start | bytes 8388608
  63.8 2.9 %collective-permute-start.6 = (bf16[1536,384]{1,0:T(8,128)(2,1)S(1)}, bf16[1536,384]{1,0:T(8,128)(2,1)S(1)}, u32[]{:S(2)}, u32[]{:S(2)}) collective-permute-start(bf16[1536,384]{1,0:T(8,128)(2,1)S(1)} %get-tuple-element.35), channel_id=1, source_target_pairs={{0,4},{4,0},{8,12},{12,8},{16,20},{20,16},{24,28},{28,24},{1,5},{5... | collective-permute-start | bytes 3538952 | tf_op jit(solution)/shard_map/ppermute | solution.py:50
  66.8 6.4 %collective-permute-start.8 = (bf16[192,384]{1,0:T(8,128)(2,1)S(1)}, bf16[192,384]{1,0:T(8,128)(2,1)S(1)}, u32[]{:S(2)}, u32[]{:S(2)}) collective-permute-start(bf16[192,384]{1,0:T(8,128)(2,1)S(1)} %get-tuple-element.37), channel_id=1, source_target_pairs={{0,8},{4,12},{8,0},{12,4},{16,24},{20,28},{24,16},{28,20},{1,9},{5... | collective-permute-start | bytes 442376 | tf_op jit(solution)/shard_map/ppermute | solution.py:50
  68.3 6.7 %collective-permute-start.9 = (bf16[192,384]{1,0:T(8,128)(2,1)S(1)}, bf16[192,384]{1,0:T(8,128)(2,1)S(1)}, u32[]{:S(2)}, u32[]{:S(2)}) collective-permute-start(bf16[192,384]{1,0:T(8,128)(2,1)S(1)} %get-tuple-element.38), channel_id=1, source_target_pairs={{0,16},{4,20},{8,24},{12,28},{16,0},{20,4},{24,8},{28,12},{1,17},{... | collective-permute-start | bytes 442376 | tf_op jit(solution)/shard_map/ppermute | solution.py:50
  69.9 7.4 %collective-permute-start.7 = (bf16[192,384]{1,0:T(8,128)(2,1)S(1)}, bf16[192,384]{1,0:T(8,128)(2,1)S(1)}, u32[]{:S(2)}, u32[]{:S(2)}) collective-permute-start(bf16[192,384]{1,0:T(8,128)(2,1)S(1)} %get-tuple-element.36), channel_id=1, source_target_pairs={{0,8},{4,12},{8,0},{12,4},{16,24},{20,28},{24,16},{28,20},{1,9},{5... | collective-permute-start | bytes 442376 | tf_op jit(solution)/shard_map/ppermute | solution.py:50
  70.5 7.7 %collective-permute-start.12 = (bf16[192,384]{1,0:T(8,128)(2,1)S(1)}, bf16[192,384]{1,0:T(8,128)(2,1)S(1)}, u32[]{:S(2)}, u32[]{:S(2)}) collective-permute-start(bf16[192,384]{1,0:T(8,128)(2,1)S(1)} %get-tuple-element.41), channel_id=1, source_target_pairs={{0,16},{4,20},{8,24},{12,28},{16,0},{20,4},{24,8},{28,12},{1,17},{... | collective-permute-start | bytes 442376 | tf_op jit(solution)/shard_map/ppermute | solution.py:50
  75.2 5.2 %collective-permute-start.10 = (bf16[192,384]{1,0:T(8,128)(2,1)S(1)}, bf16[192,384]{1,0:T(8,128)(2,1)S(1)}, u32[]{:S(2)}, u32[]{:S(2)}) collective-permute-start(bf16[192,384]{1,0:T(8,128)(2,1)S(1)} %get-tuple-element.39), channel_id=1, source_target_pairs={{0,16},{4,20},{8,24},{12,28},{16,0},{20,4},{24,8},{28,12},{1,17},{... | collective-permute-start | bytes 442376 | tf_op jit(solution)/shard_map/ppermute | solution.py:50
  76.8 5.1 %collective-permute-start.11 = (bf16[192,384]{1,0:T(8,128)(2,1)S(1)}, bf16[192,384]{1,0:T(8,128)(2,1)S(1)}, u32[]{:S(2)}, u32[]{:S(2)}) collective-permute-start(bf16[192,384]{1,0:T(8,128)(2,1)S(1)} %get-tuple-element.40), channel_id=1, source_target_pairs={{0,8},{4,12},{8,0},{12,4},{16,24},{20,28},{24,16},{28,20},{1,9},{5... | collective-permute-start | bytes 442376 | tf_op jit(solution)/shard_map/ppermute | solution.py:50
  82.1 6.0 %collective-permute-start.15 = (bf16[192,384]{1,0:T(8,128)(2,1)S(1)}, bf16[192,384]{1,0:T(8,128)(2,1)S(1)}, u32[]{:S(2)}, u32[]{:S(2)}) collective-permute-start(bf16[192,384]{1,0:T(8,128)(2,1)S(1)} %get-tuple-element.42.low_ref), channel_id=1, source_target_pairs={{0,16},{4,20},{8,24},{12,28},{16,0},{20,4},{24,8},{28,12},{1,17},{... | collective-permute-start | bytes 442376 | tf_op jit(solution)/shard_map/ppermute | solution.py:50
  82.7 6.2 %collective-permute-start.14 = (bf16[192,384]{1,0:T(8,128)(2,1)S(1)}, bf16[192,384]{1,0:T(8,128)(2,1)S(1)}, u32[]{:S(2)}, u32[]{:S(2)}) collective-permute-start(bf16[192,384]{1,0:T(8,128)(2,1)S(1)} %get-tuple-element.43.high_ref), channel_id=1, source_target_pairs={{0,8},{4,12},{8,0},{12,4},{16,24},{20,28},{24,16},{28,20},{1,9},{5... | collective-permute-start | bytes 442376 | tf_op jit(solution)/shard_map/ppermute | solution.py:50
  82.8 7.7 %collective-permute-start.13 = (bf16[192,384]{1,0:T(8,128)(2,1)S(1)}, bf16[192,384]{1,0:T(8,128)(2,1)S(1)}, u32[]{:S(2)}, u32[]{:S(2)}) collective-permute-start(bf16[192,384]{1,0:T(8,128)(2,1)S(1)} %get-tuple-element.44.refs_0_), channel_id=1, source_target_pairs={{0,8},{4,12},{8,0},{12,4},{16,24},{20,28},{24,16},{28,20},{1,9},{5... | collective-permute-start | bytes 442376 | tf_op jit(solution)/shard_map/ppermute | solution.py:50
  84.8 5.7 %collective-permute-start.16 = (bf16[192,384]{1,0:T(8,128)(2,1)S(1)}, bf16[192,384]{1,0:T(8,128)(2,1)S(1)}, u32[]{:S(2)}, u32[]{:S(2)}) collective-permute-start(bf16[192,384]{1,0:T(8,128)(2,1)S(1)} %get-tuple-element.45.refs_1_), channel_id=1, source_target_pairs={{0,16},{4,20},{8,24},{12,28},{16,0},{20,4},{24,8},{28,12},{1,17},{... | collective-permute-start | bytes 442376 | tf_op jit(solution)/shard_map/ppermute | solution.py:50
  88.1 5.1 %collective-permute-start.17 = (bf16[192,384]{1,0:T(8,128)(2,1)S(1)}, bf16[192,384]{1,0:T(8,128)(2,1)S(1)}, u32[]{:S(2)}, u32[]{:S(2)}) collective-permute-start(bf16[192,384]{1,0:T(8,128)(2,1)S(1)} %collective-permute-done.15.refs_4_), channel_id=1, source_target_pairs={{0,8},{4,12},{8,0},{12,4},{16,24},{20,28},{24,16},{28,20},{1,9},{5... | collective-permute-start | bytes 442376 | tf_op jit(solution)/shard_map/ppermute | solution.py:50
  88.9 5.1 %collective-permute-start.18 = (bf16[192,384]{1,0:T(8,128)(2,1)S(1)}, bf16[192,384]{1,0:T(8,128)(2,1)S(1)}, u32[]{:S(2)}, u32[]{:S(2)}) collective-permute-start(bf16[192,384]{1,0:T(8,128)(2,1)S(1)} %collective-permute-done.14.refs_3_), channel_id=1, source_target_pairs={{0,16},{4,20},{8,24},{12,28},{16,0},{20,4},{24,8},{28,12},{1,17},{... | collective-permute-start | bytes 442376 | tf_op jit(solution)/shard_map/ppermute | solution.py:50
  94.2 2.9 %collective-permute-start.19 = (bf16[1536,384]{1,0:T(8,128)(2,1)S(1)}, bf16[1536,384]{1,0:T(8,128)(2,1)S(1)}, u32[]{:S(2)}, u32[]{:S(2)}) collective-permute-start(bf16[1536,384]{1,0:T(8,128)(2,1)S(1)} %shard_map.87.refs_0_.refs_1_.refs_2_.refs_3_), channel_id=1, source_target_pairs={{0,4},{4,0},{8,12},{12,8},{16,20},{20,16},{24,28},{28,24},{1,5},{5... | collective-permute-start | bytes 3538952 | tf_op jit(solution)/shard_map/ppermute | solution.py:50
  99.6 9.7 %collective-permute-start.20 = (bf16[384,384]{1,0:T(8,128)(2,1)S(1)}, bf16[384,384]{1,0:T(8,128)(2,1)S(1)}, u32[]{:S(2)}, u32[]{:S(2)}) collective-permute-start(bf16[384,384]{1,0:T(8,128)(2,1)S(1)} %shard_map.89), channel_id=1, source_target_pairs={{0,3},{1,0},{2,1},{3,2},{4,7},{5,4},{6,5},{7,6},{8,11},{9,8},{10,9... | collective-permute-start | bytes 884744 | tf_op jit(solution)/shard_map/ppermute | solution.py:46
  104.4 11.8 %collective-permute-start.22 = (bf16[384,384]{1,0:T(8,128)(2,1)S(1)}, bf16[384,384]{1,0:T(8,128)(2,1)S(1)}, u32[]{:S(2)}, u32[]{:S(2)}) collective-permute-start(bf16[384,384]{1,0:T(8,128)(2,1)S(1)} %shard_map.90), channel_id=1, source_target_pairs={{0,1},{1,2},{2,3},{3,0},{4,5},{5,6},{6,7},{7,4},{8,9},{9,10},{10,1... | collective-permute-start | bytes 884744 | tf_op jit(solution)/shard_map/ppermute | solution.py:46
  109.4 12.5 %collective-permute-start.21 = (bf16[384,384]{1,0:T(8,128)(2,1)S(1)}, bf16[384,384]{1,0:T(8,128)(2,1)S(1)}, u32[]{:S(2)}, u32[]{:S(2)}) collective-permute-start(bf16[384,384]{1,0:T(8,128)(2,1)S(1)} %add_convert_fusion.2), channel_id=1, source_target_pairs={{0,3},{1,0},{2,1},{3,2},{4,7},{5,4},{6,5},{7,6},{8,11},{9,8},{10,9... | collective-permute-start | bytes 884744 | tf_op jit(solution)/shard_map/ppermute | solution.py:46
  122.8 6.0 %collective-permute-start.28 = (bf16[96,384]{1,0:T(8,128)(2,1)S(1)}, bf16[96,384]{1,0:T(8,128)(2,1)S(1)}, u32[]{:S(2)}, u32[]{:S(2)}) collective-permute-start(bf16[96,384]{1,0:T(8,128)(2,1)S(1)} %get-tuple-element.56), channel_id=1, source_target_pairs={{0,24},{4,28},{8,16},{12,20},{16,8},{20,12},{24,0},{28,4},{1,25},{... | collective-permute-start | bytes 221192 | tf_op jit(solution)/shard_map/ppermute | solution.py:50
  124.0 8.7 %collective-permute-start.26 = (bf16[96,384]{1,0:T(8,128)(2,1)S(1)}, bf16[96,384]{1,0:T(8,128)(2,1)S(1)}, u32[]{:S(2)}, u32[]{:S(2)}) collective-permute-start(bf16[96,384]{1,0:T(8,128)(2,1)S(1)} %get-tuple-element.57), channel_id=1, source_target_pairs={{0,16},{4,20},{8,24},{12,28},{16,0},{20,4},{24,8},{28,12},{1,17},{... | collective-permute-start | bytes 221192 | tf_op jit(solution)/shard_map/ppermute | solution.py:50
  125.5 8.0 %collective-permute-start.24 = (bf16[96,384]{1,0:T(8,128)(2,1)S(1)}, bf16[96,384]{1,0:T(8,128)(2,1)S(1)}, u32[]{:S(2)}, u32[]{:S(2)}) collective-permute-start(bf16[96,384]{1,0:T(8,128)(2,1)S(1)} %get-tuple-element.58), channel_id=1, source_target_pairs={{0,8},{4,12},{8,0},{12,4},{16,24},{20,28},{24,16},{28,20},{1,9},{5... | collective-permute-start | bytes 221192 | tf_op jit(solution)/shard_map/ppermute | solution.py:50
  126.4 7.2 %collective-permute-start.23 = (bf16[96,384]{1,0:T(8,128)(2,1)S(1)}, bf16[96,384]{1,0:T(8,128)(2,1)S(1)}, u32[]{:S(2)}, u32[]{:S(2)}) collective-permute-start(bf16[96,384]{1,0:T(8,128)(2,1)S(1)} %get-tuple-element.59), channel_id=1, source_target_pairs={{0,0},{1,8},{2,16},{3,24},{4,4},{5,12},{6,20},{7,28},{8,1},{9,9},{... | collective-permute-start | bytes 221192 | tf_op jit(solution)/shard_map/ppermute | solution.py:92
  128.8 13.1 %collective-permute-start.29 = (bf16[96,384]{1,0:T(8,128)(2,1)S(1)}, bf16[96,384]{1,0:T(8,128)(2,1)S(1)}, u32[]{:S(2)}, u32[]{:S(2)}) collective-permute-start(bf16[96,384]{1,0:T(8,128)(2,1)S(1)} %collective-permute-done.28), channel_id=1, source_target_pairs={{0,3},{1,11},{2,19},{3,27},{4,7},{5,15},{6,23},{7,31},{8,2},{9,10}... | collective-permute-start | bytes 221192 | tf_op jit(solution)/shard_map/ppermute | solution.py:92
  132.7 9.2 %collective-permute-start.27 = (bf16[96,384]{1,0:T(8,128)(2,1)S(1)}, bf16[96,384]{1,0:T(8,128)(2,1)S(1)}, u32[]{:S(2)}, u32[]{:S(2)}) collective-permute-start(bf16[96,384]{1,0:T(8,128)(2,1)S(1)} %collective-permute-done.26), channel_id=1, source_target_pairs={{0,2},{1,10},{2,18},{3,26},{4,6},{5,14},{6,22},{7,30},{8,3},{9,11}... | collective-permute-start | bytes 221192 | tf_op jit(solution)/shard_map/ppermute | solution.py:92
  133.6 4.9 %collective-permute-start.25 = (bf16[96,384]{1,0:T(8,128)(2,1)S(1)}, bf16[96,384]{1,0:T(8,128)(2,1)S(1)}, u32[]{:S(2)}, u32[]{:S(2)}) collective-permute-start(bf16[96,384]{1,0:T(8,128)(2,1)S(1)} %collective-permute-done.24), channel_id=1, source_target_pairs={{0,1},{1,9},{2,17},{3,25},{4,5},{5,13},{6,21},{7,29},{8,0},{9,8},{... | collective-permute-start | bytes 221192 | tf_op jit(solution)/shard_map/ppermute | solution.py:92
  138.5 7.9 %collective-permute-start.32 = (bf16[192,384]{1,0:T(8,128)(2,1)S(1)}, bf16[192,384]{1,0:T(8,128)(2,1)S(1)}, u32[]{:S(2)}, u32[]{:S(2)}) collective-permute-start(bf16[192,384]{1,0:T(8,128)(2,1)S(1)} %constant_dynamic-update-slice_fusion.low_ref), channel_id=1, source_target_pairs={{0,16},{4,20},{8,24},{12,28},{16,0},{20,4},{24,8},{28,12},{1,17},{... | collective-permute-start | bytes 442376 | tf_op jit(solution)/shard_map/ppermute | solution.py:50
  141.9 6.4 %collective-permute-start.31 = (bf16[192,384]{1,0:T(8,128)(2,1)S(1)}, bf16[192,384]{1,0:T(8,128)(2,1)S(1)}, u32[]{:S(2)}, u32[]{:S(2)}) collective-permute-start(bf16[192,384]{1,0:T(8,128)(2,1)S(1)} %constant_dynamic-update-slice_fusion.2.high_ref), channel_id=1, source_target_pairs={{0,8},{4,12},{8,0},{12,4},{16,24},{20,28},{24,16},{28,20},{1,9},{5... | collective-permute-start | bytes 442376 | tf_op jit(solution)/shard_map/ppermute | solution.py:50
  143.7 6.1 %collective-permute-start.30 = (bf16[192,384]{1,0:T(8,128)(2,1)S(1)}, bf16[192,384]{1,0:T(8,128)(2,1)S(1)}, u32[]{:S(2)}, u32[]{:S(2)}) collective-permute-start(bf16[192,384]{1,0:T(8,128)(2,1)S(1)} %get-tuple-element.48.refs_0_), channel_id=1, source_target_pairs={{0,8},{4,12},{8,0},{12,4},{16,24},{20,28},{24,16},{28,20},{1,9},{5... | collective-permute-start | bytes 442376 | tf_op jit(solution)/shard_map/ppermute | solution.py:50
  144.1 5.8 %collective-permute-start.33 = (bf16[192,384]{1,0:T(8,128)(2,1)S(1)}, bf16[192,384]{1,0:T(8,128)(2,1)S(1)}, u32[]{:S(2)}, u32[]{:S(2)}) collective-permute-start(bf16[192,384]{1,0:T(8,128)(2,1)S(1)} %get-tuple-element.49.refs_1_), channel_id=1, source_target_pairs={{0,16},{4,20},{8,24},{12,28},{16,0},{20,4},{24,8},{28,12},{1,17},{... | collective-permute-start | bytes 442376 | tf_op jit(solution)/shard_map/ppermute | solution.py:50
  146.4 5.1 %collective-permute-start.34 = (bf16[192,384]{1,0:T(8,128)(2,1)S(1)}, bf16[192,384]{1,0:T(8,128)(2,1)S(1)}, u32[]{:S(2)}, u32[]{:S(2)}) collective-permute-start(bf16[192,384]{1,0:T(8,128)(2,1)S(1)} %collective-permute-done.32.refs_4_), channel_id=1, source_target_pairs={{0,8},{4,12},{8,0},{12,4},{16,24},{20,28},{24,16},{28,20},{1,9},{5... | collective-permute-start | bytes 442376 | tf_op jit(solution)/shard_map/ppermute | solution.py:50
  148.3 5.1 %collective-permute-start.35 = (bf16[192,384]{1,0:T(8,128)(2,1)S(1)}, bf16[192,384]{1,0:T(8,128)(2,1)S(1)}, u32[]{:S(2)}, u32[]{:S(2)}) collective-permute-start(bf16[192,384]{1,0:T(8,128)(2,1)S(1)} %collective-permute-done.31.refs_3_), channel_id=1, source_target_pairs={{0,16},{4,20},{8,24},{12,28},{16,0},{20,4},{24,8},{28,12},{1,17},{... | collective-permute-start | bytes 442376 | tf_op jit(solution)/shard_map/ppermute | solution.py:50
  153.5 2.9 %collective-permute-start.36 = (bf16[1536,384]{1,0:T(8,128)(2,1)S(1)}, bf16[1536,384]{1,0:T(8,128)(2,1)S(1)}, u32[]{:S(2)}, u32[]{:S(2)}) collective-permute-start(bf16[1536,384]{1,0:T(8,128)(2,1)S(1)} %shard_map.92.refs_0_.refs_1_.refs_2_.refs_3_), channel_id=1, source_target_pairs={{0,4},{4,0},{8,12},{12,8},{16,20},{20,16},{24,28},{28,24},{1,5},{5... | collective-permute-start | bytes 3538952 | tf_op jit(solution)/shard_map/ppermute | solution.py:50
  158.4 13.6 %collective-permute-start.37 = (bf16[384,512]{1,0:T(8,128)(2,1)S(1)}, bf16[384,512]{1,0:T(8,128)(2,1)S(1)}, u32[]{:S(2)}, u32[]{:S(2)}) collective-permute-start(bf16[384,512]{1,0:T(8,128)(2,1)S(1)} %get-tuple-element.52), channel_id=1, source_target_pairs={{0,3},{1,0},{2,1},{3,2},{4,7},{5,4},{6,5},{7,6},{8,11},{9,8},{10,9... | collective-permute-start | bytes 1179656 | tf_op jit(solution)/shard_map/ppermute | solution.py:46
  163.8 17.0 %collective-permute-start.39 = (bf16[384,512]{1,0:T(8,128)(2,1)S(1)}, bf16[384,512]{1,0:T(8,128)(2,1)S(1)}, u32[]{:S(2)}, u32[]{:S(2)}) collective-permute-start(bf16[384,512]{1,0:T(8,128)(2,1)S(1)} %shard_map.95), channel_id=1, source_target_pairs={{0,1},{1,2},{2,3},{3,0},{4,5},{5,6},{6,7},{7,4},{8,9},{9,10},{10,1... | collective-permute-start | bytes 1179656 | tf_op jit(solution)/shard_map/ppermute | solution.py:46
  172.0 36.7 %copy-start.2 = (bf16[512,2048]{1,0:T(8,128)(2,1)S(1)}, bf16[512,2048]{1,0:T(8,128)(2,1)}, u32[]{:S(2)}) copy-start(bf16[512,2048]{1,0:T(8,128)(2,1)} %a_ref.19) | copy-start | bytes 6291460
  172.2 16.6 %collective-permute-start.38 = (bf16[384,512]{1,0:T(8,128)(2,1)S(1)}, bf16[384,512]{1,0:T(8,128)(2,1)S(1)}, u32[]{:S(2)}, u32[]{:S(2)}) collective-permute-start(bf16[384,512]{1,0:T(8,128)(2,1)S(1)} %add_convert_fusion.1), channel_id=1, source_target_pairs={{0,3},{1,0},{2,1},{3,2},{4,7},{5,4},{6,5},{7,6},{8,11},{9,8},{10,9... | collective-permute-start | bytes 1179656 | tf_op jit(solution)/shard_map/ppermute | solution.py:46
  188.9 13.9 %collective-permute-start.40 = (bf16[384,512]{1,0:T(8,128)(2,1)S(1)}, bf16[384,512]{1,0:T(8,128)(2,1)S(1)}, u32[]{:S(2)}, u32[]{:S(2)}) collective-permute-start(bf16[384,512]{1,0:T(8,128)(2,1)S(1)} %add_convert_fusion.refs_1_), channel_id=1, source_target_pairs={{0,1},{1,2},{2,3},{3,0},{4,5},{5,6},{6,7},{7,4},{8,9},{9,10},{10,1... | collective-permute-start | bytes 1179656 | tf_op jit(solution)/shard_map/ppermute | solution.py:46
  189.6 19.2 %collective-permute-start.41 = (bf16[384,512]{1,0:T(8,128)(2,1)S(1)}, bf16[384,512]{1,0:T(8,128)(2,1)S(1)}, u32[]{:S(2)}, u32[]{:S(2)}) collective-permute-start(bf16[384,512]{1,0:T(8,128)(2,1)S(1)} %add_convert_fusion.refs_1_), channel_id=1, source_target_pairs={{0,3},{1,0},{2,1},{3,2},{4,7},{5,4},{6,5},{7,6},{8,11},{9,8},{10,9... | collective-permute-start | bytes 1179656 | tf_op jit(solution)/shard_map/ppermute | solution.py:46
  202.8 15.9 %collective-permute-start.42 = (bf16[384,512]{1,0:T(8,128)(2,1)S(1)}, bf16[384,512]{1,0:T(8,128)(2,1)S(1)}, u32[]{:S(2)}, u32[]{:S(2)}) collective-permute-start(bf16[384,512]{1,0:T(8,128)(2,1)S(1)} %collective-permute-done.40.refs_2_), channel_id=1, source_target_pairs={{0,1},{1,2},{2,3},{3,0},{4,5},{5,6},{6,7},{7,4},{8,9},{9,10},{10,1... | collective-permute-start | bytes 1179656 | tf_op jit(solution)/shard_map/ppermute | solution.py:46

commit v11 on v10

--- a/solution.py
+++ b/solution.py
@@ -63,17 +63,12 @@
 
 
 def gather_front(low, high, n):
-    rows = low.shape[0]
     x_high, y_low = swap(high, n, 2), swap(low, n, 4)
     low, high = again(low, high)
     x_low, y_high = swap(low, n, 2), swap(high, n, 4)
     corner_low, corner_high = swap(y_low, n, 2), swap(x_high, n, 4)
     mine = stack([low, high, x_low, x_high, y_low, y_high, corner_low, corner_high])
-    return [
-        (chip, core, chip * 2 * rows, 2 * rows, blocks)
-        for core, blocks in ((0, mine), (1, swap(mine, n, 1)))
-        for chip in range(4)
-    ]
+    return mine, swap(mine, n, 1)
 
 
 def to_plane(x, n):
@@ -283,27 +278,22 @@
     return kernel_call(body, outs, [], [low, high], [], [], 0, 8 * low.size)
 
 
-def assemble(pieces, piece_refs, target_ref, sems, base):
-    copies = []
-    for (chip, core, row, rows, _), ref in zip(pieces, piece_refs):
-        place = pl.ds(pl.multiple_of(base(2 * chip + core), rows), rows)
-        source = ref.at[pl.ds(row, rows)]
-        copies.append(pltpu.make_async_copy(source, target_ref.at[place], sems.at[len(copies)]))
-    return copies
-
-
-def root_products(at, inverse, pieces, offsets, kinds, n_row, n_front):
+def root_products(at, inverse, spans, offsets, kinds, n_row, n_front):
     span_rows = inverse.shape[1]
     rows = inverse.shape[0] // n_row
-    width = pieces[0][-1].shape[1]
+    width = spans[0].shape[1]
     piece_rows = span_rows // n_front
-    count, many = len(offsets), len(pieces)
-
-    def body(at_ref, a_ref, *refs):
-        piece_refs, out_refs, (x_ref, sems) = refs[:many], refs[many : many + count], refs[many + count :]
-        copies = assemble(
-            pieces, piece_refs, x_ref, sems, lambda d: lax.bitwise_xor(at_ref[1], d) * piece_rows
-        )
+    count = len(offsets)
+
+    def body(at_ref, a_ref, mine_ref, other_ref, *refs):
+        out_refs, (x_ref, sems) = refs[:count], refs[count:]
+        copies = []
+        for core, ref in enumerate((mine_ref, other_ref)):
+            for chip in range(n_front // 2):
+                start = lax.bitwise_xor(at_ref[1], 2 * chip + core) * piece_rows
+                place = pl.ds(pl.multiple_of(start, piece_rows), piece_rows)
+                source = ref.at[pl.ds(chip * piece_rows, piece_rows)]
+                copies.append(pltpu.make_async_copy(source, x_ref.at[place], sems.at[len(copies)]))
         for copy in copies:
             copy.start()
         for copy in copies:
@@ -313,41 +303,41 @@
             out_ref[...] = dot(a_ref[place, :], x_ref[...]).astype(out_ref.dtype)
 
     outs = [jax.ShapeDtypeStruct((rows, width), kind) for kind in kinds]
-    scratch = [pltpu.VMEM((span_rows, width), BF16), pltpu.SemaphoreType.DMA((many,))]
+    scratch = [pltpu.VMEM((span_rows, width), BF16), pltpu.SemaphoreType.DMA((n_front,))]
     share = 2 * rows * span_rows * count
-    held = [inverse] + [block for *_, block in pieces]
-    return kernel_call(body, outs, [at], held, [], scratch, share * width, share)
-
-
-def border_pick(at, local_index, coupling, pieces, offset, n_row, n_front):
+    return kernel_call(body, outs, [at], [inverse, *spans], [], scratch, share * width, share)
+
+
+def border_pick(at, local_index, coupling, spans, offset, n_row, n_front):
     rows, depth = coupling.shape[0], coupling.shape[1] // n_row
-    piece_rows, width = pieces[0][3], pieces[0][-1].shape[1]
-    span_rows = piece_rows * n_front
-    many = len(pieces)
-
-    def body(at_ref, index_ref, a_ref, *refs):
-        piece_refs, (out_ref, picked_ref, span_ref, sems) = refs[:many], refs[many:]
-
-        def base(d):
-            there = lax.bitwise_xor(at_ref[1], d)
-            return lax.rem(there, 2) * (span_rows // 2) + lax.shift_right_logical(there, 1) * piece_rows
-
-        copies = assemble(pieces, piece_refs, span_ref, sems, base)
-        for copy in copies:
-            copy.start()
-        for copy in copies:
-            copy.wait()
+    (span_rows, width), chips = spans[0].shape, n_front // 2
+    piece_blocks = span_rows // chips // BLK
+
+    def body(at_ref, index_ref, a_ref, mine_ref, other_ref, out_ref, picked_ref):
         for j in range(rows // BLK):
-            source = pl.ds(pl.multiple_of(index_ref[j] * BLK, BLK), BLK)
-            picked_ref[:, pl.ds(j * BLK, BLK)] = jnp.transpose(span_ref[source, :])
+            target = index_ref[j]
+            core = lax.div(target, chips * piece_blocks)
+            within = lax.rem(target, chips * piece_blocks)
+            chip = lax.bitwise_xor(lax.div(within, piece_blocks), lax.shift_right_logical(at_ref[1], 1))
+            slot = chip * piece_blocks + lax.rem(within, piece_blocks)
+            source = pl.ds(pl.multiple_of(slot * BLK, BLK), BLK)
+            goal = pl.ds(j * BLK, BLK)
+            here = core == lax.rem(at_ref[1], 2)
+
+            @pl.when(here)
+            def _():
+                picked_ref[:, goal] = jnp.transpose(mine_ref[source, :])
+
+            @pl.when(jnp.logical_not(here))
+            def _():
+                picked_ref[:, goal] = jnp.transpose(other_ref[source, :])
+
         columns = pl.ds(pl.multiple_of(owner(at_ref, offset, n_row) * depth, depth), depth)
         out_ref[...] = dot(picked_ref[...], a_ref[:, columns]).astype(BF16)
 
     outs = [jax.ShapeDtypeStruct((width, depth), BF16), jax.ShapeDtypeStruct((width, rows), BF16)]
-    scratch = [pltpu.VMEM((span_rows, width), BF16), pltpu.SemaphoreType.DMA((many,))]
     share = 2 * rows * depth
-    held = [coupling] + [block for *_, block in pieces]
-    return kernel_call(body, outs, [at, local_index], held, [], scratch, share * width, share)
+    return kernel_call(body, outs, [at, local_index], [coupling, *spans], [], [], share * width, share)
 
 
 def border_backward(at, coupling, picked, offsets, kinds, n_row):

time: 221 us -> 222 us (level)
  transfers between devices with their start and end apart: 43 -> 43, of which waited for: 33 -> 34; matrix products, arithmetic and copies ran while one was open for 0% -> 0% of each run, Pallas kernels for 10% -> 10%
where the time goes in v11:
time: 222 us; the launch traced here: 221 us
  waiting for transfers between devices  122 us (55%)
  starting transfers between devices  58.2 us (26%)
  Pallas kernels  33.5 us (15%)
  local copies, waits for them, and re-layouts  5.47 us (2%)
    ppermute x15, waiting for transfers between devices, shift(): return lax.ppermute(x, 'row', [(i, (i + by) % size) for i in range(size)])  85.8 us
    pallas_call x21, Pallas kernels, kernel_call(): pl.pallas_call(body, out_shape=out_shape, grid_spec=pltpu.PrefetchScalarG...  33.5 us
    ppermute x24, waiting for transfers between devices, swap(): return lax.ppermute(x, 'front', [(i, i ^ by) for i in range(size)])  31.2 us
    ppermute x15, starting transfers between devices, shift(): return lax.ppermute(x, 'row', [(i, (i + by) % size) for i in range(size)])  28.2 us
    ppermute x24, starting transfers between devices, swap(): return lax.ppermute(x, 'front', [(i, i ^ by) for i in range(size)])  24.6 us
    unnamed x16, local copies, waits for them, and re-layouts  5.4 us
    ppermute x4, starting transfers between devices, to_plane(): moved.append(lax.ppermute(quarter, ('front', 'row'), perm))  5.39 us
    ppermute x4, waiting for transfers between devices, to_plane(): moved.append(lax.ppermute(quarter, ('front', 'row'), perm))  4.89 us
  transfers between devices with their start and end apart: 43, of which 34 were waited for; matrix products, arithmetic and copies ran while one was open for 0% of the time, Pallas kernels for 10%

profile of v11, /device:TPU:0, one launch (start us, length us, event | category | flops | bytes accessed | tf_op | source)
XLA Modules:
  0.0 221.4 jit_solution(7124364849205007099)
XLA Ops:
  0.6 3.1 %collective-permute-start = (bf16[512,384]{1,0:T(8,128)(2,1)}, bf16[512,384]{1,0:T(8,128)(2,1)S(1)}, u32[]{:S(2)}, u32[]{:S(2)}) collective-permute-start(bf16[512,384]{1,0:T(8,128)(2,1)} %refs_0_.1), channel_id=1, source_target_pairs={{0,1},{1,2},{2,3},{3,0},{4,5},{5,6},{6,7},{7,4},{8,9},{9,10},{10,1... | collective-permute-start | bytes 1179656 | tf_op jit(solution)/shard_map/ppermute | solution.py:46
  3.7 2.1 collective-permute-start.1
  5.8 10.1 %collective-permute-done.refs_1_ = bf16[512,384]{1,0:T(8,128)(2,1)S(1)} collective-permute-done((bf16[512,384]{1,0:T(8,128)(2,1)}, bf16[512,384]{1,0:T(8,128)(2,1)S(1)}, u32[]{:S(2)}, u32[]{:S(2)}) %collective-permute-start) | collective-permute-done | bytes 393248 | tf_op jit(solution)/shard_map/ppermute | solution.py:46
  16.0 7.1 %collective-permute-done.1.refs_2_ = bf16[512,384]{1,0:T(8,128)(2,1)S(1)} collective-permute-done((bf16[512,384]{1,0:T(8,128)(2,1)}, bf16[512,384]{1,0:T(8,128)(2,1)S(1)}, u32[]{:S(2)}, u32[]{:S(2)}) %collective-permute-start.1) | collective-permute-done | bytes 393248 | tf_op jit(solution)/shard_map/ppermute | solution.py:46
  23.1 1.6 copy-done.1
  25.7 1.5 shard_map.77.refs_0_
  27.3 4.7 %collective-permute-done.2.refs_1_ = bf16[512,384]{1,0:T(8,128)(2,1)S(1)} collective-permute-done((bf16[512,384]{1,0:T(8,128)(2,1)S(1)}, bf16[512,384]{1,0:T(8,128)(2,1)S(1)}, u32[]{:S(2)}, u32[]{:S(2)}) %collective-permute-start.2) | collective-permute-done | bytes 393248 | tf_op jit(solution)/shard_map/ppermute | solution.py:46
  32.0 1.7 shard_map.78
  33.7 3.8 %collective-permute-start.3 = (bf16[512,384]{1,0:T(8,128)(2,1)}, bf16[512,384]{1,0:T(8,128)(2,1)}, u32[]{:S(2)}, u32[]{:S(2)}) collective-permute-start(bf16[512,384]{1,0:T(8,128)(2,1)} %get-tuple-element.29.refs_0_), channel_id=1, source_target_pairs={{0,3},{1,0},{2,1},{3,2},{4,7},{5,4},{6,5},{7,6},{8,11},{9,8},{10,9... | collective-permute-start | bytes 1179656 | tf_op jit(solution)/shard_map/ppermute | solution.py:46
  37.5 10.2 %collective-permute-done.4.refs_1_ = bf16[512,384]{1,0:T(8,128)(2,1)S(1)} collective-permute-done((bf16[512,384]{1,0:T(8,128)(2,1)}, bf16[512,384]{1,0:T(8,128)(2,1)S(1)}, u32[]{:S(2)}, u32[]{:S(2)}) %collective-permute-start.4) | collective-permute-done | bytes 393248 | tf_op jit(solution)/shard_map/ppermute | solution.py:46
  47.8 2.8 %copy-done = bf16[1536,2048]{1,0:T(8,128)(2,1)S(1)} copy-done((bf16[1536,2048]{1,0:T(8,128)(2,1)S(1)}, bf16[1536,2048]{1,0:T(8,128)(2,1)}, u32[]{:S(2)}) %copy-start) | copy-done | bytes 6291480
  50.6 4.0 %shard_map.79 = (f32[1536,384]{1,0:T(8,128)S(1)}, f32[384,384]{1,0:T(8,128)S(1)}) custom-call(s32[2]{0:T(128)S(1)} %pad_add_fusion.at_ref, bf16[1536,2048]{1,0:T(8,128)(2,1)S(1)} %copy-done, bf16[512,384]{1,0:T(8,128)(2,1)} %get-tuple-element.29.refs_0_, bf16[512,384]{1,0:T(8,128)(2,1)S(1)} %collective-permute-done.4.refs_1_, f32[3072,384]{1,0:T(8,128)} %refs_2_.2), custom_call_target="tpu_custom_call" | custom-call | flops 1207959552 | bytes 3145728 | tf_op jit(solution)/shard_map/pallas_call | solution.py:29
  54.6 5.2 %shard_map.80 = (f32[1536,384]{1,0:T(8,128)S(1)}, bf16[1536,3072]{1,0:T(8,128)(2,1)S(1)}) custom-call(s32[2]{0:T(128)S(1)} %pad_add_fusion.at_ref, bf16[1536,2048]{1,0:T(8,128)(2,1)S(1)} %bitcast.5, bf16[512,384]{1,0:T(8,128)(2,1)} %collective-permute-done.3.refs_0_, f32[1536,384]{1,0:T(8,128)S(1)} %get-tuple-element.30.refs_1_, bf16[1536,3072]{1,0:T(8,128)(2,1)} %refs_2_.3), custom_call_target="tpu_custom_call" | custom-call | flops 603979776 | bytes 1572864 | tf_op jit(solution)/shard_map/pallas_call | solution.py:29
  59.8 1.6 collective-permute-done.5.refs_0_
  61.4 2.4 %shard_map.81 = (bf16[1536,384]{1,0:T(8,128)(2,1)S(1)}, bf16[1536,384]{1,0:T(8,128)(2,1)S(1)}) custom-call(s32[2]{0:T(128)S(1)} %pad_add_fusion.at_ref, s32[12]{0:T(128)S(1)} %subtract_bitcast_fusion.index_ref, bf16[1536,2048]{1,0:T(8,128)(2,1)S(1)} %bitcast.5, bf16[512,384]{1,0:T(8,128)(2,1)S(1)} %collective-permute-done.5.refs_0_, ...), custom_call_target="tpu_custom_call" | custom-call | flops 603979776 | bytes 1572864 | tf_op jit(solution)/shard_map/pallas_call | solution.py:29
  63.9 2.8 %collective-permute-done.6.came_ref = bf16[1536,384]{1,0:T(8,128)(2,1)S(1)} collective-permute-done((bf16[1536,384]{1,0:T(8,128)(2,1)S(1)}, bf16[1536,384]{1,0:T(8,128)(2,1)S(1)}, u32[]{:S(2)}, u32[]{:S(2)}) %collective-permute-start.6) | collective-permute-done | bytes 1179680 | tf_op jit(solution)/shard_map/ppermute | solution.py:50
  66.8 1.6 collective-permute-start.8
  68.3 1.5 collective-permute-start.9
  71.0 2.2 collective-permute-done.8.low_ref
  73.2 1.9 collective-permute-done.9.high_ref
  75.2 1.6 collective-permute-start.10
  78.2 2.2 collective-permute-done.10.refs_1_
  80.4 1.5 collective-permute-done.11.refs_2_
  82.8 2.0 collective-permute-start.13
  84.8 1.5 collective-permute-start.16
  86.3 1.7 collective-permute-done.15.refs_4_
  88.9 1.1 collective-permute-start.18
  90.5 2.7 %collective-permute-done.17.refs_6_ = bf16[192,384]{1,0:T(8,128)(2,1)S(1)} collective-permute-done((bf16[192,384]{1,0:T(8,128)(2,1)S(1)}, bf16[192,384]{1,0:T(8,128)(2,1)S(1)}, u32[]{:S(2)}, u32[]{:S(2)}) %collective-permute-start.17) | collective-permute-done | bytes 147488 | tf_op jit(solution)/shard_map/ppermute | solution.py:50
  94.2 2.8 %collective-permute-done.19.other_ref = bf16[1536,384]{1,0:T(8,128)(2,1)S(1)} collective-permute-done((bf16[1536,384]{1,0:T(8,128)(2,1)S(1)}, bf16[1536,384]{1,0:T(8,128)(2,1)S(1)}, u32[]{:S(2)}, u32[]{:S(2)}) %collective-permute-start.19) | collective-permute-done | bytes 1179680 | tf_op jit(solution)/shard_map/ppermute | solution.py:50
  97.1 2.5 %shard_map.89 = bf16[384,384]{1,0:T(8,128)(2,1)S(1)} custom-call(s32[2]{0:T(128)S(1)} %pad_add_fusion.at_ref, bf16[1536,3072]{1,0:T(8,128)(2,1)S(1)} %get-tuple-element.31.a_ref, bf16[1536,384]{1,0:T(8,128)(2,1)S(1)} %shard_map.87.mine_ref, bf16[1536,384]{1,0:T(8,128)(2,1)S(1)} %collective-permute-done.19.other_ref), custom_call_target="tpu_custom_call" | custom-call | flops 905969664 | bytes 2359296 | tf_op jit(solution)/shard_map/pallas_call | solution.py:29
  99.6 2.3 %collective-permute-start.20 = (bf16[384,384]{1,0:T(8,128)(2,1)S(1)}, bf16[384,384]{1,0:T(8,128)(2,1)S(1)}, u32[]{:S(2)}, u32[]{:S(2)}) collective-permute-start(bf16[384,384]{1,0:T(8,128)(2,1)S(1)} %shard_map.89), channel_id=1, source_target_pairs={{0,3},{1,0},{2,1},{3,2},{4,7},{5,4},{6,5},{7,6},{8,11},{9,8},{10,9... | collective-permute-start | bytes 884744 | tf_op jit(solution)/shard_map/ppermute | solution.py:46
  101.9 2.5 %shard_map.90 = bf16[384,384]{1,0:T(8,128)(2,1)S(1)} custom-call(s32[2]{0:T(128)S(1)} %pad_add_fusion.at_ref, bf16[1536,3072]{1,0:T(8,128)(2,1)S(1)} %get-tuple-element.31.a_ref, bf16[1536,384]{1,0:T(8,128)(2,1)S(1)} %shard_map.87.mine_ref, bf16[1536,384]{1,0:T(8,128)(2,1)S(1)} %collective-permute-done.19.other_ref), custom_call_target="tpu_custom_call" | custom-call | flops 905969664 | bytes 2359296 | tf_op jit(solution)/shard_map/pallas_call | solution.py:29
  104.5 3.7 %shard_map.88 = (f32[384,384]{1,0:T(8,128)S(1)}, f32[384,384]{1,0:T(8,128)S(1)}) custom-call(s32[2]{0:T(128)S(1)} %pad_add_fusion.at_ref, bf16[1536,3072]{1,0:T(8,128)(2,1)S(1)} %get-tuple-element.31.a_ref, bf16[1536,384]{1,0:T(8,128)(2,1)S(1)} %shard_map.87.mine_ref, bf16[1536,384]{1,0:T(8,128)(2,1)S(1)} %collective-permute-done.19.other_ref), custom_call_target="tpu_custom_call" | custom-call | flops 1811939328 | bytes 4718592 | tf_op jit(solution)/shard_map/pallas_call | solution.py:29
  108.2 1.1 collective-permute-done.20
  109.4 4.3 %collective-permute-start.21 = (bf16[384,384]{1,0:T(8,128)(2,1)S(1)}, bf16[384,384]{1,0:T(8,128)(2,1)S(1)}, u32[]{:S(2)}, u32[]{:S(2)}) collective-permute-start(bf16[384,384]{1,0:T(8,128)(2,1)S(1)} %add_convert_fusion.2), channel_id=1, source_target_pairs={{0,3},{1,0},{2,1},{3,2},{4,7},{5,4},{6,5},{7,6},{8,11},{9,8},{10,9... | collective-permute-start | bytes 884744 | tf_op jit(solution)/shard_map/ppermute | solution.py:46
  113.7 2.5 %collective-permute-done.22 = bf16[384,384]{1,0:T(8,128)(2,1)S(1)} collective-permute-done((bf16[384,384]{1,0:T(8,128)(2,1)S(1)}, bf16[384,384]{1,0:T(8,128)(2,1)S(1)}, u32[]{:S(2)}, u32[]{:S(2)}) %collective-permute-start.22) | collective-permute-done | bytes 294944 | tf_op jit(solution)/shard_map/ppermute | solution.py:46
  116.2 5.7 %collective-permute-done.21 = bf16[384,384]{1,0:T(8,128)(2,1)S(1)} collective-permute-done((bf16[384,384]{1,0:T(8,128)(2,1)S(1)}, bf16[384,384]{1,0:T(8,128)(2,1)S(1)}, u32[]{:S(2)}, u32[]{:S(2)}) %collective-permute-start.21) | collective-permute-done | bytes 294944 | tf_op jit(solution)/shard_map/ppermute | solution.py:46
  122.8 1.2 collective-permute-start.28
  123.9 1.6 collective-permute-start.26
  127.0 1.8 collective-permute-done.28
  128.8 3.9 %collective-permute-start.29 = (bf16[96,384]{1,0:T(8,128)(2,1)S(1)}, bf16[96,384]{1,0:T(8,128)(2,1)S(1)}, u32[]{:S(2)}, u32[]{:S(2)}) collective-permute-start(bf16[96,384]{1,0:T(8,128)(2,1)S(1)} %collective-permute-done.28), channel_id=1, source_target_pairs={{0,3},{1,11},{2,19},{3,27},{4,7},{5,15},{6,23},{7,31},{8,2},{9,10}... | collective-permute-start | bytes 221192 | tf_op jit(solution)/shard_map/ppermute | solution.py:87
  133.5 4.9 %collective-permute-done.25 = bf16[96,384]{1,0:T(8,128)(2,1)S(1)} collective-permute-done((bf16[96,384]{1,0:T(8,128)(2,1)S(1)}, bf16[96,384]{1,0:T(8,128)(2,1)S(1)}, u32[]{:S(2)}, u32[]{:S(2)}) %collective-permute-start.25) | collective-permute-done | bytes 73760 | tf_op jit(solution)/shard_map/ppermute | solution.py:87
  138.4 3.4 %collective-permute-start.32 = (bf16[192,384]{1,0:T(8,128)(2,1)S(1)}, bf16[192,384]{1,0:T(8,128)(2,1)S(1)}, u32[]{:S(2)}, u32[]{:S(2)}) collective-permute-start(bf16[192,384]{1,0:T(8,128)(2,1)S(1)} %constant_dynamic-update-slice_fusion.low_ref), channel_id=1, source_target_pairs={{0,16},{4,20},{8,24},{12,28},{16,0},{20,4},{24,8},{28,12},{1,17},{... | collective-permute-start | bytes 442376 | tf_op jit(solution)/shard_map/ppermute | solution.py:50
  141.9 1.8 collective-permute-start.31
  144.1 2.3 %collective-permute-done.32.refs_4_ = bf16[192,384]{1,0:T(8,128)(2,1)S(1)} collective-permute-done((bf16[192,384]{1,0:T(8,128)(2,1)S(1)}, bf16[192,384]{1,0:T(8,128)(2,1)S(1)}, u32[]{:S(2)}, u32[]{:S(2)}) %collective-permute-start.32) | collective-permute-done | bytes 147488 | tf_op jit(solution)/shard_map/ppermute | solution.py:50
  146.4 1.8 collective-permute-start.34
  148.3 1.3 collective-permute-start.35
  149.9 1.6 collective-permute-done.34.refs_6_
  151.5 1.9 collective-permute-done.35.refs_7_
  153.6 2.8 %collective-permute-done.36.other_ref = bf16[1536,384]{1,0:T(8,128)(2,1)S(1)} collective-permute-done((bf16[1536,384]{1,0:T(8,128)(2,1)S(1)}, bf16[1536,384]{1,0:T(8,128)(2,1)S(1)}, u32[]{:S(2)}, u32[]{:S(2)}) %collective-permute-start.36) | collective-permute-done | bytes 1179680 | tf_op jit(solution)/shard_map/ppermute | solution.py:50
  156.5 2.6 %shard_map.93 = (bf16[384,512]{1,0:T(8,128)(2,1)S(1)}, bf16[384,1536]{1,0:T(8,128)(2,1)S(1)}) custom-call(s32[2]{0:T(128)S(1)} %pad_add_fusion.at_ref, s32[12]{0:T(128)S(1)} %subtract_bitcast_fusion.index_ref, bf16[1536,2048]{1,0:T(8,128)(2,1)S(1)} %bitcast.5, bf16[1536,384]{1,0:T(8,128)(2,1)S(1)} %shard_map.92.mine_ref, ...), custom_call_target="tpu_custom_call" | custom-call | flops 603979776 | bytes 1572864 | tf_op jit(solution)/shard_map/pallas_call | solution.py:29
  159.0 4.3 %collective-permute-start.37 = (bf16[384,512]{1,0:T(8,128)(2,1)S(1)}, bf16[384,512]{1,0:T(8,128)(2,1)S(1)}, u32[]{:S(2)}, u32[]{:S(2)}) collective-permute-start(bf16[384,512]{1,0:T(8,128)(2,1)S(1)} %get-tuple-element.52), channel_id=1, source_target_pairs={{0,3},{1,0},{2,1},{3,2},{4,7},{5,4},{6,5},{7,6},{8,11},{9,8},{10,9... | collective-permute-start | bytes 1179656 | tf_op jit(solution)/shard_map/ppermute | solution.py:46
  163.3 1.3 shard_map.95
  164.7 1.9 shard_map.94
  166.6 6.2 %collective-permute-done.37 = bf16[384,512]{1,0:T(8,128)(2,1)S(1)} collective-permute-done((bf16[384,512]{1,0:T(8,128)(2,1)S(1)}, bf16[384,512]{1,0:T(8,128)(2,1)S(1)}, u32[]{:S(2)}, u32[]{:S(2)}) %collective-permute-start.37) | collective-permute-done | bytes 393248 | tf_op jit(solution)/shard_map/ppermute | solution.py:46
  173.0 4.3 %collective-permute-start.38 = (bf16[384,512]{1,0:T(8,128)(2,1)S(1)}, bf16[384,512]{1,0:T(8,128)(2,1)S(1)}, u32[]{:S(2)}, u32[]{:S(2)}) collective-permute-start(bf16[384,512]{1,0:T(8,128)(2,1)S(1)} %add_convert_fusion.1), channel_id=1, source_target_pairs={{0,3},{1,0},{2,1},{3,2},{4,7},{5,4},{6,5},{7,6},{8,11},{9,8},{10,9... | collective-permute-start | bytes 1179656 | tf_op jit(solution)/shard_map/ppermute | solution.py:46
  177.3 4.4 %collective-permute-done.39 = bf16[384,512]{1,0:T(8,128)(2,1)S(1)} collective-permute-done((bf16[384,512]{1,0:T(8,128)(2,1)S(1)}, bf16[384,512]{1,0:T(8,128)(2,1)S(1)}, u32[]{:S(2)}, u32[]{:S(2)}) %collective-permute-start.39) | collective-permute-done | bytes 393248 | tf_op jit(solution)/shard_map/ppermute | solution.py:46
  181.7 7.9 %collective-permute-done.38 = bf16[384,512]{1,0:T(8,128)(2,1)S(1)} collective-permute-done((bf16[384,512]{1,0:T(8,128)(2,1)S(1)}, bf16[384,512]{1,0:T(8,128)(2,1)S(1)}, u32[]{:S(2)}, u32[]{:S(2)}) %collective-permute-start.38) | collective-permute-done | bytes 393248 | tf_op jit(solution)/shard_map/ppermute | solution.py:46
  190.4 3.3 %collective-permute-start.41 = (bf16[384,512]{1,0:T(8,128)(2,1)S(1)}, bf16[384,512]{1,0:T(8,128)(2,1)S(1)}, u32[]{:S(2)}, u32[]{:S(2)}) collective-permute-start(bf16[384,512]{1,0:T(8,128)(2,1)S(1)} %add_convert_fusion.refs_1_), channel_id=1, source_target_pairs={{0,3},{1,0},{2,1},{3,2},{4,7},{5,4},{6,5},{7,6},{8,11},{9,8},{10,9... | collective-permute-start | bytes 1179656 | tf_op jit(solution)/shard_map/ppermute | solution.py:46
  193.7 10.0 %collective-permute-done.40.refs_2_ = bf16[384,512]{1,0:T(8,128)(2,1)S(1)} collective-permute-done((bf16[384,512]{1,0:T(8,128)(2,1)S(1)}, bf16[384,512]{1,0:T(8,128)(2,1)S(1)}, u32[]{:S(2)}, u32[]{:S(2)}) %collective-permute-start.40) | collective-permute-done | bytes 393248 | tf_op jit(solution)/shard_map/ppermute | solution.py:46
  203.7 5.9 %collective-permute-done.41.refs_3_ = bf16[384,512]{1,0:T(8,128)(2,1)S(1)} collective-permute-done((bf16[384,512]{1,0:T(8,128)(2,1)S(1)}, bf16[384,512]{1,0:T(8,128)(2,1)S(1)}, u32[]{:S(2)}, u32[]{:S(2)}) %collective-permute-start.41) | collective-permute-done | bytes 393248 | tf_op jit(solution)/shard_map/ppermute | solution.py:46
  209.6 1.5 shard_map.96.refs_0_
  211.1 8.4 %collective-permute-done.42.refs_1_ = bf16[384,512]{1,0:T(8,128)(2,1)S(1)} collective-permute-done((bf16[384,512]{1,0:T(8,128)(2,1)S(1)}, bf16[384,512]{1,0:T(8,128)(2,1)S(1)}, u32[]{:S(2)}, u32[]{:S(2)}) %collective-permute-start.42) | collective-permute-done | bytes 393248 | tf_op jit(solution)/shard_map/ppermute | solution.py:46
  219.5 1.9 shard_map.97
  (69 shorter events, 12.7 us)
Async XLA Ops:
  0.6 15.3 %collective-permute-start = (bf16[512,384]{1,0:T(8,128)(2,1)}, bf16[512,384]{1,0:T(8,128)(2,1)S(1)}, u32[]{:S(2)}, u32[]{:S(2)}) collective-permute-start(bf16[512,384]{1,0:T(8,128)(2,1)} %refs_0_.1), channel_id=1, source_target_pairs={{0,1},{1,2},{2,3},{3,0},{4,5},{5,6},{6,7},{7,4},{8,9},{9,10},{10,1... | collective-permute-start | bytes 1179656 | tf_op jit(solution)/shard_map/ppermute | solution.py:46
  3.7 19.4 %collective-permute-start.1 = (bf16[512,384]{1,0:T(8,128)(2,1)}, bf16[512,384]{1,0:T(8,128)(2,1)S(1)}, u32[]{:S(2)}, u32[]{:S(2)}) collective-permute-start(bf16[512,384]{1,0:T(8,128)(2,1)} %refs_0_.1), channel_id=1, source_target_pairs={{0,3},{1,0},{2,1},{3,2},{4,7},{5,4},{6,5},{7,6},{8,11},{9,8},{10,9... | collective-permute-start | bytes 1179656 | tf_op jit(solution)/shard_map/ppermute | solution.py:46
  15.9 16.0 %collective-permute-start.2 = (bf16[512,384]{1,0:T(8,128)(2,1)S(1)}, bf16[512,384]{1,0:T(8,128)(2,1)S(1)}, u32[]{:S(2)}, u32[]{:S(2)}) collective-permute-start(bf16[512,384]{1,0:T(8,128)(2,1)S(1)} %collective-permute-done.refs_1_), channel_id=1, source_target_pairs={{0,1},{1,2},{2,3},{3,0},{4,5},{5,6},{6,7},{7,4},{8,9},{9,10},{10,1... | collective-permute-start | bytes 1179656 | tf_op jit(solution)/shard_map/ppermute | solution.py:46
  23.1 1.6 copy-start.1
  24.7 1.0 copy-start.3
  25.7 28.8 %slice-start = ((s8[6291456]{0:T(1024)(128)(4,1)}), s8[2097152]{0:T(1024)(128)(4,1)S(1)}, s32[]{:S(2)}) async-start(s8[6291456]{0:T(1024)(128)(4,1)} %bitcast.4), calls=%async_computation | async-start | bytes 4194304
  27.2 20.5 %copy-start.4 = (s32[1,12]{1,0:T(1,128)S(1)}, s32[1,12]{1,0:T(1,128)}, u32[]{:S(2)}) copy-start(s32[1,12]{1,0:T(1,128)} %param.11) | copy-start | bytes 148
  33.7 14.1 %collective-permute-start.4 = (bf16[512,384]{1,0:T(8,128)(2,1)}, bf16[512,384]{1,0:T(8,128)(2,1)S(1)}, u32[]{:S(2)}, u32[]{:S(2)}) collective-permute-start(bf16[512,384]{1,0:T(8,128)(2,1)} %get-tuple-element.29.refs_0_), channel_id=1, source_target_pairs={{0,1},{1,2},{2,3},{3,0},{4,5},{5,6},{6,7},{7,4},{8,9},{9,10},{10,1... | collective-permute-start | bytes 1179656 | tf_op jit(solution)/shard_map/ppermute | solution.py:46
  33.7 20.8 %collective-permute-start.3 = (bf16[512,384]{1,0:T(8,128)(2,1)}, bf16[512,384]{1,0:T(8,128)(2,1)}, u32[]{:S(2)}, u32[]{:S(2)}) collective-permute-start(bf16[512,384]{1,0:T(8,128)(2,1)} %get-tuple-element.29.refs_0_), channel_id=1, source_target_pairs={{0,3},{1,0},{2,1},{3,2},{4,7},{5,4},{6,5},{7,6},{8,11},{9,8},{10,9... | collective-permute-start | bytes 1179656 | tf_op jit(solution)/shard_map/ppermute | solution.py:46
  47.8 13.6 %collective-permute-start.5 = (bf16[512,384]{1,0:T(8,128)(2,1)S(1)}, bf16[512,384]{1,0:T(8,128)(2,1)S(1)}, u32[]{:S(2)}, u32[]{:S(2)}) collective-permute-start(bf16[512,384]{1,0:T(8,128)(2,1)S(1)} %collective-permute-done.4.refs_1_), channel_id=1, source_target_pairs={{0,1},{1,2},{2,3},{3,0},{4,5},{5,6},{6,7},{7,4},{8,9},{9,10},{10,1... | collective-permute-start | bytes 1179656 | tf_op jit(solution)/shard_map/ppermute | solution.py:46
  47.8 2.8 %copy-start = (bf16[1536,2048]{1,0:T(8,128)(2,1)S(1)}, bf16[1536,2048]{1,0:T(8,128)(2,1)}, u32[]{:S(2)}) copy-start(bf16[1536,2048]{1,0:T(8,128)(2,1)} %a_ref.17) | copy-start | bytes 18874372
  50.6 4.0 %slice-start.1 = ((s8[6291456]{0:T(1024)(128)(4,1)}), s8[4194304]{0:T(1024)(128)(4,1)S(1)}, s32[]{:S(2)}) async-start(s8[6291456]{0:T(1024)(128)(4,1)} %bitcast.4), calls=%async_computation.1 | async-start | bytes 8388608
  63.8 2.9 %collective-permute-start.6 = (bf16[1536,384]{1,0:T(8,128)(2,1)S(1)}, bf16[1536,384]{1,0:T(8,128)(2,1)S(1)}, u32[]{:S(2)}, u32[]{:S(2)}) collective-permute-start(bf16[1536,384]{1,0:T(8,128)(2,1)S(1)} %get-tuple-element.35), channel_id=1, source_target_pairs={{0,4},{4,0},{8,12},{12,8},{16,20},{20,16},{24,28},{28,24},{1,5},{5... | collective-permute-start | bytes 3538952 | tf_op jit(solution)/shard_map/ppermute | solution.py:50
  66.8 6.4 %collective-permute-start.8 = (bf16[192,384]{1,0:T(8,128)(2,1)S(1)}, bf16[192,384]{1,0:T(8,128)(2,1)S(1)}, u32[]{:S(2)}, u32[]{:S(2)}) collective-permute-start(bf16[192,384]{1,0:T(8,128)(2,1)S(1)} %get-tuple-element.37), channel_id=1, source_target_pairs={{0,8},{4,12},{8,0},{12,4},{16,24},{20,28},{24,16},{28,20},{1,9},{5... | collective-permute-start | bytes 442376 | tf_op jit(solution)/shard_map/ppermute | solution.py:50
  68.3 6.7 %collective-permute-start.9 = (bf16[192,384]{1,0:T(8,128)(2,1)S(1)}, bf16[192,384]{1,0:T(8,128)(2,1)S(1)}, u32[]{:S(2)}, u32[]{:S(2)}) collective-permute-start(bf16[192,384]{1,0:T(8,128)(2,1)S(1)} %get-tuple-element.38), channel_id=1, source_target_pairs={{0,16},{4,20},{8,24},{12,28},{16,0},{20,4},{24,8},{28,12},{1,17},{... | collective-permute-start | bytes 442376 | tf_op jit(solution)/shard_map/ppermute | solution.py:50
  69.9 7.4 %collective-permute-start.7 = (bf16[192,384]{1,0:T(8,128)(2,1)S(1)}, bf16[192,384]{1,0:T(8,128)(2,1)S(1)}, u32[]{:S(2)}, u32[]{:S(2)}) collective-permute-start(bf16[192,384]{1,0:T(8,128)(2,1)S(1)} %get-tuple-element.36), channel_id=1, source_target_pairs={{0,8},{4,12},{8,0},{12,4},{16,24},{20,28},{24,16},{28,20},{1,9},{5... | collective-permute-start | bytes 442376 | tf_op jit(solution)/shard_map/ppermute | solution.py:50
  70.5 7.7 %collective-permute-start.12 = (bf16[192,384]{1,0:T(8,128)(2,1)S(1)}, bf16[192,384]{1,0:T(8,128)(2,1)S(1)}, u32[]{:S(2)}, u32[]{:S(2)}) collective-permute-start(bf16[192,384]{1,0:T(8,128)(2,1)S(1)} %get-tuple-element.41), channel_id=1, source_target_pairs={{0,16},{4,20},{8,24},{12,28},{16,0},{20,4},{24,8},{28,12},{1,17},{... | collective-permute-start | bytes 442376 | tf_op jit(solution)/shard_map/ppermute | solution.py:50
  75.2 5.2 %collective-permute-start.10 = (bf16[192,384]{1,0:T(8,128)(2,1)S(1)}, bf16[192,384]{1,0:T(8,128)(2,1)S(1)}, u32[]{:S(2)}, u32[]{:S(2)}) collective-permute-start(bf16[192,384]{1,0:T(8,128)(2,1)S(1)} %get-tuple-element.39), channel_id=1, source_target_pairs={{0,16},{4,20},{8,24},{12,28},{16,0},{20,4},{24,8},{28,12},{1,17},{... | collective-permute-start | bytes 442376 | tf_op jit(solution)/shard_map/ppermute | solution.py:50
  76.8 5.1 %collective-permute-start.11 = (bf16[192,384]{1,0:T(8,128)(2,1)S(1)}, bf16[192,384]{1,0:T(8,128)(2,1)S(1)}, u32[]{:S(2)}, u32[]{:S(2)}) collective-permute-start(bf16[192,384]{1,0:T(8,128)(2,1)S(1)} %get-tuple-element.40), channel_id=1, source_target_pairs={{0,8},{4,12},{8,0},{12,4},{16,24},{20,28},{24,16},{28,20},{1,9},{5... | collective-permute-start | bytes 442376 | tf_op jit(solution)/shard_map/ppermute | solution.py:50
  82.1 6.0 %collective-permute-start.15 = (bf16[192,384]{1,0:T(8,128)(2,1)S(1)}, bf16[192,384]{1,0:T(8,128)(2,1)S(1)}, u32[]{:S(2)}, u32[]{:S(2)}) collective-permute-start(bf16[192,384]{1,0:T(8,128)(2,1)S(1)} %get-tuple-element.42.low_ref), channel_id=1, source_target_pairs={{0,16},{4,20},{8,24},{12,28},{16,0},{20,4},{24,8},{28,12},{1,17},{... | collective-permute-start | bytes 442376 | tf_op jit(solution)/shard_map/ppermute | solution.py:50
  82.7 6.2 %collective-permute-start.14 = (bf16[192,384]{1,0:T(8,128)(2,1)S(1)}, bf16[192,384]{1,0:T(8,128)(2,1)S(1)}, u32[]{:S(2)}, u32[]{:S(2)}) collective-permute-start(bf16[192,384]{1,0:T(8,128)(2,1)S(1)} %get-tuple-element.43.high_ref), channel_id=1, source_target_pairs={{0,8},{4,12},{8,0},{12,4},{16,24},{20,28},{24,16},{28,20},{1,9},{5... | collective-permute-start | bytes 442376 | tf_op jit(solution)/shard_map/ppermute | solution.py:50
  82.8 7.7 %collective-permute-start.13 = (bf16[192,384]{1,0:T(8,128)(2,1)S(1)}, bf16[192,384]{1,0:T(8,128)(2,1)S(1)}, u32[]{:S(2)}, u32[]{:S(2)}) collective-permute-start(bf16[192,384]{1,0:T(8,128)(2,1)S(1)} %get-tuple-element.44.refs_0_), channel_id=1, source_target_pairs={{0,8},{4,12},{8,0},{12,4},{16,24},{20,28},{24,16},{28,20},{1,9},{5... | collective-permute-start | bytes 442376 | tf_op jit(solution)/shard_map/ppermute | solution.py:50
  84.8 5.7 %collective-permute-start.16 = (bf16[192,384]{1,0:T(8,128)(2,1)S(1)}, bf16[192,384]{1,0:T(8,128)(2,1)S(1)}, u32[]{:S(2)}, u32[]{:S(2)}) collective-permute-start(bf16[192,384]{1,0:T(8,128)(2,1)S(1)} %get-tuple-element.45.refs_1_), channel_id=1, source_target_pairs={{0,16},{4,20},{8,24},{12,28},{16,0},{20,4},{24,8},{28,12},{1,17},{... | collective-permute-start | bytes 442376 | tf_op jit(solution)/shard_map/ppermute | solution.py:50
  88.1 5.1 %collective-permute-start.17 = (bf16[192,384]{1,0:T(8,128)(2,1)S(1)}, bf16[192,384]{1,0:T(8,128)(2,1)S(1)}, u32[]{:S(2)}, u32[]{:S(2)}) collective-permute-start(bf16[192,384]{1,0:T(8,128)(2,1)S(1)} %collective-permute-done.15.refs_4_), channel_id=1, source_target_pairs={{0,8},{4,12},{8,0},{12,4},{16,24},{20,28},{24,16},{28,20},{1,9},{5... | collective-permute-start | bytes 442376 | tf_op jit(solution)/shard_map/ppermute | solution.py:50
  88.9 5.1 %collective-permute-start.18 = (bf16[192,384]{1,0:T(8,128)(2,1)S(1)}, bf16[192,384]{1,0:T(8,128)(2,1)S(1)}, u32[]{:S(2)}, u32[]{:S(2)}) collective-permute-start(bf16[192,384]{1,0:T(8,128)(2,1)S(1)} %collective-permute-done.14.refs_3_), channel_id=1, source_target_pairs={{0,16},{4,20},{8,24},{12,28},{16,0},{20,4},{24,8},{28,12},{1,17},{... | collective-permute-start | bytes 442376 | tf_op jit(solution)/shard_map/ppermute | solution.py:50
  94.2 2.9 %collective-permute-start.19 = (bf16[1536,384]{1,0:T(8,128)(2,1)S(1)}, bf16[1536,384]{1,0:T(8,128)(2,1)S(1)}, u32[]{:S(2)}, u32[]{:S(2)}) collective-permute-start(bf16[1536,384]{1,0:T(8,128)(2,1)S(1)} %shard_map.87.mine_ref), channel_id=1, source_target_pairs={{0,4},{4,0},{8,12},{12,8},{16,20},{20,16},{24,28},{28,24},{1,5},{5... | collective-permute-start | bytes 3538952 | tf_op jit(solution)/shard_map/ppermute | solution.py:50
  99.6 9.7 %collective-permute-start.20 = (bf16[384,384]{1,0:T(8,128)(2,1)S(1)}, bf16[384,384]{1,0:T(8,128)(2,1)S(1)}, u32[]{:S(2)}, u32[]{:S(2)}) collective-permute-start(bf16[384,384]{1,0:T(8,128)(2,1)S(1)} %shard_map.89), channel_id=1, source_target_pairs={{0,3},{1,0},{2,1},{3,2},{4,7},{5,4},{6,5},{7,6},{8,11},{9,8},{10,9... | collective-permute-start | bytes 884744 | tf_op jit(solution)/shard_map/ppermute | solution.py:46
  104.4 11.8 %collective-permute-start.22 = (bf16[384,384]{1,0:T(8,128)(2,1)S(1)}, bf16[384,384]{1,0:T(8,128)(2,1)S(1)}, u32[]{:S(2)}, u32[]{:S(2)}) collective-permute-start(bf16[384,384]{1,0:T(8,128)(2,1)S(1)} %shard_map.90), channel_id=1, source_target_pairs={{0,1},{1,2},{2,3},{3,0},{4,5},{5,6},{6,7},{7,4},{8,9},{9,10},{10,1... | collective-permute-start | bytes 884744 | tf_op jit(solution)/shard_map/ppermute | solution.py:46
  109.4 12.5 %collective-permute-start.21 = (bf16[384,384]{1,0:T(8,128)(2,1)S(1)}, bf16[384,384]{1,0:T(8,128)(2,1)S(1)}, u32[]{:S(2)}, u32[]{:S(2)}) collective-permute-start(bf16[384,384]{1,0:T(8,128)(2,1)S(1)} %add_convert_fusion.2), channel_id=1, source_target_pairs={{0,3},{1,0},{2,1},{3,2},{4,7},{5,4},{6,5},{7,6},{8,11},{9,8},{10,9... | collective-permute-start | bytes 884744 | tf_op jit(solution)/shard_map/ppermute | solution.py:46
  122.8 6.0 %collective-permute-start.28 = (bf16[96,384]{1,0:T(8,128)(2,1)S(1)}, bf16[96,384]{1,0:T(8,128)(2,1)S(1)}, u32[]{:S(2)}, u32[]{:S(2)}) collective-permute-start(bf16[96,384]{1,0:T(8,128)(2,1)S(1)} %get-tuple-element.56), channel_id=1, source_target_pairs={{0,24},{4,28},{8,16},{12,20},{16,8},{20,12},{24,0},{28,4},{1,25},{... | collective-permute-start | bytes 221192 | tf_op jit(solution)/shard_map/ppermute | solution.py:50
  123.9 8.7 %collective-permute-start.26 = (bf16[96,384]{1,0:T(8,128)(2,1)S(1)}, bf16[96,384]{1,0:T(8,128)(2,1)S(1)}, u32[]{:S(2)}, u32[]{:S(2)}) collective-permute-start(bf16[96,384]{1,0:T(8,128)(2,1)S(1)} %get-tuple-element.57), channel_id=1, source_target_pairs={{0,16},{4,20},{8,24},{12,28},{16,0},{20,4},{24,8},{28,12},{1,17},{... | collective-permute-start | bytes 221192 | tf_op jit(solution)/shard_map/ppermute | solution.py:50
  125.5 8.0 %collective-permute-start.24 = (bf16[96,384]{1,0:T(8,128)(2,1)S(1)}, bf16[96,384]{1,0:T(8,128)(2,1)S(1)}, u32[]{:S(2)}, u32[]{:S(2)}) collective-permute-start(bf16[96,384]{1,0:T(8,128)(2,1)S(1)} %get-tuple-element.58), channel_id=1, source_target_pairs={{0,8},{4,12},{8,0},{12,4},{16,24},{20,28},{24,16},{28,20},{1,9},{5... | collective-permute-start | bytes 221192 | tf_op jit(solution)/shard_map/ppermute | solution.py:50
  126.3 7.2 %collective-permute-start.23 = (bf16[96,384]{1,0:T(8,128)(2,1)S(1)}, bf16[96,384]{1,0:T(8,128)(2,1)S(1)}, u32[]{:S(2)}, u32[]{:S(2)}) collective-permute-start(bf16[96,384]{1,0:T(8,128)(2,1)S(1)} %get-tuple-element.59), channel_id=1, source_target_pairs={{0,0},{1,8},{2,16},{3,24},{4,4},{5,12},{6,20},{7,28},{8,1},{9,9},{... | collective-permute-start | bytes 221192 | tf_op jit(solution)/shard_map/ppermute | solution.py:87
  128.8 13.1 %collective-permute-start.29 = (bf16[96,384]{1,0:T(8,128)(2,1)S(1)}, bf16[96,384]{1,0:T(8,128)(2,1)S(1)}, u32[]{:S(2)}, u32[]{:S(2)}) collective-permute-start(bf16[96,384]{1,0:T(8,128)(2,1)S(1)} %collective-permute-done.28), channel_id=1, source_target_pairs={{0,3},{1,11},{2,19},{3,27},{4,7},{5,15},{6,23},{7,31},{8,2},{9,10}... | collective-permute-start | bytes 221192 | tf_op jit(solution)/shard_map/ppermute | solution.py:87
  132.7 9.2 %collective-permute-start.27 = (bf16[96,384]{1,0:T(8,128)(2,1)S(1)}, bf16[96,384]{1,0:T(8,128)(2,1)S(1)}, u32[]{:S(2)}, u32[]{:S(2)}) collective-permute-start(bf16[96,384]{1,0:T(8,128)(2,1)S(1)} %collective-permute-done.26), channel_id=1, source_target_pairs={{0,2},{1,10},{2,18},{3,26},{4,6},{5,14},{6,22},{7,30},{8,3},{9,11}... | collective-permute-start | bytes 221192 | tf_op jit(solution)/shard_map/ppermute | solution.py:87
  133.5 4.9 %collective-permute-start.25 = (bf16[96,384]{1,0:T(8,128)(2,1)S(1)}, bf16[96,384]{1,0:T(8,128)(2,1)S(1)}, u32[]{:S(2)}, u32[]{:S(2)}) collective-permute-start(bf16[96,384]{1,0:T(8,128)(2,1)S(1)} %collective-permute-done.24), channel_id=1, source_target_pairs={{0,1},{1,9},{2,17},{3,25},{4,5},{5,13},{6,21},{7,29},{8,0},{9,8},{... | collective-permute-start | bytes 221192 | tf_op jit(solution)/shard_map/ppermute | solution.py:87
  138.4 7.9 %collective-permute-start.32 = (bf16[192,384]{1,0:T(8,128)(2,1)S(1)}, bf16[192,384]{1,0:T(8,128)(2,1)S(1)}, u32[]{:S(2)}, u32[]{:S(2)}) collective-permute-start(bf16[192,384]{1,0:T(8,128)(2,1)S(1)} %constant_dynamic-update-slice_fusion.low_ref), channel_id=1, source_target_pairs={{0,16},{4,20},{8,24},{12,28},{16,0},{20,4},{24,8},{28,12},{1,17},{... | collective-permute-start | bytes 442376 | tf_op jit(solution)/shard_map/ppermute | solution.py:50
  141.9 6.4 %collective-permute-start.31 = (bf16[192,384]{1,0:T(8,128)(2,1)S(1)}, bf16[192,384]{1,0:T(8,128)(2,1)S(1)}, u32[]{:S(2)}, u32[]{:S(2)}) collective-permute-start(bf16[192,384]{1,0:T(8,128)(2,1)S(1)} %constant_dynamic-update-slice_fusion.2.high_ref), channel_id=1, source_target_pairs={{0,8},{4,12},{8,0},{12,4},{16,24},{20,28},{24,16},{28,20},{1,9},{5... | collective-permute-start | bytes 442376 | tf_op jit(solution)/shard_map/ppermute | solution.py:50
  143.7 6.2 %collective-permute-start.30 = (bf16[192,384]{1,0:T(8,128)(2,1)S(1)}, bf16[192,384]{1,0:T(8,128)(2,1)S(1)}, u32[]{:S(2)}, u32[]{:S(2)}) collective-permute-start(bf16[192,384]{1,0:T(8,128)(2,1)S(1)} %get-tuple-element.48.refs_0_), channel_id=1, source_target_pairs={{0,8},{4,12},{8,0},{12,4},{16,24},{20,28},{24,16},{28,20},{1,9},{5... | collective-permute-start | bytes 442376 | tf_op jit(solution)/shard_map/ppermute | solution.py:50
  144.1 5.8 %collective-permute-start.33 = (bf16[192,384]{1,0:T(8,128)(2,1)S(1)}, bf16[192,384]{1,0:T(8,128)(2,1)S(1)}, u32[]{:S(2)}, u32[]{:S(2)}) collective-permute-start(bf16[192,384]{1,0:T(8,128)(2,1)S(1)} %get-tuple-element.49.refs_1_), channel_id=1, source_target_pairs={{0,16},{4,20},{8,24},{12,28},{16,0},{20,4},{24,8},{28,12},{1,17},{... | collective-permute-start | bytes 442376 | tf_op jit(solution)/shard_map/ppermute | solution.py:50
  146.4 5.1 %collective-permute-start.34 = (bf16[192,384]{1,0:T(8,128)(2,1)S(1)}, bf16[192,384]{1,0:T(8,128)(2,1)S(1)}, u32[]{:S(2)}, u32[]{:S(2)}) collective-permute-start(bf16[192,384]{1,0:T(8,128)(2,1)S(1)} %collective-permute-done.32.refs_4_), channel_id=1, source_target_pairs={{0,8},{4,12},{8,0},{12,4},{16,24},{20,28},{24,16},{28,20},{1,9},{5... | collective-permute-start | bytes 442376 | tf_op jit(solution)/shard_map/ppermute | solution.py:50
  148.3 5.1 %collective-permute-start.35 = (bf16[192,384]{1,0:T(8,128)(2,1)S(1)}, bf16[192,384]{1,0:T(8,128)(2,1)S(1)}, u32[]{:S(2)}, u32[]{:S(2)}) collective-permute-start(bf16[192,384]{1,0:T(8,128)(2,1)S(1)} %collective-permute-done.31.refs_3_), channel_id=1, source_target_pairs={{0,16},{4,20},{8,24},{12,28},{16,0},{20,4},{24,8},{28,12},{1,17},{... | collective-permute-start | bytes 442376 | tf_op jit(solution)/shard_map/ppermute | solution.py:50
  153.5 2.9 %collective-permute-start.36 = (bf16[1536,384]{1,0:T(8,128)(2,1)S(1)}, bf16[1536,384]{1,0:T(8,128)(2,1)S(1)}, u32[]{:S(2)}, u32[]{:S(2)}) collective-permute-start(bf16[1536,384]{1,0:T(8,128)(2,1)S(1)} %shard_map.92.mine_ref), channel_id=1, source_target_pairs={{0,4},{4,0},{8,12},{12,8},{16,20},{20,16},{24,28},{28,24},{1,5},{5... | collective-permute-start | bytes 3538952 | tf_op jit(solution)/shard_map/ppermute | solution.py:50
  159.0 13.8 %collective-permute-start.37 = (bf16[384,512]{1,0:T(8,128)(2,1)S(1)}, bf16[384,512]{1,0:T(8,128)(2,1)S(1)}, u32[]{:S(2)}, u32[]{:S(2)}) collective-permute-start(bf16[384,512]{1,0:T(8,128)(2,1)S(1)} %get-tuple-element.52), channel_id=1, source_target_pairs={{0,3},{1,0},{2,1},{3,2},{4,7},{5,4},{6,5},{7,6},{8,11},{9,8},{10,9... | collective-permute-start | bytes 1179656 | tf_op jit(solution)/shard_map/ppermute | solution.py:46
  164.6 17.0 %collective-permute-start.39 = (bf16[384,512]{1,0:T(8,128)(2,1)S(1)}, bf16[384,512]{1,0:T(8,128)(2,1)S(1)}, u32[]{:S(2)}, u32[]{:S(2)}) collective-permute-start(bf16[384,512]{1,0:T(8,128)(2,1)S(1)} %shard_map.95), channel_id=1, source_target_pairs={{0,1},{1,2},{2,3},{3,0},{4,5},{5,6},{6,7},{7,4},{8,9},{9,10},{10,1... | collective-permute-start | bytes 1179656 | tf_op jit(solution)/shard_map/ppermute | solution.py:46
  172.8 36.8 %copy-start.2 = (bf16[512,2048]{1,0:T(8,128)(2,1)S(1)}, bf16[512,2048]{1,0:T(8,128)(2,1)}, u32[]{:S(2)}) copy-start(bf16[512,2048]{1,0:T(8,128)(2,1)} %a_ref.19) | copy-start | bytes 6291460
  173.0 16.6 %collective-permute-start.38 = (bf16[384,512]{1,0:T(8,128)(2,1)S(1)}, bf16[384,512]{1,0:T(8,128)(2,1)S(1)}, u32[]{:S(2)}, u32[]{:S(2)}) collective-permute-start(bf16[384,512]{1,0:T(8,128)(2,1)S(1)} %add_convert_fusion.1), channel_id=1, source_target_pairs={{0,3},{1,0},{2,1},{3,2},{4,7},{5,4},{6,5},{7,6},{8,11},{9,8},{10,9... | collective-permute-start | bytes 1179656 | tf_op jit(solution)/shard_map/ppermute | solution.py:46
  189.8 13.9 %collective-permute-start.40 = (bf16[384,512]{1,0:T(8,128)(2,1)S(1)}, bf16[384,512]{1,0:T(8,128)(2,1)S(1)}, u32[]{:S(2)}, u32[]{:S(2)}) collective-permute-start(bf16[384,512]{1,0:T(8,128)(2,1)S(1)} %add_convert_fusion.refs_1_), channel_id=1, source_target_pairs={{0,1},{1,2},{2,3},{3,0},{4,5},{5,6},{6,7},{7,4},{8,9},{9,10},{10,1... | collective-permute-start | bytes 1179656 | tf_op jit(solution)/shard_map/ppermute | solution.py:46
  190.4 19.2 %collective-permute-start.41 = (bf16[384,512]{1,0:T(8,128)(2,1)S(1)}, bf16[384,512]{1,0:T(8,128)(2,1)S(1)}, u32[]{:S(2)}, u32[]{:S(2)}) collective-permute-start(bf16[384,512]{1,0:T(8,128)(2,1)S(1)} %add_convert_fusion.refs_1_), channel_id=1, source_target_pairs={{0,3},{1,0},{2,1},{3,2},{4,7},{5,4},{6,5},{7,6},{8,11},{9,8},{10,9... | collective-permute-start | bytes 1179656 | tf_op jit(solution)/shard_map/ppermute | solution.py:46
  203.7 15.9 %collective-permute-start.42 = (bf16[384,512]{1,0:T(8,128)(2,1)S(1)}, bf16[384,512]{1,0:T(8,128)(2,1)S(1)}, u32[]{:S(2)}, u32[]{:S(2)}) collective-permute-start(bf16[384,512]{1,0:T(8,128)(2,1)S(1)} %collective-permute-done.40.refs_2_), channel_id=1, source_target_pairs={{0,1},{1,2},{2,3},{3,0},{4,5},{5,6},{6,7},{7,4},{8,9},{9,10},{10,1... | collective-permute-start | bytes 1179656 | tf_op jit(solution)/shard_map/ppermute | solution.py:46

commit v12 on v10

--- a/solution.py
+++ b/solution.py
@@ -50,6 +50,10 @@
     return lax.ppermute(x, "front", [(i, i ^ by) for i in range(size)])
 
 
+def cross(x, n, even, odd):
+    return lax.ppermute(x, "front", [(i, i ^ (odd if i % 2 else even)) for i in range(n)])
+
+
 def gather_row(x, n):
     found = [(0, x)]
     up, down = x, x
@@ -62,16 +66,17 @@
     return found
 
 
-def gather_front(low, high, n):
-    rows = low.shape[0]
-    x_high, y_low = swap(high, n, 2), swap(low, n, 4)
-    low, high = again(low, high)
-    x_low, y_high = swap(low, n, 2), swap(high, n, 4)
-    corner_low, corner_high = swap(y_low, n, 2), swap(x_high, n, 4)
-    mine = stack([low, high, x_low, x_high, y_low, y_high, corner_low, corner_high])
+def gather_front(at, first, second, n):
+    rows = first.shape[0]
+    near, side = cross(first, n, 2, 4), cross(second, n, 4, 2)
+    first, second = again(first, second)
+    near_late, side_late = cross(second, n, 2, 4), cross(first, n, 4, 2)
+    far, far_late = cross(near, n, 4, 2), cross(side, n, 2, 4)
+    blocks = [second, first, near_late, near, side, side_late, far_late, far]
+    mine = stack(at, blocks, [0, 1, 2, 3, 4, 5, 6, 7], [1, 0, 5, 4, 3, 2, 7, 6])
     return [
-        (chip, core, chip * 2 * rows, 2 * rows, blocks)
-        for core, blocks in ((0, mine), (1, swap(mine, n, 1)))
+        (chip, core, chip * 2 * rows, 2 * rows, found)
+        for core, found in ((0, mine), (1, swap(mine, n, 1)))
         for chip in range(4)
     ]
 
@@ -225,53 +230,66 @@
     return total
 
 
-def sum_halves(keep, came, halves):
+def half_rows(at_ref, rows, even, odd):
+    place = jnp.where(lax.rem(at_ref[1], 2) == 0, even, odd)
+    return pl.ds(pl.multiple_of(place * rows, rows), rows)
+
+
+def sum_halves(at, keep, came, halves):
     rows, width = keep.shape[0] // 8, keep.shape[1]
     outs = [jax.ShapeDtypeStruct((rows, width), BF16)] * len(halves)
-
-    def body(keep_ref, came_ref, *out_refs):
-        for (chip, which), out_ref in zip(halves, out_refs):
-            place = slice((2 * chip + which) * rows, (2 * chip + which + 1) * rows)
-            out_ref[...] = added(keep_ref[place, :], came_ref[place, :]).astype(BF16)
-
-    return kernel_call(body, outs, [], [keep, came], [], [], keep.size, keep.size)
-
-
-def sum_relayed(keep, came, low, high):
-    rows, width = low.shape
-
-    def body(keep_ref, came_ref, low_ref, high_ref, x_ref, y_ref):
-        for half, add_ref, out_ref in ((3, high_ref, x_ref), (4, low_ref, y_ref)):
-            place = slice(half * rows, (half + 1) * rows)
-            out_ref[...] = added(keep_ref[place, :], came_ref[place, :], add_ref[...]).astype(BF16)
+    more = [add for _, _, add in halves if add is not None]
+
+    def body(at_ref, keep_ref, came_ref, *refs):
+        more_refs, out_refs = list(refs[: len(more)]), refs[len(more) :]
+        for (even, odd, add), out_ref in zip(halves, out_refs):
+            place = half_rows(at_ref, rows, even, odd)
+            extra = [] if add is None else [more_refs.pop(0)[...]]
+            out_ref[...] = added(keep_ref[place, :], came_ref[place, :], *extra).astype(BF16)
+
+    return kernel_call(body, outs, [at], [keep, came, *more], [], [], 2 * keep.size, 2 * keep.size)
+
+
+def own_part(at, own_rhs, keep, came, first, second):
+    rows, width = own_rhs.shape[0] // 2, own_rhs.shape[1]
+
+    def body(at_ref, rhs_ref, keep_ref, came_ref, *refs):
+        for i, (even, odd) in enumerate(((1, 0), (0, 1))):
+            place = half_rows(at_ref, rows, even, odd)
+            adds = [ref[...] for ref in refs[2 * i : 2 * i + 2]]
+            total = added(keep_ref[place, :], came_ref[place, :], *adds)
+            refs[4 + i][...] = (rhs_ref[place, :] - total).astype(BF16)
 
     outs = [jax.ShapeDtypeStruct((rows, width), BF16)] * 2
-    return kernel_call(body, outs, [], [keep, came, low, high], [], [], 2 * keep.size, 2 * keep.size)
-
-
-def own_part(own_rhs, keep, came, low, high):
-    half, width = own_rhs.shape[0] // 2, own_rhs.shape[1]
-
-    def body(rhs_ref, keep_ref, came_ref, *refs):
-        *add_refs, low_ref, high_ref = refs
-        for start, adds, out_ref in ((0, add_refs[:2], low_ref), (half, add_refs[2:], high_ref)):
-            place = slice(start, start + half)
-            total = added(keep_ref[place, :], came_ref[place, :], *[ref[...] for ref in adds])
-            out_ref[...] = (rhs_ref[place, :] - total).astype(BF16)
-
-    outs = [jax.ShapeDtypeStruct((half, width), BF16)] * 2
-    return kernel_call(body, outs, [], [own_rhs, keep, came, *low, *high], [], [], keep.size, keep.size)
-
-
-def stack(blocks):
+    held = [own_rhs, keep, came, *first, *second]
+    return kernel_call(body, outs, [at], held, [], [], keep.size, keep.size)
+
+
+def stack(at, blocks, even, odd):
     rows, width = blocks[0].shape
 
-    def body(*refs):
-        for i, ref in enumerate(refs[:-1]):
-            refs[-1][i * rows : (i + 1) * rows, :] = ref[...]
+    def body(at_ref, *refs):
+        for ref, one, two in zip(refs, even, odd):
+            refs[-1][half_rows(at_ref, rows, one, two), :] = ref[...]
 
     out = jax.ShapeDtypeStruct((len(blocks) * rows, width), BF16)
-    return kernel_call(body, out, [], blocks, [], [], 0, 4 * len(blocks) * rows * width)
+    return kernel_call(body, out, [at], blocks, [], [], 0, 4 * len(blocks) * rows * width)
+
+
+def by_core(at, low, high):
+    def body(at_ref, low_ref, high_ref, first_ref, second_ref):
+        even = lax.rem(at_ref[1], 2) == 0
+
+        @pl.when(even)
+        def _():
+            first_ref[...], second_ref[...] = high_ref[...], low_ref[...]
+
+        @pl.when(jnp.logical_not(even))
+        def _():
+            first_ref[...], second_ref[...] = low_ref[...], high_ref[...]
+
+    outs = [jax.ShapeDtypeStruct(low.shape, BF16)] * 2
+    return kernel_call(body, outs, [at], [low, high], [], [], 0, 8 * low.size)
 
 
 def again(low, high):
@@ -398,13 +416,14 @@
         at, local_index, border_coupling, found[-1:], partial, n_row, n_front, span_rows
     )
     came = swap(send, n_front, 1)
-    low, high = sum_halves(keep, came, [(3, 0), (3, 1)])
-    low, high = swap(low, n_front, 2), swap(high, n_front, 4)
-    x_low, y_high = sum_halves(keep, came, [(1, 0), (2, 1)])
-    x_low, y_high = swap(x_low, n_front, 2), swap(y_high, n_front, 4)
-    x_high, y_low = sum_relayed(keep, came, low, high)
-    x_high, y_low = swap(x_high, n_front, 2), swap(y_low, n_front, 4)
-    pieces = gather_front(*own_part(own_rhs, keep, came, (x_low, y_low), (x_high, y_high)), n_front)
+    low, high = sum_halves(at, keep, came, [(6, 7, None), (7, 6, None)])
+    near, side = cross(low, n_front, 2, 4), cross(high, n_front, 4, 2)
+    plain = sum_halves(at, keep, came, [(2, 5, None), (5, 2, None)])
+    near_plain, side_plain = cross(plain[0], n_front, 2, 4), cross(plain[1], n_front, 4, 2)
+    relayed = sum_halves(at, keep, came, [(4, 3, near), (3, 4, side)])
+    side_sum, near_sum = cross(relayed[0], n_front, 4, 2), cross(relayed[1], n_front, 2, 4)
+    halves = own_part(at, own_rhs, keep, came, (side_plain, near_sum), (near_plain, side_sum))
+    pieces = gather_front(at, *halves, n_front)
 
     def root(offsets, kind):
         outs = root_products(at, inverse, pieces, offsets, [kind] * len(offsets), n_row, n_front)
@@ -415,7 +434,7 @@
         first.update(root([offset], BF16))
     rest = root(later_at + [0], F32)
     root_solution = scatter_row(first, rest, rest[0], n_row)
-    spans = gather_front(*to_plane(root_solution.astype(BF16), n_row), n_front)
+    spans = gather_front(at, *by_core(at, *to_plane(root_solution.astype(BF16), n_row)), n_front)
 
     out, picked = border_pick(at, local_index, border_coupling, spans, first_at[0], n_row, n_front)
     first = {first_at[0]: out}

time: 221 us -> 223 us (level)
  waiting for transfers between devices: 122 us -> 115 us
  starting transfers between devices: 58.3 us -> 63.5 us
  Pallas kernels: 32.9 us -> 36.8 us
    ppermute x0 -> x18, starting transfers between devices: none -> 28.4 us  [cross(): lax.ppermute(x, 'front', [(i, i ^ (odd if i % 2 else even)) for i in rang...]
    ppermute x24 -> x6, starting transfers between devices: 24.7 us -> 3.77 us  [swap(): return lax.ppermute(x, 'front', [(i, i ^ by) for i in range(size)])]
    ppermute x24 -> x6, waiting for transfers between devices: 31.1 us -> 11.2 us  [swap(): return lax.ppermute(x, 'front', [(i, i ^ by) for i in range(size)])]
    ppermute x0 -> x18, waiting for transfers between devices: none -> 15.4 us  [cross(): lax.ppermute(x, 'front', [(i, i ^ (odd if i % 2 else even)) for i in rang...]
    ppermute x15, starting transfers between devices: 28.2 us -> 24.1 us  [shift(): return lax.ppermute(x, 'row', [(i, (i + by) % size) for i in range(size)])]
    pallas_call x21 -> x22, Pallas kernels: 32.9 us -> 36.8 us  [kernel_call(): pl.pallas_call(body, out_shape=out_shape, grid_spec=pltpu.PrefetchScalarG...]
    unnamed x16 -> x14, local copies, waits for them, and re-layouts: 5.4 us -> 5.38 us
  transfers between devices with their start and end apart: 43 -> 43, of which waited for: 33 -> 29; matrix products, arithmetic and copies ran while one was open for 0% -> 0% of each run, Pallas kernels for 10% -> 10%
where the time goes in v12:
time: 223 us
  waiting for transfers between devices  115 us (52%)
  starting transfers between devices  63.5 us (28%)
  Pallas kernels  36.8 us (17%)
  local copies, waits for them, and re-layouts  5.41 us (2%)
    ppermute x15, waiting for transfers between devices, shift(): return lax.ppermute(x, 'row', [(i, (i + by) % size) for i in range(size)])  84.4 us
    pallas_call x22, Pallas kernels, kernel_call(): pl.pallas_call(body, out_shape=out_shape, grid_spec=pltpu.PrefetchScalarG...  36.8 us
    ppermute x18, starting transfers between devices, cross(): lax.ppermute(x, 'front', [(i, i ^ (odd if i % 2 else even)) for i in rang...  28.4 us
    ppermute x15, starting transfers between devices, shift(): return lax.ppermute(x, 'row', [(i, (i + by) % size) for i in range(size)])  24.1 us
    ppermute x18, waiting for transfers between devices, cross(): lax.ppermute(x, 'front', [(i, i ^ (odd if i % 2 else even)) for i in rang...  15.4 us
    ppermute x6, waiting for transfers between devices, swap(): return lax.ppermute(x, 'front', [(i, i ^ by) for i in range(size)])  11.2 us
    ppermute x4, starting transfers between devices, to_plane(): moved.append(lax.ppermute(quarter, ('front', 'row'), perm))  7.14 us
    unnamed x14, local copies, waits for them, and re-layouts  5.38 us
  transfers between devices with their start and end apart: 43, of which 29 were waited for; matrix products, arithmetic and copies ran while one was open for 0% of the time, Pallas kernels for 10%

profile of v12, /device:TPU:0, one launch (start us, length us, event | category | flops | bytes accessed | tf_op | source)
XLA Modules:
  0.0 222.8 jit_solution(1728469213124203682)
XLA Ops:
  0.6 3.1 %collective-permute-start = (bf16[512,384]{1,0:T(8,128)(2,1)}, bf16[512,384]{1,0:T(8,128)(2,1)S(1)}, u32[]{:S(2)}, u32[]{:S(2)}) collective-permute-start(bf16[512,384]{1,0:T(8,128)(2,1)} %refs_0_.1), channel_id=1, source_target_pairs={{0,1},{1,2},{2,3},{3,0},{4,5},{5,6},{6,7},{7,4},{8,9},{9,10},{10,1... | collective-permute-start | bytes 1179656 | tf_op jit(solution)/shard_map/ppermute | solution.py:46
  3.7 2.1 collective-permute-start.1
  5.8 10.1 %collective-permute-done.refs_1_ = bf16[512,384]{1,0:T(8,128)(2,1)S(1)} collective-permute-done((bf16[512,384]{1,0:T(8,128)(2,1)}, bf16[512,384]{1,0:T(8,128)(2,1)S(1)}, u32[]{:S(2)}, u32[]{:S(2)}) %collective-permute-start) | collective-permute-done | bytes 393248 | tf_op jit(solution)/shard_map/ppermute | solution.py:46
  16.0 7.1 %collective-permute-done.1.refs_2_ = bf16[512,384]{1,0:T(8,128)(2,1)S(1)} collective-permute-done((bf16[512,384]{1,0:T(8,128)(2,1)}, bf16[512,384]{1,0:T(8,128)(2,1)S(1)}, u32[]{:S(2)}, u32[]{:S(2)}) %collective-permute-start.1) | collective-permute-done | bytes 393248 | tf_op jit(solution)/shard_map/ppermute | solution.py:46
  23.1 1.6 copy-done.1
  24.7 1.0 copy-done.3
  25.7 1.5 shard_map.77.refs_0_
  27.3 4.7 %collective-permute-done.2.refs_1_ = bf16[512,384]{1,0:T(8,128)(2,1)S(1)} collective-permute-done((bf16[512,384]{1,0:T(8,128)(2,1)S(1)}, bf16[512,384]{1,0:T(8,128)(2,1)S(1)}, u32[]{:S(2)}, u32[]{:S(2)}) %collective-permute-start.2) | collective-permute-done | bytes 393248 | tf_op jit(solution)/shard_map/ppermute | solution.py:46
  32.0 1.7 shard_map.78
  33.7 3.8 %collective-permute-start.3 = (bf16[512,384]{1,0:T(8,128)(2,1)}, bf16[512,384]{1,0:T(8,128)(2,1)}, u32[]{:S(2)}, u32[]{:S(2)}) collective-permute-start(bf16[512,384]{1,0:T(8,128)(2,1)} %get-tuple-element.31.refs_0_), channel_id=1, source_target_pairs={{0,3},{1,0},{2,1},{3,2},{4,7},{5,4},{6,5},{7,6},{8,11},{9,8},{10,9... | collective-permute-start | bytes 1179656 | tf_op jit(solution)/shard_map/ppermute | solution.py:46
  37.5 10.2 %collective-permute-done.4.refs_1_ = bf16[512,384]{1,0:T(8,128)(2,1)S(1)} collective-permute-done((bf16[512,384]{1,0:T(8,128)(2,1)}, bf16[512,384]{1,0:T(8,128)(2,1)S(1)}, u32[]{:S(2)}, u32[]{:S(2)}) %collective-permute-start.4) | collective-permute-done | bytes 393248 | tf_op jit(solution)/shard_map/ppermute | solution.py:46
  47.8 2.8 %copy-done = bf16[1536,2048]{1,0:T(8,128)(2,1)S(1)} copy-done((bf16[1536,2048]{1,0:T(8,128)(2,1)S(1)}, bf16[1536,2048]{1,0:T(8,128)(2,1)}, u32[]{:S(2)}) %copy-start) | copy-done | bytes 6291480
  50.6 4.0 %shard_map.79 = (f32[1536,384]{1,0:T(8,128)S(1)}, f32[384,384]{1,0:T(8,128)S(1)}) custom-call(s32[2]{0:T(128)S(1)} %pad_add_fusion.at_ref, bf16[1536,2048]{1,0:T(8,128)(2,1)S(1)} %copy-done, bf16[512,384]{1,0:T(8,128)(2,1)} %get-tuple-element.31.refs_0_, bf16[512,384]{1,0:T(8,128)(2,1)S(1)} %collective-permute-done.4.refs_1_, f32[3072,384]{1,0:T(8,128)} %refs_2_.2), custom_call_target="tpu_custom_call" | custom-call | flops 1207959552 | bytes 3145728 | tf_op jit(solution)/shard_map/pallas_call | solution.py:29
  54.6 5.2 %shard_map.80 = (f32[1536,384]{1,0:T(8,128)S(1)}, bf16[1536,3072]{1,0:T(8,128)(2,1)S(1)}) custom-call(s32[2]{0:T(128)S(1)} %pad_add_fusion.at_ref, bf16[1536,2048]{1,0:T(8,128)(2,1)S(1)} %bitcast.5, bf16[512,384]{1,0:T(8,128)(2,1)} %collective-permute-done.3.refs_0_, f32[1536,384]{1,0:T(8,128)S(1)} %get-tuple-element.32.refs_1_, bf16[1536,3072]{1,0:T(8,128)(2,1)} %refs_2_.3), custom_call_target="tpu_custom_call" | custom-call | flops 603979776 | bytes 1572864 | tf_op jit(solution)/shard_map/pallas_call | solution.py:29
  59.8 1.6 collective-permute-done.5.refs_0_
  61.4 2.4 %shard_map.81 = (bf16[1536,384]{1,0:T(8,128)(2,1)S(1)}, bf16[1536,384]{1,0:T(8,128)(2,1)S(1)}) custom-call(s32[2]{0:T(128)S(1)} %pad_add_fusion.at_ref, s32[12]{0:T(128)S(1)} %subtract_bitcast_fusion.index_ref, bf16[1536,2048]{1,0:T(8,128)(2,1)S(1)} %bitcast.5, bf16[512,384]{1,0:T(8,128)(2,1)S(1)} %collective-permute-done.5.refs_0_, ...), custom_call_target="tpu_custom_call" | custom-call | flops 603979776 | bytes 1572864 | tf_op jit(solution)/shard_map/pallas_call | solution.py:29
  63.9 2.8 %collective-permute-done.6.came_ref = bf16[1536,384]{1,0:T(8,128)(2,1)S(1)} collective-permute-done((bf16[1536,384]{1,0:T(8,128)(2,1)S(1)}, bf16[1536,384]{1,0:T(8,128)(2,1)S(1)}, u32[]{:S(2)}, u32[]{:S(2)}) %collective-permute-start.6) | collective-permute-done | bytes 1179680 | tf_op jit(solution)/shard_map/ppermute | solution.py:50
  67.3 1.6 collective-permute-start.8
  68.9 1.5 collective-permute-start.9
  72.1 1.6 collective-permute-done.8.refs_0_
  76.0 1.9 collective-permute-start.12
  77.9 2.9 %collective-permute-done.10.refs_1_ = bf16[192,384]{1,0:T(8,128)(2,1)S(1)} collective-permute-done((bf16[192,384]{1,0:T(8,128)(2,1)S(1)}, bf16[192,384]{1,0:T(8,128)(2,1)S(1)}, u32[]{:S(2)}, u32[]{:S(2)}) %collective-permute-start.10) | collective-permute-done | bytes 147488 | tf_op jit(solution)/shard_map/ppermute | solution.py:54
  81.9 1.9 collective-permute-start.14
  83.8 2.0 collective-permute-start.15
  86.1 2.5 %collective-permute-done.14.refs_3_ = bf16[192,384]{1,0:T(8,128)(2,1)S(1)} collective-permute-done((bf16[192,384]{1,0:T(8,128)(2,1)S(1)}, bf16[192,384]{1,0:T(8,128)(2,1)S(1)}, u32[]{:S(2)}, u32[]{:S(2)}) %collective-permute-start.14) | collective-permute-done | bytes 147488 | tf_op jit(solution)/shard_map/ppermute | solution.py:54
  88.6 1.5 collective-permute-start.18
  90.1 2.5 %collective-permute-start.17 = (bf16[192,384]{1,0:T(8,128)(2,1)S(1)}, bf16[192,384]{1,0:T(8,128)(2,1)S(1)}, u32[]{:S(2)}, u32[]{:S(2)}) collective-permute-start(bf16[192,384]{1,0:T(8,128)(2,1)S(1)} %collective-permute-done.15.refs_4_), channel_id=1, source_target_pairs={{0,8},{4,20},{8,0},{12,28},{16,24},{20,4},{24,16},{28,12},{1,9},{5... | collective-permute-start | bytes 442376 | tf_op jit(solution)/shard_map/ppermute | solution.py:54
  92.7 1.7 collective-permute-done.18.refs_7_
  94.3 1.4 collective-permute-done.17.refs_6_
  96.4 2.8 %collective-permute-done.19.refs_4_.refs_5_.refs_6_.refs_7_ = bf16[1536,384]{1,0:T(8,128)(2,1)S(1)} collective-permute-done((bf16[1536,384]{1,0:T(8,128)(2,1)S(1)}, bf16[1536,384]{1,0:T(8,128)(2,1)S(1)}, u32[]{:S(2)}, u32[]{:S(2)}) %collective-permute-start.19) | collective-permute-done | bytes 1179680 | tf_op jit(solution)/shard_map/ppermute | solution.py:50
  99.3 2.5 %shard_map.89 = bf16[384,384]{1,0:T(8,128)(2,1)S(1)} custom-call(s32[2]{0:T(128)S(1)} %pad_add_fusion.at_ref, bf16[1536,3072]{1,0:T(8,128)(2,1)S(1)} %get-tuple-element.33.a_ref, bf16[1536,384]{1,0:T(8,128)(2,1)S(1)} %shard_map.87.refs_0_.refs_1_.refs_2_.refs_3_, bf16[1536,384]{1,0:T(8,128)(2,1)S(1)} %shard_map.87.refs_0_.refs_1_.refs_2_.refs_3_, ...), custom_call_target="tpu_custom_call" | custom-call | flops 905969664 | bytes 2359296 | tf_op jit(solution)/shard_map/pallas_call | solution.py:29
  101.8 2.3 %collective-permute-start.20 = (bf16[384,384]{1,0:T(8,128)(2,1)S(1)}, bf16[384,384]{1,0:T(8,128)(2,1)S(1)}, u32[]{:S(2)}, u32[]{:S(2)}) collective-permute-start(bf16[384,384]{1,0:T(8,128)(2,1)S(1)} %shard_map.89), channel_id=1, source_target_pairs={{0,3},{1,0},{2,1},{3,2},{4,7},{5,4},{6,5},{7,6},{8,11},{9,8},{10,9... | collective-permute-start | bytes 884744 | tf_op jit(solution)/shard_map/ppermute | solution.py:46
  104.1 2.5 %shard_map.90 = bf16[384,384]{1,0:T(8,128)(2,1)S(1)} custom-call(s32[2]{0:T(128)S(1)} %pad_add_fusion.at_ref, bf16[1536,3072]{1,0:T(8,128)(2,1)S(1)} %get-tuple-element.33.a_ref, bf16[1536,384]{1,0:T(8,128)(2,1)S(1)} %shard_map.87.refs_0_.refs_1_.refs_2_.refs_3_, bf16[1536,384]{1,0:T(8,128)(2,1)S(1)} %shard_map.87.refs_0_.refs_1_.refs_2_.refs_3_, ...), custom_call_target="tpu_custom_call" | custom-call | flops 905969664 | bytes 2359296 | tf_op jit(solution)/shard_map/pallas_call | solution.py:29
  106.7 3.8 %shard_map.88 = (f32[384,384]{1,0:T(8,128)S(1)}, f32[384,384]{1,0:T(8,128)S(1)}) custom-call(s32[2]{0:T(128)S(1)} %pad_add_fusion.at_ref, bf16[1536,3072]{1,0:T(8,128)(2,1)S(1)} %get-tuple-element.33.a_ref, bf16[1536,384]{1,0:T(8,128)(2,1)S(1)} %shard_map.87.refs_0_.refs_1_.refs_2_.refs_3_, bf16[1536,384]{1,0:T(8,128)(2,1)S(1)} %shard_map.87.refs_0_.refs_1_.refs_2_.refs_3_, ...), custom_call_target="tpu_custom_call" | custom-call | flops 1811939328 | bytes 4718592 | tf_op jit(solution)/shard_map/pallas_call | solution.py:29
  110.4 1.1 collective-permute-done.20
  111.6 4.3 %collective-permute-start.21 = (bf16[384,384]{1,0:T(8,128)(2,1)S(1)}, bf16[384,384]{1,0:T(8,128)(2,1)S(1)}, u32[]{:S(2)}, u32[]{:S(2)}) collective-permute-start(bf16[384,384]{1,0:T(8,128)(2,1)S(1)} %add_convert_fusion.2), channel_id=1, source_target_pairs={{0,3},{1,0},{2,1},{3,2},{4,7},{5,4},{6,5},{7,6},{8,11},{9,8},{10,9... | collective-permute-start | bytes 884744 | tf_op jit(solution)/shard_map/ppermute | solution.py:46
  115.9 2.5 %collective-permute-done.22 = bf16[384,384]{1,0:T(8,128)(2,1)S(1)} collective-permute-done((bf16[384,384]{1,0:T(8,128)(2,1)S(1)}, bf16[384,384]{1,0:T(8,128)(2,1)S(1)}, u32[]{:S(2)}, u32[]{:S(2)}) %collective-permute-start.22) | collective-permute-done | bytes 294944 | tf_op jit(solution)/shard_map/ppermute | solution.py:46
  118.4 5.7 %collective-permute-done.21 = bf16[384,384]{1,0:T(8,128)(2,1)S(1)} collective-permute-done((bf16[384,384]{1,0:T(8,128)(2,1)S(1)}, bf16[384,384]{1,0:T(8,128)(2,1)S(1)}, u32[]{:S(2)}, u32[]{:S(2)}) %collective-permute-start.21) | collective-permute-done | bytes 294944 | tf_op jit(solution)/shard_map/ppermute | solution.py:46
  125.7 2.8 %collective-permute-start.28 = (bf16[96,384]{1,0:T(8,128)(2,1)S(1)}, bf16[96,384]{1,0:T(8,128)(2,1)S(1)}, u32[]{:S(2)}, u32[]{:S(2)}) collective-permute-start(bf16[96,384]{1,0:T(8,128)(2,1)S(1)} %get-tuple-element.61), channel_id=1, source_target_pairs={{0,24},{4,28},{8,16},{12,20},{16,8},{20,12},{24,0},{28,4},{1,25},{... | collective-permute-start | bytes 221192 | tf_op jit(solution)/shard_map/ppermute | solution.py:50
  128.6 1.9 collective-permute-done.26
  131.5 3.3 %collective-permute-start.29 = (bf16[96,384]{1,0:T(8,128)(2,1)S(1)}, bf16[96,384]{1,0:T(8,128)(2,1)S(1)}, u32[]{:S(2)}, u32[]{:S(2)}) collective-permute-start(bf16[96,384]{1,0:T(8,128)(2,1)S(1)} %collective-permute-done.28), channel_id=1, source_target_pairs={{0,3},{1,11},{2,19},{3,27},{4,7},{5,15},{6,23},{7,31},{8,2},{9,10}... | collective-permute-start | bytes 221192 | tf_op jit(solution)/shard_map/ppermute | solution.py:97
  135.5 3.0 %collective-permute-start.25 = (bf16[96,384]{1,0:T(8,128)(2,1)S(1)}, bf16[96,384]{1,0:T(8,128)(2,1)S(1)}, u32[]{:S(2)}, u32[]{:S(2)}) collective-permute-start(bf16[96,384]{1,0:T(8,128)(2,1)S(1)} %collective-permute-done.24), channel_id=1, source_target_pairs={{0,1},{1,9},{2,17},{3,25},{4,5},{5,13},{6,21},{7,29},{8,0},{9,8},{... | collective-permute-start | bytes 221192 | tf_op jit(solution)/shard_map/ppermute | solution.py:97
  138.5 3.8 %collective-permute-done.25 = bf16[96,384]{1,0:T(8,128)(2,1)S(1)} collective-permute-done((bf16[96,384]{1,0:T(8,128)(2,1)S(1)}, bf16[96,384]{1,0:T(8,128)(2,1)S(1)}, u32[]{:S(2)}, u32[]{:S(2)}) %collective-permute-start.25) | collective-permute-done | bytes 73760 | tf_op jit(solution)/shard_map/ppermute | solution.py:97
  142.9 2.1 collective-permute-start.31
  145.0 4.9 %collective-permute-start.32 = (bf16[192,384]{1,0:T(8,128)(2,1)S(1)}, bf16[192,384]{1,0:T(8,128)(2,1)S(1)}, u32[]{:S(2)}, u32[]{:S(2)}) collective-permute-start(bf16[192,384]{1,0:T(8,128)(2,1)S(1)} %get-tuple-element.51.high_ref), channel_id=1, source_target_pairs={{0,16},{4,12},{8,24},{12,4},{16,0},{20,28},{24,8},{28,20},{1,17},{... | collective-permute-start | bytes 442376 | tf_op jit(solution)/shard_map/ppermute | solution.py:54
  150.6 4.6 %collective-permute-start.35 = (bf16[192,384]{1,0:T(8,128)(2,1)S(1)}, bf16[192,384]{1,0:T(8,128)(2,1)S(1)}, u32[]{:S(2)}, u32[]{:S(2)}) collective-permute-start(bf16[192,384]{1,0:T(8,128)(2,1)S(1)} %collective-permute-done.31.refs_3_), channel_id=1, source_target_pairs={{0,16},{4,12},{8,24},{12,4},{16,0},{20,28},{24,8},{28,20},{1,17},{... | collective-permute-start | bytes 442376 | tf_op jit(solution)/shard_map/ppermute | solution.py:54
  155.3 1.2 collective-permute-start.34
  156.5 1.9 collective-permute-done.35.refs_7_
  158.4 2.0 collective-permute-done.34.refs_6_
  161.2 2.8 %collective-permute-done.36.refs_4_.refs_5_.refs_6_.refs_7_ = bf16[1536,384]{1,0:T(8,128)(2,1)S(1)} collective-permute-done((bf16[1536,384]{1,0:T(8,128)(2,1)S(1)}, bf16[1536,384]{1,0:T(8,128)(2,1)S(1)}, u32[]{:S(2)}, u32[]{:S(2)}) %collective-permute-start.36) | collective-permute-done | bytes 1179680 | tf_op jit(solution)/shard_map/ppermute | solution.py:50
  164.0 2.0 shard_map.94
  166.0 1.2 collective-permute-start.37
  167.2 1.3 shard_map.96
  168.6 1.1 collective-permute-start.39
  169.6 1.9 shard_map.95
  171.6 14.4 %collective-permute-done.37 = bf16[384,512]{1,0:T(8,128)(2,1)S(1)} collective-permute-done((bf16[384,512]{1,0:T(8,128)(2,1)S(1)}, bf16[384,512]{1,0:T(8,128)(2,1)S(1)}, u32[]{:S(2)}, u32[]{:S(2)}) %collective-permute-start.37) | collective-permute-done | bytes 393248 | tf_op jit(solution)/shard_map/ppermute | solution.py:46
  186.2 8.2 %collective-permute-done.38 = bf16[384,512]{1,0:T(8,128)(2,1)S(1)} collective-permute-done((bf16[384,512]{1,0:T(8,128)(2,1)S(1)}, bf16[384,512]{1,0:T(8,128)(2,1)S(1)}, u32[]{:S(2)}, u32[]{:S(2)}) %collective-permute-start.38) | collective-permute-done | bytes 393248 | tf_op jit(solution)/shard_map/ppermute | solution.py:46
  194.6 4.3 %collective-permute-start.41 = (bf16[384,512]{1,0:T(8,128)(2,1)S(1)}, bf16[384,512]{1,0:T(8,128)(2,1)S(1)}, u32[]{:S(2)}, u32[]{:S(2)}) collective-permute-start(bf16[384,512]{1,0:T(8,128)(2,1)S(1)} %add_convert_fusion.refs_1_), channel_id=1, source_target_pairs={{0,3},{1,0},{2,1},{3,2},{4,7},{5,4},{6,5},{7,6},{8,11},{9,8},{10,9... | collective-permute-start | bytes 1179656 | tf_op jit(solution)/shard_map/ppermute | solution.py:46
  199.0 10.1 %collective-permute-done.40.refs_2_ = bf16[384,512]{1,0:T(8,128)(2,1)S(1)} collective-permute-done((bf16[384,512]{1,0:T(8,128)(2,1)S(1)}, bf16[384,512]{1,0:T(8,128)(2,1)S(1)}, u32[]{:S(2)}, u32[]{:S(2)}) %collective-permute-start.40) | collective-permute-done | bytes 393248 | tf_op jit(solution)/shard_map/ppermute | solution.py:46
  209.1 1.7 collective-permute-start.42
  210.8 5.2 %collective-permute-done.41.refs_3_ = bf16[384,512]{1,0:T(8,128)(2,1)S(1)} collective-permute-done((bf16[384,512]{1,0:T(8,128)(2,1)S(1)}, bf16[384,512]{1,0:T(8,128)(2,1)S(1)}, u32[]{:S(2)}, u32[]{:S(2)}) %collective-permute-start.41) | collective-permute-done | bytes 393248 | tf_op jit(solution)/shard_map/ppermute | solution.py:46
  216.0 1.5 shard_map.97.refs_0_
  217.6 3.4 %collective-permute-done.42.refs_1_ = bf16[384,512]{1,0:T(8,128)(2,1)S(1)} collective-permute-done((bf16[384,512]{1,0:T(8,128)(2,1)S(1)}, bf16[384,512]{1,0:T(8,128)(2,1)S(1)}, u32[]{:S(2)}, u32[]{:S(2)}) %collective-permute-start.42) | collective-permute-done | bytes 393248 | tf_op jit(solution)/shard_map/ppermute | solution.py:46
  220.9 1.9 shard_map.98
  (68 shorter events, 12.9 us)
Async XLA Ops:
  0.6 15.3 %collective-permute-start = (bf16[512,384]{1,0:T(8,128)(2,1)}, bf16[512,384]{1,0:T(8,128)(2,1)S(1)}, u32[]{:S(2)}, u32[]{:S(2)}) collective-permute-start(bf16[512,384]{1,0:T(8,128)(2,1)} %refs_0_.1), channel_id=1, source_target_pairs={{0,1},{1,2},{2,3},{3,0},{4,5},{5,6},{6,7},{7,4},{8,9},{9,10},{10,1... | collective-permute-start | bytes 1179656 | tf_op jit(solution)/shard_map/ppermute | solution.py:46
  3.7 19.4 %collective-permute-start.1 = (bf16[512,384]{1,0:T(8,128)(2,1)}, bf16[512,384]{1,0:T(8,128)(2,1)S(1)}, u32[]{:S(2)}, u32[]{:S(2)}) collective-permute-start(bf16[512,384]{1,0:T(8,128)(2,1)} %refs_0_.1), channel_id=1, source_target_pairs={{0,3},{1,0},{2,1},{3,2},{4,7},{5,4},{6,5},{7,6},{8,11},{9,8},{10,9... | collective-permute-start | bytes 1179656 | tf_op jit(solution)/shard_map/ppermute | solution.py:46
  15.9 16.0 %collective-permute-start.2 = (bf16[512,384]{1,0:T(8,128)(2,1)S(1)}, bf16[512,384]{1,0:T(8,128)(2,1)S(1)}, u32[]{:S(2)}, u32[]{:S(2)}) collective-permute-start(bf16[512,384]{1,0:T(8,128)(2,1)S(1)} %collective-permute-done.refs_1_), channel_id=1, source_target_pairs={{0,1},{1,2},{2,3},{3,0},{4,5},{5,6},{6,7},{7,4},{8,9},{9,10},{10,1... | collective-permute-start | bytes 1179656 | tf_op jit(solution)/shard_map/ppermute | solution.py:46
  23.1 1.6 copy-start.1
  24.7 1.0 copy-start.3
  25.7 28.8 %slice-start = ((s8[6291456]{0:T(1024)(128)(4,1)}), s8[2097152]{0:T(1024)(128)(4,1)S(1)}, s32[]{:S(2)}) async-start(s8[6291456]{0:T(1024)(128)(4,1)} %bitcast.4), calls=%async_computation | async-start | bytes 4194304
  27.2 20.5 %copy-start.4 = (s32[1,12]{1,0:T(1,128)S(1)}, s32[1,12]{1,0:T(1,128)}, u32[]{:S(2)}) copy-start(s32[1,12]{1,0:T(1,128)} %param.11) | copy-start | bytes 148
  33.7 14.1 %collective-permute-start.4 = (bf16[512,384]{1,0:T(8,128)(2,1)}, bf16[512,384]{1,0:T(8,128)(2,1)S(1)}, u32[]{:S(2)}, u32[]{:S(2)}) collective-permute-start(bf16[512,384]{1,0:T(8,128)(2,1)} %get-tuple-element.31.refs_0_), channel_id=1, source_target_pairs={{0,1},{1,2},{2,3},{3,0},{4,5},{5,6},{6,7},{7,4},{8,9},{9,10},{10,1... | collective-permute-start | bytes 1179656 | tf_op jit(solution)/shard_map/ppermute | solution.py:46
  33.7 20.8 %collective-permute-start.3 = (bf16[512,384]{1,0:T(8,128)(2,1)}, bf16[512,384]{1,0:T(8,128)(2,1)}, u32[]{:S(2)}, u32[]{:S(2)}) collective-permute-start(bf16[512,384]{1,0:T(8,128)(2,1)} %get-tuple-element.31.refs_0_), channel_id=1, source_target_pairs={{0,3},{1,0},{2,1},{3,2},{4,7},{5,4},{6,5},{7,6},{8,11},{9,8},{10,9... | collective-permute-start | bytes 1179656 | tf_op jit(solution)/shard_map/ppermute | solution.py:46
  47.8 13.6 %collective-permute-start.5 = (bf16[512,384]{1,0:T(8,128)(2,1)S(1)}, bf16[512,384]{1,0:T(8,128)(2,1)S(1)}, u32[]{:S(2)}, u32[]{:S(2)}) collective-permute-start(bf16[512,384]{1,0:T(8,128)(2,1)S(1)} %collective-permute-done.4.refs_1_), channel_id=1, source_target_pairs={{0,1},{1,2},{2,3},{3,0},{4,5},{5,6},{6,7},{7,4},{8,9},{9,10},{10,1... | collective-permute-start | bytes 1179656 | tf_op jit(solution)/shard_map/ppermute | solution.py:46
  47.8 2.8 %copy-start = (bf16[1536,2048]{1,0:T(8,128)(2,1)S(1)}, bf16[1536,2048]{1,0:T(8,128)(2,1)}, u32[]{:S(2)}) copy-start(bf16[1536,2048]{1,0:T(8,128)(2,1)} %a_ref.17) | copy-start | bytes 18874372
  50.6 4.0 %slice-start.1 = ((s8[6291456]{0:T(1024)(128)(4,1)}), s8[4194304]{0:T(1024)(128)(4,1)S(1)}, s32[]{:S(2)}) async-start(s8[6291456]{0:T(1024)(128)(4,1)} %bitcast.4), calls=%async_computation.1 | async-start | bytes 8388608
  63.8 2.9 %collective-permute-start.6 = (bf16[1536,384]{1,0:T(8,128)(2,1)S(1)}, bf16[1536,384]{1,0:T(8,128)(2,1)S(1)}, u32[]{:S(2)}, u32[]{:S(2)}) collective-permute-start(bf16[1536,384]{1,0:T(8,128)(2,1)S(1)} %get-tuple-element.37), channel_id=1, source_target_pairs={{0,4},{4,0},{8,12},{12,8},{16,20},{20,16},{24,28},{28,24},{1,5},{5... | collective-permute-start | bytes 3538952 | tf_op jit(solution)/shard_map/ppermute | solution.py:50
  67.3 6.5 %collective-permute-start.8 = (bf16[192,384]{1,0:T(8,128)(2,1)S(1)}, bf16[192,384]{1,0:T(8,128)(2,1)S(1)}, u32[]{:S(2)}, u32[]{:S(2)}) collective-permute-start(bf16[192,384]{1,0:T(8,128)(2,1)S(1)} %get-tuple-element.39), channel_id=1, source_target_pairs={{0,8},{4,20},{8,0},{12,28},{16,24},{20,4},{24,16},{28,12},{1,9},{5... | collective-permute-start | bytes 442376 | tf_op jit(solution)/shard_map/ppermute | solution.py:54
  68.9 5.7 %collective-permute-start.9 = (bf16[192,384]{1,0:T(8,128)(2,1)S(1)}, bf16[192,384]{1,0:T(8,128)(2,1)S(1)}, u32[]{:S(2)}, u32[]{:S(2)}) collective-permute-start(bf16[192,384]{1,0:T(8,128)(2,1)S(1)} %get-tuple-element.40), channel_id=1, source_target_pairs={{0,16},{4,12},{8,24},{12,4},{16,0},{20,28},{24,8},{28,20},{1,17},{... | collective-permute-start | bytes 442376 | tf_op jit(solution)/shard_map/ppermute | solution.py:54
  71.1 6.9 %collective-permute-start.7 = (bf16[192,384]{1,0:T(8,128)(2,1)S(1)}, bf16[192,384]{1,0:T(8,128)(2,1)S(1)}, u32[]{:S(2)}, u32[]{:S(2)}) collective-permute-start(bf16[192,384]{1,0:T(8,128)(2,1)S(1)} %get-tuple-element.38), channel_id=1, source_target_pairs={{0,16},{4,12},{8,24},{12,4},{16,0},{20,28},{24,8},{28,20},{1,17},{... | collective-permute-start | bytes 442376 | tf_op jit(solution)/shard_map/ppermute | solution.py:54
  71.6 6.3 %collective-permute-start.11 = (bf16[192,384]{1,0:T(8,128)(2,1)S(1)}, bf16[192,384]{1,0:T(8,128)(2,1)S(1)}, u32[]{:S(2)}, u32[]{:S(2)}) collective-permute-start(bf16[192,384]{1,0:T(8,128)(2,1)S(1)} %get-tuple-element.42), channel_id=1, source_target_pairs={{0,8},{4,20},{8,0},{12,28},{16,24},{20,4},{24,16},{28,12},{1,9},{5... | collective-permute-start | bytes 442376 | tf_op jit(solution)/shard_map/ppermute | solution.py:54
  75.3 5.5 %collective-permute-start.10 = (bf16[192,384]{1,0:T(8,128)(2,1)S(1)}, bf16[192,384]{1,0:T(8,128)(2,1)S(1)}, u32[]{:S(2)}, u32[]{:S(2)}) collective-permute-start(bf16[192,384]{1,0:T(8,128)(2,1)S(1)} %get-tuple-element.41), channel_id=1, source_target_pairs={{0,8},{4,20},{8,0},{12,28},{16,24},{20,4},{24,16},{28,12},{1,9},{5... | collective-permute-start | bytes 442376 | tf_op jit(solution)/shard_map/ppermute | solution.py:54
  76.0 5.1 %collective-permute-start.12 = (bf16[192,384]{1,0:T(8,128)(2,1)S(1)}, bf16[192,384]{1,0:T(8,128)(2,1)S(1)}, u32[]{:S(2)}, u32[]{:S(2)}) collective-permute-start(bf16[192,384]{1,0:T(8,128)(2,1)S(1)} %get-tuple-element.43), channel_id=1, source_target_pairs={{0,16},{4,12},{8,24},{12,4},{16,0},{20,28},{24,8},{28,20},{1,17},{... | collective-permute-start | bytes 442376 | tf_op jit(solution)/shard_map/ppermute | solution.py:54
  81.9 6.7 %collective-permute-start.14 = (bf16[192,384]{1,0:T(8,128)(2,1)S(1)}, bf16[192,384]{1,0:T(8,128)(2,1)S(1)}, u32[]{:S(2)}, u32[]{:S(2)}) collective-permute-start(bf16[192,384]{1,0:T(8,128)(2,1)S(1)} %get-tuple-element.44.low_ref), channel_id=1, source_target_pairs={{0,8},{4,20},{8,0},{12,28},{16,24},{20,4},{24,16},{28,12},{1,9},{5... | collective-permute-start | bytes 442376 | tf_op jit(solution)/shard_map/ppermute | solution.py:54
  83.8 6.3 %collective-permute-start.15 = (bf16[192,384]{1,0:T(8,128)(2,1)S(1)}, bf16[192,384]{1,0:T(8,128)(2,1)S(1)}, u32[]{:S(2)}, u32[]{:S(2)}) collective-permute-start(bf16[192,384]{1,0:T(8,128)(2,1)S(1)} %get-tuple-element.45.high_ref), channel_id=1, source_target_pairs={{0,16},{4,12},{8,24},{12,4},{16,0},{20,28},{24,8},{28,20},{1,17},{... | collective-permute-start | bytes 442376 | tf_op jit(solution)/shard_map/ppermute | solution.py:54
  85.8 6.8 %collective-permute-start.13 = (bf16[192,384]{1,0:T(8,128)(2,1)S(1)}, bf16[192,384]{1,0:T(8,128)(2,1)S(1)}, u32[]{:S(2)}, u32[]{:S(2)}) collective-permute-start(bf16[192,384]{1,0:T(8,128)(2,1)S(1)} %get-tuple-element.46.refs_0_), channel_id=1, source_target_pairs={{0,8},{4,20},{8,0},{12,28},{16,24},{20,4},{24,16},{28,12},{1,9},{5... | collective-permute-start | bytes 442376 | tf_op jit(solution)/shard_map/ppermute | solution.py:54
  86.0 6.7 %collective-permute-start.16 = (bf16[192,384]{1,0:T(8,128)(2,1)S(1)}, bf16[192,384]{1,0:T(8,128)(2,1)S(1)}, u32[]{:S(2)}, u32[]{:S(2)}) collective-permute-start(bf16[192,384]{1,0:T(8,128)(2,1)S(1)} %get-tuple-element.47.refs_1_), channel_id=1, source_target_pairs={{0,16},{4,12},{8,24},{12,4},{16,0},{20,28},{24,8},{28,20},{1,17},{... | collective-permute-start | bytes 442376 | tf_op jit(solution)/shard_map/ppermute | solution.py:54
  88.6 5.7 %collective-permute-start.18 = (bf16[192,384]{1,0:T(8,128)(2,1)S(1)}, bf16[192,384]{1,0:T(8,128)(2,1)S(1)}, u32[]{:S(2)}, u32[]{:S(2)}) collective-permute-start(bf16[192,384]{1,0:T(8,128)(2,1)S(1)} %collective-permute-done.14.refs_3_), channel_id=1, source_target_pairs={{0,16},{4,12},{8,24},{12,4},{16,0},{20,28},{24,8},{28,20},{1,17},{... | collective-permute-start | bytes 442376 | tf_op jit(solution)/shard_map/ppermute | solution.py:54
  90.1 5.6 %collective-permute-start.17 = (bf16[192,384]{1,0:T(8,128)(2,1)S(1)}, bf16[192,384]{1,0:T(8,128)(2,1)S(1)}, u32[]{:S(2)}, u32[]{:S(2)}) collective-permute-start(bf16[192,384]{1,0:T(8,128)(2,1)S(1)} %collective-permute-done.15.refs_4_), channel_id=1, source_target_pairs={{0,8},{4,20},{8,0},{12,28},{16,24},{20,4},{24,16},{28,12},{1,9},{5... | collective-permute-start | bytes 442376 | tf_op jit(solution)/shard_map/ppermute | solution.py:54
  96.4 2.9 %collective-permute-start.19 = (bf16[1536,384]{1,0:T(8,128)(2,1)S(1)}, bf16[1536,384]{1,0:T(8,128)(2,1)S(1)}, u32[]{:S(2)}, u32[]{:S(2)}) collective-permute-start(bf16[1536,384]{1,0:T(8,128)(2,1)S(1)} %shard_map.87.refs_0_.refs_1_.refs_2_.refs_3_), channel_id=1, source_target_pairs={{0,4},{4,0},{8,12},{12,8},{16,20},{20,16},{24,28},{28,24},{1,5},{5... | collective-permute-start | bytes 3538952 | tf_op jit(solution)/shard_map/ppermute | solution.py:50
  101.8 9.7 %collective-permute-start.20 = (bf16[384,384]{1,0:T(8,128)(2,1)S(1)}, bf16[384,384]{1,0:T(8,128)(2,1)S(1)}, u32[]{:S(2)}, u32[]{:S(2)}) collective-permute-start(bf16[384,384]{1,0:T(8,128)(2,1)S(1)} %shard_map.89), channel_id=1, source_target_pairs={{0,3},{1,0},{2,1},{3,2},{4,7},{5,4},{6,5},{7,6},{8,11},{9,8},{10,9... | collective-permute-start | bytes 884744 | tf_op jit(solution)/shard_map/ppermute | solution.py:46
  106.6 11.8 %collective-permute-start.22 = (bf16[384,384]{1,0:T(8,128)(2,1)S(1)}, bf16[384,384]{1,0:T(8,128)(2,1)S(1)}, u32[]{:S(2)}, u32[]{:S(2)}) collective-permute-start(bf16[384,384]{1,0:T(8,128)(2,1)S(1)} %shard_map.90), channel_id=1, source_target_pairs={{0,1},{1,2},{2,3},{3,0},{4,5},{5,6},{6,7},{7,4},{8,9},{9,10},{10,1... | collective-permute-start | bytes 884744 | tf_op jit(solution)/shard_map/ppermute | solution.py:46
  111.6 12.5 %collective-permute-start.21 = (bf16[384,384]{1,0:T(8,128)(2,1)S(1)}, bf16[384,384]{1,0:T(8,128)(2,1)S(1)}, u32[]{:S(2)}, u32[]{:S(2)}) collective-permute-start(bf16[384,384]{1,0:T(8,128)(2,1)S(1)} %add_convert_fusion.2), channel_id=1, source_target_pairs={{0,3},{1,0},{2,1},{3,2},{4,7},{5,4},{6,5},{7,6},{8,11},{9,8},{10,9... | collective-permute-start | bytes 884744 | tf_op jit(solution)/shard_map/ppermute | solution.py:46
  125.0 5.5 %collective-permute-start.26 = (bf16[96,384]{1,0:T(8,128)(2,1)S(1)}, bf16[96,384]{1,0:T(8,128)(2,1)S(1)}, u32[]{:S(2)}, u32[]{:S(2)}) collective-permute-start(bf16[96,384]{1,0:T(8,128)(2,1)S(1)} %get-tuple-element.60), channel_id=1, source_target_pairs={{0,16},{4,20},{8,24},{12,28},{16,0},{20,4},{24,8},{28,12},{1,17},{... | collective-permute-start | bytes 221192 | tf_op jit(solution)/shard_map/ppermute | solution.py:50
  125.7 5.8 %collective-permute-start.28 = (bf16[96,384]{1,0:T(8,128)(2,1)S(1)}, bf16[96,384]{1,0:T(8,128)(2,1)S(1)}, u32[]{:S(2)}, u32[]{:S(2)}) collective-permute-start(bf16[96,384]{1,0:T(8,128)(2,1)S(1)} %get-tuple-element.61), channel_id=1, source_target_pairs={{0,24},{4,28},{8,16},{12,20},{16,8},{20,12},{24,0},{28,4},{1,25},{... | collective-permute-start | bytes 221192 | tf_op jit(solution)/shard_map/ppermute | solution.py:50
  128.6 6.9 %collective-permute-start.24 = (bf16[96,384]{1,0:T(8,128)(2,1)S(1)}, bf16[96,384]{1,0:T(8,128)(2,1)S(1)}, u32[]{:S(2)}, u32[]{:S(2)}) collective-permute-start(bf16[96,384]{1,0:T(8,128)(2,1)S(1)} %get-tuple-element.62), channel_id=1, source_target_pairs={{0,8},{4,12},{8,0},{12,4},{16,24},{20,28},{24,16},{28,20},{1,9},{5... | collective-permute-start | bytes 221192 | tf_op jit(solution)/shard_map/ppermute | solution.py:50
  130.5 8.0 %collective-permute-start.27 = (bf16[96,384]{1,0:T(8,128)(2,1)S(1)}, bf16[96,384]{1,0:T(8,128)(2,1)S(1)}, u32[]{:S(2)}, u32[]{:S(2)}) collective-permute-start(bf16[96,384]{1,0:T(8,128)(2,1)S(1)} %collective-permute-done.26), channel_id=1, source_target_pairs={{0,2},{1,10},{2,18},{3,26},{4,6},{5,14},{6,22},{7,30},{8,3},{9,11}... | collective-permute-start | bytes 221192 | tf_op jit(solution)/shard_map/ppermute | solution.py:97
  131.5 6.9 %collective-permute-start.29 = (bf16[96,384]{1,0:T(8,128)(2,1)S(1)}, bf16[96,384]{1,0:T(8,128)(2,1)S(1)}, u32[]{:S(2)}, u32[]{:S(2)}) collective-permute-start(bf16[96,384]{1,0:T(8,128)(2,1)S(1)} %collective-permute-done.28), channel_id=1, source_target_pairs={{0,3},{1,11},{2,19},{3,27},{4,7},{5,15},{6,23},{7,31},{8,2},{9,10}... | collective-permute-start | bytes 221192 | tf_op jit(solution)/shard_map/ppermute | solution.py:97
  134.8 3.7 %collective-permute-start.23 = (bf16[96,384]{1,0:T(8,128)(2,1)S(1)}, bf16[96,384]{1,0:T(8,128)(2,1)S(1)}, u32[]{:S(2)}, u32[]{:S(2)}) collective-permute-start(bf16[96,384]{1,0:T(8,128)(2,1)S(1)} %get-tuple-element.63), channel_id=1, source_target_pairs={{0,0},{1,8},{2,16},{3,24},{4,4},{5,12},{6,20},{7,28},{8,1},{9,9},{... | collective-permute-start | bytes 221192 | tf_op jit(solution)/shard_map/ppermute | solution.py:97
  135.5 6.8 %collective-permute-start.25 = (bf16[96,384]{1,0:T(8,128)(2,1)S(1)}, bf16[96,384]{1,0:T(8,128)(2,1)S(1)}, u32[]{:S(2)}, u32[]{:S(2)}) collective-permute-start(bf16[96,384]{1,0:T(8,128)(2,1)S(1)} %collective-permute-done.24), channel_id=1, source_target_pairs={{0,1},{1,9},{2,17},{3,25},{4,5},{5,13},{6,21},{7,29},{8,0},{9,8},{... | collective-permute-start | bytes 221192 | tf_op jit(solution)/shard_map/ppermute | solution.py:97
  142.9 7.7 %collective-permute-start.31 = (bf16[192,384]{1,0:T(8,128)(2,1)S(1)}, bf16[192,384]{1,0:T(8,128)(2,1)S(1)}, u32[]{:S(2)}, u32[]{:S(2)}) collective-permute-start(bf16[192,384]{1,0:T(8,128)(2,1)S(1)} %get-tuple-element.50.low_ref), channel_id=1, source_target_pairs={{0,8},{4,20},{8,0},{12,28},{16,24},{20,4},{24,16},{28,12},{1,9},{5... | collective-permute-start | bytes 442376 | tf_op jit(solution)/shard_map/ppermute | solution.py:54
  145.0 10.3 %collective-permute-start.32 = (bf16[192,384]{1,0:T(8,128)(2,1)S(1)}, bf16[192,384]{1,0:T(8,128)(2,1)S(1)}, u32[]{:S(2)}, u32[]{:S(2)}) collective-permute-start(bf16[192,384]{1,0:T(8,128)(2,1)S(1)} %get-tuple-element.51.high_ref), channel_id=1, source_target_pairs={{0,16},{4,12},{8,24},{12,4},{16,0},{20,28},{24,8},{28,20},{1,17},{... | collective-permute-start | bytes 442376 | tf_op jit(solution)/shard_map/ppermute | solution.py:54
  150.0 6.5 %collective-permute-start.30 = (bf16[192,384]{1,0:T(8,128)(2,1)S(1)}, bf16[192,384]{1,0:T(8,128)(2,1)S(1)}, u32[]{:S(2)}, u32[]{:S(2)}) collective-permute-start(bf16[192,384]{1,0:T(8,128)(2,1)S(1)} %get-tuple-element.52.refs_0_), channel_id=1, source_target_pairs={{0,8},{4,20},{8,0},{12,28},{16,24},{20,4},{24,16},{28,12},{1,9},{5... | collective-permute-start | bytes 442376 | tf_op jit(solution)/shard_map/ppermute | solution.py:54
  150.6 5.8 %collective-permute-start.33 = (bf16[192,384]{1,0:T(8,128)(2,1)S(1)}, bf16[192,384]{1,0:T(8,128)(2,1)S(1)}, u32[]{:S(2)}, u32[]{:S(2)}) collective-permute-start(bf16[192,384]{1,0:T(8,128)(2,1)S(1)} %get-tuple-element.53.refs_1_), channel_id=1, source_target_pairs={{0,16},{4,12},{8,24},{12,4},{16,0},{20,28},{24,8},{28,20},{1,17},{... | collective-permute-start | bytes 442376 | tf_op jit(solution)/shard_map/ppermute | solution.py:54
  150.6 7.8 %collective-permute-start.35 = (bf16[192,384]{1,0:T(8,128)(2,1)S(1)}, bf16[192,384]{1,0:T(8,128)(2,1)S(1)}, u32[]{:S(2)}, u32[]{:S(2)}) collective-permute-start(bf16[192,384]{1,0:T(8,128)(2,1)S(1)} %collective-permute-done.31.refs_3_), channel_id=1, source_target_pairs={{0,16},{4,12},{8,24},{12,4},{16,0},{20,28},{24,8},{28,20},{1,17},{... | collective-permute-start | bytes 442376 | tf_op jit(solution)/shard_map/ppermute | solution.py:54
  155.3 5.1 %collective-permute-start.34 = (bf16[192,384]{1,0:T(8,128)(2,1)S(1)}, bf16[192,384]{1,0:T(8,128)(2,1)S(1)}, u32[]{:S(2)}, u32[]{:S(2)}) collective-permute-start(bf16[192,384]{1,0:T(8,128)(2,1)S(1)} %collective-permute-done.32.refs_4_), channel_id=1, source_target_pairs={{0,8},{4,20},{8,0},{12,28},{16,24},{20,4},{24,16},{28,12},{1,9},{5... | collective-permute-start | bytes 442376 | tf_op jit(solution)/shard_map/ppermute | solution.py:54
  161.1 2.9 %collective-permute-start.36 = (bf16[1536,384]{1,0:T(8,128)(2,1)S(1)}, bf16[1536,384]{1,0:T(8,128)(2,1)S(1)}, u32[]{:S(2)}, u32[]{:S(2)}) collective-permute-start(bf16[1536,384]{1,0:T(8,128)(2,1)S(1)} %shard_map.93.refs_0_.refs_1_.refs_2_.refs_3_), channel_id=1, source_target_pairs={{0,4},{4,0},{8,12},{12,8},{16,20},{20,16},{24,28},{28,24},{1,5},{5... | collective-permute-start | bytes 3538952 | tf_op jit(solution)/shard_map/ppermute | solution.py:50
  166.0 20.0 %collective-permute-start.37 = (bf16[384,512]{1,0:T(8,128)(2,1)S(1)}, bf16[384,512]{1,0:T(8,128)(2,1)S(1)}, u32[]{:S(2)}, u32[]{:S(2)}) collective-permute-start(bf16[384,512]{1,0:T(8,128)(2,1)S(1)} %get-tuple-element.56), channel_id=1, source_target_pairs={{0,3},{1,0},{2,1},{3,2},{4,7},{5,4},{6,5},{7,6},{8,11},{9,8},{10,9... | collective-permute-start | bytes 1179656 | tf_op jit(solution)/shard_map/ppermute | solution.py:46
  168.6 17.6 %collective-permute-start.39 = (bf16[384,512]{1,0:T(8,128)(2,1)S(1)}, bf16[384,512]{1,0:T(8,128)(2,1)S(1)}, u32[]{:S(2)}, u32[]{:S(2)}) collective-permute-start(bf16[384,512]{1,0:T(8,128)(2,1)S(1)} %shard_map.96), channel_id=1, source_target_pairs={{0,1},{1,2},{2,3},{3,0},{4,5},{5,6},{6,7},{7,4},{8,9},{9,10},{10,1... | collective-permute-start | bytes 1179656 | tf_op jit(solution)/shard_map/ppermute | solution.py:46
  186.0 30.1 %copy-start.2 = (bf16[512,2048]{1,0:T(8,128)(2,1)S(1)}, bf16[512,2048]{1,0:T(8,128)(2,1)}, u32[]{:S(2)}) copy-start(bf16[512,2048]{1,0:T(8,128)(2,1)} %a_ref.19) | copy-start | bytes 6291460
  186.1 8.3 %collective-permute-start.38 = (bf16[384,512]{1,0:T(8,128)(2,1)S(1)}, bf16[384,512]{1,0:T(8,128)(2,1)S(1)}, u32[]{:S(2)}, u32[]{:S(2)}) collective-permute-start(bf16[384,512]{1,0:T(8,128)(2,1)S(1)} %add_convert_fusion.1), channel_id=1, source_target_pairs={{0,3},{1,0},{2,1},{3,2},{4,7},{5,4},{6,5},{7,6},{8,11},{9,8},{10,9... | collective-permute-start | bytes 1179656 | tf_op jit(solution)/shard_map/ppermute | solution.py:46
  194.6 14.5 %collective-permute-start.40 = (bf16[384,512]{1,0:T(8,128)(2,1)S(1)}, bf16[384,512]{1,0:T(8,128)(2,1)S(1)}, u32[]{:S(2)}, u32[]{:S(2)}) collective-permute-start(bf16[384,512]{1,0:T(8,128)(2,1)S(1)} %add_convert_fusion.refs_1_), channel_id=1, source_target_pairs={{0,1},{1,2},{2,3},{3,0},{4,5},{5,6},{6,7},{7,4},{8,9},{9,10},{10,1... | collective-permute-start | bytes 1179656 | tf_op jit(solution)/shard_map/ppermute | solution.py:46
  194.6 21.4 %collective-permute-start.41 = (bf16[384,512]{1,0:T(8,128)(2,1)S(1)}, bf16[384,512]{1,0:T(8,128)(2,1)S(1)}, u32[]{:S(2)}, u32[]{:S(2)}) collective-permute-start(bf16[384,512]{1,0:T(8,128)(2,1)S(1)} %add_convert_fusion.refs_1_), channel_id=1, source_target_pairs={{0,3},{1,0},{2,1},{3,2},{4,7},{5,4},{6,5},{7,6},{8,11},{9,8},{10,9... | collective-permute-start | bytes 1179656 | tf_op jit(solution)/shard_map/ppermute | solution.py:46
  209.1 11.8 %collective-permute-start.42 = (bf16[384,512]{1,0:T(8,128)(2,1)S(1)}, bf16[384,512]{1,0:T(8,128)(2,1)S(1)}, u32[]{:S(2)}, u32[]{:S(2)}) collective-permute-start(bf16[384,512]{1,0:T(8,128)(2,1)S(1)} %collective-permute-done.40.refs_2_), channel_id=1, source_target_pairs={{0,1},{1,2},{2,3},{3,0},{4,5},{5,6},{6,7},{7,4},{8,9},{9,10},{10,1... | collective-permute-start | bytes 1179656 | tf_op jit(solution)/shard_map/ppermute | solution.py:46

commit v13 on v12

--- a/solution.py
+++ b/solution.py
@@ -10,6 +10,7 @@
 BLK = 128
 F32 = jnp.float32
 BF16 = jnp.bfloat16
+PLACE = ("row", "front")
 VMEM = pl.BlockSpec(memory_space=pltpu.VMEM)
 ANY = pl.BlockSpec(memory_space=pl.ANY)
 
@@ -24,10 +25,18 @@
 
 def kernel_call(body, outs, scalars, held, placed, scratch, flops, nbytes, final=False, loose=()):
     size = sum(2 * math.prod(s.shape) for s in scratch if s.dtype == BF16)
+    if scalars and scalars[0] is PLACE:
+        scalars = scalars[1:]
+
+        def placed_body(*refs):
+            body([lax.axis_index(name) for name in PLACE], *refs)
+
+    else:
+        placed_body = body
     single = not isinstance(outs, list)
     out_shape = [o if final else pltpu.VMEM(o.shape, o.dtype) for o in ([outs] if single else outs)]
     results = pl.pallas_call(
-        body,
+        placed_body,
         out_shape=out_shape,
         grid_spec=pltpu.PrefetchScalarGridSpec(
             num_scalar_prefetch=len(scalars),
@@ -384,8 +393,7 @@
 
 def solve(n_front, n_row, rhs_front, rhs_root, pivot_inverse, border_coupling, root_inverse, border_map):
     row_at = lax.axis_index("row").astype(jnp.int32)
-    front_at = lax.axis_index("front").astype(jnp.int32)
-    at = jnp.stack([row_at, front_at])
+    at = PLACE
     span_rows = root_inverse.shape[1]
     piece_rows, width = span_rows // n_front, rhs_front.shape[1]
     local_index = border_map[0] - row_at * (span_rows // BLK)

time: 223 us -> 220 us (0.987)
  waiting for transfers between devices: 115 us -> 136 us
  starting transfers between devices: 63.5 us -> 48.3 us
  Pallas kernels: 36.8 us -> 26.9 us
    ppermute x15, waiting for transfers between devices: 84.4 us -> 98.4 us  [shift(): return lax.ppermute(x, 'row', [(i, (i + by) % size) for i in range(size)])]
    pallas_call x22, Pallas kernels: 36.8 us -> 26.9 us  [kernel_call(): pl.pallas_call(placed_body, out_shape=out_shape, grid_spec=pltpu.Prefetch...]
    ppermute x15, starting transfers between devices: 24.1 us -> 17.4 us  [shift(): return lax.ppermute(x, 'row', [(i, (i + by) % size) for i in range(size)])]
    ppermute x18, starting transfers between devices: 28.4 us -> 21.8 us  [cross(): lax.ppermute(x, 'front', [(i, i ^ (odd if i % 2 else even)) for i in rang...]
    ppermute x18, waiting for transfers between devices: 15.4 us -> 22 us  [cross(): lax.ppermute(x, 'front', [(i, i ^ (odd if i % 2 else even)) for i in rang...]
  transfers between devices with their start and end apart: 43 -> 43, of which waited for: 29 -> 34; matrix products, arithmetic and copies ran while one was open for 0% -> 0% of each run, Pallas kernels for 10% -> 8%
where the time goes in v13:
time: 220 us; the launch traced here: 219 us
  waiting for transfers between devices  136 us (62%)
  starting transfers between devices  48.3 us (22%)
  Pallas kernels  26.9 us (12%)
  local copies, waits for them, and re-layouts  5.41 us (2%)
    ppermute x15, waiting for transfers between devices, shift(): return lax.ppermute(x, 'row', [(i, (i + by) % size) for i in range(size)])  98.4 us
    pallas_call x22, Pallas kernels, kernel_call(): pl.pallas_call(placed_body, out_shape=out_shape, grid_spec=pltpu.Prefetch...  26.9 us
    ppermute x18, waiting for transfers between devices, cross(): lax.ppermute(x, 'front', [(i, i ^ (odd if i % 2 else even)) for i in rang...  22 us
    ppermute x18, starting transfers between devices, cross(): lax.ppermute(x, 'front', [(i, i ^ (odd if i % 2 else even)) for i in rang...  21.8 us
    ppermute x15, starting transfers between devices, shift(): return lax.ppermute(x, 'row', [(i, (i + by) % size) for i in range(size)])  17.4 us
    ppermute x6, waiting for transfers between devices, swap(): return lax.ppermute(x, 'front', [(i, i ^ by) for i in range(size)])  11.9 us
    unnamed x14, local copies, waits for them, and re-layouts  5.38 us
    ppermute x4, starting transfers between devices, to_plane(): moved.append(lax.ppermute(quarter, ('front', 'row'), perm))  5.32 us
  transfers between devices with their start and end apart: 43, of which 34 were waited for; matrix products, arithmetic and copies ran while one was open for 0% of the time, Pallas kernels for 8%

profile of v13, /device:TPU:0, one launch (start us, length us, event | category | flops | bytes accessed | tf_op | source)
XLA Modules:
  0.0 219.1 jit_solution(8401061210170865118)
XLA Ops:
  0.6 3.1 %collective-permute-start = (bf16[512,384]{1,0:T(8,128)(2,1)}, bf16[512,384]{1,0:T(8,128)(2,1)S(1)}, u32[]{:S(2)}, u32[]{:S(2)}) collective-permute-start(bf16[512,384]{1,0:T(8,128)(2,1)} %refs_1_.5), channel_id=1, source_target_pairs={{0,1},{1,2},{2,3},{3,0},{4,5},{5,6},{6,7},{7,4},{8,9},{9,10},{10,1... | collective-permute-start | bytes 1179656 | tf_op jit(solution)/shard_map/ppermute | solution.py:55
  3.7 2.1 collective-permute-start.1
  5.8 10.1 %collective-permute-done.refs_2_ = bf16[512,384]{1,0:T(8,128)(2,1)S(1)} collective-permute-done((bf16[512,384]{1,0:T(8,128)(2,1)}, bf16[512,384]{1,0:T(8,128)(2,1)S(1)}, u32[]{:S(2)}, u32[]{:S(2)}) %collective-permute-start) | collective-permute-done | bytes 393248 | tf_op jit(solution)/shard_map/ppermute | solution.py:55
  15.9 7.2 %collective-permute-done.1.refs_3_ = bf16[512,384]{1,0:T(8,128)(2,1)S(1)} collective-permute-done((bf16[512,384]{1,0:T(8,128)(2,1)}, bf16[512,384]{1,0:T(8,128)(2,1)S(1)}, u32[]{:S(2)}, u32[]{:S(2)}) %collective-permute-start.1) | collective-permute-done | bytes 393248 | tf_op jit(solution)/shard_map/ppermute | solution.py:55
  23.1 1.6 copy-done.1
  24.7 1.0 copy-done.3
  25.7 1.0 shard_map.77.refs_1_
  26.7 5.2 %collective-permute-done.2.refs_2_ = bf16[512,384]{1,0:T(8,128)(2,1)S(1)} collective-permute-done((bf16[512,384]{1,0:T(8,128)(2,1)S(1)}, bf16[512,384]{1,0:T(8,128)(2,1)S(1)}, u32[]{:S(2)}, u32[]{:S(2)}) %collective-permute-start.2) | collective-permute-done | bytes 393248 | tf_op jit(solution)/shard_map/ppermute | solution.py:55
  32.0 1.2 shard_map.78
  33.1 3.8 %collective-permute-start.3 = (bf16[512,384]{1,0:T(8,128)(2,1)}, bf16[512,384]{1,0:T(8,128)(2,1)}, u32[]{:S(2)}, u32[]{:S(2)}) collective-permute-start(bf16[512,384]{1,0:T(8,128)(2,1)} %get-tuple-element.31.refs_1_), channel_id=1, source_target_pairs={{0,3},{1,0},{2,1},{3,2},{4,7},{5,4},{6,5},{7,6},{8,11},{9,8},{10,9... | collective-permute-start | bytes 1179656 | tf_op jit(solution)/shard_map/ppermute | solution.py:55
  37.0 10.2 %collective-permute-done.4.refs_2_ = bf16[512,384]{1,0:T(8,128)(2,1)S(1)} collective-permute-done((bf16[512,384]{1,0:T(8,128)(2,1)}, bf16[512,384]{1,0:T(8,128)(2,1)S(1)}, u32[]{:S(2)}, u32[]{:S(2)}) %collective-permute-start.4) | collective-permute-done | bytes 393248 | tf_op jit(solution)/shard_map/ppermute | solution.py:55
  47.2 2.8 %copy-done = bf16[1536,2048]{1,0:T(8,128)(2,1)S(1)} copy-done((bf16[1536,2048]{1,0:T(8,128)(2,1)S(1)}, bf16[1536,2048]{1,0:T(8,128)(2,1)}, u32[]{:S(2)}) %copy-start) | copy-done | bytes 6291480
  50.0 3.3 %shard_map.79 = (f32[1536,384]{1,0:T(8,128)S(1)}, f32[384,384]{1,0:T(8,128)S(1)}) custom-call(bf16[1536,2048]{1,0:T(8,128)(2,1)S(1)} %copy-done, bf16[512,384]{1,0:T(8,128)(2,1)} %get-tuple-element.31.refs_1_, bf16[512,384]{1,0:T(8,128)(2,1)S(1)} %collective-permute-done.4.refs_2_, f32[3072,384]{1,0:T(8,128)} %refs_3_.2), custom_call_target="tpu_custom_call" | custom-call | flops 1207959552 | bytes 3145728 | tf_op jit(solution)/shard_map/pallas_call | solution.py:38
  53.3 4.7 %shard_map.80 = (f32[1536,384]{1,0:T(8,128)S(1)}, bf16[1536,3072]{1,0:T(8,128)(2,1)S(1)}) custom-call(bf16[1536,2048]{1,0:T(8,128)(2,1)S(1)} %bitcast.3, bf16[512,384]{1,0:T(8,128)(2,1)} %collective-permute-done.3.refs_1_, f32[1536,384]{1,0:T(8,128)S(1)} %get-tuple-element.32.refs_2_, bf16[1536,3072]{1,0:T(8,128)(2,1)} %refs_3_.3), custom_call_target="tpu_custom_call" | custom-call | flops 603979776 | bytes 1572864 | tf_op jit(solution)/shard_map/pallas_call | solution.py:38
  58.0 2.8 %collective-permute-done.5.refs_2_ = bf16[512,384]{1,0:T(8,128)(2,1)S(1)} collective-permute-done((bf16[512,384]{1,0:T(8,128)(2,1)S(1)}, bf16[512,384]{1,0:T(8,128)(2,1)S(1)}, u32[]{:S(2)}, u32[]{:S(2)}) %collective-permute-start.5) | collective-permute-done | bytes 393248 | tf_op jit(solution)/shard_map/ppermute | solution.py:55
  60.8 2.4 %shard_map.81 = (bf16[1536,384]{1,0:T(8,128)(2,1)S(1)}, bf16[1536,384]{1,0:T(8,128)(2,1)S(1)}) custom-call(s32[12]{0:T(128)S(1)} %subtract_bitcast_fusion.refs_0_, bf16[1536,2048]{1,0:T(8,128)(2,1)S(1)} %bitcast.3, bf16[512,384]{1,0:T(8,128)(2,1)S(1)} %collective-permute-done.5.refs_2_, f32[1536,384]{1,0:T(8,128)S(1)} %get-tuple-element.35.refs_3_), custom_call_target="tpu_custom_call" | custom-call | flops 603979776 | bytes 1572864 | tf_op jit(solution)/shard_map/pallas_call | solution.py:38
  63.3 2.8 %collective-permute-done.6.refs_1_.refs_2_ = bf16[1536,384]{1,0:T(8,128)(2,1)S(1)} collective-permute-done((bf16[1536,384]{1,0:T(8,128)(2,1)S(1)}, bf16[1536,384]{1,0:T(8,128)(2,1)S(1)}, u32[]{:S(2)}, u32[]{:S(2)}) %collective-permute-start.6) | collective-permute-done | bytes 1179680 | tf_op jit(solution)/shard_map/ppermute | solution.py:59
  66.2 1.6 collective-permute-start.8
  67.8 1.5 collective-permute-start.9
  70.5 2.2 %collective-permute-done.8.refs_2_ = bf16[192,384]{1,0:T(8,128)(2,1)S(1)} collective-permute-done((bf16[192,384]{1,0:T(8,128)(2,1)S(1)}, bf16[192,384]{1,0:T(8,128)(2,1)S(1)}, u32[]{:S(2)}, u32[]{:S(2)}) %collective-permute-start.8) | collective-permute-done | bytes 147488 | tf_op jit(solution)/shard_map/ppermute | solution.py:63
  72.7 1.5 collective-permute-done.9.refs_3_
  75.3 1.5 collective-permute-start.12
  76.8 2.8 %collective-permute-done.10.refs_4_ = bf16[192,384]{1,0:T(8,128)(2,1)S(1)} collective-permute-done((bf16[192,384]{1,0:T(8,128)(2,1)S(1)}, bf16[192,384]{1,0:T(8,128)(2,1)S(1)}, u32[]{:S(2)}, u32[]{:S(2)}) %collective-permute-start.10) | collective-permute-done | bytes 147488 | tf_op jit(solution)/shard_map/ppermute | solution.py:63
  80.6 1.6 collective-permute-start.15
  82.9 1.4 collective-permute-start.13
  84.8 2.6 %collective-permute-done.15.refs_4_ = bf16[192,384]{1,0:T(8,128)(2,1)S(1)} collective-permute-done((bf16[192,384]{1,0:T(8,128)(2,1)S(1)}, bf16[192,384]{1,0:T(8,128)(2,1)S(1)}, u32[]{:S(2)}, u32[]{:S(2)}) %collective-permute-start.15) | collective-permute-done | bytes 147488 | tf_op jit(solution)/shard_map/ppermute | solution.py:63
  87.5 1.1 collective-permute-start.17
  88.5 1.2 collective-permute-start.18
  90.6 2.0 collective-permute-done.17.refs_6_
  92.6 1.1 collective-permute-done.18.refs_7_
  93.9 2.8 %collective-permute-done.19.refs_5_.refs_6_.refs_7_.refs_8_ = bf16[1536,384]{1,0:T(8,128)(2,1)S(1)} collective-permute-done((bf16[1536,384]{1,0:T(8,128)(2,1)S(1)}, bf16[1536,384]{1,0:T(8,128)(2,1)S(1)}, u32[]{:S(2)}, u32[]{:S(2)}) %collective-permute-start.19) | collective-permute-done | bytes 1179680 | tf_op jit(solution)/shard_map/ppermute | solution.py:59
  96.7 1.9 shard_map.89
  98.7 1.1 collective-permute-start.20
  99.8 1.9 shard_map.90
  101.7 1.0 collective-permute-start.22
  102.7 3.2 %shard_map.88 = (f32[384,384]{1,0:T(8,128)S(1)}, f32[384,384]{1,0:T(8,128)S(1)}) custom-call(bf16[1536,3072]{1,0:T(8,128)(2,1)S(1)} %get-tuple-element.33.refs_0_, bf16[1536,384]{1,0:T(8,128)(2,1)S(1)} %shard_map.87.refs_1_.refs_2_.refs_3_.refs_4_, bf16[1536,384]{1,0:T(8,128)(2,1)S(1)} %shard_map.87.refs_1_.refs_2_.refs_3_.refs_4_, ...), custom_call_target="tpu_custom_call" | custom-call | flops 1811939328 | bytes 4718592 | tf_op jit(solution)/shard_map/pallas_call | solution.py:38
  105.9 8.0 %collective-permute-done.20 = bf16[384,384]{1,0:T(8,128)(2,1)S(1)} collective-permute-done((bf16[384,384]{1,0:T(8,128)(2,1)S(1)}, bf16[384,384]{1,0:T(8,128)(2,1)S(1)}, u32[]{:S(2)}, u32[]{:S(2)}) %collective-permute-start.20) | collective-permute-done | bytes 294944 | tf_op jit(solution)/shard_map/ppermute | solution.py:55
  114.5 6.2 %collective-permute-done.21 = bf16[384,384]{1,0:T(8,128)(2,1)S(1)} collective-permute-done((bf16[384,384]{1,0:T(8,128)(2,1)S(1)}, bf16[384,384]{1,0:T(8,128)(2,1)S(1)}, u32[]{:S(2)}, u32[]{:S(2)}) %collective-permute-start.21) | collective-permute-done | bytes 294944 | tf_op jit(solution)/shard_map/ppermute | solution.py:55
  121.7 1.3 collective-permute-start.26
  123.0 1.3 collective-permute-start.28
  124.2 1.0 collective-permute-start.24
  126.8 2.5 %collective-permute-done.28 = bf16[96,384]{1,0:T(8,128)(2,1)S(1)} collective-permute-done((bf16[96,384]{1,0:T(8,128)(2,1)S(1)}, bf16[96,384]{1,0:T(8,128)(2,1)S(1)}, u32[]{:S(2)}, u32[]{:S(2)}) %collective-permute-start.28) | collective-permute-done | bytes 73760 | tf_op jit(solution)/shard_map/ppermute | solution.py:59
  129.3 1.4 collective-permute-start.29
  131.4 2.6 %collective-permute-start.25 = (bf16[96,384]{1,0:T(8,128)(2,1)S(1)}, bf16[96,384]{1,0:T(8,128)(2,1)S(1)}, u32[]{:S(2)}, u32[]{:S(2)}) collective-permute-start(bf16[96,384]{1,0:T(8,128)(2,1)S(1)} %collective-permute-done.24), channel_id=1, source_target_pairs={{0,1},{1,9},{2,17},{3,25},{4,5},{5,13},{6,21},{7,29},{8,0},{9,8},{... | collective-permute-start | bytes 221192 | tf_op jit(solution)/shard_map/ppermute | solution.py:106
  134.0 1.1 collective-permute-done.29
  135.1 3.0 %collective-permute-done.25 = bf16[96,384]{1,0:T(8,128)(2,1)S(1)} collective-permute-done((bf16[96,384]{1,0:T(8,128)(2,1)S(1)}, bf16[96,384]{1,0:T(8,128)(2,1)S(1)}, u32[]{:S(2)}, u32[]{:S(2)}) %collective-permute-start.25) | collective-permute-done | bytes 73760 | tf_op jit(solution)/shard_map/ppermute | solution.py:106
  138.2 6.5 %collective-permute-start.32 = (bf16[192,384]{1,0:T(8,128)(2,1)S(1)}, bf16[192,384]{1,0:T(8,128)(2,1)S(1)}, u32[]{:S(2)}, u32[]{:S(2)}) collective-permute-start(bf16[192,384]{1,0:T(8,128)(2,1)S(1)} %get-tuple-element.51.high_ref), channel_id=1, source_target_pairs={{0,16},{4,12},{8,24},{12,4},{16,0},{20,28},{24,8},{28,20},{1,17},{... | collective-permute-start | bytes 442376 | tf_op jit(solution)/shard_map/ppermute | solution.py:63
  144.7 2.1 collective-permute-start.30
  147.8 2.0 collective-permute-done.31.refs_3_
  149.9 1.5 collective-permute-done.30.refs_2_
  152.0 1.0 collective-permute-done.34.refs_6_
  153.0 2.0 collective-permute-done.35.refs_7_
  155.2 2.8 %collective-permute-done.36.refs_6_.refs_7_.refs_8_.refs_9_ = bf16[1536,384]{1,0:T(8,128)(2,1)S(1)} collective-permute-done((bf16[1536,384]{1,0:T(8,128)(2,1)S(1)}, bf16[1536,384]{1,0:T(8,128)(2,1)S(1)}, u32[]{:S(2)}, u32[]{:S(2)}) %collective-permute-start.36) | collective-permute-done | bytes 1179680 | tf_op jit(solution)/shard_map/ppermute | solution.py:59
  158.0 2.0 shard_map.94
  161.6 1.6 collective-permute-start.39
  163.1 1.4 shard_map.95
  164.6 15.1 %collective-permute-done.37 = bf16[384,512]{1,0:T(8,128)(2,1)S(1)} collective-permute-done((bf16[384,512]{1,0:T(8,128)(2,1)S(1)}, bf16[384,512]{1,0:T(8,128)(2,1)S(1)}, u32[]{:S(2)}, u32[]{:S(2)}) %collective-permute-start.37) | collective-permute-done | bytes 393248 | tf_op jit(solution)/shard_map/ppermute | solution.py:55
  179.9 10.0 %collective-permute-done.38 = bf16[384,512]{1,0:T(8,128)(2,1)S(1)} collective-permute-done((bf16[384,512]{1,0:T(8,128)(2,1)S(1)}, bf16[384,512]{1,0:T(8,128)(2,1)S(1)}, u32[]{:S(2)}, u32[]{:S(2)}) %collective-permute-start.38) | collective-permute-done | bytes 393248 | tf_op jit(solution)/shard_map/ppermute | solution.py:55
  190.1 3.8 %collective-permute-start.41 = (bf16[384,512]{1,0:T(8,128)(2,1)S(1)}, bf16[384,512]{1,0:T(8,128)(2,1)S(1)}, u32[]{:S(2)}, u32[]{:S(2)}) collective-permute-start(bf16[384,512]{1,0:T(8,128)(2,1)S(1)} %add_convert_fusion.refs_2_), channel_id=1, source_target_pairs={{0,3},{1,0},{2,1},{3,2},{4,7},{5,4},{6,5},{7,6},{8,11},{9,8},{10,9... | collective-permute-start | bytes 1179656 | tf_op jit(solution)/shard_map/ppermute | solution.py:55
  193.9 10.0 %collective-permute-done.40.refs_3_ = bf16[384,512]{1,0:T(8,128)(2,1)S(1)} collective-permute-done((bf16[384,512]{1,0:T(8,128)(2,1)S(1)}, bf16[384,512]{1,0:T(8,128)(2,1)S(1)}, u32[]{:S(2)}, u32[]{:S(2)}) %collective-permute-start.40) | collective-permute-done | bytes 393248 | tf_op jit(solution)/shard_map/ppermute | solution.py:55
  203.9 4.9 %collective-permute-done.41.refs_4_ = bf16[384,512]{1,0:T(8,128)(2,1)S(1)} collective-permute-done((bf16[384,512]{1,0:T(8,128)(2,1)S(1)}, bf16[384,512]{1,0:T(8,128)(2,1)S(1)}, u32[]{:S(2)}, u32[]{:S(2)}) %collective-permute-start.41) | collective-permute-done | bytes 393248 | tf_op jit(solution)/shard_map/ppermute | solution.py:55
  208.8 1.0 shard_map.97.refs_1_
  209.8 8.0 %collective-permute-done.42.refs_2_ = bf16[384,512]{1,0:T(8,128)(2,1)S(1)} collective-permute-done((bf16[384,512]{1,0:T(8,128)(2,1)S(1)}, bf16[384,512]{1,0:T(8,128)(2,1)S(1)}, u32[]{:S(2)}, u32[]{:S(2)}) %collective-permute-start.42) | collective-permute-done | bytes 393248 | tf_op jit(solution)/shard_map/ppermute | solution.py:55
  217.8 1.3 shard_map.98
  (67 shorter events, 13.3 us)
Async XLA Ops:
  0.6 15.3 %collective-permute-start = (bf16[512,384]{1,0:T(8,128)(2,1)}, bf16[512,384]{1,0:T(8,128)(2,1)S(1)}, u32[]{:S(2)}, u32[]{:S(2)}) collective-permute-start(bf16[512,384]{1,0:T(8,128)(2,1)} %refs_1_.5), channel_id=1, source_target_pairs={{0,1},{1,2},{2,3},{3,0},{4,5},{5,6},{6,7},{7,4},{8,9},{9,10},{10,1... | collective-permute-start | bytes 1179656 | tf_op jit(solution)/shard_map/ppermute | solution.py:55
  3.7 19.4 %collective-permute-start.1 = (bf16[512,384]{1,0:T(8,128)(2,1)}, bf16[512,384]{1,0:T(8,128)(2,1)S(1)}, u32[]{:S(2)}, u32[]{:S(2)}) collective-permute-start(bf16[512,384]{1,0:T(8,128)(2,1)} %refs_1_.5), channel_id=1, source_target_pairs={{0,3},{1,0},{2,1},{3,2},{4,7},{5,4},{6,5},{7,6},{8,11},{9,8},{10,9... | collective-permute-start | bytes 1179656 | tf_op jit(solution)/shard_map/ppermute | solution.py:55
  15.9 16.0 %collective-permute-start.2 = (bf16[512,384]{1,0:T(8,128)(2,1)S(1)}, bf16[512,384]{1,0:T(8,128)(2,1)S(1)}, u32[]{:S(2)}, u32[]{:S(2)}) collective-permute-start(bf16[512,384]{1,0:T(8,128)(2,1)S(1)} %collective-permute-done.refs_2_), channel_id=1, source_target_pairs={{0,1},{1,2},{2,3},{3,0},{4,5},{5,6},{6,7},{7,4},{8,9},{9,10},{10,1... | collective-permute-start | bytes 1179656 | tf_op jit(solution)/shard_map/ppermute | solution.py:55
  23.1 1.6 copy-start.1
  24.7 1.0 copy-start.3
  25.7 27.6 %slice-start = ((s8[6291456]{0:T(1024)(128)(4,1)}), s8[2097152]{0:T(1024)(128)(4,1)S(1)}, s32[]{:S(2)}) async-start(s8[6291456]{0:T(1024)(128)(4,1)} %bitcast.2), calls=%async_computation | async-start | bytes 4194304
  26.7 20.5 %copy-start.4 = (s32[1,12]{1,0:T(1,128)S(1)}, s32[1,12]{1,0:T(1,128)}, u32[]{:S(2)}) copy-start(s32[1,12]{1,0:T(1,128)} %param.11) | copy-start | bytes 148
  33.1 14.1 %collective-permute-start.4 = (bf16[512,384]{1,0:T(8,128)(2,1)}, bf16[512,384]{1,0:T(8,128)(2,1)S(1)}, u32[]{:S(2)}, u32[]{:S(2)}) collective-permute-start(bf16[512,384]{1,0:T(8,128)(2,1)} %get-tuple-element.31.refs_1_), channel_id=1, source_target_pairs={{0,1},{1,2},{2,3},{3,0},{4,5},{5,6},{6,7},{7,4},{8,9},{9,10},{10,1... | collective-permute-start | bytes 1179656 | tf_op jit(solution)/shard_map/ppermute | solution.py:55
  33.1 20.2 %collective-permute-start.3 = (bf16[512,384]{1,0:T(8,128)(2,1)}, bf16[512,384]{1,0:T(8,128)(2,1)}, u32[]{:S(2)}, u32[]{:S(2)}) collective-permute-start(bf16[512,384]{1,0:T(8,128)(2,1)} %get-tuple-element.31.refs_1_), channel_id=1, source_target_pairs={{0,3},{1,0},{2,1},{3,2},{4,7},{5,4},{6,5},{7,6},{8,11},{9,8},{10,9... | collective-permute-start | bytes 1179656 | tf_op jit(solution)/shard_map/ppermute | solution.py:55
  47.2 13.6 %collective-permute-start.5 = (bf16[512,384]{1,0:T(8,128)(2,1)S(1)}, bf16[512,384]{1,0:T(8,128)(2,1)S(1)}, u32[]{:S(2)}, u32[]{:S(2)}) collective-permute-start(bf16[512,384]{1,0:T(8,128)(2,1)S(1)} %collective-permute-done.4.refs_2_), channel_id=1, source_target_pairs={{0,1},{1,2},{2,3},{3,0},{4,5},{5,6},{6,7},{7,4},{8,9},{9,10},{10,1... | collective-permute-start | bytes 1179656 | tf_op jit(solution)/shard_map/ppermute | solution.py:55
  47.2 2.8 %copy-start = (bf16[1536,2048]{1,0:T(8,128)(2,1)S(1)}, bf16[1536,2048]{1,0:T(8,128)(2,1)}, u32[]{:S(2)}) copy-start(bf16[1536,2048]{1,0:T(8,128)(2,1)} %refs_1_.9) | copy-start | bytes 18874372
  50.0 3.3 %slice-start.1 = ((s8[6291456]{0:T(1024)(128)(4,1)}), s8[4194304]{0:T(1024)(128)(4,1)S(1)}, s32[]{:S(2)}) async-start(s8[6291456]{0:T(1024)(128)(4,1)} %bitcast.2), calls=%async_computation.1 | async-start | bytes 8388608
  63.2 2.9 %collective-permute-start.6 = (bf16[1536,384]{1,0:T(8,128)(2,1)S(1)}, bf16[1536,384]{1,0:T(8,128)(2,1)S(1)}, u32[]{:S(2)}, u32[]{:S(2)}) collective-permute-start(bf16[1536,384]{1,0:T(8,128)(2,1)S(1)} %get-tuple-element.37), channel_id=1, source_target_pairs={{0,4},{4,0},{8,12},{12,8},{16,20},{20,16},{24,28},{28,24},{1,5},{5... | collective-permute-start | bytes 3538952 | tf_op jit(solution)/shard_map/ppermute | solution.py:59
  66.2 6.5 %collective-permute-start.8 = (bf16[192,384]{1,0:T(8,128)(2,1)S(1)}, bf16[192,384]{1,0:T(8,128)(2,1)S(1)}, u32[]{:S(2)}, u32[]{:S(2)}) collective-permute-start(bf16[192,384]{1,0:T(8,128)(2,1)S(1)} %get-tuple-element.39), channel_id=1, source_target_pairs={{0,8},{4,20},{8,0},{12,28},{16,24},{20,4},{24,16},{28,12},{1,9},{5... | collective-permute-start | bytes 442376 | tf_op jit(solution)/shard_map/ppermute | solution.py:63
  67.8 6.5 %collective-permute-start.9 = (bf16[192,384]{1,0:T(8,128)(2,1)S(1)}, bf16[192,384]{1,0:T(8,128)(2,1)S(1)}, u32[]{:S(2)}, u32[]{:S(2)}) collective-permute-start(bf16[192,384]{1,0:T(8,128)(2,1)S(1)} %get-tuple-element.40), channel_id=1, source_target_pairs={{0,16},{4,12},{8,24},{12,4},{16,0},{20,28},{24,8},{28,20},{1,17},{... | collective-permute-start | bytes 442376 | tf_op jit(solution)/shard_map/ppermute | solution.py:63
  69.4 7.4 %collective-permute-start.11 = (bf16[192,384]{1,0:T(8,128)(2,1)S(1)}, bf16[192,384]{1,0:T(8,128)(2,1)S(1)}, u32[]{:S(2)}, u32[]{:S(2)}) collective-permute-start(bf16[192,384]{1,0:T(8,128)(2,1)S(1)} %get-tuple-element.42), channel_id=1, source_target_pairs={{0,8},{4,20},{8,0},{12,28},{16,24},{20,4},{24,16},{28,12},{1,9},{5... | collective-permute-start | bytes 442376 | tf_op jit(solution)/shard_map/ppermute | solution.py:63
  70.0 6.8 %collective-permute-start.7 = (bf16[192,384]{1,0:T(8,128)(2,1)S(1)}, bf16[192,384]{1,0:T(8,128)(2,1)S(1)}, u32[]{:S(2)}, u32[]{:S(2)}) collective-permute-start(bf16[192,384]{1,0:T(8,128)(2,1)S(1)} %get-tuple-element.38), channel_id=1, source_target_pairs={{0,16},{4,12},{8,24},{12,4},{16,0},{20,28},{24,8},{28,20},{1,17},{... | collective-permute-start | bytes 442376 | tf_op jit(solution)/shard_map/ppermute | solution.py:63
  74.3 5.2 %collective-permute-start.10 = (bf16[192,384]{1,0:T(8,128)(2,1)S(1)}, bf16[192,384]{1,0:T(8,128)(2,1)S(1)}, u32[]{:S(2)}, u32[]{:S(2)}) collective-permute-start(bf16[192,384]{1,0:T(8,128)(2,1)S(1)} %get-tuple-element.41), channel_id=1, source_target_pairs={{0,8},{4,20},{8,0},{12,28},{16,24},{20,4},{24,16},{28,12},{1,9},{5... | collective-permute-start | bytes 442376 | tf_op jit(solution)/shard_map/ppermute | solution.py:63
  75.3 5.1 %collective-permute-start.12 = (bf16[192,384]{1,0:T(8,128)(2,1)S(1)}, bf16[192,384]{1,0:T(8,128)(2,1)S(1)}, u32[]{:S(2)}, u32[]{:S(2)}) collective-permute-start(bf16[192,384]{1,0:T(8,128)(2,1)S(1)} %get-tuple-element.43), channel_id=1, source_target_pairs={{0,16},{4,12},{8,24},{12,4},{16,0},{20,28},{24,8},{28,20},{1,17},{... | collective-permute-start | bytes 442376 | tf_op jit(solution)/shard_map/ppermute | solution.py:63
  80.6 6.9 %collective-permute-start.15 = (bf16[192,384]{1,0:T(8,128)(2,1)S(1)}, bf16[192,384]{1,0:T(8,128)(2,1)S(1)}, u32[]{:S(2)}, u32[]{:S(2)}) collective-permute-start(bf16[192,384]{1,0:T(8,128)(2,1)S(1)} %get-tuple-element.45.high_ref), channel_id=1, source_target_pairs={{0,16},{4,12},{8,24},{12,4},{16,0},{20,28},{24,8},{28,20},{1,17},{... | collective-permute-start | bytes 442376 | tf_op jit(solution)/shard_map/ppermute | solution.py:63
  82.2 6.3 %collective-permute-start.14 = (bf16[192,384]{1,0:T(8,128)(2,1)S(1)}, bf16[192,384]{1,0:T(8,128)(2,1)S(1)}, u32[]{:S(2)}, u32[]{:S(2)}) collective-permute-start(bf16[192,384]{1,0:T(8,128)(2,1)S(1)} %get-tuple-element.44.low_ref), channel_id=1, source_target_pairs={{0,8},{4,20},{8,0},{12,28},{16,24},{20,4},{24,16},{28,12},{1,9},{5... | collective-permute-start | bytes 442376 | tf_op jit(solution)/shard_map/ppermute | solution.py:63
  82.9 7.7 %collective-permute-start.13 = (bf16[192,384]{1,0:T(8,128)(2,1)S(1)}, bf16[192,384]{1,0:T(8,128)(2,1)S(1)}, u32[]{:S(2)}, u32[]{:S(2)}) collective-permute-start(bf16[192,384]{1,0:T(8,128)(2,1)S(1)} %get-tuple-element.46.refs_0_), channel_id=1, source_target_pairs={{0,8},{4,20},{8,0},{12,28},{16,24},{20,4},{24,16},{28,12},{1,9},{5... | collective-permute-start | bytes 442376 | tf_op jit(solution)/shard_map/ppermute | solution.py:63
  84.3 6.3 %collective-permute-start.16 = (bf16[192,384]{1,0:T(8,128)(2,1)S(1)}, bf16[192,384]{1,0:T(8,128)(2,1)S(1)}, u32[]{:S(2)}, u32[]{:S(2)}) collective-permute-start(bf16[192,384]{1,0:T(8,128)(2,1)S(1)} %get-tuple-element.47.refs_1_), channel_id=1, source_target_pairs={{0,16},{4,12},{8,24},{12,4},{16,0},{20,28},{24,8},{28,20},{1,17},{... | collective-permute-start | bytes 442376 | tf_op jit(solution)/shard_map/ppermute | solution.py:63
  87.5 5.1 %collective-permute-start.17 = (bf16[192,384]{1,0:T(8,128)(2,1)S(1)}, bf16[192,384]{1,0:T(8,128)(2,1)S(1)}, u32[]{:S(2)}, u32[]{:S(2)}) collective-permute-start(bf16[192,384]{1,0:T(8,128)(2,1)S(1)} %collective-permute-done.15.refs_4_), channel_id=1, source_target_pairs={{0,8},{4,20},{8,0},{12,28},{16,24},{20,4},{24,16},{28,12},{1,9},{5... | collective-permute-start | bytes 442376 | tf_op jit(solution)/shard_map/ppermute | solution.py:63
  88.5 5.1 %collective-permute-start.18 = (bf16[192,384]{1,0:T(8,128)(2,1)S(1)}, bf16[192,384]{1,0:T(8,128)(2,1)S(1)}, u32[]{:S(2)}, u32[]{:S(2)}) collective-permute-start(bf16[192,384]{1,0:T(8,128)(2,1)S(1)} %collective-permute-done.14.refs_3_), channel_id=1, source_target_pairs={{0,16},{4,12},{8,24},{12,4},{16,0},{20,28},{24,8},{28,20},{1,17},{... | collective-permute-start | bytes 442376 | tf_op jit(solution)/shard_map/ppermute | solution.py:63
  93.8 2.9 %collective-permute-start.19 = (bf16[1536,384]{1,0:T(8,128)(2,1)S(1)}, bf16[1536,384]{1,0:T(8,128)(2,1)S(1)}, u32[]{:S(2)}, u32[]{:S(2)}) collective-permute-start(bf16[1536,384]{1,0:T(8,128)(2,1)S(1)} %shard_map.87.refs_1_.refs_2_.refs_3_.refs_4_), channel_id=1, source_target_pairs={{0,4},{4,0},{8,12},{12,8},{16,20},{20,16},{24,28},{28,24},{1,5},{5... | collective-permute-start | bytes 3538952 | tf_op jit(solution)/shard_map/ppermute | solution.py:59
  98.7 15.3 %collective-permute-start.20 = (bf16[384,384]{1,0:T(8,128)(2,1)S(1)}, bf16[384,384]{1,0:T(8,128)(2,1)S(1)}, u32[]{:S(2)}, u32[]{:S(2)}) collective-permute-start(bf16[384,384]{1,0:T(8,128)(2,1)S(1)} %shard_map.89), channel_id=1, source_target_pairs={{0,3},{1,0},{2,1},{3,2},{4,7},{5,4},{6,5},{7,6},{8,11},{9,8},{10,9... | collective-permute-start | bytes 884744 | tf_op jit(solution)/shard_map/ppermute | solution.py:55
  101.7 12.8 %collective-permute-start.22 = (bf16[384,384]{1,0:T(8,128)(2,1)S(1)}, bf16[384,384]{1,0:T(8,128)(2,1)S(1)}, u32[]{:S(2)}, u32[]{:S(2)}) collective-permute-start(bf16[384,384]{1,0:T(8,128)(2,1)S(1)} %shard_map.90), channel_id=1, source_target_pairs={{0,1},{1,2},{2,3},{3,0},{4,5},{5,6},{6,7},{7,4},{8,9},{9,10},{10,1... | collective-permute-start | bytes 884744 | tf_op jit(solution)/shard_map/ppermute | solution.py:55
  114.0 6.8 %collective-permute-start.21 = (bf16[384,384]{1,0:T(8,128)(2,1)S(1)}, bf16[384,384]{1,0:T(8,128)(2,1)S(1)}, u32[]{:S(2)}, u32[]{:S(2)}) collective-permute-start(bf16[384,384]{1,0:T(8,128)(2,1)S(1)} %add_convert_fusion.2), channel_id=1, source_target_pairs={{0,3},{1,0},{2,1},{3,2},{4,7},{5,4},{6,5},{7,6},{8,11},{9,8},{10,9... | collective-permute-start | bytes 884744 | tf_op jit(solution)/shard_map/ppermute | solution.py:55
  121.7 4.4 %collective-permute-start.26 = (bf16[96,384]{1,0:T(8,128)(2,1)S(1)}, bf16[96,384]{1,0:T(8,128)(2,1)S(1)}, u32[]{:S(2)}, u32[]{:S(2)}) collective-permute-start(bf16[96,384]{1,0:T(8,128)(2,1)S(1)} %get-tuple-element.60), channel_id=1, source_target_pairs={{0,16},{4,20},{8,24},{12,28},{16,0},{20,4},{24,8},{28,12},{1,17},{... | collective-permute-start | bytes 221192 | tf_op jit(solution)/shard_map/ppermute | solution.py:59
  123.0 6.3 %collective-permute-start.28 = (bf16[96,384]{1,0:T(8,128)(2,1)S(1)}, bf16[96,384]{1,0:T(8,128)(2,1)S(1)}, u32[]{:S(2)}, u32[]{:S(2)}) collective-permute-start(bf16[96,384]{1,0:T(8,128)(2,1)S(1)} %get-tuple-element.61), channel_id=1, source_target_pairs={{0,24},{4,28},{8,16},{12,20},{16,8},{20,12},{24,0},{28,4},{1,25},{... | collective-permute-start | bytes 221192 | tf_op jit(solution)/shard_map/ppermute | solution.py:59
  124.2 7.1 %collective-permute-start.24 = (bf16[96,384]{1,0:T(8,128)(2,1)S(1)}, bf16[96,384]{1,0:T(8,128)(2,1)S(1)}, u32[]{:S(2)}, u32[]{:S(2)}) collective-permute-start(bf16[96,384]{1,0:T(8,128)(2,1)S(1)} %get-tuple-element.62), channel_id=1, source_target_pairs={{0,8},{4,12},{8,0},{12,4},{16,24},{20,28},{24,16},{28,20},{1,9},{5... | collective-permute-start | bytes 221192 | tf_op jit(solution)/shard_map/ppermute | solution.py:59
  126.1 7.9 %collective-permute-start.27 = (bf16[96,384]{1,0:T(8,128)(2,1)S(1)}, bf16[96,384]{1,0:T(8,128)(2,1)S(1)}, u32[]{:S(2)}, u32[]{:S(2)}) collective-permute-start(bf16[96,384]{1,0:T(8,128)(2,1)S(1)} %collective-permute-done.26), channel_id=1, source_target_pairs={{0,2},{1,10},{2,18},{3,26},{4,6},{5,14},{6,22},{7,30},{8,3},{9,11}... | collective-permute-start | bytes 221192 | tf_op jit(solution)/shard_map/ppermute | solution.py:106
  129.3 5.8 %collective-permute-start.29 = (bf16[96,384]{1,0:T(8,128)(2,1)S(1)}, bf16[96,384]{1,0:T(8,128)(2,1)S(1)}, u32[]{:S(2)}, u32[]{:S(2)}) collective-permute-start(bf16[96,384]{1,0:T(8,128)(2,1)S(1)} %collective-permute-done.28), channel_id=1, source_target_pairs={{0,3},{1,11},{2,19},{3,27},{4,7},{5,15},{6,23},{7,31},{8,2},{9,10}... | collective-permute-start | bytes 221192 | tf_op jit(solution)/shard_map/ppermute | solution.py:106
  130.7 4.4 %collective-permute-start.23 = (bf16[96,384]{1,0:T(8,128)(2,1)S(1)}, bf16[96,384]{1,0:T(8,128)(2,1)S(1)}, u32[]{:S(2)}, u32[]{:S(2)}) collective-permute-start(bf16[96,384]{1,0:T(8,128)(2,1)S(1)} %get-tuple-element.63), channel_id=1, source_target_pairs={{0,0},{1,8},{2,16},{3,24},{4,4},{5,12},{6,20},{7,28},{8,1},{9,9},{... | collective-permute-start | bytes 221192 | tf_op jit(solution)/shard_map/ppermute | solution.py:106
  131.4 6.8 %collective-permute-start.25 = (bf16[96,384]{1,0:T(8,128)(2,1)S(1)}, bf16[96,384]{1,0:T(8,128)(2,1)S(1)}, u32[]{:S(2)}, u32[]{:S(2)}) collective-permute-start(bf16[96,384]{1,0:T(8,128)(2,1)S(1)} %collective-permute-done.24), channel_id=1, source_target_pairs={{0,1},{1,9},{2,17},{3,25},{4,5},{5,13},{6,21},{7,29},{8,0},{9,8},{... | collective-permute-start | bytes 221192 | tf_op jit(solution)/shard_map/ppermute | solution.py:106
  138.2 9.6 %collective-permute-start.32 = (bf16[192,384]{1,0:T(8,128)(2,1)S(1)}, bf16[192,384]{1,0:T(8,128)(2,1)S(1)}, u32[]{:S(2)}, u32[]{:S(2)}) collective-permute-start(bf16[192,384]{1,0:T(8,128)(2,1)S(1)} %get-tuple-element.51.high_ref), channel_id=1, source_target_pairs={{0,16},{4,12},{8,24},{12,4},{16,0},{20,28},{24,8},{28,20},{1,17},{... | collective-permute-start | bytes 442376 | tf_op jit(solution)/shard_map/ppermute | solution.py:63
  144.7 5.1 %collective-permute-start.31 = (bf16[192,384]{1,0:T(8,128)(2,1)S(1)}, bf16[192,384]{1,0:T(8,128)(2,1)S(1)}, u32[]{:S(2)}, u32[]{:S(2)}) collective-permute-start(bf16[192,384]{1,0:T(8,128)(2,1)S(1)} %get-tuple-element.50.low_ref), channel_id=1, source_target_pairs={{0,8},{4,20},{8,0},{12,28},{16,24},{20,4},{24,16},{28,12},{1,9},{5... | collective-permute-start | bytes 442376 | tf_op jit(solution)/shard_map/ppermute | solution.py:63
  144.7 6.7 %collective-permute-start.30 = (bf16[192,384]{1,0:T(8,128)(2,1)S(1)}, bf16[192,384]{1,0:T(8,128)(2,1)S(1)}, u32[]{:S(2)}, u32[]{:S(2)}) collective-permute-start(bf16[192,384]{1,0:T(8,128)(2,1)S(1)} %get-tuple-element.52.refs_0_), channel_id=1, source_target_pairs={{0,8},{4,20},{8,0},{12,28},{16,24},{20,4},{24,16},{28,12},{1,9},{5... | collective-permute-start | bytes 442376 | tf_op jit(solution)/shard_map/ppermute | solution.py:63
  146.8 5.1 %collective-permute-start.33 = (bf16[192,384]{1,0:T(8,128)(2,1)S(1)}, bf16[192,384]{1,0:T(8,128)(2,1)S(1)}, u32[]{:S(2)}, u32[]{:S(2)}) collective-permute-start(bf16[192,384]{1,0:T(8,128)(2,1)S(1)} %get-tuple-element.53.refs_1_), channel_id=1, source_target_pairs={{0,16},{4,12},{8,24},{12,4},{16,0},{20,28},{24,8},{28,20},{1,17},{... | collective-permute-start | bytes 442376 | tf_op jit(solution)/shard_map/ppermute | solution.py:63
  147.8 5.2 %collective-permute-start.34 = (bf16[192,384]{1,0:T(8,128)(2,1)S(1)}, bf16[192,384]{1,0:T(8,128)(2,1)S(1)}, u32[]{:S(2)}, u32[]{:S(2)}) collective-permute-start(bf16[192,384]{1,0:T(8,128)(2,1)S(1)} %collective-permute-done.32.refs_4_), channel_id=1, source_target_pairs={{0,8},{4,20},{8,0},{12,28},{16,24},{20,4},{24,16},{28,12},{1,9},{5... | collective-permute-start | bytes 442376 | tf_op jit(solution)/shard_map/ppermute | solution.py:63
  149.8 5.1 %collective-permute-start.35 = (bf16[192,384]{1,0:T(8,128)(2,1)S(1)}, bf16[192,384]{1,0:T(8,128)(2,1)S(1)}, u32[]{:S(2)}, u32[]{:S(2)}) collective-permute-start(bf16[192,384]{1,0:T(8,128)(2,1)S(1)} %collective-permute-done.31.refs_3_), channel_id=1, source_target_pairs={{0,16},{4,12},{8,24},{12,4},{16,0},{20,28},{24,8},{28,20},{1,17},{... | collective-permute-start | bytes 442376 | tf_op jit(solution)/shard_map/ppermute | solution.py:63
  155.1 2.9 %collective-permute-start.36 = (bf16[1536,384]{1,0:T(8,128)(2,1)S(1)}, bf16[1536,384]{1,0:T(8,128)(2,1)S(1)}, u32[]{:S(2)}, u32[]{:S(2)}) collective-permute-start(bf16[1536,384]{1,0:T(8,128)(2,1)S(1)} %shard_map.93.refs_2_.refs_3_.refs_4_.refs_5_), channel_id=1, source_target_pairs={{0,4},{4,0},{8,12},{12,8},{16,20},{20,16},{24,28},{28,24},{1,5},{5... | collective-permute-start | bytes 3538952 | tf_op jit(solution)/shard_map/ppermute | solution.py:59
  160.0 19.6 %collective-permute-start.37 = (bf16[384,512]{1,0:T(8,128)(2,1)S(1)}, bf16[384,512]{1,0:T(8,128)(2,1)S(1)}, u32[]{:S(2)}, u32[]{:S(2)}) collective-permute-start(bf16[384,512]{1,0:T(8,128)(2,1)S(1)} %get-tuple-element.56), channel_id=1, source_target_pairs={{0,3},{1,0},{2,1},{3,2},{4,7},{5,4},{6,5},{7,6},{8,11},{9,8},{10,9... | collective-permute-start | bytes 1179656 | tf_op jit(solution)/shard_map/ppermute | solution.py:55
  161.6 18.3 %collective-permute-start.39 = (bf16[384,512]{1,0:T(8,128)(2,1)S(1)}, bf16[384,512]{1,0:T(8,128)(2,1)S(1)}, u32[]{:S(2)}, u32[]{:S(2)}) collective-permute-start(bf16[384,512]{1,0:T(8,128)(2,1)S(1)} %shard_map.96), channel_id=1, source_target_pairs={{0,1},{1,2},{2,3},{3,0},{4,5},{5,6},{6,7},{7,4},{8,9},{9,10},{10,1... | collective-permute-start | bytes 1179656 | tf_op jit(solution)/shard_map/ppermute | solution.py:55
  179.7 29.1 %copy-start.2 = (bf16[512,2048]{1,0:T(8,128)(2,1)S(1)}, bf16[512,2048]{1,0:T(8,128)(2,1)}, u32[]{:S(2)}) copy-start(bf16[512,2048]{1,0:T(8,128)(2,1)} %refs_0_.11) | copy-start | bytes 6291460
  179.8 10.0 %collective-permute-start.38 = (bf16[384,512]{1,0:T(8,128)(2,1)S(1)}, bf16[384,512]{1,0:T(8,128)(2,1)S(1)}, u32[]{:S(2)}, u32[]{:S(2)}) collective-permute-start(bf16[384,512]{1,0:T(8,128)(2,1)S(1)} %add_convert_fusion.1), channel_id=1, source_target_pairs={{0,3},{1,0},{2,1},{3,2},{4,7},{5,4},{6,5},{7,6},{8,11},{9,8},{10,9... | collective-permute-start | bytes 1179656 | tf_op jit(solution)/shard_map/ppermute | solution.py:55
  190.0 13.9 %collective-permute-start.40 = (bf16[384,512]{1,0:T(8,128)(2,1)S(1)}, bf16[384,512]{1,0:T(8,128)(2,1)S(1)}, u32[]{:S(2)}, u32[]{:S(2)}) collective-permute-start(bf16[384,512]{1,0:T(8,128)(2,1)S(1)} %add_convert_fusion.refs_2_), channel_id=1, source_target_pairs={{0,1},{1,2},{2,3},{3,0},{4,5},{5,6},{6,7},{7,4},{8,9},{9,10},{10,1... | collective-permute-start | bytes 1179656 | tf_op jit(solution)/shard_map/ppermute | solution.py:55
  190.1 18.7 %collective-permute-start.41 = (bf16[384,512]{1,0:T(8,128)(2,1)S(1)}, bf16[384,512]{1,0:T(8,128)(2,1)S(1)}, u32[]{:S(2)}, u32[]{:S(2)}) collective-permute-start(bf16[384,512]{1,0:T(8,128)(2,1)S(1)} %add_convert_fusion.refs_2_), channel_id=1, source_target_pairs={{0,3},{1,0},{2,1},{3,2},{4,7},{5,4},{6,5},{7,6},{8,11},{9,8},{10,9... | collective-permute-start | bytes 1179656 | tf_op jit(solution)/shard_map/ppermute | solution.py:55
  203.9 13.9 %collective-permute-start.42 = (bf16[384,512]{1,0:T(8,128)(2,1)S(1)}, bf16[384,512]{1,0:T(8,128)(2,1)S(1)}, u32[]{:S(2)}, u32[]{:S(2)}) collective-permute-start(bf16[384,512]{1,0:T(8,128)(2,1)S(1)} %collective-permute-done.40.refs_3_), channel_id=1, source_target_pairs={{0,1},{1,2},{2,3},{3,0},{4,5},{5,6},{6,7},{7,4},{8,9},{9,10},{10,1... | collective-permute-start | bytes 1179656 | tf_op jit(solution)/shard_map/ppermute | solution.py:55

commit v14 on v10

--- a/solution.py
+++ b/solution.py
@@ -10,6 +10,7 @@
 BLK = 128
 F32 = jnp.float32
 BF16 = jnp.bfloat16
+PLACE = ("row", "front")
 VMEM = pl.BlockSpec(memory_space=pltpu.VMEM)
 ANY = pl.BlockSpec(memory_space=pl.ANY)
 
@@ -24,10 +25,18 @@
 
 def kernel_call(body, outs, scalars, held, placed, scratch, flops, nbytes, final=False, loose=()):
     size = sum(2 * math.prod(s.shape) for s in scratch if s.dtype == BF16)
+    if scalars and scalars[0] is PLACE:
+        scalars = scalars[1:]
+
+        def placed_body(*refs):
+            body([lax.axis_index(name) for name in PLACE], *refs)
+
+    else:
+        placed_body = body
     single = not isinstance(outs, list)
     out_shape = [o if final else pltpu.VMEM(o.shape, o.dtype) for o in ([outs] if single else outs)]
     results = pl.pallas_call(
-        body,
+        placed_body,
         out_shape=out_shape,
         grid_spec=pltpu.PrefetchScalarGridSpec(
             num_scalar_prefetch=len(scalars),
@@ -366,8 +375,7 @@
 
 def solve(n_front, n_row, rhs_front, rhs_root, pivot_inverse, border_coupling, root_inverse, border_map):
     row_at = lax.axis_index("row").astype(jnp.int32)
-    front_at = lax.axis_index("front").astype(jnp.int32)
-    at = jnp.stack([row_at, front_at])
+    at = PLACE
     span_rows = root_inverse.shape[1]
     piece_rows, width = span_rows // n_front, rhs_front.shape[1]
     local_index = border_map[0] - row_at * (span_rows // BLK)

time: 221 us -> 217 us (0.982)
  Pallas kernels: 32.9 us -> 26.8 us
  waiting for transfers between devices: 122 us -> 128 us
  starting transfers between devices: 58.3 us -> 54.1 us
    ppermute x15, waiting for transfers between devices: 85.6 us -> 95.8 us  [shift(): return lax.ppermute(x, 'row', [(i, (i + by) % size) for i in range(size)])]
    pallas_call x21, Pallas kernels: 32.9 us -> 26.8 us  [kernel_call(): pl.pallas_call(placed_body, out_shape=out_shape, grid_spec=pltpu.Prefetch...]
    ppermute x15, starting transfers between devices: 28.2 us -> 22.5 us  [shift(): return lax.ppermute(x, 'row', [(i, (i + by) % size) for i in range(size)])]
    ppermute x4, starting transfers between devices: 5.41 us -> 7.7 us  [to_plane(): moved.append(lax.ppermute(quarter, ('front', 'row'), perm))]
  transfers between devices with their start and end apart: 43 -> 43, of which waited for: 33 -> 34; matrix products, arithmetic and copies ran while one was open for 0% -> 0% of each run, Pallas kernels for 10% -> 8%
where the time goes in v14:
time: 217 us; the launch traced here: 216 us
  waiting for transfers between devices  128 us (59%)
  starting transfers between devices  54.1 us (25%)
  Pallas kernels  26.8 us (12%)
  local copies, waits for them, and re-layouts  5.46 us (3%)
    ppermute x15, waiting for transfers between devices, shift(): return lax.ppermute(x, 'row', [(i, (i + by) % size) for i in range(size)])  95.8 us
    ppermute x24, waiting for transfers between devices, swap(): return lax.ppermute(x, 'front', [(i, i ^ by) for i in range(size)])  29.1 us
    pallas_call x21, Pallas kernels, kernel_call(): pl.pallas_call(placed_body, out_shape=out_shape, grid_spec=pltpu.Prefetch...  26.8 us
    ppermute x24, starting transfers between devices, swap(): return lax.ppermute(x, 'front', [(i, i ^ by) for i in range(size)])  23.8 us
    ppermute x15, starting transfers between devices, shift(): return lax.ppermute(x, 'row', [(i, (i + by) % size) for i in range(size)])  22.5 us
    ppermute x4, starting transfers between devices, to_plane(): moved.append(lax.ppermute(quarter, ('front', 'row'), perm))  7.7 us
    unnamed x16, local copies, waits for them, and re-layouts  5.4 us
  transfers between devices with their start and end apart: 43, of which 34 were waited for; matrix products, arithmetic and copies ran while one was open for 0% of the time, Pallas kernels for 8%

profile of v14, /device:TPU:0, one launch (start us, length us, event | category | flops | bytes accessed | tf_op | source)
XLA Modules:
  0.0 216.3 jit_solution(2544567983397990246)
XLA Ops:
  0.6 3.1 %collective-permute-start = (bf16[512,384]{1,0:T(8,128)(2,1)}, bf16[512,384]{1,0:T(8,128)(2,1)S(1)}, u32[]{:S(2)}, u32[]{:S(2)}) collective-permute-start(bf16[512,384]{1,0:T(8,128)(2,1)} %refs_1_.5), channel_id=1, source_target_pairs={{0,1},{1,2},{2,3},{3,0},{4,5},{5,6},{6,7},{7,4},{8,9},{9,10},{10,1... | collective-permute-start | bytes 1179656 | tf_op jit(solution)/shard_map/ppermute | solution.py:55
  3.7 2.1 collective-permute-start.1
  5.8 10.1 %collective-permute-done.refs_2_ = bf16[512,384]{1,0:T(8,128)(2,1)S(1)} collective-permute-done((bf16[512,384]{1,0:T(8,128)(2,1)}, bf16[512,384]{1,0:T(8,128)(2,1)S(1)}, u32[]{:S(2)}, u32[]{:S(2)}) %collective-permute-start) | collective-permute-done | bytes 393248 | tf_op jit(solution)/shard_map/ppermute | solution.py:55
  15.9 7.2 %collective-permute-done.1.refs_3_ = bf16[512,384]{1,0:T(8,128)(2,1)S(1)} collective-permute-done((bf16[512,384]{1,0:T(8,128)(2,1)}, bf16[512,384]{1,0:T(8,128)(2,1)S(1)}, u32[]{:S(2)}, u32[]{:S(2)}) %collective-permute-start.1) | collective-permute-done | bytes 393248 | tf_op jit(solution)/shard_map/ppermute | solution.py:55
  23.1 1.6 copy-done.1
  24.7 1.0 copy-done.3
  25.7 1.0 shard_map.77.refs_1_
  26.7 5.2 %collective-permute-done.2.refs_2_ = bf16[512,384]{1,0:T(8,128)(2,1)S(1)} collective-permute-done((bf16[512,384]{1,0:T(8,128)(2,1)S(1)}, bf16[512,384]{1,0:T(8,128)(2,1)S(1)}, u32[]{:S(2)}, u32[]{:S(2)}) %collective-permute-start.2) | collective-permute-done | bytes 393248 | tf_op jit(solution)/shard_map/ppermute | solution.py:55
  32.0 1.2 shard_map.78
  33.1 3.8 %collective-permute-start.3 = (bf16[512,384]{1,0:T(8,128)(2,1)}, bf16[512,384]{1,0:T(8,128)(2,1)}, u32[]{:S(2)}, u32[]{:S(2)}) collective-permute-start(bf16[512,384]{1,0:T(8,128)(2,1)} %get-tuple-element.29.refs_1_), channel_id=1, source_target_pairs={{0,3},{1,0},{2,1},{3,2},{4,7},{5,4},{6,5},{7,6},{8,11},{9,8},{10,9... | collective-permute-start | bytes 1179656 | tf_op jit(solution)/shard_map/ppermute | solution.py:55
  37.0 10.2 %collective-permute-done.4.refs_2_ = bf16[512,384]{1,0:T(8,128)(2,1)S(1)} collective-permute-done((bf16[512,384]{1,0:T(8,128)(2,1)}, bf16[512,384]{1,0:T(8,128)(2,1)S(1)}, u32[]{:S(2)}, u32[]{:S(2)}) %collective-permute-start.4) | collective-permute-done | bytes 393248 | tf_op jit(solution)/shard_map/ppermute | solution.py:55
  47.2 2.8 %copy-done = bf16[1536,2048]{1,0:T(8,128)(2,1)S(1)} copy-done((bf16[1536,2048]{1,0:T(8,128)(2,1)S(1)}, bf16[1536,2048]{1,0:T(8,128)(2,1)}, u32[]{:S(2)}) %copy-start) | copy-done | bytes 6291480
  50.0 3.3 %shard_map.79 = (f32[1536,384]{1,0:T(8,128)S(1)}, f32[384,384]{1,0:T(8,128)S(1)}) custom-call(bf16[1536,2048]{1,0:T(8,128)(2,1)S(1)} %copy-done, bf16[512,384]{1,0:T(8,128)(2,1)} %get-tuple-element.29.refs_1_, bf16[512,384]{1,0:T(8,128)(2,1)S(1)} %collective-permute-done.4.refs_2_, f32[3072,384]{1,0:T(8,128)} %refs_3_.2), custom_call_target="tpu_custom_call" | custom-call | flops 1207959552 | bytes 3145728 | tf_op jit(solution)/shard_map/pallas_call | solution.py:38
  53.3 4.7 %shard_map.80 = (f32[1536,384]{1,0:T(8,128)S(1)}, bf16[1536,3072]{1,0:T(8,128)(2,1)S(1)}) custom-call(bf16[1536,2048]{1,0:T(8,128)(2,1)S(1)} %bitcast.3, bf16[512,384]{1,0:T(8,128)(2,1)} %collective-permute-done.3.refs_1_, f32[1536,384]{1,0:T(8,128)S(1)} %get-tuple-element.30.refs_2_, bf16[1536,3072]{1,0:T(8,128)(2,1)} %refs_3_.3), custom_call_target="tpu_custom_call" | custom-call | flops 603979776 | bytes 1572864 | tf_op jit(solution)/shard_map/pallas_call | solution.py:38
  58.0 2.8 %collective-permute-done.5.refs_2_ = bf16[512,384]{1,0:T(8,128)(2,1)S(1)} collective-permute-done((bf16[512,384]{1,0:T(8,128)(2,1)S(1)}, bf16[512,384]{1,0:T(8,128)(2,1)S(1)}, u32[]{:S(2)}, u32[]{:S(2)}) %collective-permute-start.5) | collective-permute-done | bytes 393248 | tf_op jit(solution)/shard_map/ppermute | solution.py:55
  60.8 2.4 %shard_map.81 = (bf16[1536,384]{1,0:T(8,128)(2,1)S(1)}, bf16[1536,384]{1,0:T(8,128)(2,1)S(1)}) custom-call(s32[12]{0:T(128)S(1)} %subtract_bitcast_fusion.refs_0_, bf16[1536,2048]{1,0:T(8,128)(2,1)S(1)} %bitcast.3, bf16[512,384]{1,0:T(8,128)(2,1)S(1)} %collective-permute-done.5.refs_2_, f32[1536,384]{1,0:T(8,128)S(1)} %get-tuple-element.33.refs_3_), custom_call_target="tpu_custom_call" | custom-call | flops 603979776 | bytes 1572864 | tf_op jit(solution)/shard_map/pallas_call | solution.py:38
  63.3 2.8 %collective-permute-done.6.came_ref = bf16[1536,384]{1,0:T(8,128)(2,1)S(1)} collective-permute-done((bf16[1536,384]{1,0:T(8,128)(2,1)S(1)}, bf16[1536,384]{1,0:T(8,128)(2,1)S(1)}, u32[]{:S(2)}, u32[]{:S(2)}) %collective-permute-start.6) | collective-permute-done | bytes 1179680 | tf_op jit(solution)/shard_map/ppermute | solution.py:59
  66.2 1.6 collective-permute-start.8
  67.8 1.5 collective-permute-start.9
  70.5 2.0 collective-permute-done.8.low_ref
  72.4 2.1 collective-permute-done.9.high_ref
  74.6 1.6 collective-permute-start.10
  76.7 0.9 collective-permute-done.12.refs_3_
  77.7 2.2 collective-permute-done.10.refs_1_
  79.8 1.5 collective-permute-done.11.refs_2_
  82.6 1.6 collective-permute-start.13
  84.2 1.5 collective-permute-start.16
  85.7 1.7 collective-permute-done.15.refs_4_
  88.3 1.1 collective-permute-start.18
  89.9 2.7 %collective-permute-done.17.refs_6_ = bf16[192,384]{1,0:T(8,128)(2,1)S(1)} collective-permute-done((bf16[192,384]{1,0:T(8,128)(2,1)S(1)}, bf16[192,384]{1,0:T(8,128)(2,1)S(1)}, u32[]{:S(2)}, u32[]{:S(2)}) %collective-permute-start.17) | collective-permute-done | bytes 147488 | tf_op jit(solution)/shard_map/ppermute | solution.py:59
  93.7 2.8 %collective-permute-done.19.refs_5_.refs_6_.refs_7_.refs_8_ = bf16[1536,384]{1,0:T(8,128)(2,1)S(1)} collective-permute-done((bf16[1536,384]{1,0:T(8,128)(2,1)S(1)}, bf16[1536,384]{1,0:T(8,128)(2,1)S(1)}, u32[]{:S(2)}, u32[]{:S(2)}) %collective-permute-start.19) | collective-permute-done | bytes 1179680 | tf_op jit(solution)/shard_map/ppermute | solution.py:59
  96.5 2.0 shard_map.89
  98.4 1.1 collective-permute-start.20
  99.5 1.9 shard_map.90
  101.5 1.0 collective-permute-start.22
  102.5 3.2 %shard_map.88 = (f32[384,384]{1,0:T(8,128)S(1)}, f32[384,384]{1,0:T(8,128)S(1)}) custom-call(bf16[1536,3072]{1,0:T(8,128)(2,1)S(1)} %get-tuple-element.31.refs_0_, bf16[1536,384]{1,0:T(8,128)(2,1)S(1)} %shard_map.87.refs_1_.refs_2_.refs_3_.refs_4_, bf16[1536,384]{1,0:T(8,128)(2,1)S(1)} %shard_map.87.refs_1_.refs_2_.refs_3_.refs_4_, ...), custom_call_target="tpu_custom_call" | custom-call | flops 1811939328 | bytes 4718592 | tf_op jit(solution)/shard_map/pallas_call | solution.py:38
  105.7 8.1 %collective-permute-done.20 = bf16[384,384]{1,0:T(8,128)(2,1)S(1)} collective-permute-done((bf16[384,384]{1,0:T(8,128)(2,1)S(1)}, bf16[384,384]{1,0:T(8,128)(2,1)S(1)}, u32[]{:S(2)}, u32[]{:S(2)}) %collective-permute-start.20) | collective-permute-done | bytes 294944 | tf_op jit(solution)/shard_map/ppermute | solution.py:55
  114.3 6.3 %collective-permute-done.21 = bf16[384,384]{1,0:T(8,128)(2,1)S(1)} collective-permute-done((bf16[384,384]{1,0:T(8,128)(2,1)S(1)}, bf16[384,384]{1,0:T(8,128)(2,1)S(1)}, u32[]{:S(2)}, u32[]{:S(2)}) %collective-permute-start.21) | collective-permute-done | bytes 294944 | tf_op jit(solution)/shard_map/ppermute | solution.py:55
  120.6 0.9 fusion
  121.5 1.2 collective-permute-start.26
  122.7 1.5 collective-permute-start.28
  126.0 4.6 %collective-permute-start.27 = (bf16[96,384]{1,0:T(8,128)(2,1)S(1)}, bf16[96,384]{1,0:T(8,128)(2,1)S(1)}, u32[]{:S(2)}, u32[]{:S(2)}) collective-permute-start(bf16[96,384]{1,0:T(8,128)(2,1)S(1)} %collective-permute-done.26), channel_id=1, source_target_pairs={{0,2},{1,10},{2,18},{3,26},{4,6},{5,14},{6,22},{7,30},{8,3},{9,11}... | collective-permute-start | bytes 221192 | tf_op jit(solution)/shard_map/ppermute | solution.py:101
  130.5 2.5 %collective-permute-start.29 = (bf16[96,384]{1,0:T(8,128)(2,1)S(1)}, bf16[96,384]{1,0:T(8,128)(2,1)S(1)}, u32[]{:S(2)}, u32[]{:S(2)}) collective-permute-start(bf16[96,384]{1,0:T(8,128)(2,1)S(1)} %collective-permute-done.28), channel_id=1, source_target_pairs={{0,3},{1,11},{2,19},{3,27},{4,7},{5,15},{6,23},{7,31},{8,2},{9,10}... | collective-permute-start | bytes 221192 | tf_op jit(solution)/shard_map/ppermute | solution.py:101
  133.1 2.8 %collective-permute-done.29 = bf16[96,384]{1,0:T(8,128)(2,1)S(1)} collective-permute-done((bf16[96,384]{1,0:T(8,128)(2,1)S(1)}, bf16[96,384]{1,0:T(8,128)(2,1)S(1)}, u32[]{:S(2)}, u32[]{:S(2)}) %collective-permute-start.29) | collective-permute-done | bytes 73760 | tf_op jit(solution)/shard_map/ppermute | solution.py:101
  135.9 3.3 %collective-permute-start.31 = (bf16[192,384]{1,0:T(8,128)(2,1)S(1)}, bf16[192,384]{1,0:T(8,128)(2,1)S(1)}, u32[]{:S(2)}, u32[]{:S(2)}) collective-permute-start(bf16[192,384]{1,0:T(8,128)(2,1)S(1)} %constant_dynamic-update-slice_fusion.2.high_ref), channel_id=1, source_target_pairs={{0,8},{4,12},{8,0},{12,4},{16,24},{20,28},{24,16},{28,20},{1,9},{5... | collective-permute-start | bytes 442376 | tf_op jit(solution)/shard_map/ppermute | solution.py:59
  139.8 1.5 collective-permute-start.30
  141.4 2.2 collective-permute-done.31.refs_3_
  144.3 2.1 collective-permute-start.34
  146.5 2.2 %collective-permute-done.35.refs_7_ = bf16[192,384]{1,0:T(8,128)(2,1)S(1)} collective-permute-done((bf16[192,384]{1,0:T(8,128)(2,1)S(1)}, bf16[192,384]{1,0:T(8,128)(2,1)S(1)}, u32[]{:S(2)}, u32[]{:S(2)}) %collective-permute-start.35) | collective-permute-done | bytes 147488 | tf_op jit(solution)/shard_map/ppermute | solution.py:59
  149.7 2.8 %collective-permute-done.36.refs_6_.refs_7_.refs_8_.refs_9_ = bf16[1536,384]{1,0:T(8,128)(2,1)S(1)} collective-permute-done((bf16[1536,384]{1,0:T(8,128)(2,1)S(1)}, bf16[1536,384]{1,0:T(8,128)(2,1)S(1)}, u32[]{:S(2)}, u32[]{:S(2)}) %collective-permute-start.36) | collective-permute-done | bytes 1179680 | tf_op jit(solution)/shard_map/ppermute | solution.py:59
  152.6 2.0 shard_map.93
  154.6 3.1 %collective-permute-start.37 = (bf16[384,512]{1,0:T(8,128)(2,1)S(1)}, bf16[384,512]{1,0:T(8,128)(2,1)S(1)}, u32[]{:S(2)}, u32[]{:S(2)}) collective-permute-start(bf16[384,512]{1,0:T(8,128)(2,1)S(1)} %get-tuple-element.52), channel_id=1, source_target_pairs={{0,3},{1,0},{2,1},{3,2},{4,7},{5,4},{6,5},{7,6},{8,11},{9,8},{10,9... | collective-permute-start | bytes 1179656 | tf_op jit(solution)/shard_map/ppermute | solution.py:55
  158.5 1.4 shard_map.94
  160.0 7.2 %collective-permute-done.37 = bf16[384,512]{1,0:T(8,128)(2,1)S(1)} collective-permute-done((bf16[384,512]{1,0:T(8,128)(2,1)S(1)}, bf16[384,512]{1,0:T(8,128)(2,1)S(1)}, u32[]{:S(2)}, u32[]{:S(2)}) %collective-permute-start.37) | collective-permute-done | bytes 393248 | tf_op jit(solution)/shard_map/ppermute | solution.py:55
  167.3 4.3 %collective-permute-start.38 = (bf16[384,512]{1,0:T(8,128)(2,1)S(1)}, bf16[384,512]{1,0:T(8,128)(2,1)S(1)}, u32[]{:S(2)}, u32[]{:S(2)}) collective-permute-start(bf16[384,512]{1,0:T(8,128)(2,1)S(1)} %add_convert_fusion.1), channel_id=1, source_target_pairs={{0,3},{1,0},{2,1},{3,2},{4,7},{5,4},{6,5},{7,6},{8,11},{9,8},{10,9... | collective-permute-start | bytes 1179656 | tf_op jit(solution)/shard_map/ppermute | solution.py:55
  171.7 6.6 %collective-permute-done.39 = bf16[384,512]{1,0:T(8,128)(2,1)S(1)} collective-permute-done((bf16[384,512]{1,0:T(8,128)(2,1)S(1)}, bf16[384,512]{1,0:T(8,128)(2,1)S(1)}, u32[]{:S(2)}, u32[]{:S(2)}) %collective-permute-start.39) | collective-permute-done | bytes 393248 | tf_op jit(solution)/shard_map/ppermute | solution.py:55
  178.3 7.2 %collective-permute-done.38 = bf16[384,512]{1,0:T(8,128)(2,1)S(1)} collective-permute-done((bf16[384,512]{1,0:T(8,128)(2,1)S(1)}, bf16[384,512]{1,0:T(8,128)(2,1)S(1)}, u32[]{:S(2)}, u32[]{:S(2)}) %collective-permute-start.38) | collective-permute-done | bytes 393248 | tf_op jit(solution)/shard_map/ppermute | solution.py:55
  185.6 1.0 collective-permute-start.40
  186.6 2.9 %collective-permute-start.41 = (bf16[384,512]{1,0:T(8,128)(2,1)S(1)}, bf16[384,512]{1,0:T(8,128)(2,1)S(1)}, u32[]{:S(2)}, u32[]{:S(2)}) collective-permute-start(bf16[384,512]{1,0:T(8,128)(2,1)S(1)} %add_convert_fusion.refs_2_), channel_id=1, source_target_pairs={{0,3},{1,0},{2,1},{3,2},{4,7},{5,4},{6,5},{7,6},{8,11},{9,8},{10,9... | collective-permute-start | bytes 1179656 | tf_op jit(solution)/shard_map/ppermute | solution.py:55
  189.5 10.0 %collective-permute-done.40.refs_3_ = bf16[384,512]{1,0:T(8,128)(2,1)S(1)} collective-permute-done((bf16[384,512]{1,0:T(8,128)(2,1)S(1)}, bf16[384,512]{1,0:T(8,128)(2,1)S(1)}, u32[]{:S(2)}, u32[]{:S(2)}) %collective-permute-start.40) | collective-permute-done | bytes 393248 | tf_op jit(solution)/shard_map/ppermute | solution.py:55
  199.5 7.0 %collective-permute-done.41.refs_4_ = bf16[384,512]{1,0:T(8,128)(2,1)S(1)} collective-permute-done((bf16[384,512]{1,0:T(8,128)(2,1)S(1)}, bf16[384,512]{1,0:T(8,128)(2,1)S(1)}, u32[]{:S(2)}, u32[]{:S(2)}) %collective-permute-start.41) | collective-permute-done | bytes 393248 | tf_op jit(solution)/shard_map/ppermute | solution.py:55
  206.5 1.0 shard_map.96.refs_1_
  207.5 7.4 %collective-permute-done.42.refs_2_ = bf16[384,512]{1,0:T(8,128)(2,1)S(1)} collective-permute-done((bf16[384,512]{1,0:T(8,128)(2,1)S(1)}, bf16[384,512]{1,0:T(8,128)(2,1)S(1)}, u32[]{:S(2)}, u32[]{:S(2)}) %collective-permute-start.42) | collective-permute-done | bytes 393248 | tf_op jit(solution)/shard_map/ppermute | solution.py:55
  214.9 1.3 shard_map.97
  (68 shorter events, 11.8 us)
Async XLA Ops:
  0.6 15.3 %collective-permute-start = (bf16[512,384]{1,0:T(8,128)(2,1)}, bf16[512,384]{1,0:T(8,128)(2,1)S(1)}, u32[]{:S(2)}, u32[]{:S(2)}) collective-permute-start(bf16[512,384]{1,0:T(8,128)(2,1)} %refs_1_.5), channel_id=1, source_target_pairs={{0,1},{1,2},{2,3},{3,0},{4,5},{5,6},{6,7},{7,4},{8,9},{9,10},{10,1... | collective-permute-start | bytes 1179656 | tf_op jit(solution)/shard_map/ppermute | solution.py:55
  3.7 19.4 %collective-permute-start.1 = (bf16[512,384]{1,0:T(8,128)(2,1)}, bf16[512,384]{1,0:T(8,128)(2,1)S(1)}, u32[]{:S(2)}, u32[]{:S(2)}) collective-permute-start(bf16[512,384]{1,0:T(8,128)(2,1)} %refs_1_.5), channel_id=1, source_target_pairs={{0,3},{1,0},{2,1},{3,2},{4,7},{5,4},{6,5},{7,6},{8,11},{9,8},{10,9... | collective-permute-start | bytes 1179656 | tf_op jit(solution)/shard_map/ppermute | solution.py:55
  15.9 16.0 %collective-permute-start.2 = (bf16[512,384]{1,0:T(8,128)(2,1)S(1)}, bf16[512,384]{1,0:T(8,128)(2,1)S(1)}, u32[]{:S(2)}, u32[]{:S(2)}) collective-permute-start(bf16[512,384]{1,0:T(8,128)(2,1)S(1)} %collective-permute-done.refs_2_), channel_id=1, source_target_pairs={{0,1},{1,2},{2,3},{3,0},{4,5},{5,6},{6,7},{7,4},{8,9},{9,10},{10,1... | collective-permute-start | bytes 1179656 | tf_op jit(solution)/shard_map/ppermute | solution.py:55
  23.1 1.6 copy-start.1
  24.7 1.0 copy-start.3
  25.7 27.6 %slice-start = ((s8[6291456]{0:T(1024)(128)(4,1)}), s8[2097152]{0:T(1024)(128)(4,1)S(1)}, s32[]{:S(2)}) async-start(s8[6291456]{0:T(1024)(128)(4,1)} %bitcast.2), calls=%async_computation | async-start | bytes 4194304
  26.7 20.5 %copy-start.4 = (s32[1,12]{1,0:T(1,128)S(1)}, s32[1,12]{1,0:T(1,128)}, u32[]{:S(2)}) copy-start(s32[1,12]{1,0:T(1,128)} %param.11) | copy-start | bytes 148
  33.1 14.1 %collective-permute-start.4 = (bf16[512,384]{1,0:T(8,128)(2,1)}, bf16[512,384]{1,0:T(8,128)(2,1)S(1)}, u32[]{:S(2)}, u32[]{:S(2)}) collective-permute-start(bf16[512,384]{1,0:T(8,128)(2,1)} %get-tuple-element.29.refs_1_), channel_id=1, source_target_pairs={{0,1},{1,2},{2,3},{3,0},{4,5},{5,6},{6,7},{7,4},{8,9},{9,10},{10,1... | collective-permute-start | bytes 1179656 | tf_op jit(solution)/shard_map/ppermute | solution.py:55
  33.1 20.2 %collective-permute-start.3 = (bf16[512,384]{1,0:T(8,128)(2,1)}, bf16[512,384]{1,0:T(8,128)(2,1)}, u32[]{:S(2)}, u32[]{:S(2)}) collective-permute-start(bf16[512,384]{1,0:T(8,128)(2,1)} %get-tuple-element.29.refs_1_), channel_id=1, source_target_pairs={{0,3},{1,0},{2,1},{3,2},{4,7},{5,4},{6,5},{7,6},{8,11},{9,8},{10,9... | collective-permute-start | bytes 1179656 | tf_op jit(solution)/shard_map/ppermute | solution.py:55
  47.2 13.6 %collective-permute-start.5 = (bf16[512,384]{1,0:T(8,128)(2,1)S(1)}, bf16[512,384]{1,0:T(8,128)(2,1)S(1)}, u32[]{:S(2)}, u32[]{:S(2)}) collective-permute-start(bf16[512,384]{1,0:T(8,128)(2,1)S(1)} %collective-permute-done.4.refs_2_), channel_id=1, source_target_pairs={{0,1},{1,2},{2,3},{3,0},{4,5},{5,6},{6,7},{7,4},{8,9},{9,10},{10,1... | collective-permute-start | bytes 1179656 | tf_op jit(solution)/shard_map/ppermute | solution.py:55
  47.2 2.8 %copy-start = (bf16[1536,2048]{1,0:T(8,128)(2,1)S(1)}, bf16[1536,2048]{1,0:T(8,128)(2,1)}, u32[]{:S(2)}) copy-start(bf16[1536,2048]{1,0:T(8,128)(2,1)} %refs_1_.9) | copy-start | bytes 18874372
  50.0 3.3 %slice-start.1 = ((s8[6291456]{0:T(1024)(128)(4,1)}), s8[4194304]{0:T(1024)(128)(4,1)S(1)}, s32[]{:S(2)}) async-start(s8[6291456]{0:T(1024)(128)(4,1)} %bitcast.2), calls=%async_computation.1 | async-start | bytes 8388608
  63.2 2.9 %collective-permute-start.6 = (bf16[1536,384]{1,0:T(8,128)(2,1)S(1)}, bf16[1536,384]{1,0:T(8,128)(2,1)S(1)}, u32[]{:S(2)}, u32[]{:S(2)}) collective-permute-start(bf16[1536,384]{1,0:T(8,128)(2,1)S(1)} %get-tuple-element.35), channel_id=1, source_target_pairs={{0,4},{4,0},{8,12},{12,8},{16,20},{20,16},{24,28},{28,24},{1,5},{5... | collective-permute-start | bytes 3538952 | tf_op jit(solution)/shard_map/ppermute | solution.py:59
  66.2 6.2 %collective-permute-start.8 = (bf16[192,384]{1,0:T(8,128)(2,1)S(1)}, bf16[192,384]{1,0:T(8,128)(2,1)S(1)}, u32[]{:S(2)}, u32[]{:S(2)}) collective-permute-start(bf16[192,384]{1,0:T(8,128)(2,1)S(1)} %get-tuple-element.37), channel_id=1, source_target_pairs={{0,8},{4,12},{8,0},{12,4},{16,24},{20,28},{24,16},{28,20},{1,9},{5... | collective-permute-start | bytes 442376 | tf_op jit(solution)/shard_map/ppermute | solution.py:59
  67.8 6.7 %collective-permute-start.9 = (bf16[192,384]{1,0:T(8,128)(2,1)S(1)}, bf16[192,384]{1,0:T(8,128)(2,1)S(1)}, u32[]{:S(2)}, u32[]{:S(2)}) collective-permute-start(bf16[192,384]{1,0:T(8,128)(2,1)S(1)} %get-tuple-element.38), channel_id=1, source_target_pairs={{0,16},{4,20},{8,24},{12,28},{16,0},{20,4},{24,8},{28,12},{1,17},{... | collective-permute-start | bytes 442376 | tf_op jit(solution)/shard_map/ppermute | solution.py:59
  69.3 8.3 %collective-permute-start.12 = (bf16[192,384]{1,0:T(8,128)(2,1)S(1)}, bf16[192,384]{1,0:T(8,128)(2,1)S(1)}, u32[]{:S(2)}, u32[]{:S(2)}) collective-permute-start(bf16[192,384]{1,0:T(8,128)(2,1)S(1)} %get-tuple-element.41), channel_id=1, source_target_pairs={{0,16},{4,20},{8,24},{12,28},{16,0},{20,4},{24,8},{28,12},{1,17},{... | collective-permute-start | bytes 442376 | tf_op jit(solution)/shard_map/ppermute | solution.py:59
  69.9 7.7 %collective-permute-start.7 = (bf16[192,384]{1,0:T(8,128)(2,1)S(1)}, bf16[192,384]{1,0:T(8,128)(2,1)S(1)}, u32[]{:S(2)}, u32[]{:S(2)}) collective-permute-start(bf16[192,384]{1,0:T(8,128)(2,1)S(1)} %get-tuple-element.36), channel_id=1, source_target_pairs={{0,8},{4,12},{8,0},{12,4},{16,24},{20,28},{24,16},{28,20},{1,9},{5... | collective-permute-start | bytes 442376 | tf_op jit(solution)/shard_map/ppermute | solution.py:59
  74.6 5.2 %collective-permute-start.10 = (bf16[192,384]{1,0:T(8,128)(2,1)S(1)}, bf16[192,384]{1,0:T(8,128)(2,1)S(1)}, u32[]{:S(2)}, u32[]{:S(2)}) collective-permute-start(bf16[192,384]{1,0:T(8,128)(2,1)S(1)} %get-tuple-element.39), channel_id=1, source_target_pairs={{0,16},{4,20},{8,24},{12,28},{16,0},{20,4},{24,8},{28,12},{1,17},{... | collective-permute-start | bytes 442376 | tf_op jit(solution)/shard_map/ppermute | solution.py:59
  76.2 5.1 %collective-permute-start.11 = (bf16[192,384]{1,0:T(8,128)(2,1)S(1)}, bf16[192,384]{1,0:T(8,128)(2,1)S(1)}, u32[]{:S(2)}, u32[]{:S(2)}) collective-permute-start(bf16[192,384]{1,0:T(8,128)(2,1)S(1)} %get-tuple-element.40), channel_id=1, source_target_pairs={{0,8},{4,12},{8,0},{12,4},{16,24},{20,28},{24,16},{28,20},{1,9},{5... | collective-permute-start | bytes 442376 | tf_op jit(solution)/shard_map/ppermute | solution.py:59
  81.5 6.0 %collective-permute-start.15 = (bf16[192,384]{1,0:T(8,128)(2,1)S(1)}, bf16[192,384]{1,0:T(8,128)(2,1)S(1)}, u32[]{:S(2)}, u32[]{:S(2)}) collective-permute-start(bf16[192,384]{1,0:T(8,128)(2,1)S(1)} %get-tuple-element.42.low_ref), channel_id=1, source_target_pairs={{0,16},{4,20},{8,24},{12,28},{16,0},{20,4},{24,8},{28,12},{1,17},{... | collective-permute-start | bytes 442376 | tf_op jit(solution)/shard_map/ppermute | solution.py:59
  82.1 6.2 %collective-permute-start.14 = (bf16[192,384]{1,0:T(8,128)(2,1)S(1)}, bf16[192,384]{1,0:T(8,128)(2,1)S(1)}, u32[]{:S(2)}, u32[]{:S(2)}) collective-permute-start(bf16[192,384]{1,0:T(8,128)(2,1)S(1)} %get-tuple-element.43.high_ref), channel_id=1, source_target_pairs={{0,8},{4,12},{8,0},{12,4},{16,24},{20,28},{24,16},{28,20},{1,9},{5... | collective-permute-start | bytes 442376 | tf_op jit(solution)/shard_map/ppermute | solution.py:59
  82.6 7.3 %collective-permute-start.13 = (bf16[192,384]{1,0:T(8,128)(2,1)S(1)}, bf16[192,384]{1,0:T(8,128)(2,1)S(1)}, u32[]{:S(2)}, u32[]{:S(2)}) collective-permute-start(bf16[192,384]{1,0:T(8,128)(2,1)S(1)} %get-tuple-element.44.refs_0_), channel_id=1, source_target_pairs={{0,8},{4,12},{8,0},{12,4},{16,24},{20,28},{24,16},{28,20},{1,9},{5... | collective-permute-start | bytes 442376 | tf_op jit(solution)/shard_map/ppermute | solution.py:59
  84.2 5.7 %collective-permute-start.16 = (bf16[192,384]{1,0:T(8,128)(2,1)S(1)}, bf16[192,384]{1,0:T(8,128)(2,1)S(1)}, u32[]{:S(2)}, u32[]{:S(2)}) collective-permute-start(bf16[192,384]{1,0:T(8,128)(2,1)S(1)} %get-tuple-element.45.refs_1_), channel_id=1, source_target_pairs={{0,16},{4,20},{8,24},{12,28},{16,0},{20,4},{24,8},{28,12},{1,17},{... | collective-permute-start | bytes 442376 | tf_op jit(solution)/shard_map/ppermute | solution.py:59
  87.5 5.1 %collective-permute-start.17 = (bf16[192,384]{1,0:T(8,128)(2,1)S(1)}, bf16[192,384]{1,0:T(8,128)(2,1)S(1)}, u32[]{:S(2)}, u32[]{:S(2)}) collective-permute-start(bf16[192,384]{1,0:T(8,128)(2,1)S(1)} %collective-permute-done.15.refs_4_), channel_id=1, source_target_pairs={{0,8},{4,12},{8,0},{12,4},{16,24},{20,28},{24,16},{28,20},{1,9},{5... | collective-permute-start | bytes 442376 | tf_op jit(solution)/shard_map/ppermute | solution.py:59
  88.3 5.1 %collective-permute-start.18 = (bf16[192,384]{1,0:T(8,128)(2,1)S(1)}, bf16[192,384]{1,0:T(8,128)(2,1)S(1)}, u32[]{:S(2)}, u32[]{:S(2)}) collective-permute-start(bf16[192,384]{1,0:T(8,128)(2,1)S(1)} %collective-permute-done.14.refs_3_), channel_id=1, source_target_pairs={{0,16},{4,20},{8,24},{12,28},{16,0},{20,4},{24,8},{28,12},{1,17},{... | collective-permute-start | bytes 442376 | tf_op jit(solution)/shard_map/ppermute | solution.py:59
  93.6 2.9 %collective-permute-start.19 = (bf16[1536,384]{1,0:T(8,128)(2,1)S(1)}, bf16[1536,384]{1,0:T(8,128)(2,1)S(1)}, u32[]{:S(2)}, u32[]{:S(2)}) collective-permute-start(bf16[1536,384]{1,0:T(8,128)(2,1)S(1)} %shard_map.87.refs_1_.refs_2_.refs_3_.refs_4_), channel_id=1, source_target_pairs={{0,4},{4,0},{8,12},{12,8},{16,20},{20,16},{24,28},{28,24},{1,5},{5... | collective-permute-start | bytes 3538952 | tf_op jit(solution)/shard_map/ppermute | solution.py:59
  98.4 15.3 %collective-permute-start.20 = (bf16[384,384]{1,0:T(8,128)(2,1)S(1)}, bf16[384,384]{1,0:T(8,128)(2,1)S(1)}, u32[]{:S(2)}, u32[]{:S(2)}) collective-permute-start(bf16[384,384]{1,0:T(8,128)(2,1)S(1)} %shard_map.89), channel_id=1, source_target_pairs={{0,3},{1,0},{2,1},{3,2},{4,7},{5,4},{6,5},{7,6},{8,11},{9,8},{10,9... | collective-permute-start | bytes 884744 | tf_op jit(solution)/shard_map/ppermute | solution.py:55
  101.5 12.8 %collective-permute-start.22 = (bf16[384,384]{1,0:T(8,128)(2,1)S(1)}, bf16[384,384]{1,0:T(8,128)(2,1)S(1)}, u32[]{:S(2)}, u32[]{:S(2)}) collective-permute-start(bf16[384,384]{1,0:T(8,128)(2,1)S(1)} %shard_map.90), channel_id=1, source_target_pairs={{0,1},{1,2},{2,3},{3,0},{4,5},{5,6},{6,7},{7,4},{8,9},{9,10},{10,1... | collective-permute-start | bytes 884744 | tf_op jit(solution)/shard_map/ppermute | solution.py:55
  113.8 6.8 %collective-permute-start.21 = (bf16[384,384]{1,0:T(8,128)(2,1)S(1)}, bf16[384,384]{1,0:T(8,128)(2,1)S(1)}, u32[]{:S(2)}, u32[]{:S(2)}) collective-permute-start(bf16[384,384]{1,0:T(8,128)(2,1)S(1)} %add_convert_fusion.2), channel_id=1, source_target_pairs={{0,3},{1,0},{2,1},{3,2},{4,7},{5,4},{6,5},{7,6},{8,11},{9,8},{10,9... | collective-permute-start | bytes 884744 | tf_op jit(solution)/shard_map/ppermute | solution.py:55
  121.5 4.4 %collective-permute-start.26 = (bf16[96,384]{1,0:T(8,128)(2,1)S(1)}, bf16[96,384]{1,0:T(8,128)(2,1)S(1)}, u32[]{:S(2)}, u32[]{:S(2)}) collective-permute-start(bf16[96,384]{1,0:T(8,128)(2,1)S(1)} %get-tuple-element.57), channel_id=1, source_target_pairs={{0,16},{4,20},{8,24},{12,28},{16,0},{20,4},{24,8},{28,12},{1,17},{... | collective-permute-start | bytes 221192 | tf_op jit(solution)/shard_map/ppermute | solution.py:59
  122.7 7.8 %collective-permute-start.28 = (bf16[96,384]{1,0:T(8,128)(2,1)S(1)}, bf16[96,384]{1,0:T(8,128)(2,1)S(1)}, u32[]{:S(2)}, u32[]{:S(2)}) collective-permute-start(bf16[96,384]{1,0:T(8,128)(2,1)S(1)} %get-tuple-element.56), channel_id=1, source_target_pairs={{0,24},{4,28},{8,16},{12,20},{16,8},{20,12},{24,0},{28,4},{1,25},{... | collective-permute-start | bytes 221192 | tf_op jit(solution)/shard_map/ppermute | solution.py:59
  124.2 8.8 %collective-permute-start.24 = (bf16[96,384]{1,0:T(8,128)(2,1)S(1)}, bf16[96,384]{1,0:T(8,128)(2,1)S(1)}, u32[]{:S(2)}, u32[]{:S(2)}) collective-permute-start(bf16[96,384]{1,0:T(8,128)(2,1)S(1)} %get-tuple-element.58), channel_id=1, source_target_pairs={{0,8},{4,12},{8,0},{12,4},{16,24},{20,28},{24,16},{28,20},{1,9},{5... | collective-permute-start | bytes 221192 | tf_op jit(solution)/shard_map/ppermute | solution.py:59
  125.1 7.9 %collective-permute-start.23 = (bf16[96,384]{1,0:T(8,128)(2,1)S(1)}, bf16[96,384]{1,0:T(8,128)(2,1)S(1)}, u32[]{:S(2)}, u32[]{:S(2)}) collective-permute-start(bf16[96,384]{1,0:T(8,128)(2,1)S(1)} %get-tuple-element.59), channel_id=1, source_target_pairs={{0,0},{1,8},{2,16},{3,24},{4,4},{5,12},{6,20},{7,28},{8,1},{9,9},{... | collective-permute-start | bytes 221192 | tf_op jit(solution)/shard_map/ppermute | solution.py:101
  126.0 7.1 %collective-permute-start.27 = (bf16[96,384]{1,0:T(8,128)(2,1)S(1)}, bf16[96,384]{1,0:T(8,128)(2,1)S(1)}, u32[]{:S(2)}, u32[]{:S(2)}) collective-permute-start(bf16[96,384]{1,0:T(8,128)(2,1)S(1)} %collective-permute-done.26), channel_id=1, source_target_pairs={{0,2},{1,10},{2,18},{3,26},{4,6},{5,14},{6,22},{7,30},{8,3},{9,11}... | collective-permute-start | bytes 221192 | tf_op jit(solution)/shard_map/ppermute | solution.py:101
  130.5 5.3 %collective-permute-start.29 = (bf16[96,384]{1,0:T(8,128)(2,1)S(1)}, bf16[96,384]{1,0:T(8,128)(2,1)S(1)}, u32[]{:S(2)}, u32[]{:S(2)}) collective-permute-start(bf16[96,384]{1,0:T(8,128)(2,1)S(1)} %collective-permute-done.28), channel_id=1, source_target_pairs={{0,3},{1,11},{2,19},{3,27},{4,7},{5,15},{6,23},{7,31},{8,2},{9,10}... | collective-permute-start | bytes 221192 | tf_op jit(solution)/shard_map/ppermute | solution.py:101
  133.0 6.1 %collective-permute-start.25 = (bf16[96,384]{1,0:T(8,128)(2,1)S(1)}, bf16[96,384]{1,0:T(8,128)(2,1)S(1)}, u32[]{:S(2)}, u32[]{:S(2)}) collective-permute-start(bf16[96,384]{1,0:T(8,128)(2,1)S(1)} %collective-permute-done.24), channel_id=1, source_target_pairs={{0,1},{1,9},{2,17},{3,25},{4,5},{5,13},{6,21},{7,29},{8,0},{9,8},{... | collective-permute-start | bytes 221192 | tf_op jit(solution)/shard_map/ppermute | solution.py:101
  135.9 7.7 %collective-permute-start.31 = (bf16[192,384]{1,0:T(8,128)(2,1)S(1)}, bf16[192,384]{1,0:T(8,128)(2,1)S(1)}, u32[]{:S(2)}, u32[]{:S(2)}) collective-permute-start(bf16[192,384]{1,0:T(8,128)(2,1)S(1)} %constant_dynamic-update-slice_fusion.2.high_ref), channel_id=1, source_target_pairs={{0,8},{4,12},{8,0},{12,4},{16,24},{20,28},{24,16},{28,20},{1,9},{5... | collective-permute-start | bytes 442376 | tf_op jit(solution)/shard_map/ppermute | solution.py:59
  139.1 5.2 %collective-permute-start.32 = (bf16[192,384]{1,0:T(8,128)(2,1)S(1)}, bf16[192,384]{1,0:T(8,128)(2,1)S(1)}, u32[]{:S(2)}, u32[]{:S(2)}) collective-permute-start(bf16[192,384]{1,0:T(8,128)(2,1)S(1)} %constant_dynamic-update-slice_fusion.low_ref), channel_id=1, source_target_pairs={{0,16},{4,20},{8,24},{12,28},{16,0},{20,4},{24,8},{28,12},{1,17},{... | collective-permute-start | bytes 442376 | tf_op jit(solution)/shard_map/ppermute | solution.py:59
  139.8 6.6 %collective-permute-start.30 = (bf16[192,384]{1,0:T(8,128)(2,1)S(1)}, bf16[192,384]{1,0:T(8,128)(2,1)S(1)}, u32[]{:S(2)}, u32[]{:S(2)}) collective-permute-start(bf16[192,384]{1,0:T(8,128)(2,1)S(1)} %get-tuple-element.48.refs_0_), channel_id=1, source_target_pairs={{0,8},{4,12},{8,0},{12,4},{16,24},{20,28},{24,16},{28,20},{1,9},{5... | collective-permute-start | bytes 442376 | tf_op jit(solution)/shard_map/ppermute | solution.py:59
  141.4 5.1 %collective-permute-start.33 = (bf16[192,384]{1,0:T(8,128)(2,1)S(1)}, bf16[192,384]{1,0:T(8,128)(2,1)S(1)}, u32[]{:S(2)}, u32[]{:S(2)}) collective-permute-start(bf16[192,384]{1,0:T(8,128)(2,1)S(1)} %get-tuple-element.49.refs_1_), channel_id=1, source_target_pairs={{0,16},{4,20},{8,24},{12,28},{16,0},{20,4},{24,8},{28,12},{1,17},{... | collective-permute-start | bytes 442376 | tf_op jit(solution)/shard_map/ppermute | solution.py:59
  143.6 5.1 %collective-permute-start.35 = (bf16[192,384]{1,0:T(8,128)(2,1)S(1)}, bf16[192,384]{1,0:T(8,128)(2,1)S(1)}, u32[]{:S(2)}, u32[]{:S(2)}) collective-permute-start(bf16[192,384]{1,0:T(8,128)(2,1)S(1)} %collective-permute-done.31.refs_3_), channel_id=1, source_target_pairs={{0,16},{4,20},{8,24},{12,28},{16,0},{20,4},{24,8},{28,12},{1,17},{... | collective-permute-start | bytes 442376 | tf_op jit(solution)/shard_map/ppermute | solution.py:59
  144.3 5.2 %collective-permute-start.34 = (bf16[192,384]{1,0:T(8,128)(2,1)S(1)}, bf16[192,384]{1,0:T(8,128)(2,1)S(1)}, u32[]{:S(2)}, u32[]{:S(2)}) collective-permute-start(bf16[192,384]{1,0:T(8,128)(2,1)S(1)} %collective-permute-done.32.refs_4_), channel_id=1, source_target_pairs={{0,8},{4,12},{8,0},{12,4},{16,24},{20,28},{24,16},{28,20},{1,9},{5... | collective-permute-start | bytes 442376 | tf_op jit(solution)/shard_map/ppermute | solution.py:59
  149.7 2.9 %collective-permute-start.36 = (bf16[1536,384]{1,0:T(8,128)(2,1)S(1)}, bf16[1536,384]{1,0:T(8,128)(2,1)S(1)}, u32[]{:S(2)}, u32[]{:S(2)}) collective-permute-start(bf16[1536,384]{1,0:T(8,128)(2,1)S(1)} %shard_map.92.refs_2_.refs_3_.refs_4_.refs_5_), channel_id=1, source_target_pairs={{0,4},{4,0},{8,12},{12,8},{16,20},{20,16},{24,28},{28,24},{1,5},{5... | collective-permute-start | bytes 3538952 | tf_op jit(solution)/shard_map/ppermute | solution.py:59
  154.6 12.6 %collective-permute-start.37 = (bf16[384,512]{1,0:T(8,128)(2,1)S(1)}, bf16[384,512]{1,0:T(8,128)(2,1)S(1)}, u32[]{:S(2)}, u32[]{:S(2)}) collective-permute-start(bf16[384,512]{1,0:T(8,128)(2,1)S(1)} %get-tuple-element.52), channel_id=1, source_target_pairs={{0,3},{1,0},{2,1},{3,2},{4,7},{5,4},{6,5},{7,6},{8,11},{9,8},{10,9... | collective-permute-start | bytes 1179656 | tf_op jit(solution)/shard_map/ppermute | solution.py:55
  158.5 19.8 %collective-permute-start.39 = (bf16[384,512]{1,0:T(8,128)(2,1)S(1)}, bf16[384,512]{1,0:T(8,128)(2,1)S(1)}, u32[]{:S(2)}, u32[]{:S(2)}) collective-permute-start(bf16[384,512]{1,0:T(8,128)(2,1)S(1)} %shard_map.95), channel_id=1, source_target_pairs={{0,1},{1,2},{2,3},{3,0},{4,5},{5,6},{6,7},{7,4},{8,9},{9,10},{10,1... | collective-permute-start | bytes 1179656 | tf_op jit(solution)/shard_map/ppermute | solution.py:55
  167.2 39.3 %copy-start.2 = (bf16[512,2048]{1,0:T(8,128)(2,1)S(1)}, bf16[512,2048]{1,0:T(8,128)(2,1)}, u32[]{:S(2)}) copy-start(bf16[512,2048]{1,0:T(8,128)(2,1)} %refs_0_.11) | copy-start | bytes 6291460
  167.3 18.1 %collective-permute-start.38 = (bf16[384,512]{1,0:T(8,128)(2,1)S(1)}, bf16[384,512]{1,0:T(8,128)(2,1)S(1)}, u32[]{:S(2)}, u32[]{:S(2)}) collective-permute-start(bf16[384,512]{1,0:T(8,128)(2,1)S(1)} %add_convert_fusion.1), channel_id=1, source_target_pairs={{0,3},{1,0},{2,1},{3,2},{4,7},{5,4},{6,5},{7,6},{8,11},{9,8},{10,9... | collective-permute-start | bytes 1179656 | tf_op jit(solution)/shard_map/ppermute | solution.py:55
  185.6 13.9 %collective-permute-start.40 = (bf16[384,512]{1,0:T(8,128)(2,1)S(1)}, bf16[384,512]{1,0:T(8,128)(2,1)S(1)}, u32[]{:S(2)}, u32[]{:S(2)}) collective-permute-start(bf16[384,512]{1,0:T(8,128)(2,1)S(1)} %add_convert_fusion.refs_2_), channel_id=1, source_target_pairs={{0,1},{1,2},{2,3},{3,0},{4,5},{5,6},{6,7},{7,4},{8,9},{9,10},{10,1... | collective-permute-start | bytes 1179656 | tf_op jit(solution)/shard_map/ppermute | solution.py:55
  186.6 19.9 %collective-permute-start.41 = (bf16[384,512]{1,0:T(8,128)(2,1)S(1)}, bf16[384,512]{1,0:T(8,128)(2,1)S(1)}, u32[]{:S(2)}, u32[]{:S(2)}) collective-permute-start(bf16[384,512]{1,0:T(8,128)(2,1)S(1)} %add_convert_fusion.refs_2_), channel_id=1, source_target_pairs={{0,3},{1,0},{2,1},{3,2},{4,7},{5,4},{6,5},{7,6},{8,11},{9,8},{10,9... | collective-permute-start | bytes 1179656 | tf_op jit(solution)/shard_map/ppermute | solution.py:55
  199.5 15.4 %collective-permute-start.42 = (bf16[384,512]{1,0:T(8,128)(2,1)S(1)}, bf16[384,512]{1,0:T(8,128)(2,1)S(1)}, u32[]{:S(2)}, u32[]{:S(2)}) collective-permute-start(bf16[384,512]{1,0:T(8,128)(2,1)S(1)} %collective-permute-done.40.refs_3_), channel_id=1, source_target_pairs={{0,1},{1,2},{2,3},{3,0},{4,5},{5,6},{6,7},{7,4},{8,9},{9,10},{10,1... | collective-permute-start | bytes 1179656 | tf_op jit(solution)/shard_map/ppermute | solution.py:55

commit v15 on v14

--- a/solution.py
+++ b/solution.py
@@ -155,7 +155,7 @@
 
 
 def border_tile(rows):
-    return BLK * next(k for k in (4, 3, 2, 1) if rows // BLK % k == 0)
+    return BLK * next(k for k in (6, 4, 3, 2, 1) if rows // BLK % k == 0)
 
 
 def border_partial(at, coupling, found, n_row, partial, source, fetch_rows):

time: 217 us -> 216 us (level)
  transfers between devices with their start and end apart: 43 -> 43, of which waited for: 34 -> 35; matrix products, arithmetic and copies ran while one was open for 0% -> 0% of each run, Pallas kernels for 8% -> 8%
where the time goes in v15:
time: 216 us
  waiting for transfers between devices  129 us (60%)
  starting transfers between devices  53.2 us (25%)
  Pallas kernels  26.5 us (12%)
  local copies, waits for them, and re-layouts  5.46 us (3%)
    ppermute x15, waiting for transfers between devices, shift(): return lax.ppermute(x, 'row', [(i, (i + by) % size) for i in range(size)])  96.2 us
    ppermute x24, waiting for transfers between devices, swap(): return lax.ppermute(x, 'front', [(i, i ^ by) for i in range(size)])  29.6 us
    pallas_call x21, Pallas kernels, kernel_call(): pl.pallas_call(placed_body, out_shape=out_shape, grid_spec=pltpu.Prefetch...  26.5 us
    ppermute x24, starting transfers between devices, swap(): return lax.ppermute(x, 'front', [(i, i ^ by) for i in range(size)])  23.2 us
    ppermute x15, starting transfers between devices, shift(): return lax.ppermute(x, 'row', [(i, (i + by) % size) for i in range(size)])  22.5 us
    ppermute x4, starting transfers between devices, to_plane(): moved.append(lax.ppermute(quarter, ('front', 'row'), perm))  7.52 us
    unnamed x16, local copies, waits for them, and re-layouts  5.4 us
  transfers between devices with their start and end apart: 43, of which 35 were waited for; matrix products, arithmetic and copies ran while one was open for 0% of the time, Pallas kernels for 8%

profile of v15, /device:TPU:0, one launch (start us, length us, event | category | flops | bytes accessed | tf_op | source)
XLA Modules:
  0.0 216.1 jit_solution(10717186307995857257)
XLA Ops:
  0.6 3.1 %collective-permute-start = (bf16[512,384]{1,0:T(8,128)(2,1)}, bf16[512,384]{1,0:T(8,128)(2,1)S(1)}, u32[]{:S(2)}, u32[]{:S(2)}) collective-permute-start(bf16[512,384]{1,0:T(8,128)(2,1)} %refs_1_.5), channel_id=1, source_target_pairs={{0,1},{1,2},{2,3},{3,0},{4,5},{5,6},{6,7},{7,4},{8,9},{9,10},{10,1... | collective-permute-start | bytes 1179656 | tf_op jit(solution)/shard_map/ppermute | solution.py:55
  3.7 2.1 collective-permute-start.1
  5.8 10.1 %collective-permute-done.refs_2_ = bf16[512,384]{1,0:T(8,128)(2,1)S(1)} collective-permute-done((bf16[512,384]{1,0:T(8,128)(2,1)}, bf16[512,384]{1,0:T(8,128)(2,1)S(1)}, u32[]{:S(2)}, u32[]{:S(2)}) %collective-permute-start) | collective-permute-done | bytes 393248 | tf_op jit(solution)/shard_map/ppermute | solution.py:55
  15.9 7.2 %collective-permute-done.1.refs_3_ = bf16[512,384]{1,0:T(8,128)(2,1)S(1)} collective-permute-done((bf16[512,384]{1,0:T(8,128)(2,1)}, bf16[512,384]{1,0:T(8,128)(2,1)S(1)}, u32[]{:S(2)}, u32[]{:S(2)}) %collective-permute-start.1) | collective-permute-done | bytes 393248 | tf_op jit(solution)/shard_map/ppermute | solution.py:55
  23.1 1.6 copy-done.1
  24.7 1.0 copy-done.3
  25.7 1.0 shard_map.77.refs_1_
  26.7 5.2 %collective-permute-done.2.refs_2_ = bf16[512,384]{1,0:T(8,128)(2,1)S(1)} collective-permute-done((bf16[512,384]{1,0:T(8,128)(2,1)S(1)}, bf16[512,384]{1,0:T(8,128)(2,1)S(1)}, u32[]{:S(2)}, u32[]{:S(2)}) %collective-permute-start.2) | collective-permute-done | bytes 393248 | tf_op jit(solution)/shard_map/ppermute | solution.py:55
  32.0 1.2 shard_map.78
  33.1 3.8 %collective-permute-start.3 = (bf16[512,384]{1,0:T(8,128)(2,1)}, bf16[512,384]{1,0:T(8,128)(2,1)}, u32[]{:S(2)}, u32[]{:S(2)}) collective-permute-start(bf16[512,384]{1,0:T(8,128)(2,1)} %get-tuple-element.29.refs_1_), channel_id=1, source_target_pairs={{0,3},{1,0},{2,1},{3,2},{4,7},{5,4},{6,5},{7,6},{8,11},{9,8},{10,9... | collective-permute-start | bytes 1179656 | tf_op jit(solution)/shard_map/ppermute | solution.py:55
  37.0 10.2 %collective-permute-done.4.refs_2_ = bf16[512,384]{1,0:T(8,128)(2,1)S(1)} collective-permute-done((bf16[512,384]{1,0:T(8,128)(2,1)}, bf16[512,384]{1,0:T(8,128)(2,1)S(1)}, u32[]{:S(2)}, u32[]{:S(2)}) %collective-permute-start.4) | collective-permute-done | bytes 393248 | tf_op jit(solution)/shard_map/ppermute | solution.py:55
  47.2 2.8 %copy-done = bf16[1536,2048]{1,0:T(8,128)(2,1)S(1)} copy-done((bf16[1536,2048]{1,0:T(8,128)(2,1)S(1)}, bf16[1536,2048]{1,0:T(8,128)(2,1)}, u32[]{:S(2)}) %copy-start) | copy-done | bytes 6291480
  50.0 3.1 %shard_map.79 = (f32[1536,384]{1,0:T(8,128)S(1)}, f32[384,384]{1,0:T(8,128)S(1)}) custom-call(bf16[1536,2048]{1,0:T(8,128)(2,1)S(1)} %copy-done, bf16[512,384]{1,0:T(8,128)(2,1)} %get-tuple-element.29.refs_1_, bf16[512,384]{1,0:T(8,128)(2,1)S(1)} %collective-permute-done.4.refs_2_, f32[3072,384]{1,0:T(8,128)} %refs_3_.2), custom_call_target="tpu_custom_call" | custom-call | flops 1207959552 | bytes 3145728 | tf_op jit(solution)/shard_map/pallas_call | solution.py:38
  53.3 4.7 %shard_map.80 = (f32[1536,384]{1,0:T(8,128)S(1)}, bf16[1536,3072]{1,0:T(8,128)(2,1)S(1)}) custom-call(bf16[1536,2048]{1,0:T(8,128)(2,1)S(1)} %bitcast.3, bf16[512,384]{1,0:T(8,128)(2,1)} %collective-permute-done.3.refs_1_, f32[1536,384]{1,0:T(8,128)S(1)} %get-tuple-element.30.refs_2_, bf16[1536,3072]{1,0:T(8,128)(2,1)} %refs_3_.3), custom_call_target="tpu_custom_call" | custom-call | flops 603979776 | bytes 1572864 | tf_op jit(solution)/shard_map/pallas_call | solution.py:38
  58.0 2.8 %collective-permute-done.5.refs_2_ = bf16[512,384]{1,0:T(8,128)(2,1)S(1)} collective-permute-done((bf16[512,384]{1,0:T(8,128)(2,1)S(1)}, bf16[512,384]{1,0:T(8,128)(2,1)S(1)}, u32[]{:S(2)}, u32[]{:S(2)}) %collective-permute-start.5) | collective-permute-done | bytes 393248 | tf_op jit(solution)/shard_map/ppermute | solution.py:55
  60.8 2.2 %shard_map.81 = (bf16[1536,384]{1,0:T(8,128)(2,1)S(1)}, bf16[1536,384]{1,0:T(8,128)(2,1)S(1)}) custom-call(s32[12]{0:T(128)S(1)} %subtract_bitcast_fusion.refs_0_, bf16[1536,2048]{1,0:T(8,128)(2,1)S(1)} %bitcast.3, bf16[512,384]{1,0:T(8,128)(2,1)S(1)} %collective-permute-done.5.refs_2_, f32[1536,384]{1,0:T(8,128)S(1)} %get-tuple-element.33.refs_3_), custom_call_target="tpu_custom_call" | custom-call | flops 603979776 | bytes 1572864 | tf_op jit(solution)/shard_map/pallas_call | solution.py:38
  63.1 2.8 %collective-permute-done.6.came_ref = bf16[1536,384]{1,0:T(8,128)(2,1)S(1)} collective-permute-done((bf16[1536,384]{1,0:T(8,128)(2,1)S(1)}, bf16[1536,384]{1,0:T(8,128)(2,1)S(1)}, u32[]{:S(2)}, u32[]{:S(2)}) %collective-permute-start.6) | collective-permute-done | bytes 1179680 | tf_op jit(solution)/shard_map/ppermute | solution.py:59
  66.0 1.6 collective-permute-start.8
  67.6 1.5 collective-permute-start.9
  70.3 2.0 collective-permute-done.8.low_ref
  72.3 2.1 collective-permute-done.9.high_ref
  74.4 1.6 collective-permute-start.10
  76.6 0.9 collective-permute-done.12.refs_3_
  77.5 2.2 collective-permute-done.10.refs_1_
  79.7 1.5 collective-permute-done.11.refs_2_
  82.5 1.6 collective-permute-start.13
  84.0 1.5 collective-permute-start.16
  85.6 1.7 collective-permute-done.15.refs_4_
  88.2 1.1 collective-permute-start.18
  89.8 2.7 %collective-permute-done.17.refs_6_ = bf16[192,384]{1,0:T(8,128)(2,1)S(1)} collective-permute-done((bf16[192,384]{1,0:T(8,128)(2,1)S(1)}, bf16[192,384]{1,0:T(8,128)(2,1)S(1)}, u32[]{:S(2)}, u32[]{:S(2)}) %collective-permute-start.17) | collective-permute-done | bytes 147488 | tf_op jit(solution)/shard_map/ppermute | solution.py:59
  93.5 2.8 %collective-permute-done.19.refs_5_.refs_6_.refs_7_.refs_8_ = bf16[1536,384]{1,0:T(8,128)(2,1)S(1)} collective-permute-done((bf16[1536,384]{1,0:T(8,128)(2,1)S(1)}, bf16[1536,384]{1,0:T(8,128)(2,1)S(1)}, u32[]{:S(2)}, u32[]{:S(2)}) %collective-permute-start.19) | collective-permute-done | bytes 1179680 | tf_op jit(solution)/shard_map/ppermute | solution.py:59
  96.3 2.0 shard_map.89
  98.3 0.9 collective-permute-start.20
  99.2 1.9 shard_map.90
  101.2 1.2 collective-permute-start.22
  102.4 3.2 %shard_map.88 = (f32[384,384]{1,0:T(8,128)S(1)}, f32[384,384]{1,0:T(8,128)S(1)}) custom-call(bf16[1536,3072]{1,0:T(8,128)(2,1)S(1)} %get-tuple-element.31.refs_0_, bf16[1536,384]{1,0:T(8,128)(2,1)S(1)} %shard_map.87.refs_1_.refs_2_.refs_3_.refs_4_, bf16[1536,384]{1,0:T(8,128)(2,1)S(1)} %shard_map.87.refs_1_.refs_2_.refs_3_.refs_4_, ...), custom_call_target="tpu_custom_call" | custom-call | flops 1811939328 | bytes 4718592 | tf_op jit(solution)/shard_map/pallas_call | solution.py:38
  105.6 8.0 %collective-permute-done.20 = bf16[384,384]{1,0:T(8,128)(2,1)S(1)} collective-permute-done((bf16[384,384]{1,0:T(8,128)(2,1)S(1)}, bf16[384,384]{1,0:T(8,128)(2,1)S(1)}, u32[]{:S(2)}, u32[]{:S(2)}) %collective-permute-start.20) | collective-permute-done | bytes 294944 | tf_op jit(solution)/shard_map/ppermute | solution.py:55
  114.2 6.3 %collective-permute-done.21 = bf16[384,384]{1,0:T(8,128)(2,1)S(1)} collective-permute-done((bf16[384,384]{1,0:T(8,128)(2,1)S(1)}, bf16[384,384]{1,0:T(8,128)(2,1)S(1)}, u32[]{:S(2)}, u32[]{:S(2)}) %collective-permute-start.21) | collective-permute-done | bytes 294944 | tf_op jit(solution)/shard_map/ppermute | solution.py:55
  120.4 0.9 fusion
  121.4 1.2 collective-permute-start.26
  122.6 1.5 collective-permute-start.28
  125.8 4.6 %collective-permute-start.27 = (bf16[96,384]{1,0:T(8,128)(2,1)S(1)}, bf16[96,384]{1,0:T(8,128)(2,1)S(1)}, u32[]{:S(2)}, u32[]{:S(2)}) collective-permute-start(bf16[96,384]{1,0:T(8,128)(2,1)S(1)} %collective-permute-done.26), channel_id=1, source_target_pairs={{0,2},{1,10},{2,18},{3,26},{4,6},{5,14},{6,22},{7,30},{8,3},{9,11}... | collective-permute-start | bytes 221192 | tf_op jit(solution)/shard_map/ppermute | solution.py:101
  130.4 2.3 %collective-permute-start.29 = (bf16[96,384]{1,0:T(8,128)(2,1)S(1)}, bf16[96,384]{1,0:T(8,128)(2,1)S(1)}, u32[]{:S(2)}, u32[]{:S(2)}) collective-permute-start(bf16[96,384]{1,0:T(8,128)(2,1)S(1)} %collective-permute-done.28), channel_id=1, source_target_pairs={{0,3},{1,11},{2,19},{3,27},{4,7},{5,15},{6,23},{7,31},{8,2},{9,10}... | collective-permute-start | bytes 221192 | tf_op jit(solution)/shard_map/ppermute | solution.py:101
  132.7 3.0 %collective-permute-done.29 = bf16[96,384]{1,0:T(8,128)(2,1)S(1)} collective-permute-done((bf16[96,384]{1,0:T(8,128)(2,1)S(1)}, bf16[96,384]{1,0:T(8,128)(2,1)S(1)}, u32[]{:S(2)}, u32[]{:S(2)}) %collective-permute-start.29) | collective-permute-done | bytes 73760 | tf_op jit(solution)/shard_map/ppermute | solution.py:101
  135.7 3.2 %collective-permute-start.31 = (bf16[192,384]{1,0:T(8,128)(2,1)S(1)}, bf16[192,384]{1,0:T(8,128)(2,1)S(1)}, u32[]{:S(2)}, u32[]{:S(2)}) collective-permute-start(bf16[192,384]{1,0:T(8,128)(2,1)S(1)} %constant_dynamic-update-slice_fusion.2.high_ref), channel_id=1, source_target_pairs={{0,8},{4,12},{8,0},{12,4},{16,24},{20,28},{24,16},{28,20},{1,9},{5... | collective-permute-start | bytes 442376 | tf_op jit(solution)/shard_map/ppermute | solution.py:59
  139.5 1.7 collective-permute-start.30
  141.2 2.2 %collective-permute-done.31.refs_3_ = bf16[192,384]{1,0:T(8,128)(2,1)S(1)} collective-permute-done((bf16[192,384]{1,0:T(8,128)(2,1)S(1)}, bf16[192,384]{1,0:T(8,128)(2,1)S(1)}, u32[]{:S(2)}, u32[]{:S(2)}) %collective-permute-start.31) | collective-permute-done | bytes 147488 | tf_op jit(solution)/shard_map/ppermute | solution.py:59
  144.2 1.8 collective-permute-start.34
  146.4 2.2 %collective-permute-done.35.refs_7_ = bf16[192,384]{1,0:T(8,128)(2,1)S(1)} collective-permute-done((bf16[192,384]{1,0:T(8,128)(2,1)S(1)}, bf16[192,384]{1,0:T(8,128)(2,1)S(1)}, u32[]{:S(2)}, u32[]{:S(2)}) %collective-permute-start.35) | collective-permute-done | bytes 147488 | tf_op jit(solution)/shard_map/ppermute | solution.py:59
  149.5 2.8 %collective-permute-done.36.refs_6_.refs_7_.refs_8_.refs_9_ = bf16[1536,384]{1,0:T(8,128)(2,1)S(1)} collective-permute-done((bf16[1536,384]{1,0:T(8,128)(2,1)S(1)}, bf16[1536,384]{1,0:T(8,128)(2,1)S(1)}, u32[]{:S(2)}, u32[]{:S(2)}) %collective-permute-start.36) | collective-permute-done | bytes 1179680 | tf_op jit(solution)/shard_map/ppermute | solution.py:59
  152.3 2.0 shard_map.93
  154.3 3.0 %collective-permute-start.37 = (bf16[384,512]{1,0:T(8,128)(2,1)S(1)}, bf16[384,512]{1,0:T(8,128)(2,1)S(1)}, u32[]{:S(2)}, u32[]{:S(2)}) collective-permute-start(bf16[384,512]{1,0:T(8,128)(2,1)S(1)} %get-tuple-element.52), channel_id=1, source_target_pairs={{0,3},{1,0},{2,1},{3,2},{4,7},{5,4},{6,5},{7,6},{8,11},{9,8},{10,9... | collective-permute-start | bytes 1179656 | tf_op jit(solution)/shard_map/ppermute | solution.py:55
  158.2 1.4 shard_map.94
  159.7 7.2 %collective-permute-done.37 = bf16[384,512]{1,0:T(8,128)(2,1)S(1)} collective-permute-done((bf16[384,512]{1,0:T(8,128)(2,1)S(1)}, bf16[384,512]{1,0:T(8,128)(2,1)S(1)}, u32[]{:S(2)}, u32[]{:S(2)}) %collective-permute-start.37) | collective-permute-done | bytes 393248 | tf_op jit(solution)/shard_map/ppermute | solution.py:55
  167.0 4.3 %collective-permute-start.38 = (bf16[384,512]{1,0:T(8,128)(2,1)S(1)}, bf16[384,512]{1,0:T(8,128)(2,1)S(1)}, u32[]{:S(2)}, u32[]{:S(2)}) collective-permute-start(bf16[384,512]{1,0:T(8,128)(2,1)S(1)} %add_convert_fusion.1), channel_id=1, source_target_pairs={{0,3},{1,0},{2,1},{3,2},{4,7},{5,4},{6,5},{7,6},{8,11},{9,8},{10,9... | collective-permute-start | bytes 1179656 | tf_op jit(solution)/shard_map/ppermute | solution.py:55
  171.3 6.7 %collective-permute-done.39 = bf16[384,512]{1,0:T(8,128)(2,1)S(1)} collective-permute-done((bf16[384,512]{1,0:T(8,128)(2,1)S(1)}, bf16[384,512]{1,0:T(8,128)(2,1)S(1)}, u32[]{:S(2)}, u32[]{:S(2)}) %collective-permute-start.39) | collective-permute-done | bytes 393248 | tf_op jit(solution)/shard_map/ppermute | solution.py:55
  178.1 7.2 %collective-permute-done.38 = bf16[384,512]{1,0:T(8,128)(2,1)S(1)} collective-permute-done((bf16[384,512]{1,0:T(8,128)(2,1)S(1)}, bf16[384,512]{1,0:T(8,128)(2,1)S(1)}, u32[]{:S(2)}, u32[]{:S(2)}) %collective-permute-start.38) | collective-permute-done | bytes 393248 | tf_op jit(solution)/shard_map/ppermute | solution.py:55
  185.5 1.0 collective-permute-start.40
  186.4 2.9 %collective-permute-start.41 = (bf16[384,512]{1,0:T(8,128)(2,1)S(1)}, bf16[384,512]{1,0:T(8,128)(2,1)S(1)}, u32[]{:S(2)}, u32[]{:S(2)}) collective-permute-start(bf16[384,512]{1,0:T(8,128)(2,1)S(1)} %add_convert_fusion.refs_2_), channel_id=1, source_target_pairs={{0,3},{1,0},{2,1},{3,2},{4,7},{5,4},{6,5},{7,6},{8,11},{9,8},{10,9... | collective-permute-start | bytes 1179656 | tf_op jit(solution)/shard_map/ppermute | solution.py:55
  189.3 10.0 %collective-permute-done.40.refs_3_ = bf16[384,512]{1,0:T(8,128)(2,1)S(1)} collective-permute-done((bf16[384,512]{1,0:T(8,128)(2,1)S(1)}, bf16[384,512]{1,0:T(8,128)(2,1)S(1)}, u32[]{:S(2)}, u32[]{:S(2)}) %collective-permute-start.40) | collective-permute-done | bytes 393248 | tf_op jit(solution)/shard_map/ppermute | solution.py:55
  199.4 7.0 %collective-permute-done.41.refs_4_ = bf16[384,512]{1,0:T(8,128)(2,1)S(1)} collective-permute-done((bf16[384,512]{1,0:T(8,128)(2,1)S(1)}, bf16[384,512]{1,0:T(8,128)(2,1)S(1)}, u32[]{:S(2)}, u32[]{:S(2)}) %collective-permute-start.41) | collective-permute-done | bytes 393248 | tf_op jit(solution)/shard_map/ppermute | solution.py:55
  206.3 1.0 shard_map.96.refs_1_
  207.3 7.5 %collective-permute-done.42.refs_2_ = bf16[384,512]{1,0:T(8,128)(2,1)S(1)} collective-permute-done((bf16[384,512]{1,0:T(8,128)(2,1)S(1)}, bf16[384,512]{1,0:T(8,128)(2,1)S(1)}, u32[]{:S(2)}, u32[]{:S(2)}) %collective-permute-start.42) | collective-permute-done | bytes 393248 | tf_op jit(solution)/shard_map/ppermute | solution.py:55
  214.8 1.3 shard_map.97
  (68 shorter events, 11.9 us)
Async XLA Ops:
  0.6 15.3 %collective-permute-start = (bf16[512,384]{1,0:T(8,128)(2,1)}, bf16[512,384]{1,0:T(8,128)(2,1)S(1)}, u32[]{:S(2)}, u32[]{:S(2)}) collective-permute-start(bf16[512,384]{1,0:T(8,128)(2,1)} %refs_1_.5), channel_id=1, source_target_pairs={{0,1},{1,2},{2,3},{3,0},{4,5},{5,6},{6,7},{7,4},{8,9},{9,10},{10,1... | collective-permute-start | bytes 1179656 | tf_op jit(solution)/shard_map/ppermute | solution.py:55
  3.7 19.4 %collective-permute-start.1 = (bf16[512,384]{1,0:T(8,128)(2,1)}, bf16[512,384]{1,0:T(8,128)(2,1)S(1)}, u32[]{:S(2)}, u32[]{:S(2)}) collective-permute-start(bf16[512,384]{1,0:T(8,128)(2,1)} %refs_1_.5), channel_id=1, source_target_pairs={{0,3},{1,0},{2,1},{3,2},{4,7},{5,4},{6,5},{7,6},{8,11},{9,8},{10,9... | collective-permute-start | bytes 1179656 | tf_op jit(solution)/shard_map/ppermute | solution.py:55
  15.9 16.0 %collective-permute-start.2 = (bf16[512,384]{1,0:T(8,128)(2,1)S(1)}, bf16[512,384]{1,0:T(8,128)(2,1)S(1)}, u32[]{:S(2)}, u32[]{:S(2)}) collective-permute-start(bf16[512,384]{1,0:T(8,128)(2,1)S(1)} %collective-permute-done.refs_2_), channel_id=1, source_target_pairs={{0,1},{1,2},{2,3},{3,0},{4,5},{5,6},{6,7},{7,4},{8,9},{9,10},{10,1... | collective-permute-start | bytes 1179656 | tf_op jit(solution)/shard_map/ppermute | solution.py:55
  23.1 1.6 copy-start.1
  24.7 1.0 copy-start.3
  25.7 27.6 %slice-start = ((s8[6291456]{0:T(1024)(128)(4,1)}), s8[2097152]{0:T(1024)(128)(4,1)S(1)}, s32[]{:S(2)}) async-start(s8[6291456]{0:T(1024)(128)(4,1)} %bitcast.2), calls=%async_computation | async-start | bytes 4194304
  26.7 20.5 %copy-start.4 = (s32[1,12]{1,0:T(1,128)S(1)}, s32[1,12]{1,0:T(1,128)}, u32[]{:S(2)}) copy-start(s32[1,12]{1,0:T(1,128)} %param.11) | copy-start | bytes 148
  33.1 14.1 %collective-permute-start.4 = (bf16[512,384]{1,0:T(8,128)(2,1)}, bf16[512,384]{1,0:T(8,128)(2,1)S(1)}, u32[]{:S(2)}, u32[]{:S(2)}) collective-permute-start(bf16[512,384]{1,0:T(8,128)(2,1)} %get-tuple-element.29.refs_1_), channel_id=1, source_target_pairs={{0,1},{1,2},{2,3},{3,0},{4,5},{5,6},{6,7},{7,4},{8,9},{9,10},{10,1... | collective-permute-start | bytes 1179656 | tf_op jit(solution)/shard_map/ppermute | solution.py:55
  33.1 20.2 %collective-permute-start.3 = (bf16[512,384]{1,0:T(8,128)(2,1)}, bf16[512,384]{1,0:T(8,128)(2,1)}, u32[]{:S(2)}, u32[]{:S(2)}) collective-permute-start(bf16[512,384]{1,0:T(8,128)(2,1)} %get-tuple-element.29.refs_1_), channel_id=1, source_target_pairs={{0,3},{1,0},{2,1},{3,2},{4,7},{5,4},{6,5},{7,6},{8,11},{9,8},{10,9... | collective-permute-start | bytes 1179656 | tf_op jit(solution)/shard_map/ppermute | solution.py:55
  47.2 13.6 %collective-permute-start.5 = (bf16[512,384]{1,0:T(8,128)(2,1)S(1)}, bf16[512,384]{1,0:T(8,128)(2,1)S(1)}, u32[]{:S(2)}, u32[]{:S(2)}) collective-permute-start(bf16[512,384]{1,0:T(8,128)(2,1)S(1)} %collective-permute-done.4.refs_2_), channel_id=1, source_target_pairs={{0,1},{1,2},{2,3},{3,0},{4,5},{5,6},{6,7},{7,4},{8,9},{9,10},{10,1... | collective-permute-start | bytes 1179656 | tf_op jit(solution)/shard_map/ppermute | solution.py:55
  47.2 2.8 %copy-start = (bf16[1536,2048]{1,0:T(8,128)(2,1)S(1)}, bf16[1536,2048]{1,0:T(8,128)(2,1)}, u32[]{:S(2)}) copy-start(bf16[1536,2048]{1,0:T(8,128)(2,1)} %refs_1_.9) | copy-start | bytes 18874372
  50.0 3.3 %slice-start.1 = ((s8[6291456]{0:T(1024)(128)(4,1)}), s8[4194304]{0:T(1024)(128)(4,1)S(1)}, s32[]{:S(2)}) async-start(s8[6291456]{0:T(1024)(128)(4,1)} %bitcast.2), calls=%async_computation.1 | async-start | bytes 8388608
  63.1 2.9 %collective-permute-start.6 = (bf16[1536,384]{1,0:T(8,128)(2,1)S(1)}, bf16[1536,384]{1,0:T(8,128)(2,1)S(1)}, u32[]{:S(2)}, u32[]{:S(2)}) collective-permute-start(bf16[1536,384]{1,0:T(8,128)(2,1)S(1)} %get-tuple-element.35), channel_id=1, source_target_pairs={{0,4},{4,0},{8,12},{12,8},{16,20},{20,16},{24,28},{28,24},{1,5},{5... | collective-permute-start | bytes 3538952 | tf_op jit(solution)/shard_map/ppermute | solution.py:59
  66.0 6.2 %collective-permute-start.8 = (bf16[192,384]{1,0:T(8,128)(2,1)S(1)}, bf16[192,384]{1,0:T(8,128)(2,1)S(1)}, u32[]{:S(2)}, u32[]{:S(2)}) collective-permute-start(bf16[192,384]{1,0:T(8,128)(2,1)S(1)} %get-tuple-element.37), channel_id=1, source_target_pairs={{0,8},{4,12},{8,0},{12,4},{16,24},{20,28},{24,16},{28,20},{1,9},{5... | collective-permute-start | bytes 442376 | tf_op jit(solution)/shard_map/ppermute | solution.py:59
  67.6 6.7 %collective-permute-start.9 = (bf16[192,384]{1,0:T(8,128)(2,1)S(1)}, bf16[192,384]{1,0:T(8,128)(2,1)S(1)}, u32[]{:S(2)}, u32[]{:S(2)}) collective-permute-start(bf16[192,384]{1,0:T(8,128)(2,1)S(1)} %get-tuple-element.38), channel_id=1, source_target_pairs={{0,16},{4,20},{8,24},{12,28},{16,0},{20,4},{24,8},{28,12},{1,17},{... | collective-permute-start | bytes 442376 | tf_op jit(solution)/shard_map/ppermute | solution.py:59
  69.2 8.3 %collective-permute-start.12 = (bf16[192,384]{1,0:T(8,128)(2,1)S(1)}, bf16[192,384]{1,0:T(8,128)(2,1)S(1)}, u32[]{:S(2)}, u32[]{:S(2)}) collective-permute-start(bf16[192,384]{1,0:T(8,128)(2,1)S(1)} %get-tuple-element.41), channel_id=1, source_target_pairs={{0,16},{4,20},{8,24},{12,28},{16,0},{20,4},{24,8},{28,12},{1,17},{... | collective-permute-start | bytes 442376 | tf_op jit(solution)/shard_map/ppermute | solution.py:59
  69.8 7.7 %collective-permute-start.7 = (bf16[192,384]{1,0:T(8,128)(2,1)S(1)}, bf16[192,384]{1,0:T(8,128)(2,1)S(1)}, u32[]{:S(2)}, u32[]{:S(2)}) collective-permute-start(bf16[192,384]{1,0:T(8,128)(2,1)S(1)} %get-tuple-element.36), channel_id=1, source_target_pairs={{0,8},{4,12},{8,0},{12,4},{16,24},{20,28},{24,16},{28,20},{1,9},{5... | collective-permute-start | bytes 442376 | tf_op jit(solution)/shard_map/ppermute | solution.py:59
  74.4 5.2 %collective-permute-start.10 = (bf16[192,384]{1,0:T(8,128)(2,1)S(1)}, bf16[192,384]{1,0:T(8,128)(2,1)S(1)}, u32[]{:S(2)}, u32[]{:S(2)}) collective-permute-start(bf16[192,384]{1,0:T(8,128)(2,1)S(1)} %get-tuple-element.39), channel_id=1, source_target_pairs={{0,16},{4,20},{8,24},{12,28},{16,0},{20,4},{24,8},{28,12},{1,17},{... | collective-permute-start | bytes 442376 | tf_op jit(solution)/shard_map/ppermute | solution.py:59
  76.0 5.1 %collective-permute-start.11 = (bf16[192,384]{1,0:T(8,128)(2,1)S(1)}, bf16[192,384]{1,0:T(8,128)(2,1)S(1)}, u32[]{:S(2)}, u32[]{:S(2)}) collective-permute-start(bf16[192,384]{1,0:T(8,128)(2,1)S(1)} %get-tuple-element.40), channel_id=1, source_target_pairs={{0,8},{4,12},{8,0},{12,4},{16,24},{20,28},{24,16},{28,20},{1,9},{5... | collective-permute-start | bytes 442376 | tf_op jit(solution)/shard_map/ppermute | solution.py:59
  81.4 6.0 %collective-permute-start.15 = (bf16[192,384]{1,0:T(8,128)(2,1)S(1)}, bf16[192,384]{1,0:T(8,128)(2,1)S(1)}, u32[]{:S(2)}, u32[]{:S(2)}) collective-permute-start(bf16[192,384]{1,0:T(8,128)(2,1)S(1)} %get-tuple-element.42.low_ref), channel_id=1, source_target_pairs={{0,16},{4,20},{8,24},{12,28},{16,0},{20,4},{24,8},{28,12},{1,17},{... | collective-permute-start | bytes 442376 | tf_op jit(solution)/shard_map/ppermute | solution.py:59
  81.9 6.2 %collective-permute-start.14 = (bf16[192,384]{1,0:T(8,128)(2,1)S(1)}, bf16[192,384]{1,0:T(8,128)(2,1)S(1)}, u32[]{:S(2)}, u32[]{:S(2)}) collective-permute-start(bf16[192,384]{1,0:T(8,128)(2,1)S(1)} %get-tuple-element.43.high_ref), channel_id=1, source_target_pairs={{0,8},{4,12},{8,0},{12,4},{16,24},{20,28},{24,16},{28,20},{1,9},{5... | collective-permute-start | bytes 442376 | tf_op jit(solution)/shard_map/ppermute | solution.py:59
  82.5 7.3 %collective-permute-start.13 = (bf16[192,384]{1,0:T(8,128)(2,1)S(1)}, bf16[192,384]{1,0:T(8,128)(2,1)S(1)}, u32[]{:S(2)}, u32[]{:S(2)}) collective-permute-start(bf16[192,384]{1,0:T(8,128)(2,1)S(1)} %get-tuple-element.44.refs_0_), channel_id=1, source_target_pairs={{0,8},{4,12},{8,0},{12,4},{16,24},{20,28},{24,16},{28,20},{1,9},{5... | collective-permute-start | bytes 442376 | tf_op jit(solution)/shard_map/ppermute | solution.py:59
  84.0 5.7 %collective-permute-start.16 = (bf16[192,384]{1,0:T(8,128)(2,1)S(1)}, bf16[192,384]{1,0:T(8,128)(2,1)S(1)}, u32[]{:S(2)}, u32[]{:S(2)}) collective-permute-start(bf16[192,384]{1,0:T(8,128)(2,1)S(1)} %get-tuple-element.45.refs_1_), channel_id=1, source_target_pairs={{0,16},{4,20},{8,24},{12,28},{16,0},{20,4},{24,8},{28,12},{1,17},{... | collective-permute-start | bytes 442376 | tf_op jit(solution)/shard_map/ppermute | solution.py:59
  87.3 5.1 %collective-permute-start.17 = (bf16[192,384]{1,0:T(8,128)(2,1)S(1)}, bf16[192,384]{1,0:T(8,128)(2,1)S(1)}, u32[]{:S(2)}, u32[]{:S(2)}) collective-permute-start(bf16[192,384]{1,0:T(8,128)(2,1)S(1)} %collective-permute-done.15.refs_4_), channel_id=1, source_target_pairs={{0,8},{4,12},{8,0},{12,4},{16,24},{20,28},{24,16},{28,20},{1,9},{5... | collective-permute-start | bytes 442376 | tf_op jit(solution)/shard_map/ppermute | solution.py:59
  88.2 5.1 %collective-permute-start.18 = (bf16[192,384]{1,0:T(8,128)(2,1)S(1)}, bf16[192,384]{1,0:T(8,128)(2,1)S(1)}, u32[]{:S(2)}, u32[]{:S(2)}) collective-permute-start(bf16[192,384]{1,0:T(8,128)(2,1)S(1)} %collective-permute-done.14.refs_3_), channel_id=1, source_target_pairs={{0,16},{4,20},{8,24},{12,28},{16,0},{20,4},{24,8},{28,12},{1,17},{... | collective-permute-start | bytes 442376 | tf_op jit(solution)/shard_map/ppermute | solution.py:59
  93.4 2.9 %collective-permute-start.19 = (bf16[1536,384]{1,0:T(8,128)(2,1)S(1)}, bf16[1536,384]{1,0:T(8,128)(2,1)S(1)}, u32[]{:S(2)}, u32[]{:S(2)}) collective-permute-start(bf16[1536,384]{1,0:T(8,128)(2,1)S(1)} %shard_map.87.refs_1_.refs_2_.refs_3_.refs_4_), channel_id=1, source_target_pairs={{0,4},{4,0},{8,12},{12,8},{16,20},{20,16},{24,28},{28,24},{1,5},{5... | collective-permute-start | bytes 3538952 | tf_op jit(solution)/shard_map/ppermute | solution.py:59
  98.3 15.3 %collective-permute-start.20 = (bf16[384,384]{1,0:T(8,128)(2,1)S(1)}, bf16[384,384]{1,0:T(8,128)(2,1)S(1)}, u32[]{:S(2)}, u32[]{:S(2)}) collective-permute-start(bf16[384,384]{1,0:T(8,128)(2,1)S(1)} %shard_map.89), channel_id=1, source_target_pairs={{0,3},{1,0},{2,1},{3,2},{4,7},{5,4},{6,5},{7,6},{8,11},{9,8},{10,9... | collective-permute-start | bytes 884744 | tf_op jit(solution)/shard_map/ppermute | solution.py:55
  101.2 13.0 %collective-permute-start.22 = (bf16[384,384]{1,0:T(8,128)(2,1)S(1)}, bf16[384,384]{1,0:T(8,128)(2,1)S(1)}, u32[]{:S(2)}, u32[]{:S(2)}) collective-permute-start(bf16[384,384]{1,0:T(8,128)(2,1)S(1)} %shard_map.90), channel_id=1, source_target_pairs={{0,1},{1,2},{2,3},{3,0},{4,5},{5,6},{6,7},{7,4},{8,9},{9,10},{10,1... | collective-permute-start | bytes 884744 | tf_op jit(solution)/shard_map/ppermute | solution.py:55
  113.7 6.8 %collective-permute-start.21 = (bf16[384,384]{1,0:T(8,128)(2,1)S(1)}, bf16[384,384]{1,0:T(8,128)(2,1)S(1)}, u32[]{:S(2)}, u32[]{:S(2)}) collective-permute-start(bf16[384,384]{1,0:T(8,128)(2,1)S(1)} %add_convert_fusion.2), channel_id=1, source_target_pairs={{0,3},{1,0},{2,1},{3,2},{4,7},{5,4},{6,5},{7,6},{8,11},{9,8},{10,9... | collective-permute-start | bytes 884744 | tf_op jit(solution)/shard_map/ppermute | solution.py:55
  121.4 4.4 %collective-permute-start.26 = (bf16[96,384]{1,0:T(8,128)(2,1)S(1)}, bf16[96,384]{1,0:T(8,128)(2,1)S(1)}, u32[]{:S(2)}, u32[]{:S(2)}) collective-permute-start(bf16[96,384]{1,0:T(8,128)(2,1)S(1)} %get-tuple-element.57), channel_id=1, source_target_pairs={{0,16},{4,20},{8,24},{12,28},{16,0},{20,4},{24,8},{28,12},{1,17},{... | collective-permute-start | bytes 221192 | tf_op jit(solution)/shard_map/ppermute | solution.py:59
  122.6 7.8 %collective-permute-start.28 = (bf16[96,384]{1,0:T(8,128)(2,1)S(1)}, bf16[96,384]{1,0:T(8,128)(2,1)S(1)}, u32[]{:S(2)}, u32[]{:S(2)}) collective-permute-start(bf16[96,384]{1,0:T(8,128)(2,1)S(1)} %get-tuple-element.56), channel_id=1, source_target_pairs={{0,24},{4,28},{8,16},{12,20},{16,8},{20,12},{24,0},{28,4},{1,25},{... | collective-permute-start | bytes 221192 | tf_op jit(solution)/shard_map/ppermute | solution.py:59
  124.1 8.6 %collective-permute-start.24 = (bf16[96,384]{1,0:T(8,128)(2,1)S(1)}, bf16[96,384]{1,0:T(8,128)(2,1)S(1)}, u32[]{:S(2)}, u32[]{:S(2)}) collective-permute-start(bf16[96,384]{1,0:T(8,128)(2,1)S(1)} %get-tuple-element.58), channel_id=1, source_target_pairs={{0,8},{4,12},{8,0},{12,4},{16,24},{20,28},{24,16},{28,20},{1,9},{5... | collective-permute-start | bytes 221192 | tf_op jit(solution)/shard_map/ppermute | solution.py:59
  124.9 7.7 %collective-permute-start.23 = (bf16[96,384]{1,0:T(8,128)(2,1)S(1)}, bf16[96,384]{1,0:T(8,128)(2,1)S(1)}, u32[]{:S(2)}, u32[]{:S(2)}) collective-permute-start(bf16[96,384]{1,0:T(8,128)(2,1)S(1)} %get-tuple-element.59), channel_id=1, source_target_pairs={{0,0},{1,8},{2,16},{3,24},{4,4},{5,12},{6,20},{7,28},{8,1},{9,9},{... | collective-permute-start | bytes 221192 | tf_op jit(solution)/shard_map/ppermute | solution.py:101
  125.8 6.9 %collective-permute-start.27 = (bf16[96,384]{1,0:T(8,128)(2,1)S(1)}, bf16[96,384]{1,0:T(8,128)(2,1)S(1)}, u32[]{:S(2)}, u32[]{:S(2)}) collective-permute-start(bf16[96,384]{1,0:T(8,128)(2,1)S(1)} %collective-permute-done.26), channel_id=1, source_target_pairs={{0,2},{1,10},{2,18},{3,26},{4,6},{5,14},{6,22},{7,30},{8,3},{9,11}... | collective-permute-start | bytes 221192 | tf_op jit(solution)/shard_map/ppermute | solution.py:101
  130.4 5.3 %collective-permute-start.29 = (bf16[96,384]{1,0:T(8,128)(2,1)S(1)}, bf16[96,384]{1,0:T(8,128)(2,1)S(1)}, u32[]{:S(2)}, u32[]{:S(2)}) collective-permute-start(bf16[96,384]{1,0:T(8,128)(2,1)S(1)} %collective-permute-done.28), channel_id=1, source_target_pairs={{0,3},{1,11},{2,19},{3,27},{4,7},{5,15},{6,23},{7,31},{8,2},{9,10}... | collective-permute-start | bytes 221192 | tf_op jit(solution)/shard_map/ppermute | solution.py:101
  132.7 6.3 %collective-permute-start.25 = (bf16[96,384]{1,0:T(8,128)(2,1)S(1)}, bf16[96,384]{1,0:T(8,128)(2,1)S(1)}, u32[]{:S(2)}, u32[]{:S(2)}) collective-permute-start(bf16[96,384]{1,0:T(8,128)(2,1)S(1)} %collective-permute-done.24), channel_id=1, source_target_pairs={{0,1},{1,9},{2,17},{3,25},{4,5},{5,13},{6,21},{7,29},{8,0},{9,8},{... | collective-permute-start | bytes 221192 | tf_op jit(solution)/shard_map/ppermute | solution.py:101
  135.7 7.7 %collective-permute-start.31 = (bf16[192,384]{1,0:T(8,128)(2,1)S(1)}, bf16[192,384]{1,0:T(8,128)(2,1)S(1)}, u32[]{:S(2)}, u32[]{:S(2)}) collective-permute-start(bf16[192,384]{1,0:T(8,128)(2,1)S(1)} %constant_dynamic-update-slice_fusion.2.high_ref), channel_id=1, source_target_pairs={{0,8},{4,12},{8,0},{12,4},{16,24},{20,28},{24,16},{28,20},{1,9},{5... | collective-permute-start | bytes 442376 | tf_op jit(solution)/shard_map/ppermute | solution.py:59
  139.0 5.2 %collective-permute-start.32 = (bf16[192,384]{1,0:T(8,128)(2,1)S(1)}, bf16[192,384]{1,0:T(8,128)(2,1)S(1)}, u32[]{:S(2)}, u32[]{:S(2)}) collective-permute-start(bf16[192,384]{1,0:T(8,128)(2,1)S(1)} %constant_dynamic-update-slice_fusion.low_ref), channel_id=1, source_target_pairs={{0,16},{4,20},{8,24},{12,28},{16,0},{20,4},{24,8},{28,12},{1,17},{... | collective-permute-start | bytes 442376 | tf_op jit(solution)/shard_map/ppermute | solution.py:59
  139.5 6.5 %collective-permute-start.30 = (bf16[192,384]{1,0:T(8,128)(2,1)S(1)}, bf16[192,384]{1,0:T(8,128)(2,1)S(1)}, u32[]{:S(2)}, u32[]{:S(2)}) collective-permute-start(bf16[192,384]{1,0:T(8,128)(2,1)S(1)} %get-tuple-element.48.refs_0_), channel_id=1, source_target_pairs={{0,8},{4,12},{8,0},{12,4},{16,24},{20,28},{24,16},{28,20},{1,9},{5... | collective-permute-start | bytes 442376 | tf_op jit(solution)/shard_map/ppermute | solution.py:59
  141.2 5.1 %collective-permute-start.33 = (bf16[192,384]{1,0:T(8,128)(2,1)S(1)}, bf16[192,384]{1,0:T(8,128)(2,1)S(1)}, u32[]{:S(2)}, u32[]{:S(2)}) collective-permute-start(bf16[192,384]{1,0:T(8,128)(2,1)S(1)} %get-tuple-element.49.refs_1_), channel_id=1, source_target_pairs={{0,16},{4,20},{8,24},{12,28},{16,0},{20,4},{24,8},{28,12},{1,17},{... | collective-permute-start | bytes 442376 | tf_op jit(solution)/shard_map/ppermute | solution.py:59
  143.4 5.1 %collective-permute-start.35 = (bf16[192,384]{1,0:T(8,128)(2,1)S(1)}, bf16[192,384]{1,0:T(8,128)(2,1)S(1)}, u32[]{:S(2)}, u32[]{:S(2)}) collective-permute-start(bf16[192,384]{1,0:T(8,128)(2,1)S(1)} %collective-permute-done.31.refs_3_), channel_id=1, source_target_pairs={{0,16},{4,20},{8,24},{12,28},{16,0},{20,4},{24,8},{28,12},{1,17},{... | collective-permute-start | bytes 442376 | tf_op jit(solution)/shard_map/ppermute | solution.py:59
  144.2 5.1 %collective-permute-start.34 = (bf16[192,384]{1,0:T(8,128)(2,1)S(1)}, bf16[192,384]{1,0:T(8,128)(2,1)S(1)}, u32[]{:S(2)}, u32[]{:S(2)}) collective-permute-start(bf16[192,384]{1,0:T(8,128)(2,1)S(1)} %collective-permute-done.32.refs_4_), channel_id=1, source_target_pairs={{0,8},{4,12},{8,0},{12,4},{16,24},{20,28},{24,16},{28,20},{1,9},{5... | collective-permute-start | bytes 442376 | tf_op jit(solution)/shard_map/ppermute | solution.py:59
  149.4 2.9 %collective-permute-start.36 = (bf16[1536,384]{1,0:T(8,128)(2,1)S(1)}, bf16[1536,384]{1,0:T(8,128)(2,1)S(1)}, u32[]{:S(2)}, u32[]{:S(2)}) collective-permute-start(bf16[1536,384]{1,0:T(8,128)(2,1)S(1)} %shard_map.92.refs_2_.refs_3_.refs_4_.refs_5_), channel_id=1, source_target_pairs={{0,4},{4,0},{8,12},{12,8},{16,20},{20,16},{24,28},{28,24},{1,5},{5... | collective-permute-start | bytes 3538952 | tf_op jit(solution)/shard_map/ppermute | solution.py:59
  154.3 12.5 %collective-permute-start.37 = (bf16[384,512]{1,0:T(8,128)(2,1)S(1)}, bf16[384,512]{1,0:T(8,128)(2,1)S(1)}, u32[]{:S(2)}, u32[]{:S(2)}) collective-permute-start(bf16[384,512]{1,0:T(8,128)(2,1)S(1)} %get-tuple-element.52), channel_id=1, source_target_pairs={{0,3},{1,0},{2,1},{3,2},{4,7},{5,4},{6,5},{7,6},{8,11},{9,8},{10,9... | collective-permute-start | bytes 1179656 | tf_op jit(solution)/shard_map/ppermute | solution.py:55
  158.2 19.9 %collective-permute-start.39 = (bf16[384,512]{1,0:T(8,128)(2,1)S(1)}, bf16[384,512]{1,0:T(8,128)(2,1)S(1)}, u32[]{:S(2)}, u32[]{:S(2)}) collective-permute-start(bf16[384,512]{1,0:T(8,128)(2,1)S(1)} %shard_map.95), channel_id=1, source_target_pairs={{0,1},{1,2},{2,3},{3,0},{4,5},{5,6},{6,7},{7,4},{8,9},{9,10},{10,1... | collective-permute-start | bytes 1179656 | tf_op jit(solution)/shard_map/ppermute | solution.py:55
  166.9 39.4 %copy-start.2 = (bf16[512,2048]{1,0:T(8,128)(2,1)S(1)}, bf16[512,2048]{1,0:T(8,128)(2,1)}, u32[]{:S(2)}) copy-start(bf16[512,2048]{1,0:T(8,128)(2,1)} %refs_0_.11) | copy-start | bytes 6291460
  167.0 18.3 %collective-permute-start.38 = (bf16[384,512]{1,0:T(8,128)(2,1)S(1)}, bf16[384,512]{1,0:T(8,128)(2,1)S(1)}, u32[]{:S(2)}, u32[]{:S(2)}) collective-permute-start(bf16[384,512]{1,0:T(8,128)(2,1)S(1)} %add_convert_fusion.1), channel_id=1, source_target_pairs={{0,3},{1,0},{2,1},{3,2},{4,7},{5,4},{6,5},{7,6},{8,11},{9,8},{10,9... | collective-permute-start | bytes 1179656 | tf_op jit(solution)/shard_map/ppermute | solution.py:55
  185.5 13.9 %collective-permute-start.40 = (bf16[384,512]{1,0:T(8,128)(2,1)S(1)}, bf16[384,512]{1,0:T(8,128)(2,1)S(1)}, u32[]{:S(2)}, u32[]{:S(2)}) collective-permute-start(bf16[384,512]{1,0:T(8,128)(2,1)S(1)} %add_convert_fusion.refs_2_), channel_id=1, source_target_pairs={{0,1},{1,2},{2,3},{3,0},{4,5},{5,6},{6,7},{7,4},{8,9},{9,10},{10,1... | collective-permute-start | bytes 1179656 | tf_op jit(solution)/shard_map/ppermute | solution.py:55
  186.4 19.9 %collective-permute-start.41 = (bf16[384,512]{1,0:T(8,128)(2,1)S(1)}, bf16[384,512]{1,0:T(8,128)(2,1)S(1)}, u32[]{:S(2)}, u32[]{:S(2)}) collective-permute-start(bf16[384,512]{1,0:T(8,128)(2,1)S(1)} %add_convert_fusion.refs_2_), channel_id=1, source_target_pairs={{0,3},{1,0},{2,1},{3,2},{4,7},{5,4},{6,5},{7,6},{8,11},{9,8},{10,9... | collective-permute-start | bytes 1179656 | tf_op jit(solution)/shard_map/ppermute | solution.py:55
  199.4 15.4 %collective-permute-start.42 = (bf16[384,512]{1,0:T(8,128)(2,1)S(1)}, bf16[384,512]{1,0:T(8,128)(2,1)S(1)}, u32[]{:S(2)}, u32[]{:S(2)}) collective-permute-start(bf16[384,512]{1,0:T(8,128)(2,1)S(1)} %collective-permute-done.40.refs_3_), channel_id=1, source_target_pairs={{0,1},{1,2},{2,3},{3,0},{4,5},{5,6},{6,7},{7,4},{8,9},{9,10},{10,1... | collective-permute-start | bytes 1179656 | tf_op jit(solution)/shard_map/ppermute | solution.py:55
